TPU v7x, 32 devices: a whole 2x2x4 slice. The times are simulated.
32 devices in a mesh: grp: 2 (over y), patch: 4 (over z), head: 2 (over x), sub: 2 (over core).
Axes of the slice: x: 2, y: 2, z: 4, core: 2. Of those that a mesh axis runs over, the one named last changes fastest.
Arguments:
- queries: bfloat16 [2048, 4096], P(('grp', 'patch'), ('head', 'sub')), parts along dimension 0, may hold values from -140 to 140
- fresh_kv: bfloat16 [2, 2048, 4096], P(None, ('grp', 'patch'), ('head', 'sub')), parts along dimension 1, may hold values from -9 to 9
- cached_kv: bfloat16 [2, 2048, 4096], P(None, 'grp', ('head', 'sub')), parts along dimension 1, may hold values from -5 to 5
- exponents: int32 [2, 16, 32], P(None, ('grp', 'patch'), ('head', 'sub')), parts along dimension 1, may hold values from -10 to -7
- out_weight: bfloat16 [4096, 5120], P(('head', 'sub'), 'patch'), may hold values from -0.09375 to 0.09375
- hidden_in: bfloat16 [2048, 5120], P(('grp', 'patch', 'head', 'sub')), parts along dimension 0, may hold values from -6 to 6
- attn_gate: float32 [5120], replicated, may hold values from 0.25 to 1.75
Outputs:
- mixed: bfloat16 [2048, 5120], P(('grp', 'patch', 'head', 'sub')), parts along dimension 0
There are 2 independent parts, one for each index of `grp`. A program takes and returns all parts, laid end to end along the dimension named above; an argument that names none is the same for every part. Nothing has to cross between parts.
All inputs are finite; a program needn't handle non-finite values.
Results may differ from a plain program's by a relative error of at most 0.0095.
Values may be sent and summed in bfloat16 or wider, within the bound.
No kernel may reach another device: no remote copies, remote signals or barrier semaphores. Data moves between devices by JAX's collectives and lax.ppermute only.
A program may use at most 128 MiB of HBM per device.

v0:
```python
import jax
import jax.numpy as jnp
from jax import lax
from jax.sharding import PartitionSpec as P

HEAD_DIM = 128
SCALE_ROWS = 128


SATURATION = 448.0


def block_scale(exps_float, head_dim):
    grown = jnp.repeat(exps_float, head_dim, axis=2)
    return jnp.exp2(grown)[:, :, None, :]


def decode(codes_blocks, exps_blocks, cached_rows):
    stacked, block_count, block_rows, channels = codes_blocks.shape
    scale_up = block_scale(exps_blocks.astype(jnp.float32), HEAD_DIM)
    cached_blocks = cached_rows.astype(jnp.float32).reshape(
        stacked, block_count, block_rows, channels
    )
    decoded = (cached_blocks + codes_blocks.astype(jnp.float32) * scale_up).astype(jnp.bfloat16)
    return decoded.reshape(stacked, block_count * block_rows, channels)


def body(queries, fresh_kv, cached_kv, exponents, out_weight, hidden_in, attn_gate):
    tok_dev, channels = queries.shape
    heads_dev = channels // HEAD_DIM
    block_count = tok_dev // SCALE_ROWS
    factor = HEAD_DIM ** (-0.5)
    row_start = lax.axis_index("patch") * tok_dev
    own_cached = lax.dynamic_slice_in_dim(cached_kv, row_start, tok_dev, 1)
    exps_float = exponents.astype(jnp.float32)
    residual = (fresh_kv.astype(jnp.float32) - own_cached.astype(jnp.float32)).reshape(
        2, block_count, SCALE_ROWS, channels
    )
    codes_own = jnp.clip(
        residual * block_scale(-exps_float, HEAD_DIM), -SATURATION, SATURATION
    ).astype(jnp.bfloat16)
    exps_wire = exponents.astype(jnp.bfloat16)
    query_heads = queries.reshape(tok_dev, heads_dev, HEAD_DIM)
    codes_all, exps_all = (
        lax.all_gather(codes_own, "patch", axis=1, tiled=True),
        lax.all_gather(exps_wire, "patch", axis=1, tiled=True),
    )
    decoded = decode(codes_all, exps_all, cached_kv)
    key_count = decoded.shape[1]
    key_heads = decoded[0].reshape(key_count, heads_dev, HEAD_DIM)
    value_heads = decoded[1].reshape(key_count, heads_dev, HEAD_DIM)
    scores = (
        jnp.einsum("qhd,khd->hqk", query_heads, key_heads, preferred_element_type=jnp.float32)
        * factor
    )
    peak = jnp.max(scores, axis=2, keepdims=True)
    expo = jnp.exp(scores - peak)
    weights = (expo / jnp.sum(expo, axis=2, keepdims=True)).astype(jnp.bfloat16)
    attended = jnp.einsum("hqk,khd->qhd", weights, value_heads, preferred_element_type=jnp.float32)
    attended = attended.astype(jnp.bfloat16).reshape(tok_dev, channels)
    partial_terms = jnp.dot(
        attended,
        lax.all_gather(out_weight, "patch", axis=1, tiled=True),
        preferred_element_type=jnp.float32,
    )
    projected = lax.psum_scatter(
        partial_terms.astype(jnp.bfloat16), ("head", "sub"), scatter_dimension=0, tiled=True
    ).astype(jnp.float32)
    return (hidden_in.astype(jnp.float32) + attn_gate * projected).astype(jnp.bfloat16)


def solution(mesh):
    in_specs = (
        P(("grp", "patch"), ("head", "sub")),
        P(None, ("grp", "patch"), ("head", "sub")),
        P(None, "grp", ("head", "sub")),
        P(None, ("grp", "patch"), ("head", "sub")),
        P(("head", "sub"), "patch"),
        P(("grp", "patch", "head", "sub"), None),
        P(),
    )
    out_specs = P(("grp", "patch", "head", "sub"), None)
    return jax.shard_map(body, mesh=mesh, in_specs=in_specs, out_specs=out_specs, check_vma=False)
```

profile of v0, /device:TPU:0, one launch (start us, length us, event | category | flops | bytes accessed | tf_op | source)
XLA Modules:
  0.0 328.3 jit_solution(17870861583141890833)
XLA Ops:
  6.5 0.0 copy-start
  6.5 0.0 all-gather.3.cloned.1.call-start
  6.5 0.7 multiply_exponential_fusion.1
  7.3 0.1 broadcast_in_dim.4
  7.4 1.9 convert_subtract_fusion
  9.3 0.0 copy-start.4
  9.3 1.3 clamp_convert_fusion
  10.6 0.0 all-gather.3.cloned.1.call-update
  10.6 0.0 all-gather.5.cloned.1.call-start
  10.7 0.7 all-gather.5.cloned.1.call-update
  11.4 0.0 reduce-scatter.2.cloned.1.call-start
  11.4 0.0 copy-done.4
  11.5 12.6 %all_gather.10 = bf16[2,8,8]{2,0,1:T(2,128)(2,1)S(1)} all-gather(bf16[2,2,8]{2,0,1:T(2,128)(2,1)S(1)} %copy_convert_fusion), channel_id=1, replica_groups=mesh['grp'=2,'patch'=4,'head'=2,'sub'=2] {'patch'}, dimensions={1}, use_global_device_ids=true | all-gather | bytes 320 | tf_op jit(solution)/shard_map/all_gather | solution.py:46
  24.1 0.1 copy.27
  24.2 0.1 broadcast_bitcast_fusion
  24.2 70.0 %all-gather.3.cloned.1.call-done = bf16[2,8,128,1024]{3,2,1,0:T(8,128)(2,1)} async-done(((bf16[2,2,128,1024]{3,2,1,0:T(8,128)(2,1)}), bf16[2,8,128,1024]{3,2,1,0:T(8,128)(2,1)}) %all-gather.3.cloned.1.call-update) | async-done | bytes 4194320 | tf_op jit(solution)/shard_map/all_gather | solution.py:45
  94.3 5.7 %fusion.1 = bf16[2,8,128,1024]{3,2,1,0:T(8,128)(2,1)S(1)} fusion(bf16[2,8,128,1024]{3,2,1,0:T(8,128)(2,1)} %bitcast.50, bf16[2,8,128,1024]{3,2,1,0:T(8,128)(2,1)} %all-gather.3.cloned.1.call-done, f32[2,8,1024]{2,1,0:T(8,128)S(1)} %broadcast_bitcast_fusion), kind=kLoop, calls=%fused_computation.2 | loop fusion | flops 10485760 | bytes 12648448 | tf_op jit(solution)/shard_map/convert_element_type | solution.py:24
  99.9 0.7 fusion.25
  100.6 0.6 copy.36
  101.2 0.6 copy.35
  101.9 0.0 copy-done
  101.9 1.3 fusion.10
  103.1 0.0 copy-start.1
  103.2 2.2 fusion.26
  105.4 1.6 copy-done.1
  106.9 9.1 %fusion.12 = bf16[8,128,256]{2,1,0:T(8,128)(2,1)S(1)} fusion(f32[8,256]{1,0:T(8,128)S(1)} %fusion.26, bf16[1024,8,128]{2,1,0:T(8,128)(2,1)S(1)} %bitcast.51, f32[8,1024,256]{2,1,0:T(8,128)} %copy-done.1), kind=kOutput, calls=%fused_computation.18 | convolution fusion | flops 547621888 | bytes 11018240 | tf_op jit(solution)/shard_map/hqk,khd->qhd/dot_general | solution.py:59
  116.0 162.3 %all-gather.5.cloned.1.call-done = bf16[1024,5120]{1,0:T(8,128)(2,1)} async-done(((bf16[1024,1280]{1,0:T(8,128)(2,1)}), bf16[1024,5120]{1,0:T(8,128)(2,1)}) %all-gather.5.cloned.1.call-update) | async-done | bytes 10485776 | tf_op jit(solution)/shard_map/all_gather | solution.py:63
  278.3 0.0 copy-start.2
  278.3 0.0 copy-start.3
  278.3 8.3 %convolution_convert_fusion = bf16[256,5120]{1,0:T(8,128)(2,1)} fusion(bf16[256,1024]{0,1:T(8,128)(2,1)S(1)} %bitcast.52, bf16[1024,5120]{1,0:T(8,128)(2,1)} %all-gather.5.cloned.1.call-done), kind=kOutput, calls=%fused_computation.9 | convolution fusion | flops 2685665280 | bytes 13631488 | tf_op jit(solution)/shard_map/dot_general | solution.py:61
  286.7 0.0 reduce-scatter.2.cloned.1.call-update
  286.7 33.0 %reduce-scatter.2.cloned.1.call-done = bf16[64,5120]{1,0:T(8,128)(2,1)} async-done(((bf16[256,5120]{1,0:T(8,128)(2,1)}), bf16[64,5120]{1,0:T(8,128)(2,1)}) %reduce-scatter.2.cloned.1.call-update) | async-done | bytes 655376 | tf_op jit(solution)/shard_map/reduce_scatter | solution.py:66
  319.7 0.0 copy-done.2
  319.7 0.0 copy-done.3
  319.7 2.1 add_convert_fusion
  (3 shorter events, 0.0 us)
Async XLA Ops:
  6.5 95.3 %copy-start = (bf16[256,1024]{1,0:T(8,128)(2,1)S(1)}, bf16[256,1024]{1,0:T(8,128)(2,1)}, u32[]{:S(2)}) copy-start(bf16[256,1024]{1,0:T(8,128)(2,1)} %param.7) | copy-start | bytes 1572868
  6.5 87.7 %all-gather.3.cloned.1.call-start = ((), (), s32[]{:S(2)}) async-start(), calls=%async_computation.1 | async-start | bytes 5242880 | tf_op jit(solution)/shard_map/all_gather | solution.py:45
  9.3 2.1 copy-start.4
  10.6 267.7 %all-gather.5.cloned.1.call-start = ((), (), s32[]{:S(2)}) async-start(), calls=%async_computation.2 | async-start | bytes 13107200 | tf_op jit(solution)/shard_map/all_gather | solution.py:63
  11.4 308.3 %reduce-scatter.2.cloned.1.call-start = ((), (), s32[]{:S(2)}) async-start(), calls=%async_computation.3 | async-start | bytes 3276800 | tf_op jit(solution)/shard_map/reduce_scatter | solution.py:66
  103.1 3.8 %copy-start.1 = (f32[8,1024,256]{2,1,0:T(8,128)}, f32[8,1024,256]{2,1,0:T(8,128)S(1)}, u32[]{:S(2)}) copy-start(f32[8,1024,256]{2,1,0:T(8,128)S(1)} %fusion.10) | copy-start | bytes 25165828
  278.3 41.4 %copy-start.2 = (bf16[64,5120]{1,0:T(8,128)(2,1)S(1)}, bf16[64,5120]{1,0:T(8,128)(2,1)}, u32[]{:S(2)}) copy-start(bf16[64,5120]{1,0:T(8,128)(2,1)} %param.12) | copy-start | bytes 1966084
  278.3 41.4 %copy-start.3 = (f32[5120]{0:T(1024)S(1)}, f32[5120]{0:T(1024)}, u32[]{:S(2)}) copy-start(f32[5120]{0:T(1024)} %param.13) | copy-start | bytes 61444
Sparse Core Ops, SparseCore 0:
  10.8 83.4 all-gather.2
  95.8 182.4 all-gather.4
  286.8 32.8 reduce-scatter.1
where the time goes:
time: 329 us; the launch traced here: 328 us
  waiting for transfers between devices  266 us (81%)
  matrix products  18.7 us (6%)
  other arithmetic  14 us (4%)
  between operations  13.2 us (4%)
  blocking collectives  12.6 us (4%)
  local copies, waits for them, and re-layouts  3.77 us (1%)
    all_gather x1, waiting for transfers between devices, body(): lax.all_gather(out_weight, 'patch', axis=1, tiled=True)  162 us
    all_gather x1, waiting for transfers between devices, body(): lax.all_gather(codes_own, 'patch', axis=1, tiled=True)  70 us
    reduce_scatter x1, waiting for transfers between devices, body(): lax.psum_scatter(partial_terms.astype(jnp.bfloat16), ('head', 'sub'), sca...  33 us
    all_gather x1, blocking collectives, body(): lax.all_gather(exps_wire, 'patch', axis=1, tiled=True)  12.6 us
    dot_general x1, matrix products, body(): jnp.einsum('hqk,khd->qhd', weights, value_heads, preferred_element_type=j...  9.06 us
    dot_general x1, matrix products, body(): jnp.dot(attended, lax.all_gather(out_weight, 'patch', axis=1, tiled=True)...  8.34 us
  transfers between devices with their start and end apart: 3, of which 3 were waited for; matrix products, arithmetic and copies ran while one was open for 6% of the time, Pallas kernels for 0%

commit v1 on v0

v1 whole, which is shorter than its diff:
```python
import functools
import math

import jax
import jax.numpy as jnp
from jax import lax
from jax.experimental import pallas as pl
from jax.experimental.pallas import tpu as pltpu
from jax.sharding import PartitionSpec as P

HEAD_DIM = 128
SCALE_ROWS = 128
SATURATION = 448.0
VMEM_BYTES = 48 * 1024 * 1024


def shift_pairs(groups, step):
    pairs = []
    for group in groups:
        count = len(group)
        pairs += [(group[at], group[(at + step) % count]) for at in range(count)]
    return pairs


def pack_kernel(split, where_ref, exps_ref, q_ref, fresh_ref, cached_ref, *outs):
    tok = q_ref.shape[0]
    feat = q_ref.shape[1] // split
    for rel in range(split):
        dest = lax.rem(where_ref[1] + rel, split)
        cols = pl.ds(pl.multiple_of(dest * feat, HEAD_DIM), feat)
        outs[rel][0] = q_ref[:, cols]
        for stacked in range(2):
            for head in range(feat // HEAD_DIM):
                head_at = dest * (feat // HEAD_DIM) + head
                lanes = pl.ds(pl.multiple_of(head_at * HEAD_DIM, HEAD_DIM), HEAD_DIM)
                for block in range(tok // SCALE_ROWS):
                    rows = pl.ds(block * SCALE_ROWS, SCALE_ROWS)
                    power = jnp.full(
                        (1, HEAD_DIM), exps_ref[stacked, block, head_at].astype(jnp.float32)
                    )
                    cached = cached_ref[stacked, rows, lanes].astype(jnp.float32)
                    residual = fresh_ref[stacked, rows, lanes].astype(jnp.float32) - cached
                    codes = jnp.clip(
                        residual * jnp.exp2(-power), -SATURATION, SATURATION
                    ).astype(jnp.bfloat16)
                    decoded = cached + codes.astype(jnp.float32) * jnp.exp2(power)
                    outs[rel][
                        1 + stacked, rows, pl.ds(head * HEAD_DIM, HEAD_DIM)
                    ] = decoded.astype(jnp.bfloat16)


def pack(split, where, exponents, queries, fresh_kv, cached_kv):
    tok, channels = queries.shape
    feat = channels // split
    piece = jax.ShapeDtypeStruct((3, tok, feat), jnp.bfloat16)
    return pl.pallas_call(
        functools.partial(pack_kernel, split),
        out_shape=[piece] * split,
        grid_spec=pltpu.PrefetchScalarGridSpec(
            num_scalar_prefetch=1,
            grid=(1,),
            in_specs=[
                pl.BlockSpec(memory_space=pltpu.SMEM),
                pl.BlockSpec((tok, channels), lambda i, w: (0, 0)),
                pl.BlockSpec((2, tok, channels), lambda i, w: (0, 0, 0)),
                pl.BlockSpec((2, tok, channels), lambda i, w: (0, w[0], 0)),
            ],
            out_specs=[pl.BlockSpec((3, tok, feat), lambda i, w: (0, 0, 0))] * split,
        ),
        compiler_params=pltpu.CompilerParams(vmem_limit_bytes=VMEM_BYTES),
        name="pack",
    )(where, exponents, queries, fresh_kv, cached_kv)


def attend_kernel(split, count, where_ref, *refs):
    out_ref = refs[-1]
    q_refs, kv_refs = refs[:split], refs[split:-1]
    tok = q_refs[0].shape[1]
    feat = q_refs[0].shape[2]
    factor = HEAD_DIM**-0.5 * math.log2(math.e)
    for head in range(feat // HEAD_DIM):
        lanes = pl.ds(head * HEAD_DIM, HEAD_DIM)
        keys = jnp.concatenate([ref[1, :, lanes] for ref in kv_refs], axis=0)
        values = jnp.concatenate([ref[2, :, lanes] for ref in kv_refs], axis=0)
        for rel in range(split):
            scores = lax.dot_general(
                q_refs[rel][0, :, lanes],
                keys,
                (((1,), (1,)), ((), ())),
                preferred_element_type=jnp.float32,
            )
            peak = jnp.max(scores, axis=1, keepdims=True)
            expo = jnp.exp2((scores - peak) * factor)
            total = jnp.sum(expo, axis=1, keepdims=True)
            mix = jnp.dot(
                expo.astype(jnp.bfloat16), values, preferred_element_type=jnp.float32
            )
            source = lax.rem(where_ref[1] + split - rel, split)
            out_ref[source, :, lanes] = (mix / total).astype(jnp.bfloat16)


def attend(where, pieces, kv_pieces):
    split = len(pieces)
    _, tok, feat = pieces[0].shape
    whole = pl.BlockSpec((3, tok, feat), lambda i, w: (0, 0, 0))
    return pl.pallas_call(
        functools.partial(attend_kernel, split, len(kv_pieces)),
        out_shape=jax.ShapeDtypeStruct((split, tok, feat), jnp.bfloat16),
        grid_spec=pltpu.PrefetchScalarGridSpec(
            num_scalar_prefetch=1,
            grid=(1,),
            in_specs=[whole] * (split + len(kv_pieces)),
            out_specs=pl.BlockSpec((split, tok, feat), lambda i, w: (0, 0, 0)),
        ),
        compiler_params=pltpu.CompilerParams(vmem_limit_bytes=VMEM_BYTES),
        name="attend",
    )(where, *pieces, *kv_pieces)


def project_kernel(where_ref, att_ref, weight_ref, *refs):
    outs, acc_ref = refs[:-1], refs[-1]
    n_head, n_sub, rows, cols = acc_ref.shape
    split, _, tok, feat = att_ref.shape
    acc = jnp.dot(att_ref[0, 0], weight_ref[:feat], preferred_element_type=jnp.float32)
    for at in range(1, split):
        acc += jnp.dot(
            att_ref[at, 0],
            weight_ref[at * feat : (at + 1) * feat],
            preferred_element_type=jnp.float32,
        )
    acc_ref[...] = acc.reshape(n_head, n_sub, rows, cols)
    for sub_rel in range(n_sub):
        sub_at = lax.rem(where_ref[3] + sub_rel, n_sub)
        for head_rel in range(n_head):
            head_at = lax.rem(where_ref[2] + head_rel, n_head)
            outs[sub_rel][head_rel, 0] = acc_ref[head_at, sub_at].astype(jnp.bfloat16)


def project(where, gathered, weight, n_head, n_sub):
    n_patch, split, tok, feat = gathered.shape
    cols = weight.shape[1]
    rows = tok // (n_head * n_sub)
    shape = jax.ShapeDtypeStruct((n_head, n_patch, rows, cols), jnp.bfloat16)
    return pl.pallas_call(
        project_kernel,
        out_shape=[shape] * n_sub,
        grid_spec=pltpu.PrefetchScalarGridSpec(
            num_scalar_prefetch=1,
            grid=(n_patch,),
            in_specs=[
                pl.BlockSpec(
                    (split, 1, tok, feat),
                    lambda i, w: (lax.div(i, split), lax.rem(i, split), 0, 0),
                ),
                pl.BlockSpec(weight.shape, lambda i, w: (0, 0)),
            ],
            out_specs=[
                pl.BlockSpec(
                    (n_head, 1, rows, cols),
                    lambda i, w: (0, lax.rem(i + n_patch - w[0], n_patch), 0, 0),
                )
            ]
            * n_sub,
            scratch_shapes=[pltpu.VMEM((n_head, n_sub, rows, cols), jnp.float32)],
        ),
        compiler_params=pltpu.CompilerParams(vmem_limit_bytes=VMEM_BYTES),
        name="project",
    )(where, gathered, weight)


def body(sizes, queries, fresh_kv, cached_kv, exponents, out_weight, hidden_in, attn_gate):
    n_patch, n_head, n_sub = sizes["patch"], sizes["head"], sizes["sub"]
    tok, channels = queries.shape
    split = math.gcd(channels // HEAD_DIM, n_patch)
    patch_at = lax.axis_index("patch")
    where = jnp.stack(
        [patch_at, lax.rem(patch_at, split), lax.axis_index("head"), lax.axis_index("sub")]
    ).astype(jnp.int32)

    sent = pack(split, where, exponents, queries, fresh_kv, cached_kv)
    near = [list(range(at, at + split)) for at in range(0, n_patch, split)]
    pieces = [sent[0]] + [
        lax.ppermute(sent[rel], "patch", shift_pairs(near, rel)) for rel in range(1, split)
    ]
    kv_pieces = list(pieces)
    far = [list(range(at, n_patch, split)) for at in range(split)]
    for rel in range(1, n_patch // split):
        kv_pieces += [lax.ppermute(x, "patch", shift_pairs(far, rel)) for x in pieces]

    attended = attend(where, pieces, kv_pieces)
    gathered = lax.all_gather(attended, "patch", axis=0)

    terms = project(where, gathered, out_weight, n_head, n_sub)
    partial = terms[0].astype(jnp.float32)
    ring = [list(range(n_sub))]
    for rel in range(1, n_sub):
        partial += lax.ppermute(terms[rel], "sub", shift_pairs(ring, rel)).astype(jnp.float32)
    ring = [list(range(n_head))]
    total = partial[0]
    for rel in range(1, n_head):
        arrived = lax.ppermute(partial[rel].astype(jnp.bfloat16), "head", shift_pairs(ring, rel))
        total += arrived.astype(jnp.float32)
    ring = [list(range(n_patch))]
    total = total.astype(jnp.bfloat16)
    blocks = [total[0]] + [
        lax.ppermute(total[rel], "patch", shift_pairs(ring, rel)) for rel in range(1, n_patch)
    ]
    order = jnp.roll(jnp.stack([blocks[-at % n_patch] for at in range(n_patch)]), patch_at, axis=0)
    projected = order.transpose(1, 0, 2).reshape(hidden_in.shape).astype(jnp.float32)
    return (hidden_in.astype(jnp.float32) + attn_gate * projected).astype(jnp.bfloat16)


def solution(mesh):
    in_specs = (
        P(("grp", "patch"), ("head", "sub")),
        P(None, ("grp", "patch"), ("head", "sub")),
        P(None, "grp", ("head", "sub")),
        P(None, ("grp", "patch"), ("head", "sub")),
        P(("head", "sub"), "patch"),
        P(("grp", "patch", "head", "sub"), None),
        P(),
    )
    out_specs = P(("grp", "patch", "head", "sub"), None)
    sizes = dict(mesh.shape)
    return jax.shard_map(
        functools.partial(body, sizes),
        mesh=mesh,
        in_specs=in_specs,
        out_specs=out_specs,
        check_vma=False,
    )
```

time: 329 us -> 156 us (0.47)
  waiting for transfers between devices: 266 us -> 108 us
  matrix products: 18.7 us -> 0 us
  Pallas kernels: 0 us -> 14.5 us
  blocking collectives: 12.6 us -> 0 us
  other arithmetic: 14 us -> 1.61 us
  starting transfers between devices: 0.08 us -> 11.7 us
    all_gather x2 -> x1, waiting for transfers between devices: 232 us -> 53.7 us  [body(): gathered = lax.all_gather(attended, 'patch', axis=0)]
    ppermute x0 -> x8, waiting for transfers between devices: none -> 54.7 us  [the longest x3 24.2 us: body(): lax.ppermute(sent[rel], 'patch', shift_pairs(near, rel))]
    reduce_scatter x1 -> x0, waiting for transfers between devices: 33 us -> none  [body(): lax.psum_scatter(partial_terms.astype(jnp.bfloat16), ('head', 'sub'), sca...]
    dot_general x3 -> x0, matrix products: 18.7 us -> none  [the longest x1 9.06 us: body(): jnp.einsum('hqk,khd->qhd', weights, value_heads, preferred_element_type=j...]
    pallas_call x0 -> x3, Pallas kernels: none -> 14.5 us  [the longest x1 6.57 us: project(): pl.pallas_call(project_kernel, out_shape=[shape] * n_sub, grid_spec=pltpu...]
    all_gather x1 -> x0, blocking collectives: 12.6 us -> none  [body(): lax.all_gather(exps_wire, 'patch', axis=1, tiled=True)]
    ppermute x0 -> x8, starting transfers between devices: none -> 11.7 us  [the longest x3 7.01 us: body(): lax.ppermute(sent[rel], 'patch', shift_pairs(near, rel))]
    convert_element_type x3 -> x1, other arithmetic: 6.94 us -> 0.15 us  [body(): total = total.astype(jnp.bfloat16)]
  transfers between devices with their start and end apart: 3 -> 9, of which waited for: 3 -> 7; matrix products, arithmetic and copies ran while one was open for 6% -> 0% of each run, Pallas kernels for 0% -> 0%
where the time goes in v1:
time: 156 us
  waiting for transfers between devices  108 us (69%)
  Pallas kernels  14.5 us (9%)
  between operations  13.5 us (9%)
  starting transfers between devices  11.7 us (8%)
  local copies, waits for them, and re-layouts  5.81 us (4%)
  other arithmetic  1.61 us (1%)
    all_gather x1, waiting for transfers between devices, body(): gathered = lax.all_gather(attended, 'patch', axis=0)  53.7 us
    ppermute x3, waiting for transfers between devices, body(): lax.ppermute(sent[rel], 'patch', shift_pairs(near, rel))  24.2 us
    ppermute x1, waiting for transfers between devices, body(): lax.ppermute(partial[rel].astype(jnp.bfloat16), 'head', shift_pairs(ring,...  15.3 us
    ppermute x3, waiting for transfers between devices, body(): lax.ppermute(total[rel], 'patch', shift_pairs(ring, rel))  12.2 us
    ppermute x3, starting transfers between devices, body(): lax.ppermute(sent[rel], 'patch', shift_pairs(near, rel))  7.01 us
    pallas_call x1, Pallas kernels, project(): pl.pallas_call(project_kernel, out_shape=[shape] * n_sub, grid_spec=pltpu...  6.57 us
    unnamed x18, local copies, waits for them, and re-layouts  5.58 us
    pallas_call x1, Pallas kernels, attend(): pl.pallas_call(functools.partial(attend_kernel, split, len(kv_pieces)), o...  5.4 us
  transfers between devices with their start and end apart: 9, of which 7 were waited for; matrix products, arithmetic and copies ran while one was open for 0% of the time, Pallas kernels for 0%

profile of v1, /device:TPU:0, one launch (start us, length us, event | category | flops | bytes accessed | tf_op | source)
XLA Modules:
  0.0 155.5 jit_solution(15128412509407182851)
XLA Ops:
  6.5 0.0 all-gather.3.cloned.1.call-start
  6.5 0.1 pad_add_fusion.where_ref
  6.6 0.0 copy-start.1
  6.6 1.2 copy-done.1
  7.8 0.0 copy-start.2
  7.8 1.0 copy-done.2
  8.9 0.0 copy-start.3
  8.9 0.7 copy-done.3
  9.6 2.5 %pack.1 = (bf16[3,256,256]{2,1,0:T(8,128)(2,1)S(1)}, bf16[3,256,256]{2,1,0:T(8,128)(2,1)S(1)}, bf16[3,256,256]{2,1,0:T(8,128)(2,1)S(1)}, bf16[3,256,256]{2,1,0:T(8,128)(2,1)S(1)}) custom-call(s32[4]{0:T(128)S(1)} %pad_add_fusion.where_ref, s32[2,2,8]{2,1,0:T(2,128)S(1)} %copy-done.3, bf16[256,1024]{1,0:T(8,128)(2,1)S(1)} %copy-done.2, ...), custom_call_target="tpu_custom_call" | custom-call | tf_op jit(solution)/shard_map/pack/pallas_call | solution.py:56
  12.1 3.1 %collective-permute-start = (bf16[3,256,256]{2,1,0:T(8,128)(2,1)S(1)}, bf16[3,256,256]{2,1,0:T(8,128)(2,1)S(1)}, u32[]{:S(2)}, u32[]{:S(2)}) collective-permute-start(bf16[3,256,256]{2,1,0:T(8,128)(2,1)S(1)} %get-tuple-element.12), channel_id=1, source_target_pairs={{0,4},{4,8},{8,12},{12,0},{1,5},{5,9},{9,13},{13,1},{2,6},{6,10},{... | collective-permute-start | bytes 1179656 | tf_op jit(solution)/shard_map/ppermute | solution.py:183
  15.1 2.6 %collective-permute-start.1 = (bf16[3,256,256]{2,1,0:T(8,128)(2,1)S(1)}, bf16[3,256,256]{2,1,0:T(8,128)(2,1)S(1)}, u32[]{:S(2)}, u32[]{:S(2)}) collective-permute-start(bf16[3,256,256]{2,1,0:T(8,128)(2,1)S(1)} %get-tuple-element.13), channel_id=1, source_target_pairs={{0,8},{4,12},{8,0},{12,4},{1,9},{5,13},{9,1},{13,5},{2,10},{6,14},... | collective-permute-start | bytes 1179656 | tf_op jit(solution)/shard_map/ppermute | solution.py:183
  17.7 1.3 collective-permute-start.2
  19.1 8.2 %collective-permute-done.refs_1_.refs_5_ = bf16[3,256,256]{2,1,0:T(8,128)(2,1)S(1)} collective-permute-done((bf16[3,256,256]{2,1,0:T(8,128)(2,1)S(1)}, bf16[3,256,256]{2,1,0:T(8,128)(2,1)S(1)}, u32[]{:S(2)}, u32[]{:S(2)}) %collective-permute-start) | collective-permute-done | bytes 393248 | tf_op jit(solution)/shard_map/ppermute | solution.py:183
  27.3 16.0 %collective-permute-done.1.refs_2_.refs_6_ = bf16[3,256,256]{2,1,0:T(8,128)(2,1)S(1)} collective-permute-done((bf16[3,256,256]{2,1,0:T(8,128)(2,1)S(1)}, bf16[3,256,256]{2,1,0:T(8,128)(2,1)S(1)}, u32[]{:S(2)}, u32[]{:S(2)}) %collective-permute-start.1) | collective-permute-done | bytes 393248 | tf_op jit(solution)/shard_map/ppermute | solution.py:183
  43.3 0.0 collective-permute-done.2.refs_3_.refs_7_
  43.3 5.4 %attend.1 = bf16[4,256,256]{2,1,0:T(8,128)(2,1)} custom-call(s32[4]{0:T(128)S(1)} %pad_add_fusion.where_ref, bf16[3,256,256]{2,1,0:T(8,128)(2,1)S(1)} %get-tuple-element.11.refs_0_.refs_4_, bf16[3,256,256]{2,1,0:T(8,128)(2,1)S(1)} %collective-permute-done.refs_1_.refs_5_, bf16[3,256,256]{2,1,0:T(8,128)(2,1)S(1)} %collective-permute-done.1.refs_2_.refs_6_, ...), custom_call_target="tpu_custom_call" | custom-call | tf_op jit(solution)/shard_map/attend/pallas_call | solution.py:106
  48.7 0.0 all-gather.3.cloned.1.call-update
  48.7 53.7 %all-gather.3.cloned.1.call-done = bf16[16,256,256]{2,1,0:T(8,128)(2,1)} async-done(((bf16[4,256,256]{2,1,0:T(8,128)(2,1)}), bf16[16,256,256]{2,1,0:T(8,128)(2,1)}) %all-gather.3.cloned.1.call-update) | async-done | bytes 2097168 | tf_op jit(solution)/shard_map/all_gather | solution.py:191
  102.4 0.0 copy-start
  102.4 1.6 %copy-done = bf16[16,256,256]{2,1,0:T(8,128)(2,1)S(1)} copy-done((bf16[16,256,256]{2,1,0:T(8,128)(2,1)S(1)}, bf16[16,256,256]{2,1,0:T(8,128)(2,1)}, u32[]{:S(2)}) %copy-start) | copy-done | bytes 2097176
  104.0 6.6 %project.1 = (bf16[2,4,64,1280]{3,2,1,0:T(8,128)(2,1)S(1)}, bf16[2,4,64,1280]{3,2,1,0:T(8,128)(2,1)S(1)}) custom-call(s32[4]{0:T(128)S(1)} %pad_add_fusion.where_ref, bf16[4,4,256,256]{3,2,1,0:T(8,128)(2,1)S(1)} %bitcast.32, bf16[1024,1280]{1,0:T(8,128)(2,1)} %weight_ref.1), custom_call_target="tpu_custom_call" | custom-call | tf_op jit(solution)/shard_map/project/pallas_call | solution.py:144
  110.5 0.1 collective-permute-start.3
  110.6 3.0 %collective-permute-done.3 = bf16[2,4,64,1280]{3,2,1,0:T(8,128)(2,1)S(1)} collective-permute-done((bf16[2,4,64,1280]{3,2,1,0:T(8,128)(2,1)S(1)}, bf16[2,4,64,1280]{3,2,1,0:T(8,128)(2,1)S(1)}, u32[]{:S(2)}, u32[]{:S(2)}) %collective-permute-start.3) | collective-permute-done | bytes 1310752 | tf_op jit(solution)/shard_map/ppermute | solution.py:197
  113.6 0.3 convert_add_fusion
  113.9 0.1 fusion.2
  114.0 1.5 collective-permute-start.4
  115.5 15.3 %collective-permute-done.4 = bf16[4,64,1280]{2,1,0:T(8,128)(2,1)S(1)} collective-permute-done((bf16[4,64,1280]{2,1,0:T(8,128)(2,1)S(1)}, bf16[4,64,1280]{2,1,0:T(8,128)(2,1)S(1)}, u32[]{:S(2)}, u32[]{:S(2)}) %collective-permute-start.4) | collective-permute-done | bytes 655392 | tf_op jit(solution)/shard_map/ppermute | solution.py:201
  130.8 0.2 fusion.1
  131.1 1.2 collective-permute-start.5
  132.2 0.9 collective-permute-start.7
  133.1 1.0 collective-permute-start.6
  134.2 6.3 %collective-permute-done.5 = bf16[64,1280]{1,0:T(8,128)(2,1)S(1)} collective-permute-done((bf16[64,1280]{1,0:T(8,128)(2,1)S(1)}, bf16[64,1280]{1,0:T(8,128)(2,1)S(1)}, u32[]{:S(2)}, u32[]{:S(2)}) %collective-permute-start.5) | collective-permute-done | bytes 163872 | tf_op jit(solution)/shard_map/ppermute | solution.py:206
  140.5 5.9 %collective-permute-done.6 = bf16[64,1280]{1,0:T(8,128)(2,1)S(1)} collective-permute-done((bf16[64,1280]{1,0:T(8,128)(2,1)S(1)}, bf16[64,1280]{1,0:T(8,128)(2,1)S(1)}, u32[]{:S(2)}, u32[]{:S(2)}) %collective-permute-start.6) | collective-permute-done | bytes 163872 | tf_op jit(solution)/shard_map/ppermute | solution.py:206
  146.4 0.0 collective-permute-done.7
  146.5 0.1 convert_bitcast_fusion
  146.6 0.0 copy-start.4
  146.6 0.0 copy-start.5
  146.6 0.1 copy.10
  146.8 1.0 copy-done.4
  147.7 0.0 copy-done.5
  147.7 1.0 add_convert_fusion
  (8 shorter events, 0.1 us)
Async XLA Ops:
  6.5 95.8 %all-gather.3.cloned.1.call-start = ((), (), s32[]{:S(2)}) async-start(), calls=%async_computation | async-start | bytes 2621440 | tf_op jit(solution)/shard_map/all_gather | solution.py:191
  6.6 1.2 copy-start.1
  7.8 1.0 copy-start.2
  8.9 0.7 copy-start.3
  12.1 15.2 %collective-permute-start = (bf16[3,256,256]{2,1,0:T(8,128)(2,1)S(1)}, bf16[3,256,256]{2,1,0:T(8,128)(2,1)S(1)}, u32[]{:S(2)}, u32[]{:S(2)}) collective-permute-start(bf16[3,256,256]{2,1,0:T(8,128)(2,1)S(1)} %get-tuple-element.12), channel_id=1, source_target_pairs={{0,4},{4,8},{8,12},{12,0},{1,5},{5,9},{9,13},{13,1},{2,6},{6,10},{... | collective-permute-start | bytes 1179656 | tf_op jit(solution)/shard_map/ppermute | solution.py:183
  15.1 28.1 %collective-permute-start.1 = (bf16[3,256,256]{2,1,0:T(8,128)(2,1)S(1)}, bf16[3,256,256]{2,1,0:T(8,128)(2,1)S(1)}, u32[]{:S(2)}, u32[]{:S(2)}) collective-permute-start(bf16[3,256,256]{2,1,0:T(8,128)(2,1)S(1)} %get-tuple-element.13), channel_id=1, source_target_pairs={{0,8},{4,12},{8,0},{12,4},{1,9},{5,13},{9,1},{13,5},{2,10},{6,14},... | collective-permute-start | bytes 1179656 | tf_op jit(solution)/shard_map/ppermute | solution.py:183
  17.7 25.5 %collective-permute-start.2 = (bf16[3,256,256]{2,1,0:T(8,128)(2,1)S(1)}, bf16[3,256,256]{2,1,0:T(8,128)(2,1)S(1)}, u32[]{:S(2)}, u32[]{:S(2)}) collective-permute-start(bf16[3,256,256]{2,1,0:T(8,128)(2,1)S(1)} %get-tuple-element.14), channel_id=1, source_target_pairs={{0,12},{4,0},{8,4},{12,8},{1,13},{5,1},{9,5},{13,9},{2,14},{6,2},{... | collective-permute-start | bytes 1179656 | tf_op jit(solution)/shard_map/ppermute | solution.py:183
  102.4 1.6 %copy-start = (bf16[16,256,256]{2,1,0:T(8,128)(2,1)S(1)}, bf16[16,256,256]{2,1,0:T(8,128)(2,1)}, u32[]{:S(2)}) copy-start(bf16[16,256,256]{2,1,0:T(8,128)(2,1)} %all-gather.3.cloned.1.call-done) | copy-start | bytes 6291460
  110.5 3.1 %collective-permute-start.3 = (bf16[2,4,64,1280]{3,2,1,0:T(8,128)(2,1)S(1)}, bf16[2,4,64,1280]{3,2,1,0:T(8,128)(2,1)S(1)}, u32[]{:S(2)}, u32[]{:S(2)}) collective-permute-start(bf16[2,4,64,1280]{3,2,1,0:T(8,128)(2,1)S(1)} %get-tuple-element.16), channel_id=1, source_target_pairs={{0,1},{1,0},{2,3},{3,2},{4,5},{5,4},{6,7},{7,6},{8,9},{9,8},{10,11... | collective-permute-start | bytes 3932168 | tf_op jit(solution)/shard_map/ppermute | solution.py:197
  114.0 16.8 %collective-permute-start.4 = (bf16[4,64,1280]{2,1,0:T(8,128)(2,1)S(1)}, bf16[4,64,1280]{2,1,0:T(8,128)(2,1)S(1)}, u32[]{:S(2)}, u32[]{:S(2)}) collective-permute-start(bf16[4,64,1280]{2,1,0:T(8,128)(2,1)S(1)} %fusion.2), channel_id=1, source_target_pairs={{0,2},{2,0},{1,3},{3,1},{4,6},{6,4},{5,7},{7,5},{8,10},{10,8},{9,1... | collective-permute-start | bytes 1966088 | tf_op jit(solution)/shard_map/ppermute | solution.py:201
  131.1 9.4 %collective-permute-start.5 = (bf16[64,1280]{1,0:T(8,128)(2,1)S(1)}, bf16[64,1280]{1,0:T(8,128)(2,1)S(1)}, u32[]{:S(2)}, u32[]{:S(2)}) collective-permute-start(bf16[64,1280]{1,0:T(8,128)(2,1)S(1)} %get-tuple-element.20), channel_id=1, source_target_pairs={{0,12},{4,0},{8,4},{12,8},{1,13},{5,1},{9,5},{13,9},{2,14},{6,2},{... | collective-permute-start | bytes 491528 | tf_op jit(solution)/shard_map/ppermute | solution.py:206
  132.2 14.1 %collective-permute-start.7 = (bf16[64,1280]{1,0:T(8,128)(2,1)S(1)}, bf16[64,1280]{1,0:T(8,128)(2,1)S(1)}, u32[]{:S(2)}, u32[]{:S(2)}) collective-permute-start(bf16[64,1280]{1,0:T(8,128)(2,1)S(1)} %get-tuple-element.17), channel_id=1, source_target_pairs={{0,4},{4,8},{8,12},{12,0},{1,5},{5,9},{9,13},{13,1},{2,6},{6,10},{... | collective-permute-start | bytes 491528 | tf_op jit(solution)/shard_map/ppermute | solution.py:206
  133.1 13.2 %collective-permute-start.6 = (bf16[64,1280]{1,0:T(8,128)(2,1)S(1)}, bf16[64,1280]{1,0:T(8,128)(2,1)S(1)}, u32[]{:S(2)}, u32[]{:S(2)}) collective-permute-start(bf16[64,1280]{1,0:T(8,128)(2,1)S(1)} %get-tuple-element.19), channel_id=1, source_target_pairs={{0,8},{4,12},{8,0},{12,4},{1,9},{5,13},{9,1},{13,5},{2,10},{6,14},... | collective-permute-start | bytes 491528 | tf_op jit(solution)/shard_map/ppermute | solution.py:206
  146.6 1.1 copy-start.4
  146.6 1.1 copy-start.5
Sparse Core Ops, SparseCore 0:
  48.8 53.4 all-gather.2

commit v2 on v0

v2 whole, which is shorter than its diff:
```python
import functools
import math

import jax
import jax.numpy as jnp
from jax import lax
from jax.experimental import pallas as pl
from jax.experimental.pallas import tpu as pltpu
from jax.sharding import PartitionSpec as P

HEAD_DIM = 128
SCALE_ROWS = 128
SATURATION = 448.0
VMEM_BYTES = 60 * 1024 * 1024


def spec(shape):
    return pl.BlockSpec(shape, lambda i, w: (0,) * len(shape))


def call(kernel, name, out_shape, grid, in_specs, out_specs, scratch=(), cost=None):
    return pl.pallas_call(
        kernel,
        out_shape=out_shape,
        grid_spec=pltpu.PrefetchScalarGridSpec(
            num_scalar_prefetch=1,
            grid=(grid,),
            in_specs=in_specs,
            out_specs=out_specs,
            scratch_shapes=list(scratch),
        ),
        compiler_params=pltpu.CompilerParams(vmem_limit_bytes=VMEM_BYTES),
        cost_estimate=cost,
        name=name,
    )


def swap(x, axes, count, mask, only=None):
    pairs = [(at, at ^ mask) for at in range(count) if only is None or at in only]
    return lax.ppermute(x, axes, pairs)


def pack_kernel(split, per, chunk, where_ref, exps_ref, q_ref, fresh_ref, cached_ref, *outs):
    step = pl.program_id(0)
    tok = q_ref.shape[0]
    head_at = (where_ref[1] ^ step) * per + chunk
    for rel in range(split):

        @pl.when(step == rel)
        def fill(out=outs[rel]):
            out[0] = q_ref[...]
            for stacked in range(2):
                for block in range(tok // SCALE_ROWS):
                    rows = pl.ds(block * SCALE_ROWS, SCALE_ROWS)
                    power = jnp.full(
                        (1, HEAD_DIM), exps_ref[stacked, block, head_at].astype(jnp.float32)
                    )
                    cached = cached_ref[stacked, rows].astype(jnp.float32)
                    residual = fresh_ref[stacked, rows].astype(jnp.float32) - cached
                    codes = jnp.clip(
                        residual * jnp.exp2(-power), -SATURATION, SATURATION
                    ).astype(jnp.bfloat16)
                    decoded = cached + codes.astype(jnp.float32) * jnp.exp2(power)
                    out[1 + stacked, rows] = decoded.astype(jnp.bfloat16)


def pack(split, per, chunk, where, exponents, queries, fresh_kv, cached_kv):
    tok = queries.shape[0]
    piece = jax.ShapeDtypeStruct((3, tok, HEAD_DIM), jnp.bfloat16)

    def column(i, w):
        return (w[1] ^ i) * per + chunk

    return call(
        functools.partial(pack_kernel, split, per, chunk),
        "pack",
        [piece] * split,
        split,
        [
            pl.BlockSpec(memory_space=pltpu.SMEM),
            pl.BlockSpec((tok, HEAD_DIM), lambda i, w: (0, column(i, w))),
            pl.BlockSpec((2, tok, HEAD_DIM), lambda i, w: (0, 0, column(i, w))),
            pl.BlockSpec((2, tok, HEAD_DIM), lambda i, w: (0, w[0], column(i, w))),
        ],
        [spec(piece.shape)] * split,
    )(where, exponents, queries, fresh_kv, cached_kv)


def attend_kernel(split, n_kv, where_ref, *refs):
    q_refs, kv_refs = refs[:split], refs[split : split + n_kv]
    outs, mix_ref = refs[split + n_kv : -1], refs[-1]
    tok = q_refs[0].shape[1]
    factor = HEAD_DIM**-0.5 * math.log2(math.e)
    keys = jnp.concatenate([ref[1] for ref in kv_refs], axis=0)
    values = jnp.concatenate([ref[2] for ref in kv_refs], axis=0)
    values = jnp.concatenate([values, jnp.ones_like(values)], axis=1)
    for rel in range(split):
        scores = lax.dot_general(
            q_refs[rel][0], keys, (((1,), (1,)), ((), ())), preferred_element_type=jnp.float32
        )
        peak = jnp.max(scores, axis=1, keepdims=True)
        expo = jnp.exp2((scores - peak) * factor).astype(jnp.bfloat16)
        mix = jnp.dot(expo, values, preferred_element_type=jnp.float32)
        mix = mix[:, :HEAD_DIM] / mix[:, HEAD_DIM:]
        mix_ref[...] = mix.reshape(mix_ref.shape)
        for at, out in enumerate(outs):
            out[where_ref[1] ^ rel] = mix_ref[where_ref[2] ^ at].astype(jnp.bfloat16)


def attend(where, n_rel, pieces, kv_pieces):
    split = len(pieces)
    _, tok, feat = pieces[0].shape
    rows = tok // n_rel
    out = jax.ShapeDtypeStruct((split, rows, feat), jnp.bfloat16)
    return call(
        functools.partial(attend_kernel, split, len(kv_pieces)),
        "attend",
        [out] * n_rel,
        1,
        [spec(pieces[0].shape)] * (split + len(kv_pieces)),
        [spec(out.shape)] * n_rel,
        [pltpu.VMEM((n_rel, rows, feat), jnp.float32)],
    )(where, *pieces, *kv_pieces)


def project_kernel(plan, n_slots, n_weights, with_acc, last, where_ref, *refs):
    slots, refs = refs[:n_slots], refs[n_slots:]
    weights, refs = refs[:n_weights], refs[n_weights:]
    acc_in, refs = (refs[0], refs[1:]) if with_acc else (None, refs)
    if last:
        outs, held_ref, acc_ref = refs[:-2], refs[-2], refs[-1]
    else:
        outs, held_ref = refs[:-1], refs[-1]
    split = held_ref.shape[0]

    @pl.when(pl.program_id(0) == 0)
    def arrange():
        rows = slots[0].shape[0]
        for at, slot in enumerate(slots):
            group, near = divmod(at, split)
            held_ref[where_ref[1] ^ near, group * rows : (group + 1) * rows] = slot[...]

    acc = acc_in[...] if with_acc else None
    for head, lanes, parts in plan:
        place = head(where_ref) if callable(head) else head
        weight = [weights[index][part, 0] if part is not None else weights[index][0] for index, part in parts]
        weight = jnp.concatenate(weight, axis=0) if len(weight) > 1 else weight[0]
        term = jnp.dot(
            held_ref[place, :, lanes * HEAD_DIM : (lanes + len(parts)) * HEAD_DIM],
            weight,
            preferred_element_type=jnp.float32,
        )
        acc = term if acc is None else acc + term
    if not last:
        outs[0][...] = acc
    else:
        acc_ref[...] = acc.reshape(acc_ref.shape)
        for at, out in enumerate(outs):
            group, near = divmod(at, split)
            out[...] = acc_ref[group, where_ref[1] ^ near].astype(jnp.bfloat16)


def project(plan, split, chunk, where, slots, weights, acc, last):
    rows, lanes = slots[0].shape
    total = rows * len(slots) // split
    cols = weights[0].shape[-1]
    wide = 256 if cols % 256 == 0 else cols
    specs = [spec(slots[0].shape)] * len(slots)
    for weight in weights:
        if weight.ndim == 4:
            specs.append(
                pl.BlockSpec((weight.shape[0], 1, HEAD_DIM, wide), lambda i, w: (0, chunk, 0, i))
            )
        else:
            specs.append(pl.BlockSpec((1, HEAD_DIM, wide), lambda i, w: (chunk, 0, i)))
    whole = pl.BlockSpec((total, wide), lambda i, w: (0, i))
    if acc is not None:
        specs.append(whole)
    scratch = [pltpu.VMEM((split, total, lanes), jnp.bfloat16)]
    if last:
        piece = rows // split
        out_shape = [jax.ShapeDtypeStruct((piece, cols), jnp.bfloat16)] * len(slots)
        out_specs = [pl.BlockSpec((piece, wide), lambda i, w: (0, i))] * len(slots)
        scratch.append(pltpu.VMEM((len(slots) // split, split, piece, wide), jnp.float32))
    else:
        out_shape = [jax.ShapeDtypeStruct((total, cols), jnp.float32)]
        out_specs = [whole]
    kernel = functools.partial(
        project_kernel, plan, len(slots), len(weights), acc is not None, last
    )
    operands = [*slots, *weights] + ([] if acc is None else [acc])
    return call(kernel, "project", out_shape, cols // wide, specs, out_specs, scratch)(
        where, *operands
    )


def mix_kernel(n_patch, where_ref, hidden_ref, gate_ref, *refs):
    out_ref = refs[-1]
    cols = refs[0].shape[1]
    for rel in range(n_patch):
        lanes = pl.ds(pl.multiple_of((where_ref[0] ^ rel) * cols, HEAD_DIM), cols)
        mixed = hidden_ref[:, lanes].astype(jnp.float32) + gate_ref[:, lanes] * refs[rel][
            ...
        ].astype(jnp.float32)
        out_ref[:, lanes] = mixed.astype(jnp.bfloat16)


def mix(where, hidden_in, attn_gate, blocks):
    rows, width = hidden_in.shape
    n_patch = len(blocks)
    if blocks[0].shape[1] % HEAD_DIM:
        order = jnp.stack(blocks)[where[0] ^ jnp.arange(n_patch)]
        projected = order.transpose(1, 0, 2).reshape(rows, width).astype(jnp.float32)
        return (hidden_in.astype(jnp.float32) + attn_gate * projected).astype(jnp.bfloat16)
    return call(
        functools.partial(mix_kernel, n_patch),
        "mix",
        jax.ShapeDtypeStruct((rows, width), jnp.bfloat16),
        1,
        [spec((rows, width)), spec((1, width))] + [spec(blocks[0].shape)] * n_patch,
        spec((rows, width)),
    )(where, hidden_in, attn_gate[None], *blocks)


def share_weight(sizes, split, per, out_weight, where):
    n_head, n_sub = sizes["head"], sizes["sub"]
    n_rel = n_head * n_sub
    cols = out_weight.shape[1]
    own = out_weight.reshape(split, per, HEAD_DIM, cols)
    if (n_head, n_sub, sizes["grp"], split) != (2, 2, 2, 4):
        weights = [own] + [swap(own, ("head", "sub"), n_rel, rel) for rel in range(1, n_rel)]
        plan = []
        for at in range(split):
            for rel in range(0, n_rel, 2):
                plan.append((at, rel, [(rel, at), (rel + 1, at)]))
        return weights, plan
    across = []
    for half in range(2):
        mine = lax.dynamic_index_in_dim(own, 2 * where[3] + half, 0, keepdims=False)
        across.append(swap(mine, "head", 2, 1))
    passed = [swap(x, "grp", 2, 1) for x in across]
    weights = [own, swap(own, "sub", 2, 1)]
    for x in across + passed:
        weights += [x, swap(x, "sub", 2, 1)]
    plan = [(at, 0, [(0, at), (1, at)]) for at in range(4)]
    for flip in range(2):
        for half in range(2):
            index = 2 + 2 * (2 * flip + half)

            def head(where_ref, flip=flip, half=half):
                return 2 * (where_ref[3] ^ flip) + half

            plan.append((head, 2, [(index, None), (index + 1, None)]))
    return weights, plan


def gather(x, where, n_patch):
    if n_patch != 4:
        return [x] + [swap(x, "patch", n_patch, rel) for rel in range(1, n_patch)]
    far = swap(x, "patch", 4, 2)
    next_to = swap(x, "patch", 4, 1)
    middle = swap(x, "patch", 4, 3, (1, 2))
    ends = lax.ppermute(far, "patch", [(1, 0), (2, 3)])
    inner = (where[0] == 1) | (where[0] == 2)
    return [x, next_to, far, jnp.where(inner, middle, ends)]


def body(sizes, queries, fresh_kv, cached_kv, exponents, out_weight, hidden_in, attn_gate):
    n_patch, n_rel = sizes["patch"], sizes["head"] * sizes["sub"]
    heads = queries.shape[1] // HEAD_DIM
    split = math.gcd(heads, n_patch)
    per = heads // split
    patch_at = lax.axis_index("patch")
    where = jnp.stack(
        [
            patch_at,
            patch_at % split,
            lax.axis_index("head") * sizes["sub"] + lax.axis_index("sub"),
            lax.axis_index("grp"),
        ]
    ).astype(jnp.int32)

    arrived = []
    for chunk in range(per):
        sent = pack(split, per, chunk, where, exponents, queries, fresh_kv, cached_kv)
        pieces = [sent[0]] + [
            swap(sent[rel], "patch", n_patch, rel) for rel in range(1, split)
        ]
        arrived.append(pieces)
    weights, plan = share_weight(sizes, split, per, out_weight, where)

    slots = []
    for pieces in arrived:
        kv_pieces = list(pieces)
        for rel in range(split, n_patch, split):
            kv_pieces += [swap(x, "patch", n_patch, rel) for x in pieces]
        out = attend(where, n_rel, pieces, kv_pieces)
        out = [out[0]] + [swap(out[rel], ("head", "sub"), n_rel, rel) for rel in range(1, n_rel)]
        flat = [x.reshape(-1, HEAD_DIM) for x in out]
        slots.append(gather(jnp.concatenate(flat, axis=1), where, n_patch))

    acc = None
    for chunk in range(per):
        acc = project(plan, split, chunk, where, slots[chunk], weights, acc, chunk == per - 1)
        if chunk < per - 1:
            acc = acc[0]
    blocks = [acc[0]] + [swap(acc[rel], "patch", n_patch, rel) for rel in range(1, n_patch)]
    return mix(where, hidden_in, attn_gate, blocks)


def solution(mesh):
    in_specs = (
        P(("grp", "patch"), ("head", "sub")),
        P(None, ("grp", "patch"), ("head", "sub")),
        P(None, "grp", ("head", "sub")),
        P(None, ("grp", "patch"), ("head", "sub")),
        P(("head", "sub"), "patch"),
        P(("grp", "patch", "head", "sub"), None),
        P(),
    )
    out_specs = P(("grp", "patch", "head", "sub"), None)
    return jax.shard_map(
        functools.partial(body, dict(mesh.shape)),
        mesh=mesh,
        in_specs=in_specs,
        out_specs=out_specs,
        check_vma=False,
    )
```

time: 329 us -> 159 us (0.48)
  waiting for transfers between devices: 266 us -> 74.4 us
  starting transfers between devices: 0.08 us -> 39.8 us
  Pallas kernels: 0 us -> 34.5 us
  matrix products: 18.7 us -> 0 us
  between operations: 13.2 us -> 0.28 us
  blocking collectives: 12.6 us -> 0 us
  other arithmetic: 14 us -> 4.91 us
    all_gather x2 -> x0, waiting for transfers between devices: 232 us -> none  [the longest x1 162 us: body(): lax.all_gather(out_weight, 'patch', axis=1, tiled=True)]
    ppermute x0 -> x32, waiting for transfers between devices: none -> 74.4 us  [the longest x30 60.4 us: swap(): return lax.ppermute(x, axes, pairs)]
    ppermute x0 -> x32, starting transfers between devices: none -> 39.8 us  [the longest x30 37.2 us: swap(): return lax.ppermute(x, axes, pairs)]
    pallas_call x0 -> x7, Pallas kernels: none -> 34.5 us  [the longest x2 14.1 us: project(): call(kernel, 'project', out_shape, cols // wide, specs, out_specs, scratch)]
    reduce_scatter x1 -> x0, waiting for transfers between devices: 33 us -> none  [body(): lax.psum_scatter(partial_terms.astype(jnp.bfloat16), ('head', 'sub'), sca...]
    dot_general x3 -> x0, matrix products: 18.7 us -> none  [the longest x1 9.06 us: body(): jnp.einsum('hqk,khd->qhd', weights, value_heads, preferred_element_type=j...]
    all_gather x1 -> x0, blocking collectives: 12.6 us -> none  [body(): lax.all_gather(exps_wire, 'patch', axis=1, tiled=True)]
    convert_element_type x4 -> x0, other arithmetic: 9.06 us -> none  [the longest x1 5.65 us: decode(): (cached_blocks + codes_blocks.astype(jnp.float32) * scale_up).astype(jnp....]
  transfers between devices with their start and end apart: 3 -> 32, of which waited for: 3 -> 14; matrix products, arithmetic and copies ran while one was open for 6% -> 4% of each run, Pallas kernels for 0% -> 15%
where the time goes in v2:
time: 159 us; the launch traced here: 158 us
  waiting for transfers between devices  74.4 us (47%)
  starting transfers between devices  39.8 us (25%)
  Pallas kernels  34.5 us (22%)
  other arithmetic  4.91 us (3%)
  local copies, waits for them, and re-layouts  4.09 us (3%)
    ppermute x30, waiting for transfers between devices, swap(): return lax.ppermute(x, axes, pairs)  60.4 us
    ppermute x30, starting transfers between devices, swap(): return lax.ppermute(x, axes, pairs)  37.2 us
    pallas_call x2, Pallas kernels, project(): call(kernel, 'project', out_shape, cols // wide, specs, out_specs, scratch)  14.1 us
    ppermute x2, waiting for transfers between devices, gather(): ends = lax.ppermute(far, 'patch', [(1, 0), (2, 3)])  14.1 us
    pallas_call x2, Pallas kernels, attend(): call(functools.partial(attend_kernel, split, len(kv_pieces)), 'attend', [...  9.02 us
    pallas_call x2, Pallas kernels, pack(): call(functools.partial(pack_kernel, split, per, chunk), 'pack', [piece] *...  8.31 us
    select_n x2, other arithmetic, gather(): return [x, next_to, far, jnp.where(inner, middle, ends)]  3.37 us
  transfers between devices with their start and end apart: 32, of which 14 were waited for; matrix products, arithmetic and copies ran while one was open for 4% of the time, Pallas kernels for 15%

profile of v2, /device:TPU:0, one launch (start us, length us, event | category | flops | bytes accessed | tf_op | source)
XLA Modules:
  0.0 158.0 jit_solution(11650662073847290745)
XLA Ops:
  0.5 0.6 pad_add_fusion.where_ref
  1.1 4.1 %pack.3 = (bf16[3,256,128]{2,1,0:T(8,128)(2,1)}, bf16[3,256,128]{2,1,0:T(8,128)(2,1)}, bf16[3,256,128]{2,1,0:T(8,128)(2,1)}, bf16[3,256,128]{2,1,0:T(8,128)(2,1)}) custom-call(s32[4]{0:T(128)} %pad_add_fusion.where_ref, s32[2,2,8]{2,1,0:T(2,128)} %exps_ref.3, bf16[256,1024]{1,0:T(8,128)(2,1)} %q_ref.3, bf16[2,256,1024]{2,1,0:T(8,128)(2,1)} %fresh_ref.3, ...), custom_call_target="tpu_custom_call" | custom-call | tf_op jit(solution)/shard_map/pack/pallas_call | solution.py:74
  5.2 2.6 %collective-permute-start.19 = (bf16[3,256,128]{2,1,0:T(8,128)(2,1)}, bf16[3,256,128]{2,1,0:T(8,128)(2,1)S(1)}, u32[]{:S(2)}, u32[]{:S(2)}) collective-permute-start(bf16[3,256,128]{2,1,0:T(8,128)(2,1)} %get-tuple-element.34), channel_id=1, source_target_pairs={{0,4},{4,0},{8,12},{12,8},{1,5},{5,1},{9,13},{13,9},{2,6},{6,2},{1... | collective-permute-start | bytes 589832 | tf_op jit(solution)/shard_map/ppermute | solution.py:40
  7.8 2.6 %collective-permute-start.20 = (bf16[3,256,128]{2,1,0:T(8,128)(2,1)}, bf16[3,256,128]{2,1,0:T(8,128)(2,1)S(1)}, u32[]{:S(2)}, u32[]{:S(2)}) collective-permute-start(bf16[3,256,128]{2,1,0:T(8,128)(2,1)} %get-tuple-element.35), channel_id=1, source_target_pairs={{0,8},{4,12},{8,0},{12,4},{1,9},{5,13},{9,1},{13,5},{2,10},{6,14},... | collective-permute-start | bytes 589832 | tf_op jit(solution)/shard_map/ppermute | solution.py:40
  10.4 4.2 %pack.2 = (bf16[3,256,128]{2,1,0:T(8,128)(2,1)}, bf16[3,256,128]{2,1,0:T(8,128)(2,1)}, bf16[3,256,128]{2,1,0:T(8,128)(2,1)}, bf16[3,256,128]{2,1,0:T(8,128)(2,1)}) custom-call(s32[4]{0:T(128)} %pad_add_fusion.where_ref, s32[2,2,8]{2,1,0:T(2,128)} %exps_ref.3, bf16[256,1024]{1,0:T(8,128)(2,1)} %q_ref.3, bf16[2,256,1024]{2,1,0:T(8,128)(2,1)} %fresh_ref.3, ...), custom_call_target="tpu_custom_call" | custom-call | tf_op jit(solution)/shard_map/pack/pallas_call | solution.py:74
  14.6 0.9 collective-permute-start
  15.5 1.9 %collective-permute-done.19.refs_1_.refs_5_ = bf16[3,256,128]{2,1,0:T(8,128)(2,1)S(1)} collective-permute-done((bf16[3,256,128]{2,1,0:T(8,128)(2,1)}, bf16[3,256,128]{2,1,0:T(8,128)(2,1)S(1)}, u32[]{:S(2)}, u32[]{:S(2)}) %collective-permute-start.19) | collective-permute-done | bytes 196640 | tf_op jit(solution)/shard_map/ppermute | solution.py:40
  17.4 7.8 %collective-permute-done.20.refs_2_.refs_6_ = bf16[3,256,128]{2,1,0:T(8,128)(2,1)S(1)} collective-permute-done((bf16[3,256,128]{2,1,0:T(8,128)(2,1)}, bf16[3,256,128]{2,1,0:T(8,128)(2,1)S(1)}, u32[]{:S(2)}, u32[]{:S(2)}) %collective-permute-start.20) | collective-permute-done | bytes 196640 | tf_op jit(solution)/shard_map/ppermute | solution.py:40
  25.1 0.7 copy-done.12
  25.9 4.5 %attend.3 = (bf16[4,64,128]{2,1,0:T(8,128)(2,1)}, bf16[4,64,128]{2,1,0:T(8,128)(2,1)}, bf16[4,64,128]{2,1,0:T(8,128)(2,1)}, bf16[4,64,128]{2,1,0:T(8,128)(2,1)}) custom-call(s32[4]{0:T(128)} %pad_add_fusion.where_ref, bf16[3,256,128]{2,1,0:T(8,128)(2,1)} %get-tuple-element.33.refs_0_.refs_4_, bf16[3,256,128]{2,1,0:T(8,128)(2,1)} %copy-done.11, ...), custom_call_target="tpu_custom_call" | custom-call | tf_op jit(solution)/shard_map/attend/pallas_call | solution.py:115
  30.4 5.1 %collective-permute-start.1 = (bf16[3,256,128]{2,1,0:T(8,128)(2,1)}, bf16[3,256,128]{2,1,0:T(8,128)(2,1)S(1)}, u32[]{:S(2)}, u32[]{:S(2)}) collective-permute-start(bf16[3,256,128]{2,1,0:T(8,128)(2,1)} %get-tuple-element.27), channel_id=1, source_target_pairs={{0,8},{4,12},{8,0},{12,4},{1,9},{5,13},{9,1},{13,5},{2,10},{6,14},... | collective-permute-start | bytes 589832 | tf_op jit(solution)/shard_map/ppermute | solution.py:40
  35.5 1.3 collective-permute-start.2
  36.9 1.5 collective-permute-start.23
  38.4 1.2 dynamic-slice_bitcast_fusion
  39.6 1.8 %collective-permute-done.23 = bf16[4,64,128]{2,1,0:T(8,128)(2,1)S(1)} collective-permute-done((bf16[4,64,128]{2,1,0:T(8,128)(2,1)}, bf16[4,64,128]{2,1,0:T(8,128)(2,1)S(1)}, u32[]{:S(2)}, u32[]{:S(2)}) %collective-permute-start.23) | collective-permute-done | bytes 65568 | tf_op jit(solution)/shard_map/ppermute | solution.py:40
  41.4 2.2 %collective-permute-start.11 = (bf16[2,128,1280]{2,1,0:T(8,128)(2,1)}, bf16[2,128,1280]{2,1,0:T(8,128)(2,1)S(1)}, u32[]{:S(2)}, u32[]{:S(2)}) collective-permute-start(bf16[2,128,1280]{2,1,0:T(8,128)(2,1)} %get-tuple-element.46), channel_id=1, source_target_pairs={{0,2},{2,0},{1,3},{3,1},{4,6},{6,4},{5,7},{7,5},{8,10},{10,8},{9,1... | collective-permute-start | bytes 1966088 | tf_op jit(solution)/shard_map/ppermute | solution.py:40
  43.6 6.3 %collective-permute-done.1.refs_2_.refs_6_ = bf16[3,256,128]{2,1,0:T(8,128)(2,1)S(1)} collective-permute-done((bf16[3,256,128]{2,1,0:T(8,128)(2,1)}, bf16[3,256,128]{2,1,0:T(8,128)(2,1)S(1)}, u32[]{:S(2)}, u32[]{:S(2)}) %collective-permute-start.1) | collective-permute-done | bytes 196640 | tf_op jit(solution)/shard_map/ppermute | solution.py:40
  49.9 0.7 copy-done.9
  50.7 4.5 %attend.2 = (bf16[4,64,128]{2,1,0:T(8,128)(2,1)}, bf16[4,64,128]{2,1,0:T(8,128)(2,1)}, bf16[4,64,128]{2,1,0:T(8,128)(2,1)}, bf16[4,64,128]{2,1,0:T(8,128)(2,1)}) custom-call(s32[4]{0:T(128)} %pad_add_fusion.where_ref, bf16[3,256,128]{2,1,0:T(8,128)(2,1)} %get-tuple-element.25.refs_0_.refs_4_, bf16[3,256,128]{2,1,0:T(8,128)(2,1)} %copy-done.8, ...), custom_call_target="tpu_custom_call" | custom-call | tf_op jit(solution)/shard_map/attend/pallas_call | solution.py:115
  55.2 1.5 collective-permute-done.3
  56.6 1.5 collective-permute-start.4
  58.1 14.6 %collective-permute-done.4 = bf16[4,64,128]{2,1,0:T(8,128)(2,1)S(1)} collective-permute-done((bf16[4,64,128]{2,1,0:T(8,128)(2,1)}, bf16[4,64,128]{2,1,0:T(8,128)(2,1)S(1)}, u32[]{:S(2)}, u32[]{:S(2)}) %collective-permute-start.4) | collective-permute-done | bytes 65568 | tf_op jit(solution)/shard_map/ppermute | solution.py:40
  72.7 4.5 %collective-permute-done.5 = bf16[4,64,128]{2,1,0:T(8,128)(2,1)S(1)} collective-permute-done((bf16[4,64,128]{2,1,0:T(8,128)(2,1)}, bf16[4,64,128]{2,1,0:T(8,128)(2,1)S(1)}, u32[]{:S(2)}, u32[]{:S(2)}) %collective-permute-start.5) | collective-permute-done | bytes 65568 | tf_op jit(solution)/shard_map/ppermute | solution.py:40
  77.2 1.4 collective-permute-start.27
  79.0 0.9 pad_maximum_fusion.refs_0_
  79.9 6.9 %collective-permute-start.7 = (bf16[256,512]{1,0:T(8,128)(2,1)S(1)}, bf16[256,512]{1,0:T(8,128)(2,1)S(1)}, u32[]{:S(2)}, u32[]{:S(2)}) collective-permute-start(bf16[256,512]{1,0:T(8,128)(2,1)S(1)} %pad_maximum_fusion.refs_0_), channel_id=1, source_target_pairs={{0,8},{4,12},{8,0},{12,4},{1,9},{5,13},{9,1},{13,5},{2,10},{6,14},... | collective-permute-start | bytes 786440 | tf_op jit(solution)/shard_map/ppermute | solution.py:40
  86.9 1.4 collective-permute-start.8
  88.3 1.5 collective-permute-start.15
  89.8 0.5 collective-permute-start.17
  90.3 9.3 %collective-permute-done.7.refs_2_ = bf16[256,512]{1,0:T(8,128)(2,1)S(1)} collective-permute-done((bf16[256,512]{1,0:T(8,128)(2,1)S(1)}, bf16[256,512]{1,0:T(8,128)(2,1)S(1)}, u32[]{:S(2)}, u32[]{:S(2)}) %collective-permute-start.7) | collective-permute-done | bytes 262176 | tf_op jit(solution)/shard_map/ppermute | solution.py:40
  99.6 1.3 collective-permute-start.28
  101.0 7.0 %collective-permute-done.28 = bf16[256,512]{1,0:T(8,128)(2,1)} collective-permute-done((bf16[256,512]{1,0:T(8,128)(2,1)S(1)}, bf16[256,512]{1,0:T(8,128)(2,1)}, u32[]{:S(2)}, u32[]{:S(2)}) %collective-permute-start.28) | collective-permute-done | bytes 262176 | tf_op jit(solution)/shard_map/ppermute | solution.py:263
  108.0 1.3 collective-permute-start.9
  109.2 7.1 %collective-permute-done.9 = bf16[256,512]{1,0:T(8,128)(2,1)} collective-permute-done((bf16[256,512]{1,0:T(8,128)(2,1)S(1)}, bf16[256,512]{1,0:T(8,128)(2,1)}, u32[]{:S(2)}, u32[]{:S(2)}) %collective-permute-start.9) | collective-permute-done | bytes 262176 | tf_op jit(solution)/shard_map/ppermute | solution.py:263
  116.3 0.5 collective-permute-start.16
  116.8 1.4 collective-permute-done.17.refs_12_
  118.4 2.0 %collective-permute-start.6 = (bf16[256,512]{1,0:T(8,128)(2,1)}, bf16[256,512]{1,0:T(8,128)(2,1)S(1)}, u32[]{:S(2)}, u32[]{:S(2)}) collective-permute-start(bf16[256,512]{1,0:T(8,128)(2,1)} %copy-done.7), channel_id=1, source_target_pairs={{0,4},{4,0},{8,12},{12,8},{1,5},{5,1},{9,13},{13,9},{2,6},{6,2},{1... | collective-permute-start | bytes 786440 | tf_op jit(solution)/shard_map/ppermute | solution.py:40
  120.4 1.7 %broadcast_select_fusion.refs_3_ = bf16[256,512]{1,0:T(8,128)(2,1)} fusion(bf16[256,512]{1,0:T(8,128)(2,1)} %collective-permute-done.27, bf16[256,512]{1,0:T(8,128)(2,1)} %collective-permute-done.28, pred[]{:T(512)S(6)} %or.4), kind=kLoop, calls=%fused_computation.4 | loop fusion | flops 131072 | bytes 786433 | tf_op jit(solution)/shard_map/jit(_where)/select_n | solution.py:265
  122.1 1.7 %broadcast_select_fusion.1.refs_3_ = bf16[256,512]{1,0:T(8,128)(2,1)} fusion(bf16[256,512]{1,0:T(8,128)(2,1)} %collective-permute-done.8, bf16[256,512]{1,0:T(8,128)(2,1)} %collective-permute-done.9, pred[]{:T(512)S(6)} %or.4), kind=kLoop, calls=%fused_computation.5 | loop fusion | flops 131072 | bytes 786433 | tf_op jit(solution)/shard_map/jit(_where)/select_n | solution.py:265
  123.8 6.9 %project.2.refs_14_ = f32[256,1280]{1,0:T(8,128)} custom-call(s32[4]{0:T(128)} %pad_add_fusion.where_ref, bf16[256,512]{1,0:T(8,128)(2,1)} %copy-done.6, bf16[256,512]{1,0:T(8,128)(2,1)} %copy-done.16, bf16[256,512]{1,0:T(8,128)(2,1)} %copy-done.14, bf16[256,512]{1,0:T(8,128)(2,1)} %broadcast_select_fusion.refs_3_, bf16[4,2,128,1280]{3,2,1,0:T(8,128)(2,1)} %bitcast.19, ...), custom_call_target="tpu_custom_call" | custom-call | tf_op jit(solution)/shard_map/project/pallas_call | solution.py:192
  130.8 0.7 copy-done.17
  131.5 7.1 %project.3 = (bf16[64,1280]{1,0:T(8,128)(2,1)}, bf16[64,1280]{1,0:T(8,128)(2,1)}, bf16[64,1280]{1,0:T(8,128)(2,1)}, bf16[64,1280]{1,0:T(8,128)(2,1)}) custom-call(s32[4]{0:T(128)} %pad_add_fusion.where_ref, bf16[256,512]{1,0:T(8,128)(2,1)} %copy-done.7, bf16[256,512]{1,0:T(8,128)(2,1)} %copy-done.17, bf16[256,512]{1,0:T(8,128)(2,1)} %copy-done.15, ...), custom_call_target="tpu_custom_call" | custom-call | tf_op jit(solution)/shard_map/project/pallas_call | solution.py:192
  138.9 1.9 %collective-permute-start.30 = (bf16[64,1280]{1,0:T(8,128)(2,1)}, bf16[64,1280]{1,0:T(8,128)(2,1)S(1)}, u32[]{:S(2)}, u32[]{:S(2)}) collective-permute-start(bf16[64,1280]{1,0:T(8,128)(2,1)} %get-tuple-element.43), channel_id=1, source_target_pairs={{0,8},{4,12},{8,0},{12,4},{1,9},{5,13},{9,1},{13,5},{2,10},{6,14},... | collective-permute-start | bytes 491528 | tf_op jit(solution)/shard_map/ppermute | solution.py:40
  140.9 2.2 %collective-permute-start.31 = (bf16[64,1280]{1,0:T(8,128)(2,1)}, bf16[64,1280]{1,0:T(8,128)(2,1)S(1)}, u32[]{:S(2)}, u32[]{:S(2)}) collective-permute-start(bf16[64,1280]{1,0:T(8,128)(2,1)} %get-tuple-element.44), channel_id=1, source_target_pairs={{0,12},{4,8},{8,4},{12,0},{1,13},{5,9},{9,5},{13,1},{2,14},{6,10},... | collective-permute-start | bytes 491528 | tf_op jit(solution)/shard_map/ppermute | solution.py:40
  143.1 4.9 %collective-permute-done.29.refs_1_ = bf16[64,1280]{1,0:T(8,128)(2,1)S(1)} collective-permute-done((bf16[64,1280]{1,0:T(8,128)(2,1)}, bf16[64,1280]{1,0:T(8,128)(2,1)S(1)}, u32[]{:S(2)}, u32[]{:S(2)}) %collective-permute-start.29) | collective-permute-done | bytes 163872 | tf_op jit(solution)/shard_map/ppermute | solution.py:40
  148.0 6.2 %collective-permute-done.30.refs_2_ = bf16[64,1280]{1,0:T(8,128)(2,1)S(1)} collective-permute-done((bf16[64,1280]{1,0:T(8,128)(2,1)}, bf16[64,1280]{1,0:T(8,128)(2,1)S(1)}, u32[]{:S(2)}, u32[]{:S(2)}) %collective-permute-start.30) | collective-permute-done | bytes 163872 | tf_op jit(solution)/shard_map/ppermute | solution.py:40
  154.2 0.7 copy-done.19
  154.9 3.1 %mix.1 = bf16[64,5120]{1,0:T(8,128)(2,1)} custom-call(s32[4]{0:T(128)} %pad_add_fusion.where_ref, bf16[64,5120]{1,0:T(8,128)(2,1)} %hidden_ref.1, f32[1,5120]{1,0:T(1,128)} %bitcast.30, bf16[64,1280]{1,0:T(8,128)(2,1)} %get-tuple-element.41.refs_0_, bf16[64,1280]{1,0:T(8,128)(2,1)} %copy-done.18, bf16[64,1280]{1,0:T(8,128)(2,1)} %copy-done.19, ...), custom_call_target="tpu_custom_call" | custom-call | tf_op jit(solution)/shard_map/mix/pallas_call | solution.py:215
  (73 shorter events, 1.9 us)
Async XLA Ops:
  0.0 123.8 %collective-permute-start.10 = (bf16[4,2,128,1280]{3,2,1,0:T(8,128)(2,1)}, bf16[4,2,128,1280]{3,2,1,0:T(8,128)(2,1)}, u32[]{:S(2)}, u32[]{:S(2)}) collective-permute-start(bf16[4,2,128,1280]{3,2,1,0:T(8,128)(2,1)} %bitcast.18), channel_id=1, source_target_pairs={{0,1},{1,0},{2,3},{3,2},{4,5},{5,4},{6,7},{7,6},{8,9},{9,8},{10,11... | collective-permute-start | bytes 7864328 | tf_op jit(solution)/shard_map/ppermute | solution.py:40
  5.2 12.2 %collective-permute-start.19 = (bf16[3,256,128]{2,1,0:T(8,128)(2,1)}, bf16[3,256,128]{2,1,0:T(8,128)(2,1)S(1)}, u32[]{:S(2)}, u32[]{:S(2)}) collective-permute-start(bf16[3,256,128]{2,1,0:T(8,128)(2,1)} %get-tuple-element.34), channel_id=1, source_target_pairs={{0,4},{4,0},{8,12},{12,8},{1,5},{5,1},{9,13},{13,9},{2,6},{6,2},{1... | collective-permute-start | bytes 589832 | tf_op jit(solution)/shard_map/ppermute | solution.py:40
  7.8 17.4 %collective-permute-start.20 = (bf16[3,256,128]{2,1,0:T(8,128)(2,1)}, bf16[3,256,128]{2,1,0:T(8,128)(2,1)S(1)}, u32[]{:S(2)}, u32[]{:S(2)}) collective-permute-start(bf16[3,256,128]{2,1,0:T(8,128)(2,1)} %get-tuple-element.35), channel_id=1, source_target_pairs={{0,8},{4,12},{8,0},{12,4},{1,9},{5,13},{9,1},{13,5},{2,10},{6,14},... | collective-permute-start | bytes 589832 | tf_op jit(solution)/shard_map/ppermute | solution.py:40
  10.4 28.0 %copy-start = (bf16[1024,1280]{1,0:T(8,128)(2,1)S(1)}, bf16[1024,1280]{1,0:T(8,128)(2,1)}, u32[]{:S(2)}) copy-start(bf16[1024,1280]{1,0:T(8,128)(2,1)} %param.11) | copy-start | bytes 7864324
  10.4 14.8 %collective-permute-start.21 = (bf16[3,256,128]{2,1,0:T(8,128)(2,1)}, bf16[3,256,128]{2,1,0:T(8,128)(2,1)S(1)}, u32[]{:S(2)}, u32[]{:S(2)}) collective-permute-start(bf16[3,256,128]{2,1,0:T(8,128)(2,1)} %get-tuple-element.36), channel_id=1, source_target_pairs={{0,12},{4,8},{8,4},{12,0},{1,13},{5,9},{9,5},{13,1},{2,14},{6,10},... | collective-permute-start | bytes 589832 | tf_op jit(solution)/shard_map/ppermute | solution.py:40
  14.6 22.3 %collective-permute-start = (bf16[3,256,128]{2,1,0:T(8,128)(2,1)}, bf16[3,256,128]{2,1,0:T(8,128)(2,1)S(1)}, u32[]{:S(2)}, u32[]{:S(2)}) collective-permute-start(bf16[3,256,128]{2,1,0:T(8,128)(2,1)} %get-tuple-element.26), channel_id=1, source_target_pairs={{0,4},{4,0},{8,12},{12,8},{1,5},{5,1},{9,13},{13,9},{2,6},{6,2},{1... | collective-permute-start | bytes 589832 | tf_op jit(solution)/shard_map/ppermute | solution.py:40
  17.3 7.8 %copy-start.11 = (bf16[3,256,128]{2,1,0:T(8,128)(2,1)}, bf16[3,256,128]{2,1,0:T(8,128)(2,1)S(1)}, u32[]{:S(2)}) copy-start(bf16[3,256,128]{2,1,0:T(8,128)(2,1)S(1)} %collective-permute-done.19.refs_1_.refs_5_) | copy-start | bytes 589828
  25.1 0.8 copy-start.13
  30.4 13.1 %copy-start.21 = (bf16[4,64,128]{2,1,0:T(8,128)(2,1)S(1)}, bf16[4,64,128]{2,1,0:T(8,128)(2,1)}, u32[]{:S(2)}) copy-start(bf16[4,64,128]{2,1,0:T(8,128)(2,1)} %get-tuple-element.37) | copy-start | bytes 196612
  30.4 8.0 %collective-permute-start.22 = (bf16[4,64,128]{2,1,0:T(8,128)(2,1)}, bf16[4,64,128]{2,1,0:T(8,128)(2,1)S(1)}, u32[]{:S(2)}, u32[]{:S(2)}) collective-permute-start(bf16[4,64,128]{2,1,0:T(8,128)(2,1)} %get-tuple-element.38), channel_id=1, source_target_pairs={{0,1},{1,0},{2,3},{3,2},{4,5},{5,4},{6,7},{7,6},{8,9},{9,8},{10,11... | collective-permute-start | bytes 196616 | tf_op jit(solution)/shard_map/ppermute | solution.py:40
  30.4 19.5 %collective-permute-start.1 = (bf16[3,256,128]{2,1,0:T(8,128)(2,1)}, bf16[3,256,128]{2,1,0:T(8,128)(2,1)S(1)}, u32[]{:S(2)}, u32[]{:S(2)}) collective-permute-start(bf16[3,256,128]{2,1,0:T(8,128)(2,1)} %get-tuple-element.27), channel_id=1, source_target_pairs={{0,8},{4,12},{8,0},{12,4},{1,9},{5,13},{9,1},{13,5},{2,10},{6,14},... | collective-permute-start | bytes 589832 | tf_op jit(solution)/shard_map/ppermute | solution.py:40
  35.5 14.4 %collective-permute-start.2 = (bf16[3,256,128]{2,1,0:T(8,128)(2,1)}, bf16[3,256,128]{2,1,0:T(8,128)(2,1)S(1)}, u32[]{:S(2)}, u32[]{:S(2)}) collective-permute-start(bf16[3,256,128]{2,1,0:T(8,128)(2,1)} %get-tuple-element.28), channel_id=1, source_target_pairs={{0,12},{4,8},{8,4},{12,0},{1,13},{5,9},{9,5},{13,1},{2,14},{6,10},... | collective-permute-start | bytes 589832 | tf_op jit(solution)/shard_map/ppermute | solution.py:40
  36.9 13.1 %copy-start.8 = (bf16[3,256,128]{2,1,0:T(8,128)(2,1)}, bf16[3,256,128]{2,1,0:T(8,128)(2,1)S(1)}, u32[]{:S(2)}) copy-start(bf16[3,256,128]{2,1,0:T(8,128)(2,1)S(1)} %collective-permute-done.refs_1_.refs_5_) | copy-start | bytes 589828
  36.9 4.5 %collective-permute-start.23 = (bf16[4,64,128]{2,1,0:T(8,128)(2,1)}, bf16[4,64,128]{2,1,0:T(8,128)(2,1)S(1)}, u32[]{:S(2)}, u32[]{:S(2)}) collective-permute-start(bf16[4,64,128]{2,1,0:T(8,128)(2,1)} %get-tuple-element.39), channel_id=1, source_target_pairs={{0,2},{1,3},{2,0},{3,1},{4,6},{5,7},{6,4},{7,5},{8,10},{9,11},{10,... | collective-permute-start | bytes 196616 | tf_op jit(solution)/shard_map/ppermute | solution.py:40
  38.4 5.1 %collective-permute-start.24 = (bf16[4,64,128]{2,1,0:T(8,128)(2,1)}, bf16[4,64,128]{2,1,0:T(8,128)(2,1)S(1)}, u32[]{:S(2)}, u32[]{:S(2)}) collective-permute-start(bf16[4,64,128]{2,1,0:T(8,128)(2,1)} %get-tuple-element.40), channel_id=1, source_target_pairs={{0,3},{1,2},{2,1},{3,0},{4,7},{5,6},{6,5},{7,4},{8,11},{9,10},{10,... | collective-permute-start | bytes 196616 | tf_op jit(solution)/shard_map/ppermute | solution.py:40
  41.4 46.9 %collective-permute-start.11 = (bf16[2,128,1280]{2,1,0:T(8,128)(2,1)}, bf16[2,128,1280]{2,1,0:T(8,128)(2,1)S(1)}, u32[]{:S(2)}, u32[]{:S(2)}) collective-permute-start(bf16[2,128,1280]{2,1,0:T(8,128)(2,1)} %get-tuple-element.46), channel_id=1, source_target_pairs={{0,2},{2,0},{1,3},{3,1},{4,6},{6,4},{5,7},{7,5},{8,10},{10,8},{9,1... | collective-permute-start | bytes 1966088 | tf_op jit(solution)/shard_map/ppermute | solution.py:40
  43.5 46.3 %collective-permute-start.13 = (bf16[2,128,1280]{2,1,0:T(8,128)(2,1)}, bf16[2,128,1280]{2,1,0:T(8,128)(2,1)S(1)}, u32[]{:S(2)}, u32[]{:S(2)}) collective-permute-start(bf16[2,128,1280]{2,1,0:T(8,128)(2,1)} %get-tuple-element.45), channel_id=1, source_target_pairs={{0,2},{2,0},{1,3},{3,1},{4,6},{6,4},{5,7},{7,5},{8,10},{10,8},{9,1... | collective-permute-start | bytes 1966088 | tf_op jit(solution)/shard_map/ppermute | solution.py:40
  43.6 80.2 %copy-start.6 = (bf16[256,512]{1,0:T(8,128)(2,1)}, bf16[256,512]{1,0:T(8,128)(2,1)S(1)}, u32[]{:S(2)}) copy-start(bf16[256,512]{1,0:T(8,128)(2,1)S(1)} %pad_maximum_fusion.1.refs_0_) | copy-start | bytes 786436
  49.9 28.7 %collective-permute-start.26 = (bf16[256,512]{1,0:T(8,128)(2,1)S(1)}, bf16[256,512]{1,0:T(8,128)(2,1)S(1)}, u32[]{:S(2)}, u32[]{:S(2)}) collective-permute-start(bf16[256,512]{1,0:T(8,128)(2,1)S(1)} %pad_maximum_fusion.1.refs_0_), channel_id=1, source_target_pairs={{0,8},{4,12},{8,0},{12,4},{1,9},{5,13},{9,1},{13,5},{2,10},{6,14},... | collective-permute-start | bytes 786440 | tf_op jit(solution)/shard_map/ppermute | solution.py:40
  55.2 1.5 collective-permute-start.3
  56.6 16.0 %collective-permute-start.4 = (bf16[4,64,128]{2,1,0:T(8,128)(2,1)}, bf16[4,64,128]{2,1,0:T(8,128)(2,1)S(1)}, u32[]{:S(2)}, u32[]{:S(2)}) collective-permute-start(bf16[4,64,128]{2,1,0:T(8,128)(2,1)} %get-tuple-element.31), channel_id=1, source_target_pairs={{0,2},{1,3},{2,0},{3,1},{4,6},{5,7},{6,4},{7,5},{8,10},{9,11},{10,... | collective-permute-start | bytes 196616 | tf_op jit(solution)/shard_map/ppermute | solution.py:40
  72.7 4.5 %collective-permute-start.5 = (bf16[4,64,128]{2,1,0:T(8,128)(2,1)}, bf16[4,64,128]{2,1,0:T(8,128)(2,1)S(1)}, u32[]{:S(2)}, u32[]{:S(2)}) collective-permute-start(bf16[4,64,128]{2,1,0:T(8,128)(2,1)} %get-tuple-element.32), channel_id=1, source_target_pairs={{0,3},{1,2},{2,1},{3,0},{4,7},{5,6},{6,5},{7,4},{8,11},{9,10},{10,... | collective-permute-start | bytes 196616 | tf_op jit(solution)/shard_map/ppermute | solution.py:40
  77.2 2.6 %collective-permute-start.27 = (bf16[256,512]{1,0:T(8,128)(2,1)S(1)}, bf16[256,512]{1,0:T(8,128)(2,1)}, u32[]{:S(2)}, u32[]{:S(2)}) collective-permute-start(bf16[256,512]{1,0:T(8,128)(2,1)S(1)} %pad_maximum_fusion.1.refs_0_), channel_id=1, source_target_pairs={{4,8},{8,4},{5,9},{9,5},{6,10},{10,6},{7,11},{11,7},{20,24},{24,20... | collective-permute-start | bytes 786440 | tf_op jit(solution)/shard_map/ppermute | solution.py:40
  78.6 39.7 %copy-start.14 = (bf16[256,512]{1,0:T(8,128)(2,1)}, bf16[256,512]{1,0:T(8,128)(2,1)S(1)}, u32[]{:S(2)}) copy-start(bf16[256,512]{1,0:T(8,128)(2,1)S(1)} %collective-permute-done.26.refs_2_) | copy-start | bytes 786436
  78.6 8.3 %collective-permute-start.25 = (bf16[256,512]{1,0:T(8,128)(2,1)S(1)}, bf16[256,512]{1,0:T(8,128)(2,1)S(1)}, u32[]{:S(2)}, u32[]{:S(2)}) collective-permute-start(bf16[256,512]{1,0:T(8,128)(2,1)S(1)} %pad_maximum_fusion.1.refs_0_), channel_id=1, source_target_pairs={{0,4},{4,0},{8,12},{12,8},{1,5},{5,1},{9,13},{13,9},{2,6},{6,2},{1... | collective-permute-start | bytes 786440 | tf_op jit(solution)/shard_map/ppermute | solution.py:40
  79.8 38.4 %copy-start.7 = (bf16[256,512]{1,0:T(8,128)(2,1)}, bf16[256,512]{1,0:T(8,128)(2,1)S(1)}, u32[]{:S(2)}) copy-start(bf16[256,512]{1,0:T(8,128)(2,1)S(1)} %pad_maximum_fusion.refs_0_) | copy-start | bytes 786436
  79.9 19.7 %collective-permute-start.7 = (bf16[256,512]{1,0:T(8,128)(2,1)S(1)}, bf16[256,512]{1,0:T(8,128)(2,1)S(1)}, u32[]{:S(2)}, u32[]{:S(2)}) collective-permute-start(bf16[256,512]{1,0:T(8,128)(2,1)S(1)} %pad_maximum_fusion.refs_0_), channel_id=1, source_target_pairs={{0,8},{4,12},{8,0},{12,4},{1,9},{5,13},{9,1},{13,5},{2,10},{6,14},... | collective-permute-start | bytes 786440 | tf_op jit(solution)/shard_map/ppermute | solution.py:40
  86.9 31.3 %copy-start.16 = (bf16[256,512]{1,0:T(8,128)(2,1)}, bf16[256,512]{1,0:T(8,128)(2,1)S(1)}, u32[]{:S(2)}) copy-start(bf16[256,512]{1,0:T(8,128)(2,1)S(1)} %collective-permute-done.25.refs_1_) | copy-start | bytes 786436
  86.9 13.9 %collective-permute-start.8 = (bf16[256,512]{1,0:T(8,128)(2,1)S(1)}, bf16[256,512]{1,0:T(8,128)(2,1)}, u32[]{:S(2)}, u32[]{:S(2)}) collective-permute-start(bf16[256,512]{1,0:T(8,128)(2,1)S(1)} %pad_maximum_fusion.refs_0_), channel_id=1, source_target_pairs={{4,8},{8,4},{5,9},{9,5},{6,10},{10,6},{7,11},{11,7},{20,24},{24,20... | collective-permute-start | bytes 786440 | tf_op jit(solution)/shard_map/ppermute | solution.py:40
  88.3 35.5 %copy-start.1 = (bf16[2,128,1280]{2,1,0:T(8,128)(2,1)}, bf16[2,128,1280]{2,1,0:T(8,128)(2,1)S(1)}, u32[]{:S(2)}) copy-start(bf16[2,128,1280]{2,1,0:T(8,128)(2,1)S(1)} %collective-permute-done.11.refs_6_) | copy-start | bytes 1966084
  88.3 28.0 %collective-permute-start.15 = (bf16[2,128,1280]{2,1,0:T(8,128)(2,1)S(1)}, bf16[2,128,1280]{2,1,0:T(8,128)(2,1)S(1)}, u32[]{:S(2)}, u32[]{:S(2)}) collective-permute-start(bf16[2,128,1280]{2,1,0:T(8,128)(2,1)S(1)} %collective-permute-done.11.refs_6_), channel_id=1, source_target_pairs={{0,16},{16,0},{1,17},{17,1},{2,18},{18,2},{3,19},{19,3},{4,20},{20... | collective-permute-start | bytes 1966088 | tf_op jit(solution)/shard_map/ppermute | solution.py:40
  89.8 34.0 %copy-start.2 = (bf16[2,128,1280]{2,1,0:T(8,128)(2,1)}, bf16[2,128,1280]{2,1,0:T(8,128)(2,1)S(1)}, u32[]{:S(2)}) copy-start(bf16[2,128,1280]{2,1,0:T(8,128)(2,1)S(1)} %collective-permute-done.13.refs_8_) | copy-start | bytes 1966084
  89.8 28.4 %collective-permute-start.17 = (bf16[2,128,1280]{2,1,0:T(8,128)(2,1)S(1)}, bf16[2,128,1280]{2,1,0:T(8,128)(2,1)S(1)}, u32[]{:S(2)}, u32[]{:S(2)}) collective-permute-start(bf16[2,128,1280]{2,1,0:T(8,128)(2,1)S(1)} %collective-permute-done.13.refs_8_), channel_id=1, source_target_pairs={{0,16},{16,0},{1,17},{17,1},{2,18},{18,2},{3,19},{19,3},{4,20},{20... | collective-permute-start | bytes 1966088 | tf_op jit(solution)/shard_map/ppermute | solution.py:40
  99.6 18.7 %copy-start.15 = (bf16[256,512]{1,0:T(8,128)(2,1)}, bf16[256,512]{1,0:T(8,128)(2,1)S(1)}, u32[]{:S(2)}) copy-start(bf16[256,512]{1,0:T(8,128)(2,1)S(1)} %collective-permute-done.7.refs_2_) | copy-start | bytes 786436
  99.6 8.4 %collective-permute-start.28 = (bf16[256,512]{1,0:T(8,128)(2,1)S(1)}, bf16[256,512]{1,0:T(8,128)(2,1)}, u32[]{:S(2)}, u32[]{:S(2)}) collective-permute-start(bf16[256,512]{1,0:T(8,128)(2,1)S(1)} %collective-permute-done.26.refs_2_), channel_id=1, source_target_pairs={{4,0},{8,12},{5,1},{9,13},{6,2},{10,14},{7,3},{11,15},{20,16},{24,... | collective-permute-start | bytes 786440 | tf_op jit(solution)/shard_map/ppermute | solution.py:263
  100.9 17.5 %collective-permute-start.12 = (bf16[2,128,1280]{2,1,0:T(8,128)(2,1)S(1)}, bf16[2,128,1280]{2,1,0:T(8,128)(2,1)S(1)}, u32[]{:S(2)}, u32[]{:S(2)}) collective-permute-start(bf16[2,128,1280]{2,1,0:T(8,128)(2,1)S(1)} %collective-permute-done.11.refs_6_), channel_id=1, source_target_pairs={{0,1},{1,0},{2,3},{3,2},{4,5},{5,4},{6,7},{7,6},{8,9},{9,8},{10,11... | collective-permute-start | bytes 1966088 | tf_op jit(solution)/shard_map/ppermute | solution.py:40
  108.0 8.4 %collective-permute-start.9 = (bf16[256,512]{1,0:T(8,128)(2,1)S(1)}, bf16[256,512]{1,0:T(8,128)(2,1)}, u32[]{:S(2)}, u32[]{:S(2)}) collective-permute-start(bf16[256,512]{1,0:T(8,128)(2,1)S(1)} %collective-permute-done.7.refs_2_), channel_id=1, source_target_pairs={{4,0},{8,12},{5,1},{9,13},{6,2},{10,14},{7,3},{11,15},{20,16},{24,... | collective-permute-start | bytes 786440 | tf_op jit(solution)/shard_map/ppermute | solution.py:263
  116.3 7.4 %collective-permute-start.14 = (bf16[2,128,1280]{2,1,0:T(8,128)(2,1)S(1)}, bf16[2,128,1280]{2,1,0:T(8,128)(2,1)}, u32[]{:S(2)}, u32[]{:S(2)}) collective-permute-start(bf16[2,128,1280]{2,1,0:T(8,128)(2,1)S(1)} %collective-permute-done.13.refs_8_), channel_id=1, source_target_pairs={{0,1},{1,0},{2,3},{3,2},{4,5},{5,4},{6,7},{7,6},{8,9},{9,8},{10,11... | collective-permute-start | bytes 1966088 | tf_op jit(solution)/shard_map/ppermute | solution.py:40
  116.3 7.5 %copy-start.3 = (bf16[2,128,1280]{2,1,0:T(8,128)(2,1)}, bf16[2,128,1280]{2,1,0:T(8,128)(2,1)S(1)}, u32[]{:S(2)}) copy-start(bf16[2,128,1280]{2,1,0:T(8,128)(2,1)S(1)} %collective-permute-done.15.refs_10_) | copy-start | bytes 1966084
  116.3 7.4 %collective-permute-start.16 = (bf16[2,128,1280]{2,1,0:T(8,128)(2,1)S(1)}, bf16[2,128,1280]{2,1,0:T(8,128)(2,1)}, u32[]{:S(2)}, u32[]{:S(2)}) collective-permute-start(bf16[2,128,1280]{2,1,0:T(8,128)(2,1)S(1)} %collective-permute-done.15.refs_10_), channel_id=1, source_target_pairs={{0,1},{1,0},{2,3},{3,2},{4,5},{5,4},{6,7},{7,6},{8,9},{9,8},{10,11... | collective-permute-start | bytes 1966088 | tf_op jit(solution)/shard_map/ppermute | solution.py:40
  118.3 5.5 %copy-start.4 = (bf16[2,128,1280]{2,1,0:T(8,128)(2,1)}, bf16[2,128,1280]{2,1,0:T(8,128)(2,1)S(1)}, u32[]{:S(2)}) copy-start(bf16[2,128,1280]{2,1,0:T(8,128)(2,1)S(1)} %collective-permute-done.17.refs_12_) | copy-start | bytes 1966084
  118.3 5.5 %collective-permute-start.18 = (bf16[2,128,1280]{2,1,0:T(8,128)(2,1)S(1)}, bf16[2,128,1280]{2,1,0:T(8,128)(2,1)}, u32[]{:S(2)}, u32[]{:S(2)}) collective-permute-start(bf16[2,128,1280]{2,1,0:T(8,128)(2,1)S(1)} %collective-permute-done.17.refs_12_), channel_id=1, source_target_pairs={{0,1},{1,0},{2,3},{3,2},{4,5},{5,4},{6,7},{7,6},{8,9},{9,8},{10,11... | collective-permute-start | bytes 1966088 | tf_op jit(solution)/shard_map/ppermute | solution.py:40
  118.4 5.4 %copy-start.5 = (bf16[2,128,1280]{2,1,0:T(8,128)(2,1)}, bf16[2,128,1280]{2,1,0:T(8,128)(2,1)S(1)}, u32[]{:S(2)}) copy-start(bf16[2,128,1280]{2,1,0:T(8,128)(2,1)S(1)} %collective-permute-done.12.refs_7_) | copy-start | bytes 1966084
  118.4 12.4 %collective-permute-start.6 = (bf16[256,512]{1,0:T(8,128)(2,1)}, bf16[256,512]{1,0:T(8,128)(2,1)S(1)}, u32[]{:S(2)}, u32[]{:S(2)}) collective-permute-start(bf16[256,512]{1,0:T(8,128)(2,1)} %copy-done.7), channel_id=1, source_target_pairs={{0,4},{4,0},{8,12},{12,8},{1,5},{5,1},{9,13},{13,9},{2,6},{6,2},{1... | collective-permute-start | bytes 786440 | tf_op jit(solution)/shard_map/ppermute | solution.py:40
  138.6 9.4 %collective-permute-start.29 = (bf16[64,1280]{1,0:T(8,128)(2,1)}, bf16[64,1280]{1,0:T(8,128)(2,1)S(1)}, u32[]{:S(2)}, u32[]{:S(2)}) collective-permute-start(bf16[64,1280]{1,0:T(8,128)(2,1)} %get-tuple-element.42), channel_id=1, source_target_pairs={{0,4},{4,0},{8,12},{12,8},{1,5},{5,1},{9,13},{13,9},{2,6},{6,2},{1... | collective-permute-start | bytes 491528 | tf_op jit(solution)/shard_map/ppermute | solution.py:40
  138.9 15.2 %collective-permute-start.30 = (bf16[64,1280]{1,0:T(8,128)(2,1)}, bf16[64,1280]{1,0:T(8,128)(2,1)S(1)}, u32[]{:S(2)}, u32[]{:S(2)}) collective-permute-start(bf16[64,1280]{1,0:T(8,128)(2,1)} %get-tuple-element.43), channel_id=1, source_target_pairs={{0,8},{4,12},{8,0},{12,4},{1,9},{5,13},{9,1},{13,5},{2,10},{6,14},... | collective-permute-start | bytes 491528 | tf_op jit(solution)/shard_map/ppermute | solution.py:40
  140.9 13.3 %collective-permute-start.31 = (bf16[64,1280]{1,0:T(8,128)(2,1)}, bf16[64,1280]{1,0:T(8,128)(2,1)S(1)}, u32[]{:S(2)}, u32[]{:S(2)}) collective-permute-start(bf16[64,1280]{1,0:T(8,128)(2,1)} %get-tuple-element.44), channel_id=1, source_target_pairs={{0,12},{4,8},{8,4},{12,0},{1,13},{5,9},{9,5},{13,1},{2,14},{6,10},... | collective-permute-start | bytes 491528 | tf_op jit(solution)/shard_map/ppermute | solution.py:40
  148.0 6.2 %copy-start.18 = (bf16[64,1280]{1,0:T(8,128)(2,1)}, bf16[64,1280]{1,0:T(8,128)(2,1)S(1)}, u32[]{:S(2)}) copy-start(bf16[64,1280]{1,0:T(8,128)(2,1)S(1)} %collective-permute-done.29.refs_1_) | copy-start | bytes 491524
  (6 other events, 4.2 us)

commit v3 on v0

v3 whole, which is shorter than its diff:
```python
import functools
import math

import jax
import jax.numpy as jnp
from jax import lax
from jax.experimental import pallas as pl
from jax.experimental.pallas import tpu as pltpu
from jax.sharding import PartitionSpec as P

HEAD_DIM = 128
SCALE_ROWS = 128
SATURATION = 448.0
VMEM_BYTES = 32 * 1024 * 1024


def spec(shape):
    return pl.BlockSpec(shape, lambda i, w: (0,) * len(shape))


def call(kernel, name, out_shape, grid, in_specs, out_specs, scratch=(), cost=None):
    return pl.pallas_call(
        kernel,
        out_shape=out_shape,
        grid_spec=pltpu.PrefetchScalarGridSpec(
            num_scalar_prefetch=1,
            grid=(grid,),
            in_specs=in_specs,
            out_specs=out_specs,
            scratch_shapes=list(scratch),
        ),
        compiler_params=pltpu.CompilerParams(vmem_limit_bytes=VMEM_BYTES),
        cost_estimate=cost,
        name=name,
    )


def swap(x, axes, count, mask, only=None):
    pairs = [(at, at ^ mask) for at in range(count) if only is None or at in only]
    return lax.ppermute(x, axes, pairs)


def pack_kernel(split, per, where_ref, exps_ref, q_ref, fresh_ref, cached_ref, *outs):
    rows = q_ref.shape[0]
    block = pl.program_id(0) * rows // SCALE_ROWS
    for dest in range(split):
        for chunk in range(per):
            head = dest * per + chunk
            lanes = slice(head * HEAD_DIM, (head + 1) * HEAD_DIM)
            outs[chunk][dest, 0] = q_ref[:, lanes]
            for stacked in range(2):
                power = jnp.full((1, HEAD_DIM), exps_ref[stacked, block, head].astype(jnp.float32))
                cached = cached_ref[stacked, :, lanes].astype(jnp.float32)
                residual = fresh_ref[stacked, :, lanes].astype(jnp.float32) - cached
                codes = jnp.clip(
                    residual * jnp.exp2(-power), -SATURATION, SATURATION
                ).astype(jnp.bfloat16)
                decoded = cached + codes.astype(jnp.float32) * jnp.exp2(power)
                outs[chunk][dest, 1 + stacked] = decoded.astype(jnp.bfloat16)


def pack(split, per, where, exponents, queries, fresh_kv, cached_kv):
    tok, channels = queries.shape
    rows = SCALE_ROWS // 2
    steps = tok // rows
    out = jax.ShapeDtypeStruct((split, 3, tok, HEAD_DIM), jnp.bfloat16)
    return call(
        functools.partial(pack_kernel, split, per),
        "pack",
        [out] * per,
        steps,
        [
            pl.BlockSpec(memory_space=pltpu.SMEM),
            pl.BlockSpec((rows, channels), lambda i, w: (i, 0)),
            pl.BlockSpec((2, rows, channels), lambda i, w: (0, i, 0)),
            pl.BlockSpec((2, rows, channels), lambda i, w: (0, w[0] * steps + i, 0)),
        ],
        [pl.BlockSpec((split, 3, rows, HEAD_DIM), lambda i, w: (0, 0, i, 0))] * per,
    )(where, exponents, queries, fresh_kv, cached_kv)


def attend_kernel(where_ref, q_ref, kv_ref, out_ref):
    split = q_ref.shape[0]
    n_rel, _, rows, _ = out_ref.shape
    factor = HEAD_DIM**-0.5 * math.log2(math.e)
    keys = kv_ref[:, 1].reshape(-1, HEAD_DIM)
    values = kv_ref[:, 2].reshape(-1, HEAD_DIM)
    values = jnp.concatenate([values, jnp.ones_like(values)], axis=1)
    for at in range(split):
        scores = lax.dot_general(
            q_ref[at, 0], keys, (((1,), (1,)), ((), ())), preferred_element_type=jnp.float32
        )
        peak = jnp.max(scores, axis=1, keepdims=True)
        expo = jnp.exp2((scores - peak) * factor).astype(jnp.bfloat16)
        mix = jnp.dot(expo, values, preferred_element_type=jnp.float32)
        mix = (mix[:, :HEAD_DIM] / mix[:, HEAD_DIM:]).astype(jnp.bfloat16)
        for rel in range(n_rel):
            out_ref[rel, at] = mix[rel * rows : (rel + 1) * rows]


def attend(where, n_rel, arrived, everyone):
    split, _, tok, feat = arrived.shape
    out = jax.ShapeDtypeStruct((n_rel, split, tok // n_rel, feat), jnp.bfloat16)
    return call(
        attend_kernel,
        "attend",
        out,
        1,
        [spec(arrived.shape), spec(everyone.shape)],
        spec(out.shape),
    )(where, arrived, everyone)


def project_kernel(split, n_slots, with_acc, last, where_ref, *refs):
    slots, weight_ref, refs = refs[:n_slots], refs[n_slots], refs[n_slots + 1 :]
    acc_ref, refs = (refs[0], refs[1:]) if with_acc else (None, refs)
    out_ref, held_ref = refs
    n_rel, rows, _ = slots[0].shape

    @pl.when(pl.program_id(0) == 0)
    def arrange():
        for at, slot in enumerate(slots):
            group, near = divmod(at, split)
            for rel in range(n_rel):
                lane = (rel * split + (where_ref[1] ^ near)) * HEAD_DIM
                held_ref[
                    group * rows : (group + 1) * rows,
                    pl.ds(pl.multiple_of(lane, HEAD_DIM), HEAD_DIM),
                ] = slot[rel]

    acc = jnp.dot(held_ref[...], weight_ref[0], preferred_element_type=jnp.float32)
    if with_acc:
        acc += acc_ref[...]
    if not last:
        out_ref[...] = acc
    else:
        piece = rows // split
        for group in range(n_slots // split):
            for at in range(split):
                start = group * rows + at * piece
                out_ref[(where_ref[2] ^ group) * split + at] = acc[start : start + piece].astype(
                    jnp.bfloat16
                )


def project(split, where, slots, weight_at, acc, last):
    weight, index = weight_at
    n_rel, rows, _ = slots[0].shape
    total = rows * len(slots) // split
    _, depth, cols = weight.shape
    wide = 256 if cols % 256 == 0 else cols
    whole = pl.BlockSpec((total, wide), lambda i, w: (0, i))
    specs = [spec(slots[0].shape)] * len(slots)
    specs.append(pl.BlockSpec((1, depth, wide), lambda i, w: (index, 0, i)))
    if acc is not None:
        specs.append(whole)
    if last:
        piece = rows // split
        out = jax.ShapeDtypeStruct((len(slots), piece, cols), jnp.bfloat16)
        out_spec = pl.BlockSpec((len(slots), piece, wide), lambda i, w: (0, 0, i))
    else:
        out = jax.ShapeDtypeStruct((total, cols), jnp.float32)
        out_spec = whole
    operands = [*slots, weight] + ([] if acc is None else [acc])
    return call(
        functools.partial(project_kernel, split, len(slots), acc is not None, last),
        "project",
        out,
        cols // wide,
        specs,
        out_spec,
        [pltpu.VMEM((total, depth), jnp.bfloat16)],
    )(where, *operands)


def mix_kernel(where_ref, hidden_ref, gate_ref, block_ref, out_ref):
    mixed = hidden_ref[...].astype(jnp.float32) + gate_ref[...] * block_ref[0].astype(jnp.float32)
    out_ref[...] = mixed.astype(jnp.bfloat16)


def mix(where, hidden_in, attn_gate, blocks):
    rows, width = hidden_in.shape
    n_patch, _, cols = blocks.shape
    if cols % HEAD_DIM:
        projected = blocks.transpose(1, 0, 2).reshape(rows, width).astype(jnp.float32)
        return (hidden_in.astype(jnp.float32) + attn_gate * projected).astype(jnp.bfloat16)
    return call(
        mix_kernel,
        "mix",
        jax.ShapeDtypeStruct((rows, width), jnp.bfloat16),
        n_patch,
        [
            pl.BlockSpec((rows, cols), lambda i, w: (0, i)),
            pl.BlockSpec((1, cols), lambda i, w: (0, i)),
            pl.BlockSpec((1, rows, cols), lambda i, w: (i, 0, 0)),
        ],
        pl.BlockSpec((rows, cols), lambda i, w: (0, i)),
    )(where, hidden_in, attn_gate[None], blocks)


def share_weight(sizes, split, per, out_weight):
    cols = out_weight.shape[1]
    own = out_weight.reshape(split, per, HEAD_DIM, cols)
    if per == sizes["grp"]:
        mine = lax.dynamic_index_in_dim(own, lax.axis_index("grp"), 1, keepdims=False)
        shared = lax.all_gather(mine, ("grp", "head", "sub"), axis=0, tiled=True)
        shared = shared.reshape(per, -1, cols)
        return [(shared, chunk) for chunk in range(per)]
    return [
        (
            lax.all_gather(own[:, chunk], ("head", "sub"), axis=0, tiled=True).reshape(1, -1, cols),
            0,
        )
        for chunk in range(per)
    ]


def gather(x, where, n_patch):
    if n_patch != 4:
        return [x] + [swap(x, "patch", n_patch, rel) for rel in range(1, n_patch)]
    far = swap(x, "patch", 4, 2)
    next_to = swap(x, "patch", 4, 1)
    middle = swap(x, "patch", 4, 3, (1, 2))
    ends = lax.ppermute(far, "patch", [(1, 0), (2, 3)])
    inner = (where[0] == 1) | (where[0] == 2)
    return [x, next_to, far, jnp.where(inner, middle, ends)]


def body(sizes, queries, fresh_kv, cached_kv, exponents, out_weight, hidden_in, attn_gate):
    n_patch, n_rel = sizes["patch"], sizes["head"] * sizes["sub"]
    heads = queries.shape[1] // HEAD_DIM
    split = math.gcd(heads, n_patch)
    per = heads // split
    patch_at = lax.axis_index("patch")
    where = jnp.stack([patch_at, patch_at % split, patch_at // split]).astype(jnp.int32)
    near, far = None, None
    if split < n_patch:
        near = [list(range(at, at + split)) for at in range(0, n_patch, split)]
        far = [list(range(at, n_patch, split)) for at in range(split)]

    weights = share_weight(sizes, split, per, out_weight)
    sent = pack(split, per, where, exponents, queries, fresh_kv, cached_kv)
    arrived = [lax.all_to_all(x, "patch", 0, 0, axis_index_groups=near) for x in sent]
    slots = []
    for x in arrived:
        everyone = x if far is None else lax.all_gather(
            x, "patch", axis=0, tiled=True, axis_index_groups=far
        )
        out = lax.all_to_all(attend(where, n_rel, x, everyone), ("head", "sub"), 0, 0)
        slots.append(gather(out.reshape(n_rel, -1, HEAD_DIM), where, n_patch))
    acc = None
    for chunk in range(per):
        acc = project(split, where, slots[chunk], weights[chunk], acc, chunk == per - 1)
    return mix(where, hidden_in, attn_gate, lax.all_to_all(acc, "patch", 0, 0))


def solution(mesh):
    in_specs = (
        P(("grp", "patch"), ("head", "sub")),
        P(None, ("grp", "patch"), ("head", "sub")),
        P(None, "grp", ("head", "sub")),
        P(None, ("grp", "patch"), ("head", "sub")),
        P(("head", "sub"), "patch"),
        P(("grp", "patch", "head", "sub"), None),
        P(),
    )
    out_specs = P(("grp", "patch", "head", "sub"), None)
    return jax.shard_map(
        functools.partial(body, dict(mesh.shape)),
        mesh=mesh,
        in_specs=in_specs,
        out_specs=out_specs,
        check_vma=False,
    )
```

time: 329 us -> 171 us (0.52)
  waiting for transfers between devices: 266 us -> 41.8 us
  blocking collectives: 12.6 us -> 65.4 us
  matrix products: 18.7 us -> 0 us
  Pallas kernels: 0 us -> 17.9 us
  starting transfers between devices: 0.08 us -> 16.7 us
  other arithmetic: 14 us -> 2.04 us
  local copies, waits for them, and re-layouts: 3.77 us -> 12.9 us
    all_gather x2 -> x1, waiting for transfers between devices: 232 us -> 0.01 us  [share_weight(): shared = lax.all_gather(mine, ('grp', 'head', 'sub'), axis=0, tiled=True)]
    all_to_all x0 -> x4, blocking collectives: none -> 65.4 us  [the longest x1 26.2 us: body(): lax.all_to_all(x, 'patch', 0, 0, axis_index_groups=near)]
    reduce_scatter x1 -> x0, waiting for transfers between devices: 33 us -> none  [body(): lax.psum_scatter(partial_terms.astype(jnp.bfloat16), ('head', 'sub'), sca...]
    all_to_all x0 -> x1, waiting for transfers between devices: none -> 23.9 us  [body(): lax.all_to_all(x, 'patch', 0, 0, axis_index_groups=near)]
    dot_general x3 -> x0, matrix products: 18.7 us -> none  [the longest x1 9.06 us: body(): jnp.einsum('hqk,khd->qhd', weights, value_heads, preferred_element_type=j...]
    ppermute x0 -> x8, waiting for transfers between devices: none -> 17.9 us  [the longest x6 14.1 us: swap(): return lax.ppermute(x, axes, pairs)]
    pallas_call x0 -> x6, Pallas kernels: none -> 17.9 us  [the longest x2 9.15 us: project(): call(functools.partial(project_kernel, split, len(slots), acc is not None...]
    ppermute x0 -> x8, starting transfers between devices: none -> 13.2 us  [the longest x6 10.6 us: swap(): return lax.ppermute(x, axes, pairs)]
  transfers between devices with their start and end apart: 3 -> 10, of which waited for: 3 -> 4; matrix products, arithmetic and copies ran while one was open for 6% -> 1% of each run, Pallas kernels for 0% -> 7%
where the time goes in v3:
time: 171 us; the launch traced here: 170 us
  blocking collectives  65.4 us (38%)
  waiting for transfers between devices  41.8 us (24%)
  Pallas kernels  17.9 us (10%)
  starting transfers between devices  16.7 us (10%)
  between operations  13.6 us (8%)
  local copies, waits for them, and re-layouts  12.9 us (8%)
  other arithmetic  2.04 us (1%)
    all_to_all x1, blocking collectives, body(): lax.all_to_all(x, 'patch', 0, 0, axis_index_groups=near)  26.2 us
    all_to_all x1, waiting for transfers between devices, body(): lax.all_to_all(x, 'patch', 0, 0, axis_index_groups=near)  23.9 us
    all_to_all x2, blocking collectives, body(): lax.all_to_all(attend(where, n_rel, x, everyone), ('head', 'sub'), 0, 0)  20.7 us
    all_to_all x1, blocking collectives, body(): return mix(where, hidden_in, attn_gate, lax.all_to_all(acc, 'patch', 0, 0))  18.5 us
    ppermute x6, waiting for transfers between devices, swap(): return lax.ppermute(x, axes, pairs)  14.1 us
    unnamed x30, local copies, waits for them, and re-layouts  11.8 us
    ppermute x6, starting transfers between devices, swap(): return lax.ppermute(x, axes, pairs)  10.6 us
    pallas_call x2, Pallas kernels, project(): call(functools.partial(project_kernel, split, len(slots), acc is not None...  9.15 us
  transfers between devices with their start and end apart: 10, of which 4 were waited for; matrix products, arithmetic and copies ran while one was open for 1% of the time, Pallas kernels for 7%

profile of v3, /device:TPU:0, one launch (start us, length us, event | category | flops | bytes accessed | tf_op | source)
XLA Modules:
  0.0 170.3 jit_solution(9199287100458159865)
XLA Ops:
  6.5 0.0 all-gather.3.cloned.1.call-start
  6.6 1.7 %copy-done = bf16[1024,1280]{1,0:T(8,128)(2,1)S(1)} copy-done((bf16[1024,1280]{1,0:T(8,128)(2,1)S(1)}, bf16[1024,1280]{1,0:T(8,128)(2,1)}, u32[]{:S(2)}) %copy-start) | copy-done | bytes 2621464
  8.3 1.1 constant_dynamic-slice_fusion
  9.4 0.0 all-gather.3.cloned.1.call-update
  9.5 0.1 pad_add_fusion.where_ref
  9.6 2.2 %copy-done.3 = bf16[2,1024,1024]{2,1,0:T(8,128)(2,1)S(1)} copy-done((bf16[2,1024,1024]{2,1,0:T(8,128)(2,1)S(1)}, bf16[2,1024,1024]{2,1,0:T(8,128)(2,1)}, u32[]{:S(2)}) %copy-start.3) | copy-done | bytes 4194328
  11.7 1.2 copy-done.5
  13.0 2.2 %pack.1 = (bf16[4,3,256,128]{3,2,1,0:T(8,128)(2,1)S(1)}, bf16[4,3,256,128]{3,2,1,0:T(8,128)(2,1)S(1)}) custom-call(s32[3]{0:T(128)S(1)} %pad_add_fusion.where_ref, s32[2,2,8]{2,1,0:T(2,128)S(1)} %copy-done.14, bf16[256,1024]{1,0:T(8,128)(2,1)S(1)} %copy-done.8, bf16[2,256,1024]{2,1,0:T(8,128)(2,1)S(1)} %copy-done.5, bf16[2,1024,1024]{2,1,0:T(8,128)(2,1)S(1)} %copy-done.3), custom_call_target="tpu_custom_call" | custom-call | tf_op jit(solution)/shard_map/pack/pallas_call | solution.py:67
  15.2 26.2 %all_to_all.25.q_ref.kv_ref = bf16[4,3,256,128]{3,2,1,0:T(8,128)(2,1)S(1)} all-to-all(bf16[4,3,256,128]{3,2,1,0:T(8,128)(2,1)S(1)} %get-tuple-element.8), channel_id=1, replica_groups=mesh['grp'=2,'patch'=4,'head'=2,'sub'=2] {'patch'}, dimensions={0} | all-to-all | bytes 1572864 | tf_op jit(solution)/shard_map/all_to_all | solution.py:243
  41.4 2.2 %attend.3 = bf16[4,4,64,128]{3,2,1,0:T(8,128)(2,1)S(1)} custom-call(s32[3]{0:T(128)S(1)} %pad_add_fusion.where_ref, bf16[4,3,256,128]{3,2,1,0:T(8,128)(2,1)S(1)} %all_to_all.25.q_ref.kv_ref, bf16[4,3,256,128]{3,2,1,0:T(8,128)(2,1)S(1)} %all_to_all.25.q_ref.kv_ref), custom_call_target="tpu_custom_call" | custom-call | tf_op jit(solution)/shard_map/attend/pallas_call | solution.py:104
  43.7 12.2 %all_to_all.26 = bf16[4,4,64,128]{3,2,1,0:T(8,128)(2,1)} all-to-all(bf16[4,4,64,128]{3,2,1,0:T(8,128)(2,1)S(1)} %attend.3), channel_id=1, replica_groups=mesh['grp'=2,'patch'=4,'head'=2,'sub'=2] {'head','sub'}, dimensions={0} | all-to-all | bytes 524288 | tf_op jit(solution)/shard_map/all_to_all | solution.py:249
  55.9 0.0 copy-done.6
  55.9 3.5 %all-to-all-start = ((bf16[4,3,256,128]{3,2,1,0:T(8,128)(2,1)}), bf16[4,3,256,128]{3,2,1,0:T(8,128)(2,1)S(1)}, u32[]{:S(2)}, u32[]{:S(2)}) async-start(bf16[4,3,256,128]{3,2,1,0:T(8,128)(2,1)} %copy-done.6), calls=%async_computation | async-start | bytes 1572864 | tf_op jit(solution)/shard_map/all_to_all | solution.py:243
  59.4 2.9 %collective-permute-start.5 = (bf16[4,256,128]{2,1,0:T(8,128)(2,1)}, bf16[4,256,128]{2,1,0:T(8,128)(2,1)}, u32[]{:S(2)}, u32[]{:S(2)}) collective-permute-start(bf16[4,256,128]{2,1,0:T(8,128)(2,1)} %bitcast.11), channel_id=1, source_target_pairs={{0,8},{4,12},{8,0},{12,4},{1,9},{5,13},{9,1},{13,5},{2,10},{6,14},... | collective-permute-start | bytes 786440 | tf_op jit(solution)/shard_map/ppermute | solution.py:40
  62.3 23.9 %all-to-all-done.q_ref.kv_ref = bf16[4,3,256,128]{3,2,1,0:T(8,128)(2,1)S(1)} async-done(((bf16[4,3,256,128]{3,2,1,0:T(8,128)(2,1)}), bf16[4,3,256,128]{3,2,1,0:T(8,128)(2,1)S(1)}, u32[]{:S(2)}, u32[]{:S(2)}) %all-to-all-start) | async-done | bytes 786464 | tf_op jit(solution)/shard_map/all_to_all | solution.py:243
  86.2 2.2 %attend.2 = bf16[4,4,64,128]{3,2,1,0:T(8,128)(2,1)S(1)} custom-call(s32[3]{0:T(128)S(1)} %pad_add_fusion.where_ref, bf16[4,3,256,128]{3,2,1,0:T(8,128)(2,1)S(1)} %all-to-all-done.q_ref.kv_ref, bf16[4,3,256,128]{3,2,1,0:T(8,128)(2,1)S(1)} %all-to-all-done.q_ref.kv_ref), custom_call_target="tpu_custom_call" | custom-call | tf_op jit(solution)/shard_map/attend/pallas_call | solution.py:104
  88.4 8.4 %all_to_all.27 = bf16[4,4,64,128]{3,2,1,0:T(8,128)(2,1)S(1)} all-to-all(bf16[4,4,64,128]{3,2,1,0:T(8,128)(2,1)S(1)} %attend.2), channel_id=1, replica_groups=mesh['grp'=2,'patch'=4,'head'=2,'sub'=2] {'head','sub'}, dimensions={0} | all-to-all | bytes 524288 | tf_op jit(solution)/shard_map/all_to_all | solution.py:249
  96.8 0.0 collective-permute-start.1
  96.8 1.4 collective-permute-start.6
  98.2 0.0 collective-permute-done.5.refs_2_
  98.2 1.3 collective-permute-start.7
  99.5 1.4 collective-permute-start.2
  100.8 9.5 %collective-permute-done.1.refs_2_ = bf16[4,256,128]{2,1,0:T(8,128)(2,1)S(1)} collective-permute-done((bf16[4,256,128]{2,1,0:T(8,128)(2,1)S(1)}, bf16[4,256,128]{2,1,0:T(8,128)(2,1)S(1)}, u32[]{:S(2)}, u32[]{:S(2)}) %collective-permute-start.1) | collective-permute-done | bytes 262176 | tf_op jit(solution)/shard_map/ppermute | solution.py:40
  110.3 1.3 collective-permute-start.3
  111.6 3.3 %collective-permute-start.4 = (bf16[4,256,128]{2,1,0:T(8,128)(2,1)}, bf16[4,256,128]{2,1,0:T(8,128)(2,1)S(1)}, u32[]{:S(2)}, u32[]{:S(2)}) collective-permute-start(bf16[4,256,128]{2,1,0:T(8,128)(2,1)} %bitcast.13), channel_id=1, source_target_pairs={{0,4},{4,0},{8,12},{12,8},{1,5},{5,1},{9,13},{13,9},{2,6},{6,2},{1... | collective-permute-start | bytes 786440 | tf_op jit(solution)/shard_map/ppermute | solution.py:40
  115.0 0.0 collective-permute-done.6
  115.0 1.6 collective-permute-start
  116.6 0.0 collective-permute-done.7
  116.6 1.0 broadcast_select_fusion.refs_3_
  117.6 0.0 collective-permute-done.2
  117.6 0.0 copy-done.11
  117.6 3.9 %collective-permute-done.3 = bf16[4,256,128]{2,1,0:T(8,128)(2,1)} collective-permute-done((bf16[4,256,128]{2,1,0:T(8,128)(2,1)S(1)}, bf16[4,256,128]{2,1,0:T(8,128)(2,1)}, u32[]{:S(2)}, u32[]{:S(2)}) %collective-permute-start.3) | collective-permute-done | bytes 262176 | tf_op jit(solution)/shard_map/ppermute | solution.py:224
  121.5 1.0 broadcast_select_fusion.1.refs_3_
  122.5 4.5 %collective-permute-done.4.refs_1_ = bf16[4,256,128]{2,1,0:T(8,128)(2,1)S(1)} collective-permute-done((bf16[4,256,128]{2,1,0:T(8,128)(2,1)}, bf16[4,256,128]{2,1,0:T(8,128)(2,1)S(1)}, u32[]{:S(2)}, u32[]{:S(2)}) %collective-permute-start.4) | collective-permute-done | bytes 262176 | tf_op jit(solution)/shard_map/ppermute | solution.py:40
  127.0 0.7 copy-done.9
  127.7 4.0 %copy-done.1 = bf16[32,1,128,1280]{3,2,1,0:T(8,128)(2,1)S(1)} copy-done((bf16[32,1,128,1280]{3,2,1,0:T(8,128)(2,1)S(1)}, bf16[32,1,128,1280]{3,2,1,0:T(8,128)(2,1)}, u32[]{:S(2)}) %copy-start.1) | copy-done | bytes 10485784
  131.7 0.9 copy-done.4
  132.7 0.9 copy-done.10
  133.6 4.6 %project.2.refs_5_ = f32[256,1280]{1,0:T(8,128)S(1)} custom-call(s32[3]{0:T(128)S(1)} %pad_add_fusion.where_ref, bf16[4,256,128]{2,1,0:T(8,128)(2,1)S(1)} %bitcast.14, bf16[4,256,128]{2,1,0:T(8,128)(2,1)S(1)} %copy-done.10, bf16[4,256,128]{2,1,0:T(8,128)(2,1)} %collective-permute-done.5.refs_2_, bf16[4,256,128]{2,1,0:T(8,128)(2,1)S(1)} %broadcast_select_fusion.refs_3_, ...), custom_call_target="tpu_custom_call" | custom-call | tf_op jit(solution)/shard_map/project/pallas_call | solution.py:165
  138.3 0.0 copy-start.7
  138.3 0.0 copy-start.13
  138.3 0.0 collective-permute-done.refs_1_
  138.3 0.0 copy-done.2
  138.3 0.0 copy-done.12
  138.3 4.5 %project.3 = bf16[4,64,1280]{2,1,0:T(8,128)(2,1)S(1)} custom-call(s32[3]{0:T(128)S(1)} %pad_add_fusion.where_ref, bf16[4,256,128]{2,1,0:T(8,128)(2,1)S(1)} %bitcast.18, bf16[4,256,128]{2,1,0:T(8,128)(2,1)} %collective-permute-done.refs_1_, bf16[4,256,128]{2,1,0:T(8,128)(2,1)S(1)} %copy-done.12, bf16[4,256,128]{2,1,0:T(8,128)(2,1)S(1)} %broadcast_select_fusion.1.refs_3_, ...), custom_call_target="tpu_custom_call" | custom-call | tf_op jit(solution)/shard_map/project/pallas_call | solution.py:165
  142.8 18.5 %all_to_all.28.block_ref = bf16[4,64,1280]{2,1,0:T(8,128)(2,1)S(1)} all-to-all(bf16[4,64,1280]{2,1,0:T(8,128)(2,1)S(1)} %project.3), channel_id=1, replica_groups=mesh['grp'=2,'patch'=4,'head'=2,'sub'=2] {'patch'}, dimensions={0} | all-to-all | bytes 1310720 | tf_op jit(solution)/shard_map/all_to_all | solution.py:254
  161.4 0.0 copy-done.13
  161.4 2.1 %mix.1 = bf16[64,5120]{1,0:T(8,128)(2,1)} custom-call(s32[3]{0:T(128)S(1)} %pad_add_fusion.where_ref, bf16[64,5120]{1,0:T(8,128)(2,1)S(1)} %copy-done.7, f32[1,5120]{1,0:T(1,128)S(1)} %bitcast.19, bf16[4,64,1280]{2,1,0:T(8,128)(2,1)S(1)} %all_to_all.28.block_ref), custom_call_target="tpu_custom_call" | custom-call | tf_op jit(solution)/shard_map/mix/pallas_call | solution.py:187
  (17 shorter events, 0.0 us)
Async XLA Ops:
  6.5 1.7 %copy-start = (bf16[1024,1280]{1,0:T(8,128)(2,1)S(1)}, bf16[1024,1280]{1,0:T(8,128)(2,1)}, u32[]{:S(2)}) copy-start(bf16[1024,1280]{1,0:T(8,128)(2,1)} %param.11) | copy-start | bytes 7864324
  6.5 3.0 %copy-start.14 = (s32[2,2,8]{2,1,0:T(2,128)S(1)}, s32[2,2,8]{2,1,0:T(2,128)}, u32[]{:S(2)}) copy-start(s32[2,2,8]{2,1,0:T(2,128)} %exps_ref.1) | copy-start | bytes 388
  6.5 3.0 %copy-start.8 = (bf16[256,1024]{1,0:T(8,128)(2,1)S(1)}, bf16[256,1024]{1,0:T(8,128)(2,1)}, u32[]{:S(2)}) copy-start(bf16[256,1024]{1,0:T(8,128)(2,1)} %q_ref.1) | copy-start | bytes 1572868
  6.5 121.2 %all-gather.3.cloned.1.call-start = ((), (), s32[]{:S(2)}) async-start(), calls=%async_computation.5 | async-start | bytes 11796480 | tf_op jit(solution)/shard_map/all_gather | solution.py:206
  9.6 2.2 %copy-start.3 = (bf16[2,1024,1024]{2,1,0:T(8,128)(2,1)S(1)}, bf16[2,1024,1024]{2,1,0:T(8,128)(2,1)}, u32[]{:S(2)}) copy-start(bf16[2,1024,1024]{2,1,0:T(8,128)(2,1)} %cached_ref.1) | copy-start | bytes 12582916
  11.7 1.2 copy-start.5
  15.2 40.7 %copy-start.6 = (bf16[4,3,256,128]{3,2,1,0:T(8,128)(2,1)}, bf16[4,3,256,128]{3,2,1,0:T(8,128)(2,1)S(1)}, u32[]{:S(2)}) copy-start(bf16[4,3,256,128]{3,2,1,0:T(8,128)(2,1)S(1)} %get-tuple-element.7) | copy-start | bytes 2359300
  55.9 30.3 %all-to-all-start = ((bf16[4,3,256,128]{3,2,1,0:T(8,128)(2,1)}), bf16[4,3,256,128]{3,2,1,0:T(8,128)(2,1)S(1)}, u32[]{:S(2)}, u32[]{:S(2)}) async-start(bf16[4,3,256,128]{3,2,1,0:T(8,128)(2,1)} %copy-done.6), calls=%async_computation | async-start | bytes 1572864 | tf_op jit(solution)/shard_map/all_to_all | solution.py:243
  59.4 38.8 %collective-permute-start.5 = (bf16[4,256,128]{2,1,0:T(8,128)(2,1)}, bf16[4,256,128]{2,1,0:T(8,128)(2,1)}, u32[]{:S(2)}, u32[]{:S(2)}) collective-permute-start(bf16[4,256,128]{2,1,0:T(8,128)(2,1)} %bitcast.11), channel_id=1, source_target_pairs={{0,8},{4,12},{8,0},{12,4},{1,9},{5,13},{9,1},{13,5},{2,10},{6,14},... | collective-permute-start | bytes 786440 | tf_op jit(solution)/shard_map/ppermute | solution.py:40
  96.8 13.5 %collective-permute-start.1 = (bf16[4,256,128]{2,1,0:T(8,128)(2,1)S(1)}, bf16[4,256,128]{2,1,0:T(8,128)(2,1)S(1)}, u32[]{:S(2)}, u32[]{:S(2)}) collective-permute-start(bf16[4,256,128]{2,1,0:T(8,128)(2,1)S(1)} %bitcast.15), channel_id=1, source_target_pairs={{0,8},{4,12},{8,0},{12,4},{1,9},{5,13},{9,1},{13,5},{2,10},{6,14},... | collective-permute-start | bytes 786440 | tf_op jit(solution)/shard_map/ppermute | solution.py:40
  96.8 18.2 %collective-permute-start.6 = (bf16[4,256,128]{2,1,0:T(8,128)(2,1)}, bf16[4,256,128]{2,1,0:T(8,128)(2,1)}, u32[]{:S(2)}, u32[]{:S(2)}) collective-permute-start(bf16[4,256,128]{2,1,0:T(8,128)(2,1)} %bitcast.12), channel_id=1, source_target_pairs={{4,8},{8,4},{5,9},{9,5},{6,10},{10,6},{7,11},{11,7},{20,24},{24,20... | collective-permute-start | bytes 786440 | tf_op jit(solution)/shard_map/ppermute | solution.py:40
  98.2 18.5 %collective-permute-start.7 = (bf16[4,256,128]{2,1,0:T(8,128)(2,1)}, bf16[4,256,128]{2,1,0:T(8,128)(2,1)}, u32[]{:S(2)}, u32[]{:S(2)}) collective-permute-start(bf16[4,256,128]{2,1,0:T(8,128)(2,1)} %collective-permute-done.5.refs_2_), channel_id=1, source_target_pairs={{4,0},{8,12},{5,1},{9,13},{6,2},{10,14},{7,3},{11,15},{20,16},{24,... | collective-permute-start | bytes 786440 | tf_op jit(solution)/shard_map/ppermute | solution.py:224
  99.5 18.2 %collective-permute-start.2 = (bf16[4,256,128]{2,1,0:T(8,128)(2,1)S(1)}, bf16[4,256,128]{2,1,0:T(8,128)(2,1)}, u32[]{:S(2)}, u32[]{:S(2)}) collective-permute-start(bf16[4,256,128]{2,1,0:T(8,128)(2,1)S(1)} %bitcast.16), channel_id=1, source_target_pairs={{4,8},{8,4},{5,9},{9,5},{6,10},{10,6},{7,11},{11,7},{20,24},{24,20... | collective-permute-start | bytes 786440 | tf_op jit(solution)/shard_map/ppermute | solution.py:40
  110.3 7.3 %copy-start.11 = (bf16[4,256,128]{2,1,0:T(8,128)(2,1)}, bf16[4,256,128]{2,1,0:T(8,128)(2,1)S(1)}, u32[]{:S(2)}) copy-start(bf16[4,256,128]{2,1,0:T(8,128)(2,1)S(1)} %collective-permute-done.1.refs_2_) | copy-start | bytes 786436
  110.3 11.2 %collective-permute-start.3 = (bf16[4,256,128]{2,1,0:T(8,128)(2,1)S(1)}, bf16[4,256,128]{2,1,0:T(8,128)(2,1)}, u32[]{:S(2)}, u32[]{:S(2)}) collective-permute-start(bf16[4,256,128]{2,1,0:T(8,128)(2,1)S(1)} %collective-permute-done.1.refs_2_), channel_id=1, source_target_pairs={{4,0},{8,12},{5,1},{9,13},{6,2},{10,14},{7,3},{11,15},{20,16},{24,... | collective-permute-start | bytes 786440 | tf_op jit(solution)/shard_map/ppermute | solution.py:224
  111.6 15.4 %collective-permute-start.4 = (bf16[4,256,128]{2,1,0:T(8,128)(2,1)}, bf16[4,256,128]{2,1,0:T(8,128)(2,1)S(1)}, u32[]{:S(2)}, u32[]{:S(2)}) collective-permute-start(bf16[4,256,128]{2,1,0:T(8,128)(2,1)} %bitcast.13), channel_id=1, source_target_pairs={{0,4},{4,0},{8,12},{12,8},{1,5},{5,1},{9,13},{13,9},{2,6},{6,2},{1... | collective-permute-start | bytes 786440 | tf_op jit(solution)/shard_map/ppermute | solution.py:40
  115.0 23.3 %collective-permute-start = (bf16[4,256,128]{2,1,0:T(8,128)(2,1)S(1)}, bf16[4,256,128]{2,1,0:T(8,128)(2,1)}, u32[]{:S(2)}, u32[]{:S(2)}) collective-permute-start(bf16[4,256,128]{2,1,0:T(8,128)(2,1)S(1)} %bitcast.17), channel_id=1, source_target_pairs={{0,4},{4,0},{8,12},{12,8},{1,5},{5,1},{9,13},{13,9},{2,6},{6,2},{1... | collective-permute-start | bytes 786440 | tf_op jit(solution)/shard_map/ppermute | solution.py:40
  127.0 0.7 copy-start.9
  127.7 4.0 %copy-start.1 = (bf16[32,1,128,1280]{3,2,1,0:T(8,128)(2,1)S(1)}, bf16[32,1,128,1280]{3,2,1,0:T(8,128)(2,1)}, u32[]{:S(2)}) copy-start(bf16[32,1,128,1280]{3,2,1,0:T(8,128)(2,1)} %all-gather.3.cloned.1.call-done) | copy-start | bytes 31457284
  131.7 0.9 copy-start.4
  132.7 0.9 copy-start.10
  133.6 4.7 %copy-start.2 = (bf16[32,1,128,1280]{3,2,1,0:T(8,128)(2,1)S(1)}, bf16[32,1,128,1280]{3,2,1,0:T(8,128)(2,1)}, u32[]{:S(2)}) copy-start(bf16[32,1,128,1280]{3,2,1,0:T(8,128)(2,1)} %all-gather.3.cloned.1.call-done) | copy-start | bytes 31457284
  133.6 4.7 %copy-start.12 = (bf16[4,256,128]{2,1,0:T(8,128)(2,1)S(1)}, bf16[4,256,128]{2,1,0:T(8,128)(2,1)}, u32[]{:S(2)}) copy-start(bf16[4,256,128]{2,1,0:T(8,128)(2,1)} %copy-done.11) | copy-start | bytes 786436
  138.3 23.1 %copy-start.7 = (bf16[64,5120]{1,0:T(8,128)(2,1)S(1)}, bf16[64,5120]{1,0:T(8,128)(2,1)}, u32[]{:S(2)}) copy-start(bf16[64,5120]{1,0:T(8,128)(2,1)} %hidden_ref.1) | copy-start | bytes 1966084
  138.3 23.1 %copy-start.13 = (f32[5120]{0:T(1024)S(1)}, f32[5120]{0:T(1024)}, u32[]{:S(2)}) copy-start(f32[5120]{0:T(1024)} %param.13) | copy-start | bytes 61444
Sparse Core Ops, SparseCore 0:
  9.6 68.3 all-gather.2

commit v4 on v3

v4 whole, which is shorter than its diff:
```python
import functools
import math

import jax
import jax.numpy as jnp
from jax import lax
from jax.experimental import pallas as pl
from jax.experimental.pallas import tpu as pltpu
from jax.sharding import PartitionSpec as P

HEAD_DIM = 128
SCALE_ROWS = 128
SATURATION = 448.0
VMEM_BYTES = 32 * 1024 * 1024
ATTEND_FLOPS = 20_000_000_000
PACK_VMEM_BYTES = 60 * 1024 * 1024


def spec(shape):
    return pl.BlockSpec(shape, lambda i, w: (0,) * len(shape))


def call(kernel, name, out_shape, grid, in_specs, out_specs, scratch=(), cost=None, vmem=VMEM_BYTES):
    return pl.pallas_call(
        kernel,
        out_shape=out_shape,
        grid_spec=pltpu.PrefetchScalarGridSpec(
            num_scalar_prefetch=1,
            grid=(grid,),
            in_specs=in_specs,
            out_specs=out_specs,
            scratch_shapes=list(scratch),
        ),
        compiler_params=pltpu.CompilerParams(vmem_limit_bytes=vmem),
        cost_estimate=cost,
        name=name,
    )


def swap(x, axes, count, mask, only=None):
    pairs = [(at, at ^ mask) for at in range(count) if only is None or at in only]
    return lax.ppermute(x, axes, pairs)


def piece_place(split, per, rel, chunk):
    if rel < 2:
        return rel, chunk
    return 2 + chunk * (split - 2) + rel - 2, 0


def pack_kernel(split, per, where_ref, exps_ref, q_ref, fresh_ref, cached_ref, *outs):
    rows = q_ref.shape[0]
    block = pl.program_id(0) * rows // SCALE_ROWS
    for chunk in range(per):
        for rel in range(split):
            number, index = piece_place(split, per, rel, chunk)
            out = outs[number].at[index]
            head = (where_ref[1] ^ rel) * per + chunk
            lanes = pl.ds(pl.multiple_of(head * HEAD_DIM, HEAD_DIM), HEAD_DIM)
            out[0] = q_ref[:, lanes]
            for stacked in range(2):
                power = jnp.full((1, HEAD_DIM), exps_ref[stacked, block, head].astype(jnp.float32))
                cached = cached_ref[stacked, :, lanes].astype(jnp.float32)
                residual = fresh_ref[stacked, :, lanes].astype(jnp.float32) - cached
                codes = jnp.clip(
                    residual * jnp.exp2(-power), -SATURATION, SATURATION
                ).astype(jnp.bfloat16)
                decoded = cached + codes.astype(jnp.float32) * jnp.exp2(power)
                out[1 + stacked] = decoded.astype(jnp.bfloat16)


def pack(split, per, where, exponents, queries, fresh_kv, cached_kv):
    tok, channels = queries.shape
    rows = SCALE_ROWS // 2
    steps = tok // rows
    sizes = [per] * 2 + [1] * (per * (split - 2))
    return call(
        functools.partial(pack_kernel, split, per),
        "pack",
        [jax.ShapeDtypeStruct((size, 3, tok, HEAD_DIM), jnp.bfloat16) for size in sizes],
        steps,
        [
            pl.BlockSpec(memory_space=pltpu.SMEM),
            pl.BlockSpec((rows, channels), lambda i, w: (i, 0)),
            pl.BlockSpec((2, rows, channels), lambda i, w: (0, i, 0)),
            pl.BlockSpec((2, rows, channels), lambda i, w: (0, w[0] * steps + i, 0)),
        ],
        [pl.BlockSpec((size, 3, rows, HEAD_DIM), lambda i, w: (0, 0, i, 0)) for size in sizes],
        vmem=PACK_VMEM_BYTES,
    )(where, exponents, queries, fresh_kv, cached_kv)


def attend_kernel(split, n_kv, where_ref, *refs):
    q_refs, kv_refs, outs = refs[:split], refs[split : split + n_kv], refs[split + n_kv : -1]
    mix_ref = refs[-1]
    factor = HEAD_DIM**-0.5 * math.log2(math.e)
    keys = jnp.concatenate([ref[0, 1] for ref in kv_refs], axis=0)
    values = jnp.concatenate([ref[0, 2] for ref in kv_refs], axis=0)
    values = jnp.concatenate([values, jnp.ones_like(values)], axis=1)
    for rel in range(split):
        scores = lax.dot_general(
            q_refs[rel][0, 0], keys, (((1,), (1,)), ((), ())), preferred_element_type=jnp.float32
        )
        peak = jnp.max(scores, axis=1, keepdims=True)
        expo = jnp.exp2((scores - peak) * factor).astype(jnp.bfloat16)
        mix = jnp.dot(expo, values, preferred_element_type=jnp.float32)
        mix = mix[:, :HEAD_DIM] / mix[:, HEAD_DIM:]
        mix_ref[rel] = mix.reshape(mix_ref.shape[1:])
        for at, out in enumerate(outs):
            out[where_ref[1] ^ rel] = mix_ref[rel, where_ref[3] ^ at].astype(jnp.bfloat16)


def attend(where, n_rel, pieces, kv_pieces):
    split = len(pieces)
    _, _, tok, feat = pieces[0][0].shape
    rows = tok // n_rel
    out = jax.ShapeDtypeStruct((split, rows, feat), jnp.bfloat16)
    return call(
        functools.partial(attend_kernel, split, len(kv_pieces)),
        "attend",
        [out] * n_rel,
        1,
        [
            pl.BlockSpec((1, 3, tok, feat), lambda i, w, at=at: (at, 0, 0, 0))
            for _, at in pieces + kv_pieces
        ],
        [spec(out.shape)] * n_rel,
        [pltpu.VMEM((split, n_rel, rows, feat), jnp.float32)],
        pl.CostEstimate(flops=ATTEND_FLOPS, bytes_accessed=0, transcendentals=0),
    )(where, *[x for x, _ in pieces + kv_pieces])


def project_kernel(split, n_slots, with_acc, last, where_ref, *refs):
    slots, weight_ref, refs = refs[:n_slots], refs[n_slots], refs[n_slots + 1 :]
    acc_ref, refs = (refs[0], refs[1:]) if with_acc else (None, refs)
    outs, held_ref = refs[:-2], refs[-2]
    out_ref = outs[0]
    n_rel, rows, _ = slots[0].shape

    @pl.when(pl.program_id(0) == 0)
    def arrange():
        for at, slot in enumerate(slots):
            group, near = divmod(at, split)
            for rel in range(n_rel):
                lane = ((where_ref[3] ^ rel) * split + (where_ref[1] ^ near)) * HEAD_DIM
                held_ref[
                    group * rows : (group + 1) * rows,
                    pl.ds(pl.multiple_of(lane, HEAD_DIM), HEAD_DIM),
                ] = slot[rel]

    acc = jnp.dot(held_ref[...], weight_ref[0], preferred_element_type=jnp.float32)
    if with_acc:
        acc += acc_ref[...]
    if not last:
        out_ref[...] = acc
    else:
        full_ref = refs[-1]
        full_ref[...] = acc.reshape(full_ref.shape)
        for at, out in enumerate(outs):
            group, near = divmod(at, split)
            out[...] = full_ref[group, where_ref[1] ^ near].astype(jnp.bfloat16)


def project(split, where, slots, weight_at, acc, last):
    weight, index = weight_at
    n_rel, rows, _ = slots[0].shape
    total = rows * len(slots) // split
    _, depth, cols = weight.shape
    wide = 256 if cols % 256 == 0 else cols
    whole = pl.BlockSpec((total, wide), lambda i, w: (0, i))
    specs = [spec(slots[0].shape)] * len(slots)
    specs.append(pl.BlockSpec((1, depth, wide), lambda i, w: (index, 0, i)))
    if acc is not None:
        specs.append(whole)
    scratch = [pltpu.VMEM((total, depth), jnp.bfloat16)]
    if last:
        piece = rows // split
        out = [jax.ShapeDtypeStruct((piece, cols), jnp.bfloat16)] * len(slots)
        out_spec = [pl.BlockSpec((piece, wide), lambda i, w: (0, i))] * len(slots)
        scratch.append(pltpu.VMEM((len(slots) // split, split, piece, wide), jnp.float32))
    else:
        out = jax.ShapeDtypeStruct((total, cols), jnp.float32)
        out_spec = whole
        scratch.append(pltpu.VMEM((8, HEAD_DIM), jnp.float32))
    operands = [*slots, weight] + ([] if acc is None else [acc])
    return call(
        functools.partial(project_kernel, split, len(slots), acc is not None, last),
        "project",
        out,
        cols // wide,
        specs,
        out_spec,
        scratch,
    )(where, *operands)


def mix_kernel(n_patch, where_ref, hidden_ref, gate_ref, *refs):
    out_ref = refs[-1]
    cols = refs[0].shape[1]
    for rel in range(n_patch):
        lanes = pl.ds(pl.multiple_of((where_ref[0] ^ rel) * cols, HEAD_DIM), cols)
        mixed = hidden_ref[:, lanes].astype(jnp.float32) + gate_ref[:, lanes] * refs[rel][
            ...
        ].astype(jnp.float32)
        out_ref[:, lanes] = mixed.astype(jnp.bfloat16)


def mix(where, hidden_in, attn_gate, blocks):
    rows, width = hidden_in.shape
    n_patch, cols = len(blocks), blocks[0].shape[1]
    if cols % HEAD_DIM:
        order = jnp.stack(blocks)[where[0] ^ jnp.arange(n_patch)]
        projected = order.transpose(1, 0, 2).reshape(rows, width).astype(jnp.float32)
        return (hidden_in.astype(jnp.float32) + attn_gate * projected).astype(jnp.bfloat16)
    return call(
        functools.partial(mix_kernel, n_patch),
        "mix",
        jax.ShapeDtypeStruct((rows, width), jnp.bfloat16),
        1,
        [spec((rows, width)), spec((1, width))] + [spec(blocks[0].shape)] * n_patch,
        spec((rows, width)),
    )(where, hidden_in, attn_gate[None], *blocks)


def share_weight(sizes, split, per, out_weight):
    cols = out_weight.shape[1]
    own = out_weight.reshape(split, per, HEAD_DIM, cols)
    if per == sizes["grp"]:
        mine = lax.dynamic_index_in_dim(own, lax.axis_index("grp"), 1, keepdims=False)
        shared = lax.all_gather(mine, ("grp", "head", "sub"), axis=0, tiled=True)
        shared = shared.reshape(per, -1, cols)
        return [(shared, chunk) for chunk in range(per)]
    return [
        (
            lax.all_gather(own[:, chunk], ("head", "sub"), axis=0, tiled=True).reshape(1, -1, cols),
            0,
        )
        for chunk in range(per)
    ]


def gather(x, where, n_patch):
    if n_patch != 4:
        return [x] + [swap(x, "patch", n_patch, rel) for rel in range(1, n_patch)]
    far = swap(x, "patch", 4, 2)
    next_to = swap(x, "patch", 4, 1)
    middle = swap(x, "patch", 4, 3, (1, 2))
    far, next_to = lax.optimization_barrier((far, next_to))
    ends = lax.ppermute(far, "patch", [(1, 0), (2, 3)])
    inner = (where[0] == 1) | (where[0] == 2)
    return [x, next_to, far, jnp.where(inner, middle, ends)]


def body(sizes, queries, fresh_kv, cached_kv, exponents, out_weight, hidden_in, attn_gate):
    n_patch, n_rel = sizes["patch"], sizes["head"] * sizes["sub"]
    heads = queries.shape[1] // HEAD_DIM
    split = math.gcd(heads, n_patch)
    per = heads // split
    patch_at = lax.axis_index("patch")
    rel_at = lax.axis_index("head") * sizes["sub"] + lax.axis_index("sub")
    where = jnp.stack([patch_at, patch_at % split, patch_at // split, rel_at]).astype(jnp.int32)

    sent = pack(split, per, where, exponents, queries, fresh_kv, cached_kv)
    sent, out_weight = lax.optimization_barrier((sent, out_weight))
    arrived = [sent[0], swap(sent[1], "patch", n_patch, 1)]
    for at, x in enumerate(sent[2:]):
        arrived.append(swap(x, "patch", n_patch, 2 + at % (split - 2)))
    weights = share_weight(sizes, split, per, out_weight)
    slots = []
    for chunk in range(per):
        pieces = []
        for rel in range(split):
            number, index = piece_place(split, per, rel, chunk)
            pieces.append((arrived[number], index))
        kv_pieces = list(pieces)
        for rel in range(split, n_patch, split):
            kv_pieces += [(swap(x, "patch", n_patch, rel), at) for x, at in pieces]
        out = attend(where, n_rel, pieces, kv_pieces)
        out = [out[0]] + [swap(out[rel], ("head", "sub"), n_rel, rel) for rel in range(1, n_rel)]
        joined = jnp.stack([x.reshape(-1, HEAD_DIM) for x in out])
        slots.append(gather(joined, where, n_patch))
    acc = None
    for chunk in range(per):
        acc = project(split, where, slots[chunk], weights[chunk], acc, chunk == per - 1)
    blocks = [acc[0]] + [swap(acc[rel], "patch", n_patch, rel) for rel in range(1, n_patch)]
    return mix(where, hidden_in, attn_gate, blocks)


def solution(mesh):
    in_specs = (
        P(("grp", "patch"), ("head", "sub")),
        P(None, ("grp", "patch"), ("head", "sub")),
        P(None, "grp", ("head", "sub")),
        P(None, ("grp", "patch"), ("head", "sub")),
        P(("head", "sub"), "patch"),
        P(("grp", "patch", "head", "sub"), None),
        P(),
    )
    out_specs = P(("grp", "patch", "head", "sub"), None)
    return jax.shard_map(
        functools.partial(body, dict(mesh.shape)),
        mesh=mesh,
        in_specs=in_specs,
        out_specs=out_specs,
        check_vma=False,
    )
```

time: 171 us -> 139 us (0.81)
  blocking collectives: 65.4 us -> 0 us
  starting transfers between devices: 16.7 us -> 38.9 us
  waiting for transfers between devices: 41.8 us -> 54.1 us
  local copies, waits for them, and re-layouts: 12.9 us -> 9.18 us
    all_to_all x4 -> x0, blocking collectives: 65.4 us -> none  [the longest x1 26.2 us: body(): lax.all_to_all(x, 'patch', 0, 0, axis_index_groups=near)]
    ppermute x6 -> x20, waiting for transfers between devices: 14.1 us -> 46.4 us  [swap(): return lax.ppermute(x, axes, pairs)]
    ppermute x6 -> x20, starting transfers between devices: 10.6 us -> 36.3 us  [swap(): return lax.ppermute(x, axes, pairs)]
    all_to_all x1 -> x0, waiting for transfers between devices: 23.9 us -> none  [body(): lax.all_to_all(x, 'patch', 0, 0, axis_index_groups=near)]
    ppermute x2, waiting for transfers between devices: 3.88 us -> 7.68 us  [gather(): ends = lax.ppermute(far, 'patch', [(1, 0), (2, 3)])]
    unnamed x30 -> x32, local copies, waits for them, and re-layouts: 11.8 us -> 8.03 us
    all_to_all x1 -> x0, starting transfers between devices: 3.49 us -> none  [body(): lax.all_to_all(x, 'patch', 0, 0, axis_index_groups=near)]
    pallas_call x4, Pallas kernels: 8.77 us -> 11.1 us  [the longest x1 4.93 us: pack(): call(functools.partial(pack_kernel, split, per), 'pack', [jax.ShapeDtypeS...]
  transfers between devices with their start and end apart: 10 -> 23, of which waited for: 4 -> 12; matrix products, arithmetic and copies ran while one was open for 1% -> 2% of each run, Pallas kernels for 7% -> 3%
where the time goes in v4:
time: 139 us
  waiting for transfers between devices  54.1 us (39%)
  starting transfers between devices  38.9 us (28%)
  Pallas kernels  19.6 us (14%)
  between operations  13.6 us (10%)
  local copies, waits for them, and re-layouts  9.18 us (7%)
  other arithmetic  3.4 us (2%)
    ppermute x20, waiting for transfers between devices, swap(): return lax.ppermute(x, axes, pairs)  46.4 us
    ppermute x20, starting transfers between devices, swap(): return lax.ppermute(x, axes, pairs)  36.3 us
    pallas_call x2, Pallas kernels, project(): call(functools.partial(project_kernel, split, len(slots), acc is not None...  8.5 us
    unnamed x32, local copies, waits for them, and re-layouts  8.03 us
    ppermute x2, waiting for transfers between devices, gather(): ends = lax.ppermute(far, 'patch', [(1, 0), (2, 3)])  7.68 us
    pallas_call x1, Pallas kernels, pack(): call(functools.partial(pack_kernel, split, per), 'pack', [jax.ShapeDtypeS...  4.93 us
    pallas_call x2, Pallas kernels, attend(): call(functools.partial(attend_kernel, split, len(kv_pieces)), 'attend', [...  4.57 us
  transfers between devices with their start and end apart: 23, of which 12 were waited for; matrix products, arithmetic and copies ran while one was open for 2% of the time, Pallas kernels for 3%

profile of v4, /device:TPU:0, one launch (start us, length us, event | category | flops | bytes accessed | tf_op | source)
XLA Modules:
  0.0 138.8 jit_solution(11875792315241179879)
XLA Ops:
  6.5 0.7 pad_add_fusion.where_ref
  7.2 4.9 %pack.1 = (bf16[2,3,256,128]{3,2,1,0:T(8,128)(2,1)}, bf16[2,3,256,128]{3,2,1,0:T(8,128)(2,1)}, bf16[1,3,256,128]{3,2,1,0:T(8,128)(2,1)}, bf16[1,3,256,128]{3,2,1...) custom-call(s32[4]{0:T(128)} %pad_add_fusion.where_ref, s32[2,2,8]{2,1,0:T(2,128)} %exps_ref.1, ...), custom_call_target="tpu_custom_call" | custom-call | tf_op jit(solution)/shard_map/pack/pallas_call | solution.py:77
  12.2 1.1 constant_dynamic-slice_fusion
  13.3 0.0 all-gather.3.cloned.1.call-update
  13.3 0.0 copy-start.14
  13.4 3.1 %collective-permute-start = (bf16[2,3,256,128]{3,2,1,0:T(8,128)(2,1)S(1)}, bf16[2,3,256,128]{3,2,1,0:T(8,128)(2,1)S(1)}, u32[]{:S(2)}, u32[]{:S(2)}) collective-permute-start(bf16[2,3,256,128]{3,2,1,0:T(8,128)(2,1)S(1)} %copy-done.15), channel_id=1, source_target_pairs={{0,4},{4,0},{8,12},{12,8},{1,5},{5,1},{9,13},{13,9},{2,6},{6,2},{1... | collective-permute-start | bytes 1179656 | tf_op jit(solution)/shard_map/ppermute | solution.py:42
  16.4 2.6 %collective-permute-start.1 = (bf16[1,3,256,128]{3,2,1,0:T(8,128)(2,1)}, bf16[1,3,256,128]{3,2,1,0:T(8,128)(2,1)S(1)}, u32[]{:S(2)}, u32[]{:S(2)}) collective-permute-start(bf16[1,3,256,128]{3,2,1,0:T(8,128)(2,1)} %get-tuple-element.42), channel_id=1, source_target_pairs={{0,8},{4,12},{8,0},{12,4},{1,9},{5,13},{9,1},{13,5},{2,10},{6,14},... | collective-permute-start | bytes 589832 | tf_op jit(solution)/shard_map/ppermute | solution.py:42
  19.0 1.9 %collective-permute-start.10 = (bf16[1,3,256,128]{3,2,1,0:T(8,128)(2,1)}, bf16[1,3,256,128]{3,2,1,0:T(8,128)(2,1)S(1)}, u32[]{:S(2)}, u32[]{:S(2)}) collective-permute-start(bf16[1,3,256,128]{3,2,1,0:T(8,128)(2,1)} %get-tuple-element.51), channel_id=1, source_target_pairs={{0,8},{4,12},{8,0},{12,4},{1,9},{5,13},{9,1},{13,5},{2,10},{6,14},... | collective-permute-start | bytes 589832 | tf_op jit(solution)/shard_map/ppermute | solution.py:42
  20.9 1.9 %collective-permute-start.11 = (bf16[1,3,256,128]{3,2,1,0:T(8,128)(2,1)}, bf16[1,3,256,128]{3,2,1,0:T(8,128)(2,1)S(1)}, u32[]{:S(2)}, u32[]{:S(2)}) collective-permute-start(bf16[1,3,256,128]{3,2,1,0:T(8,128)(2,1)} %get-tuple-element.52), channel_id=1, source_target_pairs={{0,12},{4,8},{8,4},{12,0},{1,13},{5,9},{9,5},{13,1},{2,14},{6,10},... | collective-permute-start | bytes 589832 | tf_op jit(solution)/shard_map/ppermute | solution.py:42
  22.9 7.5 %collective-permute-done.1.refs_2_.refs_6_ = bf16[1,3,256,128]{3,2,1,0:T(8,128)(2,1)S(1)} collective-permute-done((bf16[1,3,256,128]{3,2,1,0:T(8,128)(2,1)}, bf16[1,3,256,128]{3,2,1,0:T(8,128)(2,1)S(1)}, u32[]{:S(2)}, u32[]{:S(2)}) %collective-permute-start.1) | collective-permute-done | bytes 196640 | tf_op jit(solution)/shard_map/ppermute | solution.py:42
  30.3 7.1 %collective-permute-done.2.refs_3_.refs_7_ = bf16[1,3,256,128]{3,2,1,0:T(8,128)(2,1)S(1)} collective-permute-done((bf16[1,3,256,128]{3,2,1,0:T(8,128)(2,1)}, bf16[1,3,256,128]{3,2,1,0:T(8,128)(2,1)S(1)}, u32[]{:S(2)}, u32[]{:S(2)}) %collective-permute-start.2) | collective-permute-done | bytes 196640 | tf_op jit(solution)/shard_map/ppermute | solution.py:42
  37.4 2.3 %attend.2 = (bf16[4,64,128]{2,1,0:T(8,128)(2,1)S(1)}, bf16[4,64,128]{2,1,0:T(8,128)(2,1)S(1)}, bf16[4,64,128]{2,1,0:T(8,128)(2,1)S(1)}, bf16[4,64,128]{2,1,0:T(8,128)(2,1)S(1)}) custom-call(s32[4]{0:T(128)S(1)} %copy-done.12, bf16[2,3,256,128]{3,2,1,0:T(8,128)(2,1)S(1)} %copy-done.13, bf16[2,3,256,128]{3,2,1,0:T(8,128)(2,1)S(1)} %collective-permute-done.refs_1_.refs_5_, ...), custom_call_target="tpu_custom_call" | custom-call | flops 20000000000 | tf_op jit(solution)/shard_map/attend/pallas_call | solution.py:118
  39.7 0.1 collective-permute-start.3
  39.8 1.6 %collective-permute-start.4 = (bf16[4,64,128]{2,1,0:T(8,128)(2,1)S(1)}, bf16[4,64,128]{2,1,0:T(8,128)(2,1)S(1)}, u32[]{:S(2)}, u32[]{:S(2)}) collective-permute-start(bf16[4,64,128]{2,1,0:T(8,128)(2,1)S(1)} %get-tuple-element.46), channel_id=1, source_target_pairs={{0,2},{1,3},{2,0},{3,1},{4,6},{5,7},{6,4},{7,5},{8,10},{9,11},{10,... | collective-permute-start | bytes 196616 | tf_op jit(solution)/shard_map/ppermute | solution.py:42
  41.4 0.3 collective-permute-start.5
  41.7 2.6 %collective-permute-done.4 = bf16[4,64,128]{2,1,0:T(8,128)(2,1)S(1)} collective-permute-done((bf16[4,64,128]{2,1,0:T(8,128)(2,1)S(1)}, bf16[4,64,128]{2,1,0:T(8,128)(2,1)S(1)}, u32[]{:S(2)}, u32[]{:S(2)}) %collective-permute-start.4) | collective-permute-done | bytes 65568 | tf_op jit(solution)/shard_map/ppermute | solution.py:42
  44.3 1.1 collective-permute-done.5
  45.4 12.5 %collective-permute-start.7 = (bf16[4,256,128]{2,1,0:T(8,128)(2,1)S(1)}, bf16[4,256,128]{2,1,0:T(8,128)(2,1)S(1)}, u32[]{:S(2)}, u32[]{:S(2)}) collective-permute-start(bf16[4,256,128]{2,1,0:T(8,128)(2,1)S(1)} %pad_maximum_fusion.refs_0_), channel_id=1, source_target_pairs={{0,4},{4,0},{8,12},{12,8},{1,5},{5,1},{9,13},{13,9},{2,6},{6,2},{1... | collective-permute-start | bytes 786440 | tf_op jit(solution)/shard_map/ppermute | solution.py:42
  57.9 1.1 collective-permute-start.6
  59.1 2.3 %attend.3 = (bf16[4,64,128]{2,1,0:T(8,128)(2,1)S(1)}, bf16[4,64,128]{2,1,0:T(8,128)(2,1)S(1)}, bf16[4,64,128]{2,1,0:T(8,128)(2,1)S(1)}, bf16[4,64,128]{2,1,0:T(8,128)(2,1)S(1)}) custom-call(s32[4]{0:T(128)S(1)} %copy-done.12, bf16[2,3,256,128]{3,2,1,0:T(8,128)(2,1)S(1)} %copy-done.14, bf16[2,3,256,128]{3,2,1,0:T(8,128)(2,1)S(1)} %collective-permute-done.refs_1_.refs_5_, ...), custom_call_target="tpu_custom_call" | custom-call | flops 20000000000 | tf_op jit(solution)/shard_map/attend/pallas_call | solution.py:118
  61.4 0.6 collective-permute-start.12
  61.9 1.5 %collective-permute-start.13 = (bf16[4,64,128]{2,1,0:T(8,128)(2,1)S(1)}, bf16[4,64,128]{2,1,0:T(8,128)(2,1)S(1)}, u32[]{:S(2)}, u32[]{:S(2)}) collective-permute-start(bf16[4,64,128]{2,1,0:T(8,128)(2,1)S(1)} %get-tuple-element.55), channel_id=1, source_target_pairs={{0,2},{1,3},{2,0},{3,1},{4,6},{5,7},{6,4},{7,5},{8,10},{9,11},{10,... | collective-permute-start | bytes 196616 | tf_op jit(solution)/shard_map/ppermute | solution.py:42
  63.4 4.8 %collective-permute-done.13 = bf16[4,64,128]{2,1,0:T(8,128)(2,1)S(1)} collective-permute-done((bf16[4,64,128]{2,1,0:T(8,128)(2,1)S(1)}, bf16[4,64,128]{2,1,0:T(8,128)(2,1)S(1)}, u32[]{:S(2)}, u32[]{:S(2)}) %collective-permute-start.13) | collective-permute-done | bytes 65568 | tf_op jit(solution)/shard_map/ppermute | solution.py:42
  68.2 1.6 %collective-permute-done.14 = bf16[4,64,128]{2,1,0:T(8,128)(2,1)S(1)} collective-permute-done((bf16[4,64,128]{2,1,0:T(8,128)(2,1)S(1)}, bf16[4,64,128]{2,1,0:T(8,128)(2,1)S(1)}, u32[]{:S(2)}, u32[]{:S(2)}) %collective-permute-start.14) | collective-permute-done | bytes 65568 | tf_op jit(solution)/shard_map/ppermute | solution.py:42
  69.9 2.0 %collective-permute-start.16 = (bf16[4,256,128]{2,1,0:T(8,128)(2,1)S(1)}, bf16[4,256,128]{2,1,0:T(8,128)(2,1)S(1)}, u32[]{:S(2)}, u32[]{:S(2)}) collective-permute-start(bf16[4,256,128]{2,1,0:T(8,128)(2,1)S(1)} %pad_maximum_fusion.1.refs_0_), channel_id=1, source_target_pairs={{0,4},{4,0},{8,12},{12,8},{1,5},{5,1},{9,13},{13,9},{2,6},{6,2},{1... | collective-permute-start | bytes 786440 | tf_op jit(solution)/shard_map/ppermute | solution.py:42
  72.0 1.4 collective-permute-start.8
  73.3 0.7 copy-done.5
  74.0 1.3 collective-permute-start.9
  75.3 0.7 copy-done.7
  76.0 1.3 collective-permute-start.17
  77.4 6.0 %collective-permute-done.16.refs_1_ = bf16[4,256,128]{2,1,0:T(8,128)(2,1)S(1)} collective-permute-done((bf16[4,256,128]{2,1,0:T(8,128)(2,1)S(1)}, bf16[4,256,128]{2,1,0:T(8,128)(2,1)S(1)}, u32[]{:S(2)}, u32[]{:S(2)}) %collective-permute-start.16) | collective-permute-done | bytes 262176 | tf_op jit(solution)/shard_map/ppermute | solution.py:42
  83.4 0.7 copy-done.9
  84.1 3.7 %collective-permute-done.15.refs_2_ = bf16[4,256,128]{2,1,0:T(8,128)(2,1)} collective-permute-done((bf16[4,256,128]{2,1,0:T(8,128)(2,1)S(1)}, bf16[4,256,128]{2,1,0:T(8,128)(2,1)}, u32[]{:S(2)}, u32[]{:S(2)}) %collective-permute-start.15) | collective-permute-done | bytes 262176 | tf_op jit(solution)/shard_map/ppermute | solution.py:42
  87.7 1.3 collective-permute-start.18
  89.1 1.3 collective-permute-done.9
  90.4 1.0 broadcast_select_fusion.1.refs_3_
  91.4 6.4 %collective-permute-done.18 = bf16[4,256,128]{2,1,0:T(8,128)(2,1)} collective-permute-done((bf16[4,256,128]{2,1,0:T(8,128)(2,1)}, bf16[4,256,128]{2,1,0:T(8,128)(2,1)}, u32[]{:S(2)}, u32[]{:S(2)}) %collective-permute-start.18) | collective-permute-done | bytes 262176 | tf_op jit(solution)/shard_map/ppermute | solution.py:249
  97.7 1.7 %broadcast_select_fusion.refs_3_ = bf16[4,256,128]{2,1,0:T(8,128)(2,1)} fusion(bf16[4,256,128]{2,1,0:T(8,128)(2,1)} %collective-permute-done.17, bf16[4,256,128]{2,1,0:T(8,128)(2,1)} %collective-permute-done.18, pred[]{:T(512)S(6)} %or.4), kind=kLoop, calls=%fused_computation.2 | loop fusion | flops 131072 | bytes 786433 | tf_op jit(solution)/shard_map/jit(_where)/select_n | solution.py:251
  99.4 4.0 %copy-done.1 = bf16[32,1,128,1280]{3,2,1,0:T(8,128)(2,1)S(1)} copy-done((bf16[32,1,128,1280]{3,2,1,0:T(8,128)(2,1)S(1)}, bf16[32,1,128,1280]{3,2,1,0:T(8,128)(2,1)}, u32[]{:S(2)}) %copy-start.1) | copy-done | bytes 10485784
  103.4 0.9 copy-done.3
  104.4 0.9 copy-done.10
  105.3 4.7 %project.2.refs_5_ = f32[256,1280]{1,0:T(8,128)S(1)} custom-call(s32[4]{0:T(128)S(1)} %copy-done.12, bf16[4,256,128]{2,1,0:T(8,128)(2,1)S(1)} %pad_maximum_fusion.1.refs_0_, bf16[4,256,128]{2,1,0:T(8,128)(2,1)S(1)} %copy-done.10, bf16[4,256,128]{2,1,0:T(8,128)(2,1)} %collective-permute-done.15.refs_2_, bf16[4,256,128]{2,1,0:T(8,128)(2,1)S(1)} %copy-done.3, ...), custom_call_target="tpu_custom_call" | custom-call | tf_op jit(solution)/shard_map/project/pallas_call | solution.py:186
  110.0 3.8 %project.3 = (bf16[64,1280]{1,0:T(8,128)(2,1)S(1)}, bf16[64,1280]{1,0:T(8,128)(2,1)S(1)}, bf16[64,1280]{1,0:T(8,128)(2,1)S(1)}, bf16[64,1280]{1,0:T(8,128)(2,1)S(1)}) custom-call(s32[4]{0:T(128)S(1)} %copy-done.12, bf16[4,256,128]{2,1,0:T(8,128)(2,1)S(1)} %pad_maximum_fusion.refs_0_, bf16[4,256,128]{2,1,0:T(8,128)(2,1)S(1)} %copy-done.6, ...), custom_call_target="tpu_custom_call" | custom-call | tf_op jit(solution)/shard_map/project/pallas_call | solution.py:186
  113.9 1.6 %collective-permute-start.19 = (bf16[64,1280]{1,0:T(8,128)(2,1)S(1)}, bf16[64,1280]{1,0:T(8,128)(2,1)S(1)}, u32[]{:S(2)}, u32[]{:S(2)}) collective-permute-start(bf16[64,1280]{1,0:T(8,128)(2,1)S(1)} %get-tuple-element.60), channel_id=1, source_target_pairs={{0,4},{4,0},{8,12},{12,8},{1,5},{5,1},{9,13},{13,9},{2,6},{6,2},{1... | collective-permute-start | bytes 491528 | tf_op jit(solution)/shard_map/ppermute | solution.py:42
  115.5 2.8 %collective-permute-start.21 = (bf16[64,1280]{1,0:T(8,128)(2,1)S(1)}, bf16[64,1280]{1,0:T(8,128)(2,1)S(1)}, u32[]{:S(2)}, u32[]{:S(2)}) collective-permute-start(bf16[64,1280]{1,0:T(8,128)(2,1)S(1)} %get-tuple-element.62), channel_id=1, source_target_pairs={{0,12},{4,8},{8,4},{12,0},{1,13},{5,9},{9,5},{13,1},{2,14},{6,10},... | collective-permute-start | bytes 491528 | tf_op jit(solution)/shard_map/ppermute | solution.py:42
  118.3 3.4 %collective-permute-done.19.refs_1_ = bf16[64,1280]{1,0:T(8,128)(2,1)S(1)} collective-permute-done((bf16[64,1280]{1,0:T(8,128)(2,1)S(1)}, bf16[64,1280]{1,0:T(8,128)(2,1)S(1)}, u32[]{:S(2)}, u32[]{:S(2)}) %collective-permute-start.19) | collective-permute-done | bytes 163872 | tf_op jit(solution)/shard_map/ppermute | solution.py:42
  121.7 8.6 %collective-permute-done.20.refs_2_ = bf16[64,1280]{1,0:T(8,128)(2,1)S(1)} collective-permute-done((bf16[64,1280]{1,0:T(8,128)(2,1)S(1)}, bf16[64,1280]{1,0:T(8,128)(2,1)S(1)}, u32[]{:S(2)}, u32[]{:S(2)}) %collective-permute-start.20) | collective-permute-done | bytes 163872 | tf_op jit(solution)/shard_map/ppermute | solution.py:42
  130.3 1.6 %mix.1 = bf16[64,5120]{1,0:T(8,128)(2,1)} custom-call(s32[4]{0:T(128)S(1)} %copy-done.12, bf16[64,5120]{1,0:T(8,128)(2,1)S(1)} %copy-done.4, f32[1,5120]{1,0:T(1,128)S(1)} %bitcast.20, bf16[64,1280]{1,0:T(8,128)(2,1)S(1)} %get-tuple-element.59.refs_0_, bf16[64,1280]{1,0:T(8,128)(2,1)S(1)} %collective-permute-done.19.refs_1_, ...), custom_call_target="tpu_custom_call" | custom-call | tf_op jit(solution)/shard_map/mix/pallas_call | solution.py:215
  (43 shorter events, 0.2 us)
Async XLA Ops:
  6.5 5.6 %copy-start = (bf16[1024,1280]{1,0:T(8,128)(2,1)S(1)}, bf16[1024,1280]{1,0:T(8,128)(2,1)}, u32[]{:S(2)}) copy-start(bf16[1024,1280]{1,0:T(8,128)(2,1)} %param.11) | copy-start | bytes 7864324
  6.5 92.9 %all-gather.3.cloned.1.call-start = ((), (), s32[]{:S(2)}) async-start(), calls=%async_computation | async-start | bytes 11796480 | tf_op jit(solution)/shard_map/all_gather | solution.py:230
  12.1 1.2 copy-start.15
  12.1 25.3 %copy-start.12 = (s32[4]{0:T(128)S(1)}, s32[4]{0:T(128)}, u32[]{:S(2)}) copy-start(s32[4]{0:T(128)} %pad_add_fusion.where_ref) | copy-start | bytes 52
  12.1 25.3 %copy-start.13 = (bf16[2,3,256,128]{3,2,1,0:T(8,128)(2,1)S(1)}, bf16[2,3,256,128]{3,2,1,0:T(8,128)(2,1)}, u32[]{:S(2)}) copy-start(bf16[2,3,256,128]{3,2,1,0:T(8,128)(2,1)} %get-tuple-element.40.refs_0_.refs_4_) | copy-start | bytes 1179652
  13.3 45.7 %copy-start.14 = (bf16[2,3,256,128]{3,2,1,0:T(8,128)(2,1)S(1)}, bf16[2,3,256,128]{3,2,1,0:T(8,128)(2,1)}, u32[]{:S(2)}) copy-start(bf16[2,3,256,128]{3,2,1,0:T(8,128)(2,1)} %get-tuple-element.40.refs_0_.refs_4_) | copy-start | bytes 1179652
  13.4 24.1 %collective-permute-start = (bf16[2,3,256,128]{3,2,1,0:T(8,128)(2,1)S(1)}, bf16[2,3,256,128]{3,2,1,0:T(8,128)(2,1)S(1)}, u32[]{:S(2)}, u32[]{:S(2)}) collective-permute-start(bf16[2,3,256,128]{3,2,1,0:T(8,128)(2,1)S(1)} %copy-done.15), channel_id=1, source_target_pairs={{0,4},{4,0},{8,12},{12,8},{1,5},{5,1},{9,13},{13,9},{2,6},{6,2},{1... | collective-permute-start | bytes 1179656 | tf_op jit(solution)/shard_map/ppermute | solution.py:42
  16.4 13.9 %collective-permute-start.1 = (bf16[1,3,256,128]{3,2,1,0:T(8,128)(2,1)}, bf16[1,3,256,128]{3,2,1,0:T(8,128)(2,1)S(1)}, u32[]{:S(2)}, u32[]{:S(2)}) collective-permute-start(bf16[1,3,256,128]{3,2,1,0:T(8,128)(2,1)} %get-tuple-element.42), channel_id=1, source_target_pairs={{0,8},{4,12},{8,0},{12,4},{1,9},{5,13},{9,1},{13,5},{2,10},{6,14},... | collective-permute-start | bytes 589832 | tf_op jit(solution)/shard_map/ppermute | solution.py:42
  19.0 18.4 %collective-permute-start.2 = (bf16[1,3,256,128]{3,2,1,0:T(8,128)(2,1)}, bf16[1,3,256,128]{3,2,1,0:T(8,128)(2,1)S(1)}, u32[]{:S(2)}, u32[]{:S(2)}) collective-permute-start(bf16[1,3,256,128]{3,2,1,0:T(8,128)(2,1)} %get-tuple-element.43), channel_id=1, source_target_pairs={{0,12},{4,8},{8,4},{12,0},{1,13},{5,9},{9,5},{13,1},{2,14},{6,10},... | collective-permute-start | bytes 589832 | tf_op jit(solution)/shard_map/ppermute | solution.py:42
  19.0 40.0 %collective-permute-start.10 = (bf16[1,3,256,128]{3,2,1,0:T(8,128)(2,1)}, bf16[1,3,256,128]{3,2,1,0:T(8,128)(2,1)S(1)}, u32[]{:S(2)}, u32[]{:S(2)}) collective-permute-start(bf16[1,3,256,128]{3,2,1,0:T(8,128)(2,1)} %get-tuple-element.51), channel_id=1, source_target_pairs={{0,8},{4,12},{8,0},{12,4},{1,9},{5,13},{9,1},{13,5},{2,10},{6,14},... | collective-permute-start | bytes 589832 | tf_op jit(solution)/shard_map/ppermute | solution.py:42
  20.9 38.1 %collective-permute-start.11 = (bf16[1,3,256,128]{3,2,1,0:T(8,128)(2,1)}, bf16[1,3,256,128]{3,2,1,0:T(8,128)(2,1)S(1)}, u32[]{:S(2)}, u32[]{:S(2)}) collective-permute-start(bf16[1,3,256,128]{3,2,1,0:T(8,128)(2,1)} %get-tuple-element.52), channel_id=1, source_target_pairs={{0,12},{4,8},{8,4},{12,0},{1,13},{5,9},{9,5},{13,1},{2,14},{6,10},... | collective-permute-start | bytes 589832 | tf_op jit(solution)/shard_map/ppermute | solution.py:42
  39.7 1.9 %collective-permute-start.3 = (bf16[4,64,128]{2,1,0:T(8,128)(2,1)S(1)}, bf16[4,64,128]{2,1,0:T(8,128)(2,1)S(1)}, u32[]{:S(2)}, u32[]{:S(2)}) collective-permute-start(bf16[4,64,128]{2,1,0:T(8,128)(2,1)S(1)} %get-tuple-element.45), channel_id=1, source_target_pairs={{0,1},{1,0},{2,3},{3,2},{4,5},{5,4},{6,7},{7,6},{8,9},{9,8},{10,11... | collective-permute-start | bytes 196616 | tf_op jit(solution)/shard_map/ppermute | solution.py:42
  39.8 4.5 %collective-permute-start.4 = (bf16[4,64,128]{2,1,0:T(8,128)(2,1)S(1)}, bf16[4,64,128]{2,1,0:T(8,128)(2,1)S(1)}, u32[]{:S(2)}, u32[]{:S(2)}) collective-permute-start(bf16[4,64,128]{2,1,0:T(8,128)(2,1)S(1)} %get-tuple-element.46), channel_id=1, source_target_pairs={{0,2},{1,3},{2,0},{3,1},{4,6},{5,7},{6,4},{7,5},{8,10},{9,11},{10,... | collective-permute-start | bytes 196616 | tf_op jit(solution)/shard_map/ppermute | solution.py:42
  41.4 4.0 %collective-permute-start.5 = (bf16[4,64,128]{2,1,0:T(8,128)(2,1)S(1)}, bf16[4,64,128]{2,1,0:T(8,128)(2,1)S(1)}, u32[]{:S(2)}, u32[]{:S(2)}) collective-permute-start(bf16[4,64,128]{2,1,0:T(8,128)(2,1)S(1)} %get-tuple-element.47), channel_id=1, source_target_pairs={{0,3},{1,2},{2,1},{3,0},{4,7},{5,6},{6,5},{7,4},{8,11},{9,10},{10,... | collective-permute-start | bytes 196616 | tf_op jit(solution)/shard_map/ppermute | solution.py:42
  45.4 27.9 %collective-permute-start.7 = (bf16[4,256,128]{2,1,0:T(8,128)(2,1)S(1)}, bf16[4,256,128]{2,1,0:T(8,128)(2,1)S(1)}, u32[]{:S(2)}, u32[]{:S(2)}) collective-permute-start(bf16[4,256,128]{2,1,0:T(8,128)(2,1)S(1)} %pad_maximum_fusion.refs_0_), channel_id=1, source_target_pairs={{0,4},{4,0},{8,12},{12,8},{1,5},{5,1},{9,13},{13,9},{2,6},{6,2},{1... | collective-permute-start | bytes 786440 | tf_op jit(solution)/shard_map/ppermute | solution.py:42
  57.9 16.1 %collective-permute-start.6 = (bf16[4,256,128]{2,1,0:T(8,128)(2,1)S(1)}, bf16[4,256,128]{2,1,0:T(8,128)(2,1)S(1)}, u32[]{:S(2)}, u32[]{:S(2)}) collective-permute-start(bf16[4,256,128]{2,1,0:T(8,128)(2,1)S(1)} %pad_maximum_fusion.refs_0_), channel_id=1, source_target_pairs={{0,8},{4,12},{8,0},{12,4},{1,9},{5,13},{9,1},{13,5},{2,10},{6,14},... | collective-permute-start | bytes 786440 | tf_op jit(solution)/shard_map/ppermute | solution.py:42
  61.4 2.1 %collective-permute-start.12 = (bf16[4,64,128]{2,1,0:T(8,128)(2,1)S(1)}, bf16[4,64,128]{2,1,0:T(8,128)(2,1)S(1)}, u32[]{:S(2)}, u32[]{:S(2)}) collective-permute-start(bf16[4,64,128]{2,1,0:T(8,128)(2,1)S(1)} %get-tuple-element.54), channel_id=1, source_target_pairs={{0,1},{1,0},{2,3},{3,2},{4,5},{5,4},{6,7},{7,6},{8,9},{9,8},{10,11... | collective-permute-start | bytes 196616 | tf_op jit(solution)/shard_map/ppermute | solution.py:42
  61.9 6.3 %collective-permute-start.13 = (bf16[4,64,128]{2,1,0:T(8,128)(2,1)S(1)}, bf16[4,64,128]{2,1,0:T(8,128)(2,1)S(1)}, u32[]{:S(2)}, u32[]{:S(2)}) collective-permute-start(bf16[4,64,128]{2,1,0:T(8,128)(2,1)S(1)} %get-tuple-element.55), channel_id=1, source_target_pairs={{0,2},{1,3},{2,0},{3,1},{4,6},{5,7},{6,4},{7,5},{8,10},{9,11},{10,... | collective-permute-start | bytes 196616 | tf_op jit(solution)/shard_map/ppermute | solution.py:42
  63.4 6.5 %collective-permute-start.14 = (bf16[4,64,128]{2,1,0:T(8,128)(2,1)S(1)}, bf16[4,64,128]{2,1,0:T(8,128)(2,1)S(1)}, u32[]{:S(2)}, u32[]{:S(2)}) collective-permute-start(bf16[4,64,128]{2,1,0:T(8,128)(2,1)S(1)} %get-tuple-element.56), channel_id=1, source_target_pairs={{0,3},{1,2},{2,1},{3,0},{4,7},{5,6},{6,5},{7,4},{8,11},{9,10},{10,... | collective-permute-start | bytes 196616 | tf_op jit(solution)/shard_map/ppermute | solution.py:42
  69.9 13.5 %collective-permute-start.16 = (bf16[4,256,128]{2,1,0:T(8,128)(2,1)S(1)}, bf16[4,256,128]{2,1,0:T(8,128)(2,1)S(1)}, u32[]{:S(2)}, u32[]{:S(2)}) collective-permute-start(bf16[4,256,128]{2,1,0:T(8,128)(2,1)S(1)} %pad_maximum_fusion.1.refs_0_), channel_id=1, source_target_pairs={{0,4},{4,0},{8,12},{12,8},{1,5},{5,1},{9,13},{13,9},{2,6},{6,2},{1... | collective-permute-start | bytes 786440 | tf_op jit(solution)/shard_map/ppermute | solution.py:42
  72.0 15.8 %collective-permute-start.15 = (bf16[4,256,128]{2,1,0:T(8,128)(2,1)S(1)}, bf16[4,256,128]{2,1,0:T(8,128)(2,1)}, u32[]{:S(2)}, u32[]{:S(2)}) collective-permute-start(bf16[4,256,128]{2,1,0:T(8,128)(2,1)S(1)} %pad_maximum_fusion.1.refs_0_), channel_id=1, source_target_pairs={{0,8},{4,12},{8,0},{12,4},{1,9},{5,13},{9,1},{13,5},{2,10},{6,14},... | collective-permute-start | bytes 786440 | tf_op jit(solution)/shard_map/ppermute | solution.py:42
  72.0 17.1 %collective-permute-start.8 = (bf16[4,256,128]{2,1,0:T(8,128)(2,1)S(1)}, bf16[4,256,128]{2,1,0:T(8,128)(2,1)}, u32[]{:S(2)}, u32[]{:S(2)}) collective-permute-start(bf16[4,256,128]{2,1,0:T(8,128)(2,1)S(1)} %pad_maximum_fusion.refs_0_), channel_id=1, source_target_pairs={{4,8},{8,4},{5,9},{9,5},{6,10},{10,6},{7,11},{11,7},{20,24},{24,20... | collective-permute-start | bytes 786440 | tf_op jit(solution)/shard_map/ppermute | solution.py:42
  73.3 0.7 copy-start.5
  74.0 16.3 %collective-permute-start.9 = (bf16[4,256,128]{2,1,0:T(8,128)(2,1)S(1)}, bf16[4,256,128]{2,1,0:T(8,128)(2,1)}, u32[]{:S(2)}, u32[]{:S(2)}) collective-permute-start(bf16[4,256,128]{2,1,0:T(8,128)(2,1)S(1)} %collective-permute-done.6.refs_2_), channel_id=1, source_target_pairs={{4,0},{8,12},{5,1},{9,13},{6,2},{10,14},{7,3},{11,15},{20,16},{24,... | collective-permute-start | bytes 786440 | tf_op jit(solution)/shard_map/ppermute | solution.py:249
  75.3 0.7 copy-start.7
  76.0 15.3 %collective-permute-start.17 = (bf16[4,256,128]{2,1,0:T(8,128)(2,1)S(1)}, bf16[4,256,128]{2,1,0:T(8,128)(2,1)}, u32[]{:S(2)}, u32[]{:S(2)}) collective-permute-start(bf16[4,256,128]{2,1,0:T(8,128)(2,1)S(1)} %pad_maximum_fusion.1.refs_0_), channel_id=1, source_target_pairs={{4,8},{8,4},{5,9},{9,5},{6,10},{10,6},{7,11},{11,7},{20,24},{24,20... | collective-permute-start | bytes 786440 | tf_op jit(solution)/shard_map/ppermute | solution.py:42
  83.4 0.7 copy-start.9
  87.7 10.0 %collective-permute-start.18 = (bf16[4,256,128]{2,1,0:T(8,128)(2,1)}, bf16[4,256,128]{2,1,0:T(8,128)(2,1)}, u32[]{:S(2)}, u32[]{:S(2)}) collective-permute-start(bf16[4,256,128]{2,1,0:T(8,128)(2,1)} %collective-permute-done.15.refs_2_), channel_id=1, source_target_pairs={{4,0},{8,12},{5,1},{9,13},{6,2},{10,14},{7,3},{11,15},{20,16},{24,... | collective-permute-start | bytes 786440 | tf_op jit(solution)/shard_map/ppermute | solution.py:249
  99.4 4.0 %copy-start.1 = (bf16[32,1,128,1280]{3,2,1,0:T(8,128)(2,1)S(1)}, bf16[32,1,128,1280]{3,2,1,0:T(8,128)(2,1)}, u32[]{:S(2)}) copy-start(bf16[32,1,128,1280]{3,2,1,0:T(8,128)(2,1)} %all-gather.3.cloned.1.call-done) | copy-start | bytes 31457284
  103.4 0.9 copy-start.3
  104.4 0.9 copy-start.10
  105.3 4.7 %copy-start.2 = (bf16[32,1,128,1280]{3,2,1,0:T(8,128)(2,1)S(1)}, bf16[32,1,128,1280]{3,2,1,0:T(8,128)(2,1)}, u32[]{:S(2)}) copy-start(bf16[32,1,128,1280]{3,2,1,0:T(8,128)(2,1)} %all-gather.3.cloned.1.call-done) | copy-start | bytes 31457284
  105.3 4.7 %copy-start.6 = (bf16[4,256,128]{2,1,0:T(8,128)(2,1)S(1)}, bf16[4,256,128]{2,1,0:T(8,128)(2,1)}, u32[]{:S(2)}) copy-start(bf16[4,256,128]{2,1,0:T(8,128)(2,1)} %copy-done.5) | copy-start | bytes 786436
  105.3 4.7 %copy-start.8 = (bf16[4,256,128]{2,1,0:T(8,128)(2,1)S(1)}, bf16[4,256,128]{2,1,0:T(8,128)(2,1)}, u32[]{:S(2)}) copy-start(bf16[4,256,128]{2,1,0:T(8,128)(2,1)} %copy-done.7) | copy-start | bytes 786436
  110.0 20.3 %copy-start.4 = (bf16[64,5120]{1,0:T(8,128)(2,1)S(1)}, bf16[64,5120]{1,0:T(8,128)(2,1)}, u32[]{:S(2)}) copy-start(bf16[64,5120]{1,0:T(8,128)(2,1)} %hidden_ref.1) | copy-start | bytes 1966084
  110.0 20.3 %copy-start.11 = (f32[5120]{0:T(1024)S(1)}, f32[5120]{0:T(1024)}, u32[]{:S(2)}) copy-start(f32[5120]{0:T(1024)} %param.13) | copy-start | bytes 61444
  113.9 7.8 %collective-permute-start.19 = (bf16[64,1280]{1,0:T(8,128)(2,1)S(1)}, bf16[64,1280]{1,0:T(8,128)(2,1)S(1)}, u32[]{:S(2)}, u32[]{:S(2)}) collective-permute-start(bf16[64,1280]{1,0:T(8,128)(2,1)S(1)} %get-tuple-element.60), channel_id=1, source_target_pairs={{0,4},{4,0},{8,12},{12,8},{1,5},{5,1},{9,13},{13,9},{2,6},{6,2},{1... | collective-permute-start | bytes 491528 | tf_op jit(solution)/shard_map/ppermute | solution.py:42
  115.5 14.8 %collective-permute-start.20 = (bf16[64,1280]{1,0:T(8,128)(2,1)S(1)}, bf16[64,1280]{1,0:T(8,128)(2,1)S(1)}, u32[]{:S(2)}, u32[]{:S(2)}) collective-permute-start(bf16[64,1280]{1,0:T(8,128)(2,1)S(1)} %get-tuple-element.61), channel_id=1, source_target_pairs={{0,8},{4,12},{8,0},{12,4},{1,9},{5,13},{9,1},{13,5},{2,10},{6,14},... | collective-permute-start | bytes 491528 | tf_op jit(solution)/shard_map/ppermute | solution.py:42
  115.5 14.8 %collective-permute-start.21 = (bf16[64,1280]{1,0:T(8,128)(2,1)S(1)}, bf16[64,1280]{1,0:T(8,128)(2,1)S(1)}, u32[]{:S(2)}, u32[]{:S(2)}) collective-permute-start(bf16[64,1280]{1,0:T(8,128)(2,1)S(1)} %get-tuple-element.62), channel_id=1, source_target_pairs={{0,12},{4,8},{8,4},{12,0},{1,13},{5,9},{9,5},{13,1},{2,14},{6,10},... | collective-permute-start | bytes 491528 | tf_op jit(solution)/shard_map/ppermute | solution.py:42
Sparse Core Ops, SparseCore 0:
  13.4 68.3 all-gather.2

commit v5 on v3

v5 whole, which is shorter than its diff:
```python
import functools
import math

import jax
import jax.numpy as jnp
from jax import lax
from jax.experimental import pallas as pl
from jax.experimental.pallas import tpu as pltpu
from jax.sharding import PartitionSpec as P

HEAD_DIM = 128
SCALE_ROWS = 128
SATURATION = 448.0
VMEM_BYTES = 32 * 1024 * 1024
PACK_VMEM_BYTES = 60 * 1024 * 1024
ATTEND_FLOPS = 5_000_000_000
PROJECT_FLOPS = 5_000_000_000

PATCH, NEAR, HEAD, SUB, INNER = range(5)


def spec(shape):
    return pl.BlockSpec(shape, lambda i, w: (0,) * len(shape))


def call(kernel, name, out_shape, grid, in_specs, out_specs, scratch=(), flops=0, vmem=VMEM_BYTES):
    return pl.pallas_call(
        kernel,
        out_shape=out_shape,
        grid_spec=pltpu.PrefetchScalarGridSpec(
            num_scalar_prefetch=1,
            grid=(grid,),
            in_specs=in_specs,
            out_specs=out_specs,
            scratch_shapes=list(scratch),
        ),
        compiler_params=pltpu.CompilerParams(vmem_limit_bytes=vmem),
        cost_estimate=pl.CostEstimate(flops=flops, bytes_accessed=0, transcendentals=0),
        name=name,
    )


def swap(x, axes, count, mask, only=None):
    pairs = [(at, at ^ mask) for at in range(count) if only is None or at in only]
    return lax.ppermute(x, axes, pairs)


def pack_kernel(split, per, where_ref, exps_ref, q_ref, fresh_ref, cached_ref, *outs):
    rows = q_ref.shape[0]
    block = pl.program_id(0) * rows // SCALE_ROWS
    for rel in range(split):
        for chunk in range(per):
            head = (where_ref[NEAR] ^ rel) * per + chunk
            lanes = pl.ds(pl.multiple_of(head * HEAD_DIM, HEAD_DIM), HEAD_DIM)
            here = pl.ds(chunk * HEAD_DIM, HEAD_DIM)
            outs[rel][0, :, here] = q_ref[:, lanes]
            for stacked in range(2):
                power = jnp.full((1, HEAD_DIM), exps_ref[stacked, block, head].astype(jnp.float32))
                cached = cached_ref[stacked, :, lanes].astype(jnp.float32)
                residual = fresh_ref[stacked, :, lanes].astype(jnp.float32) - cached
                codes = jnp.clip(
                    residual * jnp.exp2(-power), -SATURATION, SATURATION
                ).astype(jnp.bfloat16)
                decoded = cached + codes.astype(jnp.float32) * jnp.exp2(power)
                outs[rel][1 + stacked, :, here] = decoded.astype(jnp.bfloat16)


def pack(split, per, where, exponents, queries, fresh_kv, cached_kv):
    tok, channels = queries.shape
    feat = channels // split
    rows = SCALE_ROWS // 2
    steps = tok // rows
    return call(
        functools.partial(pack_kernel, split, per),
        "pack",
        [jax.ShapeDtypeStruct((3, tok, feat), jnp.bfloat16)] * split,
        steps,
        [
            pl.BlockSpec(memory_space=pltpu.SMEM),
            pl.BlockSpec((rows, channels), lambda i, w: (i, 0)),
            pl.BlockSpec((2, rows, channels), lambda i, w: (0, i, 0)),
            pl.BlockSpec((2, rows, channels), lambda i, w: (0, w[PATCH] * steps + i, 0)),
        ],
        [pl.BlockSpec((3, rows, feat), lambda i, w: (0, i, 0))] * split,
        vmem=PACK_VMEM_BYTES,
    )(where, exponents, queries, fresh_kv, cached_kv)


def attend_kernel(split, part, parts, where_ref, *refs):
    q_refs, kv_refs, out_ref = refs[:split], refs[:-1], refs[-1]
    factor = HEAD_DIM**-0.5 * math.log2(math.e)
    tok, feat = q_refs[0].shape[1:]
    count = out_ref.shape[1] // part[1]
    starts = [at * (tok // count) + part[0] for at in range(count)]
    for head in range(feat // HEAD_DIM):
        lanes = pl.ds(head * HEAD_DIM, HEAD_DIM)
        keys = jnp.concatenate([ref[1, :, lanes] for ref in kv_refs], axis=0)
        values = jnp.concatenate([ref[2, :, lanes] for ref in kv_refs], axis=0)
        values = jnp.concatenate([values, jnp.ones_like(values)], axis=1)
        for rel in range(split):
            rows = [q_refs[rel][0, start : start + part[1], lanes] for start in starts]
            query = jnp.concatenate(rows, axis=0) if len(rows) > 1 else rows[0]
            scores = lax.dot_general(
                query, keys, (((1,), (1,)), ((), ())), preferred_element_type=jnp.float32
            )
            peak = jnp.max(scores, axis=1, keepdims=True)
            expo = jnp.exp2((scores - peak) * factor).astype(jnp.bfloat16)
            mix = jnp.dot(expo, values, preferred_element_type=jnp.float32)
            mix = mix[:, :HEAD_DIM] / mix[:, HEAD_DIM:]
            out_ref[where_ref[NEAR] ^ rel, :, lanes] = mix.astype(jnp.bfloat16)


def attend(where, part, count, pieces, kv_pieces):
    split = len(pieces)
    _, tok, feat = pieces[0].shape
    out = jax.ShapeDtypeStruct((split, count * part[1], feat), jnp.bfloat16)
    return call(
        functools.partial(attend_kernel, split, part, count),
        "attend",
        out,
        1,
        [spec((3, tok, feat))] * len(kv_pieces),
        spec(out.shape),
        flops=ATTEND_FLOPS,
    )(where, *kv_pieces)


def project_kernel(split, n_slots, n_more, where_ref, *refs):
    slots, refs = refs[:n_slots], refs[n_slots:]
    more, weight_ref, refs = refs[:n_more], refs[n_more], refs[n_more + 1 :]
    outs, held_ref, acc_ref = refs[:-2], refs[-2], refs[-1]
    rows, feat = slots[0].shape
    n_sub, n_head = acc_ref.shape[3], acc_ref.shape[2]

    @pl.when(pl.program_id(0) == 0)
    def arrange():
        for at, slot in enumerate(slots):
            group, near = divmod(at, split)
            lane = (where_ref[NEAR] ^ near) * feat
            block = slot[...]
            if more and at == n_slots - 1:
                block = jnp.where(where_ref[INNER] == 1, block, more[0][...])
            held_ref[
                group * rows : (group + 1) * rows, pl.ds(pl.multiple_of(lane, HEAD_DIM), feat)
            ] = block

    acc = jnp.dot(held_ref[...], weight_ref[...], preferred_element_type=jnp.float32)
    acc_ref[...] = acc.reshape(acc_ref.shape)
    for sub in range(n_sub):
        for head in range(n_head):
            for at in range(n_slots):
                group, near = divmod(at, split)
                outs[sub][head, at] = acc_ref[
                    group, where_ref[NEAR] ^ near, where_ref[HEAD] ^ head, where_ref[SUB] ^ sub
                ].astype(jnp.bfloat16)


def project(split, where, slots, more, weight, n_head, n_sub):
    rows, feat = slots[0].shape
    n_patch = len(slots)
    total = rows * n_patch // split
    depth, cols = weight.shape
    wide = 640 if cols % 640 == 0 else cols
    piece = rows // (split * n_head * n_sub)
    return call(
        functools.partial(project_kernel, split, n_patch, len(more)),
        "project",
        [jax.ShapeDtypeStruct((n_head, n_patch, piece, cols), jnp.bfloat16)] * n_sub,
        cols // wide,
        [spec((rows, feat))] * (n_patch + len(more))
        + [pl.BlockSpec((depth, wide), lambda i, w: (0, i))],
        [pl.BlockSpec((n_head, n_patch, piece, wide), lambda i, w: (0, 0, 0, i))] * n_sub,
        [
            pltpu.VMEM((total, depth), jnp.bfloat16),
            pltpu.VMEM((n_patch // split, split, n_head, n_sub, piece, wide), jnp.float32),
        ],
        flops=PROJECT_FLOPS,
    )(where, *slots, *more, weight)


def mix_kernel(n_patch, where_ref, hidden_ref, gate_ref, *refs):
    blocks, out_ref = refs[:-1], refs[-1]
    piece, cols = blocks[0].shape
    for part in range(len(blocks) // n_patch):
        rows = pl.ds(part * piece, piece)
        for rel in range(n_patch):
            lanes = pl.ds(pl.multiple_of((where_ref[PATCH] ^ rel) * cols, HEAD_DIM), cols)
            mixed = hidden_ref[rows, lanes].astype(jnp.float32) + gate_ref[:, lanes] * blocks[
                part * n_patch + rel
            ][...].astype(jnp.float32)
            out_ref[rows, lanes] = mixed.astype(jnp.bfloat16)


def mix(where, hidden_in, attn_gate, blocks):
    rows, width = hidden_in.shape
    n_patch = len(blocks[0])
    piece, cols = blocks[0][0].shape
    if cols % HEAD_DIM:
        order = jnp.concatenate([jnp.stack(x) for x in blocks], axis=1)
        order = order[where[PATCH] ^ jnp.arange(n_patch)]
        projected = order.transpose(1, 0, 2).reshape(rows, width).astype(jnp.float32)
        return (hidden_in.astype(jnp.float32) + attn_gate * projected).astype(jnp.bfloat16)
    flat = [x for part in blocks for x in part]
    return call(
        functools.partial(mix_kernel, n_patch),
        "mix",
        jax.ShapeDtypeStruct((rows, width), jnp.bfloat16),
        1,
        [spec((rows, width)), spec((1, width))] + [spec((piece, cols))] * len(flat),
        spec((rows, width)),
    )(where, hidden_in, attn_gate[None], *flat)


def gather(x, n_patch):
    if n_patch != 4:
        return [x] + [swap(x, "patch", n_patch, rel) for rel in range(1, n_patch)], []
    far = swap(x, "patch", 4, 2)
    next_to = swap(x, "patch", 4, 1)
    middle = swap(x, "patch", 4, 3, (1, 2))
    far, next_to = lax.optimization_barrier((far, next_to))
    ends = lax.ppermute(far, "patch", [(1, 0), (2, 3)])
    return [x, next_to, far, middle], [ends]


def add_sub_kernel(n_sub, where_ref, *refs):
    terms, kept_ref, outs = refs[:n_sub], refs[n_sub], refs[n_sub + 1 :]
    for head in range(len(outs) + 1):
        total = terms[0][head].astype(jnp.float32)
        for term in terms[1:]:
            total += term[head].astype(jnp.float32)
        if head == 0:
            kept_ref[...] = total
        else:
            outs[head - 1][...] = total.astype(jnp.bfloat16)


def add_head_kernel(n_more, where_ref, kept_ref, *refs):
    for at, out in enumerate(refs[n_more:]):
        total = kept_ref[at]
        for term in refs[:n_more]:
            total += term[at].astype(jnp.float32)
        out[...] = total.astype(jnp.bfloat16)


def reduce_sub(sizes, where, terms):
    n_sub, n_head = sizes["sub"], sizes["head"]
    terms = [terms[0]] + [swap(terms[rel], "sub", n_sub, rel) for rel in range(1, n_sub)]
    shape = terms[0].shape[1:]
    return call(
        functools.partial(add_sub_kernel, n_sub),
        "add_sub",
        [jax.ShapeDtypeStruct(shape, jnp.float32)]
        + [jax.ShapeDtypeStruct(shape, jnp.bfloat16)] * (n_head - 1),
        1,
        [spec(terms[0].shape)] * n_sub,
        [spec(shape)] * n_head,
    )(where, *terms)


def reduce_head(sizes, where, sums):
    n_head = sizes["head"]
    shape = sums[0].shape
    sums = [sums[0]] + [swap(sums[rel], "head", n_head, rel) for rel in range(1, n_head)]
    return call(
        functools.partial(add_head_kernel, n_head - 1),
        "add_head",
        [jax.ShapeDtypeStruct(shape[1:], jnp.bfloat16)] * shape[0],
        1,
        [spec(shape)] * n_head,
        [spec(shape[1:])] * shape[0],
    )(where, *sums)


def body(sizes, queries, fresh_kv, cached_kv, exponents, out_weight, hidden_in, attn_gate):
    n_patch, n_head, n_sub = sizes["patch"], sizes["head"], sizes["sub"]
    tok, channels = queries.shape
    heads = channels // HEAD_DIM
    split = math.gcd(heads, n_patch)
    patch_at = lax.axis_index("patch")
    inner = (patch_at > 0) & (patch_at < n_patch - 1)
    where = jnp.stack(
        [patch_at, patch_at % split, lax.axis_index("head"), lax.axis_index("sub"), inner]
    ).astype(jnp.int32)

    sent = pack(split, heads // split, where, exponents, queries, fresh_kv, cached_kv)
    pieces = [sent[0]] + [swap(sent[rel], "patch", n_patch, rel) for rel in range(1, split)]
    kv_pieces = list(pieces)
    for rel in range(split, n_patch, split):
        kv_pieces += [swap(x, "patch", n_patch, rel) for x in pieces]

    count = n_head * n_sub
    piece = tok // count
    parts = 2 if piece % 32 == 0 else 1
    slots = []
    for part in range(parts):
        rows = (part * (piece // parts), piece // parts)
        attended = attend(where, rows, count, pieces, kv_pieces)
        attended = attended.reshape(-1, attended.shape[2])
        slots.append(gather(attended, n_patch))
    blocks = []
    for part in range(parts):
        terms = project(split, where, *slots[part], out_weight, n_head, n_sub)
        sums = reduce_sub(sizes, where, terms)
        if part + 1 < parts:
            sums, slots[part + 1] = lax.optimization_barrier((sums, slots[part + 1]))
        total = reduce_head(sizes, where, sums)
        blocks.append(
            [total[0]] + [swap(total[rel], "patch", n_patch, rel) for rel in range(1, n_patch)]
        )
    return mix(where, hidden_in, attn_gate, blocks)


def solution(mesh):
    in_specs = (
        P(("grp", "patch"), ("head", "sub")),
        P(None, ("grp", "patch"), ("head", "sub")),
        P(None, "grp", ("head", "sub")),
        P(None, ("grp", "patch"), ("head", "sub")),
        P(("head", "sub"), "patch"),
        P(("grp", "patch", "head", "sub"), None),
        P(),
    )
    out_specs = P(("grp", "patch", "head", "sub"), None)
    return jax.shard_map(
        functools.partial(body, dict(mesh.shape)),
        mesh=mesh,
        in_specs=in_specs,
        out_specs=out_specs,
        check_vma=False,
    )
```

time: 171 us -> 137 us (0.80)
  blocking collectives: 65.4 us -> 0 us
  waiting for transfers between devices: 41.8 us -> 81.5 us
  starting transfers between devices: 16.7 us -> 33.2 us
  between operations: 13.6 us -> 0.2 us
  local copies, waits for them, and re-layouts: 12.9 us -> 1.68 us
  other arithmetic: 2.04 us -> 0 us
  Pallas kernels: 17.9 us -> 19.9 us
    all_to_all x4 -> x0, blocking collectives: 65.4 us -> none  [the longest x1 26.2 us: body(): lax.all_to_all(x, 'patch', 0, 0, axis_index_groups=near)]
    ppermute x6 -> x19, waiting for transfers between devices: 14.1 us -> 67.1 us  [swap(): return lax.ppermute(x, axes, pairs)]
    all_to_all x1 -> x0, waiting for transfers between devices: 23.9 us -> none  [body(): lax.all_to_all(x, 'patch', 0, 0, axis_index_groups=near)]
    ppermute x6 -> x19, starting transfers between devices: 10.6 us -> 30.7 us  [swap(): return lax.ppermute(x, axes, pairs)]
    unnamed x30 -> x12, local copies, waits for them, and re-layouts: 11.8 us -> 1.02 us
    ppermute x2, waiting for transfers between devices: 3.88 us -> 14.3 us  [gather(): ends = lax.ppermute(far, 'patch', [(1, 0), (2, 3)])]
    all_to_all x1 -> x0, starting transfers between devices: 3.49 us -> none  [body(): lax.all_to_all(x, 'patch', 0, 0, axis_index_groups=near)]
    pallas_call x6 -> x10, Pallas kernels: 17.9 us -> 19.9 us  [the longest x2 6.36 us: project(): call(functools.partial(project_kernel, split, n_patch, len(more)), 'proje...]
  transfers between devices with their start and end apart: 10 -> 21, of which waited for: 4 -> 13; matrix products, arithmetic and copies ran while one was open for 1% -> 0% of each run, Pallas kernels for 7% -> 4%
where the time goes in v5:
time: 137 us; the launch traced here: 136 us
  waiting for transfers between devices  81.5 us (59%)
  starting transfers between devices  33.2 us (24%)
  Pallas kernels  19.9 us (15%)
  local copies, waits for them, and re-layouts  1.68 us (1%)
    ppermute x19, waiting for transfers between devices, swap(): return lax.ppermute(x, axes, pairs)  67.1 us
    ppermute x19, starting transfers between devices, swap(): return lax.ppermute(x, axes, pairs)  30.7 us
    ppermute x2, waiting for transfers between devices, gather(): ends = lax.ppermute(far, 'patch', [(1, 0), (2, 3)])  14.3 us
    pallas_call x2, Pallas kernels, project(): call(functools.partial(project_kernel, split, n_patch, len(more)), 'proje...  6.36 us
    pallas_call x1, Pallas kernels, pack(): call(functools.partial(pack_kernel, split, per), 'pack', [jax.ShapeDtypeS...  4.93 us
    pallas_call x2, Pallas kernels, attend(): call(functools.partial(attend_kernel, split, part, count), 'attend', out,...  4.48 us
  transfers between devices with their start and end apart: 21, of which 13 were waited for; matrix products, arithmetic and copies ran while one was open for 0% of the time, Pallas kernels for 4%

profile of v5, /device:TPU:0, one launch (start us, length us, event | category | flops | bytes accessed | tf_op | source)
XLA Modules:
  0.0 136.5 jit_solution(4590974677156231789)
XLA Ops:
  0.0 0.7 stack.27.where_ref
  0.7 4.9 %pack.1 = (bf16[3,256,256]{2,1,0:T(8,128)(2,1)}, bf16[3,256,256]{2,1,0:T(8,128)(2,1)}, bf16[3,256,256]{2,1,0:T(8,128)(2,1)}, bf16[3,256,256]{2,1,0:T(8,128)(2,1)}) custom-call(s32[5]{0:T(128)} %stack.27.where_ref, s32[2,2,8]{2,1,0:T(2,128)} %exps_ref.1, bf16[256,1024]{1,0:T(8,128)(2,1)} %q_ref.1, bf16[2,256,1024]{2,1,0:T(8,128)(2,1)} %fresh_ref.1, ...), custom_call_target="tpu_custom_call" | custom-call | tf_op jit(solution)/shard_map/pack/pallas_call | solution.py:73
  5.6 3.0 %collective-permute-start = (bf16[3,256,256]{2,1,0:T(8,128)(2,1)}, bf16[3,256,256]{2,1,0:T(8,128)(2,1)S(1)}, u32[]{:S(2)}, u32[]{:S(2)}) collective-permute-start(bf16[3,256,256]{2,1,0:T(8,128)(2,1)} %get-tuple-element.37), channel_id=1, source_target_pairs={{0,4},{4,0},{8,12},{12,8},{1,5},{5,1},{9,13},{13,9},{2,6},{6,2},{1... | collective-permute-start | bytes 1179656 | tf_op jit(solution)/shard_map/ppermute | solution.py:45
  8.6 2.6 %collective-permute-start.1 = (bf16[3,256,256]{2,1,0:T(8,128)(2,1)}, bf16[3,256,256]{2,1,0:T(8,128)(2,1)S(1)}, u32[]{:S(2)}, u32[]{:S(2)}) collective-permute-start(bf16[3,256,256]{2,1,0:T(8,128)(2,1)} %get-tuple-element.38), channel_id=1, source_target_pairs={{0,8},{4,12},{8,0},{12,4},{1,9},{5,13},{9,1},{13,5},{2,10},{6,14},... | collective-permute-start | bytes 1179656 | tf_op jit(solution)/shard_map/ppermute | solution.py:45
  11.2 0.0 collective-permute-start.2
  11.2 14.4 %collective-permute-done.refs_1_ = bf16[3,256,256]{2,1,0:T(8,128)(2,1)S(1)} collective-permute-done((bf16[3,256,256]{2,1,0:T(8,128)(2,1)}, bf16[3,256,256]{2,1,0:T(8,128)(2,1)S(1)}, u32[]{:S(2)}, u32[]{:S(2)}) %collective-permute-start) | collective-permute-done | bytes 393248 | tf_op jit(solution)/shard_map/ppermute | solution.py:45
  25.6 13.0 %collective-permute-done.1.refs_2_ = bf16[3,256,256]{2,1,0:T(8,128)(2,1)S(1)} collective-permute-done((bf16[3,256,256]{2,1,0:T(8,128)(2,1)}, bf16[3,256,256]{2,1,0:T(8,128)(2,1)S(1)}, u32[]{:S(2)}, u32[]{:S(2)}) %collective-permute-start.1) | collective-permute-done | bytes 393248 | tf_op jit(solution)/shard_map/ppermute | solution.py:45
  38.6 0.0 collective-permute-done.2.refs_3_
  38.6 1.0 copy-done.4
  39.6 2.2 %attend.2 = bf16[4,128,256]{2,1,0:T(8,128)(2,1)S(1)} custom-call(s32[5]{0:T(128)S(1)} %copy-done.1, bf16[3,256,256]{2,1,0:T(8,128)(2,1)S(1)} %copy-done.4, bf16[3,256,256]{2,1,0:T(8,128)(2,1)S(1)} %collective-permute-done.refs_1_, bf16[3,256,256]{2,1,0:T(8,128)(2,1)S(1)} %collective-permute-done.1.refs_2_, ...), custom_call_target="tpu_custom_call" | custom-call | flops 5000000000 | tf_op jit(solution)/shard_map/attend/pallas_call | solution.py:117
  41.9 0.0 copy-start.5
  41.9 7.6 %collective-permute-start.4 = (bf16[512,256]{1,0:T(8,128)(2,1)S(1)}, bf16[512,256]{1,0:T(8,128)(2,1)S(1)}, u32[]{:S(2)}, u32[]{:S(2)}) collective-permute-start(bf16[512,256]{1,0:T(8,128)(2,1)S(1)} %bitcast.13), channel_id=1, source_target_pairs={{0,4},{4,0},{8,12},{12,8},{1,5},{5,1},{9,13},{13,9},{2,6},{6,2},{1... | collective-permute-start | bytes 786440 | tf_op jit(solution)/shard_map/ppermute | solution.py:45
  49.5 1.1 collective-permute-start.3
  50.6 0.7 collective-permute-start.5
  51.3 7.5 %collective-permute-done.4.refs_1_ = bf16[512,256]{1,0:T(8,128)(2,1)S(1)} collective-permute-done((bf16[512,256]{1,0:T(8,128)(2,1)S(1)}, bf16[512,256]{1,0:T(8,128)(2,1)S(1)}, u32[]{:S(2)}, u32[]{:S(2)}) %collective-permute-start.4) | collective-permute-done | bytes 262176 | tf_op jit(solution)/shard_map/ppermute | solution.py:45
  58.8 6.4 %collective-permute-done.3.refs_2_ = bf16[512,256]{1,0:T(8,128)(2,1)S(1)} collective-permute-done((bf16[512,256]{1,0:T(8,128)(2,1)S(1)}, bf16[512,256]{1,0:T(8,128)(2,1)S(1)}, u32[]{:S(2)}, u32[]{:S(2)}) %collective-permute-start.3) | collective-permute-done | bytes 262176 | tf_op jit(solution)/shard_map/ppermute | solution.py:45
  65.2 1.3 collective-permute-start.6
  66.5 7.0 %collective-permute-done.6.refs_4_ = bf16[512,256]{1,0:T(8,128)(2,1)S(1)} collective-permute-done((bf16[512,256]{1,0:T(8,128)(2,1)S(1)}, bf16[512,256]{1,0:T(8,128)(2,1)S(1)}, u32[]{:S(2)}, u32[]{:S(2)}) %collective-permute-start.6) | collective-permute-done | bytes 262176 | tf_op jit(solution)/shard_map/ppermute | solution.py:221
  73.5 3.2 %project.2 = (bf16[2,4,32,1280]{3,2,1,0:T(8,128)(2,1)S(1)}, bf16[2,4,32,1280]{3,2,1,0:T(8,128)(2,1)S(1)}) custom-call(s32[5]{0:T(128)S(1)} %copy-done.1, bf16[512,256]{1,0:T(8,128)(2,1)S(1)} %bitcast.16, bf16[512,256]{1,0:T(8,128)(2,1)S(1)} %collective-permute-done.4.refs_1_, bf16[512,256]{1,0:T(8,128)(2,1)S(1)} %collective-permute-done.3.refs_2_, ...), custom_call_target="tpu_custom_call" | custom-call | flops 5000000000 | tf_op jit(solution)/shard_map/project/pallas_call | solution.py:165
  76.7 0.1 collective-permute-start.7
  76.8 2.2 %attend.3 = bf16[4,128,256]{2,1,0:T(8,128)(2,1)S(1)} custom-call(s32[5]{0:T(128)S(1)} %copy-done.1, bf16[3,256,256]{2,1,0:T(8,128)(2,1)S(1)} %copy-done.5, bf16[3,256,256]{2,1,0:T(8,128)(2,1)S(1)} %collective-permute-done.refs_1_, bf16[3,256,256]{2,1,0:T(8,128)(2,1)S(1)} %collective-permute-done.1.refs_2_, ...), custom_call_target="tpu_custom_call" | custom-call | flops 5000000000 | tf_op jit(solution)/shard_map/attend/pallas_call | solution.py:117
  79.0 0.1 collective-permute-start.9
  79.1 2.8 %collective-permute-start.8 = (bf16[512,256]{1,0:T(8,128)(2,1)S(1)}, bf16[512,256]{1,0:T(8,128)(2,1)S(1)}, u32[]{:S(2)}, u32[]{:S(2)}) collective-permute-start(bf16[512,256]{1,0:T(8,128)(2,1)S(1)} %bitcast.10), channel_id=1, source_target_pairs={{0,8},{4,12},{8,0},{12,4},{1,9},{5,13},{9,1},{13,5},{2,10},{6,14},... | collective-permute-start | bytes 786440 | tf_op jit(solution)/shard_map/ppermute | solution.py:45
  81.9 0.7 collective-permute-start.10
  82.6 10.4 %collective-permute-done.9.refs_1_ = bf16[512,256]{1,0:T(8,128)(2,1)S(1)} collective-permute-done((bf16[512,256]{1,0:T(8,128)(2,1)S(1)}, bf16[512,256]{1,0:T(8,128)(2,1)S(1)}, u32[]{:S(2)}, u32[]{:S(2)}) %collective-permute-start.9) | collective-permute-done | bytes 262176 | tf_op jit(solution)/shard_map/ppermute | solution.py:45
  93.0 1.9 %collective-permute-done.8.refs_2_ = bf16[512,256]{1,0:T(8,128)(2,1)S(1)} collective-permute-done((bf16[512,256]{1,0:T(8,128)(2,1)S(1)}, bf16[512,256]{1,0:T(8,128)(2,1)S(1)}, u32[]{:S(2)}, u32[]{:S(2)}) %collective-permute-start.8) | collective-permute-done | bytes 262176 | tf_op jit(solution)/shard_map/ppermute | solution.py:45
  94.8 1.3 collective-permute-start.11
  96.1 0.7 add_sub.2
  96.8 7.4 %collective-permute-done.11.refs_4_ = bf16[512,256]{1,0:T(8,128)(2,1)S(1)} collective-permute-done((bf16[512,256]{1,0:T(8,128)(2,1)S(1)}, bf16[512,256]{1,0:T(8,128)(2,1)S(1)}, u32[]{:S(2)}, u32[]{:S(2)}) %collective-permute-start.11) | collective-permute-done | bytes 262176 | tf_op jit(solution)/shard_map/ppermute | solution.py:221
  104.2 3.2 %project.3 = (bf16[2,4,32,1280]{3,2,1,0:T(8,128)(2,1)S(1)}, bf16[2,4,32,1280]{3,2,1,0:T(8,128)(2,1)S(1)}) custom-call(s32[5]{0:T(128)S(1)} %copy-done.1, bf16[512,256]{1,0:T(8,128)(2,1)S(1)} %bitcast.12, bf16[512,256]{1,0:T(8,128)(2,1)S(1)} %collective-permute-done.9.refs_1_, bf16[512,256]{1,0:T(8,128)(2,1)S(1)} %collective-permute-done.8.refs_2_, ...), custom_call_target="tpu_custom_call" | custom-call | flops 5000000000 | tf_op jit(solution)/shard_map/project/pallas_call | solution.py:165
  107.4 0.1 collective-permute-start.16
  107.5 1.6 %collective-permute-start.12 = (bf16[4,32,1280]{2,1,0:T(8,128)(2,1)S(1)}, bf16[4,32,1280]{2,1,0:T(8,128)(2,1)S(1)}, u32[]{:S(2)}, u32[]{:S(2)}) collective-permute-start(bf16[4,32,1280]{2,1,0:T(8,128)(2,1)S(1)} %get-tuple-element.49), channel_id=1, source_target_pairs={{0,2},{2,0},{1,3},{3,1},{4,6},{6,4},{5,7},{7,5},{8,10},{10,8},{9,1... | collective-permute-start | bytes 983048 | tf_op jit(solution)/shard_map/ppermute | solution.py:45
  109.0 0.5 collective-permute-done.16.refs_1_
  109.6 0.7 add_sub.3
  110.3 1.6 %collective-permute-start.17 = (bf16[4,32,1280]{2,1,0:T(8,128)(2,1)S(1)}, bf16[4,32,1280]{2,1,0:T(8,128)(2,1)S(1)}, u32[]{:S(2)}, u32[]{:S(2)}) collective-permute-start(bf16[4,32,1280]{2,1,0:T(8,128)(2,1)S(1)} %get-tuple-element.62), channel_id=1, source_target_pairs={{0,2},{2,0},{1,3},{3,1},{4,6},{6,4},{5,7},{7,5},{8,10},{10,8},{9,1... | collective-permute-start | bytes 983048 | tf_op jit(solution)/shard_map/ppermute | solution.py:45
  111.8 6.3 %collective-permute-done.12.refs_0_ = bf16[4,32,1280]{2,1,0:T(8,128)(2,1)S(1)} collective-permute-done((bf16[4,32,1280]{2,1,0:T(8,128)(2,1)S(1)}, bf16[4,32,1280]{2,1,0:T(8,128)(2,1)S(1)}, u32[]{:S(2)}, u32[]{:S(2)}) %collective-permute-start.12) | collective-permute-done | bytes 327712 | tf_op jit(solution)/shard_map/ppermute | solution.py:45
  118.1 0.6 add_head.2
  118.7 0.1 collective-permute-start.13
  118.8 2.8 %collective-permute-start.14 = (bf16[32,1280]{1,0:T(8,128)(2,1)S(1)}, bf16[32,1280]{1,0:T(8,128)(2,1)S(1)}, u32[]{:S(2)}, u32[]{:S(2)}) collective-permute-start(bf16[32,1280]{1,0:T(8,128)(2,1)S(1)} %get-tuple-element.52), channel_id=1, source_target_pairs={{0,8},{4,12},{8,0},{12,4},{1,9},{5,13},{9,1},{13,5},{2,10},{6,14},... | collective-permute-start | bytes 245768 | tf_op jit(solution)/shard_map/ppermute | solution.py:45
  121.5 1.6 %collective-permute-start.15 = (bf16[32,1280]{1,0:T(8,128)(2,1)S(1)}, bf16[32,1280]{1,0:T(8,128)(2,1)S(1)}, u32[]{:S(2)}, u32[]{:S(2)}) collective-permute-start(bf16[32,1280]{1,0:T(8,128)(2,1)S(1)} %get-tuple-element.53), channel_id=1, source_target_pairs={{0,12},{4,8},{8,4},{12,0},{1,13},{5,9},{9,5},{13,1},{2,14},{6,10},... | collective-permute-start | bytes 245768 | tf_op jit(solution)/shard_map/ppermute | solution.py:45
  123.1 1.5 %collective-permute-done.17.refs_0_ = bf16[4,32,1280]{2,1,0:T(8,128)(2,1)S(1)} collective-permute-done((bf16[4,32,1280]{2,1,0:T(8,128)(2,1)S(1)}, bf16[4,32,1280]{2,1,0:T(8,128)(2,1)S(1)}, u32[]{:S(2)}, u32[]{:S(2)}) %collective-permute-start.17) | collective-permute-done | bytes 327712 | tf_op jit(solution)/shard_map/ppermute | solution.py:45
  124.6 0.6 add_head.3
  125.2 0.1 collective-permute-start.18
  125.3 2.8 %collective-permute-start.19 = (bf16[32,1280]{1,0:T(8,128)(2,1)S(1)}, bf16[32,1280]{1,0:T(8,128)(2,1)S(1)}, u32[]{:S(2)}, u32[]{:S(2)}) collective-permute-start(bf16[32,1280]{1,0:T(8,128)(2,1)S(1)} %get-tuple-element.65), channel_id=1, source_target_pairs={{0,8},{4,12},{8,0},{12,4},{1,9},{5,13},{9,1},{13,5},{2,10},{6,14},... | collective-permute-start | bytes 245768 | tf_op jit(solution)/shard_map/ppermute | solution.py:45
  128.1 1.6 %collective-permute-start.20 = (bf16[32,1280]{1,0:T(8,128)(2,1)S(1)}, bf16[32,1280]{1,0:T(8,128)(2,1)S(1)}, u32[]{:S(2)}, u32[]{:S(2)}) collective-permute-start(bf16[32,1280]{1,0:T(8,128)(2,1)S(1)} %get-tuple-element.66), channel_id=1, source_target_pairs={{0,12},{4,8},{8,4},{12,0},{1,13},{5,9},{9,5},{13,1},{2,14},{6,10},... | collective-permute-start | bytes 245768 | tf_op jit(solution)/shard_map/ppermute | solution.py:45
  129.7 0.9 collective-permute-done.18.refs_5_
  130.6 4.2 %collective-permute-done.19.refs_6_ = bf16[32,1280]{1,0:T(8,128)(2,1)S(1)} collective-permute-done((bf16[32,1280]{1,0:T(8,128)(2,1)S(1)}, bf16[32,1280]{1,0:T(8,128)(2,1)S(1)}, u32[]{:S(2)}, u32[]{:S(2)}) %collective-permute-start.19) | collective-permute-done | bytes 81952 | tf_op jit(solution)/shard_map/ppermute | solution.py:45
  134.9 1.6 %mix.1 = bf16[64,5120]{1,0:T(8,128)(2,1)} custom-call(s32[5]{0:T(128)S(1)} %copy-done.1, bf16[64,5120]{1,0:T(8,128)(2,1)S(1)} %copy-done, f32[1,5120]{1,0:T(1,128)S(1)} %bitcast.8, bf16[32,1280]{1,0:T(8,128)(2,1)S(1)} %get-tuple-element.50.refs_0_, bf16[32,1280]{1,0:T(8,128)(2,1)S(1)} %collective-permute-done.13.refs_1_, ...), custom_call_target="tpu_custom_call" | custom-call | tf_op jit(solution)/shard_map/mix/pallas_call | solution.py:204
  (17 shorter events, 0.0 us)
Async XLA Ops:
  0.7 38.0 %copy-start.1 = (s32[5]{0:T(128)S(1)}, s32[5]{0:T(128)}, u32[]{:S(2)}) copy-start(s32[5]{0:T(128)} %stack.27.where_ref) | copy-start | bytes 64
  5.6 20.0 %collective-permute-start = (bf16[3,256,256]{2,1,0:T(8,128)(2,1)}, bf16[3,256,256]{2,1,0:T(8,128)(2,1)S(1)}, u32[]{:S(2)}, u32[]{:S(2)}) collective-permute-start(bf16[3,256,256]{2,1,0:T(8,128)(2,1)} %get-tuple-element.37), channel_id=1, source_target_pairs={{0,4},{4,0},{8,12},{12,8},{1,5},{5,1},{9,13},{13,9},{2,6},{6,2},{1... | collective-permute-start | bytes 1179656 | tf_op jit(solution)/shard_map/ppermute | solution.py:45
  8.6 30.0 %collective-permute-start.1 = (bf16[3,256,256]{2,1,0:T(8,128)(2,1)}, bf16[3,256,256]{2,1,0:T(8,128)(2,1)S(1)}, u32[]{:S(2)}, u32[]{:S(2)}) collective-permute-start(bf16[3,256,256]{2,1,0:T(8,128)(2,1)} %get-tuple-element.38), channel_id=1, source_target_pairs={{0,8},{4,12},{8,0},{12,4},{1,9},{5,13},{9,1},{13,5},{2,10},{6,14},... | collective-permute-start | bytes 1179656 | tf_op jit(solution)/shard_map/ppermute | solution.py:45
  11.2 27.4 %collective-permute-start.2 = (bf16[3,256,256]{2,1,0:T(8,128)(2,1)}, bf16[3,256,256]{2,1,0:T(8,128)(2,1)S(1)}, u32[]{:S(2)}, u32[]{:S(2)}) collective-permute-start(bf16[3,256,256]{2,1,0:T(8,128)(2,1)} %get-tuple-element.39), channel_id=1, source_target_pairs={{0,12},{4,8},{8,4},{12,0},{1,13},{5,9},{9,5},{13,1},{2,14},{6,10},... | collective-permute-start | bytes 1179656 | tf_op jit(solution)/shard_map/ppermute | solution.py:45
  38.6 1.0 copy-start.4
  39.6 33.9 %copy-start.3 = (bf16[1024,1280]{1,0:T(8,128)(2,1)S(1)}, bf16[1024,1280]{1,0:T(8,128)(2,1)}, u32[]{:S(2)}) copy-start(bf16[1024,1280]{1,0:T(8,128)(2,1)} %refs_5_.3) | copy-start | bytes 7864324
  41.9 34.9 %copy-start.5 = (bf16[3,256,256]{2,1,0:T(8,128)(2,1)S(1)}, bf16[3,256,256]{2,1,0:T(8,128)(2,1)}, u32[]{:S(2)}) copy-start(bf16[3,256,256]{2,1,0:T(8,128)(2,1)} %get-tuple-element.36.refs_0_) | copy-start | bytes 1179652
  41.9 16.9 %collective-permute-start.4 = (bf16[512,256]{1,0:T(8,128)(2,1)S(1)}, bf16[512,256]{1,0:T(8,128)(2,1)S(1)}, u32[]{:S(2)}, u32[]{:S(2)}) collective-permute-start(bf16[512,256]{1,0:T(8,128)(2,1)S(1)} %bitcast.13), channel_id=1, source_target_pairs={{0,4},{4,0},{8,12},{12,8},{1,5},{5,1},{9,13},{13,9},{2,6},{6,2},{1... | collective-permute-start | bytes 786440 | tf_op jit(solution)/shard_map/ppermute | solution.py:45
  49.5 15.7 %collective-permute-start.3 = (bf16[512,256]{1,0:T(8,128)(2,1)S(1)}, bf16[512,256]{1,0:T(8,128)(2,1)S(1)}, u32[]{:S(2)}, u32[]{:S(2)}) collective-permute-start(bf16[512,256]{1,0:T(8,128)(2,1)S(1)} %bitcast.14), channel_id=1, source_target_pairs={{0,8},{4,12},{8,0},{12,4},{1,9},{5,13},{9,1},{13,5},{2,10},{6,14},... | collective-permute-start | bytes 786440 | tf_op jit(solution)/shard_map/ppermute | solution.py:45
  50.6 15.9 %collective-permute-start.5 = (bf16[512,256]{1,0:T(8,128)(2,1)S(1)}, bf16[512,256]{1,0:T(8,128)(2,1)S(1)}, u32[]{:S(2)}, u32[]{:S(2)}) collective-permute-start(bf16[512,256]{1,0:T(8,128)(2,1)S(1)} %bitcast.15), channel_id=1, source_target_pairs={{4,8},{8,4},{5,9},{9,5},{6,10},{10,6},{7,11},{11,7},{20,24},{24,20... | collective-permute-start | bytes 786440 | tf_op jit(solution)/shard_map/ppermute | solution.py:45
  65.2 8.3 %collective-permute-start.6 = (bf16[512,256]{1,0:T(8,128)(2,1)S(1)}, bf16[512,256]{1,0:T(8,128)(2,1)S(1)}, u32[]{:S(2)}, u32[]{:S(2)}) collective-permute-start(bf16[512,256]{1,0:T(8,128)(2,1)S(1)} %collective-permute-done.3.refs_2_), channel_id=1, source_target_pairs={{4,0},{8,12},{5,1},{9,13},{6,2},{10,14},{7,3},{11,15},{20,16},{24,... | collective-permute-start | bytes 786440 | tf_op jit(solution)/shard_map/ppermute | solution.py:221
  76.7 19.4 %collective-permute-start.7 = (bf16[2,4,32,1280]{3,2,1,0:T(8,128)(2,1)S(1)}, bf16[2,4,32,1280]{3,2,1,0:T(8,128)(2,1)S(1)}, u32[]{:S(2)}, u32[]{:S(2)}) collective-permute-start(bf16[2,4,32,1280]{3,2,1,0:T(8,128)(2,1)S(1)} %get-tuple-element.43), channel_id=1, source_target_pairs={{0,1},{1,0},{2,3},{3,2},{4,5},{5,4},{6,7},{7,6},{8,9},{9,8},{10,11... | collective-permute-start | bytes 1966088 | tf_op jit(solution)/shard_map/ppermute | solution.py:45
  79.0 14.0 %collective-permute-start.9 = (bf16[512,256]{1,0:T(8,128)(2,1)S(1)}, bf16[512,256]{1,0:T(8,128)(2,1)S(1)}, u32[]{:S(2)}, u32[]{:S(2)}) collective-permute-start(bf16[512,256]{1,0:T(8,128)(2,1)S(1)} %bitcast.9), channel_id=1, source_target_pairs={{0,4},{4,0},{8,12},{12,8},{1,5},{5,1},{9,13},{13,9},{2,6},{6,2},{1... | collective-permute-start | bytes 786440 | tf_op jit(solution)/shard_map/ppermute | solution.py:45
  79.1 15.7 %collective-permute-start.8 = (bf16[512,256]{1,0:T(8,128)(2,1)S(1)}, bf16[512,256]{1,0:T(8,128)(2,1)S(1)}, u32[]{:S(2)}, u32[]{:S(2)}) collective-permute-start(bf16[512,256]{1,0:T(8,128)(2,1)S(1)} %bitcast.10), channel_id=1, source_target_pairs={{0,8},{4,12},{8,0},{12,4},{1,9},{5,13},{9,1},{13,5},{2,10},{6,14},... | collective-permute-start | bytes 786440 | tf_op jit(solution)/shard_map/ppermute | solution.py:45
  81.9 14.9 %collective-permute-start.10 = (bf16[512,256]{1,0:T(8,128)(2,1)S(1)}, bf16[512,256]{1,0:T(8,128)(2,1)S(1)}, u32[]{:S(2)}, u32[]{:S(2)}) collective-permute-start(bf16[512,256]{1,0:T(8,128)(2,1)S(1)} %bitcast.11), channel_id=1, source_target_pairs={{4,8},{8,4},{5,9},{9,5},{6,10},{10,6},{7,11},{11,7},{20,24},{24,20... | collective-permute-start | bytes 786440 | tf_op jit(solution)/shard_map/ppermute | solution.py:45
  94.8 9.4 %collective-permute-start.11 = (bf16[512,256]{1,0:T(8,128)(2,1)S(1)}, bf16[512,256]{1,0:T(8,128)(2,1)S(1)}, u32[]{:S(2)}, u32[]{:S(2)}) collective-permute-start(bf16[512,256]{1,0:T(8,128)(2,1)S(1)} %collective-permute-done.8.refs_2_), channel_id=1, source_target_pairs={{4,0},{8,12},{5,1},{9,13},{6,2},{10,14},{7,3},{11,15},{20,16},{24,... | collective-permute-start | bytes 786440 | tf_op jit(solution)/shard_map/ppermute | solution.py:221
  104.2 30.7 %copy-start = (bf16[64,5120]{1,0:T(8,128)(2,1)S(1)}, bf16[64,5120]{1,0:T(8,128)(2,1)}, u32[]{:S(2)}) copy-start(bf16[64,5120]{1,0:T(8,128)(2,1)} %hidden_ref.1) | copy-start | bytes 1966084
  104.2 30.7 %copy-start.2 = (f32[5120]{0:T(1024)S(1)}, f32[5120]{0:T(1024)}, u32[]{:S(2)}) copy-start(f32[5120]{0:T(1024)} %param.13) | copy-start | bytes 61444
  107.4 2.2 %collective-permute-start.16 = (bf16[2,4,32,1280]{3,2,1,0:T(8,128)(2,1)S(1)}, bf16[2,4,32,1280]{3,2,1,0:T(8,128)(2,1)S(1)}, u32[]{:S(2)}, u32[]{:S(2)}) collective-permute-start(bf16[2,4,32,1280]{3,2,1,0:T(8,128)(2,1)S(1)} %get-tuple-element.60), channel_id=1, source_target_pairs={{0,1},{1,0},{2,3},{3,2},{4,5},{5,4},{6,7},{7,6},{8,9},{9,8},{10,11... | collective-permute-start | bytes 1966088 | tf_op jit(solution)/shard_map/ppermute | solution.py:45
  107.5 10.6 %collective-permute-start.12 = (bf16[4,32,1280]{2,1,0:T(8,128)(2,1)S(1)}, bf16[4,32,1280]{2,1,0:T(8,128)(2,1)S(1)}, u32[]{:S(2)}, u32[]{:S(2)}) collective-permute-start(bf16[4,32,1280]{2,1,0:T(8,128)(2,1)S(1)} %get-tuple-element.49), channel_id=1, source_target_pairs={{0,2},{2,0},{1,3},{3,1},{4,6},{6,4},{5,7},{7,5},{8,10},{10,8},{9,1... | collective-permute-start | bytes 983048 | tf_op jit(solution)/shard_map/ppermute | solution.py:45
  110.3 14.4 %collective-permute-start.17 = (bf16[4,32,1280]{2,1,0:T(8,128)(2,1)S(1)}, bf16[4,32,1280]{2,1,0:T(8,128)(2,1)S(1)}, u32[]{:S(2)}, u32[]{:S(2)}) collective-permute-start(bf16[4,32,1280]{2,1,0:T(8,128)(2,1)S(1)} %get-tuple-element.62), channel_id=1, source_target_pairs={{0,2},{2,0},{1,3},{3,1},{4,6},{6,4},{5,7},{7,5},{8,10},{10,8},{9,1... | collective-permute-start | bytes 983048 | tf_op jit(solution)/shard_map/ppermute | solution.py:45
  118.7 9.4 %collective-permute-start.13 = (bf16[32,1280]{1,0:T(8,128)(2,1)S(1)}, bf16[32,1280]{1,0:T(8,128)(2,1)S(1)}, u32[]{:S(2)}, u32[]{:S(2)}) collective-permute-start(bf16[32,1280]{1,0:T(8,128)(2,1)S(1)} %get-tuple-element.51), channel_id=1, source_target_pairs={{0,4},{4,0},{8,12},{12,8},{1,5},{5,1},{9,13},{13,9},{2,6},{6,2},{1... | collective-permute-start | bytes 245768 | tf_op jit(solution)/shard_map/ppermute | solution.py:45
  118.8 11.0 %collective-permute-start.14 = (bf16[32,1280]{1,0:T(8,128)(2,1)S(1)}, bf16[32,1280]{1,0:T(8,128)(2,1)S(1)}, u32[]{:S(2)}, u32[]{:S(2)}) collective-permute-start(bf16[32,1280]{1,0:T(8,128)(2,1)S(1)} %get-tuple-element.52), channel_id=1, source_target_pairs={{0,8},{4,12},{8,0},{12,4},{1,9},{5,13},{9,1},{13,5},{2,10},{6,14},... | collective-permute-start | bytes 245768 | tf_op jit(solution)/shard_map/ppermute | solution.py:45
  121.5 8.2 %collective-permute-start.15 = (bf16[32,1280]{1,0:T(8,128)(2,1)S(1)}, bf16[32,1280]{1,0:T(8,128)(2,1)S(1)}, u32[]{:S(2)}, u32[]{:S(2)}) collective-permute-start(bf16[32,1280]{1,0:T(8,128)(2,1)S(1)} %get-tuple-element.53), channel_id=1, source_target_pairs={{0,12},{4,8},{8,4},{12,0},{1,13},{5,9},{9,5},{13,1},{2,14},{6,10},... | collective-permute-start | bytes 245768 | tf_op jit(solution)/shard_map/ppermute | solution.py:45
  125.2 5.4 %collective-permute-start.18 = (bf16[32,1280]{1,0:T(8,128)(2,1)S(1)}, bf16[32,1280]{1,0:T(8,128)(2,1)S(1)}, u32[]{:S(2)}, u32[]{:S(2)}) collective-permute-start(bf16[32,1280]{1,0:T(8,128)(2,1)S(1)} %get-tuple-element.64), channel_id=1, source_target_pairs={{0,4},{4,0},{8,12},{12,8},{1,5},{5,1},{9,13},{13,9},{2,6},{6,2},{1... | collective-permute-start | bytes 245768 | tf_op jit(solution)/shard_map/ppermute | solution.py:45
  125.3 9.5 %collective-permute-start.19 = (bf16[32,1280]{1,0:T(8,128)(2,1)S(1)}, bf16[32,1280]{1,0:T(8,128)(2,1)S(1)}, u32[]{:S(2)}, u32[]{:S(2)}) collective-permute-start(bf16[32,1280]{1,0:T(8,128)(2,1)S(1)} %get-tuple-element.65), channel_id=1, source_target_pairs={{0,8},{4,12},{8,0},{12,4},{1,9},{5,13},{9,1},{13,5},{2,10},{6,14},... | collective-permute-start | bytes 245768 | tf_op jit(solution)/shard_map/ppermute | solution.py:45
  128.1 6.8 %collective-permute-start.20 = (bf16[32,1280]{1,0:T(8,128)(2,1)S(1)}, bf16[32,1280]{1,0:T(8,128)(2,1)S(1)}, u32[]{:S(2)}, u32[]{:S(2)}) collective-permute-start(bf16[32,1280]{1,0:T(8,128)(2,1)S(1)} %get-tuple-element.66), channel_id=1, source_target_pairs={{0,12},{4,8},{8,4},{12,0},{1,13},{5,9},{9,5},{13,1},{2,14},{6,10},... | collective-permute-start | bytes 245768 | tf_op jit(solution)/shard_map/ppermute | solution.py:45

commit v6 on v5

--- a/solution.py
+++ b/solution.py
@@ -13,8 +13,8 @@
 SATURATION = 448.0
 VMEM_BYTES = 32 * 1024 * 1024
 PACK_VMEM_BYTES = 60 * 1024 * 1024
-ATTEND_FLOPS = 5_000_000_000
-PROJECT_FLOPS = 5_000_000_000
+ATTEND_FLOPS = 1
+PROJECT_FLOPS = 1
 
 PATCH, NEAR, HEAD, SUB, INNER = range(5)
 
@@ -23,7 +23,7 @@
     return pl.BlockSpec(shape, lambda i, w: (0,) * len(shape))
 
 
-def call(kernel, name, out_shape, grid, in_specs, out_specs, scratch=(), flops=0, vmem=VMEM_BYTES):
+def call(kernel, name, out_shape, grid, in_specs, out_specs, scratch=(), flops=1, vmem=VMEM_BYTES):
     return pl.pallas_call(
         kernel,
         out_shape=out_shape,
@@ -45,17 +45,19 @@
     return lax.ppermute(x, axes, pairs)
 
 
-def pack_kernel(split, per, where_ref, exps_ref, q_ref, fresh_ref, cached_ref, *outs):
+def pack_kernel(span, per, upper, where_ref, exps_ref, q_ref, fresh_ref, cached_ref, *outs):
     rows = q_ref.shape[0]
     block = pl.program_id(0) * rows // SCALE_ROWS
-    for rel in range(split):
+    half = (where_ref[NEAR] // span) ^ upper
+    for rel in range(span):
         for chunk in range(per):
-            head = (where_ref[NEAR] ^ rel) * per + chunk
+            head = ((where_ref[NEAR] % span) ^ rel) * per + chunk
             lanes = pl.ds(pl.multiple_of(head * HEAD_DIM, HEAD_DIM), HEAD_DIM)
             here = pl.ds(chunk * HEAD_DIM, HEAD_DIM)
             outs[rel][0, :, here] = q_ref[:, lanes]
             for stacked in range(2):
-                power = jnp.full((1, HEAD_DIM), exps_ref[stacked, block, head].astype(jnp.float32))
+                exponent = exps_ref[stacked, block, half * span * per + head]
+                power = jnp.full((1, HEAD_DIM), exponent.astype(jnp.float32))
                 cached = cached_ref[stacked, :, lanes].astype(jnp.float32)
                 residual = fresh_ref[stacked, :, lanes].astype(jnp.float32) - cached
                 codes = jnp.clip(
@@ -65,23 +67,28 @@
                 outs[rel][1 + stacked, :, here] = decoded.astype(jnp.bfloat16)
 
 
-def pack(split, per, where, exponents, queries, fresh_kv, cached_kv):
+def pack(split, per, upper, where, exponents, queries, fresh_kv, cached_kv):
     tok, channels = queries.shape
-    feat = channels // split
-    rows = SCALE_ROWS // 2
+    span = split // 2
+    wide, feat = channels // 2, channels // split
+    rows = SCALE_ROWS
     steps = tok // rows
-    return call(
-        functools.partial(pack_kernel, split, per),
+
+    def half(w):
+        return (w[NEAR] // span) ^ upper
+
+    return call(
+        functools.partial(pack_kernel, span, per, upper),
         "pack",
-        [jax.ShapeDtypeStruct((3, tok, feat), jnp.bfloat16)] * split,
+        [jax.ShapeDtypeStruct((3, tok, feat), jnp.bfloat16)] * span,
         steps,
         [
             pl.BlockSpec(memory_space=pltpu.SMEM),
-            pl.BlockSpec((rows, channels), lambda i, w: (i, 0)),
-            pl.BlockSpec((2, rows, channels), lambda i, w: (0, i, 0)),
-            pl.BlockSpec((2, rows, channels), lambda i, w: (0, w[PATCH] * steps + i, 0)),
+            pl.BlockSpec((rows, wide), lambda i, w: (i, half(w))),
+            pl.BlockSpec((2, rows, wide), lambda i, w: (0, i, half(w))),
+            pl.BlockSpec((2, rows, wide), lambda i, w: (0, w[PATCH] * steps + i, half(w))),
         ],
-        [pl.BlockSpec((3, rows, feat), lambda i, w: (0, i, 0))] * split,
+        [pl.BlockSpec((3, rows, feat), lambda i, w: (0, i, 0))] * span,
         vmem=PACK_VMEM_BYTES,
     )(where, exponents, queries, fresh_kv, cached_kv)
 
@@ -211,15 +218,25 @@
     )(where, hidden_in, attn_gate[None], *flat)
 
 
-def gather(x, n_patch):
+def gather(parts, n_patch):
     if n_patch != 4:
-        return [x] + [swap(x, "patch", n_patch, rel) for rel in range(1, n_patch)], []
-    far = swap(x, "patch", 4, 2)
-    next_to = swap(x, "patch", 4, 1)
-    middle = swap(x, "patch", 4, 3, (1, 2))
-    far, next_to = lax.optimization_barrier((far, next_to))
-    ends = lax.ppermute(far, "patch", [(1, 0), (2, 3)])
-    return [x, next_to, far, middle], [ends]
+        return [
+            ([x] + [swap(x, "patch", n_patch, rel) for rel in range(1, n_patch)], [])
+            for x in parts
+        ]
+    far = [swap(x, "patch", 4, 2) for x in parts]
+    next_to = [swap(x, "patch", 4, 1) for x in parts]
+    middle = [swap(x, "patch", 4, 3, (1, 2)) for x in parts]
+    out = []
+    for at, x in enumerate(parts):
+        far[at], next_to[at], parts = lax.optimization_barrier((far[at], next_to[at], parts))
+        ends = lax.ppermute(far[at], "patch", [(1, 0), (2, 3)])
+        if at + 1 < len(parts):
+            ends, far[at + 1], next_to[at + 1] = lax.optimization_barrier(
+                (ends, far[at + 1], next_to[at + 1])
+            )
+        out.append(([x, next_to[at], far[at], middle[at]], [ends]))
+    return out
 
 
 def add_sub_kernel(n_sub, where_ref, *refs):
@@ -282,7 +299,10 @@
         [patch_at, patch_at % split, lax.axis_index("head"), lax.axis_index("sub"), inner]
     ).astype(jnp.int32)
 
-    sent = pack(split, heads // split, where, exponents, queries, fresh_kv, cached_kv)
+    arrays = (exponents, queries, fresh_kv, cached_kv)
+    upper = pack(split, heads // split, 1, where, *arrays)
+    upper, where = lax.optimization_barrier((upper, where))
+    sent = [*pack(split, heads // split, 0, where, *arrays), *upper]
     pieces = [sent[0]] + [swap(sent[rel], "patch", n_patch, rel) for rel in range(1, split)]
     kv_pieces = list(pieces)
     for rel in range(split, n_patch, split):
@@ -291,12 +311,12 @@
     count = n_head * n_sub
     piece = tok // count
     parts = 2 if piece % 32 == 0 else 1
-    slots = []
+    attended = []
     for part in range(parts):
         rows = (part * (piece // parts), piece // parts)
-        attended = attend(where, rows, count, pieces, kv_pieces)
-        attended = attended.reshape(-1, attended.shape[2])
-        slots.append(gather(attended, n_patch))
+        x = attend(where, rows, count, pieces, kv_pieces)
+        attended.append(x.reshape(-1, x.shape[2]))
+    slots = gather(attended, n_patch)
     blocks = []
     for part in range(parts):
         terms = project(split, where, *slots[part], out_weight, n_head, n_sub)

time: 137 us -> 127 us (0.927)
  waiting for transfers between devices: 81.5 us -> 70.6 us
  Pallas kernels: 19.9 us -> 21.4 us
    ppermute x19, waiting for transfers between devices: 67.1 us -> 58.7 us  [swap(): return lax.ppermute(x, axes, pairs)]
    ppermute x2, waiting for transfers between devices: 14.3 us -> 11.9 us  [gather(): ends = lax.ppermute(far[at], 'patch', [(1, 0), (2, 3)])]
    pallas_call x1 -> x2, Pallas kernels: 4.93 us -> 6.36 us  [pack(): call(functools.partial(pack_kernel, span, per, upper), 'pack', [jax.Shape...]
where the time goes in v6:
time: 127 us; the launch traced here: 126 us
  waiting for transfers between devices  70.6 us (56%)
  starting transfers between devices  32.5 us (26%)
  Pallas kernels  21.4 us (17%)
  local copies, waits for them, and re-layouts  1.65 us (1%)
    ppermute x19, waiting for transfers between devices, swap(): return lax.ppermute(x, axes, pairs)  58.7 us
    ppermute x19, starting transfers between devices, swap(): return lax.ppermute(x, axes, pairs)  29.9 us
    ppermute x2, waiting for transfers between devices, gather(): ends = lax.ppermute(far[at], 'patch', [(1, 0), (2, 3)])  11.9 us
    pallas_call x2, Pallas kernels, project(): call(functools.partial(project_kernel, split, n_patch, len(more)), 'proje...  6.37 us
    pallas_call x2, Pallas kernels, pack(): call(functools.partial(pack_kernel, span, per, upper), 'pack', [jax.Shape...  6.36 us
    pallas_call x2, Pallas kernels, attend(): call(functools.partial(attend_kernel, split, part, count), 'attend', out,...  4.48 us
    ppermute x2, starting transfers between devices, gather(): ends = lax.ppermute(far[at], 'patch', [(1, 0), (2, 3)])  2.57 us
  transfers between devices with their start and end apart: 21, of which 13 were waited for; matrix products, arithmetic and copies ran while one was open for 0% of the time, Pallas kernels for 4%

profile of v6, /device:TPU:0, one launch (start us, length us, event | category | flops | bytes accessed | tf_op | source)
XLA Modules:
  0.0 126.3 jit_solution(397461537320258597)
XLA Ops:
  0.0 0.6 stack.27.where_ref
  0.6 3.0 %pack.2 = (bf16[3,256,256]{2,1,0:T(8,128)(2,1)}, bf16[3,256,256]{2,1,0:T(8,128)(2,1)}) custom-call(s32[5]{0:T(128)} %stack.27.where_ref, s32[2,2,8]{2,1,0:T(2,128)} %exps_ref.3, bf16[256,1024]{1,0:T(8,128)(2,1)} %q_ref.3, bf16[2,256,1024]{2,1,0:T(8,128)(2,1)} %fresh_ref.3, bf16[2,1024,1024]{2,1,0:T(8,128)(2,1)} %cached_ref.3), custom_call_target="tpu_custom_call" | custom-call | flops 1 | tf_op jit(solution)/shard_map/pack/pallas_call | solution.py:80
  3.7 0.0 copy-start
  3.7 3.3 %pack.3 = (bf16[3,256,256]{2,1,0:T(8,128)(2,1)}, bf16[3,256,256]{2,1,0:T(8,128)(2,1)}) custom-call(s32[5]{0:T(128)} %stack.27.where_ref, s32[2,2,8]{2,1,0:T(2,128)} %exps_ref.3, bf16[256,1024]{1,0:T(8,128)(2,1)} %q_ref.3, bf16[2,256,1024]{2,1,0:T(8,128)(2,1)} %fresh_ref.3, bf16[2,1024,1024]{2,1,0:T(8,128)(2,1)} %cached_ref.3), custom_call_target="tpu_custom_call" | custom-call | flops 1 | tf_op jit(solution)/shard_map/pack/pallas_call | solution.py:80
  7.0 3.0 %collective-permute-start = (bf16[3,256,256]{2,1,0:T(8,128)(2,1)}, bf16[3,256,256]{2,1,0:T(8,128)(2,1)S(1)}, u32[]{:S(2)}, u32[]{:S(2)}) collective-permute-start(bf16[3,256,256]{2,1,0:T(8,128)(2,1)} %get-tuple-element.46), channel_id=1, source_target_pairs={{0,4},{4,0},{8,12},{12,8},{1,5},{5,1},{9,13},{13,9},{2,6},{6,2},{1... | collective-permute-start | bytes 1179656 | tf_op jit(solution)/shard_map/ppermute | solution.py:45
  10.0 2.6 %collective-permute-start.1 = (bf16[3,256,256]{2,1,0:T(8,128)(2,1)S(1)}, bf16[3,256,256]{2,1,0:T(8,128)(2,1)S(1)}, u32[]{:S(2)}, u32[]{:S(2)}) collective-permute-start(bf16[3,256,256]{2,1,0:T(8,128)(2,1)S(1)} %copy-done.6), channel_id=1, source_target_pairs={{0,8},{4,12},{8,0},{12,4},{1,9},{5,13},{9,1},{13,5},{2,10},{6,14},... | collective-permute-start | bytes 1179656 | tf_op jit(solution)/shard_map/ppermute | solution.py:45
  12.6 14.5 %collective-permute-done.refs_1_ = bf16[3,256,256]{2,1,0:T(8,128)(2,1)S(1)} collective-permute-done((bf16[3,256,256]{2,1,0:T(8,128)(2,1)}, bf16[3,256,256]{2,1,0:T(8,128)(2,1)S(1)}, u32[]{:S(2)}, u32[]{:S(2)}) %collective-permute-start) | collective-permute-done | bytes 393248 | tf_op jit(solution)/shard_map/ppermute | solution.py:45
  27.1 12.7 %collective-permute-done.1.refs_2_ = bf16[3,256,256]{2,1,0:T(8,128)(2,1)S(1)} collective-permute-done((bf16[3,256,256]{2,1,0:T(8,128)(2,1)S(1)}, bf16[3,256,256]{2,1,0:T(8,128)(2,1)S(1)}, u32[]{:S(2)}, u32[]{:S(2)}) %collective-permute-start.1) | collective-permute-done | bytes 393248 | tf_op jit(solution)/shard_map/ppermute | solution.py:45
  39.8 0.0 collective-permute-done.2.refs_3_
  39.9 1.0 copy-done.1
  40.8 2.2 %attend.2 = bf16[4,128,256]{2,1,0:T(8,128)(2,1)S(1)} custom-call(s32[5]{0:T(128)S(1)} %copy-done.3, bf16[3,256,256]{2,1,0:T(8,128)(2,1)S(1)} %copy-done.1, bf16[3,256,256]{2,1,0:T(8,128)(2,1)S(1)} %collective-permute-done.refs_1_, bf16[3,256,256]{2,1,0:T(8,128)(2,1)S(1)} %collective-permute-done.1.refs_2_, ...), custom_call_target="tpu_custom_call" | custom-call | flops 1 | tf_op jit(solution)/shard_map/attend/pallas_call | solution.py:124
  43.1 8.6 %collective-permute-start.3 = (bf16[512,256]{1,0:T(8,128)(2,1)S(1)}, bf16[512,256]{1,0:T(8,128)(2,1)S(1)}, u32[]{:S(2)}, u32[]{:S(2)}) collective-permute-start(bf16[512,256]{1,0:T(8,128)(2,1)S(1)} %bitcast.12), channel_id=1, source_target_pairs={{0,8},{4,12},{8,0},{12,4},{1,9},{5,13},{9,1},{13,5},{2,10},{6,14},... | collective-permute-start | bytes 786440 | tf_op jit(solution)/shard_map/ppermute | solution.py:45
  51.7 2.2 %attend.3 = bf16[4,128,256]{2,1,0:T(8,128)(2,1)S(1)} custom-call(s32[5]{0:T(128)S(1)} %copy-done.3, bf16[3,256,256]{2,1,0:T(8,128)(2,1)S(1)} %copy-done.1, bf16[3,256,256]{2,1,0:T(8,128)(2,1)S(1)} %collective-permute-done.refs_1_, bf16[3,256,256]{2,1,0:T(8,128)(2,1)S(1)} %collective-permute-done.1.refs_2_, ...), custom_call_target="tpu_custom_call" | custom-call | flops 1 | tf_op jit(solution)/shard_map/attend/pallas_call | solution.py:124
  54.0 2.0 %collective-permute-start.7 = (bf16[512,256]{1,0:T(8,128)(2,1)S(1)}, bf16[512,256]{1,0:T(8,128)(2,1)S(1)}, u32[]{:S(2)}, u32[]{:S(2)}) collective-permute-start(bf16[512,256]{1,0:T(8,128)(2,1)S(1)} %bitcast.8), channel_id=1, source_target_pairs={{0,8},{4,12},{8,0},{12,4},{1,9},{5,13},{9,1},{13,5},{2,10},{6,14},... | collective-permute-start | bytes 786440 | tf_op jit(solution)/shard_map/ppermute | solution.py:45
  56.0 0.2 collective-permute-start.8
  56.2 11.1 %collective-permute-done.3.refs_2_ = bf16[512,256]{1,0:T(8,128)(2,1)S(1)} collective-permute-done((bf16[512,256]{1,0:T(8,128)(2,1)S(1)}, bf16[512,256]{1,0:T(8,128)(2,1)S(1)}, u32[]{:S(2)}, u32[]{:S(2)}) %collective-permute-start.3) | collective-permute-done | bytes 262176 | tf_op jit(solution)/shard_map/ppermute | solution.py:45
  67.2 1.3 %collective-permute-start.6 = (bf16[512,256]{1,0:T(8,128)(2,1)S(1)}, bf16[512,256]{1,0:T(8,128)(2,1)S(1)}, u32[]{:S(2)}, u32[]{:S(2)}) collective-permute-start(bf16[512,256]{1,0:T(8,128)(2,1)S(1)} %collective-permute-done.3.refs_2_), channel_id=1, source_target_pairs={{4,0},{8,12},{5,1},{9,13},{6,2},{10,14},{7,3},{11,15},{20,16},{24,... | collective-permute-start | bytes 786440 | tf_op jit(solution)/shard_map/ppermute | solution.py:233
  68.5 0.7 collective-permute-start.5
  69.2 5.9 %collective-permute-done.7.refs_2_ = bf16[512,256]{1,0:T(8,128)(2,1)S(1)} collective-permute-done((bf16[512,256]{1,0:T(8,128)(2,1)S(1)}, bf16[512,256]{1,0:T(8,128)(2,1)S(1)}, u32[]{:S(2)}, u32[]{:S(2)}) %collective-permute-start.7) | collective-permute-done | bytes 262176 | tf_op jit(solution)/shard_map/ppermute | solution.py:45
  75.1 1.2 collective-permute-done.8.refs_1_
  76.3 3.4 %collective-permute-done.6.refs_4_ = bf16[512,256]{1,0:T(8,128)(2,1)S(1)} collective-permute-done((bf16[512,256]{1,0:T(8,128)(2,1)S(1)}, bf16[512,256]{1,0:T(8,128)(2,1)S(1)}, u32[]{:S(2)}, u32[]{:S(2)}) %collective-permute-start.6) | collective-permute-done | bytes 262176 | tf_op jit(solution)/shard_map/ppermute | solution.py:233
  79.7 0.0 collective-permute-done.5.refs_3_
  79.7 3.2 %project.2 = (bf16[2,4,32,1280]{3,2,1,0:T(8,128)(2,1)S(1)}, bf16[2,4,32,1280]{3,2,1,0:T(8,128)(2,1)S(1)}) custom-call(s32[5]{0:T(128)S(1)} %copy-done.3, bf16[512,256]{1,0:T(8,128)(2,1)S(1)} %bitcast.15, bf16[512,256]{1,0:T(8,128)(2,1)S(1)} %collective-permute-done.4.refs_1_, bf16[512,256]{1,0:T(8,128)(2,1)S(1)} %collective-permute-done.3.refs_2_, ...), custom_call_target="tpu_custom_call" | custom-call | flops 1 | tf_op jit(solution)/shard_map/project/pallas_call | solution.py:172
  82.8 0.1 collective-permute-start.9
  82.9 0.7 collective-permute-start.10
  83.6 1.3 %collective-permute-start.11 = (bf16[512,256]{1,0:T(8,128)(2,1)S(1)}, bf16[512,256]{1,0:T(8,128)(2,1)S(1)}, u32[]{:S(2)}, u32[]{:S(2)}) collective-permute-start(bf16[512,256]{1,0:T(8,128)(2,1)S(1)} %collective-permute-done.7.refs_2_), channel_id=1, source_target_pairs={{4,0},{8,12},{5,1},{9,13},{6,2},{10,14},{7,3},{11,15},{20,16},{24,... | collective-permute-start | bytes 786440 | tf_op jit(solution)/shard_map/ppermute | solution.py:233
  84.9 0.1 collective-permute-done.9.refs_1_
  85.0 0.7 add_sub.2
  85.7 8.5 %collective-permute-done.11.refs_4_ = bf16[512,256]{1,0:T(8,128)(2,1)S(1)} collective-permute-done((bf16[512,256]{1,0:T(8,128)(2,1)S(1)}, bf16[512,256]{1,0:T(8,128)(2,1)S(1)}, u32[]{:S(2)}, u32[]{:S(2)}) %collective-permute-start.11) | collective-permute-done | bytes 262176 | tf_op jit(solution)/shard_map/ppermute | solution.py:233
  94.2 3.2 %project.3 = (bf16[2,4,32,1280]{3,2,1,0:T(8,128)(2,1)S(1)}, bf16[2,4,32,1280]{3,2,1,0:T(8,128)(2,1)S(1)}) custom-call(s32[5]{0:T(128)S(1)} %copy-done.3, bf16[512,256]{1,0:T(8,128)(2,1)S(1)} %bitcast.11, bf16[512,256]{1,0:T(8,128)(2,1)S(1)} %collective-permute-done.8.refs_1_, bf16[512,256]{1,0:T(8,128)(2,1)S(1)} %collective-permute-done.7.refs_2_, ...), custom_call_target="tpu_custom_call" | custom-call | flops 1 | tf_op jit(solution)/shard_map/project/pallas_call | solution.py:172
  97.4 0.1 collective-permute-start.16
  97.5 1.5 %collective-permute-start.12 = (bf16[4,32,1280]{2,1,0:T(8,128)(2,1)S(1)}, bf16[4,32,1280]{2,1,0:T(8,128)(2,1)S(1)}, u32[]{:S(2)}, u32[]{:S(2)}) collective-permute-start(bf16[4,32,1280]{2,1,0:T(8,128)(2,1)S(1)} %get-tuple-element.61), channel_id=1, source_target_pairs={{0,2},{2,0},{1,3},{3,1},{4,6},{6,4},{5,7},{7,5},{8,10},{10,8},{9,1... | collective-permute-start | bytes 983048 | tf_op jit(solution)/shard_map/ppermute | solution.py:45
  99.0 0.5 collective-permute-done.16.refs_1_
  99.6 0.7 add_sub.3
  100.2 1.5 %collective-permute-start.17 = (bf16[4,32,1280]{2,1,0:T(8,128)(2,1)S(1)}, bf16[4,32,1280]{2,1,0:T(8,128)(2,1)S(1)}, u32[]{:S(2)}, u32[]{:S(2)}) collective-permute-start(bf16[4,32,1280]{2,1,0:T(8,128)(2,1)S(1)} %get-tuple-element.74), channel_id=1, source_target_pairs={{0,2},{2,0},{1,3},{3,1},{4,6},{6,4},{5,7},{7,5},{8,10},{10,8},{9,1... | collective-permute-start | bytes 983048 | tf_op jit(solution)/shard_map/ppermute | solution.py:45
  101.8 6.3 %collective-permute-done.12.refs_0_ = bf16[4,32,1280]{2,1,0:T(8,128)(2,1)S(1)} collective-permute-done((bf16[4,32,1280]{2,1,0:T(8,128)(2,1)S(1)}, bf16[4,32,1280]{2,1,0:T(8,128)(2,1)S(1)}, u32[]{:S(2)}, u32[]{:S(2)}) %collective-permute-start.12) | collective-permute-done | bytes 327712 | tf_op jit(solution)/shard_map/ppermute | solution.py:45
  108.0 0.6 add_head.2
  108.7 0.1 collective-permute-start.13
  108.7 2.4 %collective-permute-start.14 = (bf16[32,1280]{1,0:T(8,128)(2,1)S(1)}, bf16[32,1280]{1,0:T(8,128)(2,1)S(1)}, u32[]{:S(2)}, u32[]{:S(2)}) collective-permute-start(bf16[32,1280]{1,0:T(8,128)(2,1)S(1)} %get-tuple-element.64), channel_id=1, source_target_pairs={{0,8},{4,12},{8,0},{12,4},{1,9},{5,13},{9,1},{13,5},{2,10},{6,14},... | collective-permute-start | bytes 245768 | tf_op jit(solution)/shard_map/ppermute | solution.py:45
  111.2 2.0 %collective-permute-start.15 = (bf16[32,1280]{1,0:T(8,128)(2,1)S(1)}, bf16[32,1280]{1,0:T(8,128)(2,1)S(1)}, u32[]{:S(2)}, u32[]{:S(2)}) collective-permute-start(bf16[32,1280]{1,0:T(8,128)(2,1)S(1)} %get-tuple-element.65), channel_id=1, source_target_pairs={{0,12},{4,8},{8,4},{12,0},{1,13},{5,9},{9,5},{13,1},{2,14},{6,10},... | collective-permute-start | bytes 245768 | tf_op jit(solution)/shard_map/ppermute | solution.py:45
  113.1 1.5 %collective-permute-done.17.refs_0_ = bf16[4,32,1280]{2,1,0:T(8,128)(2,1)S(1)} collective-permute-done((bf16[4,32,1280]{2,1,0:T(8,128)(2,1)S(1)}, bf16[4,32,1280]{2,1,0:T(8,128)(2,1)S(1)}, u32[]{:S(2)}, u32[]{:S(2)}) %collective-permute-start.17) | collective-permute-done | bytes 327712 | tf_op jit(solution)/shard_map/ppermute | solution.py:45
  114.6 0.6 add_head.3
  115.2 0.1 collective-permute-start.18
  115.3 2.4 %collective-permute-start.19 = (bf16[32,1280]{1,0:T(8,128)(2,1)S(1)}, bf16[32,1280]{1,0:T(8,128)(2,1)S(1)}, u32[]{:S(2)}, u32[]{:S(2)}) collective-permute-start(bf16[32,1280]{1,0:T(8,128)(2,1)S(1)} %get-tuple-element.77), channel_id=1, source_target_pairs={{0,8},{4,12},{8,0},{12,4},{1,9},{5,13},{9,1},{13,5},{2,10},{6,14},... | collective-permute-start | bytes 245768 | tf_op jit(solution)/shard_map/ppermute | solution.py:45
  117.7 2.0 %collective-permute-start.20 = (bf16[32,1280]{1,0:T(8,128)(2,1)S(1)}, bf16[32,1280]{1,0:T(8,128)(2,1)S(1)}, u32[]{:S(2)}, u32[]{:S(2)}) collective-permute-start(bf16[32,1280]{1,0:T(8,128)(2,1)S(1)} %get-tuple-element.78), channel_id=1, source_target_pairs={{0,12},{4,8},{8,4},{12,0},{1,13},{5,9},{9,5},{13,1},{2,14},{6,10},... | collective-permute-start | bytes 245768 | tf_op jit(solution)/shard_map/ppermute | solution.py:45
  119.7 0.6 collective-permute-done.18.refs_5_
  120.3 4.4 %collective-permute-done.19.refs_6_ = bf16[32,1280]{1,0:T(8,128)(2,1)S(1)} collective-permute-done((bf16[32,1280]{1,0:T(8,128)(2,1)S(1)}, bf16[32,1280]{1,0:T(8,128)(2,1)S(1)}, u32[]{:S(2)}, u32[]{:S(2)}) %collective-permute-start.19) | collective-permute-done | bytes 81952 | tf_op jit(solution)/shard_map/ppermute | solution.py:45
  124.7 1.6 %mix.1 = bf16[64,5120]{1,0:T(8,128)(2,1)} custom-call(s32[5]{0:T(128)S(1)} %copy-done.3, bf16[64,5120]{1,0:T(8,128)(2,1)S(1)} %copy-done.2, f32[1,5120]{1,0:T(1,128)S(1)} %bitcast.16, bf16[32,1280]{1,0:T(8,128)(2,1)S(1)} %get-tuple-element.62.refs_0_, bf16[32,1280]{1,0:T(8,128)(2,1)S(1)} %collective-permute-done.13.refs_1_, ...), custom_call_target="tpu_custom_call" | custom-call | flops 1 | tf_op jit(solution)/shard_map/mix/pallas_call | solution.py:211
  (20 shorter events, 0.0 us)
Async XLA Ops:
  3.7 6.4 %copy-start.6 = (bf16[3,256,256]{2,1,0:T(8,128)(2,1)S(1)}, bf16[3,256,256]{2,1,0:T(8,128)(2,1)}, u32[]{:S(2)}) copy-start(bf16[3,256,256]{2,1,0:T(8,128)(2,1)} %get-tuple-element.47) | copy-start | bytes 1179652
  3.7 9.0 %copy-start.5 = (bf16[3,256,256]{2,1,0:T(8,128)(2,1)S(1)}, bf16[3,256,256]{2,1,0:T(8,128)(2,1)}, u32[]{:S(2)}) copy-start(bf16[3,256,256]{2,1,0:T(8,128)(2,1)} %get-tuple-element.48) | copy-start | bytes 1179652
  3.7 36.2 %copy-start.3 = (s32[5]{0:T(128)S(1)}, s32[5]{0:T(128)}, u32[]{:S(2)}) copy-start(s32[5]{0:T(128)} %stack.27.where_ref) | copy-start | bytes 64
  3.7 76.0 %copy-start = (bf16[1024,1280]{1,0:T(8,128)(2,1)S(1)}, bf16[1024,1280]{1,0:T(8,128)(2,1)}, u32[]{:S(2)}) copy-start(bf16[1024,1280]{1,0:T(8,128)(2,1)} %refs_5_.3) | copy-start | bytes 7864324
  7.0 20.1 %collective-permute-start = (bf16[3,256,256]{2,1,0:T(8,128)(2,1)}, bf16[3,256,256]{2,1,0:T(8,128)(2,1)S(1)}, u32[]{:S(2)}, u32[]{:S(2)}) collective-permute-start(bf16[3,256,256]{2,1,0:T(8,128)(2,1)} %get-tuple-element.46), channel_id=1, source_target_pairs={{0,4},{4,0},{8,12},{12,8},{1,5},{5,1},{9,13},{13,9},{2,6},{6,2},{1... | collective-permute-start | bytes 1179656 | tf_op jit(solution)/shard_map/ppermute | solution.py:45
  10.0 29.8 %collective-permute-start.1 = (bf16[3,256,256]{2,1,0:T(8,128)(2,1)S(1)}, bf16[3,256,256]{2,1,0:T(8,128)(2,1)S(1)}, u32[]{:S(2)}, u32[]{:S(2)}) collective-permute-start(bf16[3,256,256]{2,1,0:T(8,128)(2,1)S(1)} %copy-done.6), channel_id=1, source_target_pairs={{0,8},{4,12},{8,0},{12,4},{1,9},{5,13},{9,1},{13,5},{2,10},{6,14},... | collective-permute-start | bytes 1179656 | tf_op jit(solution)/shard_map/ppermute | solution.py:45
  12.6 27.2 %collective-permute-start.2 = (bf16[3,256,256]{2,1,0:T(8,128)(2,1)S(1)}, bf16[3,256,256]{2,1,0:T(8,128)(2,1)S(1)}, u32[]{:S(2)}, u32[]{:S(2)}) collective-permute-start(bf16[3,256,256]{2,1,0:T(8,128)(2,1)S(1)} %copy-done.5), channel_id=1, source_target_pairs={{0,12},{4,8},{8,4},{12,0},{1,13},{5,9},{9,5},{13,1},{2,14},{6,10},... | collective-permute-start | bytes 1179656 | tf_op jit(solution)/shard_map/ppermute | solution.py:45
  39.8 1.0 copy-start.1
  43.1 24.1 %collective-permute-start.3 = (bf16[512,256]{1,0:T(8,128)(2,1)S(1)}, bf16[512,256]{1,0:T(8,128)(2,1)S(1)}, u32[]{:S(2)}, u32[]{:S(2)}) collective-permute-start(bf16[512,256]{1,0:T(8,128)(2,1)S(1)} %bitcast.12), channel_id=1, source_target_pairs={{0,8},{4,12},{8,0},{12,4},{1,9},{5,13},{9,1},{13,5},{2,10},{6,14},... | collective-permute-start | bytes 786440 | tf_op jit(solution)/shard_map/ppermute | solution.py:45
  51.7 15.5 %collective-permute-start.4 = (bf16[512,256]{1,0:T(8,128)(2,1)S(1)}, bf16[512,256]{1,0:T(8,128)(2,1)S(1)}, u32[]{:S(2)}, u32[]{:S(2)}) collective-permute-start(bf16[512,256]{1,0:T(8,128)(2,1)S(1)} %bitcast.13), channel_id=1, source_target_pairs={{0,4},{4,0},{8,12},{12,8},{1,5},{5,1},{9,13},{13,9},{2,6},{6,2},{1... | collective-permute-start | bytes 786440 | tf_op jit(solution)/shard_map/ppermute | solution.py:45
  54.0 21.1 %collective-permute-start.7 = (bf16[512,256]{1,0:T(8,128)(2,1)S(1)}, bf16[512,256]{1,0:T(8,128)(2,1)S(1)}, u32[]{:S(2)}, u32[]{:S(2)}) collective-permute-start(bf16[512,256]{1,0:T(8,128)(2,1)S(1)} %bitcast.8), channel_id=1, source_target_pairs={{0,8},{4,12},{8,0},{12,4},{1,9},{5,13},{9,1},{13,5},{2,10},{6,14},... | collective-permute-start | bytes 786440 | tf_op jit(solution)/shard_map/ppermute | solution.py:45
  56.0 20.3 %collective-permute-start.8 = (bf16[512,256]{1,0:T(8,128)(2,1)S(1)}, bf16[512,256]{1,0:T(8,128)(2,1)S(1)}, u32[]{:S(2)}, u32[]{:S(2)}) collective-permute-start(bf16[512,256]{1,0:T(8,128)(2,1)S(1)} %bitcast.9), channel_id=1, source_target_pairs={{0,4},{4,0},{8,12},{12,8},{1,5},{5,1},{9,13},{13,9},{2,6},{6,2},{1... | collective-permute-start | bytes 786440 | tf_op jit(solution)/shard_map/ppermute | solution.py:45
  67.2 12.4 %collective-permute-start.6 = (bf16[512,256]{1,0:T(8,128)(2,1)S(1)}, bf16[512,256]{1,0:T(8,128)(2,1)S(1)}, u32[]{:S(2)}, u32[]{:S(2)}) collective-permute-start(bf16[512,256]{1,0:T(8,128)(2,1)S(1)} %collective-permute-done.3.refs_2_), channel_id=1, source_target_pairs={{4,0},{8,12},{5,1},{9,13},{6,2},{10,14},{7,3},{11,15},{20,16},{24,... | collective-permute-start | bytes 786440 | tf_op jit(solution)/shard_map/ppermute | solution.py:233
  68.5 11.2 %collective-permute-start.5 = (bf16[512,256]{1,0:T(8,128)(2,1)S(1)}, bf16[512,256]{1,0:T(8,128)(2,1)S(1)}, u32[]{:S(2)}, u32[]{:S(2)}) collective-permute-start(bf16[512,256]{1,0:T(8,128)(2,1)S(1)} %bitcast.14), channel_id=1, source_target_pairs={{4,8},{8,4},{5,9},{9,5},{6,10},{10,6},{7,11},{11,7},{20,24},{24,20... | collective-permute-start | bytes 786440 | tf_op jit(solution)/shard_map/ppermute | solution.py:45
  82.8 2.2 %collective-permute-start.9 = (bf16[2,4,32,1280]{3,2,1,0:T(8,128)(2,1)S(1)}, bf16[2,4,32,1280]{3,2,1,0:T(8,128)(2,1)S(1)}, u32[]{:S(2)}, u32[]{:S(2)}) collective-permute-start(bf16[2,4,32,1280]{3,2,1,0:T(8,128)(2,1)S(1)} %get-tuple-element.53), channel_id=1, source_target_pairs={{0,1},{1,0},{2,3},{3,2},{4,5},{5,4},{6,7},{7,6},{8,9},{9,8},{10,11... | collective-permute-start | bytes 1966088 | tf_op jit(solution)/shard_map/ppermute | solution.py:45
  82.9 2.8 %collective-permute-start.10 = (bf16[512,256]{1,0:T(8,128)(2,1)S(1)}, bf16[512,256]{1,0:T(8,128)(2,1)S(1)}, u32[]{:S(2)}, u32[]{:S(2)}) collective-permute-start(bf16[512,256]{1,0:T(8,128)(2,1)S(1)} %bitcast.10), channel_id=1, source_target_pairs={{4,8},{8,4},{5,9},{9,5},{6,10},{10,6},{7,11},{11,7},{20,24},{24,20... | collective-permute-start | bytes 786440 | tf_op jit(solution)/shard_map/ppermute | solution.py:45
  83.6 10.6 %collective-permute-start.11 = (bf16[512,256]{1,0:T(8,128)(2,1)S(1)}, bf16[512,256]{1,0:T(8,128)(2,1)S(1)}, u32[]{:S(2)}, u32[]{:S(2)}) collective-permute-start(bf16[512,256]{1,0:T(8,128)(2,1)S(1)} %collective-permute-done.7.refs_2_), channel_id=1, source_target_pairs={{4,0},{8,12},{5,1},{9,13},{6,2},{10,14},{7,3},{11,15},{20,16},{24,... | collective-permute-start | bytes 786440 | tf_op jit(solution)/shard_map/ppermute | solution.py:233
  85.0 39.7 %copy-start.2 = (bf16[64,5120]{1,0:T(8,128)(2,1)S(1)}, bf16[64,5120]{1,0:T(8,128)(2,1)}, u32[]{:S(2)}) copy-start(bf16[64,5120]{1,0:T(8,128)(2,1)} %hidden_ref.1) | copy-start | bytes 1966084
  85.0 39.7 %copy-start.4 = (f32[5120]{0:T(1024)S(1)}, f32[5120]{0:T(1024)}, u32[]{:S(2)}) copy-start(f32[5120]{0:T(1024)} %param.13) | copy-start | bytes 61444
  97.4 2.2 %collective-permute-start.16 = (bf16[2,4,32,1280]{3,2,1,0:T(8,128)(2,1)S(1)}, bf16[2,4,32,1280]{3,2,1,0:T(8,128)(2,1)S(1)}, u32[]{:S(2)}, u32[]{:S(2)}) collective-permute-start(bf16[2,4,32,1280]{3,2,1,0:T(8,128)(2,1)S(1)} %get-tuple-element.72), channel_id=1, source_target_pairs={{0,1},{1,0},{2,3},{3,2},{4,5},{5,4},{6,7},{7,6},{8,9},{9,8},{10,11... | collective-permute-start | bytes 1966088 | tf_op jit(solution)/shard_map/ppermute | solution.py:45
  97.5 10.6 %collective-permute-start.12 = (bf16[4,32,1280]{2,1,0:T(8,128)(2,1)S(1)}, bf16[4,32,1280]{2,1,0:T(8,128)(2,1)S(1)}, u32[]{:S(2)}, u32[]{:S(2)}) collective-permute-start(bf16[4,32,1280]{2,1,0:T(8,128)(2,1)S(1)} %get-tuple-element.61), channel_id=1, source_target_pairs={{0,2},{2,0},{1,3},{3,1},{4,6},{6,4},{5,7},{7,5},{8,10},{10,8},{9,1... | collective-permute-start | bytes 983048 | tf_op jit(solution)/shard_map/ppermute | solution.py:45
  100.2 14.4 %collective-permute-start.17 = (bf16[4,32,1280]{2,1,0:T(8,128)(2,1)S(1)}, bf16[4,32,1280]{2,1,0:T(8,128)(2,1)S(1)}, u32[]{:S(2)}, u32[]{:S(2)}) collective-permute-start(bf16[4,32,1280]{2,1,0:T(8,128)(2,1)S(1)} %get-tuple-element.74), channel_id=1, source_target_pairs={{0,2},{2,0},{1,3},{3,1},{4,6},{6,4},{5,7},{7,5},{8,10},{10,8},{9,1... | collective-permute-start | bytes 983048 | tf_op jit(solution)/shard_map/ppermute | solution.py:45
  108.7 9.1 %collective-permute-start.13 = (bf16[32,1280]{1,0:T(8,128)(2,1)S(1)}, bf16[32,1280]{1,0:T(8,128)(2,1)S(1)}, u32[]{:S(2)}, u32[]{:S(2)}) collective-permute-start(bf16[32,1280]{1,0:T(8,128)(2,1)S(1)} %get-tuple-element.63), channel_id=1, source_target_pairs={{0,4},{4,0},{8,12},{12,8},{1,5},{5,1},{9,13},{13,9},{2,6},{6,2},{1... | collective-permute-start | bytes 245768 | tf_op jit(solution)/shard_map/ppermute | solution.py:45
  108.7 11.0 %collective-permute-start.14 = (bf16[32,1280]{1,0:T(8,128)(2,1)S(1)}, bf16[32,1280]{1,0:T(8,128)(2,1)S(1)}, u32[]{:S(2)}, u32[]{:S(2)}) collective-permute-start(bf16[32,1280]{1,0:T(8,128)(2,1)S(1)} %get-tuple-element.64), channel_id=1, source_target_pairs={{0,8},{4,12},{8,0},{12,4},{1,9},{5,13},{9,1},{13,5},{2,10},{6,14},... | collective-permute-start | bytes 245768 | tf_op jit(solution)/shard_map/ppermute | solution.py:45
  111.2 8.5 %collective-permute-start.15 = (bf16[32,1280]{1,0:T(8,128)(2,1)S(1)}, bf16[32,1280]{1,0:T(8,128)(2,1)S(1)}, u32[]{:S(2)}, u32[]{:S(2)}) collective-permute-start(bf16[32,1280]{1,0:T(8,128)(2,1)S(1)} %get-tuple-element.65), channel_id=1, source_target_pairs={{0,12},{4,8},{8,4},{12,0},{1,13},{5,9},{9,5},{13,1},{2,14},{6,10},... | collective-permute-start | bytes 245768 | tf_op jit(solution)/shard_map/ppermute | solution.py:45
  115.2 5.1 %collective-permute-start.18 = (bf16[32,1280]{1,0:T(8,128)(2,1)S(1)}, bf16[32,1280]{1,0:T(8,128)(2,1)S(1)}, u32[]{:S(2)}, u32[]{:S(2)}) collective-permute-start(bf16[32,1280]{1,0:T(8,128)(2,1)S(1)} %get-tuple-element.76), channel_id=1, source_target_pairs={{0,4},{4,0},{8,12},{12,8},{1,5},{5,1},{9,13},{13,9},{2,6},{6,2},{1... | collective-permute-start | bytes 245768 | tf_op jit(solution)/shard_map/ppermute | solution.py:45
  115.3 9.4 %collective-permute-start.19 = (bf16[32,1280]{1,0:T(8,128)(2,1)S(1)}, bf16[32,1280]{1,0:T(8,128)(2,1)S(1)}, u32[]{:S(2)}, u32[]{:S(2)}) collective-permute-start(bf16[32,1280]{1,0:T(8,128)(2,1)S(1)} %get-tuple-element.77), channel_id=1, source_target_pairs={{0,8},{4,12},{8,0},{12,4},{1,9},{5,13},{9,1},{13,5},{2,10},{6,14},... | collective-permute-start | bytes 245768 | tf_op jit(solution)/shard_map/ppermute | solution.py:45
  117.7 6.9 %collective-permute-start.20 = (bf16[32,1280]{1,0:T(8,128)(2,1)S(1)}, bf16[32,1280]{1,0:T(8,128)(2,1)S(1)}, u32[]{:S(2)}, u32[]{:S(2)}) collective-permute-start(bf16[32,1280]{1,0:T(8,128)(2,1)S(1)} %get-tuple-element.78), channel_id=1, source_target_pairs={{0,12},{4,8},{8,4},{12,0},{1,13},{5,9},{9,5},{13,1},{2,14},{6,10},... | collective-permute-start | bytes 245768 | tf_op jit(solution)/shard_map/ppermute | solution.py:45

commit v7 on v6

--- a/solution.py
+++ b/solution.py
@@ -45,56 +45,108 @@
     return lax.ppermute(x, axes, pairs)
 
 
-def pack_kernel(span, per, upper, where_ref, exps_ref, q_ref, fresh_ref, cached_ref, *outs):
-    rows = q_ref.shape[0]
-    block = pl.program_id(0) * rows // SCALE_ROWS
-    half = (where_ref[NEAR] // span) ^ upper
-    for rel in range(span):
-        for chunk in range(per):
-            head = ((where_ref[NEAR] % span) ^ rel) * per + chunk
-            lanes = pl.ds(pl.multiple_of(head * HEAD_DIM, HEAD_DIM), HEAD_DIM)
-            here = pl.ds(chunk * HEAD_DIM, HEAD_DIM)
-            outs[rel][0, :, here] = q_ref[:, lanes]
+def decode(fresh, cached, exponent):
+    power = jnp.full((1, HEAD_DIM), exponent.astype(jnp.float32))
+    cached = cached.astype(jnp.float32)
+    residual = fresh.astype(jnp.float32) - cached
+    codes = jnp.clip(residual * jnp.exp2(-power), -SATURATION, SATURATION).astype(jnp.bfloat16)
+    return (cached + codes.astype(jnp.float32) * jnp.exp2(power)).astype(jnp.bfloat16)
+
+
+def pack_kernel(split, per, exps_ref, q_ref, fresh_ref, cached_ref, *refs):
+    outs, (q_buf, fresh_buf, cached_buf, sems) = refs[:-4], refs[-4:]
+    patch = lax.axis_index("patch")
+    near = lax.rem(patch, split)
+    tok = q_buf.shape[0]
+    copies = []
+    for block in range(tok // SCALE_ROWS):
+        rows = pl.ds(block * SCALE_ROWS, SCALE_ROWS)
+        there = pl.ds(pl.multiple_of(patch * tok + block * SCALE_ROWS, SCALE_ROWS), SCALE_ROWS)
+        copies.append(
+            [
+                pltpu.make_async_copy(q_ref.at[rows], q_buf.at[rows], sems.at[block, 0]),
+                pltpu.make_async_copy(fresh_ref.at[:, rows], fresh_buf.at[:, rows], sems.at[block, 1]),
+                pltpu.make_async_copy(cached_ref.at[:, there], cached_buf.at[:, rows], sems.at[block, 2]),
+            ]
+        )
+        for copy in copies[-1]:
+            copy.start()
+    for block in range(tok // SCALE_ROWS):
+        rows = pl.ds(block * SCALE_ROWS, SCALE_ROWS)
+        for copy in copies[block]:
+            copy.wait()
+        for rel in range(1, split):
+            out = outs[rel - 1]
+            for chunk in range(per):
+                head = (near ^ rel) * per + chunk
+                lanes = pl.ds(pl.multiple_of(head * HEAD_DIM, HEAD_DIM), HEAD_DIM)
+                here = pl.ds(chunk * HEAD_DIM, HEAD_DIM)
+                out[0, rows, here] = q_buf[rows, lanes]
+                for stacked in range(2):
+                    out[1 + stacked, rows, here] = decode(
+                        fresh_buf[stacked, rows, lanes],
+                        cached_buf[stacked, rows, lanes],
+                        exps_ref[stacked, block, head],
+                    )
+
+
+def pack(split, exponents, queries, fresh_kv, cached_kv):
+    tok, channels = queries.shape
+    feat = channels // split
+    blocks = tok // SCALE_ROWS
+    hbm = pl.BlockSpec(memory_space=pltpu.HBM)
+    return pl.pallas_call(
+        functools.partial(pack_kernel, split, feat // HEAD_DIM),
+        out_shape=[jax.ShapeDtypeStruct((3, tok, feat), jnp.bfloat16)] * (split - 1),
+        in_specs=[pl.BlockSpec(memory_space=pltpu.SMEM), hbm, hbm, hbm],
+        out_specs=[pl.BlockSpec(memory_space=pltpu.VMEM)] * (split - 1),
+        scratch_shapes=[
+            pltpu.VMEM((tok, channels), jnp.bfloat16),
+            pltpu.VMEM((2, tok, channels), jnp.bfloat16),
+            pltpu.VMEM((2, tok, channels), jnp.bfloat16),
+            pltpu.SemaphoreType.DMA((blocks, 3)),
+        ],
+        compiler_params=pltpu.CompilerParams(vmem_limit_bytes=PACK_VMEM_BYTES),
+        name="pack",
+    )(exponents, queries, fresh_kv, cached_kv)
+
+
+def own_kernel(per, where_ref, exps_ref, q_ref, fresh_ref, cached_ref, out_ref):
+    out_ref[0] = q_ref[...]
+    for chunk in range(per):
+        lanes = pl.ds(chunk * HEAD_DIM, HEAD_DIM)
+        for block in range(q_ref.shape[0] // SCALE_ROWS):
+            rows = pl.ds(block * SCALE_ROWS, SCALE_ROWS)
             for stacked in range(2):
-                exponent = exps_ref[stacked, block, half * span * per + head]
-                power = jnp.full((1, HEAD_DIM), exponent.astype(jnp.float32))
-                cached = cached_ref[stacked, :, lanes].astype(jnp.float32)
-                residual = fresh_ref[stacked, :, lanes].astype(jnp.float32) - cached
-                codes = jnp.clip(
-                    residual * jnp.exp2(-power), -SATURATION, SATURATION
-                ).astype(jnp.bfloat16)
-                decoded = cached + codes.astype(jnp.float32) * jnp.exp2(power)
-                outs[rel][1 + stacked, :, here] = decoded.astype(jnp.bfloat16)
-
-
-def pack(split, per, upper, where, exponents, queries, fresh_kv, cached_kv):
+                out_ref[1 + stacked, rows, lanes] = decode(
+                    fresh_ref[stacked, rows, lanes],
+                    cached_ref[stacked, rows, lanes],
+                    exps_ref[stacked, block, where_ref[NEAR] * per + chunk],
+                )
+
+
+def pack_own(split, where, exponents, queries, fresh_kv, cached_kv):
     tok, channels = queries.shape
-    span = split // 2
-    wide, feat = channels // 2, channels // split
-    rows = SCALE_ROWS
-    steps = tok // rows
-
-    def half(w):
-        return (w[NEAR] // span) ^ upper
-
-    return call(
-        functools.partial(pack_kernel, span, per, upper),
-        "pack",
-        [jax.ShapeDtypeStruct((3, tok, feat), jnp.bfloat16)] * span,
-        steps,
+    feat = channels // split
+    out = jax.ShapeDtypeStruct((3, tok, feat), jnp.bfloat16)
+    return call(
+        functools.partial(own_kernel, feat // HEAD_DIM),
+        "own",
+        out,
+        1,
         [
             pl.BlockSpec(memory_space=pltpu.SMEM),
-            pl.BlockSpec((rows, wide), lambda i, w: (i, half(w))),
-            pl.BlockSpec((2, rows, wide), lambda i, w: (0, i, half(w))),
-            pl.BlockSpec((2, rows, wide), lambda i, w: (0, w[PATCH] * steps + i, half(w))),
+            pl.BlockSpec((tok, feat), lambda i, w: (0, w[NEAR])),
+            pl.BlockSpec((2, tok, feat), lambda i, w: (0, 0, w[NEAR])),
+            pl.BlockSpec((2, tok, feat), lambda i, w: (0, w[PATCH], w[NEAR])),
         ],
-        [pl.BlockSpec((3, rows, feat), lambda i, w: (0, i, 0))] * span,
+        spec(out.shape),
         vmem=PACK_VMEM_BYTES,
     )(where, exponents, queries, fresh_kv, cached_kv)
 
 
-def attend_kernel(split, part, parts, where_ref, *refs):
-    q_refs, kv_refs, out_ref = refs[:split], refs[:-1], refs[-1]
+def attend_kernel(split, part, where_ref, *refs):
+    q_refs, kv_refs, out_ref = (refs[0], *refs[split - 1 : 0 : -1]), refs[:-1], refs[-1]
     factor = HEAD_DIM**-0.5 * math.log2(math.e)
     tok, feat = q_refs[0].shape[1:]
     count = out_ref.shape[1] // part[1]
@@ -122,7 +174,7 @@
     _, tok, feat = pieces[0].shape
     out = jax.ShapeDtypeStruct((split, count * part[1], feat), jnp.bfloat16)
     return call(
-        functools.partial(attend_kernel, split, part, count),
+        functools.partial(attend_kernel, split, part),
         "attend",
         out,
         1,
@@ -226,16 +278,16 @@
         ]
     far = [swap(x, "patch", 4, 2) for x in parts]
     next_to = [swap(x, "patch", 4, 1) for x in parts]
-    middle = [swap(x, "patch", 4, 3, (1, 2)) for x in parts]
     out = []
     for at, x in enumerate(parts):
         far[at], next_to[at], parts = lax.optimization_barrier((far[at], next_to[at], parts))
+        middle = swap(parts[at], "patch", 4, 3, (1, 2))
         ends = lax.ppermute(far[at], "patch", [(1, 0), (2, 3)])
         if at + 1 < len(parts):
             ends, far[at + 1], next_to[at + 1] = lax.optimization_barrier(
                 (ends, far[at + 1], next_to[at + 1])
             )
-        out.append(([x, next_to[at], far[at], middle[at]], [ends]))
+        out.append(([x, next_to[at], far[at], middle], [ends]))
     return out
 
 
@@ -300,10 +352,10 @@
     ).astype(jnp.int32)
 
     arrays = (exponents, queries, fresh_kv, cached_kv)
-    upper = pack(split, heads // split, 1, where, *arrays)
-    upper, where = lax.optimization_barrier((upper, where))
-    sent = [*pack(split, heads // split, 0, where, *arrays), *upper]
-    pieces = [sent[0]] + [swap(sent[rel], "patch", n_patch, rel) for rel in range(1, split)]
+    sent = pack(split, *arrays)
+    far_first = [swap(sent[rel - 1], "patch", n_patch, rel) for rel in range(split - 1, 0, -1)]
+    where, sent = lax.optimization_barrier((where, sent))
+    pieces = [pack_own(split, where, *arrays), *far_first]
     kv_pieces = list(pieces)
     for rel in range(split, n_patch, split):
         kv_pieces += [swap(x, "patch", n_patch, rel) for x in pieces]
@@ -320,10 +372,7 @@
     blocks = []
     for part in range(parts):
         terms = project(split, where, *slots[part], out_weight, n_head, n_sub)
-        sums = reduce_sub(sizes, where, terms)
-        if part + 1 < parts:
-            sums, slots[part + 1] = lax.optimization_barrier((sums, slots[part + 1]))
-        total = reduce_head(sizes, where, sums)
+        total = reduce_head(sizes, where, reduce_sub(sizes, where, terms))
         blocks.append(
             [total[0]] + [swap(total[rel], "patch", n_patch, rel) for rel in range(1, n_patch)]
         )

time: 127 us -> 120 us (0.945)
  starting transfers between devices: 32.5 us -> 26.7 us
    ppermute x19, starting transfers between devices: 29.9 us -> 24.1 us  [swap(): return lax.ppermute(x, axes, pairs)]
    ppermute x2, waiting for transfers between devices: 11.9 us -> 9.6 us  [gather(): ends = lax.ppermute(far[at], 'patch', [(1, 0), (2, 3)])]
  transfers between devices with their start and end apart: 21 -> 21, of which waited for: 13 -> 12; matrix products, arithmetic and copies ran while one was open for 0% -> 1% of each run, Pallas kernels for 4% -> 12%
where the time goes in v7:
time: 120 us; the launch traced here: 119 us
  waiting for transfers between devices  69.4 us (58%)
  starting transfers between devices  26.7 us (22%)
  Pallas kernels  21.3 us (18%)
  local copies, waits for them, and re-layouts  1.68 us (1%)
    ppermute x19, waiting for transfers between devices, swap(): return lax.ppermute(x, axes, pairs)  59.8 us
    ppermute x19, starting transfers between devices, swap(): return lax.ppermute(x, axes, pairs)  24.1 us
    ppermute x2, waiting for transfers between devices, gather(): ends = lax.ppermute(far[at], 'patch', [(1, 0), (2, 3)])  9.6 us
    pallas_call x2, Pallas kernels, project(): call(functools.partial(project_kernel, split, n_patch, len(more)), 'proje...  6.37 us
    pallas_call x2, Pallas kernels, attend(): call(functools.partial(attend_kernel, split, part), 'attend', out, 1, [sp...  4.34 us
    pallas_call x1, Pallas kernels, pack(): pl.pallas_call(functools.partial(pack_kernel, split, feat // HEAD_DIM), o...  3.6 us
    pallas_call x1, Pallas kernels, pack_own(): call(functools.partial(own_kernel, feat // HEAD_DIM), 'own', out, 1, [pl....  2.84 us
    ppermute x2, starting transfers between devices, gather(): ends = lax.ppermute(far[at], 'patch', [(1, 0), (2, 3)])  2.57 us
  transfers between devices with their start and end apart: 21, of which 12 were waited for; matrix products, arithmetic and copies ran while one was open for 1% of the time, Pallas kernels for 12%

profile of v7, /device:TPU:0, one launch (start us, length us, event | category | flops | bytes accessed | tf_op | source)
XLA Modules:
  0.0 119.3 jit_solution(6146377616517249635)
XLA Ops:
  0.0 3.6 %pack.1 = (bf16[3,256,256]{2,1,0:T(8,128)(2,1)}, bf16[3,256,256]{2,1,0:T(8,128)(2,1)}, bf16[3,256,256]{2,1,0:T(8,128)(2,1)}) custom-call(s32[2,2,8]{2,1,0:T(2,128)} %exps_ref.3, bf16[256,1024]{1,0:T(8,128)(2,1)} %q_ref.3, bf16[2,256,1024]{2,1,0:T(8,128)(2,1)} %fresh_ref.3, bf16[2,1024,1024]{2,1,0:T(8,128)(2,1)} %cached_ref.3), custom_call_target="tpu_custom_call" | custom-call | tf_op jit(solution)/shard_map/pack/pallas_call | solution.py:98
  3.6 5.1 %collective-permute-start = (bf16[3,256,256]{2,1,0:T(8,128)(2,1)}, bf16[3,256,256]{2,1,0:T(8,128)(2,1)S(1)}, u32[]{:S(2)}, u32[]{:S(2)}) collective-permute-start(bf16[3,256,256]{2,1,0:T(8,128)(2,1)} %get-tuple-element.37), channel_id=1, source_target_pairs={{0,12},{4,8},{8,4},{12,0},{1,13},{5,9},{9,5},{13,1},{2,14},{6,10},... | collective-permute-start | bytes 1179656 | tf_op jit(solution)/shard_map/ppermute | solution.py:45
  8.7 0.0 collective-permute-start.1
  8.7 0.6 collective-permute-start.2
  9.4 0.7 stack.27.where_ref
  10.0 2.8 %own.1.refs_0_ = bf16[3,256,256]{2,1,0:T(8,128)(2,1)} custom-call(s32[5]{0:T(128)} %stack.27.where_ref, s32[2,2,8]{2,1,0:T(2,128)} %exps_ref.3, bf16[256,1024]{1,0:T(8,128)(2,1)} %q_ref.3, bf16[2,256,1024]{2,1,0:T(8,128)(2,1)} %fresh_ref.3, bf16[2,1024,1024]{2,1,0:T(8,128)(2,1)} %cached_ref.3), custom_call_target="tpu_custom_call" | custom-call | flops 1 | tf_op jit(solution)/shard_map/own/pallas_call | solution.py:132
  12.9 6.1 %collective-permute-done.refs_1_ = bf16[3,256,256]{2,1,0:T(8,128)(2,1)S(1)} collective-permute-done((bf16[3,256,256]{2,1,0:T(8,128)(2,1)}, bf16[3,256,256]{2,1,0:T(8,128)(2,1)S(1)}, u32[]{:S(2)}, u32[]{:S(2)}) %collective-permute-start) | collective-permute-done | bytes 393248 | tf_op jit(solution)/shard_map/ppermute | solution.py:45
  19.0 23.5 %collective-permute-done.1.refs_2_ = bf16[3,256,256]{2,1,0:T(8,128)(2,1)S(1)} collective-permute-done((bf16[3,256,256]{2,1,0:T(8,128)(2,1)}, bf16[3,256,256]{2,1,0:T(8,128)(2,1)S(1)}, u32[]{:S(2)}, u32[]{:S(2)}) %collective-permute-start.1) | collective-permute-done | bytes 393248 | tf_op jit(solution)/shard_map/ppermute | solution.py:45
  42.5 1.0 copy-done.1
  43.5 2.2 %attend.2 = bf16[4,128,256]{2,1,0:T(8,128)(2,1)S(1)} custom-call(s32[5]{0:T(128)S(1)} %copy-done.3, bf16[3,256,256]{2,1,0:T(8,128)(2,1)S(1)} %copy-done.1, bf16[3,256,256]{2,1,0:T(8,128)(2,1)S(1)} %collective-permute-done.refs_1_, bf16[3,256,256]{2,1,0:T(8,128)(2,1)S(1)} %collective-permute-done.1.refs_2_, ...), custom_call_target="tpu_custom_call" | custom-call | flops 1 | tf_op jit(solution)/shard_map/attend/pallas_call | solution.py:176
  45.7 0.1 collective-permute-start.3
  45.7 3.0 %collective-permute-start.4 = (bf16[512,256]{1,0:T(8,128)(2,1)S(1)}, bf16[512,256]{1,0:T(8,128)(2,1)S(1)}, u32[]{:S(2)}, u32[]{:S(2)}) collective-permute-start(bf16[512,256]{1,0:T(8,128)(2,1)S(1)} %bitcast.13), channel_id=1, source_target_pairs={{0,4},{4,0},{8,12},{12,8},{1,5},{5,1},{9,13},{13,9},{2,6},{6,2},{1... | collective-permute-start | bytes 786440 | tf_op jit(solution)/shard_map/ppermute | solution.py:45
  48.8 2.2 %attend.3 = bf16[4,128,256]{2,1,0:T(8,128)(2,1)S(1)} custom-call(s32[5]{0:T(128)S(1)} %copy-done.3, bf16[3,256,256]{2,1,0:T(8,128)(2,1)S(1)} %copy-done.1, bf16[3,256,256]{2,1,0:T(8,128)(2,1)S(1)} %collective-permute-done.refs_1_, bf16[3,256,256]{2,1,0:T(8,128)(2,1)S(1)} %collective-permute-done.1.refs_2_, ...), custom_call_target="tpu_custom_call" | custom-call | flops 1 | tf_op jit(solution)/shard_map/attend/pallas_call | solution.py:176
  50.9 0.1 collective-permute-start.7
  51.1 1.8 %collective-permute-start.8 = (bf16[512,256]{1,0:T(8,128)(2,1)S(1)}, bf16[512,256]{1,0:T(8,128)(2,1)S(1)}, u32[]{:S(2)}, u32[]{:S(2)}) collective-permute-start(bf16[512,256]{1,0:T(8,128)(2,1)S(1)} %bitcast.9), channel_id=1, source_target_pairs={{0,4},{4,0},{8,12},{12,8},{1,5},{5,1},{9,13},{13,9},{2,6},{6,2},{1... | collective-permute-start | bytes 786440 | tf_op jit(solution)/shard_map/ppermute | solution.py:45
  52.9 8.3 %collective-permute-done.3.refs_2_ = bf16[512,256]{1,0:T(8,128)(2,1)S(1)} collective-permute-done((bf16[512,256]{1,0:T(8,128)(2,1)S(1)}, bf16[512,256]{1,0:T(8,128)(2,1)S(1)}, u32[]{:S(2)}, u32[]{:S(2)}) %collective-permute-start.3) | collective-permute-done | bytes 262176 | tf_op jit(solution)/shard_map/ppermute | solution.py:45
  61.2 0.3 collective-permute-done.4.refs_1_
  61.5 1.3 %collective-permute-start.6 = (bf16[512,256]{1,0:T(8,128)(2,1)S(1)}, bf16[512,256]{1,0:T(8,128)(2,1)S(1)}, u32[]{:S(2)}, u32[]{:S(2)}) collective-permute-start(bf16[512,256]{1,0:T(8,128)(2,1)S(1)} %collective-permute-done.3.refs_2_), channel_id=1, source_target_pairs={{4,0},{8,12},{5,1},{9,13},{6,2},{10,14},{7,3},{11,15},{20,16},{24,... | collective-permute-start | bytes 786440 | tf_op jit(solution)/shard_map/ppermute | solution.py:285
  62.8 0.7 collective-permute-start.5
  63.5 7.2 %collective-permute-done.7.refs_2_ = bf16[512,256]{1,0:T(8,128)(2,1)S(1)} collective-permute-done((bf16[512,256]{1,0:T(8,128)(2,1)S(1)}, bf16[512,256]{1,0:T(8,128)(2,1)S(1)}, u32[]{:S(2)}, u32[]{:S(2)}) %collective-permute-start.7) | collective-permute-done | bytes 262176 | tf_op jit(solution)/shard_map/ppermute | solution.py:45
  70.7 0.9 collective-permute-done.8.refs_1_
  71.6 4.8 %collective-permute-done.6.refs_4_ = bf16[512,256]{1,0:T(8,128)(2,1)S(1)} collective-permute-done((bf16[512,256]{1,0:T(8,128)(2,1)S(1)}, bf16[512,256]{1,0:T(8,128)(2,1)S(1)}, u32[]{:S(2)}, u32[]{:S(2)}) %collective-permute-start.6) | collective-permute-done | bytes 262176 | tf_op jit(solution)/shard_map/ppermute | solution.py:285
  76.4 0.7 collective-permute-start.14
  77.1 1.3 %collective-permute-start.15 = (bf16[512,256]{1,0:T(8,128)(2,1)S(1)}, bf16[512,256]{1,0:T(8,128)(2,1)S(1)}, u32[]{:S(2)}, u32[]{:S(2)}) collective-permute-start(bf16[512,256]{1,0:T(8,128)(2,1)S(1)} %collective-permute-done.7.refs_2_), channel_id=1, source_target_pairs={{4,0},{8,12},{5,1},{9,13},{6,2},{10,14},{7,3},{11,15},{20,16},{24,... | collective-permute-start | bytes 786440 | tf_op jit(solution)/shard_map/ppermute | solution.py:285
  78.4 3.2 %project.2 = (bf16[2,4,32,1280]{3,2,1,0:T(8,128)(2,1)S(1)}, bf16[2,4,32,1280]{3,2,1,0:T(8,128)(2,1)S(1)}) custom-call(s32[5]{0:T(128)S(1)} %copy-done.3, bf16[512,256]{1,0:T(8,128)(2,1)S(1)} %bitcast.15, bf16[512,256]{1,0:T(8,128)(2,1)S(1)} %collective-permute-done.4.refs_1_, bf16[512,256]{1,0:T(8,128)(2,1)S(1)} %collective-permute-done.3.refs_2_, ...), custom_call_target="tpu_custom_call" | custom-call | flops 1 | tf_op jit(solution)/shard_map/project/pallas_call | solution.py:224
  81.6 0.0 copy-start.2
  81.6 0.0 copy-start.4
  81.6 0.1 collective-permute-start.9
  81.7 4.8 %collective-permute-done.15.refs_4_ = bf16[512,256]{1,0:T(8,128)(2,1)S(1)} collective-permute-done((bf16[512,256]{1,0:T(8,128)(2,1)S(1)}, bf16[512,256]{1,0:T(8,128)(2,1)S(1)}, u32[]{:S(2)}, u32[]{:S(2)}) %collective-permute-start.15) | collective-permute-done | bytes 262176 | tf_op jit(solution)/shard_map/ppermute | solution.py:285
  86.5 3.2 %project.3 = (bf16[2,4,32,1280]{3,2,1,0:T(8,128)(2,1)S(1)}, bf16[2,4,32,1280]{3,2,1,0:T(8,128)(2,1)S(1)}) custom-call(s32[5]{0:T(128)S(1)} %copy-done.3, bf16[512,256]{1,0:T(8,128)(2,1)S(1)} %bitcast.11, bf16[512,256]{1,0:T(8,128)(2,1)S(1)} %collective-permute-done.8.refs_1_, bf16[512,256]{1,0:T(8,128)(2,1)S(1)} %collective-permute-done.7.refs_2_, ...), custom_call_target="tpu_custom_call" | custom-call | flops 1 | tf_op jit(solution)/shard_map/project/pallas_call | solution.py:224
  89.7 0.1 collective-permute-start.16
  89.8 0.7 add_sub.2
  90.4 1.6 %collective-permute-start.10 = (bf16[4,32,1280]{2,1,0:T(8,128)(2,1)S(1)}, bf16[4,32,1280]{2,1,0:T(8,128)(2,1)S(1)}, u32[]{:S(2)}, u32[]{:S(2)}) collective-permute-start(bf16[4,32,1280]{2,1,0:T(8,128)(2,1)S(1)} %get-tuple-element.46), channel_id=1, source_target_pairs={{0,2},{2,0},{1,3},{3,1},{4,6},{6,4},{5,7},{7,5},{8,10},{10,8},{9,1... | collective-permute-start | bytes 983048 | tf_op jit(solution)/shard_map/ppermute | solution.py:45
  92.0 0.7 add_sub.3
  92.7 1.4 %collective-permute-start.17 = (bf16[4,32,1280]{2,1,0:T(8,128)(2,1)S(1)}, bf16[4,32,1280]{2,1,0:T(8,128)(2,1)S(1)}, u32[]{:S(2)}, u32[]{:S(2)}) collective-permute-start(bf16[4,32,1280]{2,1,0:T(8,128)(2,1)S(1)} %get-tuple-element.60), channel_id=1, source_target_pairs={{0,2},{2,0},{1,3},{3,1},{4,6},{6,4},{5,7},{7,5},{8,10},{10,8},{9,1... | collective-permute-start | bytes 983048 | tf_op jit(solution)/shard_map/ppermute | solution.py:45
  94.1 6.9 %collective-permute-done.10.refs_0_ = bf16[4,32,1280]{2,1,0:T(8,128)(2,1)S(1)} collective-permute-done((bf16[4,32,1280]{2,1,0:T(8,128)(2,1)S(1)}, bf16[4,32,1280]{2,1,0:T(8,128)(2,1)S(1)}, u32[]{:S(2)}, u32[]{:S(2)}) %collective-permute-start.10) | collective-permute-done | bytes 327712 | tf_op jit(solution)/shard_map/ppermute | solution.py:45
  101.0 0.6 add_head.2
  101.6 0.1 collective-permute-start.11
  101.7 2.1 %collective-permute-start.12 = (bf16[32,1280]{1,0:T(8,128)(2,1)S(1)}, bf16[32,1280]{1,0:T(8,128)(2,1)S(1)}, u32[]{:S(2)}, u32[]{:S(2)}) collective-permute-start(bf16[32,1280]{1,0:T(8,128)(2,1)S(1)} %get-tuple-element.49), channel_id=1, source_target_pairs={{0,8},{4,12},{8,0},{12,4},{1,9},{5,13},{9,1},{13,5},{2,10},{6,14},... | collective-permute-start | bytes 245768 | tf_op jit(solution)/shard_map/ppermute | solution.py:45
  103.8 2.3 %collective-permute-start.13 = (bf16[32,1280]{1,0:T(8,128)(2,1)S(1)}, bf16[32,1280]{1,0:T(8,128)(2,1)S(1)}, u32[]{:S(2)}, u32[]{:S(2)}) collective-permute-start(bf16[32,1280]{1,0:T(8,128)(2,1)S(1)} %get-tuple-element.50), channel_id=1, source_target_pairs={{0,12},{4,8},{8,4},{12,0},{1,13},{5,9},{9,5},{13,1},{2,14},{6,10},... | collective-permute-start | bytes 245768 | tf_op jit(solution)/shard_map/ppermute | solution.py:45
  106.1 1.6 %collective-permute-done.17.refs_0_ = bf16[4,32,1280]{2,1,0:T(8,128)(2,1)S(1)} collective-permute-done((bf16[4,32,1280]{2,1,0:T(8,128)(2,1)S(1)}, bf16[4,32,1280]{2,1,0:T(8,128)(2,1)S(1)}, u32[]{:S(2)}, u32[]{:S(2)}) %collective-permute-start.17) | collective-permute-done | bytes 327712 | tf_op jit(solution)/shard_map/ppermute | solution.py:45
  107.6 0.6 add_head.3
  108.2 0.1 collective-permute-start.18
  108.3 2.1 %collective-permute-start.19 = (bf16[32,1280]{1,0:T(8,128)(2,1)S(1)}, bf16[32,1280]{1,0:T(8,128)(2,1)S(1)}, u32[]{:S(2)}, u32[]{:S(2)}) collective-permute-start(bf16[32,1280]{1,0:T(8,128)(2,1)S(1)} %get-tuple-element.63), channel_id=1, source_target_pairs={{0,8},{4,12},{8,0},{12,4},{1,9},{5,13},{9,1},{13,5},{2,10},{6,14},... | collective-permute-start | bytes 245768 | tf_op jit(solution)/shard_map/ppermute | solution.py:45
  110.4 2.3 %collective-permute-start.20 = (bf16[32,1280]{1,0:T(8,128)(2,1)S(1)}, bf16[32,1280]{1,0:T(8,128)(2,1)S(1)}, u32[]{:S(2)}, u32[]{:S(2)}) collective-permute-start(bf16[32,1280]{1,0:T(8,128)(2,1)S(1)} %get-tuple-element.64), channel_id=1, source_target_pairs={{0,12},{4,8},{8,4},{12,0},{1,13},{5,9},{9,5},{13,1},{2,14},{6,10},... | collective-permute-start | bytes 245768 | tf_op jit(solution)/shard_map/ppermute | solution.py:45
  112.7 0.6 collective-permute-done.18.refs_5_
  113.3 4.4 %collective-permute-done.19.refs_6_ = bf16[32,1280]{1,0:T(8,128)(2,1)S(1)} collective-permute-done((bf16[32,1280]{1,0:T(8,128)(2,1)S(1)}, bf16[32,1280]{1,0:T(8,128)(2,1)S(1)}, u32[]{:S(2)}, u32[]{:S(2)}) %collective-permute-start.19) | collective-permute-done | bytes 81952 | tf_op jit(solution)/shard_map/ppermute | solution.py:45
  117.7 1.6 %mix.1 = bf16[64,5120]{1,0:T(8,128)(2,1)} custom-call(s32[5]{0:T(128)S(1)} %copy-done.3, bf16[64,5120]{1,0:T(8,128)(2,1)S(1)} %copy-done.2, f32[1,5120]{1,0:T(1,128)S(1)} %bitcast.16, bf16[32,1280]{1,0:T(8,128)(2,1)S(1)} %get-tuple-element.47.refs_0_, bf16[32,1280]{1,0:T(8,128)(2,1)S(1)} %collective-permute-done.11.refs_1_, ...), custom_call_target="tpu_custom_call" | custom-call | flops 1 | tf_op jit(solution)/shard_map/mix/pallas_call | solution.py:263
  (16 shorter events, 0.0 us)
Async XLA Ops:
  3.6 15.4 %collective-permute-start = (bf16[3,256,256]{2,1,0:T(8,128)(2,1)}, bf16[3,256,256]{2,1,0:T(8,128)(2,1)S(1)}, u32[]{:S(2)}, u32[]{:S(2)}) collective-permute-start(bf16[3,256,256]{2,1,0:T(8,128)(2,1)} %get-tuple-element.37), channel_id=1, source_target_pairs={{0,12},{4,8},{8,4},{12,0},{1,13},{5,9},{9,5},{13,1},{2,14},{6,10},... | collective-permute-start | bytes 1179656 | tf_op jit(solution)/shard_map/ppermute | solution.py:45
  8.7 33.8 %collective-permute-start.1 = (bf16[3,256,256]{2,1,0:T(8,128)(2,1)}, bf16[3,256,256]{2,1,0:T(8,128)(2,1)S(1)}, u32[]{:S(2)}, u32[]{:S(2)}) collective-permute-start(bf16[3,256,256]{2,1,0:T(8,128)(2,1)} %get-tuple-element.36), channel_id=1, source_target_pairs={{0,8},{4,12},{8,0},{12,4},{1,9},{5,13},{9,1},{13,5},{2,10},{6,14},... | collective-permute-start | bytes 1179656 | tf_op jit(solution)/shard_map/ppermute | solution.py:45
  8.7 33.8 %collective-permute-start.2 = (bf16[3,256,256]{2,1,0:T(8,128)(2,1)}, bf16[3,256,256]{2,1,0:T(8,128)(2,1)S(1)}, u32[]{:S(2)}, u32[]{:S(2)}) collective-permute-start(bf16[3,256,256]{2,1,0:T(8,128)(2,1)} %get-tuple-element.35), channel_id=1, source_target_pairs={{0,4},{4,0},{8,12},{12,8},{1,5},{5,1},{9,13},{13,9},{2,6},{6,2},{1... | collective-permute-start | bytes 1179656 | tf_op jit(solution)/shard_map/ppermute | solution.py:45
  10.0 32.5 %copy-start.3 = (s32[5]{0:T(128)S(1)}, s32[5]{0:T(128)}, u32[]{:S(2)}) copy-start(s32[5]{0:T(128)} %stack.27.where_ref) | copy-start | bytes 64
  10.0 68.3 %copy-start = (bf16[1024,1280]{1,0:T(8,128)(2,1)S(1)}, bf16[1024,1280]{1,0:T(8,128)(2,1)}, u32[]{:S(2)}) copy-start(bf16[1024,1280]{1,0:T(8,128)(2,1)} %refs_5_.3) | copy-start | bytes 7864324
  42.5 1.0 copy-start.1
  45.7 15.5 %collective-permute-start.3 = (bf16[512,256]{1,0:T(8,128)(2,1)S(1)}, bf16[512,256]{1,0:T(8,128)(2,1)S(1)}, u32[]{:S(2)}, u32[]{:S(2)}) collective-permute-start(bf16[512,256]{1,0:T(8,128)(2,1)S(1)} %bitcast.12), channel_id=1, source_target_pairs={{0,8},{4,12},{8,0},{12,4},{1,9},{5,13},{9,1},{13,5},{2,10},{6,14},... | collective-permute-start | bytes 786440 | tf_op jit(solution)/shard_map/ppermute | solution.py:45
  45.7 15.8 %collective-permute-start.4 = (bf16[512,256]{1,0:T(8,128)(2,1)S(1)}, bf16[512,256]{1,0:T(8,128)(2,1)S(1)}, u32[]{:S(2)}, u32[]{:S(2)}) collective-permute-start(bf16[512,256]{1,0:T(8,128)(2,1)S(1)} %bitcast.13), channel_id=1, source_target_pairs={{0,4},{4,0},{8,12},{12,8},{1,5},{5,1},{9,13},{13,9},{2,6},{6,2},{1... | collective-permute-start | bytes 786440 | tf_op jit(solution)/shard_map/ppermute | solution.py:45
  50.9 19.7 %collective-permute-start.7 = (bf16[512,256]{1,0:T(8,128)(2,1)S(1)}, bf16[512,256]{1,0:T(8,128)(2,1)S(1)}, u32[]{:S(2)}, u32[]{:S(2)}) collective-permute-start(bf16[512,256]{1,0:T(8,128)(2,1)S(1)} %bitcast.8), channel_id=1, source_target_pairs={{0,8},{4,12},{8,0},{12,4},{1,9},{5,13},{9,1},{13,5},{2,10},{6,14},... | collective-permute-start | bytes 786440 | tf_op jit(solution)/shard_map/ppermute | solution.py:45
  51.1 20.5 %collective-permute-start.8 = (bf16[512,256]{1,0:T(8,128)(2,1)S(1)}, bf16[512,256]{1,0:T(8,128)(2,1)S(1)}, u32[]{:S(2)}, u32[]{:S(2)}) collective-permute-start(bf16[512,256]{1,0:T(8,128)(2,1)S(1)} %bitcast.9), channel_id=1, source_target_pairs={{0,4},{4,0},{8,12},{12,8},{1,5},{5,1},{9,13},{13,9},{2,6},{6,2},{1... | collective-permute-start | bytes 786440 | tf_op jit(solution)/shard_map/ppermute | solution.py:45
  61.5 14.8 %collective-permute-start.6 = (bf16[512,256]{1,0:T(8,128)(2,1)S(1)}, bf16[512,256]{1,0:T(8,128)(2,1)S(1)}, u32[]{:S(2)}, u32[]{:S(2)}) collective-permute-start(bf16[512,256]{1,0:T(8,128)(2,1)S(1)} %collective-permute-done.3.refs_2_), channel_id=1, source_target_pairs={{4,0},{8,12},{5,1},{9,13},{6,2},{10,14},{7,3},{11,15},{20,16},{24,... | collective-permute-start | bytes 786440 | tf_op jit(solution)/shard_map/ppermute | solution.py:285
  62.8 15.5 %collective-permute-start.5 = (bf16[512,256]{1,0:T(8,128)(2,1)S(1)}, bf16[512,256]{1,0:T(8,128)(2,1)S(1)}, u32[]{:S(2)}, u32[]{:S(2)}) collective-permute-start(bf16[512,256]{1,0:T(8,128)(2,1)S(1)} %bitcast.14), channel_id=1, source_target_pairs={{4,8},{8,4},{5,9},{9,5},{6,10},{10,6},{7,11},{11,7},{20,24},{24,20... | collective-permute-start | bytes 786440 | tf_op jit(solution)/shard_map/ppermute | solution.py:45
  76.4 5.3 %collective-permute-start.14 = (bf16[512,256]{1,0:T(8,128)(2,1)S(1)}, bf16[512,256]{1,0:T(8,128)(2,1)S(1)}, u32[]{:S(2)}, u32[]{:S(2)}) collective-permute-start(bf16[512,256]{1,0:T(8,128)(2,1)S(1)} %bitcast.10), channel_id=1, source_target_pairs={{4,8},{8,4},{5,9},{9,5},{6,10},{10,6},{7,11},{11,7},{20,24},{24,20... | collective-permute-start | bytes 786440 | tf_op jit(solution)/shard_map/ppermute | solution.py:45
  77.1 9.4 %collective-permute-start.15 = (bf16[512,256]{1,0:T(8,128)(2,1)S(1)}, bf16[512,256]{1,0:T(8,128)(2,1)S(1)}, u32[]{:S(2)}, u32[]{:S(2)}) collective-permute-start(bf16[512,256]{1,0:T(8,128)(2,1)S(1)} %collective-permute-done.7.refs_2_), channel_id=1, source_target_pairs={{4,0},{8,12},{5,1},{9,13},{6,2},{10,14},{7,3},{11,15},{20,16},{24,... | collective-permute-start | bytes 786440 | tf_op jit(solution)/shard_map/ppermute | solution.py:285
  81.6 36.2 %copy-start.2 = (bf16[64,5120]{1,0:T(8,128)(2,1)S(1)}, bf16[64,5120]{1,0:T(8,128)(2,1)}, u32[]{:S(2)}) copy-start(bf16[64,5120]{1,0:T(8,128)(2,1)} %hidden_ref.1) | copy-start | bytes 1966084
  81.6 36.1 %copy-start.4 = (f32[5120]{0:T(1024)S(1)}, f32[5120]{0:T(1024)}, u32[]{:S(2)}) copy-start(f32[5120]{0:T(1024)} %param.13) | copy-start | bytes 61444
  81.6 8.1 %collective-permute-start.9 = (bf16[2,4,32,1280]{3,2,1,0:T(8,128)(2,1)S(1)}, bf16[2,4,32,1280]{3,2,1,0:T(8,128)(2,1)S(1)}, u32[]{:S(2)}, u32[]{:S(2)}) collective-permute-start(bf16[2,4,32,1280]{3,2,1,0:T(8,128)(2,1)S(1)} %get-tuple-element.44), channel_id=1, source_target_pairs={{0,1},{1,0},{2,3},{3,2},{4,5},{5,4},{6,7},{7,6},{8,9},{9,8},{10,11... | collective-permute-start | bytes 1966088 | tf_op jit(solution)/shard_map/ppermute | solution.py:45
  89.7 2.3 %collective-permute-start.16 = (bf16[2,4,32,1280]{3,2,1,0:T(8,128)(2,1)S(1)}, bf16[2,4,32,1280]{3,2,1,0:T(8,128)(2,1)S(1)}, u32[]{:S(2)}, u32[]{:S(2)}) collective-permute-start(bf16[2,4,32,1280]{3,2,1,0:T(8,128)(2,1)S(1)} %get-tuple-element.58), channel_id=1, source_target_pairs={{0,1},{1,0},{2,3},{3,2},{4,5},{5,4},{6,7},{7,6},{8,9},{9,8},{10,11... | collective-permute-start | bytes 1966088 | tf_op jit(solution)/shard_map/ppermute | solution.py:45
  90.4 10.6 %collective-permute-start.10 = (bf16[4,32,1280]{2,1,0:T(8,128)(2,1)S(1)}, bf16[4,32,1280]{2,1,0:T(8,128)(2,1)S(1)}, u32[]{:S(2)}, u32[]{:S(2)}) collective-permute-start(bf16[4,32,1280]{2,1,0:T(8,128)(2,1)S(1)} %get-tuple-element.46), channel_id=1, source_target_pairs={{0,2},{2,0},{1,3},{3,1},{4,6},{6,4},{5,7},{7,5},{8,10},{10,8},{9,1... | collective-permute-start | bytes 983048 | tf_op jit(solution)/shard_map/ppermute | solution.py:45
  92.7 14.9 %collective-permute-start.17 = (bf16[4,32,1280]{2,1,0:T(8,128)(2,1)S(1)}, bf16[4,32,1280]{2,1,0:T(8,128)(2,1)S(1)}, u32[]{:S(2)}, u32[]{:S(2)}) collective-permute-start(bf16[4,32,1280]{2,1,0:T(8,128)(2,1)S(1)} %get-tuple-element.60), channel_id=1, source_target_pairs={{0,2},{2,0},{1,3},{3,1},{4,6},{6,4},{5,7},{7,5},{8,10},{10,8},{9,1... | collective-permute-start | bytes 983048 | tf_op jit(solution)/shard_map/ppermute | solution.py:45
  101.6 8.8 %collective-permute-start.11 = (bf16[32,1280]{1,0:T(8,128)(2,1)S(1)}, bf16[32,1280]{1,0:T(8,128)(2,1)S(1)}, u32[]{:S(2)}, u32[]{:S(2)}) collective-permute-start(bf16[32,1280]{1,0:T(8,128)(2,1)S(1)} %get-tuple-element.48), channel_id=1, source_target_pairs={{0,4},{4,0},{8,12},{12,8},{1,5},{5,1},{9,13},{13,9},{2,6},{6,2},{1... | collective-permute-start | bytes 245768 | tf_op jit(solution)/shard_map/ppermute | solution.py:45
  101.7 11.0 %collective-permute-start.12 = (bf16[32,1280]{1,0:T(8,128)(2,1)S(1)}, bf16[32,1280]{1,0:T(8,128)(2,1)S(1)}, u32[]{:S(2)}, u32[]{:S(2)}) collective-permute-start(bf16[32,1280]{1,0:T(8,128)(2,1)S(1)} %get-tuple-element.49), channel_id=1, source_target_pairs={{0,8},{4,12},{8,0},{12,4},{1,9},{5,13},{9,1},{13,5},{2,10},{6,14},... | collective-permute-start | bytes 245768 | tf_op jit(solution)/shard_map/ppermute | solution.py:45
  103.8 8.9 %collective-permute-start.13 = (bf16[32,1280]{1,0:T(8,128)(2,1)S(1)}, bf16[32,1280]{1,0:T(8,128)(2,1)S(1)}, u32[]{:S(2)}, u32[]{:S(2)}) collective-permute-start(bf16[32,1280]{1,0:T(8,128)(2,1)S(1)} %get-tuple-element.50), channel_id=1, source_target_pairs={{0,12},{4,8},{8,4},{12,0},{1,13},{5,9},{9,5},{13,1},{2,14},{6,10},... | collective-permute-start | bytes 245768 | tf_op jit(solution)/shard_map/ppermute | solution.py:45
  108.2 5.1 %collective-permute-start.18 = (bf16[32,1280]{1,0:T(8,128)(2,1)S(1)}, bf16[32,1280]{1,0:T(8,128)(2,1)S(1)}, u32[]{:S(2)}, u32[]{:S(2)}) collective-permute-start(bf16[32,1280]{1,0:T(8,128)(2,1)S(1)} %get-tuple-element.62), channel_id=1, source_target_pairs={{0,4},{4,0},{8,12},{12,8},{1,5},{5,1},{9,13},{13,9},{2,6},{6,2},{1... | collective-permute-start | bytes 245768 | tf_op jit(solution)/shard_map/ppermute | solution.py:45
  108.3 9.4 %collective-permute-start.19 = (bf16[32,1280]{1,0:T(8,128)(2,1)S(1)}, bf16[32,1280]{1,0:T(8,128)(2,1)S(1)}, u32[]{:S(2)}, u32[]{:S(2)}) collective-permute-start(bf16[32,1280]{1,0:T(8,128)(2,1)S(1)} %get-tuple-element.63), channel_id=1, source_target_pairs={{0,8},{4,12},{8,0},{12,4},{1,9},{5,13},{9,1},{13,5},{2,10},{6,14},... | collective-permute-start | bytes 245768 | tf_op jit(solution)/shard_map/ppermute | solution.py:45
  110.4 7.3 %collective-permute-start.20 = (bf16[32,1280]{1,0:T(8,128)(2,1)S(1)}, bf16[32,1280]{1,0:T(8,128)(2,1)S(1)}, u32[]{:S(2)}, u32[]{:S(2)}) collective-permute-start(bf16[32,1280]{1,0:T(8,128)(2,1)S(1)} %get-tuple-element.64), channel_id=1, source_target_pairs={{0,12},{4,8},{8,4},{12,0},{1,13},{5,9},{9,5},{13,1},{2,14},{6,10},... | collective-permute-start | bytes 245768 | tf_op jit(solution)/shard_map/ppermute | solution.py:45

commit v8 on v7

--- a/solution.py
+++ b/solution.py
@@ -16,7 +16,7 @@
 ATTEND_FLOPS = 1
 PROJECT_FLOPS = 1
 
-PATCH, NEAR, HEAD, SUB, INNER = range(5)
+PATCH, NEAR, HEAD, SUB, INNER, GRP = range(6)
 
 
 def spec(shape):
@@ -141,7 +141,6 @@
             pl.BlockSpec((2, tok, feat), lambda i, w: (0, w[PATCH], w[NEAR])),
         ],
         spec(out.shape),
-        vmem=PACK_VMEM_BYTES,
     )(where, exponents, queries, fresh_kv, cached_kv)
 
 
@@ -340,26 +339,9 @@
     )(where, *sums)
 
 
-def body(sizes, queries, fresh_kv, cached_kv, exponents, out_weight, hidden_in, attn_gate):
+def sum_tail(sizes, where, pieces, kv_pieces, out_weight, hidden_in, attn_gate):
     n_patch, n_head, n_sub = sizes["patch"], sizes["head"], sizes["sub"]
-    tok, channels = queries.shape
-    heads = channels // HEAD_DIM
-    split = math.gcd(heads, n_patch)
-    patch_at = lax.axis_index("patch")
-    inner = (patch_at > 0) & (patch_at < n_patch - 1)
-    where = jnp.stack(
-        [patch_at, patch_at % split, lax.axis_index("head"), lax.axis_index("sub"), inner]
-    ).astype(jnp.int32)
-
-    arrays = (exponents, queries, fresh_kv, cached_kv)
-    sent = pack(split, *arrays)
-    far_first = [swap(sent[rel - 1], "patch", n_patch, rel) for rel in range(split - 1, 0, -1)]
-    where, sent = lax.optimization_barrier((where, sent))
-    pieces = [pack_own(split, where, *arrays), *far_first]
-    kv_pieces = list(pieces)
-    for rel in range(split, n_patch, split):
-        kv_pieces += [swap(x, "patch", n_patch, rel) for x in pieces]
-
+    split, tok = len(pieces), pieces[0].shape[1]
     count = n_head * n_sub
     piece = tok // count
     parts = 2 if piece % 32 == 0 else 1
@@ -377,6 +359,232 @@
             [total[0]] + [swap(total[rel], "patch", n_patch, rel) for rel in range(1, n_patch)]
         )
     return mix(where, hidden_in, attn_gate, blocks)
+
+
+def attend_halves_kernel(where_ref, *refs):
+    pieces, outs = refs[:-2], refs[-2:]
+    split = len(pieces)
+    rels = [0, *range(split - 1, 0, -1)]
+    factor = HEAD_DIM**-0.5 * math.log2(math.e)
+    rows, feat = outs[0].shape[1:]
+    for head in range(feat // HEAD_DIM):
+        lanes = pl.ds(head * HEAD_DIM, HEAD_DIM)
+        keys = jnp.concatenate([ref[1, :, lanes] for ref in pieces], axis=0)
+        values = jnp.concatenate([ref[2, :, lanes] for ref in pieces], axis=0)
+        values = jnp.concatenate([values, jnp.ones_like(values)], axis=1)
+        for half, out in enumerate(outs):
+            start = pl.multiple_of((where_ref[HEAD] ^ half) * rows, rows)
+            query = jnp.concatenate([ref[0, pl.ds(start, rows), lanes] for ref in pieces], axis=0)
+            scores = lax.dot_general(
+                query, keys, (((1,), (1,)), ((), ())), preferred_element_type=jnp.float32
+            )
+            peak = jnp.max(scores, axis=1, keepdims=True)
+            expo = jnp.exp2((scores - peak) * factor).astype(jnp.bfloat16)
+            mix = jnp.dot(expo, values, preferred_element_type=jnp.float32)
+            mix = (mix[:, :HEAD_DIM] / mix[:, HEAD_DIM:]).astype(jnp.bfloat16)
+            for at, rel in enumerate(rels):
+                out[where_ref[NEAR] ^ rel, :, lanes] = mix[at * rows : (at + 1) * rows]
+
+
+def attend_halves(where, pieces):
+    split = len(pieces)
+    _, tok, feat = pieces[0].shape
+    out = jax.ShapeDtypeStruct((split, tok // 2, feat), jnp.bfloat16)
+    outs = call(
+        attend_halves_kernel,
+        "attend",
+        [out] * 2,
+        1,
+        [spec((3, tok, feat))] * split,
+        [spec(out.shape)] * 2,
+    )(where, *pieces)
+    return [x.reshape(-1, feat) for x in outs]
+
+
+def hold_slots(slots, more, held_ref, where_ref, place):
+    feat = slots[0].shape[1]
+    for at, slot in enumerate(slots):
+        block = slot[...]
+        if at == len(slots) - 1:
+            block = jnp.where(where_ref[INNER] == 1, block, more[...])
+        lane = place(where_ref[NEAR] ^ at) * feat
+        held_ref[:, pl.ds(pl.multiple_of(lane, HEAD_DIM), feat)] = block
+
+
+def first_kernel(where_ref, *refs):
+    slots, (more, weight_ref, out_ref, held_ref) = refs[:4], refs[4:]
+
+    @pl.when(pl.program_id(0) == 0)
+    def arrange():
+        hold_slots(slots, more, held_ref, where_ref, lambda at: at)
+
+    out_ref[...] = jnp.dot(held_ref[...], weight_ref[...], preferred_element_type=jnp.float32)
+
+
+def first_product(where, slots, more, weight):
+    rows, feat = slots[0].shape
+    depth, cols = weight.shape
+    wide = cols // 2
+    return call(
+        first_kernel,
+        "first",
+        jax.ShapeDtypeStruct((rows, cols), jnp.float32),
+        2,
+        [spec((rows, feat))] * 5 + [pl.BlockSpec((depth, wide), lambda i, w: (0, i))],
+        pl.BlockSpec((rows, wide), lambda i, w: (0, i)),
+        [pltpu.VMEM((rows, depth), jnp.bfloat16)],
+    )(where, *slots, *more, weight)
+
+
+def second_kernel(where_ref, *refs):
+    slots, more, weights, (acc_in, keep_ref, send_ref, held_ref, acc_ref) = (
+        refs[:4],
+        refs[4],
+        refs[5:7],
+        refs[7:],
+    )
+
+    def place(at):
+        return 2 * ((at // 2) ^ where_ref[GRP]) + at % 2
+
+    hold_slots(slots, more, held_ref, where_ref, place)
+    depth = weights[0].shape[0]
+    acc = acc_in[...]
+    for at, weight in enumerate(weights):
+        acc += jnp.dot(
+            held_ref[:, at * depth : (at + 1) * depth],
+            weight[...],
+            preferred_element_type=jnp.float32,
+        )
+    acc_ref[...] = acc.reshape(acc_ref.shape)
+    for sub, out in enumerate((keep_ref, send_ref)):
+        for at in range(4):
+            out[at] = acc_ref[where_ref[NEAR] ^ at, where_ref[SUB] ^ sub].astype(jnp.bfloat16)
+
+
+def second_product(where, chunk, slots, more, weights, acc):
+    rows, feat = slots[0].shape
+    depth, cols = weights[0].shape
+    wide = cols // 2
+    out = jax.ShapeDtypeStruct((4, rows // 8, wide), jnp.bfloat16)
+    return call(
+        second_kernel,
+        "second",
+        [out] * 2,
+        1,
+        [spec((rows, feat))] * 5
+        + [pl.BlockSpec((depth, wide), lambda i, w: (0, chunk))] * 2
+        + [pl.BlockSpec((rows, wide), lambda i, w: (0, chunk))],
+        [spec(out.shape)] * 2,
+        [
+            pltpu.VMEM((rows, 2 * depth), jnp.bfloat16),
+            pltpu.VMEM((4, 2, rows // 8, wide), jnp.float32),
+        ],
+    )(where, *slots, *more, *weights, acc)
+
+
+def add_kernel(where_ref, keep_ref, term_ref, *outs):
+    for at, out in enumerate(outs):
+        total = keep_ref[at].astype(jnp.float32) + term_ref[at].astype(jnp.float32)
+        out[...] = total.astype(jnp.bfloat16)
+
+
+def add(where, keep, term):
+    return call(
+        add_kernel,
+        "add",
+        [jax.ShapeDtypeStruct(keep.shape[1:], jnp.bfloat16)] * keep.shape[0],
+        1,
+        [spec(keep.shape)] * 2,
+        [spec(keep.shape[1:])] * keep.shape[0],
+    )(where, keep, term)
+
+
+def share_tail(sizes, where, pieces, kv_pieces, out_weight, hidden_in, attn_gate):
+    half = out_weight.shape[0] // 2
+    out_weight, where = lax.optimization_barrier((out_weight, where))
+    start = lax.axis_index("grp") * half
+    fetched = swap(lax.dynamic_slice_in_dim(out_weight, start, half, 0), "head", 2, 1)
+    pieces, fetched = lax.optimization_barrier((pieces, fetched))
+    passed = swap(fetched, "grp", 2, 1)
+
+    mine, other = attend_halves(where, pieces)
+    other = swap(other, "head", 2, 1)
+    slots = []
+    for at, x in enumerate((mine, other)):
+        far, next_to = swap(x, "patch", 4, 2), swap(x, "patch", 4, 1)
+        far, next_to, other, x = lax.optimization_barrier((far, next_to, other, x))
+        if at == 1:
+            far, x, passed = lax.optimization_barrier((far, x, passed))
+        middle = swap(x, "patch", 4, 3, (1, 2))
+        ends = lax.ppermute(far, "patch", [(1, 0), (2, 3)])
+        slots.append(([x, next_to, far, middle], [ends]))
+    acc = first_product(where, *slots[0], out_weight)
+    terms = [second_product(where, at, *slots[1], [fetched, passed], acc) for at in range(2)]
+    blocks = []
+    for keep, send in terms:
+        total = add(where, keep, swap(send, "sub", 2, 1))
+        blocks.append([total[0]] + [swap(total[rel], "patch", 4, rel) for rel in range(1, 4)])
+    return mix_columns(where, hidden_in, attn_gate, blocks)
+
+
+def mix_columns_kernel(where_ref, hidden_ref, gate_ref, *refs):
+    blocks, out_ref = refs[:-1], refs[-1]
+    cols = blocks[0].shape[1]
+    for chunk in range(2):
+        for rel in range(4):
+            start = (2 * (where_ref[PATCH] ^ rel) + chunk) * cols
+            lanes = pl.ds(pl.multiple_of(start, HEAD_DIM), cols)
+            mixed = hidden_ref[:, lanes].astype(jnp.float32) + gate_ref[:, lanes] * blocks[
+                4 * chunk + rel
+            ][...].astype(jnp.float32)
+            out_ref[:, lanes] = mixed.astype(jnp.bfloat16)
+
+
+def mix_columns(where, hidden_in, attn_gate, blocks):
+    rows, width = hidden_in.shape
+    flat = [x for chunk in blocks for x in chunk]
+    return call(
+        mix_columns_kernel,
+        "mix",
+        jax.ShapeDtypeStruct((rows, width), jnp.bfloat16),
+        1,
+        [spec((rows, width)), spec((1, width))] + [spec(flat[0].shape)] * len(flat),
+        spec((rows, width)),
+    )(where, hidden_in, attn_gate[None], *flat)
+
+
+def body(sizes, queries, fresh_kv, cached_kv, exponents, out_weight, hidden_in, attn_gate):
+    n_patch, n_head, n_sub = sizes["patch"], sizes["head"], sizes["sub"]
+    tok, channels = queries.shape
+    heads = channels // HEAD_DIM
+    split = math.gcd(heads, n_patch)
+    patch_at = lax.axis_index("patch")
+    inner = (patch_at > 0) & (patch_at < n_patch - 1)
+    where = jnp.stack(
+        [
+            patch_at,
+            patch_at % split,
+            lax.axis_index("head"),
+            lax.axis_index("sub"),
+            inner,
+            lax.axis_index("grp"),
+        ]
+    ).astype(jnp.int32)
+
+    arrays = (exponents, queries, fresh_kv, cached_kv)
+    sent = pack(split, *arrays)
+    far_first = [swap(sent[rel - 1], "patch", n_patch, rel) for rel in range(split - 1, 0, -1)]
+    where, sent = lax.optimization_barrier((where, sent))
+    pieces = [pack_own(split, where, *arrays), *far_first]
+    kv_pieces = list(pieces)
+    for rel in range(split, n_patch, split):
+        kv_pieces += [swap(x, "patch", n_patch, rel) for x in pieces]
+
+    tail = (sizes, where, pieces, kv_pieces, out_weight, hidden_in, attn_gate)
+    if (sizes["grp"], n_head, split, n_patch) == (2, 2, 4, 4):
+        return share_tail(*tail)
+    return sum_tail(*tail)
 
 
 def solution(mesh):

time: 120 us -> 109 us (0.908)
  waiting for transfers between devices: 69.4 us -> 59.3 us
  Pallas kernels: 21.3 us -> 18.2 us
  starting transfers between devices: 26.7 us -> 28.6 us
    ppermute x19 -> x20, waiting for transfers between devices: 59.8 us -> 53.6 us  [swap(): return lax.ppermute(x, axes, pairs)]
    ppermute x2, waiting for transfers between devices: 9.6 us -> 5.64 us  [share_tail(): ends = lax.ppermute(far, 'patch', [(1, 0), (2, 3)])]
    ppermute x19 -> x20, starting transfers between devices: 24.1 us -> 26 us  [swap(): return lax.ppermute(x, axes, pairs)]
    pallas_call x9 -> x7, Pallas kernels: 14.9 us -> 13.3 us  [the longest x1 3.79 us: attend_halves(): call(attend_halves_kernel, 'attend', [out] * 2, 1, [spec((3, tok, feat))]...]
    pallas_call x1, Pallas kernels: 2.84 us -> 1.28 us  [pack_own(): call(functools.partial(own_kernel, feat // HEAD_DIM), 'own', out, 1, [pl....]
    unnamed x10 -> x18, local copies, waits for them, and re-layouts: 1.01 us -> 2.23 us
  transfers between devices with their start and end apart: 21 -> 22, of which waited for: 12 -> 11; matrix products, arithmetic and copies ran while one was open for 1% -> 0% of each run, Pallas kernels for 12% -> 10%
where the time goes in v8:
time: 109 us
  waiting for transfers between devices  59.3 us (54%)
  starting transfers between devices  28.6 us (26%)
  Pallas kernels  18.2 us (17%)
  local copies, waits for them, and re-layouts  2.41 us (2%)
    ppermute x20, waiting for transfers between devices, swap(): return lax.ppermute(x, axes, pairs)  53.6 us
    ppermute x20, starting transfers between devices, swap(): return lax.ppermute(x, axes, pairs)  26 us
    ppermute x2, waiting for transfers between devices, share_tail(): ends = lax.ppermute(far, 'patch', [(1, 0), (2, 3)])  5.64 us
    pallas_call x1, Pallas kernels, attend_halves(): call(attend_halves_kernel, 'attend', [out] * 2, 1, [spec((3, tok, feat))]...  3.79 us
    pallas_call x1, Pallas kernels, pack(): pl.pallas_call(functools.partial(pack_kernel, split, feat // HEAD_DIM), o...  3.71 us
    pallas_call x2, Pallas kernels, second_product(): call(second_kernel, 'second', [out] * 2, 1, [spec((rows, feat))] * 5 + [p...  3.56 us
    pallas_call x1, Pallas kernels, first_product(): call(first_kernel, 'first', jax.ShapeDtypeStruct((rows, cols), jnp.float3...  3.06 us
    ppermute x2, starting transfers between devices, share_tail(): ends = lax.ppermute(far, 'patch', [(1, 0), (2, 3)])  2.58 us
  transfers between devices with their start and end apart: 22, of which 11 were waited for; matrix products, arithmetic and copies ran while one was open for 0% of the time, Pallas kernels for 10%

profile of v8, /device:TPU:0, one launch (start us, length us, event | category | flops | bytes accessed | tf_op | source)
XLA Modules:
  0.0 108.7 jit_solution(10687618008385324187)
XLA Ops:
  0.0 3.7 %pack.1 = (bf16[3,256,256]{2,1,0:T(8,128)(2,1)}, bf16[3,256,256]{2,1,0:T(8,128)(2,1)}, bf16[3,256,256]{2,1,0:T(8,128)(2,1)}) custom-call(s32[2,2,8]{2,1,0:T(2,128)} %exps_ref.3, bf16[256,1024]{1,0:T(8,128)(2,1)} %q_ref.3, bf16[2,256,1024]{2,1,0:T(8,128)(2,1)} %fresh_ref.3, bf16[2,1024,1024]{2,1,0:T(8,128)(2,1)} %cached_ref.3), custom_call_target="tpu_custom_call" | custom-call | tf_op jit(solution)/shard_map/pack/pallas_call | solution.py:98
  3.7 0.0 copy-start.7
  3.7 0.0 copy-start.3
  3.7 0.0 copy-start.6
  3.8 0.1 stack.31.where_ref
  3.8 0.0 copy-start.2
  3.9 0.1 constant_dynamic-slice_fusion
  4.0 3.0 %collective-permute-start.3 = (bf16[512,1280]{1,0:T(8,128)(2,1)S(1)}, bf16[512,1280]{1,0:T(8,128)(2,1)S(1)}, u32[]{:S(2)}, u32[]{:S(2)}) collective-permute-start(bf16[512,1280]{1,0:T(8,128)(2,1)S(1)} %constant_dynamic-slice_fusion), channel_id=1, source_target_pairs={{0,2},{2,0},{1,3},{3,1},{4,6},{6,4},{5,7},{7,5},{8,10},{10,8},{9,1... | collective-permute-start | bytes 3932168 | tf_op jit(solution)/shard_map/ppermute | solution.py:45
  7.0 3.6 %collective-permute-start = (bf16[3,256,256]{2,1,0:T(8,128)(2,1)}, bf16[3,256,256]{2,1,0:T(8,128)(2,1)S(1)}, u32[]{:S(2)}, u32[]{:S(2)}) collective-permute-start(bf16[3,256,256]{2,1,0:T(8,128)(2,1)} %get-tuple-element.41), channel_id=1, source_target_pairs={{0,12},{4,8},{8,4},{12,0},{1,13},{5,9},{9,5},{13,1},{2,14},{6,10},... | collective-permute-start | bytes 1179656 | tf_op jit(solution)/shard_map/ppermute | solution.py:45
  10.6 0.8 collective-permute-start.2
  11.4 2.2 %copy-done = bf16[2,1024,1024]{2,1,0:T(8,128)(2,1)S(1)} copy-done((bf16[2,1024,1024]{2,1,0:T(8,128)(2,1)S(1)}, bf16[2,1024,1024]{2,1,0:T(8,128)(2,1)}, u32[]{:S(2)}) %copy-start) | copy-done | bytes 4194328
  13.6 1.3 %own.1.refs_0_ = bf16[3,256,256]{2,1,0:T(8,128)(2,1)S(1)} custom-call(s32[6]{0:T(128)S(1)} %stack.31.where_ref, s32[2,2,8]{2,1,0:T(2,128)S(1)} %copy-done.6, bf16[256,1024]{1,0:T(8,128)(2,1)S(1)} %copy-done.3, bf16[2,256,1024]{2,1,0:T(8,128)(2,1)S(1)} %copy-done.2, bf16[2,1024,1024]{2,1,0:T(8,128)(2,1)S(1)} %copy-done), custom_call_target="tpu_custom_call" | custom-call | flops 1 | tf_op jit(solution)/shard_map/own/pallas_call | solution.py:132
  14.8 6.3 %collective-permute-done.refs_1_ = bf16[3,256,256]{2,1,0:T(8,128)(2,1)S(1)} collective-permute-done((bf16[3,256,256]{2,1,0:T(8,128)(2,1)}, bf16[3,256,256]{2,1,0:T(8,128)(2,1)S(1)}, u32[]{:S(2)}, u32[]{:S(2)}) %collective-permute-start) | collective-permute-done | bytes 393248 | tf_op jit(solution)/shard_map/ppermute | solution.py:45
  21.1 22.9 %collective-permute-done.1.refs_2_ = bf16[3,256,256]{2,1,0:T(8,128)(2,1)S(1)} collective-permute-done((bf16[3,256,256]{2,1,0:T(8,128)(2,1)S(1)}, bf16[3,256,256]{2,1,0:T(8,128)(2,1)S(1)}, u32[]{:S(2)}, u32[]{:S(2)}) %collective-permute-start.1) | collective-permute-done | bytes 393248 | tf_op jit(solution)/shard_map/ppermute | solution.py:45
  44.0 1.5 %collective-permute-start.7 = (bf16[512,1280]{1,0:T(8,128)(2,1)S(1)}, bf16[512,1280]{1,0:T(8,128)(2,1)S(1)}, u32[]{:S(2)}, u32[]{:S(2)}) collective-permute-start(bf16[512,1280]{1,0:T(8,128)(2,1)S(1)} %collective-permute-done.3.refs_5_), channel_id=1, source_target_pairs={{0,16},{16,0},{1,17},{17,1},{2,18},{18,2},{3,19},{19,3},{4,20},{20... | collective-permute-start | bytes 3932168 | tf_op jit(solution)/shard_map/ppermute | solution.py:45
  45.6 3.8 %attend.1 = (bf16[4,128,256]{2,1,0:T(8,128)(2,1)S(1)}, bf16[4,128,256]{2,1,0:T(8,128)(2,1)S(1)}) custom-call(s32[6]{0:T(128)S(1)} %stack.31.where_ref, bf16[3,256,256]{2,1,0:T(8,128)(2,1)S(1)} %own.1.refs_0_, bf16[3,256,256]{2,1,0:T(8,128)(2,1)S(1)} %collective-permute-done.refs_1_, bf16[3,256,256]{2,1,0:T(8,128)(2,1)S(1)} %collective-permute-done.1.refs_2_, ...), custom_call_target="tpu_custom_call" | custom-call | flops 1 | tf_op jit(solution)/shard_map/attend/pallas_call | solution.py:393
  49.4 0.6 collective-permute-start.4
  50.0 3.0 %collective-permute-start.11 = (bf16[512,256]{1,0:T(8,128)(2,1)S(1)}, bf16[512,256]{1,0:T(8,128)(2,1)S(1)}, u32[]{:S(2)}, u32[]{:S(2)}) collective-permute-start(bf16[512,256]{1,0:T(8,128)(2,1)S(1)} %bitcast.10), channel_id=1, source_target_pairs={{0,4},{4,0},{8,12},{12,8},{1,5},{5,1},{9,13},{13,9},{2,6},{6,2},{1... | collective-permute-start | bytes 786440 | tf_op jit(solution)/shard_map/ppermute | solution.py:45
  53.0 3.5 %collective-permute-done.4.refs_0_ = bf16[512,256]{1,0:T(8,128)(2,1)S(1)} collective-permute-done((bf16[512,256]{1,0:T(8,128)(2,1)S(1)}, bf16[512,256]{1,0:T(8,128)(2,1)S(1)}, u32[]{:S(2)}, u32[]{:S(2)}) %collective-permute-start.4) | collective-permute-done | bytes 262176 | tf_op jit(solution)/shard_map/ppermute | solution.py:45
  56.5 2.6 %collective-permute-start.6 = (bf16[512,256]{1,0:T(8,128)(2,1)S(1)}, bf16[512,256]{1,0:T(8,128)(2,1)S(1)}, u32[]{:S(2)}, u32[]{:S(2)}) collective-permute-start(bf16[512,256]{1,0:T(8,128)(2,1)S(1)} %collective-permute-done.4.refs_0_), channel_id=1, source_target_pairs={{0,4},{4,0},{8,12},{12,8},{1,5},{5,1},{9,13},{13,9},{2,6},{6,2},{1... | collective-permute-start | bytes 786440 | tf_op jit(solution)/shard_map/ppermute | solution.py:45
  59.1 6.7 %collective-permute-done.10.refs_2_ = bf16[512,256]{1,0:T(8,128)(2,1)S(1)} collective-permute-done((bf16[512,256]{1,0:T(8,128)(2,1)S(1)}, bf16[512,256]{1,0:T(8,128)(2,1)S(1)}, u32[]{:S(2)}, u32[]{:S(2)}) %collective-permute-start.10) | collective-permute-done | bytes 262176 | tf_op jit(solution)/shard_map/ppermute | solution.py:45
  65.8 0.7 collective-permute-start.12
  66.4 1.3 %collective-permute-start.13 = (bf16[512,256]{1,0:T(8,128)(2,1)S(1)}, bf16[512,256]{1,0:T(8,128)(2,1)S(1)}, u32[]{:S(2)}, u32[]{:S(2)}) collective-permute-start(bf16[512,256]{1,0:T(8,128)(2,1)S(1)} %collective-permute-done.10.refs_2_), channel_id=1, source_target_pairs={{4,0},{8,12},{5,1},{9,13},{6,2},{10,14},{7,3},{11,15},{20,16},{24,... | collective-permute-start | bytes 786440 | tf_op jit(solution)/shard_map/ppermute | solution.py:520
  67.7 6.2 %collective-permute-done.5.refs_2_ = bf16[512,256]{1,0:T(8,128)(2,1)S(1)} collective-permute-done((bf16[512,256]{1,0:T(8,128)(2,1)S(1)}, bf16[512,256]{1,0:T(8,128)(2,1)S(1)}, u32[]{:S(2)}, u32[]{:S(2)}) %collective-permute-start.5) | collective-permute-done | bytes 262176 | tf_op jit(solution)/shard_map/ppermute | solution.py:45
  74.0 0.7 collective-permute-done.6.refs_1_
  74.7 0.7 collective-permute-start.8
  75.3 1.3 %collective-permute-start.9 = (bf16[512,256]{1,0:T(8,128)(2,1)S(1)}, bf16[512,256]{1,0:T(8,128)(2,1)S(1)}, u32[]{:S(2)}, u32[]{:S(2)}) collective-permute-start(bf16[512,256]{1,0:T(8,128)(2,1)S(1)} %collective-permute-done.5.refs_2_), channel_id=1, source_target_pairs={{4,0},{8,12},{5,1},{9,13},{6,2},{10,14},{7,3},{11,15},{20,16},{24,... | collective-permute-start | bytes 786440 | tf_op jit(solution)/shard_map/ppermute | solution.py:520
  76.7 3.6 %collective-permute-done.13.refs_4_ = bf16[512,256]{1,0:T(8,128)(2,1)S(1)} collective-permute-done((bf16[512,256]{1,0:T(8,128)(2,1)S(1)}, bf16[512,256]{1,0:T(8,128)(2,1)S(1)}, u32[]{:S(2)}, u32[]{:S(2)}) %collective-permute-start.13) | collective-permute-done | bytes 262176 | tf_op jit(solution)/shard_map/ppermute | solution.py:520
  80.3 3.1 %first.1.refs_7_ = f32[512,1280]{1,0:T(8,128)S(1)} custom-call(s32[6]{0:T(128)S(1)} %stack.31.where_ref, bf16[512,256]{1,0:T(8,128)(2,1)S(1)} %bitcast.12, bf16[512,256]{1,0:T(8,128)(2,1)S(1)} %collective-permute-done.11.refs_1_, bf16[512,256]{1,0:T(8,128)(2,1)S(1)} %collective-permute-done.10.refs_2_, bf16[512,256]{1,0:T(8,128)(2,1)S(1)} %collective-permute-done.12.refs_3_, ...), custom_call_target="tpu_custom_call" | custom-call | flops 1 | tf_op jit(solution)/shard_map/first/pallas_call | solution.py:428
  83.4 2.0 %collective-permute-done.9.refs_4_ = bf16[512,256]{1,0:T(8,128)(2,1)S(1)} collective-permute-done((bf16[512,256]{1,0:T(8,128)(2,1)S(1)}, bf16[512,256]{1,0:T(8,128)(2,1)S(1)}, u32[]{:S(2)}, u32[]{:S(2)}) %collective-permute-start.9) | collective-permute-done | bytes 262176 | tf_op jit(solution)/shard_map/ppermute | solution.py:520
  85.4 1.8 %second.3 = (bf16[4,64,640]{2,1,0:T(8,128)(2,1)S(1)}, bf16[4,64,640]{2,1,0:T(8,128)(2,1)S(1)}) custom-call(s32[6]{0:T(128)S(1)} %stack.31.where_ref, bf16[512,256]{1,0:T(8,128)(2,1)S(1)} %collective-permute-done.4.refs_0_, bf16[512,256]{1,0:T(8,128)(2,1)S(1)} %collective-permute-done.6.refs_1_, bf16[512,256]{1,0:T(8,128)(2,1)S(1)} %collective-permute-done.5.refs_2_, ...), custom_call_target="tpu_custom_call" | custom-call | flops 1 | tf_op jit(solution)/shard_map/second/pallas_call | solution.py:470
  87.2 0.0 copy-start.4
  87.2 0.0 copy-start.5
  87.2 0.1 collective-permute-start.18
  87.3 1.8 %second.2 = (bf16[4,64,640]{2,1,0:T(8,128)(2,1)S(1)}, bf16[4,64,640]{2,1,0:T(8,128)(2,1)S(1)}) custom-call(s32[6]{0:T(128)S(1)} %stack.31.where_ref, bf16[512,256]{1,0:T(8,128)(2,1)S(1)} %collective-permute-done.4.refs_0_, bf16[512,256]{1,0:T(8,128)(2,1)S(1)} %collective-permute-done.6.refs_1_, bf16[512,256]{1,0:T(8,128)(2,1)S(1)} %collective-permute-done.5.refs_2_, ...), custom_call_target="tpu_custom_call" | custom-call | flops 1 | tf_op jit(solution)/shard_map/second/pallas_call | solution.py:470
  89.0 0.6 collective-permute-start.14
  89.6 0.6 add.12
  90.2 0.3 collective-permute-start.19
  90.6 2.1 %collective-permute-start.20 = (bf16[64,640]{1,0:T(8,128)(2,1)S(1)}, bf16[64,640]{1,0:T(8,128)(2,1)S(1)}, u32[]{:S(2)}, u32[]{:S(2)}) collective-permute-start(bf16[64,640]{1,0:T(8,128)(2,1)S(1)} %get-tuple-element.71), channel_id=1, source_target_pairs={{0,8},{4,12},{8,0},{12,4},{1,9},{5,13},{9,1},{13,5},{2,10},{6,14},... | collective-permute-start | bytes 245768 | tf_op jit(solution)/shard_map/ppermute | solution.py:45
  92.7 2.0 %collective-permute-start.21 = (bf16[64,640]{1,0:T(8,128)(2,1)S(1)}, bf16[64,640]{1,0:T(8,128)(2,1)S(1)}, u32[]{:S(2)}, u32[]{:S(2)}) collective-permute-start(bf16[64,640]{1,0:T(8,128)(2,1)S(1)} %get-tuple-element.72), channel_id=1, source_target_pairs={{0,12},{4,8},{8,4},{12,0},{1,13},{5,9},{9,5},{13,1},{2,14},{6,10},... | collective-permute-start | bytes 245768 | tf_op jit(solution)/shard_map/ppermute | solution.py:45
  94.7 0.6 add.11
  95.3 0.1 collective-permute-start.15
  95.4 2.4 %collective-permute-start.16 = (bf16[64,640]{1,0:T(8,128)(2,1)S(1)}, bf16[64,640]{1,0:T(8,128)(2,1)S(1)}, u32[]{:S(2)}, u32[]{:S(2)}) collective-permute-start(bf16[64,640]{1,0:T(8,128)(2,1)S(1)} %get-tuple-element.65), channel_id=1, source_target_pairs={{0,8},{4,12},{8,0},{12,4},{1,9},{5,13},{9,1},{13,5},{2,10},{6,14},... | collective-permute-start | bytes 245768 | tf_op jit(solution)/shard_map/ppermute | solution.py:45
  97.8 2.0 %collective-permute-start.17 = (bf16[64,640]{1,0:T(8,128)(2,1)S(1)}, bf16[64,640]{1,0:T(8,128)(2,1)S(1)}, u32[]{:S(2)}, u32[]{:S(2)}) collective-permute-start(bf16[64,640]{1,0:T(8,128)(2,1)S(1)} %get-tuple-element.66), channel_id=1, source_target_pairs={{0,12},{4,8},{8,4},{12,0},{1,13},{5,9},{9,5},{13,1},{2,14},{6,10},... | collective-permute-start | bytes 245768 | tf_op jit(solution)/shard_map/ppermute | solution.py:45
  99.8 1.2 %collective-permute-done.20.refs_6_ = bf16[64,640]{1,0:T(8,128)(2,1)S(1)} collective-permute-done((bf16[64,640]{1,0:T(8,128)(2,1)S(1)}, bf16[64,640]{1,0:T(8,128)(2,1)S(1)}, u32[]{:S(2)}, u32[]{:S(2)}) %collective-permute-start.20) | collective-permute-done | bytes 81952 | tf_op jit(solution)/shard_map/ppermute | solution.py:45
  101.0 0.6 collective-permute-done.15.refs_1_
  101.7 5.4 %collective-permute-done.16.refs_2_ = bf16[64,640]{1,0:T(8,128)(2,1)S(1)} collective-permute-done((bf16[64,640]{1,0:T(8,128)(2,1)S(1)}, bf16[64,640]{1,0:T(8,128)(2,1)S(1)}, u32[]{:S(2)}, u32[]{:S(2)}) %collective-permute-start.16) | collective-permute-done | bytes 81952 | tf_op jit(solution)/shard_map/ppermute | solution.py:45
  107.1 1.6 %mix.1 = bf16[64,5120]{1,0:T(8,128)(2,1)} custom-call(s32[6]{0:T(128)S(1)} %stack.31.where_ref, bf16[64,5120]{1,0:T(8,128)(2,1)S(1)} %copy-done.4, f32[1,5120]{1,0:T(1,128)S(1)} %bitcast.13, bf16[64,640]{1,0:T(8,128)(2,1)S(1)} %get-tuple-element.63.refs_0_, bf16[64,640]{1,0:T(8,128)(2,1)S(1)} %collective-permute-done.15.refs_1_, ...), custom_call_target="tpu_custom_call" | custom-call | flops 1 | tf_op jit(solution)/shard_map/mix/pallas_call | solution.py:547
  (25 shorter events, 0.1 us)
Async XLA Ops:
  0.0 3.8 %copy-start.1 = (bf16[1024,1280]{1,0:T(8,128)(2,1)S(1)}, bf16[1024,1280]{1,0:T(8,128)(2,1)}, u32[]{:S(2)}) copy-start(bf16[1024,1280]{1,0:T(8,128)(2,1)} %refs_5_) | copy-start | bytes 7864324
  3.7 6.9 %copy-start.7 = (bf16[3,256,256]{2,1,0:T(8,128)(2,1)S(1)}, bf16[3,256,256]{2,1,0:T(8,128)(2,1)}, u32[]{:S(2)}) copy-start(bf16[3,256,256]{2,1,0:T(8,128)(2,1)} %get-tuple-element.39) | copy-start | bytes 1179652
  3.7 7.6 %copy-start.3 = (bf16[256,1024]{1,0:T(8,128)(2,1)S(1)}, bf16[256,1024]{1,0:T(8,128)(2,1)}, u32[]{:S(2)}) copy-start(bf16[256,1024]{1,0:T(8,128)(2,1)} %q_ref.3) | copy-start | bytes 1572868
  3.7 7.6 %copy-start.6 = (s32[2,2,8]{2,1,0:T(2,128)S(1)}, s32[2,2,8]{2,1,0:T(2,128)}, u32[]{:S(2)}) copy-start(s32[2,2,8]{2,1,0:T(2,128)} %exps_ref.3) | copy-start | bytes 388
  3.8 6.7 %copy-start.8 = (bf16[3,256,256]{2,1,0:T(8,128)(2,1)S(1)}, bf16[3,256,256]{2,1,0:T(8,128)(2,1)}, u32[]{:S(2)}) copy-start(bf16[3,256,256]{2,1,0:T(8,128)(2,1)} %get-tuple-element.40) | copy-start | bytes 1179652
  3.8 7.5 %copy-start.2 = (bf16[2,256,1024]{2,1,0:T(8,128)(2,1)S(1)}, bf16[2,256,1024]{2,1,0:T(8,128)(2,1)}, u32[]{:S(2)}) copy-start(bf16[2,256,1024]{2,1,0:T(8,128)(2,1)} %fresh_ref.3) | copy-start | bytes 3145732
  4.0 40.1 %collective-permute-start.3 = (bf16[512,1280]{1,0:T(8,128)(2,1)S(1)}, bf16[512,1280]{1,0:T(8,128)(2,1)S(1)}, u32[]{:S(2)}, u32[]{:S(2)}) collective-permute-start(bf16[512,1280]{1,0:T(8,128)(2,1)S(1)} %constant_dynamic-slice_fusion), channel_id=1, source_target_pairs={{0,2},{2,0},{1,3},{3,1},{4,6},{6,4},{5,7},{7,5},{8,10},{10,8},{9,1... | collective-permute-start | bytes 3932168 | tf_op jit(solution)/shard_map/ppermute | solution.py:45
  7.0 14.1 %collective-permute-start = (bf16[3,256,256]{2,1,0:T(8,128)(2,1)}, bf16[3,256,256]{2,1,0:T(8,128)(2,1)S(1)}, u32[]{:S(2)}, u32[]{:S(2)}) collective-permute-start(bf16[3,256,256]{2,1,0:T(8,128)(2,1)} %get-tuple-element.41), channel_id=1, source_target_pairs={{0,12},{4,8},{8,4},{12,0},{1,13},{5,9},{9,5},{13,1},{2,14},{6,10},... | collective-permute-start | bytes 1179656 | tf_op jit(solution)/shard_map/ppermute | solution.py:45
  10.6 33.5 %collective-permute-start.1 = (bf16[3,256,256]{2,1,0:T(8,128)(2,1)S(1)}, bf16[3,256,256]{2,1,0:T(8,128)(2,1)S(1)}, u32[]{:S(2)}, u32[]{:S(2)}) collective-permute-start(bf16[3,256,256]{2,1,0:T(8,128)(2,1)S(1)} %copy-done.8), channel_id=1, source_target_pairs={{0,8},{4,12},{8,0},{12,4},{1,9},{5,13},{9,1},{13,5},{2,10},{6,14},... | collective-permute-start | bytes 1179656 | tf_op jit(solution)/shard_map/ppermute | solution.py:45
  10.6 33.5 %collective-permute-start.2 = (bf16[3,256,256]{2,1,0:T(8,128)(2,1)S(1)}, bf16[3,256,256]{2,1,0:T(8,128)(2,1)S(1)}, u32[]{:S(2)}, u32[]{:S(2)}) collective-permute-start(bf16[3,256,256]{2,1,0:T(8,128)(2,1)S(1)} %copy-done.7), channel_id=1, source_target_pairs={{0,4},{4,0},{8,12},{12,8},{1,5},{5,1},{9,13},{13,9},{2,6},{6,2},{1... | collective-permute-start | bytes 1179656 | tf_op jit(solution)/shard_map/ppermute | solution.py:45
  11.4 2.2 %copy-start = (bf16[2,1024,1024]{2,1,0:T(8,128)(2,1)S(1)}, bf16[2,1024,1024]{2,1,0:T(8,128)(2,1)}, u32[]{:S(2)}) copy-start(bf16[2,1024,1024]{2,1,0:T(8,128)(2,1)} %cached_ref.3) | copy-start | bytes 12582916
  44.0 30.6 %collective-permute-start.7 = (bf16[512,1280]{1,0:T(8,128)(2,1)S(1)}, bf16[512,1280]{1,0:T(8,128)(2,1)S(1)}, u32[]{:S(2)}, u32[]{:S(2)}) collective-permute-start(bf16[512,1280]{1,0:T(8,128)(2,1)S(1)} %collective-permute-done.3.refs_5_), channel_id=1, source_target_pairs={{0,16},{16,0},{1,17},{17,1},{2,18},{18,2},{3,19},{19,3},{4,20},{20... | collective-permute-start | bytes 3932168 | tf_op jit(solution)/shard_map/ppermute | solution.py:45
  49.4 7.1 %collective-permute-start.4 = (bf16[512,256]{1,0:T(8,128)(2,1)S(1)}, bf16[512,256]{1,0:T(8,128)(2,1)S(1)}, u32[]{:S(2)}, u32[]{:S(2)}) collective-permute-start(bf16[512,256]{1,0:T(8,128)(2,1)S(1)} %bitcast.14), channel_id=1, source_target_pairs={{0,2},{2,0},{1,3},{3,1},{4,6},{6,4},{5,7},{7,5},{8,10},{10,8},{9,1... | collective-permute-start | bytes 786440 | tf_op jit(solution)/shard_map/ppermute | solution.py:45
  50.0 15.8 %collective-permute-start.10 = (bf16[512,256]{1,0:T(8,128)(2,1)S(1)}, bf16[512,256]{1,0:T(8,128)(2,1)S(1)}, u32[]{:S(2)}, u32[]{:S(2)}) collective-permute-start(bf16[512,256]{1,0:T(8,128)(2,1)S(1)} %bitcast.9), channel_id=1, source_target_pairs={{0,8},{4,12},{8,0},{12,4},{1,9},{5,13},{9,1},{13,5},{2,10},{6,14},... | collective-permute-start | bytes 786440 | tf_op jit(solution)/shard_map/ppermute | solution.py:45
  50.0 15.8 %collective-permute-start.11 = (bf16[512,256]{1,0:T(8,128)(2,1)S(1)}, bf16[512,256]{1,0:T(8,128)(2,1)S(1)}, u32[]{:S(2)}, u32[]{:S(2)}) collective-permute-start(bf16[512,256]{1,0:T(8,128)(2,1)S(1)} %bitcast.10), channel_id=1, source_target_pairs={{0,4},{4,0},{8,12},{12,8},{1,5},{5,1},{9,13},{13,9},{2,6},{6,2},{1... | collective-permute-start | bytes 786440 | tf_op jit(solution)/shard_map/ppermute | solution.py:45
  56.5 17.5 %collective-permute-start.5 = (bf16[512,256]{1,0:T(8,128)(2,1)S(1)}, bf16[512,256]{1,0:T(8,128)(2,1)S(1)}, u32[]{:S(2)}, u32[]{:S(2)}) collective-permute-start(bf16[512,256]{1,0:T(8,128)(2,1)S(1)} %collective-permute-done.4.refs_0_), channel_id=1, source_target_pairs={{0,8},{4,12},{8,0},{12,4},{1,9},{5,13},{9,1},{13,5},{2,10},{6,14},... | collective-permute-start | bytes 786440 | tf_op jit(solution)/shard_map/ppermute | solution.py:45
  56.5 18.2 %collective-permute-start.6 = (bf16[512,256]{1,0:T(8,128)(2,1)S(1)}, bf16[512,256]{1,0:T(8,128)(2,1)S(1)}, u32[]{:S(2)}, u32[]{:S(2)}) collective-permute-start(bf16[512,256]{1,0:T(8,128)(2,1)S(1)} %collective-permute-done.4.refs_0_), channel_id=1, source_target_pairs={{0,4},{4,0},{8,12},{12,8},{1,5},{5,1},{9,13},{13,9},{2,6},{6,2},{1... | collective-permute-start | bytes 786440 | tf_op jit(solution)/shard_map/ppermute | solution.py:45
  65.8 10.9 %collective-permute-start.12 = (bf16[512,256]{1,0:T(8,128)(2,1)S(1)}, bf16[512,256]{1,0:T(8,128)(2,1)S(1)}, u32[]{:S(2)}, u32[]{:S(2)}) collective-permute-start(bf16[512,256]{1,0:T(8,128)(2,1)S(1)} %bitcast.11), channel_id=1, source_target_pairs={{4,8},{8,4},{5,9},{9,5},{6,10},{10,6},{7,11},{11,7},{20,24},{24,20... | collective-permute-start | bytes 786440 | tf_op jit(solution)/shard_map/ppermute | solution.py:45
  66.4 13.8 %collective-permute-start.13 = (bf16[512,256]{1,0:T(8,128)(2,1)S(1)}, bf16[512,256]{1,0:T(8,128)(2,1)S(1)}, u32[]{:S(2)}, u32[]{:S(2)}) collective-permute-start(bf16[512,256]{1,0:T(8,128)(2,1)S(1)} %collective-permute-done.10.refs_2_), channel_id=1, source_target_pairs={{4,0},{8,12},{5,1},{9,13},{6,2},{10,14},{7,3},{11,15},{20,16},{24,... | collective-permute-start | bytes 786440 | tf_op jit(solution)/shard_map/ppermute | solution.py:520
  74.7 8.7 %collective-permute-start.8 = (bf16[512,256]{1,0:T(8,128)(2,1)S(1)}, bf16[512,256]{1,0:T(8,128)(2,1)S(1)}, u32[]{:S(2)}, u32[]{:S(2)}) collective-permute-start(bf16[512,256]{1,0:T(8,128)(2,1)S(1)} %collective-permute-done.4.refs_0_), channel_id=1, source_target_pairs={{4,8},{8,4},{5,9},{9,5},{6,10},{10,6},{7,11},{11,7},{20,24},{24,20... | collective-permute-start | bytes 786440 | tf_op jit(solution)/shard_map/ppermute | solution.py:45
  75.3 10.0 %collective-permute-start.9 = (bf16[512,256]{1,0:T(8,128)(2,1)S(1)}, bf16[512,256]{1,0:T(8,128)(2,1)S(1)}, u32[]{:S(2)}, u32[]{:S(2)}) collective-permute-start(bf16[512,256]{1,0:T(8,128)(2,1)S(1)} %collective-permute-done.5.refs_2_), channel_id=1, source_target_pairs={{4,0},{8,12},{5,1},{9,13},{6,2},{10,14},{7,3},{11,15},{20,16},{24,... | collective-permute-start | bytes 786440 | tf_op jit(solution)/shard_map/ppermute | solution.py:520
  87.2 19.9 %copy-start.4 = (bf16[64,5120]{1,0:T(8,128)(2,1)S(1)}, bf16[64,5120]{1,0:T(8,128)(2,1)}, u32[]{:S(2)}) copy-start(bf16[64,5120]{1,0:T(8,128)(2,1)} %hidden_ref.1) | copy-start | bytes 1966084
  87.2 19.9 %copy-start.5 = (f32[5120]{0:T(1024)S(1)}, f32[5120]{0:T(1024)}, u32[]{:S(2)}) copy-start(f32[5120]{0:T(1024)} %param.13) | copy-start | bytes 61444
  87.2 2.4 %collective-permute-start.18 = (bf16[4,64,640]{2,1,0:T(8,128)(2,1)S(1)}, bf16[4,64,640]{2,1,0:T(8,128)(2,1)S(1)}, u32[]{:S(2)}, u32[]{:S(2)}) collective-permute-start(bf16[4,64,640]{2,1,0:T(8,128)(2,1)S(1)} %get-tuple-element.68), channel_id=1, source_target_pairs={{0,1},{1,0},{2,3},{3,2},{4,5},{5,4},{6,7},{7,6},{8,9},{9,8},{10,11... | collective-permute-start | bytes 983048 | tf_op jit(solution)/shard_map/ppermute | solution.py:45
  89.0 5.7 %collective-permute-start.14 = (bf16[4,64,640]{2,1,0:T(8,128)(2,1)S(1)}, bf16[4,64,640]{2,1,0:T(8,128)(2,1)S(1)}, u32[]{:S(2)}, u32[]{:S(2)}) collective-permute-start(bf16[4,64,640]{2,1,0:T(8,128)(2,1)S(1)} %get-tuple-element.62), channel_id=1, source_target_pairs={{0,1},{1,0},{2,3},{3,2},{4,5},{5,4},{6,7},{7,6},{8,9},{9,8},{10,11... | collective-permute-start | bytes 983048 | tf_op jit(solution)/shard_map/ppermute | solution.py:45
  90.2 7.5 %collective-permute-start.19 = (bf16[64,640]{1,0:T(8,128)(2,1)S(1)}, bf16[64,640]{1,0:T(8,128)(2,1)S(1)}, u32[]{:S(2)}, u32[]{:S(2)}) collective-permute-start(bf16[64,640]{1,0:T(8,128)(2,1)S(1)} %get-tuple-element.70), channel_id=1, source_target_pairs={{0,4},{4,0},{8,12},{12,8},{1,5},{5,1},{9,13},{13,9},{2,6},{6,2},{1... | collective-permute-start | bytes 245768 | tf_op jit(solution)/shard_map/ppermute | solution.py:45
  90.6 10.4 %collective-permute-start.20 = (bf16[64,640]{1,0:T(8,128)(2,1)S(1)}, bf16[64,640]{1,0:T(8,128)(2,1)S(1)}, u32[]{:S(2)}, u32[]{:S(2)}) collective-permute-start(bf16[64,640]{1,0:T(8,128)(2,1)S(1)} %get-tuple-element.71), channel_id=1, source_target_pairs={{0,8},{4,12},{8,0},{12,4},{1,9},{5,13},{9,1},{13,5},{2,10},{6,14},... | collective-permute-start | bytes 245768 | tf_op jit(solution)/shard_map/ppermute | solution.py:45
  92.7 8.3 %collective-permute-start.21 = (bf16[64,640]{1,0:T(8,128)(2,1)S(1)}, bf16[64,640]{1,0:T(8,128)(2,1)S(1)}, u32[]{:S(2)}, u32[]{:S(2)}) collective-permute-start(bf16[64,640]{1,0:T(8,128)(2,1)S(1)} %get-tuple-element.72), channel_id=1, source_target_pairs={{0,12},{4,8},{8,4},{12,0},{1,13},{5,9},{9,5},{13,1},{2,14},{6,10},... | collective-permute-start | bytes 245768 | tf_op jit(solution)/shard_map/ppermute | solution.py:45
  95.3 6.3 %collective-permute-start.15 = (bf16[64,640]{1,0:T(8,128)(2,1)S(1)}, bf16[64,640]{1,0:T(8,128)(2,1)S(1)}, u32[]{:S(2)}, u32[]{:S(2)}) collective-permute-start(bf16[64,640]{1,0:T(8,128)(2,1)S(1)} %get-tuple-element.64), channel_id=1, source_target_pairs={{0,4},{4,0},{8,12},{12,8},{1,5},{5,1},{9,13},{13,9},{2,6},{6,2},{1... | collective-permute-start | bytes 245768 | tf_op jit(solution)/shard_map/ppermute | solution.py:45
  95.4 11.7 %collective-permute-start.16 = (bf16[64,640]{1,0:T(8,128)(2,1)S(1)}, bf16[64,640]{1,0:T(8,128)(2,1)S(1)}, u32[]{:S(2)}, u32[]{:S(2)}) collective-permute-start(bf16[64,640]{1,0:T(8,128)(2,1)S(1)} %get-tuple-element.65), channel_id=1, source_target_pairs={{0,8},{4,12},{8,0},{12,4},{1,9},{5,13},{9,1},{13,5},{2,10},{6,14},... | collective-permute-start | bytes 245768 | tf_op jit(solution)/shard_map/ppermute | solution.py:45
  97.8 9.3 %collective-permute-start.17 = (bf16[64,640]{1,0:T(8,128)(2,1)S(1)}, bf16[64,640]{1,0:T(8,128)(2,1)S(1)}, u32[]{:S(2)}, u32[]{:S(2)}) collective-permute-start(bf16[64,640]{1,0:T(8,128)(2,1)S(1)} %get-tuple-element.66), channel_id=1, source_target_pairs={{0,12},{4,8},{8,4},{12,0},{1,13},{5,9},{9,5},{13,1},{2,14},{6,10},... | collective-permute-start | bytes 245768 | tf_op jit(solution)/shard_map/ppermute | solution.py:45

commit v9 on v8

--- a/solution.py
+++ b/solution.py
@@ -401,86 +401,85 @@
     return [x.reshape(-1, feat) for x in outs]
 
 
-def hold_slots(slots, more, held_ref, where_ref, place):
+def first_kernel(where_ref, *refs):
+    slots, (more, own_ref, fetched_ref, passed_ref, out_ref, held_ref) = refs[:7], refs[7:]
     feat = slots[0].shape[1]
-    for at, slot in enumerate(slots):
-        block = slot[...]
-        if at == len(slots) - 1:
-            block = jnp.where(where_ref[INNER] == 1, block, more[...])
-        lane = place(where_ref[NEAR] ^ at) * feat
-        held_ref[:, pl.ds(pl.multiple_of(lane, HEAD_DIM), feat)] = block
-
-
-def first_kernel(where_ref, *refs):
-    slots, (more, weight_ref, out_ref, held_ref) = refs[:4], refs[4:]
 
     @pl.when(pl.program_id(0) == 0)
     def arrange():
-        hold_slots(slots, more, held_ref, where_ref, lambda at: at)
-
-    out_ref[...] = jnp.dot(held_ref[...], weight_ref[...], preferred_element_type=jnp.float32)
-
-
-def first_product(where, slots, more, weight):
+        for at, slot in enumerate(slots):
+            block = slot[...]
+            if at == 3:
+                block = jnp.where(where_ref[INNER] == 1, block, more[...])
+            place = where_ref[NEAR] ^ (at % 4)
+            if at >= 4:
+                place = 4 + (2 * ((place // 2) ^ where_ref[GRP]) + place % 2)
+            held_ref[:, pl.ds(pl.multiple_of(place * feat, HEAD_DIM), feat)] = block
+        place = where_ref[NEAR] ^ 3
+        place = 4 + (2 * ((place // 2) ^ where_ref[GRP]) + place % 2)
+        held_ref[:, pl.ds(pl.multiple_of(place * feat, HEAD_DIM), feat)] = jnp.zeros(
+            (slots[0].shape[0], feat), jnp.bfloat16
+        )
+
+    depth = 4 * feat
+    acc = jnp.dot(held_ref[:, :depth], own_ref[...], preferred_element_type=jnp.float32)
+    half = depth // 2
+    for at, weight in enumerate((fetched_ref, passed_ref)):
+        acc += jnp.dot(
+            held_ref[:, depth + at * half : depth + (at + 1) * half],
+            weight[...],
+            preferred_element_type=jnp.float32,
+        )
+    out_ref[...] = acc
+
+
+def first_product(where, slots, more, weights):
     rows, feat = slots[0].shape
-    depth, cols = weight.shape
+    cols = weights[0].shape[1]
     wide = cols // 2
     return call(
         first_kernel,
         "first",
         jax.ShapeDtypeStruct((rows, cols), jnp.float32),
         2,
-        [spec((rows, feat))] * 5 + [pl.BlockSpec((depth, wide), lambda i, w: (0, i))],
+        [spec((rows, feat))] * 8
+        + [pl.BlockSpec((x.shape[0], wide), lambda i, w: (0, i)) for x in weights],
         pl.BlockSpec((rows, wide), lambda i, w: (0, i)),
-        [pltpu.VMEM((rows, depth), jnp.bfloat16)],
-    )(where, *slots, *more, weight)
-
-
-def second_kernel(where_ref, *refs):
-    slots, more, weights, (acc_in, keep_ref, send_ref, held_ref, acc_ref) = (
-        refs[:4],
-        refs[4],
-        refs[5:7],
-        refs[7:],
+        [pltpu.VMEM((rows, 8 * feat), jnp.bfloat16)],
+    )(where, *slots, more, *weights)
+
+
+def second_kernel(where_ref, slot, more, fetched_ref, passed_ref, acc_in, keep_ref, send_ref, acc_ref):
+    feat = slot.shape[1]
+    place = where_ref[NEAR] ^ 3
+    rows = pl.ds(pl.multiple_of((place % 2) * feat, HEAD_DIM), feat)
+    weight = jnp.where(
+        (place // 2) == where_ref[GRP], fetched_ref[rows, :], passed_ref[rows, :]
     )
-
-    def place(at):
-        return 2 * ((at // 2) ^ where_ref[GRP]) + at % 2
-
-    hold_slots(slots, more, held_ref, where_ref, place)
-    depth = weights[0].shape[0]
-    acc = acc_in[...]
-    for at, weight in enumerate(weights):
-        acc += jnp.dot(
-            held_ref[:, at * depth : (at + 1) * depth],
-            weight[...],
-            preferred_element_type=jnp.float32,
-        )
+    block = jnp.where(where_ref[INNER] == 1, slot[...], more[...])
+    acc = acc_in[...] + jnp.dot(block, weight, preferred_element_type=jnp.float32)
     acc_ref[...] = acc.reshape(acc_ref.shape)
     for sub, out in enumerate((keep_ref, send_ref)):
         for at in range(4):
             out[at] = acc_ref[where_ref[NEAR] ^ at, where_ref[SUB] ^ sub].astype(jnp.bfloat16)
 
 
-def second_product(where, chunk, slots, more, weights, acc):
-    rows, feat = slots[0].shape
+def second_product(where, slot, more, weights, acc):
+    rows, feat = slot.shape
     depth, cols = weights[0].shape
     wide = cols // 2
-    out = jax.ShapeDtypeStruct((4, rows // 8, wide), jnp.bfloat16)
+    out = jax.ShapeDtypeStruct((4, rows // 8, cols), jnp.bfloat16)
     return call(
         second_kernel,
         "second",
         [out] * 2,
-        1,
-        [spec((rows, feat))] * 5
-        + [pl.BlockSpec((depth, wide), lambda i, w: (0, chunk))] * 2
-        + [pl.BlockSpec((rows, wide), lambda i, w: (0, chunk))],
-        [spec(out.shape)] * 2,
-        [
-            pltpu.VMEM((rows, 2 * depth), jnp.bfloat16),
-            pltpu.VMEM((4, 2, rows // 8, wide), jnp.float32),
-        ],
-    )(where, *slots, *more, *weights, acc)
+        2,
+        [spec((rows, feat))] * 2
+        + [pl.BlockSpec((depth, wide), lambda i, w: (0, i))] * 2
+        + [pl.BlockSpec((rows, wide), lambda i, w: (0, i))],
+        [pl.BlockSpec((4, rows // 8, wide), lambda i, w: (0, 0, i))] * 2,
+        [pltpu.VMEM((4, 2, rows // 8, wide), jnp.float32)],
+    )(where, slot, more, *weights, acc)
 
 
 def add_kernel(where_ref, keep_ref, term_ref, *outs):
@@ -513,45 +512,16 @@
     slots = []
     for at, x in enumerate((mine, other)):
         far, next_to = swap(x, "patch", 4, 2), swap(x, "patch", 4, 1)
-        far, next_to, other, x = lax.optimization_barrier((far, next_to, other, x))
-        if at == 1:
-            far, x, passed = lax.optimization_barrier((far, x, passed))
+        far, next_to, other, x, passed = lax.optimization_barrier((far, next_to, other, x, passed))
         middle = swap(x, "patch", 4, 3, (1, 2))
         ends = lax.ppermute(far, "patch", [(1, 0), (2, 3)])
-        slots.append(([x, next_to, far, middle], [ends]))
-    acc = first_product(where, *slots[0], out_weight)
-    terms = [second_product(where, at, *slots[1], [fetched, passed], acc) for at in range(2)]
-    blocks = []
-    for keep, send in terms:
-        total = add(where, keep, swap(send, "sub", 2, 1))
-        blocks.append([total[0]] + [swap(total[rel], "patch", 4, rel) for rel in range(1, 4)])
-    return mix_columns(where, hidden_in, attn_gate, blocks)
-
-
-def mix_columns_kernel(where_ref, hidden_ref, gate_ref, *refs):
-    blocks, out_ref = refs[:-1], refs[-1]
-    cols = blocks[0].shape[1]
-    for chunk in range(2):
-        for rel in range(4):
-            start = (2 * (where_ref[PATCH] ^ rel) + chunk) * cols
-            lanes = pl.ds(pl.multiple_of(start, HEAD_DIM), cols)
-            mixed = hidden_ref[:, lanes].astype(jnp.float32) + gate_ref[:, lanes] * blocks[
-                4 * chunk + rel
-            ][...].astype(jnp.float32)
-            out_ref[:, lanes] = mixed.astype(jnp.bfloat16)
-
-
-def mix_columns(where, hidden_in, attn_gate, blocks):
-    rows, width = hidden_in.shape
-    flat = [x for chunk in blocks for x in chunk]
-    return call(
-        mix_columns_kernel,
-        "mix",
-        jax.ShapeDtypeStruct((rows, width), jnp.bfloat16),
-        1,
-        [spec((rows, width)), spec((1, width))] + [spec(flat[0].shape)] * len(flat),
-        spec((rows, width)),
-    )(where, hidden_in, attn_gate[None], *flat)
+        slots.append([x, next_to, far, middle, ends])
+    first = [*slots[0][:4], *slots[1][:3]]
+    acc = first_product(where, first, slots[0][4], [out_weight, fetched, passed])
+    keep, send = second_product(where, *slots[1][3:], [fetched, passed], acc)
+    total = add(where, keep, swap(send, "sub", 2, 1))
+    blocks = [total[0]] + [swap(total[rel], "patch", 4, rel) for rel in range(3, 0, -1)]
+    return mix(where, hidden_in, attn_gate, [[blocks[0], *blocks[:0:-1]]])
 
 
 def body(sizes, queries, fresh_kv, cached_kv, exponents, out_weight, hidden_in, attn_gate):

time: 109 us -> 112 us (1.028)
  waiting for transfers between devices: 59.3 us -> 67.3 us
  starting transfers between devices: 28.6 us -> 23.6 us
    ppermute x20 -> x16, waiting for transfers between devices: 53.6 us -> 60.3 us  [swap(): return lax.ppermute(x, axes, pairs)]
    ppermute x20 -> x16, starting transfers between devices: 26 us -> 21 us  [swap(): return lax.ppermute(x, axes, pairs)]
    pallas_call x1, Pallas kernels: 3.06 us -> 5.11 us  [first_product(): call(first_kernel, 'first', jax.ShapeDtypeStruct((rows, cols), jnp.float3...]
    pallas_call x3 -> x2, Pallas kernels: 5.16 us -> 3.69 us  [the longest x1 2.05 us: second_product(): call(second_kernel, 'second', [out] * 2, 2, [spec((rows, feat))] * 2 + [p...]
    ppermute x2, waiting for transfers between devices: 5.64 us -> 7.01 us  [share_tail(): ends = lax.ppermute(far, 'patch', [(1, 0), (2, 3)])]
  transfers between devices with their start and end apart: 22 -> 18, of which waited for: 11 -> 9; matrix products, arithmetic and copies ran while one was open for 0% -> 0% of each run, Pallas kernels for 10% -> 9%
where the time goes in v9:
time: 112 us
  waiting for transfers between devices  67.3 us (60%)
  starting transfers between devices  23.6 us (21%)
  Pallas kernels  18.3 us (16%)
  local copies, waits for them, and re-layouts  2.41 us (2%)
    ppermute x16, waiting for transfers between devices, swap(): return lax.ppermute(x, axes, pairs)  60.3 us
    ppermute x16, starting transfers between devices, swap(): return lax.ppermute(x, axes, pairs)  21 us
    ppermute x2, waiting for transfers between devices, share_tail(): ends = lax.ppermute(far, 'patch', [(1, 0), (2, 3)])  7.01 us
    pallas_call x1, Pallas kernels, first_product(): call(first_kernel, 'first', jax.ShapeDtypeStruct((rows, cols), jnp.float3...  5.11 us
    pallas_call x1, Pallas kernels, attend_halves(): call(attend_halves_kernel, 'attend', [out] * 2, 1, [spec((3, tok, feat))]...  3.79 us
    pallas_call x1, Pallas kernels, pack(): pl.pallas_call(functools.partial(pack_kernel, split, feat // HEAD_DIM), o...  3.72 us
    ppermute x2, starting transfers between devices, share_tail(): ends = lax.ppermute(far, 'patch', [(1, 0), (2, 3)])  2.58 us
  transfers between devices with their start and end apart: 18, of which 9 were waited for; matrix products, arithmetic and copies ran while one was open for 0% of the time, Pallas kernels for 9%

profile of v9, /device:TPU:0, one launch (start us, length us, event | category | flops | bytes accessed | tf_op | source)
XLA Modules:
  0.0 111.8 jit_solution(7091654903920804633)
XLA Ops:
  0.0 3.7 %pack.1 = (bf16[3,256,256]{2,1,0:T(8,128)(2,1)}, bf16[3,256,256]{2,1,0:T(8,128)(2,1)}, bf16[3,256,256]{2,1,0:T(8,128)(2,1)}) custom-call(s32[2,2,8]{2,1,0:T(2,128)} %exps_ref.3, bf16[256,1024]{1,0:T(8,128)(2,1)} %q_ref.3, bf16[2,256,1024]{2,1,0:T(8,128)(2,1)} %fresh_ref.3, bf16[2,1024,1024]{2,1,0:T(8,128)(2,1)} %cached_ref.3), custom_call_target="tpu_custom_call" | custom-call | tf_op jit(solution)/shard_map/pack/pallas_call | solution.py:98
  3.7 0.0 copy-start.7
  3.7 0.0 copy-start.3
  3.8 0.0 copy-start.6
  3.8 0.1 stack.31.where_ref
  3.9 0.0 copy-start.2
  3.9 0.1 constant_dynamic-slice_fusion
  4.0 3.0 %collective-permute-start.3 = (bf16[512,1280]{1,0:T(8,128)(2,1)S(1)}, bf16[512,1280]{1,0:T(8,128)(2,1)S(1)}, u32[]{:S(2)}, u32[]{:S(2)}) collective-permute-start(bf16[512,1280]{1,0:T(8,128)(2,1)S(1)} %constant_dynamic-slice_fusion), channel_id=1, source_target_pairs={{0,2},{2,0},{1,3},{3,1},{4,6},{6,4},{5,7},{7,5},{8,10},{10,8},{9,1... | collective-permute-start | bytes 3932168 | tf_op jit(solution)/shard_map/ppermute | solution.py:45
  7.0 3.6 %collective-permute-start = (bf16[3,256,256]{2,1,0:T(8,128)(2,1)}, bf16[3,256,256]{2,1,0:T(8,128)(2,1)S(1)}, u32[]{:S(2)}, u32[]{:S(2)}) collective-permute-start(bf16[3,256,256]{2,1,0:T(8,128)(2,1)} %get-tuple-element.34), channel_id=1, source_target_pairs={{0,12},{4,8},{8,4},{12,0},{1,13},{5,9},{9,5},{13,1},{2,14},{6,10},... | collective-permute-start | bytes 1179656 | tf_op jit(solution)/shard_map/ppermute | solution.py:45
  10.6 0.0 collective-permute-start.1
  10.6 0.8 collective-permute-start.2
  11.4 2.2 %copy-done = bf16[2,1024,1024]{2,1,0:T(8,128)(2,1)S(1)} copy-done((bf16[2,1024,1024]{2,1,0:T(8,128)(2,1)S(1)}, bf16[2,1024,1024]{2,1,0:T(8,128)(2,1)}, u32[]{:S(2)}) %copy-start) | copy-done | bytes 4194328
  13.6 1.3 %own.1.refs_0_ = bf16[3,256,256]{2,1,0:T(8,128)(2,1)S(1)} custom-call(s32[6]{0:T(128)S(1)} %stack.31.where_ref, s32[2,2,8]{2,1,0:T(2,128)S(1)} %copy-done.6, bf16[256,1024]{1,0:T(8,128)(2,1)S(1)} %copy-done.3, bf16[2,256,1024]{2,1,0:T(8,128)(2,1)S(1)} %copy-done.2, bf16[2,1024,1024]{2,1,0:T(8,128)(2,1)S(1)} %copy-done), custom_call_target="tpu_custom_call" | custom-call | flops 1 | tf_op jit(solution)/shard_map/own/pallas_call | solution.py:132
  14.9 6.3 %collective-permute-done.refs_1_ = bf16[3,256,256]{2,1,0:T(8,128)(2,1)S(1)} collective-permute-done((bf16[3,256,256]{2,1,0:T(8,128)(2,1)}, bf16[3,256,256]{2,1,0:T(8,128)(2,1)S(1)}, u32[]{:S(2)}, u32[]{:S(2)}) %collective-permute-start) | collective-permute-done | bytes 393248 | tf_op jit(solution)/shard_map/ppermute | solution.py:45
  21.1 22.9 %collective-permute-done.1.refs_2_ = bf16[3,256,256]{2,1,0:T(8,128)(2,1)S(1)} collective-permute-done((bf16[3,256,256]{2,1,0:T(8,128)(2,1)S(1)}, bf16[3,256,256]{2,1,0:T(8,128)(2,1)S(1)}, u32[]{:S(2)}, u32[]{:S(2)}) %collective-permute-start.1) | collective-permute-done | bytes 393248 | tf_op jit(solution)/shard_map/ppermute | solution.py:45
  44.1 0.0 collective-permute-done.2.refs_3_
  44.1 0.0 collective-permute-done.3.refs_9_.fetched_ref
  44.1 1.5 %collective-permute-start.9 = (bf16[512,1280]{1,0:T(8,128)(2,1)S(1)}, bf16[512,1280]{1,0:T(8,128)(2,1)S(1)}, u32[]{:S(2)}, u32[]{:S(2)}) collective-permute-start(bf16[512,1280]{1,0:T(8,128)(2,1)S(1)} %collective-permute-done.3.refs_9_.fetched_ref), channel_id=1, source_target_pairs={{0,16},{16,0},{1,17},{17,1},{2,18},{18,2},{3,19},{19,3},{4,20},{20... | collective-permute-start | bytes 3932168 | tf_op jit(solution)/shard_map/ppermute | solution.py:45
  45.6 3.8 %attend.1 = (bf16[4,128,256]{2,1,0:T(8,128)(2,1)S(1)}, bf16[4,128,256]{2,1,0:T(8,128)(2,1)S(1)}) custom-call(s32[6]{0:T(128)S(1)} %stack.31.where_ref, bf16[3,256,256]{2,1,0:T(8,128)(2,1)S(1)} %own.1.refs_0_, bf16[3,256,256]{2,1,0:T(8,128)(2,1)S(1)} %collective-permute-done.refs_1_, bf16[3,256,256]{2,1,0:T(8,128)(2,1)S(1)} %collective-permute-done.1.refs_2_, ...), custom_call_target="tpu_custom_call" | custom-call | flops 1 | tf_op jit(solution)/shard_map/attend/pallas_call | solution.py:393
  49.4 0.6 collective-permute-start.4
  50.0 3.0 %collective-permute-start.8 = (bf16[512,256]{1,0:T(8,128)(2,1)S(1)}, bf16[512,256]{1,0:T(8,128)(2,1)S(1)}, u32[]{:S(2)}, u32[]{:S(2)}) collective-permute-start(bf16[512,256]{1,0:T(8,128)(2,1)S(1)} %bitcast.10), channel_id=1, source_target_pairs={{0,4},{4,0},{8,12},{12,8},{1,5},{5,1},{9,13},{13,9},{2,6},{6,2},{1... | collective-permute-start | bytes 786440 | tf_op jit(solution)/shard_map/ppermute | solution.py:45
  53.0 3.5 %collective-permute-done.4.refs_4_ = bf16[512,256]{1,0:T(8,128)(2,1)S(1)} collective-permute-done((bf16[512,256]{1,0:T(8,128)(2,1)S(1)}, bf16[512,256]{1,0:T(8,128)(2,1)S(1)}, u32[]{:S(2)}, u32[]{:S(2)}) %collective-permute-start.4) | collective-permute-done | bytes 262176 | tf_op jit(solution)/shard_map/ppermute | solution.py:45
  56.5 2.6 %collective-permute-start.6 = (bf16[512,256]{1,0:T(8,128)(2,1)S(1)}, bf16[512,256]{1,0:T(8,128)(2,1)S(1)}, u32[]{:S(2)}, u32[]{:S(2)}) collective-permute-start(bf16[512,256]{1,0:T(8,128)(2,1)S(1)} %collective-permute-done.4.refs_4_), channel_id=1, source_target_pairs={{0,4},{4,0},{8,12},{12,8},{1,5},{5,1},{9,13},{13,9},{2,6},{6,2},{1... | collective-permute-start | bytes 786440 | tf_op jit(solution)/shard_map/ppermute | solution.py:45
  59.1 6.7 %collective-permute-done.7.refs_2_ = bf16[512,256]{1,0:T(8,128)(2,1)S(1)} collective-permute-done((bf16[512,256]{1,0:T(8,128)(2,1)S(1)}, bf16[512,256]{1,0:T(8,128)(2,1)S(1)}, u32[]{:S(2)}, u32[]{:S(2)}) %collective-permute-start.7) | collective-permute-done | bytes 262176 | tf_op jit(solution)/shard_map/ppermute | solution.py:45
  65.8 0.0 collective-permute-done.8.refs_1_
  65.8 8.1 %collective-permute-done.9.refs_10_.passed_ref = bf16[512,1280]{1,0:T(8,128)(2,1)S(1)} collective-permute-done((bf16[512,1280]{1,0:T(8,128)(2,1)S(1)}, bf16[512,1280]{1,0:T(8,128)(2,1)S(1)}, u32[]{:S(2)}, u32[]{:S(2)}) %collective-permute-start.9) | collective-permute-done | bytes 1310752 | tf_op jit(solution)/shard_map/ppermute | solution.py:45
  73.9 0.7 collective-permute-start.12
  74.5 1.3 %collective-permute-start.13 = (bf16[512,256]{1,0:T(8,128)(2,1)S(1)}, bf16[512,256]{1,0:T(8,128)(2,1)S(1)}, u32[]{:S(2)}, u32[]{:S(2)}) collective-permute-start(bf16[512,256]{1,0:T(8,128)(2,1)S(1)} %collective-permute-done.7.refs_2_), channel_id=1, source_target_pairs={{4,0},{8,12},{5,1},{9,13},{6,2},{10,14},{7,3},{11,15},{20,16},{24,... | collective-permute-start | bytes 786440 | tf_op jit(solution)/shard_map/ppermute | solution.py:517
  75.8 0.0 collective-permute-done.5.refs_6_
  75.9 0.7 collective-permute-start.10
  76.5 1.3 %collective-permute-start.11 = (bf16[512,256]{1,0:T(8,128)(2,1)S(1)}, bf16[512,256]{1,0:T(8,128)(2,1)S(1)}, u32[]{:S(2)}, u32[]{:S(2)}) collective-permute-start(bf16[512,256]{1,0:T(8,128)(2,1)S(1)} %collective-permute-done.5.refs_6_), channel_id=1, source_target_pairs={{4,0},{8,12},{5,1},{9,13},{6,2},{10,14},{7,3},{11,15},{20,16},{24,... | collective-permute-start | bytes 786440 | tf_op jit(solution)/shard_map/ppermute | solution.py:517
  77.8 0.0 collective-permute-done.12.refs_3_
  77.9 7.0 %collective-permute-done.13.refs_7_ = bf16[512,256]{1,0:T(8,128)(2,1)S(1)} collective-permute-done((bf16[512,256]{1,0:T(8,128)(2,1)S(1)}, bf16[512,256]{1,0:T(8,128)(2,1)S(1)}, u32[]{:S(2)}, u32[]{:S(2)}) %collective-permute-start.13) | collective-permute-done | bytes 262176 | tf_op jit(solution)/shard_map/ppermute | solution.py:517
  84.9 5.1 %first.1.acc_in = f32[512,1280]{1,0:T(8,128)S(1)} custom-call(s32[6]{0:T(128)S(1)} %stack.31.where_ref, bf16[512,256]{1,0:T(8,128)(2,1)S(1)} %bitcast.12, bf16[512,256]{1,0:T(8,128)(2,1)S(1)} %collective-permute-done.8.refs_1_, bf16[512,256]{1,0:T(8,128)(2,1)S(1)} %collective-permute-done.7.refs_2_, bf16[512,256]{1,0:T(8,128)(2,1)S(1)} %collective-permute-done.12.refs_3_, ...), custom_call_target="tpu_custom_call" | custom-call | flops 1 | tf_op jit(solution)/shard_map/first/pallas_call | solution.py:440
  90.0 0.0 copy-start.4
  90.0 0.0 copy-start.5
  90.0 0.0 collective-permute-done.11.more
  90.0 2.1 %second.1 = (bf16[4,64,1280]{2,1,0:T(8,128)(2,1)S(1)}, bf16[4,64,1280]{2,1,0:T(8,128)(2,1)S(1)}) custom-call(s32[6]{0:T(128)S(1)} %stack.31.where_ref, bf16[512,256]{1,0:T(8,128)(2,1)S(1)} %collective-permute-done.10.slot, bf16[512,256]{1,0:T(8,128)(2,1)S(1)} %collective-permute-done.11.more, ...), custom_call_target="tpu_custom_call" | custom-call | flops 1 | tf_op jit(solution)/shard_map/second/pallas_call | solution.py:472
  92.1 0.1 collective-permute-start.14
  92.2 2.1 %collective-permute-done.14.term_ref = bf16[4,64,1280]{2,1,0:T(8,128)(2,1)S(1)} collective-permute-done((bf16[4,64,1280]{2,1,0:T(8,128)(2,1)S(1)}, bf16[4,64,1280]{2,1,0:T(8,128)(2,1)S(1)}, u32[]{:S(2)}, u32[]{:S(2)}) %collective-permute-start.14) | collective-permute-done | bytes 655392 | tf_op jit(solution)/shard_map/ppermute | solution.py:45
  94.2 0.7 add.10
  94.9 0.1 collective-permute-start.15
  95.0 2.2 %collective-permute-start.16 = (bf16[64,1280]{1,0:T(8,128)(2,1)S(1)}, bf16[64,1280]{1,0:T(8,128)(2,1)S(1)}, u32[]{:S(2)}, u32[]{:S(2)}) collective-permute-start(bf16[64,1280]{1,0:T(8,128)(2,1)S(1)} %get-tuple-element.57), channel_id=1, source_target_pairs={{0,8},{4,12},{8,0},{12,4},{1,9},{5,13},{9,1},{13,5},{2,10},{6,14},... | collective-permute-start | bytes 491528 | tf_op jit(solution)/shard_map/ppermute | solution.py:45
  97.2 2.2 %collective-permute-start.17 = (bf16[64,1280]{1,0:T(8,128)(2,1)S(1)}, bf16[64,1280]{1,0:T(8,128)(2,1)S(1)}, u32[]{:S(2)}, u32[]{:S(2)}) collective-permute-start(bf16[64,1280]{1,0:T(8,128)(2,1)S(1)} %get-tuple-element.58), channel_id=1, source_target_pairs={{0,12},{4,8},{8,4},{12,0},{1,13},{5,9},{9,5},{13,1},{2,14},{6,10},... | collective-permute-start | bytes 491528 | tf_op jit(solution)/shard_map/ppermute | solution.py:45
  99.4 4.3 %collective-permute-done.15.refs_1_ = bf16[64,1280]{1,0:T(8,128)(2,1)S(1)} collective-permute-done((bf16[64,1280]{1,0:T(8,128)(2,1)S(1)}, bf16[64,1280]{1,0:T(8,128)(2,1)S(1)}, u32[]{:S(2)}, u32[]{:S(2)}) %collective-permute-start.15) | collective-permute-done | bytes 163872 | tf_op jit(solution)/shard_map/ppermute | solution.py:45
  103.7 6.4 %collective-permute-done.16.refs_2_ = bf16[64,1280]{1,0:T(8,128)(2,1)S(1)} collective-permute-done((bf16[64,1280]{1,0:T(8,128)(2,1)S(1)}, bf16[64,1280]{1,0:T(8,128)(2,1)S(1)}, u32[]{:S(2)}, u32[]{:S(2)}) %collective-permute-start.16) | collective-permute-done | bytes 163872 | tf_op jit(solution)/shard_map/ppermute | solution.py:45
  110.1 0.0 collective-permute-done.17.refs_3_
  110.1 1.6 %mix.1 = bf16[64,5120]{1,0:T(8,128)(2,1)} custom-call(s32[6]{0:T(128)S(1)} %stack.31.where_ref, bf16[64,5120]{1,0:T(8,128)(2,1)S(1)} %copy-done.4, f32[1,5120]{1,0:T(1,128)S(1)} %bitcast.13, bf16[64,1280]{1,0:T(8,128)(2,1)S(1)} %get-tuple-element.55.refs_0_, bf16[64,1280]{1,0:T(8,128)(2,1)S(1)} %collective-permute-done.15.refs_1_, ...), custom_call_target="tpu_custom_call" | custom-call | flops 1 | tf_op jit(solution)/shard_map/mix/pallas_call | solution.py:262
  (15 shorter events, 0.0 us)
Async XLA Ops:
  0.0 3.9 %copy-start.1 = (bf16[1024,1280]{1,0:T(8,128)(2,1)S(1)}, bf16[1024,1280]{1,0:T(8,128)(2,1)}, u32[]{:S(2)}) copy-start(bf16[1024,1280]{1,0:T(8,128)(2,1)} %refs_8_) | copy-start | bytes 7864324
  3.7 6.9 %copy-start.7 = (bf16[3,256,256]{2,1,0:T(8,128)(2,1)S(1)}, bf16[3,256,256]{2,1,0:T(8,128)(2,1)}, u32[]{:S(2)}) copy-start(bf16[3,256,256]{2,1,0:T(8,128)(2,1)} %get-tuple-element.32) | copy-start | bytes 1179652
  3.7 7.6 %copy-start.3 = (bf16[256,1024]{1,0:T(8,128)(2,1)S(1)}, bf16[256,1024]{1,0:T(8,128)(2,1)}, u32[]{:S(2)}) copy-start(bf16[256,1024]{1,0:T(8,128)(2,1)} %q_ref.3) | copy-start | bytes 1572868
  3.8 7.6 %copy-start.6 = (s32[2,2,8]{2,1,0:T(2,128)S(1)}, s32[2,2,8]{2,1,0:T(2,128)}, u32[]{:S(2)}) copy-start(s32[2,2,8]{2,1,0:T(2,128)} %exps_ref.3) | copy-start | bytes 388
  3.9 6.7 %copy-start.8 = (bf16[3,256,256]{2,1,0:T(8,128)(2,1)S(1)}, bf16[3,256,256]{2,1,0:T(8,128)(2,1)}, u32[]{:S(2)}) copy-start(bf16[3,256,256]{2,1,0:T(8,128)(2,1)} %get-tuple-element.33) | copy-start | bytes 1179652
  3.9 7.5 %copy-start.2 = (bf16[2,256,1024]{2,1,0:T(8,128)(2,1)S(1)}, bf16[2,256,1024]{2,1,0:T(8,128)(2,1)}, u32[]{:S(2)}) copy-start(bf16[2,256,1024]{2,1,0:T(8,128)(2,1)} %fresh_ref.3) | copy-start | bytes 3145732
  4.0 40.1 %collective-permute-start.3 = (bf16[512,1280]{1,0:T(8,128)(2,1)S(1)}, bf16[512,1280]{1,0:T(8,128)(2,1)S(1)}, u32[]{:S(2)}, u32[]{:S(2)}) collective-permute-start(bf16[512,1280]{1,0:T(8,128)(2,1)S(1)} %constant_dynamic-slice_fusion), channel_id=1, source_target_pairs={{0,2},{2,0},{1,3},{3,1},{4,6},{6,4},{5,7},{7,5},{8,10},{10,8},{9,1... | collective-permute-start | bytes 3932168 | tf_op jit(solution)/shard_map/ppermute | solution.py:45
  7.0 14.1 %collective-permute-start = (bf16[3,256,256]{2,1,0:T(8,128)(2,1)}, bf16[3,256,256]{2,1,0:T(8,128)(2,1)S(1)}, u32[]{:S(2)}, u32[]{:S(2)}) collective-permute-start(bf16[3,256,256]{2,1,0:T(8,128)(2,1)} %get-tuple-element.34), channel_id=1, source_target_pairs={{0,12},{4,8},{8,4},{12,0},{1,13},{5,9},{9,5},{13,1},{2,14},{6,10},... | collective-permute-start | bytes 1179656 | tf_op jit(solution)/shard_map/ppermute | solution.py:45
  10.6 33.5 %collective-permute-start.1 = (bf16[3,256,256]{2,1,0:T(8,128)(2,1)S(1)}, bf16[3,256,256]{2,1,0:T(8,128)(2,1)S(1)}, u32[]{:S(2)}, u32[]{:S(2)}) collective-permute-start(bf16[3,256,256]{2,1,0:T(8,128)(2,1)S(1)} %copy-done.8), channel_id=1, source_target_pairs={{0,8},{4,12},{8,0},{12,4},{1,9},{5,13},{9,1},{13,5},{2,10},{6,14},... | collective-permute-start | bytes 1179656 | tf_op jit(solution)/shard_map/ppermute | solution.py:45
  10.6 33.5 %collective-permute-start.2 = (bf16[3,256,256]{2,1,0:T(8,128)(2,1)S(1)}, bf16[3,256,256]{2,1,0:T(8,128)(2,1)S(1)}, u32[]{:S(2)}, u32[]{:S(2)}) collective-permute-start(bf16[3,256,256]{2,1,0:T(8,128)(2,1)S(1)} %copy-done.7), channel_id=1, source_target_pairs={{0,4},{4,0},{8,12},{12,8},{1,5},{5,1},{9,13},{13,9},{2,6},{6,2},{1... | collective-permute-start | bytes 1179656 | tf_op jit(solution)/shard_map/ppermute | solution.py:45
  11.4 2.2 %copy-start = (bf16[2,1024,1024]{2,1,0:T(8,128)(2,1)S(1)}, bf16[2,1024,1024]{2,1,0:T(8,128)(2,1)}, u32[]{:S(2)}) copy-start(bf16[2,1024,1024]{2,1,0:T(8,128)(2,1)} %cached_ref.3) | copy-start | bytes 12582916
  44.1 29.8 %collective-permute-start.9 = (bf16[512,1280]{1,0:T(8,128)(2,1)S(1)}, bf16[512,1280]{1,0:T(8,128)(2,1)S(1)}, u32[]{:S(2)}, u32[]{:S(2)}) collective-permute-start(bf16[512,1280]{1,0:T(8,128)(2,1)S(1)} %collective-permute-done.3.refs_9_.fetched_ref), channel_id=1, source_target_pairs={{0,16},{16,0},{1,17},{17,1},{2,18},{18,2},{3,19},{19,3},{4,20},{20... | collective-permute-start | bytes 3932168 | tf_op jit(solution)/shard_map/ppermute | solution.py:45
  49.4 7.1 %collective-permute-start.4 = (bf16[512,256]{1,0:T(8,128)(2,1)S(1)}, bf16[512,256]{1,0:T(8,128)(2,1)S(1)}, u32[]{:S(2)}, u32[]{:S(2)}) collective-permute-start(bf16[512,256]{1,0:T(8,128)(2,1)S(1)} %bitcast.14), channel_id=1, source_target_pairs={{0,2},{2,0},{1,3},{3,1},{4,6},{6,4},{5,7},{7,5},{8,10},{10,8},{9,1... | collective-permute-start | bytes 786440 | tf_op jit(solution)/shard_map/ppermute | solution.py:45
  50.0 15.8 %collective-permute-start.7 = (bf16[512,256]{1,0:T(8,128)(2,1)S(1)}, bf16[512,256]{1,0:T(8,128)(2,1)S(1)}, u32[]{:S(2)}, u32[]{:S(2)}) collective-permute-start(bf16[512,256]{1,0:T(8,128)(2,1)S(1)} %bitcast.9), channel_id=1, source_target_pairs={{0,8},{4,12},{8,0},{12,4},{1,9},{5,13},{9,1},{13,5},{2,10},{6,14},... | collective-permute-start | bytes 786440 | tf_op jit(solution)/shard_map/ppermute | solution.py:45
  50.0 15.8 %collective-permute-start.8 = (bf16[512,256]{1,0:T(8,128)(2,1)S(1)}, bf16[512,256]{1,0:T(8,128)(2,1)S(1)}, u32[]{:S(2)}, u32[]{:S(2)}) collective-permute-start(bf16[512,256]{1,0:T(8,128)(2,1)S(1)} %bitcast.10), channel_id=1, source_target_pairs={{0,4},{4,0},{8,12},{12,8},{1,5},{5,1},{9,13},{13,9},{2,6},{6,2},{1... | collective-permute-start | bytes 786440 | tf_op jit(solution)/shard_map/ppermute | solution.py:45
  56.5 19.3 %collective-permute-start.5 = (bf16[512,256]{1,0:T(8,128)(2,1)S(1)}, bf16[512,256]{1,0:T(8,128)(2,1)S(1)}, u32[]{:S(2)}, u32[]{:S(2)}) collective-permute-start(bf16[512,256]{1,0:T(8,128)(2,1)S(1)} %collective-permute-done.4.refs_4_), channel_id=1, source_target_pairs={{0,8},{4,12},{8,0},{12,4},{1,9},{5,13},{9,1},{13,5},{2,10},{6,14},... | collective-permute-start | bytes 786440 | tf_op jit(solution)/shard_map/ppermute | solution.py:45
  56.5 19.3 %collective-permute-start.6 = (bf16[512,256]{1,0:T(8,128)(2,1)S(1)}, bf16[512,256]{1,0:T(8,128)(2,1)S(1)}, u32[]{:S(2)}, u32[]{:S(2)}) collective-permute-start(bf16[512,256]{1,0:T(8,128)(2,1)S(1)} %collective-permute-done.4.refs_4_), channel_id=1, source_target_pairs={{0,4},{4,0},{8,12},{12,8},{1,5},{5,1},{9,13},{13,9},{2,6},{6,2},{1... | collective-permute-start | bytes 786440 | tf_op jit(solution)/shard_map/ppermute | solution.py:45
  73.9 4.0 %collective-permute-start.12 = (bf16[512,256]{1,0:T(8,128)(2,1)S(1)}, bf16[512,256]{1,0:T(8,128)(2,1)S(1)}, u32[]{:S(2)}, u32[]{:S(2)}) collective-permute-start(bf16[512,256]{1,0:T(8,128)(2,1)S(1)} %bitcast.11), channel_id=1, source_target_pairs={{4,8},{8,4},{5,9},{9,5},{6,10},{10,6},{7,11},{11,7},{20,24},{24,20... | collective-permute-start | bytes 786440 | tf_op jit(solution)/shard_map/ppermute | solution.py:45
  74.5 10.3 %collective-permute-start.13 = (bf16[512,256]{1,0:T(8,128)(2,1)S(1)}, bf16[512,256]{1,0:T(8,128)(2,1)S(1)}, u32[]{:S(2)}, u32[]{:S(2)}) collective-permute-start(bf16[512,256]{1,0:T(8,128)(2,1)S(1)} %collective-permute-done.7.refs_2_), channel_id=1, source_target_pairs={{4,0},{8,12},{5,1},{9,13},{6,2},{10,14},{7,3},{11,15},{20,16},{24,... | collective-permute-start | bytes 786440 | tf_op jit(solution)/shard_map/ppermute | solution.py:517
  75.9 14.2 %collective-permute-start.10 = (bf16[512,256]{1,0:T(8,128)(2,1)S(1)}, bf16[512,256]{1,0:T(8,128)(2,1)S(1)}, u32[]{:S(2)}, u32[]{:S(2)}) collective-permute-start(bf16[512,256]{1,0:T(8,128)(2,1)S(1)} %collective-permute-done.4.refs_4_), channel_id=1, source_target_pairs={{4,8},{8,4},{5,9},{9,5},{6,10},{10,6},{7,11},{11,7},{20,24},{24,20... | collective-permute-start | bytes 786440 | tf_op jit(solution)/shard_map/ppermute | solution.py:45
  76.5 13.5 %collective-permute-start.11 = (bf16[512,256]{1,0:T(8,128)(2,1)S(1)}, bf16[512,256]{1,0:T(8,128)(2,1)S(1)}, u32[]{:S(2)}, u32[]{:S(2)}) collective-permute-start(bf16[512,256]{1,0:T(8,128)(2,1)S(1)} %collective-permute-done.5.refs_6_), channel_id=1, source_target_pairs={{4,0},{8,12},{5,1},{9,13},{6,2},{10,14},{7,3},{11,15},{20,16},{24,... | collective-permute-start | bytes 786440 | tf_op jit(solution)/shard_map/ppermute | solution.py:517
  90.0 20.1 %copy-start.4 = (bf16[64,5120]{1,0:T(8,128)(2,1)S(1)}, bf16[64,5120]{1,0:T(8,128)(2,1)}, u32[]{:S(2)}) copy-start(bf16[64,5120]{1,0:T(8,128)(2,1)} %hidden_ref.1) | copy-start | bytes 1966084
  90.0 20.1 %copy-start.5 = (f32[5120]{0:T(1024)S(1)}, f32[5120]{0:T(1024)}, u32[]{:S(2)}) copy-start(f32[5120]{0:T(1024)} %param.13) | copy-start | bytes 61444
  92.1 2.2 %collective-permute-start.14 = (bf16[4,64,1280]{2,1,0:T(8,128)(2,1)S(1)}, bf16[4,64,1280]{2,1,0:T(8,128)(2,1)S(1)}, u32[]{:S(2)}, u32[]{:S(2)}) collective-permute-start(bf16[4,64,1280]{2,1,0:T(8,128)(2,1)S(1)} %get-tuple-element.54), channel_id=1, source_target_pairs={{0,1},{1,0},{2,3},{3,2},{4,5},{5,4},{6,7},{7,6},{8,9},{9,8},{10,11... | collective-permute-start | bytes 1966088 | tf_op jit(solution)/shard_map/ppermute | solution.py:45
  94.9 8.8 %collective-permute-start.15 = (bf16[64,1280]{1,0:T(8,128)(2,1)S(1)}, bf16[64,1280]{1,0:T(8,128)(2,1)S(1)}, u32[]{:S(2)}, u32[]{:S(2)}) collective-permute-start(bf16[64,1280]{1,0:T(8,128)(2,1)S(1)} %get-tuple-element.56), channel_id=1, source_target_pairs={{0,4},{4,0},{8,12},{12,8},{1,5},{5,1},{9,13},{13,9},{2,6},{6,2},{1... | collective-permute-start | bytes 491528 | tf_op jit(solution)/shard_map/ppermute | solution.py:45
  95.0 15.1 %collective-permute-start.16 = (bf16[64,1280]{1,0:T(8,128)(2,1)S(1)}, bf16[64,1280]{1,0:T(8,128)(2,1)S(1)}, u32[]{:S(2)}, u32[]{:S(2)}) collective-permute-start(bf16[64,1280]{1,0:T(8,128)(2,1)S(1)} %get-tuple-element.57), channel_id=1, source_target_pairs={{0,8},{4,12},{8,0},{12,4},{1,9},{5,13},{9,1},{13,5},{2,10},{6,14},... | collective-permute-start | bytes 491528 | tf_op jit(solution)/shard_map/ppermute | solution.py:45
  97.2 12.9 %collective-permute-start.17 = (bf16[64,1280]{1,0:T(8,128)(2,1)S(1)}, bf16[64,1280]{1,0:T(8,128)(2,1)S(1)}, u32[]{:S(2)}, u32[]{:S(2)}) collective-permute-start(bf16[64,1280]{1,0:T(8,128)(2,1)S(1)} %get-tuple-element.58), channel_id=1, source_target_pairs={{0,12},{4,8},{8,4},{12,0},{1,13},{5,9},{9,5},{13,1},{2,14},{6,10},... | collective-permute-start | bytes 491528 | tf_op jit(solution)/shard_map/ppermute | solution.py:45

commit v10 on v9

--- a/solution.py
+++ b/solution.py
@@ -236,15 +236,15 @@
     )(where, *slots, *more, weight)
 
 
-def mix_kernel(n_patch, where_ref, hidden_ref, gate_ref, *refs):
+def mix_kernel(rels, where_ref, hidden_ref, gate_ref, *refs):
     blocks, out_ref = refs[:-1], refs[-1]
     piece, cols = blocks[0].shape
-    for part in range(len(blocks) // n_patch):
+    for part in range(len(blocks) // len(rels)):
         rows = pl.ds(part * piece, piece)
-        for rel in range(n_patch):
+        for at, rel in enumerate(rels):
             lanes = pl.ds(pl.multiple_of((where_ref[PATCH] ^ rel) * cols, HEAD_DIM), cols)
             mixed = hidden_ref[rows, lanes].astype(jnp.float32) + gate_ref[:, lanes] * blocks[
-                part * n_patch + rel
+                part * len(rels) + at
             ][...].astype(jnp.float32)
             out_ref[rows, lanes] = mixed.astype(jnp.bfloat16)
 
@@ -258,9 +258,10 @@
         order = order[where[PATCH] ^ jnp.arange(n_patch)]
         projected = order.transpose(1, 0, 2).reshape(rows, width).astype(jnp.float32)
         return (hidden_in.astype(jnp.float32) + attn_gate * projected).astype(jnp.bfloat16)
-    flat = [x for part in blocks for x in part]
-    return call(
-        functools.partial(mix_kernel, n_patch),
+    rels = [0, *range(n_patch - 1, 0, -1)]
+    flat = [part[rel] for part in blocks for rel in rels]
+    return call(
+        functools.partial(mix_kernel, rels),
         "mix",
         jax.ShapeDtypeStruct((rows, width), jnp.bfloat16),
         1,
@@ -512,7 +513,9 @@
     slots = []
     for at, x in enumerate((mine, other)):
         far, next_to = swap(x, "patch", 4, 2), swap(x, "patch", 4, 1)
-        far, next_to, other, x, passed = lax.optimization_barrier((far, next_to, other, x, passed))
+        far, next_to, other, x = lax.optimization_barrier((far, next_to, other, x))
+        if at == 1:
+            far, x, passed = lax.optimization_barrier((far, x, passed))
         middle = swap(x, "patch", 4, 3, (1, 2))
         ends = lax.ppermute(far, "patch", [(1, 0), (2, 3)])
         slots.append([x, next_to, far, middle, ends])

time: 112 us -> 109 us (0.973)
  waiting for transfers between devices: 67.3 us -> 64.1 us
    ppermute x2, waiting for transfers between devices: 7.01 us -> 3.63 us  [share_tail(): ends = lax.ppermute(far, 'patch', [(1, 0), (2, 3)])]
  transfers between devices with their start and end apart: 18 -> 18, of which waited for: 9 -> 10; matrix products, arithmetic and copies ran while one was open for 0% -> 0% of each run, Pallas kernels for 9% -> 9%
where the time goes in v10:
time: 109 us
  waiting for transfers between devices  64.1 us (59%)
  starting transfers between devices  23.6 us (22%)
  Pallas kernels  18.3 us (17%)
  local copies, waits for them, and re-layouts  2.41 us (2%)
    ppermute x16, waiting for transfers between devices, swap(): return lax.ppermute(x, axes, pairs)  60.4 us
    ppermute x16, starting transfers between devices, swap(): return lax.ppermute(x, axes, pairs)  21 us
    pallas_call x1, Pallas kernels, first_product(): call(first_kernel, 'first', jax.ShapeDtypeStruct((rows, cols), jnp.float3...  5.11 us
    pallas_call x1, Pallas kernels, attend_halves(): call(attend_halves_kernel, 'attend', [out] * 2, 1, [spec((3, tok, feat))]...  3.79 us
    pallas_call x1, Pallas kernels, pack(): pl.pallas_call(functools.partial(pack_kernel, split, feat // HEAD_DIM), o...  3.72 us
    ppermute x2, waiting for transfers between devices, share_tail(): ends = lax.ppermute(far, 'patch', [(1, 0), (2, 3)])  3.63 us
    ppermute x2, starting transfers between devices, share_tail(): ends = lax.ppermute(far, 'patch', [(1, 0), (2, 3)])  2.58 us
    unnamed x18, local copies, waits for them, and re-layouts  2.23 us
  transfers between devices with their start and end apart: 18, of which 10 were waited for; matrix products, arithmetic and copies ran while one was open for 0% of the time, Pallas kernels for 9%

profile of v10, /device:TPU:0, one launch (start us, length us, event | category | flops | bytes accessed | tf_op | source)
XLA Modules:
  0.0 108.5 jit_solution(16895706438493811774)
XLA Ops:
  0.0 3.7 %pack.1 = (bf16[3,256,256]{2,1,0:T(8,128)(2,1)}, bf16[3,256,256]{2,1,0:T(8,128)(2,1)}, bf16[3,256,256]{2,1,0:T(8,128)(2,1)}) custom-call(s32[2,2,8]{2,1,0:T(2,128)} %exps_ref.3, bf16[256,1024]{1,0:T(8,128)(2,1)} %q_ref.3, bf16[2,256,1024]{2,1,0:T(8,128)(2,1)} %fresh_ref.3, bf16[2,1024,1024]{2,1,0:T(8,128)(2,1)} %cached_ref.3), custom_call_target="tpu_custom_call" | custom-call | tf_op jit(solution)/shard_map/pack/pallas_call | solution.py:98
  3.7 0.0 copy-start.7
  3.7 0.0 copy-start.3
  3.8 0.0 copy-start.6
  3.8 0.1 stack.31.where_ref
  3.9 0.0 copy-start.2
  3.9 0.1 constant_dynamic-slice_fusion
  4.0 3.0 %collective-permute-start.3 = (bf16[512,1280]{1,0:T(8,128)(2,1)S(1)}, bf16[512,1280]{1,0:T(8,128)(2,1)S(1)}, u32[]{:S(2)}, u32[]{:S(2)}) collective-permute-start(bf16[512,1280]{1,0:T(8,128)(2,1)S(1)} %constant_dynamic-slice_fusion), channel_id=1, source_target_pairs={{0,2},{2,0},{1,3},{3,1},{4,6},{6,4},{5,7},{7,5},{8,10},{10,8},{9,1... | collective-permute-start | bytes 3932168 | tf_op jit(solution)/shard_map/ppermute | solution.py:45
  7.0 3.6 %collective-permute-start = (bf16[3,256,256]{2,1,0:T(8,128)(2,1)}, bf16[3,256,256]{2,1,0:T(8,128)(2,1)S(1)}, u32[]{:S(2)}, u32[]{:S(2)}) collective-permute-start(bf16[3,256,256]{2,1,0:T(8,128)(2,1)} %get-tuple-element.35), channel_id=1, source_target_pairs={{0,12},{4,8},{8,4},{12,0},{1,13},{5,9},{9,5},{13,1},{2,14},{6,10},... | collective-permute-start | bytes 1179656 | tf_op jit(solution)/shard_map/ppermute | solution.py:45
  10.6 0.0 collective-permute-start.1
  10.6 0.8 collective-permute-start.2
  11.4 2.2 %copy-done = bf16[2,1024,1024]{2,1,0:T(8,128)(2,1)S(1)} copy-done((bf16[2,1024,1024]{2,1,0:T(8,128)(2,1)S(1)}, bf16[2,1024,1024]{2,1,0:T(8,128)(2,1)}, u32[]{:S(2)}) %copy-start) | copy-done | bytes 4194328
  13.6 1.3 %own.1.refs_0_ = bf16[3,256,256]{2,1,0:T(8,128)(2,1)S(1)} custom-call(s32[6]{0:T(128)S(1)} %stack.31.where_ref, s32[2,2,8]{2,1,0:T(2,128)S(1)} %copy-done.6, bf16[256,1024]{1,0:T(8,128)(2,1)S(1)} %copy-done.3, bf16[2,256,1024]{2,1,0:T(8,128)(2,1)S(1)} %copy-done.2, bf16[2,1024,1024]{2,1,0:T(8,128)(2,1)S(1)} %copy-done), custom_call_target="tpu_custom_call" | custom-call | flops 1 | tf_op jit(solution)/shard_map/own/pallas_call | solution.py:132
  14.9 6.3 %collective-permute-done.refs_1_ = bf16[3,256,256]{2,1,0:T(8,128)(2,1)S(1)} collective-permute-done((bf16[3,256,256]{2,1,0:T(8,128)(2,1)}, bf16[3,256,256]{2,1,0:T(8,128)(2,1)S(1)}, u32[]{:S(2)}, u32[]{:S(2)}) %collective-permute-start) | collective-permute-done | bytes 393248 | tf_op jit(solution)/shard_map/ppermute | solution.py:45
  21.1 22.9 %collective-permute-done.1.refs_2_ = bf16[3,256,256]{2,1,0:T(8,128)(2,1)S(1)} collective-permute-done((bf16[3,256,256]{2,1,0:T(8,128)(2,1)S(1)}, bf16[3,256,256]{2,1,0:T(8,128)(2,1)S(1)}, u32[]{:S(2)}, u32[]{:S(2)}) %collective-permute-start.1) | collective-permute-done | bytes 393248 | tf_op jit(solution)/shard_map/ppermute | solution.py:45
  44.1 0.0 collective-permute-done.2.refs_3_
  44.1 0.0 collective-permute-done.3.refs_9_.fetched_ref
  44.1 1.5 %collective-permute-start.7 = (bf16[512,1280]{1,0:T(8,128)(2,1)S(1)}, bf16[512,1280]{1,0:T(8,128)(2,1)S(1)}, u32[]{:S(2)}, u32[]{:S(2)}) collective-permute-start(bf16[512,1280]{1,0:T(8,128)(2,1)S(1)} %collective-permute-done.3.refs_9_.fetched_ref), channel_id=1, source_target_pairs={{0,16},{16,0},{1,17},{17,1},{2,18},{18,2},{3,19},{19,3},{4,20},{20... | collective-permute-start | bytes 3932168 | tf_op jit(solution)/shard_map/ppermute | solution.py:45
  45.6 3.8 %attend.1 = (bf16[4,128,256]{2,1,0:T(8,128)(2,1)S(1)}, bf16[4,128,256]{2,1,0:T(8,128)(2,1)S(1)}) custom-call(s32[6]{0:T(128)S(1)} %stack.31.where_ref, bf16[3,256,256]{2,1,0:T(8,128)(2,1)S(1)} %own.1.refs_0_, bf16[3,256,256]{2,1,0:T(8,128)(2,1)S(1)} %collective-permute-done.refs_1_, bf16[3,256,256]{2,1,0:T(8,128)(2,1)S(1)} %collective-permute-done.1.refs_2_, ...), custom_call_target="tpu_custom_call" | custom-call | flops 1 | tf_op jit(solution)/shard_map/attend/pallas_call | solution.py:394
  49.4 0.6 collective-permute-start.4
  50.0 0.0 collective-permute-start.10
  50.0 3.0 %collective-permute-start.11 = (bf16[512,256]{1,0:T(8,128)(2,1)S(1)}, bf16[512,256]{1,0:T(8,128)(2,1)S(1)}, u32[]{:S(2)}, u32[]{:S(2)}) collective-permute-start(bf16[512,256]{1,0:T(8,128)(2,1)S(1)} %bitcast.10), channel_id=1, source_target_pairs={{0,4},{4,0},{8,12},{12,8},{1,5},{5,1},{9,13},{13,9},{2,6},{6,2},{1... | collective-permute-start | bytes 786440 | tf_op jit(solution)/shard_map/ppermute | solution.py:45
  53.0 3.5 %collective-permute-done.4.refs_4_ = bf16[512,256]{1,0:T(8,128)(2,1)S(1)} collective-permute-done((bf16[512,256]{1,0:T(8,128)(2,1)S(1)}, bf16[512,256]{1,0:T(8,128)(2,1)S(1)}, u32[]{:S(2)}, u32[]{:S(2)}) %collective-permute-start.4) | collective-permute-done | bytes 262176 | tf_op jit(solution)/shard_map/ppermute | solution.py:45
  56.5 0.0 collective-permute-start.5
  56.5 2.6 %collective-permute-start.6 = (bf16[512,256]{1,0:T(8,128)(2,1)S(1)}, bf16[512,256]{1,0:T(8,128)(2,1)S(1)}, u32[]{:S(2)}, u32[]{:S(2)}) collective-permute-start(bf16[512,256]{1,0:T(8,128)(2,1)S(1)} %collective-permute-done.4.refs_4_), channel_id=1, source_target_pairs={{0,4},{4,0},{8,12},{12,8},{1,5},{5,1},{9,13},{13,9},{2,6},{6,2},{1... | collective-permute-start | bytes 786440 | tf_op jit(solution)/shard_map/ppermute | solution.py:45
  59.1 6.7 %collective-permute-done.10.refs_2_ = bf16[512,256]{1,0:T(8,128)(2,1)S(1)} collective-permute-done((bf16[512,256]{1,0:T(8,128)(2,1)S(1)}, bf16[512,256]{1,0:T(8,128)(2,1)S(1)}, u32[]{:S(2)}, u32[]{:S(2)}) %collective-permute-start.10) | collective-permute-done | bytes 262176 | tf_op jit(solution)/shard_map/ppermute | solution.py:45
  65.8 0.0 collective-permute-done.11.refs_1_
  65.8 0.7 collective-permute-start.12
  66.4 1.3 %collective-permute-start.13 = (bf16[512,256]{1,0:T(8,128)(2,1)S(1)}, bf16[512,256]{1,0:T(8,128)(2,1)S(1)}, u32[]{:S(2)}, u32[]{:S(2)}) collective-permute-start(bf16[512,256]{1,0:T(8,128)(2,1)S(1)} %collective-permute-done.10.refs_2_), channel_id=1, source_target_pairs={{4,0},{8,12},{5,1},{9,13},{6,2},{10,14},{7,3},{11,15},{20,16},{24,... | collective-permute-start | bytes 786440 | tf_op jit(solution)/shard_map/ppermute | solution.py:520
  67.7 6.2 %collective-permute-done.5.refs_6_ = bf16[512,256]{1,0:T(8,128)(2,1)S(1)} collective-permute-done((bf16[512,256]{1,0:T(8,128)(2,1)S(1)}, bf16[512,256]{1,0:T(8,128)(2,1)S(1)}, u32[]{:S(2)}, u32[]{:S(2)}) %collective-permute-start.5) | collective-permute-done | bytes 262176 | tf_op jit(solution)/shard_map/ppermute | solution.py:45
  74.0 0.7 collective-permute-done.6.refs_5_
  74.7 0.7 collective-permute-start.8
  75.4 1.3 %collective-permute-start.9 = (bf16[512,256]{1,0:T(8,128)(2,1)S(1)}, bf16[512,256]{1,0:T(8,128)(2,1)S(1)}, u32[]{:S(2)}, u32[]{:S(2)}) collective-permute-start(bf16[512,256]{1,0:T(8,128)(2,1)S(1)} %collective-permute-done.5.refs_6_), channel_id=1, source_target_pairs={{4,0},{8,12},{5,1},{9,13},{6,2},{10,14},{7,3},{11,15},{20,16},{24,... | collective-permute-start | bytes 786440 | tf_op jit(solution)/shard_map/ppermute | solution.py:520
  76.7 3.6 %collective-permute-done.13.refs_7_ = bf16[512,256]{1,0:T(8,128)(2,1)S(1)} collective-permute-done((bf16[512,256]{1,0:T(8,128)(2,1)S(1)}, bf16[512,256]{1,0:T(8,128)(2,1)S(1)}, u32[]{:S(2)}, u32[]{:S(2)}) %collective-permute-start.13) | collective-permute-done | bytes 262176 | tf_op jit(solution)/shard_map/ppermute | solution.py:520
  80.3 5.1 %first.1.acc_in = f32[512,1280]{1,0:T(8,128)S(1)} custom-call(s32[6]{0:T(128)S(1)} %stack.31.where_ref, bf16[512,256]{1,0:T(8,128)(2,1)S(1)} %bitcast.12, bf16[512,256]{1,0:T(8,128)(2,1)S(1)} %collective-permute-done.11.refs_1_, bf16[512,256]{1,0:T(8,128)(2,1)S(1)} %collective-permute-done.10.refs_2_, bf16[512,256]{1,0:T(8,128)(2,1)S(1)} %collective-permute-done.12.refs_3_, ...), custom_call_target="tpu_custom_call" | custom-call | flops 1 | tf_op jit(solution)/shard_map/first/pallas_call | solution.py:441
  85.4 0.0 copy-start.4
  85.4 0.0 copy-start.5
  85.4 0.0 collective-permute-done.8.slot
  85.5 2.0 %second.1 = (bf16[4,64,1280]{2,1,0:T(8,128)(2,1)S(1)}, bf16[4,64,1280]{2,1,0:T(8,128)(2,1)S(1)}) custom-call(s32[6]{0:T(128)S(1)} %stack.31.where_ref, bf16[512,256]{1,0:T(8,128)(2,1)S(1)} %collective-permute-done.8.slot, bf16[512,256]{1,0:T(8,128)(2,1)S(1)} %collective-permute-done.9.more, bf16[512,1280]{1,0:T(8,128)(2,1)S(1)} %collective-permute-done.3.refs_9_.fetched_ref, ...), custom_call_target="tpu_custom_call" | custom-call | flops 1 | tf_op jit(solution)/shard_map/second/pallas_call | solution.py:473
  87.5 0.1 collective-permute-start.14
  87.6 2.1 %collective-permute-done.14.term_ref = bf16[4,64,1280]{2,1,0:T(8,128)(2,1)S(1)} collective-permute-done((bf16[4,64,1280]{2,1,0:T(8,128)(2,1)S(1)}, bf16[4,64,1280]{2,1,0:T(8,128)(2,1)S(1)}, u32[]{:S(2)}, u32[]{:S(2)}) %collective-permute-start.14) | collective-permute-done | bytes 655392 | tf_op jit(solution)/shard_map/ppermute | solution.py:45
  89.7 0.7 add.10
  90.4 1.9 %collective-permute-start.15 = (bf16[64,1280]{1,0:T(8,128)(2,1)S(1)}, bf16[64,1280]{1,0:T(8,128)(2,1)S(1)}, u32[]{:S(2)}, u32[]{:S(2)}) collective-permute-start(bf16[64,1280]{1,0:T(8,128)(2,1)S(1)} %get-tuple-element.58), channel_id=1, source_target_pairs={{0,12},{4,8},{8,4},{12,0},{1,13},{5,9},{9,5},{13,1},{2,14},{6,10},... | collective-permute-start | bytes 491528 | tf_op jit(solution)/shard_map/ppermute | solution.py:45
  92.3 2.5 %collective-permute-start.17 = (bf16[64,1280]{1,0:T(8,128)(2,1)S(1)}, bf16[64,1280]{1,0:T(8,128)(2,1)S(1)}, u32[]{:S(2)}, u32[]{:S(2)}) collective-permute-start(bf16[64,1280]{1,0:T(8,128)(2,1)S(1)} %get-tuple-element.60), channel_id=1, source_target_pairs={{0,4},{4,0},{8,12},{12,8},{1,5},{5,1},{9,13},{13,9},{2,6},{6,2},{1... | collective-permute-start | bytes 491528 | tf_op jit(solution)/shard_map/ppermute | solution.py:45
  94.8 4.6 %collective-permute-done.15.refs_1_ = bf16[64,1280]{1,0:T(8,128)(2,1)S(1)} collective-permute-done((bf16[64,1280]{1,0:T(8,128)(2,1)S(1)}, bf16[64,1280]{1,0:T(8,128)(2,1)S(1)}, u32[]{:S(2)}, u32[]{:S(2)}) %collective-permute-start.15) | collective-permute-done | bytes 163872 | tf_op jit(solution)/shard_map/ppermute | solution.py:45
  99.4 7.5 %collective-permute-done.16.refs_2_ = bf16[64,1280]{1,0:T(8,128)(2,1)S(1)} collective-permute-done((bf16[64,1280]{1,0:T(8,128)(2,1)S(1)}, bf16[64,1280]{1,0:T(8,128)(2,1)S(1)}, u32[]{:S(2)}, u32[]{:S(2)}) %collective-permute-start.16) | collective-permute-done | bytes 163872 | tf_op jit(solution)/shard_map/ppermute | solution.py:45
  106.9 0.0 collective-permute-done.17.refs_3_
  106.9 1.6 %mix.1 = bf16[64,5120]{1,0:T(8,128)(2,1)} custom-call(s32[6]{0:T(128)S(1)} %stack.31.where_ref, bf16[64,5120]{1,0:T(8,128)(2,1)S(1)} %copy-done.4, f32[1,5120]{1,0:T(1,128)S(1)} %bitcast.13, bf16[64,1280]{1,0:T(8,128)(2,1)S(1)} %get-tuple-element.57.refs_0_, bf16[64,1280]{1,0:T(8,128)(2,1)S(1)} %collective-permute-done.15.refs_1_, ...), custom_call_target="tpu_custom_call" | custom-call | flops 1 | tf_op jit(solution)/shard_map/mix/pallas_call | solution.py:263
  (15 shorter events, 0.0 us)
Async XLA Ops:
  0.0 3.9 %copy-start.1 = (bf16[1024,1280]{1,0:T(8,128)(2,1)S(1)}, bf16[1024,1280]{1,0:T(8,128)(2,1)}, u32[]{:S(2)}) copy-start(bf16[1024,1280]{1,0:T(8,128)(2,1)} %refs_8_) | copy-start | bytes 7864324
  3.7 6.9 %copy-start.7 = (bf16[3,256,256]{2,1,0:T(8,128)(2,1)S(1)}, bf16[3,256,256]{2,1,0:T(8,128)(2,1)}, u32[]{:S(2)}) copy-start(bf16[3,256,256]{2,1,0:T(8,128)(2,1)} %get-tuple-element.33) | copy-start | bytes 1179652
  3.7 7.6 %copy-start.3 = (bf16[256,1024]{1,0:T(8,128)(2,1)S(1)}, bf16[256,1024]{1,0:T(8,128)(2,1)}, u32[]{:S(2)}) copy-start(bf16[256,1024]{1,0:T(8,128)(2,1)} %q_ref.3) | copy-start | bytes 1572868
  3.8 7.6 %copy-start.6 = (s32[2,2,8]{2,1,0:T(2,128)S(1)}, s32[2,2,8]{2,1,0:T(2,128)}, u32[]{:S(2)}) copy-start(s32[2,2,8]{2,1,0:T(2,128)} %exps_ref.3) | copy-start | bytes 388
  3.9 6.7 %copy-start.8 = (bf16[3,256,256]{2,1,0:T(8,128)(2,1)S(1)}, bf16[3,256,256]{2,1,0:T(8,128)(2,1)}, u32[]{:S(2)}) copy-start(bf16[3,256,256]{2,1,0:T(8,128)(2,1)} %get-tuple-element.34) | copy-start | bytes 1179652
  3.9 7.5 %copy-start.2 = (bf16[2,256,1024]{2,1,0:T(8,128)(2,1)S(1)}, bf16[2,256,1024]{2,1,0:T(8,128)(2,1)}, u32[]{:S(2)}) copy-start(bf16[2,256,1024]{2,1,0:T(8,128)(2,1)} %fresh_ref.3) | copy-start | bytes 3145732
  4.0 40.1 %collective-permute-start.3 = (bf16[512,1280]{1,0:T(8,128)(2,1)S(1)}, bf16[512,1280]{1,0:T(8,128)(2,1)S(1)}, u32[]{:S(2)}, u32[]{:S(2)}) collective-permute-start(bf16[512,1280]{1,0:T(8,128)(2,1)S(1)} %constant_dynamic-slice_fusion), channel_id=1, source_target_pairs={{0,2},{2,0},{1,3},{3,1},{4,6},{6,4},{5,7},{7,5},{8,10},{10,8},{9,1... | collective-permute-start | bytes 3932168 | tf_op jit(solution)/shard_map/ppermute | solution.py:45
  7.0 14.1 %collective-permute-start = (bf16[3,256,256]{2,1,0:T(8,128)(2,1)}, bf16[3,256,256]{2,1,0:T(8,128)(2,1)S(1)}, u32[]{:S(2)}, u32[]{:S(2)}) collective-permute-start(bf16[3,256,256]{2,1,0:T(8,128)(2,1)} %get-tuple-element.35), channel_id=1, source_target_pairs={{0,12},{4,8},{8,4},{12,0},{1,13},{5,9},{9,5},{13,1},{2,14},{6,10},... | collective-permute-start | bytes 1179656 | tf_op jit(solution)/shard_map/ppermute | solution.py:45
  10.6 33.5 %collective-permute-start.1 = (bf16[3,256,256]{2,1,0:T(8,128)(2,1)S(1)}, bf16[3,256,256]{2,1,0:T(8,128)(2,1)S(1)}, u32[]{:S(2)}, u32[]{:S(2)}) collective-permute-start(bf16[3,256,256]{2,1,0:T(8,128)(2,1)S(1)} %copy-done.8), channel_id=1, source_target_pairs={{0,8},{4,12},{8,0},{12,4},{1,9},{5,13},{9,1},{13,5},{2,10},{6,14},... | collective-permute-start | bytes 1179656 | tf_op jit(solution)/shard_map/ppermute | solution.py:45
  10.6 33.5 %collective-permute-start.2 = (bf16[3,256,256]{2,1,0:T(8,128)(2,1)S(1)}, bf16[3,256,256]{2,1,0:T(8,128)(2,1)S(1)}, u32[]{:S(2)}, u32[]{:S(2)}) collective-permute-start(bf16[3,256,256]{2,1,0:T(8,128)(2,1)S(1)} %copy-done.7), channel_id=1, source_target_pairs={{0,4},{4,0},{8,12},{12,8},{1,5},{5,1},{9,13},{13,9},{2,6},{6,2},{1... | collective-permute-start | bytes 1179656 | tf_op jit(solution)/shard_map/ppermute | solution.py:45
  11.4 2.2 %copy-start = (bf16[2,1024,1024]{2,1,0:T(8,128)(2,1)S(1)}, bf16[2,1024,1024]{2,1,0:T(8,128)(2,1)}, u32[]{:S(2)}) copy-start(bf16[2,1024,1024]{2,1,0:T(8,128)(2,1)} %cached_ref.3) | copy-start | bytes 12582916
  44.1 30.6 %collective-permute-start.7 = (bf16[512,1280]{1,0:T(8,128)(2,1)S(1)}, bf16[512,1280]{1,0:T(8,128)(2,1)S(1)}, u32[]{:S(2)}, u32[]{:S(2)}) collective-permute-start(bf16[512,1280]{1,0:T(8,128)(2,1)S(1)} %collective-permute-done.3.refs_9_.fetched_ref), channel_id=1, source_target_pairs={{0,16},{16,0},{1,17},{17,1},{2,18},{18,2},{3,19},{19,3},{4,20},{20... | collective-permute-start | bytes 3932168 | tf_op jit(solution)/shard_map/ppermute | solution.py:45
  49.4 7.1 %collective-permute-start.4 = (bf16[512,256]{1,0:T(8,128)(2,1)S(1)}, bf16[512,256]{1,0:T(8,128)(2,1)S(1)}, u32[]{:S(2)}, u32[]{:S(2)}) collective-permute-start(bf16[512,256]{1,0:T(8,128)(2,1)S(1)} %bitcast.14), channel_id=1, source_target_pairs={{0,2},{2,0},{1,3},{3,1},{4,6},{6,4},{5,7},{7,5},{8,10},{10,8},{9,1... | collective-permute-start | bytes 786440 | tf_op jit(solution)/shard_map/ppermute | solution.py:45
  50.0 15.8 %collective-permute-start.10 = (bf16[512,256]{1,0:T(8,128)(2,1)S(1)}, bf16[512,256]{1,0:T(8,128)(2,1)S(1)}, u32[]{:S(2)}, u32[]{:S(2)}) collective-permute-start(bf16[512,256]{1,0:T(8,128)(2,1)S(1)} %bitcast.9), channel_id=1, source_target_pairs={{0,8},{4,12},{8,0},{12,4},{1,9},{5,13},{9,1},{13,5},{2,10},{6,14},... | collective-permute-start | bytes 786440 | tf_op jit(solution)/shard_map/ppermute | solution.py:45
  50.0 15.8 %collective-permute-start.11 = (bf16[512,256]{1,0:T(8,128)(2,1)S(1)}, bf16[512,256]{1,0:T(8,128)(2,1)S(1)}, u32[]{:S(2)}, u32[]{:S(2)}) collective-permute-start(bf16[512,256]{1,0:T(8,128)(2,1)S(1)} %bitcast.10), channel_id=1, source_target_pairs={{0,4},{4,0},{8,12},{12,8},{1,5},{5,1},{9,13},{13,9},{2,6},{6,2},{1... | collective-permute-start | bytes 786440 | tf_op jit(solution)/shard_map/ppermute | solution.py:45
  56.5 17.5 %collective-permute-start.5 = (bf16[512,256]{1,0:T(8,128)(2,1)S(1)}, bf16[512,256]{1,0:T(8,128)(2,1)S(1)}, u32[]{:S(2)}, u32[]{:S(2)}) collective-permute-start(bf16[512,256]{1,0:T(8,128)(2,1)S(1)} %collective-permute-done.4.refs_4_), channel_id=1, source_target_pairs={{0,8},{4,12},{8,0},{12,4},{1,9},{5,13},{9,1},{13,5},{2,10},{6,14},... | collective-permute-start | bytes 786440 | tf_op jit(solution)/shard_map/ppermute | solution.py:45
  56.5 18.2 %collective-permute-start.6 = (bf16[512,256]{1,0:T(8,128)(2,1)S(1)}, bf16[512,256]{1,0:T(8,128)(2,1)S(1)}, u32[]{:S(2)}, u32[]{:S(2)}) collective-permute-start(bf16[512,256]{1,0:T(8,128)(2,1)S(1)} %collective-permute-done.4.refs_4_), channel_id=1, source_target_pairs={{0,4},{4,0},{8,12},{12,8},{1,5},{5,1},{9,13},{13,9},{2,6},{6,2},{1... | collective-permute-start | bytes 786440 | tf_op jit(solution)/shard_map/ppermute | solution.py:45
  65.8 10.9 %collective-permute-start.12 = (bf16[512,256]{1,0:T(8,128)(2,1)S(1)}, bf16[512,256]{1,0:T(8,128)(2,1)S(1)}, u32[]{:S(2)}, u32[]{:S(2)}) collective-permute-start(bf16[512,256]{1,0:T(8,128)(2,1)S(1)} %bitcast.11), channel_id=1, source_target_pairs={{4,8},{8,4},{5,9},{9,5},{6,10},{10,6},{7,11},{11,7},{20,24},{24,20... | collective-permute-start | bytes 786440 | tf_op jit(solution)/shard_map/ppermute | solution.py:45
  66.4 13.9 %collective-permute-start.13 = (bf16[512,256]{1,0:T(8,128)(2,1)S(1)}, bf16[512,256]{1,0:T(8,128)(2,1)S(1)}, u32[]{:S(2)}, u32[]{:S(2)}) collective-permute-start(bf16[512,256]{1,0:T(8,128)(2,1)S(1)} %collective-permute-done.10.refs_2_), channel_id=1, source_target_pairs={{4,0},{8,12},{5,1},{9,13},{6,2},{10,14},{7,3},{11,15},{20,16},{24,... | collective-permute-start | bytes 786440 | tf_op jit(solution)/shard_map/ppermute | solution.py:520
  74.7 10.8 %collective-permute-start.8 = (bf16[512,256]{1,0:T(8,128)(2,1)S(1)}, bf16[512,256]{1,0:T(8,128)(2,1)S(1)}, u32[]{:S(2)}, u32[]{:S(2)}) collective-permute-start(bf16[512,256]{1,0:T(8,128)(2,1)S(1)} %collective-permute-done.4.refs_4_), channel_id=1, source_target_pairs={{4,8},{8,4},{5,9},{9,5},{6,10},{10,6},{7,11},{11,7},{20,24},{24,20... | collective-permute-start | bytes 786440 | tf_op jit(solution)/shard_map/ppermute | solution.py:45
  75.4 10.1 %collective-permute-start.9 = (bf16[512,256]{1,0:T(8,128)(2,1)S(1)}, bf16[512,256]{1,0:T(8,128)(2,1)S(1)}, u32[]{:S(2)}, u32[]{:S(2)}) collective-permute-start(bf16[512,256]{1,0:T(8,128)(2,1)S(1)} %collective-permute-done.5.refs_6_), channel_id=1, source_target_pairs={{4,0},{8,12},{5,1},{9,13},{6,2},{10,14},{7,3},{11,15},{20,16},{24,... | collective-permute-start | bytes 786440 | tf_op jit(solution)/shard_map/ppermute | solution.py:520
  85.4 21.5 %copy-start.4 = (bf16[64,5120]{1,0:T(8,128)(2,1)S(1)}, bf16[64,5120]{1,0:T(8,128)(2,1)}, u32[]{:S(2)}) copy-start(bf16[64,5120]{1,0:T(8,128)(2,1)} %hidden_ref.1) | copy-start | bytes 1966084
  85.4 21.5 %copy-start.5 = (f32[5120]{0:T(1024)S(1)}, f32[5120]{0:T(1024)}, u32[]{:S(2)}) copy-start(f32[5120]{0:T(1024)} %param.13) | copy-start | bytes 61444
  87.5 2.2 %collective-permute-start.14 = (bf16[4,64,1280]{2,1,0:T(8,128)(2,1)S(1)}, bf16[4,64,1280]{2,1,0:T(8,128)(2,1)S(1)}, u32[]{:S(2)}, u32[]{:S(2)}) collective-permute-start(bf16[4,64,1280]{2,1,0:T(8,128)(2,1)S(1)} %get-tuple-element.56), channel_id=1, source_target_pairs={{0,1},{1,0},{2,3},{3,2},{4,5},{5,4},{6,7},{7,6},{8,9},{9,8},{10,11... | collective-permute-start | bytes 1966088 | tf_op jit(solution)/shard_map/ppermute | solution.py:45
  90.4 9.1 %collective-permute-start.15 = (bf16[64,1280]{1,0:T(8,128)(2,1)S(1)}, bf16[64,1280]{1,0:T(8,128)(2,1)S(1)}, u32[]{:S(2)}, u32[]{:S(2)}) collective-permute-start(bf16[64,1280]{1,0:T(8,128)(2,1)S(1)} %get-tuple-element.58), channel_id=1, source_target_pairs={{0,12},{4,8},{8,4},{12,0},{1,13},{5,9},{9,5},{13,1},{2,14},{6,10},... | collective-permute-start | bytes 491528 | tf_op jit(solution)/shard_map/ppermute | solution.py:45
  92.3 14.6 %collective-permute-start.16 = (bf16[64,1280]{1,0:T(8,128)(2,1)S(1)}, bf16[64,1280]{1,0:T(8,128)(2,1)S(1)}, u32[]{:S(2)}, u32[]{:S(2)}) collective-permute-start(bf16[64,1280]{1,0:T(8,128)(2,1)S(1)} %get-tuple-element.59), channel_id=1, source_target_pairs={{0,8},{4,12},{8,0},{12,4},{1,9},{5,13},{9,1},{13,5},{2,10},{6,14},... | collective-permute-start | bytes 491528 | tf_op jit(solution)/shard_map/ppermute | solution.py:45
  92.3 14.6 %collective-permute-start.17 = (bf16[64,1280]{1,0:T(8,128)(2,1)S(1)}, bf16[64,1280]{1,0:T(8,128)(2,1)S(1)}, u32[]{:S(2)}, u32[]{:S(2)}) collective-permute-start(bf16[64,1280]{1,0:T(8,128)(2,1)S(1)} %get-tuple-element.60), channel_id=1, source_target_pairs={{0,4},{4,0},{8,12},{12,8},{1,5},{5,1},{9,13},{13,9},{2,6},{6,2},{1... | collective-permute-start | bytes 491528 | tf_op jit(solution)/shard_map/ppermute | solution.py:45

commit v11 on v10

--- a/solution.py
+++ b/solution.py
@@ -11,6 +11,7 @@
 HEAD_DIM = 128
 SCALE_ROWS = 128
 SATURATION = 448.0
+PACK_ROWS = 64
 VMEM_BYTES = 32 * 1024 * 1024
 PACK_VMEM_BYTES = 60 * 1024 * 1024
 ATTEND_FLOPS = 1
@@ -54,14 +55,15 @@
 
 
 def pack_kernel(split, per, exps_ref, q_ref, fresh_ref, cached_ref, *refs):
-    outs, (q_buf, fresh_buf, cached_buf, sems) = refs[:-4], refs[-4:]
+    outs, bufs = refs[: split - 1], refs[split - 1 : 2 * split - 2]
+    q_buf, fresh_buf, cached_buf, sems, out_sems = refs[2 * split - 2 :]
     patch = lax.axis_index("patch")
     near = lax.rem(patch, split)
     tok = q_buf.shape[0]
-    copies = []
-    for block in range(tok // SCALE_ROWS):
-        rows = pl.ds(block * SCALE_ROWS, SCALE_ROWS)
-        there = pl.ds(pl.multiple_of(patch * tok + block * SCALE_ROWS, SCALE_ROWS), SCALE_ROWS)
+    copies, sent = [], []
+    for block in range(tok // PACK_ROWS):
+        rows = pl.ds(block * PACK_ROWS, PACK_ROWS)
+        there = pl.ds(pl.multiple_of(patch * tok + block * PACK_ROWS, PACK_ROWS), PACK_ROWS)
         copies.append(
             [
                 pltpu.make_async_copy(q_ref.at[rows], q_buf.at[rows], sems.at[block, 0]),
@@ -71,40 +73,50 @@
         )
         for copy in copies[-1]:
             copy.start()
-    for block in range(tok // SCALE_ROWS):
-        rows = pl.ds(block * SCALE_ROWS, SCALE_ROWS)
+    for block in range(tok // PACK_ROWS):
+        rows = pl.ds(block * PACK_ROWS, PACK_ROWS)
         for copy in copies[block]:
             copy.wait()
-        for rel in range(1, split):
-            out = outs[rel - 1]
+        for rel in range(split - 1, 0, -1):
+            buf = bufs[rel - 1]
             for chunk in range(per):
                 head = (near ^ rel) * per + chunk
                 lanes = pl.ds(pl.multiple_of(head * HEAD_DIM, HEAD_DIM), HEAD_DIM)
                 here = pl.ds(chunk * HEAD_DIM, HEAD_DIM)
-                out[0, rows, here] = q_buf[rows, lanes]
+                buf[0, rows, here] = q_buf[rows, lanes]
                 for stacked in range(2):
-                    out[1 + stacked, rows, here] = decode(
+                    buf[1 + stacked, rows, here] = decode(
                         fresh_buf[stacked, rows, lanes],
                         cached_buf[stacked, rows, lanes],
-                        exps_ref[stacked, block, head],
+                        exps_ref[stacked, block * PACK_ROWS // SCALE_ROWS, head],
                     )
+            sent.append(
+                pltpu.make_async_copy(
+                    buf.at[:, rows], outs[rel - 1].at[:, rows], out_sems.at[block, rel - 1]
+                )
+            )
+            sent[-1].start()
+    for copy in sent:
+        copy.wait()
 
 
 def pack(split, exponents, queries, fresh_kv, cached_kv):
     tok, channels = queries.shape
     feat = channels // split
-    blocks = tok // SCALE_ROWS
+    blocks = tok // PACK_ROWS
     hbm = pl.BlockSpec(memory_space=pltpu.HBM)
     return pl.pallas_call(
         functools.partial(pack_kernel, split, feat // HEAD_DIM),
         out_shape=[jax.ShapeDtypeStruct((3, tok, feat), jnp.bfloat16)] * (split - 1),
         in_specs=[pl.BlockSpec(memory_space=pltpu.SMEM), hbm, hbm, hbm],
-        out_specs=[pl.BlockSpec(memory_space=pltpu.VMEM)] * (split - 1),
-        scratch_shapes=[
+        out_specs=[hbm] * (split - 1),
+        scratch_shapes=[pltpu.VMEM((3, tok, feat), jnp.bfloat16)] * (split - 1)
+        + [
             pltpu.VMEM((tok, channels), jnp.bfloat16),
             pltpu.VMEM((2, tok, channels), jnp.bfloat16),
             pltpu.VMEM((2, tok, channels), jnp.bfloat16),
             pltpu.SemaphoreType.DMA((blocks, 3)),
+            pltpu.SemaphoreType.DMA((blocks, split - 1)),
         ],
         compiler_params=pltpu.CompilerParams(vmem_limit_bytes=PACK_VMEM_BYTES),
         name="pack",
@@ -465,20 +477,20 @@
             out[at] = acc_ref[where_ref[NEAR] ^ at, where_ref[SUB] ^ sub].astype(jnp.bfloat16)
 
 
-def second_product(where, slot, more, weights, acc):
+def second_product(where, chunk, slot, more, weights, acc):
     rows, feat = slot.shape
     depth, cols = weights[0].shape
     wide = cols // 2
-    out = jax.ShapeDtypeStruct((4, rows // 8, cols), jnp.bfloat16)
+    out = jax.ShapeDtypeStruct((4, rows // 8, wide), jnp.bfloat16)
     return call(
         second_kernel,
         "second",
         [out] * 2,
-        2,
+        1,
         [spec((rows, feat))] * 2
-        + [pl.BlockSpec((depth, wide), lambda i, w: (0, i))] * 2
-        + [pl.BlockSpec((rows, wide), lambda i, w: (0, i))],
-        [pl.BlockSpec((4, rows // 8, wide), lambda i, w: (0, 0, i))] * 2,
+        + [pl.BlockSpec((depth, wide), lambda i, w: (0, chunk))] * 2
+        + [pl.BlockSpec((rows, wide), lambda i, w: (0, chunk))],
+        [spec(out.shape)] * 2,
         [pltpu.VMEM((4, 2, rows // 8, wide), jnp.float32)],
     )(where, slot, more, *weights, acc)
 
@@ -521,10 +533,38 @@
         slots.append([x, next_to, far, middle, ends])
     first = [*slots[0][:4], *slots[1][:3]]
     acc = first_product(where, first, slots[0][4], [out_weight, fetched, passed])
-    keep, send = second_product(where, *slots[1][3:], [fetched, passed], acc)
-    total = add(where, keep, swap(send, "sub", 2, 1))
-    blocks = [total[0]] + [swap(total[rel], "patch", 4, rel) for rel in range(3, 0, -1)]
-    return mix(where, hidden_in, attn_gate, [[blocks[0], *blocks[:0:-1]]])
+    terms = [second_product(where, at, *slots[1][3:], [fetched, passed], acc) for at in range(2)]
+    blocks = []
+    for keep, send in terms:
+        total = add(where, keep, swap(send, "sub", 2, 1))
+        blocks.append([total[0]] + [swap(total[rel], "patch", 4, rel) for rel in range(3, 0, -1)])
+    return mix_columns(where, hidden_in, attn_gate, blocks)
+
+
+def mix_columns_kernel(where_ref, hidden_ref, gate_ref, *refs):
+    blocks, out_ref = refs[:-1], refs[-1]
+    cols = blocks[0].shape[1]
+    for chunk in range(2):
+        for at, rel in enumerate((0, 3, 2, 1)):
+            start = (2 * (where_ref[PATCH] ^ rel) + chunk) * cols
+            lanes = pl.ds(pl.multiple_of(start, HEAD_DIM), cols)
+            mixed = hidden_ref[:, lanes].astype(jnp.float32) + gate_ref[:, lanes] * blocks[
+                4 * chunk + at
+            ][...].astype(jnp.float32)
+            out_ref[:, lanes] = mixed.astype(jnp.bfloat16)
+
+
+def mix_columns(where, hidden_in, attn_gate, blocks):
+    rows, width = hidden_in.shape
+    flat = [x for chunk in blocks for x in chunk]
+    return call(
+        mix_columns_kernel,
+        "mix",
+        jax.ShapeDtypeStruct((rows, width), jnp.bfloat16),
+        1,
+        [spec((rows, width)), spec((1, width))] + [spec(flat[0].shape)] * len(flat),
+        spec((rows, width)),
+    )(where, hidden_in, attn_gate[None], *flat)
 
 
 def body(sizes, queries, fresh_kv, cached_kv, exponents, out_weight, hidden_in, attn_gate):

time: 109 us -> 107 us (0.982)
  waiting for transfers between devices: 64.1 us -> 57.5 us
  starting transfers between devices: 23.6 us -> 28.3 us
    ppermute x16 -> x20, waiting for transfers between devices: 60.4 us -> 53.8 us  [swap(): return lax.ppermute(x, axes, pairs)]
    ppermute x16 -> x20, starting transfers between devices: 21 us -> 25.7 us  [swap(): return lax.ppermute(x, axes, pairs)]
    pallas_call x2 -> x3, Pallas kernels: 3.68 us -> 3.87 us  [the longest x2 2.27 us: second_product(): call(second_kernel, 'second', [out] * 2, 1, [spec((rows, feat))] * 2 + [p...]
  transfers between devices with their start and end apart: 18 -> 22, of which waited for: 10 -> 10; matrix products, arithmetic and copies ran while one was open for 0% -> 0% of each run, Pallas kernels for 9% -> 12%
where the time goes in v11:
time: 107 us
  waiting for transfers between devices  57.5 us (54%)
  starting transfers between devices  28.3 us (26%)
  Pallas kernels  18.8 us (18%)
  local copies, waits for them, and re-layouts  2.41 us (2%)
    ppermute x20, waiting for transfers between devices, swap(): return lax.ppermute(x, axes, pairs)  53.8 us
    ppermute x20, starting transfers between devices, swap(): return lax.ppermute(x, axes, pairs)  25.7 us
    pallas_call x1, Pallas kernels, first_product(): call(first_kernel, 'first', jax.ShapeDtypeStruct((rows, cols), jnp.float3...  5.11 us
    pallas_call x1, Pallas kernels, attend_halves(): call(attend_halves_kernel, 'attend', [out] * 2, 1, [spec((3, tok, feat))]...  3.79 us
    ppermute x2, waiting for transfers between devices, share_tail(): ends = lax.ppermute(far, 'patch', [(1, 0), (2, 3)])  3.63 us
    pallas_call x1, Pallas kernels, pack(): pl.pallas_call(functools.partial(pack_kernel, split, feat // HEAD_DIM), o...  3.52 us
    ppermute x2, starting transfers between devices, share_tail(): ends = lax.ppermute(far, 'patch', [(1, 0), (2, 3)])  2.58 us
    pallas_call x2, Pallas kernels, second_product(): call(second_kernel, 'second', [out] * 2, 1, [spec((rows, feat))] * 2 + [p...  2.27 us
  transfers between devices with their start and end apart: 22, of which 10 were waited for; matrix products, arithmetic and copies ran while one was open for 0% of the time, Pallas kernels for 12%

profile of v11, /device:TPU:0, one launch (start us, length us, event | category | flops | bytes accessed | tf_op | source)
XLA Modules:
  0.0 107.2 jit_solution(14081554028319234592)
XLA Ops:
  0.0 3.5 %pack.1 = (bf16[3,256,256]{2,1,0:T(8,128)(2,1)}, bf16[3,256,256]{2,1,0:T(8,128)(2,1)}, bf16[3,256,256]{2,1,0:T(8,128)(2,1)}) custom-call(s32[2,2,8]{2,1,0:T(2,128)} %exps_ref.3, bf16[256,1024]{1,0:T(8,128)(2,1)} %q_ref.3, bf16[2,256,1024]{2,1,0:T(8,128)(2,1)} %fresh_ref.3, bf16[2,1024,1024]{2,1,0:T(8,128)(2,1)} %cached_ref.3), custom_call_target="tpu_custom_call" | custom-call | tf_op jit(solution)/shard_map/pack/pallas_call | solution.py:108
  3.5 0.0 copy-start.7
  3.5 0.0 copy-start.3
  3.6 0.0 copy-start.6
  3.6 0.1 stack.31.where_ref
  3.7 0.0 copy-start.2
  3.7 0.1 constant_dynamic-slice_fusion
  3.8 3.0 %collective-permute-start.3 = (bf16[512,1280]{1,0:T(8,128)(2,1)S(1)}, bf16[512,1280]{1,0:T(8,128)(2,1)S(1)}, u32[]{:S(2)}, u32[]{:S(2)}) collective-permute-start(bf16[512,1280]{1,0:T(8,128)(2,1)S(1)} %constant_dynamic-slice_fusion), channel_id=1, source_target_pairs={{0,2},{2,0},{1,3},{3,1},{4,6},{6,4},{5,7},{7,5},{8,10},{10,8},{9,1... | collective-permute-start | bytes 3932168 | tf_op jit(solution)/shard_map/ppermute | solution.py:46
  6.8 3.6 %collective-permute-start = (bf16[3,256,256]{2,1,0:T(8,128)(2,1)}, bf16[3,256,256]{2,1,0:T(8,128)(2,1)S(1)}, u32[]{:S(2)}, u32[]{:S(2)}) collective-permute-start(bf16[3,256,256]{2,1,0:T(8,128)(2,1)} %get-tuple-element.41), channel_id=1, source_target_pairs={{0,12},{4,8},{8,4},{12,0},{1,13},{5,9},{9,5},{13,1},{2,14},{6,10},... | collective-permute-start | bytes 1179656 | tf_op jit(solution)/shard_map/ppermute | solution.py:46
  10.4 0.8 collective-permute-start.2
  11.2 2.2 %copy-done = bf16[2,1024,1024]{2,1,0:T(8,128)(2,1)S(1)} copy-done((bf16[2,1024,1024]{2,1,0:T(8,128)(2,1)S(1)}, bf16[2,1024,1024]{2,1,0:T(8,128)(2,1)}, u32[]{:S(2)}) %copy-start) | copy-done | bytes 4194328
  13.4 1.3 %own.1.refs_0_ = bf16[3,256,256]{2,1,0:T(8,128)(2,1)S(1)} custom-call(s32[6]{0:T(128)S(1)} %stack.31.where_ref, s32[2,2,8]{2,1,0:T(2,128)S(1)} %copy-done.6, bf16[256,1024]{1,0:T(8,128)(2,1)S(1)} %copy-done.3, bf16[2,256,1024]{2,1,0:T(8,128)(2,1)S(1)} %copy-done.2, bf16[2,1024,1024]{2,1,0:T(8,128)(2,1)S(1)} %copy-done), custom_call_target="tpu_custom_call" | custom-call | flops 1 | tf_op jit(solution)/shard_map/own/pallas_call | solution.py:144
  14.7 6.3 %collective-permute-done.refs_1_ = bf16[3,256,256]{2,1,0:T(8,128)(2,1)S(1)} collective-permute-done((bf16[3,256,256]{2,1,0:T(8,128)(2,1)}, bf16[3,256,256]{2,1,0:T(8,128)(2,1)S(1)}, u32[]{:S(2)}, u32[]{:S(2)}) %collective-permute-start) | collective-permute-done | bytes 393248 | tf_op jit(solution)/shard_map/ppermute | solution.py:46
  20.9 22.9 %collective-permute-done.1.refs_2_ = bf16[3,256,256]{2,1,0:T(8,128)(2,1)S(1)} collective-permute-done((bf16[3,256,256]{2,1,0:T(8,128)(2,1)S(1)}, bf16[3,256,256]{2,1,0:T(8,128)(2,1)S(1)}, u32[]{:S(2)}, u32[]{:S(2)}) %collective-permute-start.1) | collective-permute-done | bytes 393248 | tf_op jit(solution)/shard_map/ppermute | solution.py:46
  43.9 1.5 %collective-permute-start.7 = (bf16[512,1280]{1,0:T(8,128)(2,1)S(1)}, bf16[512,1280]{1,0:T(8,128)(2,1)S(1)}, u32[]{:S(2)}, u32[]{:S(2)}) collective-permute-start(bf16[512,1280]{1,0:T(8,128)(2,1)S(1)} %collective-permute-done.3.refs_9_.fetched_ref), channel_id=1, source_target_pairs={{0,16},{16,0},{1,17},{17,1},{2,18},{18,2},{3,19},{19,3},{4,20},{20... | collective-permute-start | bytes 3932168 | tf_op jit(solution)/shard_map/ppermute | solution.py:46
  45.4 3.8 %attend.1 = (bf16[4,128,256]{2,1,0:T(8,128)(2,1)S(1)}, bf16[4,128,256]{2,1,0:T(8,128)(2,1)S(1)}) custom-call(s32[6]{0:T(128)S(1)} %stack.31.where_ref, bf16[3,256,256]{2,1,0:T(8,128)(2,1)S(1)} %own.1.refs_0_, bf16[3,256,256]{2,1,0:T(8,128)(2,1)S(1)} %collective-permute-done.refs_1_, bf16[3,256,256]{2,1,0:T(8,128)(2,1)S(1)} %collective-permute-done.1.refs_2_, ...), custom_call_target="tpu_custom_call" | custom-call | flops 1 | tf_op jit(solution)/shard_map/attend/pallas_call | solution.py:406
  49.2 0.6 collective-permute-start.4
  49.8 3.0 %collective-permute-start.11 = (bf16[512,256]{1,0:T(8,128)(2,1)S(1)}, bf16[512,256]{1,0:T(8,128)(2,1)S(1)}, u32[]{:S(2)}, u32[]{:S(2)}) collective-permute-start(bf16[512,256]{1,0:T(8,128)(2,1)S(1)} %bitcast.10), channel_id=1, source_target_pairs={{0,4},{4,0},{8,12},{12,8},{1,5},{5,1},{9,13},{13,9},{2,6},{6,2},{1... | collective-permute-start | bytes 786440 | tf_op jit(solution)/shard_map/ppermute | solution.py:46
  52.8 3.5 %collective-permute-done.4.refs_4_ = bf16[512,256]{1,0:T(8,128)(2,1)S(1)} collective-permute-done((bf16[512,256]{1,0:T(8,128)(2,1)S(1)}, bf16[512,256]{1,0:T(8,128)(2,1)S(1)}, u32[]{:S(2)}, u32[]{:S(2)}) %collective-permute-start.4) | collective-permute-done | bytes 262176 | tf_op jit(solution)/shard_map/ppermute | solution.py:46
  56.3 0.0 collective-permute-start.5
  56.3 2.6 %collective-permute-start.6 = (bf16[512,256]{1,0:T(8,128)(2,1)S(1)}, bf16[512,256]{1,0:T(8,128)(2,1)S(1)}, u32[]{:S(2)}, u32[]{:S(2)}) collective-permute-start(bf16[512,256]{1,0:T(8,128)(2,1)S(1)} %collective-permute-done.4.refs_4_), channel_id=1, source_target_pairs={{0,4},{4,0},{8,12},{12,8},{1,5},{5,1},{9,13},{13,9},{2,6},{6,2},{1... | collective-permute-start | bytes 786440 | tf_op jit(solution)/shard_map/ppermute | solution.py:46
  58.9 6.7 %collective-permute-done.10.refs_2_ = bf16[512,256]{1,0:T(8,128)(2,1)S(1)} collective-permute-done((bf16[512,256]{1,0:T(8,128)(2,1)S(1)}, bf16[512,256]{1,0:T(8,128)(2,1)S(1)}, u32[]{:S(2)}, u32[]{:S(2)}) %collective-permute-start.10) | collective-permute-done | bytes 262176 | tf_op jit(solution)/shard_map/ppermute | solution.py:46
  65.6 0.7 collective-permute-start.12
  66.2 1.3 %collective-permute-start.13 = (bf16[512,256]{1,0:T(8,128)(2,1)S(1)}, bf16[512,256]{1,0:T(8,128)(2,1)S(1)}, u32[]{:S(2)}, u32[]{:S(2)}) collective-permute-start(bf16[512,256]{1,0:T(8,128)(2,1)S(1)} %collective-permute-done.10.refs_2_), channel_id=1, source_target_pairs={{4,0},{8,12},{5,1},{9,13},{6,2},{10,14},{7,3},{11,15},{20,16},{24,... | collective-permute-start | bytes 786440 | tf_op jit(solution)/shard_map/ppermute | solution.py:532
  67.5 6.2 %collective-permute-done.5.refs_6_ = bf16[512,256]{1,0:T(8,128)(2,1)S(1)} collective-permute-done((bf16[512,256]{1,0:T(8,128)(2,1)S(1)}, bf16[512,256]{1,0:T(8,128)(2,1)S(1)}, u32[]{:S(2)}, u32[]{:S(2)}) %collective-permute-start.5) | collective-permute-done | bytes 262176 | tf_op jit(solution)/shard_map/ppermute | solution.py:46
  73.8 0.7 collective-permute-done.6.refs_5_
  74.5 0.0 collective-permute-done.7.refs_10_.passed_ref
  74.5 0.7 collective-permute-start.8
  75.2 1.3 %collective-permute-start.9 = (bf16[512,256]{1,0:T(8,128)(2,1)S(1)}, bf16[512,256]{1,0:T(8,128)(2,1)S(1)}, u32[]{:S(2)}, u32[]{:S(2)}) collective-permute-start(bf16[512,256]{1,0:T(8,128)(2,1)S(1)} %collective-permute-done.5.refs_6_), channel_id=1, source_target_pairs={{4,0},{8,12},{5,1},{9,13},{6,2},{10,14},{7,3},{11,15},{20,16},{24,... | collective-permute-start | bytes 786440 | tf_op jit(solution)/shard_map/ppermute | solution.py:532
  76.5 0.0 collective-permute-done.12.refs_3_
  76.5 3.6 %collective-permute-done.13.refs_7_ = bf16[512,256]{1,0:T(8,128)(2,1)S(1)} collective-permute-done((bf16[512,256]{1,0:T(8,128)(2,1)S(1)}, bf16[512,256]{1,0:T(8,128)(2,1)S(1)}, u32[]{:S(2)}, u32[]{:S(2)}) %collective-permute-start.13) | collective-permute-done | bytes 262176 | tf_op jit(solution)/shard_map/ppermute | solution.py:532
  80.1 5.1 %first.1.acc_in = f32[512,1280]{1,0:T(8,128)S(1)} custom-call(s32[6]{0:T(128)S(1)} %stack.31.where_ref, bf16[512,256]{1,0:T(8,128)(2,1)S(1)} %bitcast.12, bf16[512,256]{1,0:T(8,128)(2,1)S(1)} %collective-permute-done.11.refs_1_, bf16[512,256]{1,0:T(8,128)(2,1)S(1)} %collective-permute-done.10.refs_2_, bf16[512,256]{1,0:T(8,128)(2,1)S(1)} %collective-permute-done.12.refs_3_, ...), custom_call_target="tpu_custom_call" | custom-call | flops 1 | tf_op jit(solution)/shard_map/first/pallas_call | solution.py:453
  85.2 1.1 %second.3 = (bf16[4,64,640]{2,1,0:T(8,128)(2,1)S(1)}, bf16[4,64,640]{2,1,0:T(8,128)(2,1)S(1)}) custom-call(s32[6]{0:T(128)S(1)} %stack.31.where_ref, bf16[512,256]{1,0:T(8,128)(2,1)S(1)} %collective-permute-done.8.slot, bf16[512,256]{1,0:T(8,128)(2,1)S(1)} %collective-permute-done.9.more, bf16[512,1280]{1,0:T(8,128)(2,1)S(1)} %collective-permute-done.3.refs_9_.fetched_ref, ...), custom_call_target="tpu_custom_call" | custom-call | flops 1 | tf_op jit(solution)/shard_map/second/pallas_call | solution.py:485
  86.4 0.0 copy-start.4
  86.4 0.0 copy-start.5
  86.4 0.1 collective-permute-start.18
  86.5 1.1 %second.2 = (bf16[4,64,640]{2,1,0:T(8,128)(2,1)S(1)}, bf16[4,64,640]{2,1,0:T(8,128)(2,1)S(1)}) custom-call(s32[6]{0:T(128)S(1)} %stack.31.where_ref, bf16[512,256]{1,0:T(8,128)(2,1)S(1)} %collective-permute-done.8.slot, bf16[512,256]{1,0:T(8,128)(2,1)S(1)} %collective-permute-done.9.more, bf16[512,1280]{1,0:T(8,128)(2,1)S(1)} %collective-permute-done.3.refs_9_.fetched_ref, ...), custom_call_target="tpu_custom_call" | custom-call | flops 1 | tf_op jit(solution)/shard_map/second/pallas_call | solution.py:485
  87.6 0.6 collective-permute-start.14
  88.2 0.6 add.12
  88.8 1.9 %collective-permute-start.19 = (bf16[64,640]{1,0:T(8,128)(2,1)S(1)}, bf16[64,640]{1,0:T(8,128)(2,1)S(1)}, u32[]{:S(2)}, u32[]{:S(2)}) collective-permute-start(bf16[64,640]{1,0:T(8,128)(2,1)S(1)} %get-tuple-element.70), channel_id=1, source_target_pairs={{0,12},{4,8},{8,4},{12,0},{1,13},{5,9},{9,5},{13,1},{2,14},{6,10},... | collective-permute-start | bytes 245768 | tf_op jit(solution)/shard_map/ppermute | solution.py:46
  90.7 2.6 %collective-permute-start.21 = (bf16[64,640]{1,0:T(8,128)(2,1)S(1)}, bf16[64,640]{1,0:T(8,128)(2,1)S(1)}, u32[]{:S(2)}, u32[]{:S(2)}) collective-permute-start(bf16[64,640]{1,0:T(8,128)(2,1)S(1)} %get-tuple-element.72), channel_id=1, source_target_pairs={{0,4},{4,0},{8,12},{12,8},{1,5},{5,1},{9,13},{13,9},{2,6},{6,2},{1... | collective-permute-start | bytes 245768 | tf_op jit(solution)/shard_map/ppermute | solution.py:46
  93.3 0.6 add.11
  93.9 1.9 %collective-permute-start.15 = (bf16[64,640]{1,0:T(8,128)(2,1)S(1)}, bf16[64,640]{1,0:T(8,128)(2,1)S(1)}, u32[]{:S(2)}, u32[]{:S(2)}) collective-permute-start(bf16[64,640]{1,0:T(8,128)(2,1)S(1)} %get-tuple-element.64), channel_id=1, source_target_pairs={{0,12},{4,8},{8,4},{12,0},{1,13},{5,9},{9,5},{13,1},{2,14},{6,10},... | collective-permute-start | bytes 245768 | tf_op jit(solution)/shard_map/ppermute | solution.py:46
  95.8 0.3 collective-permute-done.19.refs_5_
  96.0 2.3 %collective-permute-start.17 = (bf16[64,640]{1,0:T(8,128)(2,1)S(1)}, bf16[64,640]{1,0:T(8,128)(2,1)S(1)}, u32[]{:S(2)}, u32[]{:S(2)}) collective-permute-start(bf16[64,640]{1,0:T(8,128)(2,1)S(1)} %get-tuple-element.66), channel_id=1, source_target_pairs={{0,4},{4,0},{8,12},{12,8},{1,5},{5,1},{9,13},{13,9},{2,6},{6,2},{1... | collective-permute-start | bytes 245768 | tf_op jit(solution)/shard_map/ppermute | solution.py:46
  98.4 3.0 %collective-permute-done.20.refs_6_ = bf16[64,640]{1,0:T(8,128)(2,1)S(1)} collective-permute-done((bf16[64,640]{1,0:T(8,128)(2,1)S(1)}, bf16[64,640]{1,0:T(8,128)(2,1)S(1)}, u32[]{:S(2)}, u32[]{:S(2)}) %collective-permute-start.20) | collective-permute-done | bytes 81952 | tf_op jit(solution)/shard_map/ppermute | solution.py:46
  101.3 4.3 %collective-permute-done.16.refs_2_ = bf16[64,640]{1,0:T(8,128)(2,1)S(1)} collective-permute-done((bf16[64,640]{1,0:T(8,128)(2,1)S(1)}, bf16[64,640]{1,0:T(8,128)(2,1)S(1)}, u32[]{:S(2)}, u32[]{:S(2)}) %collective-permute-start.16) | collective-permute-done | bytes 81952 | tf_op jit(solution)/shard_map/ppermute | solution.py:46
  105.6 1.6 %mix.1 = bf16[64,5120]{1,0:T(8,128)(2,1)} custom-call(s32[6]{0:T(128)S(1)} %stack.31.where_ref, bf16[64,5120]{1,0:T(8,128)(2,1)S(1)} %copy-done.4, f32[1,5120]{1,0:T(1,128)S(1)} %bitcast.13, bf16[64,640]{1,0:T(8,128)(2,1)S(1)} %get-tuple-element.63.refs_0_, bf16[64,640]{1,0:T(8,128)(2,1)S(1)} %collective-permute-done.15.refs_1_, ...), custom_call_target="tpu_custom_call" | custom-call | flops 1 | tf_op jit(solution)/shard_map/mix/pallas_call | solution.py:560
  (25 shorter events, 0.1 us)
Async XLA Ops:
  0.0 3.7 %copy-start.1 = (bf16[1024,1280]{1,0:T(8,128)(2,1)S(1)}, bf16[1024,1280]{1,0:T(8,128)(2,1)}, u32[]{:S(2)}) copy-start(bf16[1024,1280]{1,0:T(8,128)(2,1)} %refs_8_) | copy-start | bytes 7864324
  3.5 6.9 %copy-start.7 = (bf16[3,256,256]{2,1,0:T(8,128)(2,1)S(1)}, bf16[3,256,256]{2,1,0:T(8,128)(2,1)}, u32[]{:S(2)}) copy-start(bf16[3,256,256]{2,1,0:T(8,128)(2,1)} %get-tuple-element.39) | copy-start | bytes 1179652
  3.5 7.6 %copy-start.3 = (bf16[256,1024]{1,0:T(8,128)(2,1)S(1)}, bf16[256,1024]{1,0:T(8,128)(2,1)}, u32[]{:S(2)}) copy-start(bf16[256,1024]{1,0:T(8,128)(2,1)} %q_ref.3) | copy-start | bytes 1572868
  3.6 7.6 %copy-start.6 = (s32[2,2,8]{2,1,0:T(2,128)S(1)}, s32[2,2,8]{2,1,0:T(2,128)}, u32[]{:S(2)}) copy-start(s32[2,2,8]{2,1,0:T(2,128)} %exps_ref.3) | copy-start | bytes 388
  3.7 6.7 %copy-start.8 = (bf16[3,256,256]{2,1,0:T(8,128)(2,1)S(1)}, bf16[3,256,256]{2,1,0:T(8,128)(2,1)}, u32[]{:S(2)}) copy-start(bf16[3,256,256]{2,1,0:T(8,128)(2,1)} %get-tuple-element.40) | copy-start | bytes 1179652
  3.7 7.5 %copy-start.2 = (bf16[2,256,1024]{2,1,0:T(8,128)(2,1)S(1)}, bf16[2,256,1024]{2,1,0:T(8,128)(2,1)}, u32[]{:S(2)}) copy-start(bf16[2,256,1024]{2,1,0:T(8,128)(2,1)} %fresh_ref.3) | copy-start | bytes 3145732
  3.8 40.1 %collective-permute-start.3 = (bf16[512,1280]{1,0:T(8,128)(2,1)S(1)}, bf16[512,1280]{1,0:T(8,128)(2,1)S(1)}, u32[]{:S(2)}, u32[]{:S(2)}) collective-permute-start(bf16[512,1280]{1,0:T(8,128)(2,1)S(1)} %constant_dynamic-slice_fusion), channel_id=1, source_target_pairs={{0,2},{2,0},{1,3},{3,1},{4,6},{6,4},{5,7},{7,5},{8,10},{10,8},{9,1... | collective-permute-start | bytes 3932168 | tf_op jit(solution)/shard_map/ppermute | solution.py:46
  6.8 14.1 %collective-permute-start = (bf16[3,256,256]{2,1,0:T(8,128)(2,1)}, bf16[3,256,256]{2,1,0:T(8,128)(2,1)S(1)}, u32[]{:S(2)}, u32[]{:S(2)}) collective-permute-start(bf16[3,256,256]{2,1,0:T(8,128)(2,1)} %get-tuple-element.41), channel_id=1, source_target_pairs={{0,12},{4,8},{8,4},{12,0},{1,13},{5,9},{9,5},{13,1},{2,14},{6,10},... | collective-permute-start | bytes 1179656 | tf_op jit(solution)/shard_map/ppermute | solution.py:46
  10.4 33.5 %collective-permute-start.1 = (bf16[3,256,256]{2,1,0:T(8,128)(2,1)S(1)}, bf16[3,256,256]{2,1,0:T(8,128)(2,1)S(1)}, u32[]{:S(2)}, u32[]{:S(2)}) collective-permute-start(bf16[3,256,256]{2,1,0:T(8,128)(2,1)S(1)} %copy-done.8), channel_id=1, source_target_pairs={{0,8},{4,12},{8,0},{12,4},{1,9},{5,13},{9,1},{13,5},{2,10},{6,14},... | collective-permute-start | bytes 1179656 | tf_op jit(solution)/shard_map/ppermute | solution.py:46
  10.4 33.5 %collective-permute-start.2 = (bf16[3,256,256]{2,1,0:T(8,128)(2,1)S(1)}, bf16[3,256,256]{2,1,0:T(8,128)(2,1)S(1)}, u32[]{:S(2)}, u32[]{:S(2)}) collective-permute-start(bf16[3,256,256]{2,1,0:T(8,128)(2,1)S(1)} %copy-done.7), channel_id=1, source_target_pairs={{0,4},{4,0},{8,12},{12,8},{1,5},{5,1},{9,13},{13,9},{2,6},{6,2},{1... | collective-permute-start | bytes 1179656 | tf_op jit(solution)/shard_map/ppermute | solution.py:46
  11.2 2.2 %copy-start = (bf16[2,1024,1024]{2,1,0:T(8,128)(2,1)S(1)}, bf16[2,1024,1024]{2,1,0:T(8,128)(2,1)}, u32[]{:S(2)}) copy-start(bf16[2,1024,1024]{2,1,0:T(8,128)(2,1)} %cached_ref.3) | copy-start | bytes 12582916
  43.9 30.6 %collective-permute-start.7 = (bf16[512,1280]{1,0:T(8,128)(2,1)S(1)}, bf16[512,1280]{1,0:T(8,128)(2,1)S(1)}, u32[]{:S(2)}, u32[]{:S(2)}) collective-permute-start(bf16[512,1280]{1,0:T(8,128)(2,1)S(1)} %collective-permute-done.3.refs_9_.fetched_ref), channel_id=1, source_target_pairs={{0,16},{16,0},{1,17},{17,1},{2,18},{18,2},{3,19},{19,3},{4,20},{20... | collective-permute-start | bytes 3932168 | tf_op jit(solution)/shard_map/ppermute | solution.py:46
  49.2 7.1 %collective-permute-start.4 = (bf16[512,256]{1,0:T(8,128)(2,1)S(1)}, bf16[512,256]{1,0:T(8,128)(2,1)S(1)}, u32[]{:S(2)}, u32[]{:S(2)}) collective-permute-start(bf16[512,256]{1,0:T(8,128)(2,1)S(1)} %bitcast.14), channel_id=1, source_target_pairs={{0,2},{2,0},{1,3},{3,1},{4,6},{6,4},{5,7},{7,5},{8,10},{10,8},{9,1... | collective-permute-start | bytes 786440 | tf_op jit(solution)/shard_map/ppermute | solution.py:46
  49.8 15.8 %collective-permute-start.10 = (bf16[512,256]{1,0:T(8,128)(2,1)S(1)}, bf16[512,256]{1,0:T(8,128)(2,1)S(1)}, u32[]{:S(2)}, u32[]{:S(2)}) collective-permute-start(bf16[512,256]{1,0:T(8,128)(2,1)S(1)} %bitcast.9), channel_id=1, source_target_pairs={{0,8},{4,12},{8,0},{12,4},{1,9},{5,13},{9,1},{13,5},{2,10},{6,14},... | collective-permute-start | bytes 786440 | tf_op jit(solution)/shard_map/ppermute | solution.py:46
  49.8 15.8 %collective-permute-start.11 = (bf16[512,256]{1,0:T(8,128)(2,1)S(1)}, bf16[512,256]{1,0:T(8,128)(2,1)S(1)}, u32[]{:S(2)}, u32[]{:S(2)}) collective-permute-start(bf16[512,256]{1,0:T(8,128)(2,1)S(1)} %bitcast.10), channel_id=1, source_target_pairs={{0,4},{4,0},{8,12},{12,8},{1,5},{5,1},{9,13},{13,9},{2,6},{6,2},{1... | collective-permute-start | bytes 786440 | tf_op jit(solution)/shard_map/ppermute | solution.py:46
  56.3 17.5 %collective-permute-start.5 = (bf16[512,256]{1,0:T(8,128)(2,1)S(1)}, bf16[512,256]{1,0:T(8,128)(2,1)S(1)}, u32[]{:S(2)}, u32[]{:S(2)}) collective-permute-start(bf16[512,256]{1,0:T(8,128)(2,1)S(1)} %collective-permute-done.4.refs_4_), channel_id=1, source_target_pairs={{0,8},{4,12},{8,0},{12,4},{1,9},{5,13},{9,1},{13,5},{2,10},{6,14},... | collective-permute-start | bytes 786440 | tf_op jit(solution)/shard_map/ppermute | solution.py:46
  56.3 18.2 %collective-permute-start.6 = (bf16[512,256]{1,0:T(8,128)(2,1)S(1)}, bf16[512,256]{1,0:T(8,128)(2,1)S(1)}, u32[]{:S(2)}, u32[]{:S(2)}) collective-permute-start(bf16[512,256]{1,0:T(8,128)(2,1)S(1)} %collective-permute-done.4.refs_4_), channel_id=1, source_target_pairs={{0,4},{4,0},{8,12},{12,8},{1,5},{5,1},{9,13},{13,9},{2,6},{6,2},{1... | collective-permute-start | bytes 786440 | tf_op jit(solution)/shard_map/ppermute | solution.py:46
  65.6 10.9 %collective-permute-start.12 = (bf16[512,256]{1,0:T(8,128)(2,1)S(1)}, bf16[512,256]{1,0:T(8,128)(2,1)S(1)}, u32[]{:S(2)}, u32[]{:S(2)}) collective-permute-start(bf16[512,256]{1,0:T(8,128)(2,1)S(1)} %bitcast.11), channel_id=1, source_target_pairs={{4,8},{8,4},{5,9},{9,5},{6,10},{10,6},{7,11},{11,7},{20,24},{24,20... | collective-permute-start | bytes 786440 | tf_op jit(solution)/shard_map/ppermute | solution.py:46
  66.2 13.8 %collective-permute-start.13 = (bf16[512,256]{1,0:T(8,128)(2,1)S(1)}, bf16[512,256]{1,0:T(8,128)(2,1)S(1)}, u32[]{:S(2)}, u32[]{:S(2)}) collective-permute-start(bf16[512,256]{1,0:T(8,128)(2,1)S(1)} %collective-permute-done.10.refs_2_), channel_id=1, source_target_pairs={{4,0},{8,12},{5,1},{9,13},{6,2},{10,14},{7,3},{11,15},{20,16},{24,... | collective-permute-start | bytes 786440 | tf_op jit(solution)/shard_map/ppermute | solution.py:532
  74.5 10.7 %collective-permute-start.8 = (bf16[512,256]{1,0:T(8,128)(2,1)S(1)}, bf16[512,256]{1,0:T(8,128)(2,1)S(1)}, u32[]{:S(2)}, u32[]{:S(2)}) collective-permute-start(bf16[512,256]{1,0:T(8,128)(2,1)S(1)} %collective-permute-done.4.refs_4_), channel_id=1, source_target_pairs={{4,8},{8,4},{5,9},{9,5},{6,10},{10,6},{7,11},{11,7},{20,24},{24,20... | collective-permute-start | bytes 786440 | tf_op jit(solution)/shard_map/ppermute | solution.py:46
  75.2 10.1 %collective-permute-start.9 = (bf16[512,256]{1,0:T(8,128)(2,1)S(1)}, bf16[512,256]{1,0:T(8,128)(2,1)S(1)}, u32[]{:S(2)}, u32[]{:S(2)}) collective-permute-start(bf16[512,256]{1,0:T(8,128)(2,1)S(1)} %collective-permute-done.5.refs_6_), channel_id=1, source_target_pairs={{4,0},{8,12},{5,1},{9,13},{6,2},{10,14},{7,3},{11,15},{20,16},{24,... | collective-permute-start | bytes 786440 | tf_op jit(solution)/shard_map/ppermute | solution.py:532
  86.4 19.2 %copy-start.4 = (bf16[64,5120]{1,0:T(8,128)(2,1)S(1)}, bf16[64,5120]{1,0:T(8,128)(2,1)}, u32[]{:S(2)}) copy-start(bf16[64,5120]{1,0:T(8,128)(2,1)} %hidden_ref.1) | copy-start | bytes 1966084
  86.4 19.2 %copy-start.5 = (f32[5120]{0:T(1024)S(1)}, f32[5120]{0:T(1024)}, u32[]{:S(2)}) copy-start(f32[5120]{0:T(1024)} %param.13) | copy-start | bytes 61444
  86.4 1.8 %collective-permute-start.18 = (bf16[4,64,640]{2,1,0:T(8,128)(2,1)S(1)}, bf16[4,64,640]{2,1,0:T(8,128)(2,1)S(1)}, u32[]{:S(2)}, u32[]{:S(2)}) collective-permute-start(bf16[4,64,640]{2,1,0:T(8,128)(2,1)S(1)} %get-tuple-element.68), channel_id=1, source_target_pairs={{0,1},{1,0},{2,3},{3,2},{4,5},{5,4},{6,7},{7,6},{8,9},{9,8},{10,11... | collective-permute-start | bytes 983048 | tf_op jit(solution)/shard_map/ppermute | solution.py:46
  87.6 5.6 %collective-permute-start.14 = (bf16[4,64,640]{2,1,0:T(8,128)(2,1)S(1)}, bf16[4,64,640]{2,1,0:T(8,128)(2,1)S(1)}, u32[]{:S(2)}, u32[]{:S(2)}) collective-permute-start(bf16[4,64,640]{2,1,0:T(8,128)(2,1)S(1)} %get-tuple-element.62), channel_id=1, source_target_pairs={{0,1},{1,0},{2,3},{3,2},{4,5},{5,4},{6,7},{7,6},{8,9},{9,8},{10,11... | collective-permute-start | bytes 983048 | tf_op jit(solution)/shard_map/ppermute | solution.py:46
  88.8 7.2 %collective-permute-start.19 = (bf16[64,640]{1,0:T(8,128)(2,1)S(1)}, bf16[64,640]{1,0:T(8,128)(2,1)S(1)}, u32[]{:S(2)}, u32[]{:S(2)}) collective-permute-start(bf16[64,640]{1,0:T(8,128)(2,1)S(1)} %get-tuple-element.70), channel_id=1, source_target_pairs={{0,12},{4,8},{8,4},{12,0},{1,13},{5,9},{9,5},{13,1},{2,14},{6,10},... | collective-permute-start | bytes 245768 | tf_op jit(solution)/shard_map/ppermute | solution.py:46
  90.7 10.6 %collective-permute-start.20 = (bf16[64,640]{1,0:T(8,128)(2,1)S(1)}, bf16[64,640]{1,0:T(8,128)(2,1)S(1)}, u32[]{:S(2)}, u32[]{:S(2)}) collective-permute-start(bf16[64,640]{1,0:T(8,128)(2,1)S(1)} %get-tuple-element.71), channel_id=1, source_target_pairs={{0,8},{4,12},{8,0},{12,4},{1,9},{5,13},{9,1},{13,5},{2,10},{6,14},... | collective-permute-start | bytes 245768 | tf_op jit(solution)/shard_map/ppermute | solution.py:46
  90.7 10.6 %collective-permute-start.21 = (bf16[64,640]{1,0:T(8,128)(2,1)S(1)}, bf16[64,640]{1,0:T(8,128)(2,1)S(1)}, u32[]{:S(2)}, u32[]{:S(2)}) collective-permute-start(bf16[64,640]{1,0:T(8,128)(2,1)S(1)} %get-tuple-element.72), channel_id=1, source_target_pairs={{0,4},{4,0},{8,12},{12,8},{1,5},{5,1},{9,13},{13,9},{2,6},{6,2},{1... | collective-permute-start | bytes 245768 | tf_op jit(solution)/shard_map/ppermute | solution.py:46
  93.9 7.4 %collective-permute-start.15 = (bf16[64,640]{1,0:T(8,128)(2,1)S(1)}, bf16[64,640]{1,0:T(8,128)(2,1)S(1)}, u32[]{:S(2)}, u32[]{:S(2)}) collective-permute-start(bf16[64,640]{1,0:T(8,128)(2,1)S(1)} %get-tuple-element.64), channel_id=1, source_target_pairs={{0,12},{4,8},{8,4},{12,0},{1,13},{5,9},{9,5},{13,1},{2,14},{6,10},... | collective-permute-start | bytes 245768 | tf_op jit(solution)/shard_map/ppermute | solution.py:46
  95.8 9.8 %collective-permute-start.16 = (bf16[64,640]{1,0:T(8,128)(2,1)S(1)}, bf16[64,640]{1,0:T(8,128)(2,1)S(1)}, u32[]{:S(2)}, u32[]{:S(2)}) collective-permute-start(bf16[64,640]{1,0:T(8,128)(2,1)S(1)} %get-tuple-element.65), channel_id=1, source_target_pairs={{0,8},{4,12},{8,0},{12,4},{1,9},{5,13},{9,1},{13,5},{2,10},{6,14},... | collective-permute-start | bytes 245768 | tf_op jit(solution)/shard_map/ppermute | solution.py:46
  96.0 9.6 %collective-permute-start.17 = (bf16[64,640]{1,0:T(8,128)(2,1)S(1)}, bf16[64,640]{1,0:T(8,128)(2,1)S(1)}, u32[]{:S(2)}, u32[]{:S(2)}) collective-permute-start(bf16[64,640]{1,0:T(8,128)(2,1)S(1)} %get-tuple-element.66), channel_id=1, source_target_pairs={{0,4},{4,0},{8,12},{12,8},{1,5},{5,1},{9,13},{13,9},{2,6},{6,2},{1... | collective-permute-start | bytes 245768 | tf_op jit(solution)/shard_map/ppermute | solution.py:46

commit v12 on v11

--- a/solution.py
+++ b/solution.py
@@ -415,72 +415,55 @@
 
 
 def first_kernel(where_ref, *refs):
-    slots, (more, own_ref, fetched_ref, passed_ref, out_ref, held_ref) = refs[:7], refs[7:]
-    feat = slots[0].shape[1]
+    slots, (more, own_ref, partner_ref, out_ref, held_ref) = refs[:7], refs[7:]
+    rows, feat = slots[0].shape
+    depth = own_ref.shape[0]
 
     @pl.when(pl.program_id(0) == 0)
     def arrange():
-        for at, slot in enumerate(slots):
-            block = slot[...]
-            if at == 3:
+        for index in range(8):
+            half, at = divmod(index, 4)
+            if index == 7:
+                block = jnp.zeros((rows, feat), jnp.bfloat16)
+            else:
+                block = slots[index][...]
+            if index == 3:
                 block = jnp.where(where_ref[INNER] == 1, block, more[...])
-            place = where_ref[NEAR] ^ (at % 4)
-            if at >= 4:
-                place = 4 + (2 * ((place // 2) ^ where_ref[GRP]) + place % 2)
-            held_ref[:, pl.ds(pl.multiple_of(place * feat, HEAD_DIM), feat)] = block
-        place = where_ref[NEAR] ^ 3
-        place = 4 + (2 * ((place // 2) ^ where_ref[GRP]) + place % 2)
-        held_ref[:, pl.ds(pl.multiple_of(place * feat, HEAD_DIM), feat)] = jnp.zeros(
-            (slots[0].shape[0], feat), jnp.bfloat16
-        )
-
-    depth = 4 * feat
+            lane = half * depth + (where_ref[NEAR] ^ at) * feat
+            held_ref[:, pl.ds(pl.multiple_of(lane, HEAD_DIM), feat)] = block
+
     acc = jnp.dot(held_ref[:, :depth], own_ref[...], preferred_element_type=jnp.float32)
-    half = depth // 2
-    for at, weight in enumerate((fetched_ref, passed_ref)):
-        acc += jnp.dot(
-            held_ref[:, depth + at * half : depth + (at + 1) * half],
-            weight[...],
-            preferred_element_type=jnp.float32,
-        )
+    acc += jnp.dot(held_ref[:, depth:], partner_ref[...], preferred_element_type=jnp.float32)
     out_ref[...] = acc
 
 
 def first_product(where, slots, more, weights):
     rows, feat = slots[0].shape
-    cols = weights[0].shape[1]
+    depth, cols = weights[0].shape
     wide = cols // 2
     return call(
         first_kernel,
         "first",
         jax.ShapeDtypeStruct((rows, cols), jnp.float32),
         2,
-        [spec((rows, feat))] * 8
-        + [pl.BlockSpec((x.shape[0], wide), lambda i, w: (0, i)) for x in weights],
+        [spec((rows, feat))] * 8 + [pl.BlockSpec((depth, wide), lambda i, w: (0, i))] * 2,
         pl.BlockSpec((rows, wide), lambda i, w: (0, i)),
-        [pltpu.VMEM((rows, 8 * feat), jnp.bfloat16)],
+        [pltpu.VMEM((rows, 2 * depth), jnp.bfloat16)],
     )(where, *slots, more, *weights)
 
 
-def second_kernel(where_ref, slot, more, fetched_ref, passed_ref, acc_in, keep_ref, send_ref, acc_ref):
-    feat = slot.shape[1]
-    place = where_ref[NEAR] ^ 3
-    rows = pl.ds(pl.multiple_of((place % 2) * feat, HEAD_DIM), feat)
-    weight = jnp.where(
-        (place // 2) == where_ref[GRP], fetched_ref[rows, :], passed_ref[rows, :]
-    )
+def second_kernel(where_ref, slot, more, weight_ref, acc_in, keep_ref, send_ref, acc_ref):
     block = jnp.where(where_ref[INNER] == 1, slot[...], more[...])
-    acc = acc_in[...] + jnp.dot(block, weight, preferred_element_type=jnp.float32)
+    acc = acc_in[...] + jnp.dot(block, weight_ref[...], preferred_element_type=jnp.float32)
     acc_ref[...] = acc.reshape(acc_ref.shape)
     for sub, out in enumerate((keep_ref, send_ref)):
         for at in range(4):
             out[at] = acc_ref[where_ref[NEAR] ^ at, where_ref[SUB] ^ sub].astype(jnp.bfloat16)
 
 
-def second_product(where, chunk, slot, more, weights, acc):
+def second_product(where, chunk, slot, more, weight, acc):
     rows, feat = slot.shape
-    depth, cols = weights[0].shape
-    wide = cols // 2
+    wide = weight.shape[1] // 2
     out = jax.ShapeDtypeStruct((4, rows // 8, wide), jnp.bfloat16)
     return call(
         second_kernel,
@@ -488,11 +471,11 @@
         [out] * 2,
         1,
         [spec((rows, feat))] * 2
-        + [pl.BlockSpec((depth, wide), lambda i, w: (0, chunk))] * 2
+        + [pl.BlockSpec((feat, wide), lambda i, w: (w[NEAR] ^ 3, chunk))]
         + [pl.BlockSpec((rows, wide), lambda i, w: (0, chunk))],
         [spec(out.shape)] * 2,
         [pltpu.VMEM((4, 2, rows // 8, wide), jnp.float32)],
-    )(where, slot, more, *weights, acc)
+    )(where, slot, more, weight, acc)
 
 
 def add_kernel(where_ref, keep_ref, term_ref, *outs):
@@ -513,12 +496,7 @@
 
 
 def share_tail(sizes, where, pieces, kv_pieces, out_weight, hidden_in, attn_gate):
-    half = out_weight.shape[0] // 2
-    out_weight, where = lax.optimization_barrier((out_weight, where))
-    start = lax.axis_index("grp") * half
-    fetched = swap(lax.dynamic_slice_in_dim(out_weight, start, half, 0), "head", 2, 1)
-    pieces, fetched = lax.optimization_barrier((pieces, fetched))
-    passed = swap(fetched, "grp", 2, 1)
+    fetched = swap(out_weight, "head", 2, 1)
 
     mine, other = attend_halves(where, pieces)
     other = swap(other, "head", 2, 1)
@@ -527,13 +505,13 @@
         far, next_to = swap(x, "patch", 4, 2), swap(x, "patch", 4, 1)
         far, next_to, other, x = lax.optimization_barrier((far, next_to, other, x))
         if at == 1:
-            far, x, passed = lax.optimization_barrier((far, x, passed))
+            far, x, fetched = lax.optimization_barrier((far, x, fetched))
         middle = swap(x, "patch", 4, 3, (1, 2))
         ends = lax.ppermute(far, "patch", [(1, 0), (2, 3)])
         slots.append([x, next_to, far, middle, ends])
     first = [*slots[0][:4], *slots[1][:3]]
-    acc = first_product(where, first, slots[0][4], [out_weight, fetched, passed])
-    terms = [second_product(where, at, *slots[1][3:], [fetched, passed], acc) for at in range(2)]
+    acc = first_product(where, first, slots[0][4], [out_weight, fetched])
+    terms = [second_product(where, at, *slots[1][3:], fetched, acc) for at in range(2)]
     blocks = []
     for keep, send in terms:
         total = add(where, keep, swap(send, "sub", 2, 1))

time: 107 us -> 114 us (1.065)
  waiting for transfers between devices: 57.5 us -> 61.7 us
    ppermute x20 -> x19, waiting for transfers between devices: 53.8 us -> 58.9 us  [swap(): return lax.ppermute(x, axes, pairs)]
    unnamed x18 -> x14, local copies, waits for them, and re-layouts: 2.23 us -> 3.43 us
    ppermute x20 -> x19, starting transfers between devices: 25.7 us -> 26.3 us  [swap(): return lax.ppermute(x, axes, pairs)]
  transfers between devices with their start and end apart: 22 -> 21, of which waited for: 10 -> 9; matrix products, arithmetic and copies ran while one was open for 0% -> 0% of each run, Pallas kernels for 12% -> 15%
where the time goes in v12:
time: 114 us
  waiting for transfers between devices  61.7 us (54%)
  starting transfers between devices  28.9 us (25%)
  Pallas kernels  19.3 us (17%)
  local copies, waits for them, and re-layouts  3.51 us (3%)
    ppermute x19, waiting for transfers between devices, swap(): return lax.ppermute(x, axes, pairs)  58.9 us
    ppermute x19, starting transfers between devices, swap(): return lax.ppermute(x, axes, pairs)  26.3 us
    pallas_call x1, Pallas kernels, first_product(): call(first_kernel, 'first', jax.ShapeDtypeStruct((rows, cols), jnp.float3...  5.07 us
    pallas_call x1, Pallas kernels, attend_halves(): call(attend_halves_kernel, 'attend', [out] * 2, 1, [spec((3, tok, feat))]...  4.77 us
    unnamed x14, local copies, waits for them, and re-layouts  3.43 us
    pallas_call x1, Pallas kernels, pack(): pl.pallas_call(functools.partial(pack_kernel, split, feat // HEAD_DIM), o...  3.39 us
    ppermute x2, waiting for transfers between devices, share_tail(): ends = lax.ppermute(far, 'patch', [(1, 0), (2, 3)])  2.82 us
    ppermute x2, starting transfers between devices, share_tail(): ends = lax.ppermute(far, 'patch', [(1, 0), (2, 3)])  2.58 us
  transfers between devices with their start and end apart: 21, of which 9 were waited for; matrix products, arithmetic and copies ran while one was open for 0% of the time, Pallas kernels for 15%

profile of v12, /device:TPU:0, one launch (start us, length us, event | category | flops | bytes accessed | tf_op | source)
XLA Modules:
  0.0 113.6 jit_solution(5098950100687278452)
XLA Ops:
  0.0 2.9 %collective-permute-start.6 = (bf16[1024,1280]{1,0:T(8,128)(2,1)}, bf16[1024,1280]{1,0:T(8,128)(2,1)S(1)}, u32[]{:S(2)}, u32[]{:S(2)}) collective-permute-start(bf16[1024,1280]{1,0:T(8,128)(2,1)} %refs_8_.1), channel_id=1, source_target_pairs={{0,2},{2,0},{1,3},{3,1},{4,6},{6,4},{5,7},{7,5},{8,10},{10,8},{9,1... | collective-permute-start | bytes 7864328 | tf_op jit(solution)/shard_map/ppermute | solution.py:46
  2.9 3.4 %pack.1 = (bf16[3,256,256]{2,1,0:T(8,128)(2,1)}, bf16[3,256,256]{2,1,0:T(8,128)(2,1)}, bf16[3,256,256]{2,1,0:T(8,128)(2,1)}) custom-call(s32[2,2,8]{2,1,0:T(2,128)} %exps_ref.3, bf16[256,1024]{1,0:T(8,128)(2,1)} %q_ref.3, bf16[2,256,1024]{2,1,0:T(8,128)(2,1)} %fresh_ref.3, bf16[2,1024,1024]{2,1,0:T(8,128)(2,1)} %cached_ref.3), custom_call_target="tpu_custom_call" | custom-call | tf_op jit(solution)/shard_map/pack/pallas_call | solution.py:108
  6.3 3.7 %collective-permute-start = (bf16[3,256,256]{2,1,0:T(8,128)(2,1)}, bf16[3,256,256]{2,1,0:T(8,128)(2,1)S(1)}, u32[]{:S(2)}, u32[]{:S(2)}) collective-permute-start(bf16[3,256,256]{2,1,0:T(8,128)(2,1)} %get-tuple-element.34), channel_id=1, source_target_pairs={{0,12},{4,8},{8,4},{12,0},{1,13},{5,9},{9,5},{13,1},{2,14},{6,10},... | collective-permute-start | bytes 1179656 | tf_op jit(solution)/shard_map/ppermute | solution.py:46
  10.0 0.8 collective-permute-start.2
  10.8 0.1 stack.31.where_ref
  10.9 0.0 copy-start
  10.9 2.2 %copy-done = bf16[2,1024,1024]{2,1,0:T(8,128)(2,1)S(1)} copy-done((bf16[2,1024,1024]{2,1,0:T(8,128)(2,1)S(1)}, bf16[2,1024,1024]{2,1,0:T(8,128)(2,1)}, u32[]{:S(2)}) %copy-start) | copy-done | bytes 4194328
  13.1 1.2 %copy-done.1 = bf16[2,256,1024]{2,1,0:T(8,128)(2,1)S(1)} copy-done((bf16[2,256,1024]{2,1,0:T(8,128)(2,1)S(1)}, bf16[2,256,1024]{2,1,0:T(8,128)(2,1)}, u32[]{:S(2)}) %copy-start.1) | copy-done | bytes 1048600
  14.3 1.3 %own.1.refs_0_ = bf16[3,256,256]{2,1,0:T(8,128)(2,1)S(1)} custom-call(s32[6]{0:T(128)S(1)} %stack.31.where_ref, s32[2,2,8]{2,1,0:T(2,128)S(1)} %copy-done.6, bf16[256,1024]{1,0:T(8,128)(2,1)S(1)} %copy-done.3, bf16[2,256,1024]{2,1,0:T(8,128)(2,1)S(1)} %copy-done.1, bf16[2,1024,1024]{2,1,0:T(8,128)(2,1)S(1)} %copy-done), custom_call_target="tpu_custom_call" | custom-call | flops 1 | tf_op jit(solution)/shard_map/own/pallas_call | solution.py:144
  15.6 5.0 %collective-permute-done.refs_1_ = bf16[3,256,256]{2,1,0:T(8,128)(2,1)S(1)} collective-permute-done((bf16[3,256,256]{2,1,0:T(8,128)(2,1)}, bf16[3,256,256]{2,1,0:T(8,128)(2,1)S(1)}, u32[]{:S(2)}, u32[]{:S(2)}) %collective-permute-start) | collective-permute-done | bytes 393248 | tf_op jit(solution)/shard_map/ppermute | solution.py:46
  20.6 23.0 %collective-permute-done.1.refs_2_ = bf16[3,256,256]{2,1,0:T(8,128)(2,1)} collective-permute-done((bf16[3,256,256]{2,1,0:T(8,128)(2,1)}, bf16[3,256,256]{2,1,0:T(8,128)(2,1)}, u32[]{:S(2)}, u32[]{:S(2)}) %collective-permute-start.1) | collective-permute-done | bytes 393248 | tf_op jit(solution)/shard_map/ppermute | solution.py:46
  43.6 0.0 collective-permute-done.2.refs_3_
  43.6 4.8 %attend.1 = (bf16[4,128,256]{2,1,0:T(8,128)(2,1)S(1)}, bf16[4,128,256]{2,1,0:T(8,128)(2,1)S(1)}) custom-call(s32[6]{0:T(128)S(1)} %stack.31.where_ref, bf16[3,256,256]{2,1,0:T(8,128)(2,1)S(1)} %own.1.refs_0_, bf16[3,256,256]{2,1,0:T(8,128)(2,1)S(1)} %collective-permute-done.refs_1_, bf16[3,256,256]{2,1,0:T(8,128)(2,1)} %collective-permute-done.1.refs_2_, ...), custom_call_target="tpu_custom_call" | custom-call | flops 1 | tf_op jit(solution)/shard_map/attend/pallas_call | solution.py:406
  48.4 0.6 collective-permute-start.3
  49.0 3.0 %collective-permute-start.9 = (bf16[512,256]{1,0:T(8,128)(2,1)S(1)}, bf16[512,256]{1,0:T(8,128)(2,1)S(1)}, u32[]{:S(2)}, u32[]{:S(2)}) collective-permute-start(bf16[512,256]{1,0:T(8,128)(2,1)S(1)} %bitcast.10), channel_id=1, source_target_pairs={{0,8},{4,12},{8,0},{12,4},{1,9},{5,13},{9,1},{13,5},{2,10},{6,14},... | collective-permute-start | bytes 786440 | tf_op jit(solution)/shard_map/ppermute | solution.py:46
  52.0 13.6 %collective-permute-done.3.refs_4_ = bf16[512,256]{1,0:T(8,128)(2,1)S(1)} collective-permute-done((bf16[512,256]{1,0:T(8,128)(2,1)S(1)}, bf16[512,256]{1,0:T(8,128)(2,1)S(1)}, u32[]{:S(2)}, u32[]{:S(2)}) %collective-permute-start.3) | collective-permute-done | bytes 262176 | tf_op jit(solution)/shard_map/ppermute | solution.py:46
  65.6 2.8 %collective-permute-start.4 = (bf16[512,256]{1,0:T(8,128)(2,1)S(1)}, bf16[512,256]{1,0:T(8,128)(2,1)S(1)}, u32[]{:S(2)}, u32[]{:S(2)}) collective-permute-start(bf16[512,256]{1,0:T(8,128)(2,1)S(1)} %collective-permute-done.3.refs_4_), channel_id=1, source_target_pairs={{0,8},{4,12},{8,0},{12,4},{1,9},{5,13},{9,1},{13,5},{2,10},{6,14},... | collective-permute-start | bytes 786440 | tf_op jit(solution)/shard_map/ppermute | solution.py:46
  68.5 1.6 %collective-permute-start.5 = (bf16[512,256]{1,0:T(8,128)(2,1)S(1)}, bf16[512,256]{1,0:T(8,128)(2,1)S(1)}, u32[]{:S(2)}, u32[]{:S(2)}) collective-permute-start(bf16[512,256]{1,0:T(8,128)(2,1)S(1)} %collective-permute-done.3.refs_4_), channel_id=1, source_target_pairs={{0,4},{4,0},{8,12},{12,8},{1,5},{5,1},{9,13},{13,9},{2,6},{6,2},{1... | collective-permute-start | bytes 786440 | tf_op jit(solution)/shard_map/ppermute | solution.py:46
  70.1 0.0 collective-permute-done.10.refs_1_
  70.1 0.7 collective-permute-start.11
  70.7 1.3 %collective-permute-start.12 = (bf16[512,256]{1,0:T(8,128)(2,1)S(1)}, bf16[512,256]{1,0:T(8,128)(2,1)S(1)}, u32[]{:S(2)}, u32[]{:S(2)}) collective-permute-start(bf16[512,256]{1,0:T(8,128)(2,1)S(1)} %collective-permute-done.9.refs_2_), channel_id=1, source_target_pairs={{4,0},{8,12},{5,1},{9,13},{6,2},{10,14},{7,3},{11,15},{20,16},{24,... | collective-permute-start | bytes 786440 | tf_op jit(solution)/shard_map/ppermute | solution.py:510
  72.0 8.8 %collective-permute-done.4.refs_6_ = bf16[512,256]{1,0:T(8,128)(2,1)S(1)} collective-permute-done((bf16[512,256]{1,0:T(8,128)(2,1)S(1)}, bf16[512,256]{1,0:T(8,128)(2,1)S(1)}, u32[]{:S(2)}, u32[]{:S(2)}) %collective-permute-start.4) | collective-permute-done | bytes 262176 | tf_op jit(solution)/shard_map/ppermute | solution.py:46
  80.8 1.1 collective-permute-done.5.refs_5_
  81.9 0.7 collective-permute-start.7
  82.6 1.3 %collective-permute-start.8 = (bf16[512,256]{1,0:T(8,128)(2,1)S(1)}, bf16[512,256]{1,0:T(8,128)(2,1)S(1)}, u32[]{:S(2)}, u32[]{:S(2)}) collective-permute-start(bf16[512,256]{1,0:T(8,128)(2,1)S(1)} %collective-permute-done.4.refs_6_), channel_id=1, source_target_pairs={{4,0},{8,12},{5,1},{9,13},{6,2},{10,14},{7,3},{11,15},{20,16},{24,... | collective-permute-start | bytes 786440 | tf_op jit(solution)/shard_map/ppermute | solution.py:510
  83.9 0.0 collective-permute-done.11.refs_3_
  83.9 2.8 %collective-permute-done.12.refs_7_ = bf16[512,256]{1,0:T(8,128)(2,1)S(1)} collective-permute-done((bf16[512,256]{1,0:T(8,128)(2,1)S(1)}, bf16[512,256]{1,0:T(8,128)(2,1)S(1)}, u32[]{:S(2)}, u32[]{:S(2)}) %collective-permute-start.12) | collective-permute-done | bytes 262176 | tf_op jit(solution)/shard_map/ppermute | solution.py:510
  86.7 5.1 %first.1.acc_in = f32[512,1280]{1,0:T(8,128)S(1)} custom-call(s32[6]{0:T(128)S(1)} %stack.31.where_ref, bf16[512,256]{1,0:T(8,128)(2,1)S(1)} %bitcast.12, bf16[512,256]{1,0:T(8,128)(2,1)S(1)} %collective-permute-done.10.refs_1_, bf16[512,256]{1,0:T(8,128)(2,1)S(1)} %collective-permute-done.9.refs_2_, bf16[512,256]{1,0:T(8,128)(2,1)S(1)} %collective-permute-done.11.refs_3_, ...), custom_call_target="tpu_custom_call" | custom-call | flops 1 | tf_op jit(solution)/shard_map/first/pallas_call | solution.py:444
  91.8 0.0 collective-permute-done.7.slot
  91.8 1.0 second.3
  92.8 0.0 copy-start.4
  92.8 0.0 copy-start.5
  92.8 0.1 collective-permute-start.17
  92.9 1.0 second.2
  93.9 0.6 collective-permute-start.13
  94.4 0.1 collective-permute-done.17.term_ref
  94.5 0.6 add.8
  95.1 2.2 %collective-permute-start.18 = (bf16[64,640]{1,0:T(8,128)(2,1)S(1)}, bf16[64,640]{1,0:T(8,128)(2,1)S(1)}, u32[]{:S(2)}, u32[]{:S(2)}) collective-permute-start(bf16[64,640]{1,0:T(8,128)(2,1)S(1)} %get-tuple-element.56), channel_id=1, source_target_pairs={{0,12},{4,8},{8,4},{12,0},{1,13},{5,9},{9,5},{13,1},{2,14},{6,10},... | collective-permute-start | bytes 245768 | tf_op jit(solution)/shard_map/ppermute | solution.py:46
  97.3 0.0 collective-permute-start.19
  97.3 2.3 %collective-permute-start.20 = (bf16[64,640]{1,0:T(8,128)(2,1)S(1)}, bf16[64,640]{1,0:T(8,128)(2,1)S(1)}, u32[]{:S(2)}, u32[]{:S(2)}) collective-permute-start(bf16[64,640]{1,0:T(8,128)(2,1)S(1)} %get-tuple-element.58), channel_id=1, source_target_pairs={{0,4},{4,0},{8,12},{12,8},{1,5},{5,1},{9,13},{13,9},{2,6},{6,2},{1... | collective-permute-start | bytes 245768 | tf_op jit(solution)/shard_map/ppermute | solution.py:46
  99.6 0.6 add.7
  100.2 2.2 %collective-permute-start.14 = (bf16[64,640]{1,0:T(8,128)(2,1)S(1)}, bf16[64,640]{1,0:T(8,128)(2,1)S(1)}, u32[]{:S(2)}, u32[]{:S(2)}) collective-permute-start(bf16[64,640]{1,0:T(8,128)(2,1)S(1)} %get-tuple-element.50), channel_id=1, source_target_pairs={{0,12},{4,8},{8,4},{12,0},{1,13},{5,9},{9,5},{13,1},{2,14},{6,10},... | collective-permute-start | bytes 245768 | tf_op jit(solution)/shard_map/ppermute | solution.py:46
  102.4 2.3 %collective-permute-start.16 = (bf16[64,640]{1,0:T(8,128)(2,1)S(1)}, bf16[64,640]{1,0:T(8,128)(2,1)S(1)}, u32[]{:S(2)}, u32[]{:S(2)}) collective-permute-start(bf16[64,640]{1,0:T(8,128)(2,1)S(1)} %get-tuple-element.52), channel_id=1, source_target_pairs={{0,4},{4,0},{8,12},{12,8},{1,5},{5,1},{9,13},{13,9},{2,6},{6,2},{1... | collective-permute-start | bytes 245768 | tf_op jit(solution)/shard_map/ppermute | solution.py:46
  104.7 3.2 %collective-permute-done.19.refs_6_ = bf16[64,640]{1,0:T(8,128)(2,1)S(1)} collective-permute-done((bf16[64,640]{1,0:T(8,128)(2,1)S(1)}, bf16[64,640]{1,0:T(8,128)(2,1)S(1)}, u32[]{:S(2)}, u32[]{:S(2)}) %collective-permute-start.19) | collective-permute-done | bytes 81952 | tf_op jit(solution)/shard_map/ppermute | solution.py:46
  107.8 0.0 collective-permute-done.20.refs_7_
  107.8 0.0 collective-permute-done.14.refs_1_
  107.8 4.2 %collective-permute-done.15.refs_2_ = bf16[64,640]{1,0:T(8,128)(2,1)S(1)} collective-permute-done((bf16[64,640]{1,0:T(8,128)(2,1)S(1)}, bf16[64,640]{1,0:T(8,128)(2,1)S(1)}, u32[]{:S(2)}, u32[]{:S(2)}) %collective-permute-start.15) | collective-permute-done | bytes 81952 | tf_op jit(solution)/shard_map/ppermute | solution.py:46
  112.0 1.6 %mix.1 = bf16[64,5120]{1,0:T(8,128)(2,1)} custom-call(s32[6]{0:T(128)S(1)} %stack.31.where_ref, bf16[64,5120]{1,0:T(8,128)(2,1)S(1)} %copy-done.4, f32[1,5120]{1,0:T(1,128)S(1)} %bitcast.13, bf16[64,640]{1,0:T(8,128)(2,1)S(1)} %get-tuple-element.49.refs_0_, bf16[64,640]{1,0:T(8,128)(2,1)S(1)} %collective-permute-done.14.refs_1_, ...), custom_call_target="tpu_custom_call" | custom-call | flops 1 | tf_op jit(solution)/shard_map/mix/pallas_call | solution.py:538
  (18 shorter events, 0.0 us)
Async XLA Ops:
  0.0 10.9 %copy-start.6 = (s32[2,2,8]{2,1,0:T(2,128)S(1)}, s32[2,2,8]{2,1,0:T(2,128)}, u32[]{:S(2)}) copy-start(s32[2,2,8]{2,1,0:T(2,128)} %exps_ref.3) | copy-start | bytes 388
  0.0 10.9 %copy-start.3 = (bf16[256,1024]{1,0:T(8,128)(2,1)S(1)}, bf16[256,1024]{1,0:T(8,128)(2,1)}, u32[]{:S(2)}) copy-start(bf16[256,1024]{1,0:T(8,128)(2,1)} %q_ref.3) | copy-start | bytes 1572868
  0.0 81.9 %collective-permute-start.6 = (bf16[1024,1280]{1,0:T(8,128)(2,1)}, bf16[1024,1280]{1,0:T(8,128)(2,1)S(1)}, u32[]{:S(2)}, u32[]{:S(2)}) collective-permute-start(bf16[1024,1280]{1,0:T(8,128)(2,1)} %refs_8_.1), channel_id=1, source_target_pairs={{0,2},{2,0},{1,3},{3,1},{4,6},{6,4},{5,7},{7,5},{8,10},{10,8},{9,1... | collective-permute-start | bytes 7864328 | tf_op jit(solution)/shard_map/ppermute | solution.py:46
  6.3 14.2 %collective-permute-start = (bf16[3,256,256]{2,1,0:T(8,128)(2,1)}, bf16[3,256,256]{2,1,0:T(8,128)(2,1)S(1)}, u32[]{:S(2)}, u32[]{:S(2)}) collective-permute-start(bf16[3,256,256]{2,1,0:T(8,128)(2,1)} %get-tuple-element.34), channel_id=1, source_target_pairs={{0,12},{4,8},{8,4},{12,0},{1,13},{5,9},{9,5},{13,1},{2,14},{6,10},... | collective-permute-start | bytes 1179656 | tf_op jit(solution)/shard_map/ppermute | solution.py:46
  10.0 33.6 %collective-permute-start.1 = (bf16[3,256,256]{2,1,0:T(8,128)(2,1)}, bf16[3,256,256]{2,1,0:T(8,128)(2,1)}, u32[]{:S(2)}, u32[]{:S(2)}) collective-permute-start(bf16[3,256,256]{2,1,0:T(8,128)(2,1)} %get-tuple-element.33), channel_id=1, source_target_pairs={{0,8},{4,12},{8,0},{12,4},{1,9},{5,13},{9,1},{13,5},{2,10},{6,14},... | collective-permute-start | bytes 1179656 | tf_op jit(solution)/shard_map/ppermute | solution.py:46
  10.0 33.6 %collective-permute-start.2 = (bf16[3,256,256]{2,1,0:T(8,128)(2,1)}, bf16[3,256,256]{2,1,0:T(8,128)(2,1)}, u32[]{:S(2)}, u32[]{:S(2)}) collective-permute-start(bf16[3,256,256]{2,1,0:T(8,128)(2,1)} %get-tuple-element.32), channel_id=1, source_target_pairs={{0,4},{4,0},{8,12},{12,8},{1,5},{5,1},{9,13},{13,9},{2,6},{6,2},{1... | collective-permute-start | bytes 1179656 | tf_op jit(solution)/shard_map/ppermute | solution.py:46
  10.9 2.2 %copy-start = (bf16[2,1024,1024]{2,1,0:T(8,128)(2,1)S(1)}, bf16[2,1024,1024]{2,1,0:T(8,128)(2,1)}, u32[]{:S(2)}) copy-start(bf16[2,1024,1024]{2,1,0:T(8,128)(2,1)} %cached_ref.3) | copy-start | bytes 12582916
  13.1 1.2 %copy-start.1 = (bf16[2,256,1024]{2,1,0:T(8,128)(2,1)S(1)}, bf16[2,256,1024]{2,1,0:T(8,128)(2,1)}, u32[]{:S(2)}) copy-start(bf16[2,256,1024]{2,1,0:T(8,128)(2,1)} %fresh_ref.3) | copy-start | bytes 3145732
  14.3 72.4 %copy-start.2 = (bf16[1024,1280]{1,0:T(8,128)(2,1)S(1)}, bf16[1024,1280]{1,0:T(8,128)(2,1)}, u32[]{:S(2)}) copy-start(bf16[1024,1280]{1,0:T(8,128)(2,1)} %refs_8_.1) | copy-start | bytes 7864324
  48.4 17.3 %collective-permute-start.3 = (bf16[512,256]{1,0:T(8,128)(2,1)S(1)}, bf16[512,256]{1,0:T(8,128)(2,1)S(1)}, u32[]{:S(2)}, u32[]{:S(2)}) collective-permute-start(bf16[512,256]{1,0:T(8,128)(2,1)S(1)} %bitcast.14), channel_id=1, source_target_pairs={{0,2},{2,0},{1,3},{3,1},{4,6},{6,4},{5,7},{7,5},{8,10},{10,8},{9,1... | collective-permute-start | bytes 786440 | tf_op jit(solution)/shard_map/ppermute | solution.py:46
  49.0 21.1 %collective-permute-start.10 = (bf16[512,256]{1,0:T(8,128)(2,1)S(1)}, bf16[512,256]{1,0:T(8,128)(2,1)S(1)}, u32[]{:S(2)}, u32[]{:S(2)}) collective-permute-start(bf16[512,256]{1,0:T(8,128)(2,1)S(1)} %bitcast.9), channel_id=1, source_target_pairs={{0,4},{4,0},{8,12},{12,8},{1,5},{5,1},{9,13},{13,9},{2,6},{6,2},{1... | collective-permute-start | bytes 786440 | tf_op jit(solution)/shard_map/ppermute | solution.py:46
  49.0 21.1 %collective-permute-start.9 = (bf16[512,256]{1,0:T(8,128)(2,1)S(1)}, bf16[512,256]{1,0:T(8,128)(2,1)S(1)}, u32[]{:S(2)}, u32[]{:S(2)}) collective-permute-start(bf16[512,256]{1,0:T(8,128)(2,1)S(1)} %bitcast.10), channel_id=1, source_target_pairs={{0,8},{4,12},{8,0},{12,4},{1,9},{5,13},{9,1},{13,5},{2,10},{6,14},... | collective-permute-start | bytes 786440 | tf_op jit(solution)/shard_map/ppermute | solution.py:46
  65.6 15.2 %collective-permute-start.4 = (bf16[512,256]{1,0:T(8,128)(2,1)S(1)}, bf16[512,256]{1,0:T(8,128)(2,1)S(1)}, u32[]{:S(2)}, u32[]{:S(2)}) collective-permute-start(bf16[512,256]{1,0:T(8,128)(2,1)S(1)} %collective-permute-done.3.refs_4_), channel_id=1, source_target_pairs={{0,8},{4,12},{8,0},{12,4},{1,9},{5,13},{9,1},{13,5},{2,10},{6,14},... | collective-permute-start | bytes 786440 | tf_op jit(solution)/shard_map/ppermute | solution.py:46
  68.5 13.4 %collective-permute-start.5 = (bf16[512,256]{1,0:T(8,128)(2,1)S(1)}, bf16[512,256]{1,0:T(8,128)(2,1)S(1)}, u32[]{:S(2)}, u32[]{:S(2)}) collective-permute-start(bf16[512,256]{1,0:T(8,128)(2,1)S(1)} %collective-permute-done.3.refs_4_), channel_id=1, source_target_pairs={{0,4},{4,0},{8,12},{12,8},{1,5},{5,1},{9,13},{13,9},{2,6},{6,2},{1... | collective-permute-start | bytes 786440 | tf_op jit(solution)/shard_map/ppermute | solution.py:46
  70.1 13.8 %collective-permute-start.11 = (bf16[512,256]{1,0:T(8,128)(2,1)S(1)}, bf16[512,256]{1,0:T(8,128)(2,1)S(1)}, u32[]{:S(2)}, u32[]{:S(2)}) collective-permute-start(bf16[512,256]{1,0:T(8,128)(2,1)S(1)} %bitcast.11), channel_id=1, source_target_pairs={{4,8},{8,4},{5,9},{9,5},{6,10},{10,6},{7,11},{11,7},{20,24},{24,20... | collective-permute-start | bytes 786440 | tf_op jit(solution)/shard_map/ppermute | solution.py:46
  70.7 15.9 %collective-permute-start.12 = (bf16[512,256]{1,0:T(8,128)(2,1)S(1)}, bf16[512,256]{1,0:T(8,128)(2,1)S(1)}, u32[]{:S(2)}, u32[]{:S(2)}) collective-permute-start(bf16[512,256]{1,0:T(8,128)(2,1)S(1)} %collective-permute-done.9.refs_2_), channel_id=1, source_target_pairs={{4,0},{8,12},{5,1},{9,13},{6,2},{10,14},{7,3},{11,15},{20,16},{24,... | collective-permute-start | bytes 786440 | tf_op jit(solution)/shard_map/ppermute | solution.py:510
  81.9 9.9 %collective-permute-start.7 = (bf16[512,256]{1,0:T(8,128)(2,1)S(1)}, bf16[512,256]{1,0:T(8,128)(2,1)S(1)}, u32[]{:S(2)}, u32[]{:S(2)}) collective-permute-start(bf16[512,256]{1,0:T(8,128)(2,1)S(1)} %collective-permute-done.3.refs_4_), channel_id=1, source_target_pairs={{4,8},{8,4},{5,9},{9,5},{6,10},{10,6},{7,11},{11,7},{20,24},{24,20... | collective-permute-start | bytes 786440 | tf_op jit(solution)/shard_map/ppermute | solution.py:46
  82.6 9.2 %collective-permute-start.8 = (bf16[512,256]{1,0:T(8,128)(2,1)S(1)}, bf16[512,256]{1,0:T(8,128)(2,1)S(1)}, u32[]{:S(2)}, u32[]{:S(2)}) collective-permute-start(bf16[512,256]{1,0:T(8,128)(2,1)S(1)} %collective-permute-done.4.refs_6_), channel_id=1, source_target_pairs={{4,0},{8,12},{5,1},{9,13},{6,2},{10,14},{7,3},{11,15},{20,16},{24,... | collective-permute-start | bytes 786440 | tf_op jit(solution)/shard_map/ppermute | solution.py:510
  92.8 19.2 %copy-start.4 = (bf16[64,5120]{1,0:T(8,128)(2,1)S(1)}, bf16[64,5120]{1,0:T(8,128)(2,1)}, u32[]{:S(2)}) copy-start(bf16[64,5120]{1,0:T(8,128)(2,1)} %hidden_ref.1) | copy-start | bytes 1966084
  92.8 19.2 %copy-start.5 = (f32[5120]{0:T(1024)S(1)}, f32[5120]{0:T(1024)}, u32[]{:S(2)}) copy-start(f32[5120]{0:T(1024)} %param.13) | copy-start | bytes 61444
  92.8 1.7 %collective-permute-start.17 = (bf16[4,64,640]{2,1,0:T(8,128)(2,1)S(1)}, bf16[4,64,640]{2,1,0:T(8,128)(2,1)S(1)}, u32[]{:S(2)}, u32[]{:S(2)}) collective-permute-start(bf16[4,64,640]{2,1,0:T(8,128)(2,1)S(1)} %get-tuple-element.54), channel_id=1, source_target_pairs={{0,1},{1,0},{2,3},{3,2},{4,5},{5,4},{6,7},{7,6},{8,9},{9,8},{10,11... | collective-permute-start | bytes 983048 | tf_op jit(solution)/shard_map/ppermute | solution.py:46
  93.9 5.7 %collective-permute-start.13 = (bf16[4,64,640]{2,1,0:T(8,128)(2,1)S(1)}, bf16[4,64,640]{2,1,0:T(8,128)(2,1)S(1)}, u32[]{:S(2)}, u32[]{:S(2)}) collective-permute-start(bf16[4,64,640]{2,1,0:T(8,128)(2,1)S(1)} %get-tuple-element.48), channel_id=1, source_target_pairs={{0,1},{1,0},{2,3},{3,2},{4,5},{5,4},{6,7},{7,6},{8,9},{9,8},{10,11... | collective-permute-start | bytes 983048 | tf_op jit(solution)/shard_map/ppermute | solution.py:46
  95.1 7.3 %collective-permute-start.18 = (bf16[64,640]{1,0:T(8,128)(2,1)S(1)}, bf16[64,640]{1,0:T(8,128)(2,1)S(1)}, u32[]{:S(2)}, u32[]{:S(2)}) collective-permute-start(bf16[64,640]{1,0:T(8,128)(2,1)S(1)} %get-tuple-element.56), channel_id=1, source_target_pairs={{0,12},{4,8},{8,4},{12,0},{1,13},{5,9},{9,5},{13,1},{2,14},{6,10},... | collective-permute-start | bytes 245768 | tf_op jit(solution)/shard_map/ppermute | solution.py:46
  97.3 10.5 %collective-permute-start.19 = (bf16[64,640]{1,0:T(8,128)(2,1)S(1)}, bf16[64,640]{1,0:T(8,128)(2,1)S(1)}, u32[]{:S(2)}, u32[]{:S(2)}) collective-permute-start(bf16[64,640]{1,0:T(8,128)(2,1)S(1)} %get-tuple-element.57), channel_id=1, source_target_pairs={{0,8},{4,12},{8,0},{12,4},{1,9},{5,13},{9,1},{13,5},{2,10},{6,14},... | collective-permute-start | bytes 245768 | tf_op jit(solution)/shard_map/ppermute | solution.py:46
  97.3 10.5 %collective-permute-start.20 = (bf16[64,640]{1,0:T(8,128)(2,1)S(1)}, bf16[64,640]{1,0:T(8,128)(2,1)S(1)}, u32[]{:S(2)}, u32[]{:S(2)}) collective-permute-start(bf16[64,640]{1,0:T(8,128)(2,1)S(1)} %get-tuple-element.58), channel_id=1, source_target_pairs={{0,4},{4,0},{8,12},{12,8},{1,5},{5,1},{9,13},{13,9},{2,6},{6,2},{1... | collective-permute-start | bytes 245768 | tf_op jit(solution)/shard_map/ppermute | solution.py:46
  100.2 7.6 %collective-permute-start.14 = (bf16[64,640]{1,0:T(8,128)(2,1)S(1)}, bf16[64,640]{1,0:T(8,128)(2,1)S(1)}, u32[]{:S(2)}, u32[]{:S(2)}) collective-permute-start(bf16[64,640]{1,0:T(8,128)(2,1)S(1)} %get-tuple-element.50), channel_id=1, source_target_pairs={{0,12},{4,8},{8,4},{12,0},{1,13},{5,9},{9,5},{13,1},{2,14},{6,10},... | collective-permute-start | bytes 245768 | tf_op jit(solution)/shard_map/ppermute | solution.py:46
  102.4 9.6 %collective-permute-start.15 = (bf16[64,640]{1,0:T(8,128)(2,1)S(1)}, bf16[64,640]{1,0:T(8,128)(2,1)S(1)}, u32[]{:S(2)}, u32[]{:S(2)}) collective-permute-start(bf16[64,640]{1,0:T(8,128)(2,1)S(1)} %get-tuple-element.51), channel_id=1, source_target_pairs={{0,8},{4,12},{8,0},{12,4},{1,9},{5,13},{9,1},{13,5},{2,10},{6,14},... | collective-permute-start | bytes 245768 | tf_op jit(solution)/shard_map/ppermute | solution.py:46
  102.4 9.6 %collective-permute-start.16 = (bf16[64,640]{1,0:T(8,128)(2,1)S(1)}, bf16[64,640]{1,0:T(8,128)(2,1)S(1)}, u32[]{:S(2)}, u32[]{:S(2)}) collective-permute-start(bf16[64,640]{1,0:T(8,128)(2,1)S(1)} %get-tuple-element.52), channel_id=1, source_target_pairs={{0,4},{4,0},{8,12},{12,8},{1,5},{5,1},{9,13},{13,9},{2,6},{6,2},{1... | collective-permute-start | bytes 245768 | tf_op jit(solution)/shard_map/ppermute | solution.py:46

commit v13 on v11

--- a/solution.py
+++ b/solution.py
@@ -54,9 +54,16 @@
     return (cached + codes.astype(jnp.float32) * jnp.exp2(power)).astype(jnp.bfloat16)
 
 
+def piece_place(split, per, rel, chunk):
+    if rel < split - 1 or rel == 0:
+        return rel, chunk
+    return rel + chunk, 0
+
+
 def pack_kernel(split, per, exps_ref, q_ref, fresh_ref, cached_ref, *refs):
-    outs, bufs = refs[: split - 1], refs[split - 1 : 2 * split - 2]
-    q_buf, fresh_buf, cached_buf, sems, out_sems = refs[2 * split - 2 :]
+    count = split - 2 + per
+    outs, bufs = refs[:count], refs[count : 2 * count]
+    q_buf, fresh_buf, cached_buf, sems, out_sems = refs[2 * count :]
     patch = lax.axis_index("patch")
     near = lax.rem(patch, split)
     tok = q_buf.shape[0]
@@ -78,11 +85,11 @@
         for copy in copies[block]:
             copy.wait()
         for rel in range(split - 1, 0, -1):
-            buf = bufs[rel - 1]
             for chunk in range(per):
                 head = (near ^ rel) * per + chunk
                 lanes = pl.ds(pl.multiple_of(head * HEAD_DIM, HEAD_DIM), HEAD_DIM)
-                here = pl.ds(chunk * HEAD_DIM, HEAD_DIM)
+                number, place = piece_place(split, per, rel, chunk)
+                buf, here = bufs[number - 1], pl.ds(place * HEAD_DIM, HEAD_DIM)
                 buf[0, rows, here] = q_buf[rows, lanes]
                 for stacked in range(2):
                     buf[1 + stacked, rows, here] = decode(
@@ -90,10 +97,9 @@
                         cached_buf[stacked, rows, lanes],
                         exps_ref[stacked, block * PACK_ROWS // SCALE_ROWS, head],
                     )
+        for at, (buf, out) in enumerate(zip(bufs, outs)):
             sent.append(
-                pltpu.make_async_copy(
-                    buf.at[:, rows], outs[rel - 1].at[:, rows], out_sems.at[block, rel - 1]
-                )
+                pltpu.make_async_copy(buf.at[:, rows], out.at[:, rows], out_sems.at[block, at])
             )
             sent[-1].start()
     for copy in sent:
@@ -102,21 +108,23 @@
 
 def pack(split, exponents, queries, fresh_kv, cached_kv):
     tok, channels = queries.shape
-    feat = channels // split
+    per = channels // split // HEAD_DIM
+    wide = [per] * (split - 2) + [1] * per
+    shapes = [(3, tok, x * HEAD_DIM) for x in wide]
     blocks = tok // PACK_ROWS
     hbm = pl.BlockSpec(memory_space=pltpu.HBM)
     return pl.pallas_call(
-        functools.partial(pack_kernel, split, feat // HEAD_DIM),
-        out_shape=[jax.ShapeDtypeStruct((3, tok, feat), jnp.bfloat16)] * (split - 1),
+        functools.partial(pack_kernel, split, per),
+        out_shape=[jax.ShapeDtypeStruct(shape, jnp.bfloat16) for shape in shapes],
         in_specs=[pl.BlockSpec(memory_space=pltpu.SMEM), hbm, hbm, hbm],
-        out_specs=[hbm] * (split - 1),
-        scratch_shapes=[pltpu.VMEM((3, tok, feat), jnp.bfloat16)] * (split - 1)
+        out_specs=[hbm] * len(shapes),
+        scratch_shapes=[pltpu.VMEM(shape, jnp.bfloat16) for shape in shapes]
         + [
             pltpu.VMEM((tok, channels), jnp.bfloat16),
             pltpu.VMEM((2, tok, channels), jnp.bfloat16),
             pltpu.VMEM((2, tok, channels), jnp.bfloat16),
             pltpu.SemaphoreType.DMA((blocks, 3)),
-            pltpu.SemaphoreType.DMA((blocks, split - 1)),
+            pltpu.SemaphoreType.DMA((blocks, len(shapes))),
         ],
         compiler_params=pltpu.CompilerParams(vmem_limit_bytes=PACK_VMEM_BYTES),
         name="pack",
@@ -352,8 +360,16 @@
     )(where, *sums)
 
 
-def sum_tail(sizes, where, pieces, kv_pieces, out_weight, hidden_in, attn_gate):
+def sum_tail(sizes, where, chunks, out_weight, hidden_in, attn_gate):
     n_patch, n_head, n_sub = sizes["patch"], sizes["head"], sizes["sub"]
+    pieces = []
+    for same in zip(*chunks):
+        cut = [x[:, :, at * HEAD_DIM : (at + 1) * HEAD_DIM] for x, at in same]
+        pieces.append(jnp.concatenate(cut, axis=2))
+    pieces = [pieces[0], *pieces[:0:-1]]
+    kv_pieces = list(pieces)
+    for rel in range(len(pieces), n_patch, len(pieces)):
+        kv_pieces += [swap(x, "patch", n_patch, rel) for x in pieces]
     split, tok = len(pieces), pieces[0].shape[1]
     count = n_head * n_sub
     piece = tok // count
@@ -374,67 +390,66 @@
     return mix(where, hidden_in, attn_gate, blocks)
 
 
-def attend_halves_kernel(where_ref, *refs):
+def attend_halves_kernel(rels, where_ref, *refs):
     pieces, outs = refs[:-2], refs[-2:]
-    split = len(pieces)
-    rels = [0, *range(split - 1, 0, -1)]
     factor = HEAD_DIM**-0.5 * math.log2(math.e)
-    rows, feat = outs[0].shape[1:]
-    for head in range(feat // HEAD_DIM):
-        lanes = pl.ds(head * HEAD_DIM, HEAD_DIM)
-        keys = jnp.concatenate([ref[1, :, lanes] for ref in pieces], axis=0)
-        values = jnp.concatenate([ref[2, :, lanes] for ref in pieces], axis=0)
-        values = jnp.concatenate([values, jnp.ones_like(values)], axis=1)
-        for half, out in enumerate(outs):
-            start = pl.multiple_of((where_ref[HEAD] ^ half) * rows, rows)
-            query = jnp.concatenate([ref[0, pl.ds(start, rows), lanes] for ref in pieces], axis=0)
-            scores = lax.dot_general(
-                query, keys, (((1,), (1,)), ((), ())), preferred_element_type=jnp.float32
-            )
-            peak = jnp.max(scores, axis=1, keepdims=True)
-            expo = jnp.exp2((scores - peak) * factor).astype(jnp.bfloat16)
-            mix = jnp.dot(expo, values, preferred_element_type=jnp.float32)
-            mix = (mix[:, :HEAD_DIM] / mix[:, HEAD_DIM:]).astype(jnp.bfloat16)
-            for at, rel in enumerate(rels):
-                out[where_ref[NEAR] ^ rel, :, lanes] = mix[at * rows : (at + 1) * rows]
-
-
-def attend_halves(where, pieces):
-    split = len(pieces)
-    _, tok, feat = pieces[0].shape
-    out = jax.ShapeDtypeStruct((split, tok // 2, feat), jnp.bfloat16)
+    rows = outs[0].shape[1]
+    keys = jnp.concatenate([ref[1] for ref in pieces], axis=0)
+    values = jnp.concatenate([ref[2] for ref in pieces], axis=0)
+    values = jnp.concatenate([values, jnp.ones_like(values)], axis=1)
+    for half, out in enumerate(outs):
+        start = pl.multiple_of((where_ref[HEAD] ^ half) * rows, rows)
+        query = jnp.concatenate([ref[0, pl.ds(start, rows)] for ref in pieces], axis=0)
+        scores = lax.dot_general(
+            query, keys, (((1,), (1,)), ((), ())), preferred_element_type=jnp.float32
+        )
+        peak = jnp.max(scores, axis=1, keepdims=True)
+        expo = jnp.exp2((scores - peak) * factor).astype(jnp.bfloat16)
+        mix = jnp.dot(expo, values, preferred_element_type=jnp.float32)
+        mix = (mix[:, :HEAD_DIM] / mix[:, HEAD_DIM:]).astype(jnp.bfloat16)
+        for at, rel in enumerate(rels):
+            out[where_ref[NEAR] ^ rel] = mix[at * rows : (at + 1) * rows]
+
+
+def attend_halves(where, chunk):
+    tok = chunk[0][0].shape[1]
+    rels = [0, *range(len(chunk) - 1, 0, -1)]
+    chunk = [chunk[rel] for rel in rels]
+    out = jax.ShapeDtypeStruct((len(chunk), tok // 2, HEAD_DIM), jnp.bfloat16)
     outs = call(
-        attend_halves_kernel,
+        functools.partial(attend_halves_kernel, rels),
         "attend",
         [out] * 2,
         1,
-        [spec((3, tok, feat))] * split,
+        [pl.BlockSpec((3, tok, HEAD_DIM), lambda i, w, at=at: (0, 0, at)) for _, at in chunk],
         [spec(out.shape)] * 2,
-    )(where, *pieces)
-    return [x.reshape(-1, feat) for x in outs]
+    )(where, *[x for x, _ in chunk])
+    return [x.reshape(-1, HEAD_DIM) for x in outs]
 
 
 def first_kernel(where_ref, *refs):
     slots, (more, own_ref, fetched_ref, passed_ref, out_ref, held_ref) = refs[:7], refs[7:]
-    feat = slots[0].shape[1]
+    depth = own_ref.shape[0]
+
+    def put(at, chunk, value):
+        place = where_ref[NEAR] ^ at
+        there = 4 + (2 * ((place // 2) ^ where_ref[GRP]) + place % 2)
+        for half, spot in enumerate((place, there)):
+            lane = (2 * spot + chunk) * HEAD_DIM
+            held_ref[:, pl.ds(pl.multiple_of(lane, HEAD_DIM), HEAD_DIM)] = value[
+                :, half * HEAD_DIM : (half + 1) * HEAD_DIM
+            ]
 
     @pl.when(pl.program_id(0) == 0)
     def arrange():
-        for at, slot in enumerate(slots):
+        for index, slot in enumerate(slots):
+            chunk, at = divmod(index, 4)
             block = slot[...]
             if at == 3:
                 block = jnp.where(where_ref[INNER] == 1, block, more[...])
-            place = where_ref[NEAR] ^ (at % 4)
-            if at >= 4:
-                place = 4 + (2 * ((place // 2) ^ where_ref[GRP]) + place % 2)
-            held_ref[:, pl.ds(pl.multiple_of(place * feat, HEAD_DIM), feat)] = block
-        place = where_ref[NEAR] ^ 3
-        place = 4 + (2 * ((place // 2) ^ where_ref[GRP]) + place % 2)
-        held_ref[:, pl.ds(pl.multiple_of(place * feat, HEAD_DIM), feat)] = jnp.zeros(
-            (slots[0].shape[0], feat), jnp.bfloat16
-        )
-
-    depth = 4 * feat
+            put(at, chunk, block)
+        put(3, 1, jnp.zeros(more.shape, jnp.bfloat16))
+
     acc = jnp.dot(held_ref[:, :depth], own_ref[...], preferred_element_type=jnp.float32)
     half = depth // 2
     for at, weight in enumerate((fetched_ref, passed_ref)):
@@ -448,7 +463,7 @@
 
 def first_product(where, slots, more, weights):
     rows, feat = slots[0].shape
-    cols = weights[0].shape[1]
+    depth, cols = weights[0].shape
     wide = cols // 2
     return call(
         first_kernel,
@@ -458,17 +473,17 @@
         [spec((rows, feat))] * 8
         + [pl.BlockSpec((x.shape[0], wide), lambda i, w: (0, i)) for x in weights],
         pl.BlockSpec((rows, wide), lambda i, w: (0, i)),
-        [pltpu.VMEM((rows, 8 * feat), jnp.bfloat16)],
+        [pltpu.VMEM((rows, 2 * depth), jnp.bfloat16)],
     )(where, *slots, more, *weights)
 
 
-def second_kernel(where_ref, slot, more, fetched_ref, passed_ref, acc_in, keep_ref, send_ref, acc_ref):
-    feat = slot.shape[1]
+def second_kernel(
+    where_ref, slot, more, own_ref, fetched_ref, passed_ref, acc_in, keep_ref, send_ref, acc_ref
+):
     place = where_ref[NEAR] ^ 3
-    rows = pl.ds(pl.multiple_of((place % 2) * feat, HEAD_DIM), feat)
-    weight = jnp.where(
-        (place // 2) == where_ref[GRP], fetched_ref[rows, :], passed_ref[rows, :]
-    )
+    here = pl.ds(pl.multiple_of((2 * (place % 2) + 1) * HEAD_DIM, HEAD_DIM), HEAD_DIM)
+    partner = jnp.where((place // 2) == where_ref[GRP], fetched_ref[here, :], passed_ref[here, :])
+    weight = jnp.concatenate([own_ref[...], partner], axis=0)
     block = jnp.where(where_ref[INNER] == 1, slot[...], more[...])
     acc = acc_in[...] + jnp.dot(block, weight, preferred_element_type=jnp.float32)
     acc_ref[...] = acc.reshape(acc_ref.shape)
@@ -479,7 +494,7 @@
 
 def second_product(where, chunk, slot, more, weights, acc):
     rows, feat = slot.shape
-    depth, cols = weights[0].shape
+    depth, cols = weights[1].shape
     wide = cols // 2
     out = jax.ShapeDtypeStruct((4, rows // 8, wide), jnp.bfloat16)
     return call(
@@ -488,6 +503,7 @@
         [out] * 2,
         1,
         [spec((rows, feat))] * 2
+        + [pl.BlockSpec((HEAD_DIM, wide), lambda i, w: (2 * (w[NEAR] ^ 3) + 1, chunk))]
         + [pl.BlockSpec((depth, wide), lambda i, w: (0, chunk))] * 2
         + [pl.BlockSpec((rows, wide), lambda i, w: (0, chunk))],
         [spec(out.shape)] * 2,
@@ -512,28 +528,35 @@
     )(where, keep, term)
 
 
-def share_tail(sizes, where, pieces, kv_pieces, out_weight, hidden_in, attn_gate):
+def share_tail(sizes, where, chunks, out_weight, hidden_in, attn_gate):
     half = out_weight.shape[0] // 2
     out_weight, where = lax.optimization_barrier((out_weight, where))
     start = lax.axis_index("grp") * half
     fetched = swap(lax.dynamic_slice_in_dim(out_weight, start, half, 0), "head", 2, 1)
-    pieces, fetched = lax.optimization_barrier((pieces, fetched))
+    early, fetched = lax.optimization_barrier(([x for x, _ in chunks[0]], fetched))
+    chunks[0] = [(x, place) for x, (_, place) in zip(early, chunks[0])]
     passed = swap(fetched, "grp", 2, 1)
 
-    mine, other = attend_halves(where, pieces)
+    mine, other = attend_halves(where, chunks[0])
     other = swap(other, "head", 2, 1)
-    slots = []
-    for at, x in enumerate((mine, other)):
-        far, next_to = swap(x, "patch", 4, 2), swap(x, "patch", 4, 1)
-        far, next_to, other, x = lax.optimization_barrier((far, next_to, other, x))
+    late, other = lax.optimization_barrier(([x for x, _ in chunks[1]], other))
+    joined = jnp.concatenate([mine, other], axis=1)
+    chunks[1] = [(x, place) for x, (_, place) in zip(late, chunks[1])]
+    mine, other = attend_halves(where, chunks[1])
+    slots = [[joined], [jnp.concatenate([mine, swap(other, "head", 2, 1)], axis=1)]]
+    for at, slot in enumerate(slots):
+        far, next_to = swap(slot[0], "patch", 4, 2), swap(slot[0], "patch", 4, 1)
+        far, next_to, slots[1][0], slot[0] = lax.optimization_barrier(
+            (far, next_to, slots[1][0], slot[0])
+        )
         if at == 1:
-            far, x, passed = lax.optimization_barrier((far, x, passed))
-        middle = swap(x, "patch", 4, 3, (1, 2))
+            far, slot[0], passed = lax.optimization_barrier((far, slot[0], passed))
+        middle = swap(slot[0], "patch", 4, 3, (1, 2))
         ends = lax.ppermute(far, "patch", [(1, 0), (2, 3)])
-        slots.append([x, next_to, far, middle, ends])
-    first = [*slots[0][:4], *slots[1][:3]]
-    acc = first_product(where, first, slots[0][4], [out_weight, fetched, passed])
-    terms = [second_product(where, at, *slots[1][3:], [fetched, passed], acc) for at in range(2)]
+        slot += [next_to, far, middle, ends]
+    weights = [out_weight, fetched, passed]
+    acc = first_product(where, [*slots[0][:4], *slots[1][:3]], slots[0][4], weights)
+    terms = [second_product(where, at, *slots[1][3:], weights, acc) for at in range(2)]
     blocks = []
     for keep, send in terms:
         total = add(where, keep, swap(send, "sub", 2, 1))
@@ -587,15 +610,17 @@
 
     arrays = (exponents, queries, fresh_kv, cached_kv)
     sent = pack(split, *arrays)
-    far_first = [swap(sent[rel - 1], "patch", n_patch, rel) for rel in range(split - 1, 0, -1)]
+    arrived = {
+        at + 1: swap(x, "patch", n_patch, min(at + 1, split - 1)) for at, x in enumerate(sent)
+    }
     where, sent = lax.optimization_barrier((where, sent))
-    pieces = [pack_own(split, where, *arrays), *far_first]
-    kv_pieces = list(pieces)
-    for rel in range(split, n_patch, split):
-        kv_pieces += [swap(x, "patch", n_patch, rel) for x in pieces]
-
-    tail = (sizes, where, pieces, kv_pieces, out_weight, hidden_in, attn_gate)
-    if (sizes["grp"], n_head, split, n_patch) == (2, 2, 4, 4):
+    arrived[0] = pack_own(split, where, *arrays)
+    chunks = []
+    for chunk in range(heads // split):
+        places = [piece_place(split, heads // split, rel, chunk) for rel in range(split)]
+        chunks.append([(arrived[number], place) for number, place in places])
+    tail = (sizes, where, chunks, out_weight, hidden_in, attn_gate)
+    if (sizes["grp"], n_head, split, n_patch, heads) == (2, 2, 4, 4, 8):
         return share_tail(*tail)
     return sum_tail(*tail)
 

time: 107 us -> 110 us (1.028)
  starting transfers between devices: 28.3 us -> 34.4 us
  waiting for transfers between devices: 57.5 us -> 52.3 us
  Pallas kernels: 18.8 us -> 20.2 us
    ppermute x20 -> x22, starting transfers between devices: 25.7 us -> 31.8 us  [swap(): return lax.ppermute(x, axes, pairs)]
    ppermute x20 -> x22, waiting for transfers between devices: 53.8 us -> 50.8 us  [swap(): return lax.ppermute(x, axes, pairs)]
    ppermute x2, waiting for transfers between devices: 3.63 us -> 1.51 us  [share_tail(): ends = lax.ppermute(far, 'patch', [(1, 0), (2, 3)])]
    pallas_call x2 -> x3, Pallas kernels: 7.31 us -> 8.42 us  [the longest x2 4.87 us: attend_halves(): call(functools.partial(attend_halves_kernel, rels), 'attend', [out] * 2,...]
    unnamed x18 -> x20, local copies, waits for them, and re-layouts: 2.23 us -> 2.23 us
  transfers between devices with their start and end apart: 22 -> 24, of which waited for: 10 -> 11; matrix products, arithmetic and copies ran while one was open for 0% -> 0% of each run, Pallas kernels for 12% -> 13%
where the time goes in v13:
time: 110 us
  waiting for transfers between devices  52.3 us (48%)
  starting transfers between devices  34.4 us (31%)
  Pallas kernels  20.2 us (18%)
  local copies, waits for them, and re-layouts  2.41 us (2%)
    ppermute x22, waiting for transfers between devices, swap(): return lax.ppermute(x, axes, pairs)  50.8 us
    ppermute x22, starting transfers between devices, swap(): return lax.ppermute(x, axes, pairs)  31.8 us
    pallas_call x1, Pallas kernels, first_product(): call(first_kernel, 'first', jax.ShapeDtypeStruct((rows, cols), jnp.float3...  5.42 us
    pallas_call x2, Pallas kernels, attend_halves(): call(functools.partial(attend_halves_kernel, rels), 'attend', [out] * 2,...  4.87 us
    pallas_call x1, Pallas kernels, pack(): pl.pallas_call(functools.partial(pack_kernel, split, per), out_shape=[jax...  3.55 us
    ppermute x2, starting transfers between devices, share_tail(): ends = lax.ppermute(far, 'patch', [(1, 0), (2, 3)])  2.58 us
    unnamed x20, local copies, waits for them, and re-layouts  2.23 us
  transfers between devices with their start and end apart: 24, of which 11 were waited for; matrix products, arithmetic and copies ran while one was open for 0% of the time, Pallas kernels for 13%

profile of v13, /device:TPU:0, one launch (start us, length us, event | category | flops | bytes accessed | tf_op | source)
XLA Modules:
  0.0 109.5 jit_solution(9354582857266240097)
XLA Ops:
  0.0 3.5 %pack.1 = (bf16[3,256,256]{2,1,0:T(8,128)(2,1)}, bf16[3,256,256]{2,1,0:T(8,128)(2,1)}, bf16[3,256,128]{2,1,0:T(8,128)(2,1)}, bf16[3,256,128]{2,1,0:T(8,128)(2,1)}) custom-call(s32[2,2,8]{2,1,0:T(2,128)} %exps_ref.3, bf16[256,1024]{1,0:T(8,128)(2,1)} %q_ref.3, bf16[2,256,1024]{2,1,0:T(8,128)(2,1)} %fresh_ref.3, bf16[2,1024,1024]{2,1,0:T(8,128)(2,1)} %cached_ref.3), custom_call_target="tpu_custom_call" | custom-call | tf_op jit(solution)/shard_map/pack/pallas_call | solution.py:116
  3.6 0.1 stack.31.where_ref
  3.7 0.1 constant_dynamic-slice_fusion
  3.8 3.0 %collective-permute-start.3 = (bf16[512,1280]{1,0:T(8,128)(2,1)S(1)}, bf16[512,1280]{1,0:T(8,128)(2,1)S(1)}, u32[]{:S(2)}, u32[]{:S(2)}) collective-permute-start(bf16[512,1280]{1,0:T(8,128)(2,1)S(1)} %constant_dynamic-slice_fusion), channel_id=1, source_target_pairs={{0,2},{2,0},{1,3},{3,1},{4,6},{6,4},{5,7},{7,5},{8,10},{10,8},{9,1... | collective-permute-start | bytes 3932168 | tf_op jit(solution)/shard_map/ppermute | solution.py:46
  6.8 1.6 %collective-permute-start = (bf16[3,256,256]{2,1,0:T(8,128)(2,1)S(1)}, bf16[3,256,256]{2,1,0:T(8,128)(2,1)S(1)}, u32[]{:S(2)}, u32[]{:S(2)}) collective-permute-start(bf16[3,256,256]{2,1,0:T(8,128)(2,1)S(1)} %copy-done.8), channel_id=1, source_target_pairs={{0,4},{4,0},{8,12},{12,8},{1,5},{5,1},{9,13},{13,9},{2,6},{6,2},{1... | collective-permute-start | bytes 1179656 | tf_op jit(solution)/shard_map/ppermute | solution.py:46
  8.4 2.6 %collective-permute-start.1 = (bf16[3,256,256]{2,1,0:T(8,128)(2,1)S(1)}, bf16[3,256,256]{2,1,0:T(8,128)(2,1)S(1)}, u32[]{:S(2)}, u32[]{:S(2)}) collective-permute-start(bf16[3,256,256]{2,1,0:T(8,128)(2,1)S(1)} %copy-done.7), channel_id=1, source_target_pairs={{0,8},{4,12},{8,0},{12,4},{1,9},{5,13},{9,1},{13,5},{2,10},{6,14},... | collective-permute-start | bytes 1179656 | tf_op jit(solution)/shard_map/ppermute | solution.py:46
  11.0 0.2 collective-permute-start.2
  11.2 2.2 %copy-done.1 = bf16[2,1024,1024]{2,1,0:T(8,128)(2,1)S(1)} copy-done((bf16[2,1024,1024]{2,1,0:T(8,128)(2,1)S(1)}, bf16[2,1024,1024]{2,1,0:T(8,128)(2,1)}, u32[]{:S(2)}) %copy-start.1) | copy-done | bytes 4194328
  13.4 1.3 %own.1.refs_0_ = bf16[3,256,256]{2,1,0:T(8,128)(2,1)S(1)} custom-call(s32[6]{0:T(128)S(1)} %stack.31.where_ref, s32[2,2,8]{2,1,0:T(2,128)S(1)} %copy-done.6, bf16[256,1024]{1,0:T(8,128)(2,1)S(1)} %copy-done.3, bf16[2,256,1024]{2,1,0:T(8,128)(2,1)S(1)} %copy-done.2, bf16[2,1024,1024]{2,1,0:T(8,128)(2,1)S(1)} %copy-done.1), custom_call_target="tpu_custom_call" | custom-call | flops 1 | tf_op jit(solution)/shard_map/own/pallas_call | solution.py:152
  14.7 17.5 %collective-permute-done.2.refs_1_ = bf16[3,256,128]{2,1,0:T(8,128)(2,1)S(1)} collective-permute-done((bf16[3,256,128]{2,1,0:T(8,128)(2,1)}, bf16[3,256,128]{2,1,0:T(8,128)(2,1)S(1)}, u32[]{:S(2)}, u32[]{:S(2)}) %collective-permute-start.2) | collective-permute-done | bytes 196640 | tf_op jit(solution)/shard_map/ppermute | solution.py:46
  32.2 1.8 %collective-permute-done.1.refs_2_ = bf16[3,256,256]{2,1,0:T(8,128)(2,1)S(1)} collective-permute-done((bf16[3,256,256]{2,1,0:T(8,128)(2,1)S(1)}, bf16[3,256,256]{2,1,0:T(8,128)(2,1)S(1)}, u32[]{:S(2)}, u32[]{:S(2)}) %collective-permute-start.1) | collective-permute-done | bytes 393248 | tf_op jit(solution)/shard_map/ppermute | solution.py:46
  34.0 1.6 %collective-permute-done.3.refs_9_.fetched_ref = bf16[512,1280]{1,0:T(8,128)(2,1)S(1)} collective-permute-done((bf16[512,1280]{1,0:T(8,128)(2,1)S(1)}, bf16[512,1280]{1,0:T(8,128)(2,1)S(1)}, u32[]{:S(2)}, u32[]{:S(2)}) %collective-permute-start.3) | collective-permute-done | bytes 1310752 | tf_op jit(solution)/shard_map/ppermute | solution.py:46
  35.6 1.8 %collective-permute-start.11 = (bf16[512,1280]{1,0:T(8,128)(2,1)S(1)}, bf16[512,1280]{1,0:T(8,128)(2,1)S(1)}, u32[]{:S(2)}, u32[]{:S(2)}) collective-permute-start(bf16[512,1280]{1,0:T(8,128)(2,1)S(1)} %collective-permute-done.3.refs_9_.fetched_ref), channel_id=1, source_target_pairs={{0,16},{16,0},{1,17},{17,1},{2,18},{18,2},{3,19},{19,3},{4,20},{20... | collective-permute-start | bytes 3932168 | tf_op jit(solution)/shard_map/ppermute | solution.py:46
  37.4 3.6 %collective-permute-start.4 = (bf16[3,256,128]{2,1,0:T(8,128)(2,1)S(1)}, bf16[3,256,128]{2,1,0:T(8,128)(2,1)S(1)}, u32[]{:S(2)}, u32[]{:S(2)}) collective-permute-start(bf16[3,256,128]{2,1,0:T(8,128)(2,1)S(1)} %copy-done.9), channel_id=1, source_target_pairs={{0,12},{4,8},{8,4},{12,0},{1,13},{5,9},{9,5},{13,1},{2,14},{6,10},... | collective-permute-start | bytes 589832 | tf_op jit(solution)/shard_map/ppermute | solution.py:46
  41.0 2.4 %attend.2 = (bf16[4,128,128]{2,1,0:T(8,128)(2,1)S(1)}, bf16[4,128,128]{2,1,0:T(8,128)(2,1)S(1)}) custom-call(s32[6]{0:T(128)S(1)} %stack.31.where_ref, bf16[3,256,256]{2,1,0:T(8,128)(2,1)S(1)} %own.1.refs_0_, bf16[3,256,128]{2,1,0:T(8,128)(2,1)S(1)} %collective-permute-done.2.refs_1_, bf16[3,256,256]{2,1,0:T(8,128)(2,1)S(1)} %collective-permute-done.1.refs_2_, ...), custom_call_target="tpu_custom_call" | custom-call | flops 1 | tf_op jit(solution)/shard_map/attend/pallas_call | solution.py:419
  43.4 1.6 %collective-permute-start.5 = (bf16[512,128]{1,0:T(8,128)(2,1)S(1)}, bf16[512,128]{1,0:T(8,128)(2,1)S(1)}, u32[]{:S(2)}, u32[]{:S(2)}) collective-permute-start(bf16[512,128]{1,0:T(8,128)(2,1)S(1)} %bitcast.14), channel_id=1, source_target_pairs={{0,2},{2,0},{1,3},{3,1},{4,6},{6,4},{5,7},{7,5},{8,10},{10,8},{9,1... | collective-permute-start | bytes 393224 | tf_op jit(solution)/shard_map/ppermute | solution.py:46
  45.0 3.5 %collective-permute-done.5 = bf16[512,128]{1,0:T(8,128)(2,1)S(1)} collective-permute-done((bf16[512,128]{1,0:T(8,128)(2,1)S(1)}, bf16[512,128]{1,0:T(8,128)(2,1)S(1)}, u32[]{:S(2)}, u32[]{:S(2)}) %collective-permute-start.5) | collective-permute-done | bytes 131104 | tf_op jit(solution)/shard_map/ppermute | solution.py:46
  48.5 1.3 %collective-permute-start.6 = (bf16[512,256]{1,0:T(8,128)(2,1)S(1)}, bf16[512,256]{1,0:T(8,128)(2,1)S(1)}, u32[]{:S(2)}, u32[]{:S(2)}) collective-permute-start(bf16[512,256]{1,0:T(8,128)(2,1)S(1)} %pad_maximum_fusion.refs_0_), channel_id=1, source_target_pairs={{0,8},{4,12},{8,0},{12,4},{1,9},{5,13},{9,1},{13,5},{2,10},{6,14},... | collective-permute-start | bytes 786440 | tf_op jit(solution)/shard_map/ppermute | solution.py:46
  49.8 2.4 %attend.3 = (bf16[4,128,128]{2,1,0:T(8,128)(2,1)S(1)}, bf16[4,128,128]{2,1,0:T(8,128)(2,1)S(1)}) custom-call(s32[6]{0:T(128)S(1)} %stack.31.where_ref, bf16[3,256,256]{2,1,0:T(8,128)(2,1)S(1)} %own.1.refs_0_, bf16[3,256,128]{2,1,0:T(8,128)(2,1)S(1)} %collective-permute-done.4.refs_1_, bf16[3,256,256]{2,1,0:T(8,128)(2,1)S(1)} %collective-permute-done.1.refs_2_, ...), custom_call_target="tpu_custom_call" | custom-call | flops 1 | tf_op jit(solution)/shard_map/attend/pallas_call | solution.py:419
  52.2 1.6 %collective-permute-start.8 = (bf16[512,128]{1,0:T(8,128)(2,1)S(1)}, bf16[512,128]{1,0:T(8,128)(2,1)S(1)}, u32[]{:S(2)}, u32[]{:S(2)}) collective-permute-start(bf16[512,128]{1,0:T(8,128)(2,1)S(1)} %bitcast.15), channel_id=1, source_target_pairs={{0,2},{2,0},{1,3},{3,1},{4,6},{6,4},{5,7},{7,5},{8,10},{10,8},{9,1... | collective-permute-start | bytes 393224 | tf_op jit(solution)/shard_map/ppermute | solution.py:46
  53.8 3.5 %collective-permute-done.8 = bf16[512,128]{1,0:T(8,128)(2,1)S(1)} collective-permute-done((bf16[512,128]{1,0:T(8,128)(2,1)S(1)}, bf16[512,128]{1,0:T(8,128)(2,1)S(1)}, u32[]{:S(2)}, u32[]{:S(2)}) %collective-permute-start.8) | collective-permute-done | bytes 131104 | tf_op jit(solution)/shard_map/ppermute | solution.py:46
  57.3 3.6 %collective-permute-done.6.refs_2_ = bf16[512,256]{1,0:T(8,128)(2,1)S(1)} collective-permute-done((bf16[512,256]{1,0:T(8,128)(2,1)S(1)}, bf16[512,256]{1,0:T(8,128)(2,1)S(1)}, u32[]{:S(2)}, u32[]{:S(2)}) %collective-permute-start.6) | collective-permute-done | bytes 262176 | tf_op jit(solution)/shard_map/ppermute | solution.py:46
  60.9 3.2 %collective-permute-start.9 = (bf16[512,256]{1,0:T(8,128)(2,1)S(1)}, bf16[512,256]{1,0:T(8,128)(2,1)S(1)}, u32[]{:S(2)}, u32[]{:S(2)}) collective-permute-start(bf16[512,256]{1,0:T(8,128)(2,1)S(1)} %pad_maximum_fusion.1.refs_4_), channel_id=1, source_target_pairs={{0,8},{4,12},{8,0},{12,4},{1,9},{5,13},{9,1},{13,5},{2,10},{6,14},... | collective-permute-start | bytes 786440 | tf_op jit(solution)/shard_map/ppermute | solution.py:46
  64.1 0.7 collective-permute-start.14
  64.7 1.3 %collective-permute-start.15 = (bf16[512,256]{1,0:T(8,128)(2,1)S(1)}, bf16[512,256]{1,0:T(8,128)(2,1)S(1)}, u32[]{:S(2)}, u32[]{:S(2)}) collective-permute-start(bf16[512,256]{1,0:T(8,128)(2,1)S(1)} %collective-permute-done.6.refs_2_), channel_id=1, source_target_pairs={{4,0},{8,12},{5,1},{9,13},{6,2},{10,14},{7,3},{11,15},{20,16},{24,... | collective-permute-start | bytes 786440 | tf_op jit(solution)/shard_map/ppermute | solution.py:555
  66.0 7.5 %collective-permute-done.10.refs_5_ = bf16[512,256]{1,0:T(8,128)(2,1)S(1)} collective-permute-done((bf16[512,256]{1,0:T(8,128)(2,1)S(1)}, bf16[512,256]{1,0:T(8,128)(2,1)S(1)}, u32[]{:S(2)}, u32[]{:S(2)}) %collective-permute-start.10) | collective-permute-done | bytes 262176 | tf_op jit(solution)/shard_map/ppermute | solution.py:46
  73.5 3.4 %collective-permute-done.9.refs_6_ = bf16[512,256]{1,0:T(8,128)(2,1)S(1)} collective-permute-done((bf16[512,256]{1,0:T(8,128)(2,1)S(1)}, bf16[512,256]{1,0:T(8,128)(2,1)S(1)}, u32[]{:S(2)}, u32[]{:S(2)}) %collective-permute-start.9) | collective-permute-done | bytes 262176 | tf_op jit(solution)/shard_map/ppermute | solution.py:46
  76.9 0.7 collective-permute-start.12
  77.6 1.3 %collective-permute-start.13 = (bf16[512,256]{1,0:T(8,128)(2,1)S(1)}, bf16[512,256]{1,0:T(8,128)(2,1)S(1)}, u32[]{:S(2)}, u32[]{:S(2)}) collective-permute-start(bf16[512,256]{1,0:T(8,128)(2,1)S(1)} %collective-permute-done.9.refs_6_), channel_id=1, source_target_pairs={{4,0},{8,12},{5,1},{9,13},{6,2},{10,14},{7,3},{11,15},{20,16},{24,... | collective-permute-start | bytes 786440 | tf_op jit(solution)/shard_map/ppermute | solution.py:555
  78.9 1.5 %collective-permute-done.15.refs_7_ = bf16[512,256]{1,0:T(8,128)(2,1)S(1)} collective-permute-done((bf16[512,256]{1,0:T(8,128)(2,1)S(1)}, bf16[512,256]{1,0:T(8,128)(2,1)S(1)}, u32[]{:S(2)}, u32[]{:S(2)}) %collective-permute-start.15) | collective-permute-done | bytes 262176 | tf_op jit(solution)/shard_map/ppermute | solution.py:555
  80.4 5.4 %first.1.acc_in = f32[512,1280]{1,0:T(8,128)S(1)} custom-call(s32[6]{0:T(128)S(1)} %stack.31.where_ref, bf16[512,256]{1,0:T(8,128)(2,1)S(1)} %pad_maximum_fusion.refs_0_, bf16[512,256]{1,0:T(8,128)(2,1)S(1)} %collective-permute-done.7.refs_1_, bf16[512,256]{1,0:T(8,128)(2,1)S(1)} %collective-permute-done.6.refs_2_, ...), custom_call_target="tpu_custom_call" | custom-call | flops 1 | tf_op jit(solution)/shard_map/first/pallas_call | solution.py:468
  85.8 0.0 collective-permute-done.13.more
  85.8 1.1 second.3
  87.0 0.0 copy-start.5
  87.0 0.1 collective-permute-start.20
  87.1 1.1 second.2
  88.2 0.6 collective-permute-start.16
  88.7 0.6 add.12
  89.3 2.7 %collective-permute-start.21 = (bf16[64,640]{1,0:T(8,128)(2,1)S(1)}, bf16[64,640]{1,0:T(8,128)(2,1)S(1)}, u32[]{:S(2)}, u32[]{:S(2)}) collective-permute-start(bf16[64,640]{1,0:T(8,128)(2,1)S(1)} %get-tuple-element.88), channel_id=1, source_target_pairs={{0,12},{4,8},{8,4},{12,0},{1,13},{5,9},{9,5},{13,1},{2,14},{6,10},... | collective-permute-start | bytes 245768 | tf_op jit(solution)/shard_map/ppermute | solution.py:46
  92.1 1.5 %collective-permute-start.22 = (bf16[64,640]{1,0:T(8,128)(2,1)S(1)}, bf16[64,640]{1,0:T(8,128)(2,1)S(1)}, u32[]{:S(2)}, u32[]{:S(2)}) collective-permute-start(bf16[64,640]{1,0:T(8,128)(2,1)S(1)} %get-tuple-element.89), channel_id=1, source_target_pairs={{0,8},{4,12},{8,0},{12,4},{1,9},{5,13},{9,1},{13,5},{2,10},{6,14},... | collective-permute-start | bytes 245768 | tf_op jit(solution)/shard_map/ppermute | solution.py:46
  93.5 0.3 collective-permute-start.23
  93.9 0.6 add.11
  94.5 2.6 %collective-permute-start.17 = (bf16[64,640]{1,0:T(8,128)(2,1)S(1)}, bf16[64,640]{1,0:T(8,128)(2,1)S(1)}, u32[]{:S(2)}, u32[]{:S(2)}) collective-permute-start(bf16[64,640]{1,0:T(8,128)(2,1)S(1)} %get-tuple-element.82), channel_id=1, source_target_pairs={{0,12},{4,8},{8,4},{12,0},{1,13},{5,9},{9,5},{13,1},{2,14},{6,10},... | collective-permute-start | bytes 245768 | tf_op jit(solution)/shard_map/ppermute | solution.py:46
  97.1 0.6 collective-permute-start.18
  97.7 1.7 %collective-permute-start.19 = (bf16[64,640]{1,0:T(8,128)(2,1)S(1)}, bf16[64,640]{1,0:T(8,128)(2,1)S(1)}, u32[]{:S(2)}, u32[]{:S(2)}) collective-permute-start(bf16[64,640]{1,0:T(8,128)(2,1)S(1)} %get-tuple-element.84), channel_id=1, source_target_pairs={{0,4},{4,0},{8,12},{12,8},{1,5},{5,1},{9,13},{13,9},{2,6},{6,2},{1... | collective-permute-start | bytes 245768 | tf_op jit(solution)/shard_map/ppermute | solution.py:46
  99.5 5.0 %collective-permute-done.22.refs_6_ = bf16[64,640]{1,0:T(8,128)(2,1)S(1)} collective-permute-done((bf16[64,640]{1,0:T(8,128)(2,1)S(1)}, bf16[64,640]{1,0:T(8,128)(2,1)S(1)}, u32[]{:S(2)}, u32[]{:S(2)}) %collective-permute-start.22) | collective-permute-done | bytes 81952 | tf_op jit(solution)/shard_map/ppermute | solution.py:46
  104.5 3.4 %collective-permute-done.18.refs_2_ = bf16[64,640]{1,0:T(8,128)(2,1)S(1)} collective-permute-done((bf16[64,640]{1,0:T(8,128)(2,1)S(1)}, bf16[64,640]{1,0:T(8,128)(2,1)S(1)}, u32[]{:S(2)}, u32[]{:S(2)}) %collective-permute-start.18) | collective-permute-done | bytes 81952 | tf_op jit(solution)/shard_map/ppermute | solution.py:46
  107.9 1.6 %mix.1 = bf16[64,5120]{1,0:T(8,128)(2,1)} custom-call(s32[6]{0:T(128)S(1)} %stack.31.where_ref, bf16[64,5120]{1,0:T(8,128)(2,1)S(1)} %copy-done.4, f32[1,5120]{1,0:T(1,128)S(1)} %bitcast.13, bf16[64,640]{1,0:T(8,128)(2,1)S(1)} %get-tuple-element.81.refs_0_, bf16[64,640]{1,0:T(8,128)(2,1)S(1)} %collective-permute-done.17.refs_1_, ...), custom_call_target="tpu_custom_call" | custom-call | flops 1 | tf_op jit(solution)/shard_map/mix/pallas_call | solution.py:583
  (34 shorter events, 0.1 us)
Async XLA Ops:
  0.0 3.7 %copy-start = (bf16[1024,1280]{1,0:T(8,128)(2,1)S(1)}, bf16[1024,1280]{1,0:T(8,128)(2,1)}, u32[]{:S(2)}) copy-start(bf16[1024,1280]{1,0:T(8,128)(2,1)} %own_ref.1) | copy-start | bytes 7864324
  3.6 4.8 %copy-start.7 = (bf16[3,256,256]{2,1,0:T(8,128)(2,1)S(1)}, bf16[3,256,256]{2,1,0:T(8,128)(2,1)}, u32[]{:S(2)}) copy-start(bf16[3,256,256]{2,1,0:T(8,128)(2,1)} %get-tuple-element.49) | copy-start | bytes 1179652
  3.6 7.6 %copy-start.3 = (bf16[256,1024]{1,0:T(8,128)(2,1)S(1)}, bf16[256,1024]{1,0:T(8,128)(2,1)}, u32[]{:S(2)}) copy-start(bf16[256,1024]{1,0:T(8,128)(2,1)} %q_ref.3) | copy-start | bytes 1572868
  3.6 7.6 %copy-start.6 = (s32[2,2,8]{2,1,0:T(2,128)S(1)}, s32[2,2,8]{2,1,0:T(2,128)}, u32[]{:S(2)}) copy-start(s32[2,2,8]{2,1,0:T(2,128)} %exps_ref.3) | copy-start | bytes 388
  3.7 3.1 %copy-start.8 = (bf16[3,256,256]{2,1,0:T(8,128)(2,1)S(1)}, bf16[3,256,256]{2,1,0:T(8,128)(2,1)}, u32[]{:S(2)}) copy-start(bf16[3,256,256]{2,1,0:T(8,128)(2,1)} %get-tuple-element.48) | copy-start | bytes 1179652
  3.7 7.5 %copy-start.2 = (bf16[2,256,1024]{2,1,0:T(8,128)(2,1)S(1)}, bf16[2,256,1024]{2,1,0:T(8,128)(2,1)}, u32[]{:S(2)}) copy-start(bf16[2,256,1024]{2,1,0:T(8,128)(2,1)} %fresh_ref.3) | copy-start | bytes 3145732
  3.7 33.7 %copy-start.9 = (bf16[3,256,128]{2,1,0:T(8,128)(2,1)S(1)}, bf16[3,256,128]{2,1,0:T(8,128)(2,1)}, u32[]{:S(2)}) copy-start(bf16[3,256,128]{2,1,0:T(8,128)(2,1)} %get-tuple-element.51) | copy-start | bytes 589828
  3.8 31.8 %collective-permute-start.3 = (bf16[512,1280]{1,0:T(8,128)(2,1)S(1)}, bf16[512,1280]{1,0:T(8,128)(2,1)S(1)}, u32[]{:S(2)}, u32[]{:S(2)}) collective-permute-start(bf16[512,1280]{1,0:T(8,128)(2,1)S(1)} %constant_dynamic-slice_fusion), channel_id=1, source_target_pairs={{0,2},{2,0},{1,3},{3,1},{4,6},{6,4},{5,7},{7,5},{8,10},{10,8},{9,1... | collective-permute-start | bytes 3932168 | tf_op jit(solution)/shard_map/ppermute | solution.py:46
  6.8 25.3 %collective-permute-start = (bf16[3,256,256]{2,1,0:T(8,128)(2,1)S(1)}, bf16[3,256,256]{2,1,0:T(8,128)(2,1)S(1)}, u32[]{:S(2)}, u32[]{:S(2)}) collective-permute-start(bf16[3,256,256]{2,1,0:T(8,128)(2,1)S(1)} %copy-done.8), channel_id=1, source_target_pairs={{0,4},{4,0},{8,12},{12,8},{1,5},{5,1},{9,13},{13,9},{2,6},{6,2},{1... | collective-permute-start | bytes 1179656 | tf_op jit(solution)/shard_map/ppermute | solution.py:46
  8.4 25.6 %collective-permute-start.1 = (bf16[3,256,256]{2,1,0:T(8,128)(2,1)S(1)}, bf16[3,256,256]{2,1,0:T(8,128)(2,1)S(1)}, u32[]{:S(2)}, u32[]{:S(2)}) collective-permute-start(bf16[3,256,256]{2,1,0:T(8,128)(2,1)S(1)} %copy-done.7), channel_id=1, source_target_pairs={{0,8},{4,12},{8,0},{12,4},{1,9},{5,13},{9,1},{13,5},{2,10},{6,14},... | collective-permute-start | bytes 1179656 | tf_op jit(solution)/shard_map/ppermute | solution.py:46
  11.0 21.2 %collective-permute-start.2 = (bf16[3,256,128]{2,1,0:T(8,128)(2,1)}, bf16[3,256,128]{2,1,0:T(8,128)(2,1)S(1)}, u32[]{:S(2)}, u32[]{:S(2)}) collective-permute-start(bf16[3,256,128]{2,1,0:T(8,128)(2,1)} %get-tuple-element.50), channel_id=1, source_target_pairs={{0,12},{4,8},{8,4},{12,0},{1,13},{5,9},{9,5},{13,1},{2,14},{6,10},... | collective-permute-start | bytes 589832 | tf_op jit(solution)/shard_map/ppermute | solution.py:46
  11.2 2.2 %copy-start.1 = (bf16[2,1024,1024]{2,1,0:T(8,128)(2,1)S(1)}, bf16[2,1024,1024]{2,1,0:T(8,128)(2,1)}, u32[]{:S(2)}) copy-start(bf16[2,1024,1024]{2,1,0:T(8,128)(2,1)} %cached_ref.3) | copy-start | bytes 12582916
  35.6 41.3 %collective-permute-start.11 = (bf16[512,1280]{1,0:T(8,128)(2,1)S(1)}, bf16[512,1280]{1,0:T(8,128)(2,1)S(1)}, u32[]{:S(2)}, u32[]{:S(2)}) collective-permute-start(bf16[512,1280]{1,0:T(8,128)(2,1)S(1)} %collective-permute-done.3.refs_9_.fetched_ref), channel_id=1, source_target_pairs={{0,16},{16,0},{1,17},{17,1},{2,18},{18,2},{3,19},{19,3},{4,20},{20... | collective-permute-start | bytes 3932168 | tf_op jit(solution)/shard_map/ppermute | solution.py:46
  37.4 7.6 %collective-permute-start.4 = (bf16[3,256,128]{2,1,0:T(8,128)(2,1)S(1)}, bf16[3,256,128]{2,1,0:T(8,128)(2,1)S(1)}, u32[]{:S(2)}, u32[]{:S(2)}) collective-permute-start(bf16[3,256,128]{2,1,0:T(8,128)(2,1)S(1)} %copy-done.9), channel_id=1, source_target_pairs={{0,12},{4,8},{8,4},{12,0},{1,13},{5,9},{9,5},{13,1},{2,14},{6,10},... | collective-permute-start | bytes 589832 | tf_op jit(solution)/shard_map/ppermute | solution.py:46
  43.4 5.0 %collective-permute-start.5 = (bf16[512,128]{1,0:T(8,128)(2,1)S(1)}, bf16[512,128]{1,0:T(8,128)(2,1)S(1)}, u32[]{:S(2)}, u32[]{:S(2)}) collective-permute-start(bf16[512,128]{1,0:T(8,128)(2,1)S(1)} %bitcast.14), channel_id=1, source_target_pairs={{0,2},{2,0},{1,3},{3,1},{4,6},{6,4},{5,7},{7,5},{8,10},{10,8},{9,1... | collective-permute-start | bytes 393224 | tf_op jit(solution)/shard_map/ppermute | solution.py:46
  48.5 12.4 %collective-permute-start.6 = (bf16[512,256]{1,0:T(8,128)(2,1)S(1)}, bf16[512,256]{1,0:T(8,128)(2,1)S(1)}, u32[]{:S(2)}, u32[]{:S(2)}) collective-permute-start(bf16[512,256]{1,0:T(8,128)(2,1)S(1)} %pad_maximum_fusion.refs_0_), channel_id=1, source_target_pairs={{0,8},{4,12},{8,0},{12,4},{1,9},{5,13},{9,1},{13,5},{2,10},{6,14},... | collective-permute-start | bytes 786440 | tf_op jit(solution)/shard_map/ppermute | solution.py:46
  49.8 11.1 %collective-permute-start.7 = (bf16[512,256]{1,0:T(8,128)(2,1)S(1)}, bf16[512,256]{1,0:T(8,128)(2,1)S(1)}, u32[]{:S(2)}, u32[]{:S(2)}) collective-permute-start(bf16[512,256]{1,0:T(8,128)(2,1)S(1)} %pad_maximum_fusion.refs_0_), channel_id=1, source_target_pairs={{0,4},{4,0},{8,12},{12,8},{1,5},{5,1},{9,13},{13,9},{2,6},{6,2},{1... | collective-permute-start | bytes 786440 | tf_op jit(solution)/shard_map/ppermute | solution.py:46
  52.2 5.0 %collective-permute-start.8 = (bf16[512,128]{1,0:T(8,128)(2,1)S(1)}, bf16[512,128]{1,0:T(8,128)(2,1)S(1)}, u32[]{:S(2)}, u32[]{:S(2)}) collective-permute-start(bf16[512,128]{1,0:T(8,128)(2,1)S(1)} %bitcast.15), channel_id=1, source_target_pairs={{0,2},{2,0},{1,3},{3,1},{4,6},{6,4},{5,7},{7,5},{8,10},{10,8},{9,1... | collective-permute-start | bytes 393224 | tf_op jit(solution)/shard_map/ppermute | solution.py:46
  60.9 12.7 %collective-permute-start.10 = (bf16[512,256]{1,0:T(8,128)(2,1)S(1)}, bf16[512,256]{1,0:T(8,128)(2,1)S(1)}, u32[]{:S(2)}, u32[]{:S(2)}) collective-permute-start(bf16[512,256]{1,0:T(8,128)(2,1)S(1)} %pad_maximum_fusion.1.refs_4_), channel_id=1, source_target_pairs={{0,4},{4,0},{8,12},{12,8},{1,5},{5,1},{9,13},{13,9},{2,6},{6,2},{1... | collective-permute-start | bytes 786440 | tf_op jit(solution)/shard_map/ppermute | solution.py:46
  60.9 16.0 %collective-permute-start.9 = (bf16[512,256]{1,0:T(8,128)(2,1)S(1)}, bf16[512,256]{1,0:T(8,128)(2,1)S(1)}, u32[]{:S(2)}, u32[]{:S(2)}) collective-permute-start(bf16[512,256]{1,0:T(8,128)(2,1)S(1)} %pad_maximum_fusion.1.refs_4_), channel_id=1, source_target_pairs={{0,8},{4,12},{8,0},{12,4},{1,9},{5,13},{9,1},{13,5},{2,10},{6,14},... | collective-permute-start | bytes 786440 | tf_op jit(solution)/shard_map/ppermute | solution.py:46
  64.1 14.8 %collective-permute-start.14 = (bf16[512,256]{1,0:T(8,128)(2,1)S(1)}, bf16[512,256]{1,0:T(8,128)(2,1)S(1)}, u32[]{:S(2)}, u32[]{:S(2)}) collective-permute-start(bf16[512,256]{1,0:T(8,128)(2,1)S(1)} %pad_maximum_fusion.refs_0_), channel_id=1, source_target_pairs={{4,8},{8,4},{5,9},{9,5},{6,10},{10,6},{7,11},{11,7},{20,24},{24,20... | collective-permute-start | bytes 786440 | tf_op jit(solution)/shard_map/ppermute | solution.py:46
  64.7 15.7 %collective-permute-start.15 = (bf16[512,256]{1,0:T(8,128)(2,1)S(1)}, bf16[512,256]{1,0:T(8,128)(2,1)S(1)}, u32[]{:S(2)}, u32[]{:S(2)}) collective-permute-start(bf16[512,256]{1,0:T(8,128)(2,1)S(1)} %collective-permute-done.6.refs_2_), channel_id=1, source_target_pairs={{4,0},{8,12},{5,1},{9,13},{6,2},{10,14},{7,3},{11,15},{20,16},{24,... | collective-permute-start | bytes 786440 | tf_op jit(solution)/shard_map/ppermute | solution.py:555
  76.9 8.9 %collective-permute-start.12 = (bf16[512,256]{1,0:T(8,128)(2,1)S(1)}, bf16[512,256]{1,0:T(8,128)(2,1)S(1)}, u32[]{:S(2)}, u32[]{:S(2)}) collective-permute-start(bf16[512,256]{1,0:T(8,128)(2,1)S(1)} %pad_maximum_fusion.1.refs_4_), channel_id=1, source_target_pairs={{4,8},{8,4},{5,9},{9,5},{6,10},{10,6},{7,11},{11,7},{20,24},{24,20... | collective-permute-start | bytes 786440 | tf_op jit(solution)/shard_map/ppermute | solution.py:46
  77.6 8.3 %collective-permute-start.13 = (bf16[512,256]{1,0:T(8,128)(2,1)S(1)}, bf16[512,256]{1,0:T(8,128)(2,1)S(1)}, u32[]{:S(2)}, u32[]{:S(2)}) collective-permute-start(bf16[512,256]{1,0:T(8,128)(2,1)S(1)} %collective-permute-done.9.refs_6_), channel_id=1, source_target_pairs={{4,0},{8,12},{5,1},{9,13},{6,2},{10,14},{7,3},{11,15},{20,16},{24,... | collective-permute-start | bytes 786440 | tf_op jit(solution)/shard_map/ppermute | solution.py:555
  87.0 21.0 %copy-start.4 = (bf16[64,5120]{1,0:T(8,128)(2,1)S(1)}, bf16[64,5120]{1,0:T(8,128)(2,1)}, u32[]{:S(2)}) copy-start(bf16[64,5120]{1,0:T(8,128)(2,1)} %hidden_ref.1) | copy-start | bytes 1966084
  87.0 21.0 %copy-start.5 = (f32[5120]{0:T(1024)S(1)}, f32[5120]{0:T(1024)}, u32[]{:S(2)}) copy-start(f32[5120]{0:T(1024)} %param.13) | copy-start | bytes 61444
  87.0 1.7 %collective-permute-start.20 = (bf16[4,64,640]{2,1,0:T(8,128)(2,1)S(1)}, bf16[4,64,640]{2,1,0:T(8,128)(2,1)S(1)}, u32[]{:S(2)}, u32[]{:S(2)}) collective-permute-start(bf16[4,64,640]{2,1,0:T(8,128)(2,1)S(1)} %get-tuple-element.86), channel_id=1, source_target_pairs={{0,1},{1,0},{2,3},{3,2},{4,5},{5,4},{6,7},{7,6},{8,9},{9,8},{10,11... | collective-permute-start | bytes 983048 | tf_op jit(solution)/shard_map/ppermute | solution.py:46
  88.2 5.7 %collective-permute-start.16 = (bf16[4,64,640]{2,1,0:T(8,128)(2,1)S(1)}, bf16[4,64,640]{2,1,0:T(8,128)(2,1)S(1)}, u32[]{:S(2)}, u32[]{:S(2)}) collective-permute-start(bf16[4,64,640]{2,1,0:T(8,128)(2,1)S(1)} %get-tuple-element.80), channel_id=1, source_target_pairs={{0,1},{1,0},{2,3},{3,2},{4,5},{5,4},{6,7},{7,6},{8,9},{9,8},{10,11... | collective-permute-start | bytes 983048 | tf_op jit(solution)/shard_map/ppermute | solution.py:46
  89.3 8.4 %collective-permute-start.21 = (bf16[64,640]{1,0:T(8,128)(2,1)S(1)}, bf16[64,640]{1,0:T(8,128)(2,1)S(1)}, u32[]{:S(2)}, u32[]{:S(2)}) collective-permute-start(bf16[64,640]{1,0:T(8,128)(2,1)S(1)} %get-tuple-element.88), channel_id=1, source_target_pairs={{0,12},{4,8},{8,4},{12,0},{1,13},{5,9},{9,5},{13,1},{2,14},{6,10},... | collective-permute-start | bytes 245768 | tf_op jit(solution)/shard_map/ppermute | solution.py:46
  92.1 12.4 %collective-permute-start.22 = (bf16[64,640]{1,0:T(8,128)(2,1)S(1)}, bf16[64,640]{1,0:T(8,128)(2,1)S(1)}, u32[]{:S(2)}, u32[]{:S(2)}) collective-permute-start(bf16[64,640]{1,0:T(8,128)(2,1)S(1)} %get-tuple-element.89), channel_id=1, source_target_pairs={{0,8},{4,12},{8,0},{12,4},{1,9},{5,13},{9,1},{13,5},{2,10},{6,14},... | collective-permute-start | bytes 245768 | tf_op jit(solution)/shard_map/ppermute | solution.py:46
  93.5 11.0 %collective-permute-start.23 = (bf16[64,640]{1,0:T(8,128)(2,1)S(1)}, bf16[64,640]{1,0:T(8,128)(2,1)S(1)}, u32[]{:S(2)}, u32[]{:S(2)}) collective-permute-start(bf16[64,640]{1,0:T(8,128)(2,1)S(1)} %get-tuple-element.90), channel_id=1, source_target_pairs={{0,4},{4,0},{8,12},{12,8},{1,5},{5,1},{9,13},{13,9},{2,6},{6,2},{1... | collective-permute-start | bytes 245768 | tf_op jit(solution)/shard_map/ppermute | solution.py:46
  94.5 10.0 %collective-permute-start.17 = (bf16[64,640]{1,0:T(8,128)(2,1)S(1)}, bf16[64,640]{1,0:T(8,128)(2,1)S(1)}, u32[]{:S(2)}, u32[]{:S(2)}) collective-permute-start(bf16[64,640]{1,0:T(8,128)(2,1)S(1)} %get-tuple-element.82), channel_id=1, source_target_pairs={{0,12},{4,8},{8,4},{12,0},{1,13},{5,9},{9,5},{13,1},{2,14},{6,10},... | collective-permute-start | bytes 245768 | tf_op jit(solution)/shard_map/ppermute | solution.py:46
  97.1 10.8 %collective-permute-start.18 = (bf16[64,640]{1,0:T(8,128)(2,1)S(1)}, bf16[64,640]{1,0:T(8,128)(2,1)S(1)}, u32[]{:S(2)}, u32[]{:S(2)}) collective-permute-start(bf16[64,640]{1,0:T(8,128)(2,1)S(1)} %get-tuple-element.83), channel_id=1, source_target_pairs={{0,8},{4,12},{8,0},{12,4},{1,9},{5,13},{9,1},{13,5},{2,10},{6,14},... | collective-permute-start | bytes 245768 | tf_op jit(solution)/shard_map/ppermute | solution.py:46
  97.7 10.2 %collective-permute-start.19 = (bf16[64,640]{1,0:T(8,128)(2,1)S(1)}, bf16[64,640]{1,0:T(8,128)(2,1)S(1)}, u32[]{:S(2)}, u32[]{:S(2)}) collective-permute-start(bf16[64,640]{1,0:T(8,128)(2,1)S(1)} %get-tuple-element.84), channel_id=1, source_target_pairs={{0,4},{4,0},{8,12},{12,8},{1,5},{5,1},{9,13},{13,9},{2,6},{6,2},{1... | collective-permute-start | bytes 245768 | tf_op jit(solution)/shard_map/ppermute | solution.py:46

commit v14 on v12

--- a/solution.py
+++ b/solution.py
@@ -16,6 +16,10 @@
 PACK_VMEM_BYTES = 60 * 1024 * 1024
 ATTEND_FLOPS = 1
 PROJECT_FLOPS = 1
+OWN_FLOPS = 50_000_000_000
+FETCHED = 5
+ZERO_FLOPS = 20_000_000_000
+HALF_FLOPS = 1
 
 PATCH, NEAR, HEAD, SUB, INNER, GRP = range(6)
 
@@ -78,7 +82,7 @@
         for copy in copies[block]:
             copy.wait()
         for rel in range(split - 1, 0, -1):
-            buf = bufs[rel - 1]
+            buf = bufs[split - 1 - rel]
             for chunk in range(per):
                 head = (near ^ rel) * per + chunk
                 lanes = pl.ds(pl.multiple_of(head * HEAD_DIM, HEAD_DIM), HEAD_DIM)
@@ -92,7 +96,9 @@
                     )
             sent.append(
                 pltpu.make_async_copy(
-                    buf.at[:, rows], outs[rel - 1].at[:, rows], out_sems.at[block, rel - 1]
+                    buf.at[:, rows],
+                    outs[split - 1 - rel].at[:, rows],
+                    out_sems.at[block, rel - 1],
                 )
             )
             sent[-1].start()
@@ -153,6 +159,7 @@
             pl.BlockSpec((2, tok, feat), lambda i, w: (0, w[PATCH], w[NEAR])),
         ],
         spec(out.shape),
+        flops=OWN_FLOPS,
     )(where, exponents, queries, fresh_kv, cached_kv)
 
 
@@ -374,96 +381,142 @@
     return mix(where, hidden_in, attn_gate, blocks)
 
 
-def attend_halves_kernel(where_ref, *refs):
-    pieces, outs = refs[:-2], refs[-2:]
-    split = len(pieces)
-    rels = [0, *range(split - 1, 0, -1)]
+def attend_half_kernel(half, where_ref, *refs):
+    pieces, out = refs[:-1], refs[-1]
     factor = HEAD_DIM**-0.5 * math.log2(math.e)
-    rows, feat = outs[0].shape[1:]
+    rows, feat = out.shape[1:]
+    start = pl.multiple_of((where_ref[HEAD] ^ half) * rows, rows)
     for head in range(feat // HEAD_DIM):
         lanes = pl.ds(head * HEAD_DIM, HEAD_DIM)
         keys = jnp.concatenate([ref[1, :, lanes] for ref in pieces], axis=0)
         values = jnp.concatenate([ref[2, :, lanes] for ref in pieces], axis=0)
         values = jnp.concatenate([values, jnp.ones_like(values)], axis=1)
-        for half, out in enumerate(outs):
-            start = pl.multiple_of((where_ref[HEAD] ^ half) * rows, rows)
-            query = jnp.concatenate([ref[0, pl.ds(start, rows), lanes] for ref in pieces], axis=0)
-            scores = lax.dot_general(
-                query, keys, (((1,), (1,)), ((), ())), preferred_element_type=jnp.float32
-            )
-            peak = jnp.max(scores, axis=1, keepdims=True)
-            expo = jnp.exp2((scores - peak) * factor).astype(jnp.bfloat16)
-            mix = jnp.dot(expo, values, preferred_element_type=jnp.float32)
-            mix = (mix[:, :HEAD_DIM] / mix[:, HEAD_DIM:]).astype(jnp.bfloat16)
-            for at, rel in enumerate(rels):
-                out[where_ref[NEAR] ^ rel, :, lanes] = mix[at * rows : (at + 1) * rows]
-
-
-def attend_halves(where, pieces):
-    split = len(pieces)
+        query = jnp.concatenate([ref[0, pl.ds(start, rows), lanes] for ref in pieces], axis=0)
+        scores = lax.dot_general(
+            query, keys, (((1,), (1,)), ((), ())), preferred_element_type=jnp.float32
+        )
+        peak = jnp.max(scores, axis=1, keepdims=True)
+        expo = jnp.exp2((scores - peak) * factor).astype(jnp.bfloat16)
+        mix = jnp.dot(expo, values, preferred_element_type=jnp.float32)
+        mix = (mix[:, :HEAD_DIM] / mix[:, HEAD_DIM:]).astype(jnp.bfloat16)
+        for rel in range(len(pieces)):
+            out[where_ref[NEAR] ^ rel, :, lanes] = mix[rel * rows : (rel + 1) * rows]
+
+
+def attend_half(where, half, pieces):
     _, tok, feat = pieces[0].shape
-    out = jax.ShapeDtypeStruct((split, tok // 2, feat), jnp.bfloat16)
-    outs = call(
-        attend_halves_kernel,
+    out = jax.ShapeDtypeStruct((len(pieces), tok // 2, feat), jnp.bfloat16)
+    return call(
+        functools.partial(attend_half_kernel, half),
         "attend",
-        [out] * 2,
-        1,
-        [spec((3, tok, feat))] * split,
-        [spec(out.shape)] * 2,
-    )(where, *pieces)
-    return [x.reshape(-1, feat) for x in outs]
+        out,
+        1,
+        [spec((3, tok, feat))] * len(pieces),
+        spec(out.shape),
+        flops=HALF_FLOPS,
+    )(where, *pieces).reshape(-1, feat)
+
+
+def zeroth_kernel(where_ref, slot, weight_ref, out_ref):
+    out_ref[...] = jnp.dot(slot[...], weight_ref[...], preferred_element_type=jnp.float32)
+
+
+def zeroth_product(where, slot, weight):
+    rows, feat = slot.shape
+    cols = weight.shape[1]
+    wide = cols // 2
+    return call(
+        zeroth_kernel,
+        "zeroth",
+        jax.ShapeDtypeStruct((rows, cols), jnp.float32),
+        2,
+        [spec((rows, feat)), pl.BlockSpec((feat, wide), lambda i, w: (w[NEAR], i))],
+        pl.BlockSpec((rows, wide), lambda i, w: (0, i)),
+        flops=ZERO_FLOPS,
+    )(where, slot, weight)
+
+
+def partner_place(where_ref, head):
+    return (head + FETCHED * where_ref[GRP]) % 8
 
 
 def first_kernel(where_ref, *refs):
-    slots, (more, own_ref, partner_ref, out_ref, held_ref) = refs[:7], refs[7:]
+    slots, refs = refs[:6], refs[6:]
+    more, acc_ref, own_ref, fetched_ref, passed_ref, out_ref, held_ref = refs
     rows, feat = slots[0].shape
-    depth = own_ref.shape[0]
+    depth, cut = own_ref.shape[0], own_ref.shape[0] + fetched_ref.shape[0]
+
+    def put(place, block):
+        lanes = pl.ds(pl.multiple_of(place * HEAD_DIM, HEAD_DIM), block.shape[1])
+        held_ref[:, lanes] = block
 
     @pl.when(pl.program_id(0) == 0)
     def arrange():
-        for index in range(8):
-            half, at = divmod(index, 4)
-            if index == 7:
-                block = jnp.zeros((rows, feat), jnp.bfloat16)
-            else:
-                block = slots[index][...]
-            if index == 3:
+        nothing = jnp.zeros((rows, feat), jnp.bfloat16)
+        mine, partner = dict(zip((2, 1, 3), slots[:3])), dict(zip((0, 2, 1), slots[3:]))
+        for at in range(4):
+            place = where_ref[NEAR] ^ at
+            block = mine[at][...] if at else nothing
+            if at == 3:
                 block = jnp.where(where_ref[INNER] == 1, block, more[...])
-            lane = half * depth + (where_ref[NEAR] ^ at) * feat
-            held_ref[:, pl.ds(pl.multiple_of(lane, HEAD_DIM), feat)] = block
-
-    acc = jnp.dot(held_ref[:, :depth], own_ref[...], preferred_element_type=jnp.float32)
-    acc += jnp.dot(held_ref[:, depth:], partner_ref[...], preferred_element_type=jnp.float32)
+            put(2 * place, block)
+            block = nothing if at == 3 else partner[at][...]
+            for head in range(2):
+                there = partner_place(where_ref, 2 * place + head)
+                put(8 + there, block[:, head * HEAD_DIM : (head + 1) * HEAD_DIM])
+
+    acc = acc_ref[...]
+    acc += jnp.dot(held_ref[:, :depth], own_ref[...], preferred_element_type=jnp.float32)
+    acc += jnp.dot(held_ref[:, depth:cut], fetched_ref[...], preferred_element_type=jnp.float32)
+    acc += jnp.dot(held_ref[:, cut:], passed_ref[...], preferred_element_type=jnp.float32)
     out_ref[...] = acc
 
 
-def first_product(where, slots, more, weights):
+def first_product(where, slots, more, acc, weights):
     rows, feat = slots[0].shape
-    depth, cols = weights[0].shape
+    cols = weights[0].shape[1]
     wide = cols // 2
+    whole = pl.BlockSpec((rows, wide), lambda i, w: (0, i))
     return call(
         first_kernel,
         "first",
         jax.ShapeDtypeStruct((rows, cols), jnp.float32),
         2,
-        [spec((rows, feat))] * 8 + [pl.BlockSpec((depth, wide), lambda i, w: (0, i))] * 2,
-        pl.BlockSpec((rows, wide), lambda i, w: (0, i)),
-        [pltpu.VMEM((rows, 2 * depth), jnp.bfloat16)],
-    )(where, *slots, more, *weights)
-
-
-def second_kernel(where_ref, slot, more, weight_ref, acc_in, keep_ref, send_ref, acc_ref):
+        [spec((rows, feat))] * 7
+        + [whole]
+        + [pl.BlockSpec((x.shape[0], wide), lambda i, w: (0, i)) for x in weights],
+        whole,
+        [pltpu.VMEM((rows, 8 * feat), jnp.bfloat16)],
+    )(where, *slots, more, acc, *weights)
+
+
+def second_kernel(where_ref, slot, more, fetched_ref, passed_ref, acc_in, keep_ref, send_ref, acc_ref):
+    weight = []
+    for head in range(2):
+        place = partner_place(where_ref, 2 * (where_ref[NEAR] ^ 3) + head)
+        here = jnp.minimum(place, FETCHED - 1) * HEAD_DIM
+        there = jnp.maximum(place - FETCHED, 0) * HEAD_DIM
+        weight.append(
+            jnp.where(
+                place < FETCHED,
+                fetched_ref[pl.ds(pl.multiple_of(here, HEAD_DIM), HEAD_DIM), :],
+                passed_ref[pl.ds(pl.multiple_of(there, HEAD_DIM), HEAD_DIM), :],
+            )
+        )
     block = jnp.where(where_ref[INNER] == 1, slot[...], more[...])
-    acc = acc_in[...] + jnp.dot(block, weight_ref[...], preferred_element_type=jnp.float32)
+    acc = acc_in[...] + jnp.dot(
+        block, jnp.concatenate(weight, axis=0), preferred_element_type=jnp.float32
+    )
     acc_ref[...] = acc.reshape(acc_ref.shape)
     for sub, out in enumerate((keep_ref, send_ref)):
         for at in range(4):
             out[at] = acc_ref[where_ref[NEAR] ^ at, where_ref[SUB] ^ sub].astype(jnp.bfloat16)
 
 
-def second_product(where, chunk, slot, more, weight, acc):
+def second_product(where, chunk, slot, more, weights, acc):
     rows, feat = slot.shape
-    wide = weight.shape[1] // 2
+    cols = weights[0].shape[1]
+    wide = cols // 2
     out = jax.ShapeDtypeStruct((4, rows // 8, wide), jnp.bfloat16)
     return call(
         second_kernel,
@@ -471,11 +524,11 @@
         [out] * 2,
         1,
         [spec((rows, feat))] * 2
-        + [pl.BlockSpec((feat, wide), lambda i, w: (w[NEAR] ^ 3, chunk))]
+        + [pl.BlockSpec((x.shape[0], wide), lambda i, w: (0, chunk)) for x in weights]
         + [pl.BlockSpec((rows, wide), lambda i, w: (0, chunk))],
         [spec(out.shape)] * 2,
         [pltpu.VMEM((4, 2, rows // 8, wide), jnp.float32)],
-    )(where, slot, more, weight, acc)
+    )(where, slot, more, *weights, acc)
 
 
 def add_kernel(where_ref, keep_ref, term_ref, *outs):
@@ -496,22 +549,29 @@
 
 
 def share_tail(sizes, where, pieces, kv_pieces, out_weight, hidden_in, attn_gate):
-    fetched = swap(out_weight, "head", 2, 1)
-
-    mine, other = attend_halves(where, pieces)
-    other = swap(other, "head", 2, 1)
+    fetch, pass_on = FETCHED * HEAD_DIM, (8 - FETCHED) * HEAD_DIM
+    out_weight, where = lax.optimization_barrier((out_weight, where))
+    start = lax.axis_index("grp") * pass_on
+    fetched = swap(lax.dynamic_slice_in_dim(out_weight, start, fetch, 0), "head", 2, 1)
+    start = lax.axis_index("grp") * (fetch - pass_on)
+    passed = swap(lax.dynamic_slice_in_dim(fetched, start, pass_on, 0), "grp", 2, 1)
+
+    pieces = [pieces[0], *pieces[:0:-1]]
+    mine = attend_half(where, 0, pieces)
+    where, mine = lax.optimization_barrier((where, mine))
+    other = swap(attend_half(where, 1, pieces), "head", 2, 1)
+    acc = zeroth_product(where, mine, out_weight)
+    other, acc = lax.optimization_barrier((other, acc))
     slots = []
     for at, x in enumerate((mine, other)):
-        far, next_to = swap(x, "patch", 4, 2), swap(x, "patch", 4, 1)
-        far, next_to, other, x = lax.optimization_barrier((far, next_to, other, x))
-        if at == 1:
-            far, x, fetched = lax.optimization_barrier((far, x, fetched))
+        next_to, far = swap(x, "patch", 4, 1), swap(x, "patch", 4, 2)
+        next_to, far, other, x = lax.optimization_barrier((next_to, far, other, x))
         middle = swap(x, "patch", 4, 3, (1, 2))
         ends = lax.ppermute(far, "patch", [(1, 0), (2, 3)])
         slots.append([x, next_to, far, middle, ends])
-    first = [*slots[0][:4], *slots[1][:3]]
-    acc = first_product(where, first, slots[0][4], [out_weight, fetched])
-    terms = [second_product(where, at, *slots[1][3:], fetched, acc) for at in range(2)]
+    first = [slots[0][at] for at in (2, 1, 3)] + [slots[1][at] for at in (0, 2, 1)]
+    acc = first_product(where, first, slots[0][4], acc, [out_weight, fetched, passed])
+    terms = [second_product(where, at, *slots[1][3:], [fetched, passed], acc) for at in range(2)]
     blocks = []
     for keep, send in terms:
         total = add(where, keep, swap(send, "sub", 2, 1))
@@ -565,7 +625,9 @@
 
     arrays = (exponents, queries, fresh_kv, cached_kv)
     sent = pack(split, *arrays)
-    far_first = [swap(sent[rel - 1], "patch", n_patch, rel) for rel in range(split - 1, 0, -1)]
+    far_first = [
+        swap(x, "patch", n_patch, split - 1 - at) for at, x in enumerate(sent)
+    ]
     where, sent = lax.optimization_barrier((where, sent))
     pieces = [pack_own(split, where, *arrays), *far_first]
     kv_pieces = list(pieces)

time: 114 us -> 106 us (0.930)
  waiting for transfers between devices: 61.7 us -> 48.6 us
  Pallas kernels: 19.3 us -> 24 us
    ppermute x19 -> x20, waiting for transfers between devices: 58.9 us -> 46.1 us  [swap(): return lax.ppermute(x, axes, pairs)]
    pallas_call x1 -> x3, Pallas kernels: 4.77 us -> 8.36 us  [the longest x2 6.81 us: attend_half(): call(functools.partial(attend_half_kernel, half), 'attend', out, 1, [spec...]
    dynamic_slice x0 -> x2, local copies, waits for them, and re-layouts: none -> 1.4 us  [the longest x1 1.33 us: share_tail(): lax.dynamic_slice_in_dim(out_weight, start, fetch, 0)]
    unnamed x14 -> x16, local copies, waits for them, and re-layouts: 3.43 us -> 2.22 us
    ppermute x19 -> x20, starting transfers between devices: 26.3 us -> 26.4 us  [swap(): return lax.ppermute(x, axes, pairs)]
  transfers between devices with their start and end apart: 21 -> 22, of which waited for: 9 -> 9; matrix products, arithmetic and copies ran while one was open for 0% -> 1% of each run, Pallas kernels for 15% -> 17%
where the time goes in v14:
time: 106 us
  waiting for transfers between devices  48.6 us (46%)
  starting transfers between devices  29 us (27%)
  Pallas kernels  24 us (23%)
  local copies, waits for them, and re-layouts  3.7 us (3%)
    ppermute x20, waiting for transfers between devices, swap(): return lax.ppermute(x, axes, pairs)  46.1 us
    ppermute x20, starting transfers between devices, swap(): return lax.ppermute(x, axes, pairs)  26.4 us
    pallas_call x2, Pallas kernels, attend_half(): call(functools.partial(attend_half_kernel, half), 'attend', out, 1, [spec...  6.81 us
    pallas_call x1, Pallas kernels, first_product(): call(first_kernel, 'first', jax.ShapeDtypeStruct((rows, cols), jnp.float3...  5.73 us
    pallas_call x1, Pallas kernels, pack(): pl.pallas_call(functools.partial(pack_kernel, split, feat // HEAD_DIM), o...  3.54 us
    ppermute x2, starting transfers between devices, share_tail(): ends = lax.ppermute(far, 'patch', [(1, 0), (2, 3)])  2.58 us
    ppermute x2, waiting for transfers between devices, share_tail(): ends = lax.ppermute(far, 'patch', [(1, 0), (2, 3)])  2.5 us
    unnamed x16, local copies, waits for them, and re-layouts  2.22 us
  transfers between devices with their start and end apart: 22, of which 9 were waited for; matrix products, arithmetic and copies ran while one was open for 1% of the time, Pallas kernels for 17%

profile of v14, /device:TPU:0, one launch (start us, length us, event | category | flops | bytes accessed | tf_op | source)
XLA Modules:
  0.0 105.5 jit_solution(12504359862870140012)
XLA Ops:
  0.0 3.5 %pack.1 = (bf16[3,256,256]{2,1,0:T(8,128)(2,1)}, bf16[3,256,256]{2,1,0:T(8,128)(2,1)}, bf16[3,256,256]{2,1,0:T(8,128)(2,1)}) custom-call(s32[2,2,8]{2,1,0:T(2,128)} %exps_ref.3, bf16[256,1024]{1,0:T(8,128)(2,1)} %q_ref.3, bf16[2,256,1024]{2,1,0:T(8,128)(2,1)} %fresh_ref.3, bf16[2,1024,1024]{2,1,0:T(8,128)(2,1)} %cached_ref.3), custom_call_target="tpu_custom_call" | custom-call | tf_op jit(solution)/shard_map/pack/pallas_call | solution.py:114
  3.5 0.0 copy-start.7
  3.6 5.1 %collective-permute-start.2 = (bf16[3,256,256]{2,1,0:T(8,128)(2,1)}, bf16[3,256,256]{2,1,0:T(8,128)(2,1)S(1)}, u32[]{:S(2)}, u32[]{:S(2)}) collective-permute-start(bf16[3,256,256]{2,1,0:T(8,128)(2,1)} %get-tuple-element.33), channel_id=1, source_target_pairs={{0,12},{4,8},{8,4},{12,0},{1,13},{5,9},{9,5},{13,1},{2,14},{6,10},... | collective-permute-start | bytes 1179656 | tf_op jit(solution)/shard_map/ppermute | solution.py:50
  8.7 0.6 collective-permute-start
  9.3 0.1 stack.31.where_ref
  9.4 0.0 copy-start.5
  9.4 1.3 %constant_dynamic-slice_fusion.1 = bf16[640,1280]{1,0:T(8,128)(2,1)} fusion(bf16[1024,1280]{1,0:T(8,128)(2,1)S(1)} %copy-done, s32[]{:T(128)S(6)} %select_n.14), kind=kLoop, calls=%fused_computation.1 | loop fusion | bytes 3276804 | tf_op jit(solution)/shard_map/dynamic_slice | solution.py:555
  10.8 1.6 %collective-permute-start.8 = (bf16[640,1280]{1,0:T(8,128)(2,1)}, bf16[640,1280]{1,0:T(8,128)(2,1)S(1)}, u32[]{:S(2)}, u32[]{:S(2)}) collective-permute-start(bf16[640,1280]{1,0:T(8,128)(2,1)} %constant_dynamic-slice_fusion.1), channel_id=1, source_target_pairs={{0,2},{2,0},{1,3},{3,1},{4,6},{6,4},{5,7},{7,5},{8,10},{10,8},{9,1... | collective-permute-start | bytes 4915208 | tf_op jit(solution)/shard_map/ppermute | solution.py:50
  12.4 2.2 %copy-done.2 = bf16[2,1024,1024]{2,1,0:T(8,128)(2,1)S(1)} copy-done((bf16[2,1024,1024]{2,1,0:T(8,128)(2,1)S(1)}, bf16[2,1024,1024]{2,1,0:T(8,128)(2,1)}, u32[]{:S(2)}) %copy-start.2) | copy-done | bytes 4194328
  14.6 1.3 %own.1.refs_0_ = bf16[3,256,256]{2,1,0:T(8,128)(2,1)S(1)} custom-call(s32[6]{0:T(128)S(1)} %stack.31.where_ref, s32[2,2,8]{2,1,0:T(2,128)S(1)} %copy-done.7, bf16[256,1024]{1,0:T(8,128)(2,1)S(1)} %copy-done.5, bf16[2,256,1024]{2,1,0:T(8,128)(2,1)S(1)} %copy-done.3, bf16[2,1024,1024]{2,1,0:T(8,128)(2,1)S(1)} %copy-done.2), custom_call_target="tpu_custom_call" | custom-call | flops 49999998976 | tf_op jit(solution)/shard_map/own/pallas_call | solution.py:150
  15.9 0.0 copy-start.1
  15.9 3.1 %collective-permute-done.2.refs_3_ = bf16[3,256,256]{2,1,0:T(8,128)(2,1)S(1)} collective-permute-done((bf16[3,256,256]{2,1,0:T(8,128)(2,1)}, bf16[3,256,256]{2,1,0:T(8,128)(2,1)S(1)}, u32[]{:S(2)}, u32[]{:S(2)}) %collective-permute-start.2) | collective-permute-done | bytes 393248 | tf_op jit(solution)/shard_map/ppermute | solution.py:50
  19.0 23.5 %collective-permute-done.1.refs_2_ = bf16[3,256,256]{2,1,0:T(8,128)(2,1)S(1)} collective-permute-done((bf16[3,256,256]{2,1,0:T(8,128)(2,1)}, bf16[3,256,256]{2,1,0:T(8,128)(2,1)S(1)}, u32[]{:S(2)}, u32[]{:S(2)}) %collective-permute-start.1) | collective-permute-done | bytes 393248 | tf_op jit(solution)/shard_map/ppermute | solution.py:50
  42.4 3.4 %attend.2 = bf16[4,128,256]{2,1,0:T(8,128)(2,1)S(1)} custom-call(s32[6]{0:T(128)S(1)} %stack.31.where_ref, bf16[3,256,256]{2,1,0:T(8,128)(2,1)S(1)} %own.1.refs_0_, bf16[3,256,256]{2,1,0:T(8,128)(2,1)} %collective-permute-done.refs_1_, bf16[3,256,256]{2,1,0:T(8,128)(2,1)S(1)} %collective-permute-done.1.refs_2_, ...), custom_call_target="tpu_custom_call" | custom-call | flops 1 | tf_op jit(solution)/shard_map/attend/pallas_call | solution.py:409
  45.8 0.1 collective-permute-start.11
  45.9 3.0 %collective-permute-start.10 = (bf16[512,256]{1,0:T(8,128)(2,1)S(1)}, bf16[512,256]{1,0:T(8,128)(2,1)S(1)}, u32[]{:S(2)}, u32[]{:S(2)}) collective-permute-start(bf16[512,256]{1,0:T(8,128)(2,1)S(1)} %bitcast.10), channel_id=1, source_target_pairs={{0,4},{4,0},{8,12},{12,8},{1,5},{5,1},{9,13},{13,9},{2,6},{6,2},{1... | collective-permute-start | bytes 786440 | tf_op jit(solution)/shard_map/ppermute | solution.py:50
  49.0 3.4 %attend.3 = bf16[4,128,256]{2,1,0:T(8,128)(2,1)S(1)} custom-call(s32[6]{0:T(128)S(1)} %stack.31.where_ref, bf16[3,256,256]{2,1,0:T(8,128)(2,1)S(1)} %own.1.refs_0_, bf16[3,256,256]{2,1,0:T(8,128)(2,1)} %collective-permute-done.refs_1_, bf16[3,256,256]{2,1,0:T(8,128)(2,1)S(1)} %collective-permute-done.1.refs_2_, ...), custom_call_target="tpu_custom_call" | custom-call | flops 1 | tf_op jit(solution)/shard_map/attend/pallas_call | solution.py:409
  52.4 1.6 %collective-permute-start.3 = (bf16[512,256]{1,0:T(8,128)(2,1)S(1)}, bf16[512,256]{1,0:T(8,128)(2,1)S(1)}, u32[]{:S(2)}, u32[]{:S(2)}) collective-permute-start(bf16[512,256]{1,0:T(8,128)(2,1)S(1)} %bitcast.13), channel_id=1, source_target_pairs={{0,2},{2,0},{1,3},{3,1},{4,6},{6,4},{5,7},{7,5},{8,10},{10,8},{9,1... | collective-permute-start | bytes 786440 | tf_op jit(solution)/shard_map/ppermute | solution.py:50
  53.9 0.1 constant_dynamic-slice_fusion
  54.0 1.6 %collective-permute-start.9 = (bf16[384,1280]{1,0:T(8,128)(2,1)S(1)}, bf16[384,1280]{1,0:T(8,128)(2,1)S(1)}, u32[]{:S(2)}, u32[]{:S(2)}) collective-permute-start(bf16[384,1280]{1,0:T(8,128)(2,1)S(1)} %constant_dynamic-slice_fusion), channel_id=1, source_target_pairs={{0,16},{16,0},{1,17},{17,1},{2,18},{18,2},{3,19},{19,3},{4,20},{20... | collective-permute-start | bytes 2949128 | tf_op jit(solution)/shard_map/ppermute | solution.py:50
  55.6 1.5 %zeroth.1.refs_7_ = f32[512,1280]{1,0:T(8,128)S(1)} custom-call(s32[6]{0:T(128)S(1)} %stack.31.where_ref, bf16[512,256]{1,0:T(8,128)(2,1)S(1)} %bitcast.11, bf16[1024,1280]{1,0:T(8,128)(2,1)S(1)} %copy-done.1), custom_call_target="tpu_custom_call" | custom-call | flops 20000000000 | tf_op jit(solution)/shard_map/zeroth/pallas_call | solution.py:428
  57.1 1.9 %collective-permute-done.3.refs_3_ = bf16[512,256]{1,0:T(8,128)(2,1)S(1)} collective-permute-done((bf16[512,256]{1,0:T(8,128)(2,1)S(1)}, bf16[512,256]{1,0:T(8,128)(2,1)S(1)}, u32[]{:S(2)}, u32[]{:S(2)}) %collective-permute-start.3) | collective-permute-done | bytes 262176 | tf_op jit(solution)/shard_map/ppermute | solution.py:50
  59.0 0.4 collective-permute-start.5
  59.4 1.7 %collective-permute-start.4 = (bf16[512,256]{1,0:T(8,128)(2,1)S(1)}, bf16[512,256]{1,0:T(8,128)(2,1)S(1)}, u32[]{:S(2)}, u32[]{:S(2)}) collective-permute-start(bf16[512,256]{1,0:T(8,128)(2,1)S(1)} %collective-permute-done.3.refs_3_), channel_id=1, source_target_pairs={{0,4},{4,0},{8,12},{12,8},{1,5},{5,1},{9,13},{13,9},{2,6},{6,2},{1... | collective-permute-start | bytes 786440 | tf_op jit(solution)/shard_map/ppermute | solution.py:50
  61.2 0.7 collective-permute-start.12
  61.8 1.3 %collective-permute-start.13 = (bf16[512,256]{1,0:T(8,128)(2,1)S(1)}, bf16[512,256]{1,0:T(8,128)(2,1)S(1)}, u32[]{:S(2)}, u32[]{:S(2)}) collective-permute-start(bf16[512,256]{1,0:T(8,128)(2,1)S(1)} %collective-permute-done.11.refs_0_), channel_id=1, source_target_pairs={{4,0},{8,12},{5,1},{9,13},{6,2},{10,14},{7,3},{11,15},{20,16},{24,... | collective-permute-start | bytes 786440 | tf_op jit(solution)/shard_map/ppermute | solution.py:570
  63.1 8.8 %collective-permute-done.5.refs_4_ = bf16[512,256]{1,0:T(8,128)(2,1)S(1)} collective-permute-done((bf16[512,256]{1,0:T(8,128)(2,1)S(1)}, bf16[512,256]{1,0:T(8,128)(2,1)S(1)}, u32[]{:S(2)}, u32[]{:S(2)}) %collective-permute-start.5) | collective-permute-done | bytes 262176 | tf_op jit(solution)/shard_map/ppermute | solution.py:50
  71.9 1.4 %collective-permute-done.4.refs_5_ = bf16[512,256]{1,0:T(8,128)(2,1)S(1)} collective-permute-done((bf16[512,256]{1,0:T(8,128)(2,1)S(1)}, bf16[512,256]{1,0:T(8,128)(2,1)S(1)}, u32[]{:S(2)}, u32[]{:S(2)}) %collective-permute-start.4) | collective-permute-done | bytes 262176 | tf_op jit(solution)/shard_map/ppermute | solution.py:50
  73.3 0.7 collective-permute-start.6
  74.0 1.3 %collective-permute-start.7 = (bf16[512,256]{1,0:T(8,128)(2,1)S(1)}, bf16[512,256]{1,0:T(8,128)(2,1)S(1)}, u32[]{:S(2)}, u32[]{:S(2)}) collective-permute-start(bf16[512,256]{1,0:T(8,128)(2,1)S(1)} %collective-permute-done.5.refs_4_), channel_id=1, source_target_pairs={{4,0},{8,12},{5,1},{9,13},{6,2},{10,14},{7,3},{11,15},{20,16},{24,... | collective-permute-start | bytes 786440 | tf_op jit(solution)/shard_map/ppermute | solution.py:570
  75.3 2.5 %collective-permute-done.13.refs_6_ = bf16[512,256]{1,0:T(8,128)(2,1)S(1)} collective-permute-done((bf16[512,256]{1,0:T(8,128)(2,1)S(1)}, bf16[512,256]{1,0:T(8,128)(2,1)S(1)}, u32[]{:S(2)}, u32[]{:S(2)}) %collective-permute-start.13) | collective-permute-done | bytes 262176 | tf_op jit(solution)/shard_map/ppermute | solution.py:570
  77.8 5.7 %first.1.acc_in = f32[512,1280]{1,0:T(8,128)S(1)} custom-call(s32[6]{0:T(128)S(1)} %stack.31.where_ref, bf16[512,256]{1,0:T(8,128)(2,1)S(1)} %collective-permute-done.11.refs_0_, bf16[512,256]{1,0:T(8,128)(2,1)S(1)} %collective-permute-done.10.refs_1_, bf16[512,256]{1,0:T(8,128)(2,1)S(1)} %collective-permute-done.12.refs_2_, ...), custom_call_target="tpu_custom_call" | custom-call | flops 1 | tf_op jit(solution)/shard_map/first/pallas_call | solution.py:480
  83.5 1.1 %second.3 = (bf16[4,64,640]{2,1,0:T(8,128)(2,1)S(1)}, bf16[4,64,640]{2,1,0:T(8,128)(2,1)S(1)}) custom-call(s32[6]{0:T(128)S(1)} %stack.31.where_ref, bf16[512,256]{1,0:T(8,128)(2,1)S(1)} %collective-permute-done.6.slot, bf16[512,256]{1,0:T(8,128)(2,1)S(1)} %collective-permute-done.7.more, bf16[640,1280]{1,0:T(8,128)(2,1)S(1)} %collective-permute-done.8.refs_9_.fetched_ref, ...), custom_call_target="tpu_custom_call" | custom-call | flops 1 | tf_op jit(solution)/shard_map/second/pallas_call | solution.py:521
  84.7 0.0 copy-start.4
  84.7 0.0 copy-start.6
  84.7 0.1 collective-permute-start.18
  84.8 1.1 %second.2 = (bf16[4,64,640]{2,1,0:T(8,128)(2,1)S(1)}, bf16[4,64,640]{2,1,0:T(8,128)(2,1)S(1)}) custom-call(s32[6]{0:T(128)S(1)} %stack.31.where_ref, bf16[512,256]{1,0:T(8,128)(2,1)S(1)} %collective-permute-done.6.slot, bf16[512,256]{1,0:T(8,128)(2,1)S(1)} %collective-permute-done.7.more, bf16[640,1280]{1,0:T(8,128)(2,1)S(1)} %collective-permute-done.8.refs_9_.fetched_ref, ...), custom_call_target="tpu_custom_call" | custom-call | flops 1 | tf_op jit(solution)/shard_map/second/pallas_call | solution.py:521
  85.9 0.6 collective-permute-start.14
  86.4 0.6 add.16
  87.1 2.0 %collective-permute-start.19 = (bf16[64,640]{1,0:T(8,128)(2,1)S(1)}, bf16[64,640]{1,0:T(8,128)(2,1)S(1)}, u32[]{:S(2)}, u32[]{:S(2)}) collective-permute-start(bf16[64,640]{1,0:T(8,128)(2,1)S(1)} %get-tuple-element.58), channel_id=1, source_target_pairs={{0,12},{4,8},{8,4},{12,0},{1,13},{5,9},{9,5},{13,1},{2,14},{6,10},... | collective-permute-start | bytes 245768 | tf_op jit(solution)/shard_map/ppermute | solution.py:50
  89.1 2.4 %collective-permute-start.21 = (bf16[64,640]{1,0:T(8,128)(2,1)S(1)}, bf16[64,640]{1,0:T(8,128)(2,1)S(1)}, u32[]{:S(2)}, u32[]{:S(2)}) collective-permute-start(bf16[64,640]{1,0:T(8,128)(2,1)S(1)} %get-tuple-element.60), channel_id=1, source_target_pairs={{0,4},{4,0},{8,12},{12,8},{1,5},{5,1},{9,13},{13,9},{2,6},{6,2},{1... | collective-permute-start | bytes 245768 | tf_op jit(solution)/shard_map/ppermute | solution.py:50
  91.5 0.6 add.15
  92.1 2.0 %collective-permute-start.15 = (bf16[64,640]{1,0:T(8,128)(2,1)S(1)}, bf16[64,640]{1,0:T(8,128)(2,1)S(1)}, u32[]{:S(2)}, u32[]{:S(2)}) collective-permute-start(bf16[64,640]{1,0:T(8,128)(2,1)S(1)} %get-tuple-element.52), channel_id=1, source_target_pairs={{0,12},{4,8},{8,4},{12,0},{1,13},{5,9},{9,5},{13,1},{2,14},{6,10},... | collective-permute-start | bytes 245768 | tf_op jit(solution)/shard_map/ppermute | solution.py:50
  94.2 0.1 collective-permute-done.19.refs_5_
  94.3 2.3 %collective-permute-start.17 = (bf16[64,640]{1,0:T(8,128)(2,1)S(1)}, bf16[64,640]{1,0:T(8,128)(2,1)S(1)}, u32[]{:S(2)}, u32[]{:S(2)}) collective-permute-start(bf16[64,640]{1,0:T(8,128)(2,1)S(1)} %get-tuple-element.54), channel_id=1, source_target_pairs={{0,4},{4,0},{8,12},{12,8},{1,5},{5,1},{9,13},{13,9},{2,6},{6,2},{1... | collective-permute-start | bytes 245768 | tf_op jit(solution)/shard_map/ppermute | solution.py:50
  96.6 3.0 %collective-permute-done.20.refs_6_ = bf16[64,640]{1,0:T(8,128)(2,1)S(1)} collective-permute-done((bf16[64,640]{1,0:T(8,128)(2,1)S(1)}, bf16[64,640]{1,0:T(8,128)(2,1)S(1)}, u32[]{:S(2)}, u32[]{:S(2)}) %collective-permute-start.20) | collective-permute-done | bytes 81952 | tf_op jit(solution)/shard_map/ppermute | solution.py:50
  99.6 4.2 %collective-permute-done.16.refs_2_ = bf16[64,640]{1,0:T(8,128)(2,1)S(1)} collective-permute-done((bf16[64,640]{1,0:T(8,128)(2,1)S(1)}, bf16[64,640]{1,0:T(8,128)(2,1)S(1)}, u32[]{:S(2)}, u32[]{:S(2)}) %collective-permute-start.16) | collective-permute-done | bytes 81952 | tf_op jit(solution)/shard_map/ppermute | solution.py:50
  103.9 1.6 %mix.1 = bf16[64,5120]{1,0:T(8,128)(2,1)} custom-call(s32[6]{0:T(128)S(1)} %stack.31.where_ref, bf16[64,5120]{1,0:T(8,128)(2,1)S(1)} %copy-done.4, f32[1,5120]{1,0:T(1,128)S(1)} %bitcast.14, bf16[64,640]{1,0:T(8,128)(2,1)S(1)} %get-tuple-element.51.refs_0_, bf16[64,640]{1,0:T(8,128)(2,1)S(1)} %collective-permute-done.15.refs_1_, ...), custom_call_target="tpu_custom_call" | custom-call | flops 1 | tf_op jit(solution)/shard_map/mix/pallas_call | solution.py:598
  (26 shorter events, 0.1 us)
Async XLA Ops:
  0.0 9.4 %copy-start = (bf16[1024,1280]{1,0:T(8,128)(2,1)S(1)}, bf16[1024,1280]{1,0:T(8,128)(2,1)}, u32[]{:S(2)}) copy-start(bf16[1024,1280]{1,0:T(8,128)(2,1)} %refs_8_) | copy-start | bytes 7864324
  3.5 8.8 %copy-start.7 = (s32[2,2,8]{2,1,0:T(2,128)S(1)}, s32[2,2,8]{2,1,0:T(2,128)}, u32[]{:S(2)}) copy-start(s32[2,2,8]{2,1,0:T(2,128)} %exps_ref.3) | copy-start | bytes 388
  3.6 15.4 %collective-permute-start.2 = (bf16[3,256,256]{2,1,0:T(8,128)(2,1)}, bf16[3,256,256]{2,1,0:T(8,128)(2,1)S(1)}, u32[]{:S(2)}, u32[]{:S(2)}) collective-permute-start(bf16[3,256,256]{2,1,0:T(8,128)(2,1)} %get-tuple-element.33), channel_id=1, source_target_pairs={{0,12},{4,8},{8,4},{12,0},{1,13},{5,9},{9,5},{13,1},{2,14},{6,10},... | collective-permute-start | bytes 1179656 | tf_op jit(solution)/shard_map/ppermute | solution.py:50
  8.7 33.8 %collective-permute-start.1 = (bf16[3,256,256]{2,1,0:T(8,128)(2,1)}, bf16[3,256,256]{2,1,0:T(8,128)(2,1)S(1)}, u32[]{:S(2)}, u32[]{:S(2)}) collective-permute-start(bf16[3,256,256]{2,1,0:T(8,128)(2,1)} %get-tuple-element.34), channel_id=1, source_target_pairs={{0,8},{4,12},{8,0},{12,4},{1,9},{5,13},{9,1},{13,5},{2,10},{6,14},... | collective-permute-start | bytes 1179656 | tf_op jit(solution)/shard_map/ppermute | solution.py:50
  8.7 33.8 %collective-permute-start = (bf16[3,256,256]{2,1,0:T(8,128)(2,1)}, bf16[3,256,256]{2,1,0:T(8,128)(2,1)}, u32[]{:S(2)}, u32[]{:S(2)}) collective-permute-start(bf16[3,256,256]{2,1,0:T(8,128)(2,1)} %get-tuple-element.35), channel_id=1, source_target_pairs={{0,4},{4,0},{8,12},{12,8},{1,5},{5,1},{9,13},{13,9},{2,6},{6,2},{1... | collective-permute-start | bytes 1179656 | tf_op jit(solution)/shard_map/ppermute | solution.py:50
  9.4 3.0 %copy-start.3 = (bf16[2,256,1024]{2,1,0:T(8,128)(2,1)S(1)}, bf16[2,256,1024]{2,1,0:T(8,128)(2,1)}, u32[]{:S(2)}) copy-start(bf16[2,256,1024]{2,1,0:T(8,128)(2,1)} %fresh_ref.3) | copy-start | bytes 3145732
  9.4 3.0 %copy-start.5 = (bf16[256,1024]{1,0:T(8,128)(2,1)S(1)}, bf16[256,1024]{1,0:T(8,128)(2,1)}, u32[]{:S(2)}) copy-start(bf16[256,1024]{1,0:T(8,128)(2,1)} %q_ref.3) | copy-start | bytes 1572868
  10.8 43.2 %collective-permute-start.8 = (bf16[640,1280]{1,0:T(8,128)(2,1)}, bf16[640,1280]{1,0:T(8,128)(2,1)S(1)}, u32[]{:S(2)}, u32[]{:S(2)}) collective-permute-start(bf16[640,1280]{1,0:T(8,128)(2,1)} %constant_dynamic-slice_fusion.1), channel_id=1, source_target_pairs={{0,2},{2,0},{1,3},{3,1},{4,6},{6,4},{5,7},{7,5},{8,10},{10,8},{9,1... | collective-permute-start | bytes 4915208 | tf_op jit(solution)/shard_map/ppermute | solution.py:50
  12.4 2.2 %copy-start.2 = (bf16[2,1024,1024]{2,1,0:T(8,128)(2,1)S(1)}, bf16[2,1024,1024]{2,1,0:T(8,128)(2,1)}, u32[]{:S(2)}) copy-start(bf16[2,1024,1024]{2,1,0:T(8,128)(2,1)} %cached_ref.3) | copy-start | bytes 12582916
  15.9 39.7 %copy-start.1 = (bf16[1024,1280]{1,0:T(8,128)(2,1)S(1)}, bf16[1024,1280]{1,0:T(8,128)(2,1)}, u32[]{:S(2)}) copy-start(bf16[1024,1280]{1,0:T(8,128)(2,1)} %refs_8_) | copy-start | bytes 7864324
  45.8 15.3 %collective-permute-start.11 = (bf16[512,256]{1,0:T(8,128)(2,1)S(1)}, bf16[512,256]{1,0:T(8,128)(2,1)S(1)}, u32[]{:S(2)}, u32[]{:S(2)}) collective-permute-start(bf16[512,256]{1,0:T(8,128)(2,1)S(1)} %bitcast.9), channel_id=1, source_target_pairs={{0,8},{4,12},{8,0},{12,4},{1,9},{5,13},{9,1},{13,5},{2,10},{6,14},... | collective-permute-start | bytes 786440 | tf_op jit(solution)/shard_map/ppermute | solution.py:50
  45.9 15.2 %collective-permute-start.10 = (bf16[512,256]{1,0:T(8,128)(2,1)S(1)}, bf16[512,256]{1,0:T(8,128)(2,1)S(1)}, u32[]{:S(2)}, u32[]{:S(2)}) collective-permute-start(bf16[512,256]{1,0:T(8,128)(2,1)S(1)} %bitcast.10), channel_id=1, source_target_pairs={{0,4},{4,0},{8,12},{12,8},{1,5},{5,1},{9,13},{13,9},{2,6},{6,2},{1... | collective-permute-start | bytes 786440 | tf_op jit(solution)/shard_map/ppermute | solution.py:50
  52.4 6.7 %collective-permute-start.3 = (bf16[512,256]{1,0:T(8,128)(2,1)S(1)}, bf16[512,256]{1,0:T(8,128)(2,1)S(1)}, u32[]{:S(2)}, u32[]{:S(2)}) collective-permute-start(bf16[512,256]{1,0:T(8,128)(2,1)S(1)} %bitcast.13), channel_id=1, source_target_pairs={{0,2},{2,0},{1,3},{3,1},{4,6},{6,4},{5,7},{7,5},{8,10},{10,8},{9,1... | collective-permute-start | bytes 786440 | tf_op jit(solution)/shard_map/ppermute | solution.py:50
  54.0 23.8 %collective-permute-start.9 = (bf16[384,1280]{1,0:T(8,128)(2,1)S(1)}, bf16[384,1280]{1,0:T(8,128)(2,1)S(1)}, u32[]{:S(2)}, u32[]{:S(2)}) collective-permute-start(bf16[384,1280]{1,0:T(8,128)(2,1)S(1)} %constant_dynamic-slice_fusion), channel_id=1, source_target_pairs={{0,16},{16,0},{1,17},{17,1},{2,18},{18,2},{3,19},{19,3},{4,20},{20... | collective-permute-start | bytes 2949128 | tf_op jit(solution)/shard_map/ppermute | solution.py:50
  59.0 12.8 %collective-permute-start.5 = (bf16[512,256]{1,0:T(8,128)(2,1)S(1)}, bf16[512,256]{1,0:T(8,128)(2,1)S(1)}, u32[]{:S(2)}, u32[]{:S(2)}) collective-permute-start(bf16[512,256]{1,0:T(8,128)(2,1)S(1)} %collective-permute-done.3.refs_3_), channel_id=1, source_target_pairs={{0,8},{4,12},{8,0},{12,4},{1,9},{5,13},{9,1},{13,5},{2,10},{6,14},... | collective-permute-start | bytes 786440 | tf_op jit(solution)/shard_map/ppermute | solution.py:50
  59.4 13.9 %collective-permute-start.4 = (bf16[512,256]{1,0:T(8,128)(2,1)S(1)}, bf16[512,256]{1,0:T(8,128)(2,1)S(1)}, u32[]{:S(2)}, u32[]{:S(2)}) collective-permute-start(bf16[512,256]{1,0:T(8,128)(2,1)S(1)} %collective-permute-done.3.refs_3_), channel_id=1, source_target_pairs={{0,4},{4,0},{8,12},{12,8},{1,5},{5,1},{9,13},{13,9},{2,6},{6,2},{1... | collective-permute-start | bytes 786440 | tf_op jit(solution)/shard_map/ppermute | solution.py:50
  61.2 14.1 %collective-permute-start.12 = (bf16[512,256]{1,0:T(8,128)(2,1)S(1)}, bf16[512,256]{1,0:T(8,128)(2,1)S(1)}, u32[]{:S(2)}, u32[]{:S(2)}) collective-permute-start(bf16[512,256]{1,0:T(8,128)(2,1)S(1)} %bitcast.12), channel_id=1, source_target_pairs={{4,8},{8,4},{5,9},{9,5},{6,10},{10,6},{7,11},{11,7},{20,24},{24,20... | collective-permute-start | bytes 786440 | tf_op jit(solution)/shard_map/ppermute | solution.py:50
  61.8 16.0 %collective-permute-start.13 = (bf16[512,256]{1,0:T(8,128)(2,1)S(1)}, bf16[512,256]{1,0:T(8,128)(2,1)S(1)}, u32[]{:S(2)}, u32[]{:S(2)}) collective-permute-start(bf16[512,256]{1,0:T(8,128)(2,1)S(1)} %collective-permute-done.11.refs_0_), channel_id=1, source_target_pairs={{4,0},{8,12},{5,1},{9,13},{6,2},{10,14},{7,3},{11,15},{20,16},{24,... | collective-permute-start | bytes 786440 | tf_op jit(solution)/shard_map/ppermute | solution.py:570
  73.3 10.2 %collective-permute-start.6 = (bf16[512,256]{1,0:T(8,128)(2,1)S(1)}, bf16[512,256]{1,0:T(8,128)(2,1)S(1)}, u32[]{:S(2)}, u32[]{:S(2)}) collective-permute-start(bf16[512,256]{1,0:T(8,128)(2,1)S(1)} %collective-permute-done.3.refs_3_), channel_id=1, source_target_pairs={{4,8},{8,4},{5,9},{9,5},{6,10},{10,6},{7,11},{11,7},{20,24},{24,20... | collective-permute-start | bytes 786440 | tf_op jit(solution)/shard_map/ppermute | solution.py:50
  74.0 9.6 %collective-permute-start.7 = (bf16[512,256]{1,0:T(8,128)(2,1)S(1)}, bf16[512,256]{1,0:T(8,128)(2,1)S(1)}, u32[]{:S(2)}, u32[]{:S(2)}) collective-permute-start(bf16[512,256]{1,0:T(8,128)(2,1)S(1)} %collective-permute-done.5.refs_4_), channel_id=1, source_target_pairs={{4,0},{8,12},{5,1},{9,13},{6,2},{10,14},{7,3},{11,15},{20,16},{24,... | collective-permute-start | bytes 786440 | tf_op jit(solution)/shard_map/ppermute | solution.py:570
  84.7 19.2 %copy-start.4 = (bf16[64,5120]{1,0:T(8,128)(2,1)S(1)}, bf16[64,5120]{1,0:T(8,128)(2,1)}, u32[]{:S(2)}) copy-start(bf16[64,5120]{1,0:T(8,128)(2,1)} %hidden_ref.1) | copy-start | bytes 1966084
  84.7 19.2 %copy-start.6 = (f32[5120]{0:T(1024)S(1)}, f32[5120]{0:T(1024)}, u32[]{:S(2)}) copy-start(f32[5120]{0:T(1024)} %param.13) | copy-start | bytes 61444
  84.7 1.8 %collective-permute-start.18 = (bf16[4,64,640]{2,1,0:T(8,128)(2,1)S(1)}, bf16[4,64,640]{2,1,0:T(8,128)(2,1)S(1)}, u32[]{:S(2)}, u32[]{:S(2)}) collective-permute-start(bf16[4,64,640]{2,1,0:T(8,128)(2,1)S(1)} %get-tuple-element.56), channel_id=1, source_target_pairs={{0,1},{1,0},{2,3},{3,2},{4,5},{5,4},{6,7},{7,6},{8,9},{9,8},{10,11... | collective-permute-start | bytes 983048 | tf_op jit(solution)/shard_map/ppermute | solution.py:50
  85.9 5.6 %collective-permute-start.14 = (bf16[4,64,640]{2,1,0:T(8,128)(2,1)S(1)}, bf16[4,64,640]{2,1,0:T(8,128)(2,1)S(1)}, u32[]{:S(2)}, u32[]{:S(2)}) collective-permute-start(bf16[4,64,640]{2,1,0:T(8,128)(2,1)S(1)} %get-tuple-element.50), channel_id=1, source_target_pairs={{0,1},{1,0},{2,3},{3,2},{4,5},{5,4},{6,7},{7,6},{8,9},{9,8},{10,11... | collective-permute-start | bytes 983048 | tf_op jit(solution)/shard_map/ppermute | solution.py:50
  87.1 7.3 %collective-permute-start.19 = (bf16[64,640]{1,0:T(8,128)(2,1)S(1)}, bf16[64,640]{1,0:T(8,128)(2,1)S(1)}, u32[]{:S(2)}, u32[]{:S(2)}) collective-permute-start(bf16[64,640]{1,0:T(8,128)(2,1)S(1)} %get-tuple-element.58), channel_id=1, source_target_pairs={{0,12},{4,8},{8,4},{12,0},{1,13},{5,9},{9,5},{13,1},{2,14},{6,10},... | collective-permute-start | bytes 245768 | tf_op jit(solution)/shard_map/ppermute | solution.py:50
  89.1 10.6 %collective-permute-start.20 = (bf16[64,640]{1,0:T(8,128)(2,1)S(1)}, bf16[64,640]{1,0:T(8,128)(2,1)S(1)}, u32[]{:S(2)}, u32[]{:S(2)}) collective-permute-start(bf16[64,640]{1,0:T(8,128)(2,1)S(1)} %get-tuple-element.59), channel_id=1, source_target_pairs={{0,8},{4,12},{8,0},{12,4},{1,9},{5,13},{9,1},{13,5},{2,10},{6,14},... | collective-permute-start | bytes 245768 | tf_op jit(solution)/shard_map/ppermute | solution.py:50
  89.1 10.6 %collective-permute-start.21 = (bf16[64,640]{1,0:T(8,128)(2,1)S(1)}, bf16[64,640]{1,0:T(8,128)(2,1)S(1)}, u32[]{:S(2)}, u32[]{:S(2)}) collective-permute-start(bf16[64,640]{1,0:T(8,128)(2,1)S(1)} %get-tuple-element.60), channel_id=1, source_target_pairs={{0,4},{4,0},{8,12},{12,8},{1,5},{5,1},{9,13},{13,9},{2,6},{6,2},{1... | collective-permute-start | bytes 245768 | tf_op jit(solution)/shard_map/ppermute | solution.py:50
  92.1 7.5 %collective-permute-start.15 = (bf16[64,640]{1,0:T(8,128)(2,1)S(1)}, bf16[64,640]{1,0:T(8,128)(2,1)S(1)}, u32[]{:S(2)}, u32[]{:S(2)}) collective-permute-start(bf16[64,640]{1,0:T(8,128)(2,1)S(1)} %get-tuple-element.52), channel_id=1, source_target_pairs={{0,12},{4,8},{8,4},{12,0},{1,13},{5,9},{9,5},{13,1},{2,14},{6,10},... | collective-permute-start | bytes 245768 | tf_op jit(solution)/shard_map/ppermute | solution.py:50
  94.2 9.7 %collective-permute-start.16 = (bf16[64,640]{1,0:T(8,128)(2,1)S(1)}, bf16[64,640]{1,0:T(8,128)(2,1)S(1)}, u32[]{:S(2)}, u32[]{:S(2)}) collective-permute-start(bf16[64,640]{1,0:T(8,128)(2,1)S(1)} %get-tuple-element.53), channel_id=1, source_target_pairs={{0,8},{4,12},{8,0},{12,4},{1,9},{5,13},{9,1},{13,5},{2,10},{6,14},... | collective-permute-start | bytes 245768 | tf_op jit(solution)/shard_map/ppermute | solution.py:50
  94.3 9.6 %collective-permute-start.17 = (bf16[64,640]{1,0:T(8,128)(2,1)S(1)}, bf16[64,640]{1,0:T(8,128)(2,1)S(1)}, u32[]{:S(2)}, u32[]{:S(2)}) collective-permute-start(bf16[64,640]{1,0:T(8,128)(2,1)S(1)} %get-tuple-element.54), channel_id=1, source_target_pairs={{0,4},{4,0},{8,12},{12,8},{1,5},{5,1},{9,13},{13,9},{2,6},{6,2},{1... | collective-permute-start | bytes 245768 | tf_op jit(solution)/shard_map/ppermute | solution.py:50

commit v15 on v14

--- a/solution.py
+++ b/solution.py
@@ -12,7 +12,7 @@
 SCALE_ROWS = 128
 SATURATION = 448.0
 PACK_ROWS = 64
-VMEM_BYTES = 32 * 1024 * 1024
+VMEM_BYTES = 16 * 1024 * 1024
 PACK_VMEM_BYTES = 60 * 1024 * 1024
 ATTEND_FLOPS = 1
 PROJECT_FLOPS = 1
@@ -417,23 +417,31 @@
     )(where, *pieces).reshape(-1, feat)
 
 
-def zeroth_kernel(where_ref, slot, weight_ref, out_ref):
-    out_ref[...] = jnp.dot(slot[...], weight_ref[...], preferred_element_type=jnp.float32)
-
-
-def zeroth_product(where, slot, weight):
-    rows, feat = slot.shape
+def add_product_kernel(count, where_ref, *refs):
+    total = refs[2 * count][...] if len(refs) > 2 * count + 1 else None
+    for slot, weight in zip(refs[:count], refs[count : 2 * count]):
+        term = jnp.dot(slot[...], weight[...], preferred_element_type=jnp.float32)
+        total = term if total is None else total + term
+    refs[-1][...] = total
+
+
+def add_product(where, slots, weight, acc=None):
+    rows, feat = next(iter(slots.values())).shape
     cols = weight.shape[1]
     wide = cols // 2
-    return call(
-        zeroth_kernel,
-        "zeroth",
+    whole = pl.BlockSpec((rows, wide), lambda i, w: (0, i))
+    rels = list(slots)
+    return call(
+        functools.partial(add_product_kernel, len(rels)),
+        "products",
         jax.ShapeDtypeStruct((rows, cols), jnp.float32),
         2,
-        [spec((rows, feat)), pl.BlockSpec((feat, wide), lambda i, w: (w[NEAR], i))],
-        pl.BlockSpec((rows, wide), lambda i, w: (0, i)),
-        flops=ZERO_FLOPS,
-    )(where, slot, weight)
+        [spec((rows, feat))] * len(rels)
+        + [pl.BlockSpec((feat, wide), lambda i, w, rel=rel: (w[NEAR] ^ rel, i)) for rel in rels]
+        + ([] if acc is None else [whole]),
+        whole,
+        flops=ZERO_FLOPS if acc is None else 1,
+    )(where, *slots.values(), *[weight] * len(rels), *([] if acc is None else [acc]))
 
 
 def partner_place(where_ref, head):
@@ -441,53 +449,47 @@
 
 
 def first_kernel(where_ref, *refs):
-    slots, refs = refs[:6], refs[6:]
-    more, acc_ref, own_ref, fetched_ref, passed_ref, out_ref, held_ref = refs
-    rows, feat = slots[0].shape
-    depth, cut = own_ref.shape[0], own_ref.shape[0] + fetched_ref.shape[0]
-
-    def put(place, block):
-        lanes = pl.ds(pl.multiple_of(place * HEAD_DIM, HEAD_DIM), block.shape[1])
-        held_ref[:, lanes] = block
+    last, more, slots = refs[0], refs[1], refs[2:5]
+    acc_ref, own_ref, fetched_ref, passed_ref, out_ref, held_ref = refs[5:]
+    rows, feat = last.shape
+    cut = fetched_ref.shape[0]
+
+    def put(at, block):
+        for head in range(2):
+            there = partner_place(where_ref, 2 * (where_ref[NEAR] ^ at) + head)
+            lanes = pl.ds(pl.multiple_of(there * HEAD_DIM, HEAD_DIM), HEAD_DIM)
+            held_ref[:, lanes] = block[:, head * HEAD_DIM : (head + 1) * HEAD_DIM]
 
     @pl.when(pl.program_id(0) == 0)
     def arrange():
-        nothing = jnp.zeros((rows, feat), jnp.bfloat16)
-        mine, partner = dict(zip((2, 1, 3), slots[:3])), dict(zip((0, 2, 1), slots[3:]))
-        for at in range(4):
-            place = where_ref[NEAR] ^ at
-            block = mine[at][...] if at else nothing
-            if at == 3:
-                block = jnp.where(where_ref[INNER] == 1, block, more[...])
-            put(2 * place, block)
-            block = nothing if at == 3 else partner[at][...]
-            for head in range(2):
-                there = partner_place(where_ref, 2 * place + head)
-                put(8 + there, block[:, head * HEAD_DIM : (head + 1) * HEAD_DIM])
-
+        for at, slot in zip((0, 2, 1), slots):
+            put(at, slot[...])
+        put(3, jnp.zeros((rows, feat), jnp.bfloat16))
+
+    block = jnp.where(where_ref[INNER] == 1, last[...], more[...])
     acc = acc_ref[...]
-    acc += jnp.dot(held_ref[:, :depth], own_ref[...], preferred_element_type=jnp.float32)
-    acc += jnp.dot(held_ref[:, depth:cut], fetched_ref[...], preferred_element_type=jnp.float32)
+    acc += jnp.dot(block, own_ref[...], preferred_element_type=jnp.float32)
+    acc += jnp.dot(held_ref[:, :cut], fetched_ref[...], preferred_element_type=jnp.float32)
     acc += jnp.dot(held_ref[:, cut:], passed_ref[...], preferred_element_type=jnp.float32)
     out_ref[...] = acc
 
 
-def first_product(where, slots, more, acc, weights):
-    rows, feat = slots[0].shape
-    cols = weights[0].shape[1]
-    wide = cols // 2
+def first_product(where, last, more, slots, acc, weights):
+    rows, feat = last.shape
+    own, fetched, passed = weights
+    wide = own.shape[1] // 2
     whole = pl.BlockSpec((rows, wide), lambda i, w: (0, i))
     return call(
         first_kernel,
         "first",
-        jax.ShapeDtypeStruct((rows, cols), jnp.float32),
+        jax.ShapeDtypeStruct(acc.shape, jnp.float32),
         2,
-        [spec((rows, feat))] * 7
-        + [whole]
-        + [pl.BlockSpec((x.shape[0], wide), lambda i, w: (0, i)) for x in weights],
+        [spec((rows, feat))] * 5
+        + [whole, pl.BlockSpec((feat, wide), lambda i, w: (w[NEAR] ^ 3, i))]
+        + [pl.BlockSpec((x.shape[0], wide), lambda i, w: (0, i)) for x in (fetched, passed)],
         whole,
-        [pltpu.VMEM((rows, 8 * feat), jnp.bfloat16)],
-    )(where, *slots, more, acc, *weights)
+        [pltpu.VMEM((rows, 4 * feat), jnp.bfloat16)],
+    )(where, last, more, *slots, acc, own, fetched, passed)
 
 
 def second_kernel(where_ref, slot, more, fetched_ref, passed_ref, acc_in, keep_ref, send_ref, acc_ref):
@@ -560,17 +562,21 @@
     mine = attend_half(where, 0, pieces)
     where, mine = lax.optimization_barrier((where, mine))
     other = swap(attend_half(where, 1, pieces), "head", 2, 1)
-    acc = zeroth_product(where, mine, out_weight)
+    acc = add_product(where, {0: mine}, out_weight)
     other, acc = lax.optimization_barrier((other, acc))
     slots = []
     for at, x in enumerate((mine, other)):
         next_to, far = swap(x, "patch", 4, 1), swap(x, "patch", 4, 2)
         next_to, far, other, x = lax.optimization_barrier((next_to, far, other, x))
+        if at == 1:
+            acc = add_product(where, {2: slots[0][2], 1: slots[0][1]}, out_weight, acc)
+            far, x, acc = lax.optimization_barrier((far, x, acc))
         middle = swap(x, "patch", 4, 3, (1, 2))
         ends = lax.ppermute(far, "patch", [(1, 0), (2, 3)])
         slots.append([x, next_to, far, middle, ends])
-    first = [slots[0][at] for at in (2, 1, 3)] + [slots[1][at] for at in (0, 2, 1)]
-    acc = first_product(where, first, slots[0][4], acc, [out_weight, fetched, passed])
+    weights = [out_weight, fetched, passed]
+    partner = [slots[1][at] for at in (0, 2, 1)]
+    acc = first_product(where, *slots[0][3:], partner, acc, weights)
     terms = [second_product(where, at, *slots[1][3:], [fetched, passed], acc) for at in range(2)]
     blocks = []
     for keep, send in terms:
@@ -599,9 +605,10 @@
         mix_columns_kernel,
         "mix",
         jax.ShapeDtypeStruct((rows, width), jnp.bfloat16),
-        1,
-        [spec((rows, width)), spec((1, width))] + [spec(flat[0].shape)] * len(flat),
-        spec((rows, width)),
+        2,
+        [pl.BlockSpec((rows // 2, width), lambda i, w: (i, 0)), spec((1, width))]
+        + [pl.BlockSpec((rows // 2, flat[0].shape[1]), lambda i, w: (i, 0))] * len(flat),
+        pl.BlockSpec((rows // 2, width), lambda i, w: (i, 0)),
     )(where, hidden_in, attn_gate[None], *flat)
 
 

time: 106 us -> 108 us (1.019)
  waiting for transfers between devices: 48.6 us -> 44.3 us
  Pallas kernels: 24 us -> 27.4 us
  local copies, waits for them, and re-layouts: 3.7 us -> 6.63 us
    ppermute x20, waiting for transfers between devices: 46.1 us -> 41.8 us  [swap(): return lax.ppermute(x, axes, pairs)]
    pallas_call x2, Pallas kernels: 2.21 us -> 4.27 us  [second_product(): call(second_kernel, 'second', [out] * 2, 1, [spec((rows, feat))] * 2 + [p...]
    unnamed x16 -> x18, local copies, waits for them, and re-layouts: 2.22 us -> 3.95 us
    pallas_call x2 -> x3, Pallas kernels: 7.28 us -> 8.75 us  [the longest x1 4.97 us: first_product(): call(first_kernel, 'first', jax.ShapeDtypeStruct(acc.shape, jnp.float32),...]
    dynamic_slice x1, local copies, waits for them, and re-layouts: 0.06 us -> 1.27 us  [share_tail(): lax.dynamic_slice_in_dim(fetched, start, pass_on, 0)]
  transfers between devices with their start and end apart: 22 -> 22, of which waited for: 9 -> 9; matrix products, arithmetic and copies ran while one was open for 1% -> 2% of each run, Pallas kernels for 17% -> 19%
where the time goes in v15:
time: 108 us
  waiting for transfers between devices  44.3 us (41%)
  starting transfers between devices  29.1 us (27%)
  Pallas kernels  27.4 us (25%)
  local copies, waits for them, and re-layouts  6.63 us (6%)
    ppermute x20, waiting for transfers between devices, swap(): return lax.ppermute(x, axes, pairs)  41.8 us
    ppermute x20, starting transfers between devices, swap(): return lax.ppermute(x, axes, pairs)  26.5 us
    pallas_call x2, Pallas kernels, attend_half(): call(functools.partial(attend_half_kernel, half), 'attend', out, 1, [spec...  6.82 us
    pallas_call x1, Pallas kernels, first_product(): call(first_kernel, 'first', jax.ShapeDtypeStruct(acc.shape, jnp.float32),...  4.97 us
    pallas_call x2, Pallas kernels, second_product(): call(second_kernel, 'second', [out] * 2, 1, [spec((rows, feat))] * 2 + [p...  4.27 us
    unnamed x18, local copies, waits for them, and re-layouts  3.95 us
    pallas_call x2, Pallas kernels, add_product(): call(functools.partial(add_product_kernel, len(rels)), 'products', jax.Sh...  3.79 us
    pallas_call x1, Pallas kernels, pack(): pl.pallas_call(functools.partial(pack_kernel, split, feat // HEAD_DIM), o...  3.51 us
  transfers between devices with their start and end apart: 22, of which 9 were waited for; matrix products, arithmetic and copies ran while one was open for 2% of the time, Pallas kernels for 19%

profile of v15, /device:TPU:0, one launch (start us, length us, event | category | flops | bytes accessed | tf_op | source)
XLA Modules:
  0.0 107.7 jit_solution(11950209449301316483)
XLA Ops:
  0.0 3.5 %pack.1 = (bf16[3,256,256]{2,1,0:T(8,128)(2,1)}, bf16[3,256,256]{2,1,0:T(8,128)(2,1)}, bf16[3,256,256]{2,1,0:T(8,128)(2,1)}) custom-call(s32[2,2,8]{2,1,0:T(2,128)} %exps_ref.3, bf16[256,1024]{1,0:T(8,128)(2,1)} %q_ref.3, bf16[2,256,1024]{2,1,0:T(8,128)(2,1)} %fresh_ref.3, bf16[2,1024,1024]{2,1,0:T(8,128)(2,1)} %cached_ref.3), custom_call_target="tpu_custom_call" | custom-call | tf_op jit(solution)/shard_map/pack/pallas_call | solution.py:114
  3.5 0.0 copy-start.8
  3.5 5.1 %collective-permute-start.2 = (bf16[3,256,256]{2,1,0:T(8,128)(2,1)}, bf16[3,256,256]{2,1,0:T(8,128)(2,1)S(1)}, u32[]{:S(2)}, u32[]{:S(2)}) collective-permute-start(bf16[3,256,256]{2,1,0:T(8,128)(2,1)} %get-tuple-element.36), channel_id=1, source_target_pairs={{0,12},{4,8},{8,4},{12,0},{1,13},{5,9},{9,5},{13,1},{2,14},{6,10},... | collective-permute-start | bytes 1179656 | tf_op jit(solution)/shard_map/ppermute | solution.py:50
  8.7 0.6 collective-permute-start
  9.3 0.1 stack.31.where_ref
  9.4 1.3 %constant_dynamic-slice_fusion.1 = bf16[640,1280]{1,0:T(8,128)(2,1)} fusion(bf16[1024,1280]{1,0:T(8,128)(2,1)S(1)} %copy-done, s32[]{:T(128)S(6)} %select_n.14), kind=kLoop, calls=%fused_computation.1 | loop fusion | bytes 3276804 | tf_op jit(solution)/shard_map/dynamic_slice | solution.py:557
  10.7 1.6 %collective-permute-start.10 = (bf16[640,1280]{1,0:T(8,128)(2,1)}, bf16[640,1280]{1,0:T(8,128)(2,1)}, u32[]{:S(2)}, u32[]{:S(2)}) collective-permute-start(bf16[640,1280]{1,0:T(8,128)(2,1)} %constant_dynamic-slice_fusion.1), channel_id=1, source_target_pairs={{0,2},{2,0},{1,3},{3,1},{4,6},{6,4},{5,7},{7,5},{8,10},{10,8},{9,1... | collective-permute-start | bytes 4915208 | tf_op jit(solution)/shard_map/ppermute | solution.py:50
  12.4 2.2 %copy-done.1 = bf16[2,1024,1024]{2,1,0:T(8,128)(2,1)S(1)} copy-done((bf16[2,1024,1024]{2,1,0:T(8,128)(2,1)S(1)}, bf16[2,1024,1024]{2,1,0:T(8,128)(2,1)}, u32[]{:S(2)}) %copy-start.1) | copy-done | bytes 4194328
  14.6 1.3 %own.1.refs_0_ = bf16[3,256,256]{2,1,0:T(8,128)(2,1)S(1)} custom-call(s32[6]{0:T(128)S(1)} %stack.31.where_ref, s32[2,2,8]{2,1,0:T(2,128)S(1)} %copy-done.8, bf16[256,1024]{1,0:T(8,128)(2,1)S(1)} %copy-done.6, bf16[2,256,1024]{2,1,0:T(8,128)(2,1)S(1)} %copy-done.4, bf16[2,1024,1024]{2,1,0:T(8,128)(2,1)S(1)} %copy-done.1), custom_call_target="tpu_custom_call" | custom-call | flops 49999998976 | tf_op jit(solution)/shard_map/own/pallas_call | solution.py:150
  15.9 0.7 copy-done.2
  16.6 2.4 %collective-permute-done.2.refs_3_ = bf16[3,256,256]{2,1,0:T(8,128)(2,1)S(1)} collective-permute-done((bf16[3,256,256]{2,1,0:T(8,128)(2,1)}, bf16[3,256,256]{2,1,0:T(8,128)(2,1)S(1)}, u32[]{:S(2)}, u32[]{:S(2)}) %collective-permute-start.2) | collective-permute-done | bytes 393248 | tf_op jit(solution)/shard_map/ppermute | solution.py:50
  18.9 23.5 %collective-permute-done.1.refs_2_ = bf16[3,256,256]{2,1,0:T(8,128)(2,1)S(1)} collective-permute-done((bf16[3,256,256]{2,1,0:T(8,128)(2,1)}, bf16[3,256,256]{2,1,0:T(8,128)(2,1)S(1)}, u32[]{:S(2)}, u32[]{:S(2)}) %collective-permute-start.1) | collective-permute-done | bytes 393248 | tf_op jit(solution)/shard_map/ppermute | solution.py:50
  42.4 1.0 copy-done.3
  43.4 3.4 %attend.2 = bf16[4,128,256]{2,1,0:T(8,128)(2,1)S(1)} custom-call(s32[6]{0:T(128)S(1)} %stack.31.where_ref, bf16[3,256,256]{2,1,0:T(8,128)(2,1)S(1)} %copy-done.3, bf16[3,256,256]{2,1,0:T(8,128)(2,1)} %collective-permute-done.refs_1_, bf16[3,256,256]{2,1,0:T(8,128)(2,1)S(1)} %collective-permute-done.1.refs_2_, ...), custom_call_target="tpu_custom_call" | custom-call | flops 1 | tf_op jit(solution)/shard_map/attend/pallas_call | solution.py:409
  46.8 0.1 collective-permute-start.7
  46.9 3.0 %collective-permute-start.6 = (bf16[512,256]{1,0:T(8,128)(2,1)S(1)}, bf16[512,256]{1,0:T(8,128)(2,1)S(1)}, u32[]{:S(2)}, u32[]{:S(2)}) collective-permute-start(bf16[512,256]{1,0:T(8,128)(2,1)S(1)} %bitcast.10), channel_id=1, source_target_pairs={{0,4},{4,0},{8,12},{12,8},{1,5},{5,1},{9,13},{13,9},{2,6},{6,2},{1... | collective-permute-start | bytes 786440 | tf_op jit(solution)/shard_map/ppermute | solution.py:50
  49.9 3.4 %attend.3 = bf16[4,128,256]{2,1,0:T(8,128)(2,1)S(1)} custom-call(s32[6]{0:T(128)S(1)} %stack.31.where_ref, bf16[3,256,256]{2,1,0:T(8,128)(2,1)S(1)} %copy-done.3, bf16[3,256,256]{2,1,0:T(8,128)(2,1)} %collective-permute-done.refs_1_, bf16[3,256,256]{2,1,0:T(8,128)(2,1)S(1)} %collective-permute-done.1.refs_2_, ...), custom_call_target="tpu_custom_call" | custom-call | flops 1 | tf_op jit(solution)/shard_map/attend/pallas_call | solution.py:409
  53.3 1.6 %collective-permute-start.3 = (bf16[512,256]{1,0:T(8,128)(2,1)S(1)}, bf16[512,256]{1,0:T(8,128)(2,1)S(1)}, u32[]{:S(2)}, u32[]{:S(2)}) collective-permute-start(bf16[512,256]{1,0:T(8,128)(2,1)S(1)} %bitcast.13), channel_id=1, source_target_pairs={{0,2},{2,0},{1,3},{3,1},{4,6},{6,4},{5,7},{7,5},{8,10},{10,8},{9,1... | collective-permute-start | bytes 786440 | tf_op jit(solution)/shard_map/ppermute | solution.py:50
  54.9 1.3 %constant_dynamic-slice_fusion = bf16[384,1280]{1,0:T(8,128)(2,1)S(1)} fusion(bf16[640,1280]{1,0:T(8,128)(2,1)} %collective-permute-done.10.refs_7_.fetched_ref, s32[]{:T(128)S(6)} %select_n.15), kind=kLoop, calls=%fused_computation | loop fusion | bytes 1966084 | tf_op jit(solution)/shard_map/dynamic_slice | solution.py:559
  56.2 1.6 %collective-permute-start.11 = (bf16[384,1280]{1,0:T(8,128)(2,1)S(1)}, bf16[384,1280]{1,0:T(8,128)(2,1)S(1)}, u32[]{:S(2)}, u32[]{:S(2)}) collective-permute-start(bf16[384,1280]{1,0:T(8,128)(2,1)S(1)} %constant_dynamic-slice_fusion), channel_id=1, source_target_pairs={{0,16},{16,0},{1,17},{17,1},{2,18},{18,2},{3,19},{19,3},{4,20},{20... | collective-permute-start | bytes 2949128 | tf_op jit(solution)/shard_map/ppermute | solution.py:50
  57.8 1.5 %products.2.refs_4_ = f32[512,1280]{1,0:T(8,128)S(1)} custom-call(s32[6]{0:T(128)S(1)} %stack.31.where_ref, bf16[512,256]{1,0:T(8,128)(2,1)S(1)} %bitcast.11, bf16[1024,1280]{1,0:T(8,128)(2,1)S(1)} %copy-done), custom_call_target="tpu_custom_call" | custom-call | flops 20000000000 | tf_op jit(solution)/shard_map/products/pallas_call | solution.py:434
  59.3 0.7 collective-permute-done.3.refs_2_
  60.0 0.4 collective-permute-start.5
  60.4 1.7 %collective-permute-start.4 = (bf16[512,256]{1,0:T(8,128)(2,1)S(1)}, bf16[512,256]{1,0:T(8,128)(2,1)S(1)}, u32[]{:S(2)}, u32[]{:S(2)}) collective-permute-start(bf16[512,256]{1,0:T(8,128)(2,1)S(1)} %collective-permute-done.3.refs_2_), channel_id=1, source_target_pairs={{0,4},{4,0},{8,12},{12,8},{1,5},{5,1},{9,13},{13,9},{2,6},{6,2},{1... | collective-permute-start | bytes 786440 | tf_op jit(solution)/shard_map/ppermute | solution.py:50
  62.1 0.7 collective-permute-start.12
  62.8 1.3 %collective-permute-start.13 = (bf16[512,256]{1,0:T(8,128)(2,1)S(1)}, bf16[512,256]{1,0:T(8,128)(2,1)S(1)}, u32[]{:S(2)}, u32[]{:S(2)}) collective-permute-start(bf16[512,256]{1,0:T(8,128)(2,1)S(1)} %collective-permute-done.7.refs_0_), channel_id=1, source_target_pairs={{4,0},{8,12},{5,1},{9,13},{6,2},{10,14},{7,3},{11,15},{20,16},{24,... | collective-permute-start | bytes 786440 | tf_op jit(solution)/shard_map/ppermute | solution.py:575
  64.1 2.2 %products.3.refs_5_ = f32[512,1280]{1,0:T(8,128)S(1)} custom-call(s32[6]{0:T(128)S(1)} %stack.31.where_ref, bf16[512,256]{1,0:T(8,128)(2,1)S(1)} %collective-permute-done.7.refs_0_, bf16[512,256]{1,0:T(8,128)(2,1)S(1)} %collective-permute-done.6.refs_1_, bf16[1024,1280]{1,0:T(8,128)(2,1)S(1)} %copy-done, bf16[1024,1280]{1,0:T(8,128)(2,1)S(1)} %copy-done, ...), custom_call_target="tpu_custom_call" | custom-call | flops 1 | tf_op jit(solution)/shard_map/products/pallas_call | solution.py:434
  66.4 6.5 %collective-permute-done.5.refs_3_ = bf16[512,256]{1,0:T(8,128)(2,1)S(1)} collective-permute-done((bf16[512,256]{1,0:T(8,128)(2,1)S(1)}, bf16[512,256]{1,0:T(8,128)(2,1)S(1)}, u32[]{:S(2)}, u32[]{:S(2)}) %collective-permute-start.5) | collective-permute-done | bytes 262176 | tf_op jit(solution)/shard_map/ppermute | solution.py:50
  72.9 1.4 %collective-permute-done.4.refs_4_ = bf16[512,256]{1,0:T(8,128)(2,1)S(1)} collective-permute-done((bf16[512,256]{1,0:T(8,128)(2,1)S(1)}, bf16[512,256]{1,0:T(8,128)(2,1)S(1)}, u32[]{:S(2)}, u32[]{:S(2)}) %collective-permute-start.4) | collective-permute-done | bytes 262176 | tf_op jit(solution)/shard_map/ppermute | solution.py:50
  74.3 0.7 collective-permute-start.8
  75.0 1.3 %collective-permute-start.9 = (bf16[512,256]{1,0:T(8,128)(2,1)S(1)}, bf16[512,256]{1,0:T(8,128)(2,1)S(1)}, u32[]{:S(2)}, u32[]{:S(2)}) collective-permute-start(bf16[512,256]{1,0:T(8,128)(2,1)S(1)} %collective-permute-done.5.refs_3_), channel_id=1, source_target_pairs={{4,0},{8,12},{5,1},{9,13},{6,2},{10,14},{7,3},{11,15},{20,16},{24,... | collective-permute-start | bytes 786440 | tf_op jit(solution)/shard_map/ppermute | solution.py:575
  76.3 2.5 %collective-permute-done.13.refs_1_ = bf16[512,256]{1,0:T(8,128)(2,1)S(1)} collective-permute-done((bf16[512,256]{1,0:T(8,128)(2,1)S(1)}, bf16[512,256]{1,0:T(8,128)(2,1)S(1)}, u32[]{:S(2)}, u32[]{:S(2)}) %collective-permute-start.13) | collective-permute-done | bytes 262176 | tf_op jit(solution)/shard_map/ppermute | solution.py:575
  78.8 5.0 %first.1.acc_in = f32[512,1280]{1,0:T(8,128)S(1)} custom-call(s32[6]{0:T(128)S(1)} %stack.31.where_ref, bf16[512,256]{1,0:T(8,128)(2,1)S(1)} %collective-permute-done.12.refs_0_, bf16[512,256]{1,0:T(8,128)(2,1)S(1)} %collective-permute-done.13.refs_1_, bf16[512,256]{1,0:T(8,128)(2,1)S(1)} %collective-permute-done.3.refs_2_, ...), custom_call_target="tpu_custom_call" | custom-call | flops 1 | tf_op jit(solution)/shard_map/first/pallas_call | solution.py:482
  83.8 2.1 %second.3 = (bf16[4,64,640]{2,1,0:T(8,128)(2,1)S(1)}, bf16[4,64,640]{2,1,0:T(8,128)(2,1)S(1)}) custom-call(s32[6]{0:T(128)S(1)} %stack.31.where_ref, bf16[512,256]{1,0:T(8,128)(2,1)S(1)} %collective-permute-done.8.slot, bf16[512,256]{1,0:T(8,128)(2,1)S(1)} %collective-permute-done.9.more, bf16[640,1280]{1,0:T(8,128)(2,1)} %collective-permute-done.10.refs_7_.fetched_ref, ...), custom_call_target="tpu_custom_call" | custom-call | flops 1 | tf_op jit(solution)/shard_map/second/pallas_call | solution.py:523
  85.9 0.0 copy-start.5
  85.9 0.1 collective-permute-start.18
  86.0 2.1 %second.2 = (bf16[4,64,640]{2,1,0:T(8,128)(2,1)S(1)}, bf16[4,64,640]{2,1,0:T(8,128)(2,1)S(1)}) custom-call(s32[6]{0:T(128)S(1)} %stack.31.where_ref, bf16[512,256]{1,0:T(8,128)(2,1)S(1)} %collective-permute-done.8.slot, bf16[512,256]{1,0:T(8,128)(2,1)S(1)} %collective-permute-done.9.more, bf16[640,1280]{1,0:T(8,128)(2,1)} %collective-permute-done.10.refs_7_.fetched_ref, ...), custom_call_target="tpu_custom_call" | custom-call | flops 1 | tf_op jit(solution)/shard_map/second/pallas_call | solution.py:523
  88.2 0.6 collective-permute-start.14
  88.7 0.6 add.16
  89.3 2.0 %collective-permute-start.19 = (bf16[64,640]{1,0:T(8,128)(2,1)S(1)}, bf16[64,640]{1,0:T(8,128)(2,1)S(1)}, u32[]{:S(2)}, u32[]{:S(2)}) collective-permute-start(bf16[64,640]{1,0:T(8,128)(2,1)S(1)} %get-tuple-element.64), channel_id=1, source_target_pairs={{0,12},{4,8},{8,4},{12,0},{1,13},{5,9},{9,5},{13,1},{2,14},{6,10},... | collective-permute-start | bytes 245768 | tf_op jit(solution)/shard_map/ppermute | solution.py:50
  91.4 2.4 %collective-permute-start.21 = (bf16[64,640]{1,0:T(8,128)(2,1)S(1)}, bf16[64,640]{1,0:T(8,128)(2,1)S(1)}, u32[]{:S(2)}, u32[]{:S(2)}) collective-permute-start(bf16[64,640]{1,0:T(8,128)(2,1)S(1)} %get-tuple-element.66), channel_id=1, source_target_pairs={{0,4},{4,0},{8,12},{12,8},{1,5},{5,1},{9,13},{13,9},{2,6},{6,2},{1... | collective-permute-start | bytes 245768 | tf_op jit(solution)/shard_map/ppermute | solution.py:50
  93.8 0.6 add.15
  94.4 2.0 %collective-permute-start.15 = (bf16[64,640]{1,0:T(8,128)(2,1)S(1)}, bf16[64,640]{1,0:T(8,128)(2,1)S(1)}, u32[]{:S(2)}, u32[]{:S(2)}) collective-permute-start(bf16[64,640]{1,0:T(8,128)(2,1)S(1)} %get-tuple-element.58), channel_id=1, source_target_pairs={{0,12},{4,8},{8,4},{12,0},{1,13},{5,9},{9,5},{13,1},{2,14},{6,10},... | collective-permute-start | bytes 245768 | tf_op jit(solution)/shard_map/ppermute | solution.py:50
  96.5 0.1 collective-permute-done.19.refs_5_
  96.6 2.3 %collective-permute-start.17 = (bf16[64,640]{1,0:T(8,128)(2,1)S(1)}, bf16[64,640]{1,0:T(8,128)(2,1)S(1)}, u32[]{:S(2)}, u32[]{:S(2)}) collective-permute-start(bf16[64,640]{1,0:T(8,128)(2,1)S(1)} %get-tuple-element.60), channel_id=1, source_target_pairs={{0,4},{4,0},{8,12},{12,8},{1,5},{5,1},{9,13},{13,9},{2,6},{6,2},{1... | collective-permute-start | bytes 245768 | tf_op jit(solution)/shard_map/ppermute | solution.py:50
  98.9 2.9 %collective-permute-done.20.refs_6_ = bf16[64,640]{1,0:T(8,128)(2,1)S(1)} collective-permute-done((bf16[64,640]{1,0:T(8,128)(2,1)S(1)}, bf16[64,640]{1,0:T(8,128)(2,1)S(1)}, u32[]{:S(2)}, u32[]{:S(2)}) %collective-permute-start.20) | collective-permute-done | bytes 81952 | tf_op jit(solution)/shard_map/ppermute | solution.py:50
  101.8 4.3 %collective-permute-done.16.refs_2_ = bf16[64,640]{1,0:T(8,128)(2,1)S(1)} collective-permute-done((bf16[64,640]{1,0:T(8,128)(2,1)S(1)}, bf16[64,640]{1,0:T(8,128)(2,1)S(1)}, u32[]{:S(2)}, u32[]{:S(2)}) %collective-permute-start.16) | collective-permute-done | bytes 81952 | tf_op jit(solution)/shard_map/ppermute | solution.py:50
  106.1 1.6 %mix.1 = bf16[64,5120]{1,0:T(8,128)(2,1)} custom-call(s32[6]{0:T(128)S(1)} %stack.31.where_ref, bf16[64,5120]{1,0:T(8,128)(2,1)S(1)} %copy-done.5, f32[1,5120]{1,0:T(1,128)S(1)} %bitcast.14, bf16[64,640]{1,0:T(8,128)(2,1)S(1)} %get-tuple-element.57.refs_0_, bf16[64,640]{1,0:T(8,128)(2,1)S(1)} %collective-permute-done.15.refs_1_, ...), custom_call_target="tpu_custom_call" | custom-call | flops 1 | tf_op jit(solution)/shard_map/mix/pallas_call | solution.py:604
  (29 shorter events, 0.1 us)
Async XLA Ops:
  0.0 9.4 %copy-start = (bf16[1024,1280]{1,0:T(8,128)(2,1)S(1)}, bf16[1024,1280]{1,0:T(8,128)(2,1)}, u32[]{:S(2)}) copy-start(bf16[1024,1280]{1,0:T(8,128)(2,1)} %refs_6_) | copy-start | bytes 7864324
  3.5 8.8 %copy-start.8 = (s32[2,2,8]{2,1,0:T(2,128)S(1)}, s32[2,2,8]{2,1,0:T(2,128)}, u32[]{:S(2)}) copy-start(s32[2,2,8]{2,1,0:T(2,128)} %exps_ref.3) | copy-start | bytes 388
  3.5 15.4 %collective-permute-start.2 = (bf16[3,256,256]{2,1,0:T(8,128)(2,1)}, bf16[3,256,256]{2,1,0:T(8,128)(2,1)S(1)}, u32[]{:S(2)}, u32[]{:S(2)}) collective-permute-start(bf16[3,256,256]{2,1,0:T(8,128)(2,1)} %get-tuple-element.36), channel_id=1, source_target_pairs={{0,12},{4,8},{8,4},{12,0},{1,13},{5,9},{9,5},{13,1},{2,14},{6,10},... | collective-permute-start | bytes 1179656 | tf_op jit(solution)/shard_map/ppermute | solution.py:50
  8.6 33.8 %collective-permute-start.1 = (bf16[3,256,256]{2,1,0:T(8,128)(2,1)}, bf16[3,256,256]{2,1,0:T(8,128)(2,1)S(1)}, u32[]{:S(2)}, u32[]{:S(2)}) collective-permute-start(bf16[3,256,256]{2,1,0:T(8,128)(2,1)} %get-tuple-element.37), channel_id=1, source_target_pairs={{0,8},{4,12},{8,0},{12,4},{1,9},{5,13},{9,1},{13,5},{2,10},{6,14},... | collective-permute-start | bytes 1179656 | tf_op jit(solution)/shard_map/ppermute | solution.py:50
  8.7 33.8 %collective-permute-start = (bf16[3,256,256]{2,1,0:T(8,128)(2,1)}, bf16[3,256,256]{2,1,0:T(8,128)(2,1)}, u32[]{:S(2)}, u32[]{:S(2)}) collective-permute-start(bf16[3,256,256]{2,1,0:T(8,128)(2,1)} %get-tuple-element.38), channel_id=1, source_target_pairs={{0,4},{4,0},{8,12},{12,8},{1,5},{5,1},{9,13},{13,9},{2,6},{6,2},{1... | collective-permute-start | bytes 1179656 | tf_op jit(solution)/shard_map/ppermute | solution.py:50
  9.4 3.0 %copy-start.4 = (bf16[2,256,1024]{2,1,0:T(8,128)(2,1)S(1)}, bf16[2,256,1024]{2,1,0:T(8,128)(2,1)}, u32[]{:S(2)}) copy-start(bf16[2,256,1024]{2,1,0:T(8,128)(2,1)} %fresh_ref.3) | copy-start | bytes 3145732
  9.4 3.0 %copy-start.6 = (bf16[256,1024]{1,0:T(8,128)(2,1)S(1)}, bf16[256,1024]{1,0:T(8,128)(2,1)}, u32[]{:S(2)}) copy-start(bf16[256,1024]{1,0:T(8,128)(2,1)} %q_ref.3) | copy-start | bytes 1572868
  10.7 44.2 %collective-permute-start.10 = (bf16[640,1280]{1,0:T(8,128)(2,1)}, bf16[640,1280]{1,0:T(8,128)(2,1)}, u32[]{:S(2)}, u32[]{:S(2)}) collective-permute-start(bf16[640,1280]{1,0:T(8,128)(2,1)} %constant_dynamic-slice_fusion.1), channel_id=1, source_target_pairs={{0,2},{2,0},{1,3},{3,1},{4,6},{6,4},{5,7},{7,5},{8,10},{10,8},{9,1... | collective-permute-start | bytes 4915208 | tf_op jit(solution)/shard_map/ppermute | solution.py:50
  12.4 2.2 %copy-start.1 = (bf16[2,1024,1024]{2,1,0:T(8,128)(2,1)S(1)}, bf16[2,1024,1024]{2,1,0:T(8,128)(2,1)}, u32[]{:S(2)}) copy-start(bf16[2,1024,1024]{2,1,0:T(8,128)(2,1)} %cached_ref.3) | copy-start | bytes 12582916
  15.8 0.7 copy-start.2
  42.4 1.0 copy-start.3
  46.8 15.3 %collective-permute-start.7 = (bf16[512,256]{1,0:T(8,128)(2,1)S(1)}, bf16[512,256]{1,0:T(8,128)(2,1)S(1)}, u32[]{:S(2)}, u32[]{:S(2)}) collective-permute-start(bf16[512,256]{1,0:T(8,128)(2,1)S(1)} %bitcast.9), channel_id=1, source_target_pairs={{0,8},{4,12},{8,0},{12,4},{1,9},{5,13},{9,1},{13,5},{2,10},{6,14},... | collective-permute-start | bytes 786440 | tf_op jit(solution)/shard_map/ppermute | solution.py:50
  46.9 15.2 %collective-permute-start.6 = (bf16[512,256]{1,0:T(8,128)(2,1)S(1)}, bf16[512,256]{1,0:T(8,128)(2,1)S(1)}, u32[]{:S(2)}, u32[]{:S(2)}) collective-permute-start(bf16[512,256]{1,0:T(8,128)(2,1)S(1)} %bitcast.10), channel_id=1, source_target_pairs={{0,4},{4,0},{8,12},{12,8},{1,5},{5,1},{9,13},{13,9},{2,6},{6,2},{1... | collective-permute-start | bytes 786440 | tf_op jit(solution)/shard_map/ppermute | solution.py:50
  53.3 6.7 %collective-permute-start.3 = (bf16[512,256]{1,0:T(8,128)(2,1)S(1)}, bf16[512,256]{1,0:T(8,128)(2,1)S(1)}, u32[]{:S(2)}, u32[]{:S(2)}) collective-permute-start(bf16[512,256]{1,0:T(8,128)(2,1)S(1)} %bitcast.13), channel_id=1, source_target_pairs={{0,2},{2,0},{1,3},{3,1},{4,6},{6,4},{5,7},{7,5},{8,10},{10,8},{9,1... | collective-permute-start | bytes 786440 | tf_op jit(solution)/shard_map/ppermute | solution.py:50
  56.2 22.6 %collective-permute-start.11 = (bf16[384,1280]{1,0:T(8,128)(2,1)S(1)}, bf16[384,1280]{1,0:T(8,128)(2,1)S(1)}, u32[]{:S(2)}, u32[]{:S(2)}) collective-permute-start(bf16[384,1280]{1,0:T(8,128)(2,1)S(1)} %constant_dynamic-slice_fusion), channel_id=1, source_target_pairs={{0,16},{16,0},{1,17},{17,1},{2,18},{18,2},{3,19},{19,3},{4,20},{20... | collective-permute-start | bytes 2949128 | tf_op jit(solution)/shard_map/ppermute | solution.py:50
  60.0 12.8 %collective-permute-start.5 = (bf16[512,256]{1,0:T(8,128)(2,1)S(1)}, bf16[512,256]{1,0:T(8,128)(2,1)S(1)}, u32[]{:S(2)}, u32[]{:S(2)}) collective-permute-start(bf16[512,256]{1,0:T(8,128)(2,1)S(1)} %collective-permute-done.3.refs_2_), channel_id=1, source_target_pairs={{0,8},{4,12},{8,0},{12,4},{1,9},{5,13},{9,1},{13,5},{2,10},{6,14},... | collective-permute-start | bytes 786440 | tf_op jit(solution)/shard_map/ppermute | solution.py:50
  60.4 13.9 %collective-permute-start.4 = (bf16[512,256]{1,0:T(8,128)(2,1)S(1)}, bf16[512,256]{1,0:T(8,128)(2,1)S(1)}, u32[]{:S(2)}, u32[]{:S(2)}) collective-permute-start(bf16[512,256]{1,0:T(8,128)(2,1)S(1)} %collective-permute-done.3.refs_2_), channel_id=1, source_target_pairs={{0,4},{4,0},{8,12},{12,8},{1,5},{5,1},{9,13},{13,9},{2,6},{6,2},{1... | collective-permute-start | bytes 786440 | tf_op jit(solution)/shard_map/ppermute | solution.py:50
  62.1 14.1 %collective-permute-start.12 = (bf16[512,256]{1,0:T(8,128)(2,1)S(1)}, bf16[512,256]{1,0:T(8,128)(2,1)S(1)}, u32[]{:S(2)}, u32[]{:S(2)}) collective-permute-start(bf16[512,256]{1,0:T(8,128)(2,1)S(1)} %bitcast.12), channel_id=1, source_target_pairs={{4,8},{8,4},{5,9},{9,5},{6,10},{10,6},{7,11},{11,7},{20,24},{24,20... | collective-permute-start | bytes 786440 | tf_op jit(solution)/shard_map/ppermute | solution.py:50
  62.8 16.0 %collective-permute-start.13 = (bf16[512,256]{1,0:T(8,128)(2,1)S(1)}, bf16[512,256]{1,0:T(8,128)(2,1)S(1)}, u32[]{:S(2)}, u32[]{:S(2)}) collective-permute-start(bf16[512,256]{1,0:T(8,128)(2,1)S(1)} %collective-permute-done.7.refs_0_), channel_id=1, source_target_pairs={{4,0},{8,12},{5,1},{9,13},{6,2},{10,14},{7,3},{11,15},{20,16},{24,... | collective-permute-start | bytes 786440 | tf_op jit(solution)/shard_map/ppermute | solution.py:575
  74.3 9.5 %collective-permute-start.8 = (bf16[512,256]{1,0:T(8,128)(2,1)S(1)}, bf16[512,256]{1,0:T(8,128)(2,1)S(1)}, u32[]{:S(2)}, u32[]{:S(2)}) collective-permute-start(bf16[512,256]{1,0:T(8,128)(2,1)S(1)} %collective-permute-done.3.refs_2_), channel_id=1, source_target_pairs={{4,8},{8,4},{5,9},{9,5},{6,10},{10,6},{7,11},{11,7},{20,24},{24,20... | collective-permute-start | bytes 786440 | tf_op jit(solution)/shard_map/ppermute | solution.py:50
  75.0 8.8 %collective-permute-start.9 = (bf16[512,256]{1,0:T(8,128)(2,1)S(1)}, bf16[512,256]{1,0:T(8,128)(2,1)S(1)}, u32[]{:S(2)}, u32[]{:S(2)}) collective-permute-start(bf16[512,256]{1,0:T(8,128)(2,1)S(1)} %collective-permute-done.5.refs_3_), channel_id=1, source_target_pairs={{4,0},{8,12},{5,1},{9,13},{6,2},{10,14},{7,3},{11,15},{20,16},{24,... | collective-permute-start | bytes 786440 | tf_op jit(solution)/shard_map/ppermute | solution.py:575
  85.9 20.2 %copy-start.5 = (bf16[64,5120]{1,0:T(8,128)(2,1)S(1)}, bf16[64,5120]{1,0:T(8,128)(2,1)}, u32[]{:S(2)}) copy-start(bf16[64,5120]{1,0:T(8,128)(2,1)} %hidden_ref.1) | copy-start | bytes 1966084
  85.9 20.2 %copy-start.7 = (f32[5120]{0:T(1024)S(1)}, f32[5120]{0:T(1024)}, u32[]{:S(2)}) copy-start(f32[5120]{0:T(1024)} %param.13) | copy-start | bytes 61444
  85.9 2.8 %collective-permute-start.18 = (bf16[4,64,640]{2,1,0:T(8,128)(2,1)S(1)}, bf16[4,64,640]{2,1,0:T(8,128)(2,1)S(1)}, u32[]{:S(2)}, u32[]{:S(2)}) collective-permute-start(bf16[4,64,640]{2,1,0:T(8,128)(2,1)S(1)} %get-tuple-element.62), channel_id=1, source_target_pairs={{0,1},{1,0},{2,3},{3,2},{4,5},{5,4},{6,7},{7,6},{8,9},{9,8},{10,11... | collective-permute-start | bytes 983048 | tf_op jit(solution)/shard_map/ppermute | solution.py:50
  88.2 5.6 %collective-permute-start.14 = (bf16[4,64,640]{2,1,0:T(8,128)(2,1)S(1)}, bf16[4,64,640]{2,1,0:T(8,128)(2,1)S(1)}, u32[]{:S(2)}, u32[]{:S(2)}) collective-permute-start(bf16[4,64,640]{2,1,0:T(8,128)(2,1)S(1)} %get-tuple-element.56), channel_id=1, source_target_pairs={{0,1},{1,0},{2,3},{3,2},{4,5},{5,4},{6,7},{7,6},{8,9},{9,8},{10,11... | collective-permute-start | bytes 983048 | tf_op jit(solution)/shard_map/ppermute | solution.py:50
  89.3 7.2 %collective-permute-start.19 = (bf16[64,640]{1,0:T(8,128)(2,1)S(1)}, bf16[64,640]{1,0:T(8,128)(2,1)S(1)}, u32[]{:S(2)}, u32[]{:S(2)}) collective-permute-start(bf16[64,640]{1,0:T(8,128)(2,1)S(1)} %get-tuple-element.64), channel_id=1, source_target_pairs={{0,12},{4,8},{8,4},{12,0},{1,13},{5,9},{9,5},{13,1},{2,14},{6,10},... | collective-permute-start | bytes 245768 | tf_op jit(solution)/shard_map/ppermute | solution.py:50
  91.4 10.4 %collective-permute-start.20 = (bf16[64,640]{1,0:T(8,128)(2,1)S(1)}, bf16[64,640]{1,0:T(8,128)(2,1)S(1)}, u32[]{:S(2)}, u32[]{:S(2)}) collective-permute-start(bf16[64,640]{1,0:T(8,128)(2,1)S(1)} %get-tuple-element.65), channel_id=1, source_target_pairs={{0,8},{4,12},{8,0},{12,4},{1,9},{5,13},{9,1},{13,5},{2,10},{6,14},... | collective-permute-start | bytes 245768 | tf_op jit(solution)/shard_map/ppermute | solution.py:50
  91.4 10.4 %collective-permute-start.21 = (bf16[64,640]{1,0:T(8,128)(2,1)S(1)}, bf16[64,640]{1,0:T(8,128)(2,1)S(1)}, u32[]{:S(2)}, u32[]{:S(2)}) collective-permute-start(bf16[64,640]{1,0:T(8,128)(2,1)S(1)} %get-tuple-element.66), channel_id=1, source_target_pairs={{0,4},{4,0},{8,12},{12,8},{1,5},{5,1},{9,13},{13,9},{2,6},{6,2},{1... | collective-permute-start | bytes 245768 | tf_op jit(solution)/shard_map/ppermute | solution.py:50
  94.4 7.4 %collective-permute-start.15 = (bf16[64,640]{1,0:T(8,128)(2,1)S(1)}, bf16[64,640]{1,0:T(8,128)(2,1)S(1)}, u32[]{:S(2)}, u32[]{:S(2)}) collective-permute-start(bf16[64,640]{1,0:T(8,128)(2,1)S(1)} %get-tuple-element.58), channel_id=1, source_target_pairs={{0,12},{4,8},{8,4},{12,0},{1,13},{5,9},{9,5},{13,1},{2,14},{6,10},... | collective-permute-start | bytes 245768 | tf_op jit(solution)/shard_map/ppermute | solution.py:50
  96.5 9.7 %collective-permute-start.16 = (bf16[64,640]{1,0:T(8,128)(2,1)S(1)}, bf16[64,640]{1,0:T(8,128)(2,1)S(1)}, u32[]{:S(2)}, u32[]{:S(2)}) collective-permute-start(bf16[64,640]{1,0:T(8,128)(2,1)S(1)} %get-tuple-element.59), channel_id=1, source_target_pairs={{0,8},{4,12},{8,0},{12,4},{1,9},{5,13},{9,1},{13,5},{2,10},{6,14},... | collective-permute-start | bytes 245768 | tf_op jit(solution)/shard_map/ppermute | solution.py:50
  96.6 9.6 %collective-permute-start.17 = (bf16[64,640]{1,0:T(8,128)(2,1)S(1)}, bf16[64,640]{1,0:T(8,128)(2,1)S(1)}, u32[]{:S(2)}, u32[]{:S(2)}) collective-permute-start(bf16[64,640]{1,0:T(8,128)(2,1)S(1)} %get-tuple-element.60), channel_id=1, source_target_pairs={{0,4},{4,0},{8,12},{12,8},{1,5},{5,1},{9,13},{13,9},{2,6},{6,2},{1... | collective-permute-start | bytes 245768 | tf_op jit(solution)/shard_map/ppermute | solution.py:50

commit v16 on v15

--- a/solution.py
+++ b/solution.py
@@ -12,7 +12,7 @@
 SCALE_ROWS = 128
 SATURATION = 448.0
 PACK_ROWS = 64
-VMEM_BYTES = 16 * 1024 * 1024
+VMEM_BYTES = 32 * 1024 * 1024
 PACK_VMEM_BYTES = 60 * 1024 * 1024
 ATTEND_FLOPS = 1
 PROJECT_FLOPS = 1
@@ -146,18 +146,18 @@
 def pack_own(split, where, exponents, queries, fresh_kv, cached_kv):
     tok, channels = queries.shape
     feat = channels // split
+    patch_at, near = where[PATCH], where[NEAR]
+    queries = lax.dynamic_slice_in_dim(queries, near * feat, feat, 1)
+    fresh_kv = lax.dynamic_slice_in_dim(fresh_kv, near * feat, feat, 2)
+    cached_kv = lax.dynamic_slice(cached_kv, (0, patch_at * tok, near * feat), (2, tok, feat))
     out = jax.ShapeDtypeStruct((3, tok, feat), jnp.bfloat16)
     return call(
         functools.partial(own_kernel, feat // HEAD_DIM),
         "own",
         out,
         1,
-        [
-            pl.BlockSpec(memory_space=pltpu.SMEM),
-            pl.BlockSpec((tok, feat), lambda i, w: (0, w[NEAR])),
-            pl.BlockSpec((2, tok, feat), lambda i, w: (0, 0, w[NEAR])),
-            pl.BlockSpec((2, tok, feat), lambda i, w: (0, w[PATCH], w[NEAR])),
-        ],
+        [pl.BlockSpec(memory_space=pltpu.SMEM)]
+        + [spec(x.shape) for x in (queries, fresh_kv, cached_kv)],
         spec(out.shape),
         flops=OWN_FLOPS,
     )(where, exponents, queries, fresh_kv, cached_kv)

time: 108 us -> 108 us (level)
  waiting for transfers between devices: 44.3 us -> 42.5 us
  between operations: 0.23 us -> 1.53 us
    unnamed x18 -> x12, local copies, waits for them, and re-layouts: 3.95 us -> 1.76 us
    dynamic_slice x0 -> x2, local copies, waits for them, and re-layouts: none -> 2 us  [the longest x1 1.08 us: pack_own(): lax.dynamic_slice(cached_kv, (0, patch_at * tok, near * feat), (2, tok, f...]
    ppermute x20, waiting for transfers between devices: 41.8 us -> 40.1 us  [swap(): return lax.ppermute(x, axes, pairs)]
  transfers between devices with their start and end apart: 22 -> 22, of which waited for: 9 -> 9; matrix products, arithmetic and copies ran while one was open for 2% -> 5% of each run, Pallas kernels for 19% -> 19%
where the time goes in v16:
time: 108 us
  waiting for transfers between devices  42.5 us (39%)
  starting transfers between devices  29.1 us (27%)
  Pallas kernels  27.5 us (25%)
  local copies, waits for them, and re-layouts  7.08 us (7%)
  between operations  1.53 us (1%)
    ppermute x20, waiting for transfers between devices, swap(): return lax.ppermute(x, axes, pairs)  40.1 us
    ppermute x20, starting transfers between devices, swap(): return lax.ppermute(x, axes, pairs)  26.5 us
    pallas_call x2, Pallas kernels, attend_half(): call(functools.partial(attend_half_kernel, half), 'attend', out, 1, [spec...  6.86 us
    pallas_call x1, Pallas kernels, first_product(): call(first_kernel, 'first', jax.ShapeDtypeStruct(acc.shape, jnp.float32),...  4.97 us
    pallas_call x2, Pallas kernels, second_product(): call(second_kernel, 'second', [out] * 2, 1, [spec((rows, feat))] * 2 + [p...  4.26 us
    pallas_call x2, Pallas kernels, add_product(): call(functools.partial(add_product_kernel, len(rels)), 'products', jax.Sh...  3.79 us
    pallas_call x1, Pallas kernels, pack(): pl.pallas_call(functools.partial(pack_kernel, split, feat // HEAD_DIM), o...  3.54 us
    ppermute x2, starting transfers between devices, share_tail(): ends = lax.ppermute(far, 'patch', [(1, 0), (2, 3)])  2.58 us
  transfers between devices with their start and end apart: 22, of which 9 were waited for; matrix products, arithmetic and copies ran while one was open for 5% of the time, Pallas kernels for 19%

profile of v16, /device:TPU:0, one launch (start us, length us, event | category | flops | bytes accessed | tf_op | source)
XLA Modules:
  0.0 107.7 jit_solution(3957715343106206430)
XLA Ops:
  0.0 3.5 %pack.1 = (bf16[3,256,256]{2,1,0:T(8,128)(2,1)}, bf16[3,256,256]{2,1,0:T(8,128)(2,1)}, bf16[3,256,256]{2,1,0:T(8,128)(2,1)}) custom-call(s32[2,2,8]{2,1,0:T(2,128)} %exps_ref.3, bf16[256,1024]{1,0:T(8,128)(2,1)} %q_ref.1, bf16[2,256,1024]{2,1,0:T(8,128)(2,1)} %fresh_ref.1, bf16[2,1024,1024]{2,1,0:T(8,128)(2,1)} %cached_ref.1), custom_call_target="tpu_custom_call" | custom-call | tf_op jit(solution)/shard_map/pack/pallas_call | solution.py:114
  3.6 5.1 %collective-permute-start.2 = (bf16[3,256,256]{2,1,0:T(8,128)(2,1)}, bf16[3,256,256]{2,1,0:T(8,128)(2,1)S(1)}, u32[]{:S(2)}, u32[]{:S(2)}) collective-permute-start(bf16[3,256,256]{2,1,0:T(8,128)(2,1)} %get-tuple-element.36), channel_id=1, source_target_pairs={{0,12},{4,8},{8,4},{12,0},{1,13},{5,9},{9,5},{13,1},{2,14},{6,10},... | collective-permute-start | bytes 1179656 | tf_op jit(solution)/shard_map/ppermute | solution.py:50
  8.7 0.6 collective-permute-start
  9.3 0.1 stack.31.where_ref
  9.4 1.3 %constant_dynamic-slice_fusion.1 = bf16[640,1280]{1,0:T(8,128)(2,1)} fusion(bf16[1024,1280]{1,0:T(8,128)(2,1)S(1)} %copy-done, s32[]{:T(128)S(6)} %select_n.24), kind=kLoop, calls=%fused_computation.1 | loop fusion | bytes 3276804 | tf_op jit(solution)/shard_map/dynamic_slice | solution.py:557
  10.7 1.6 %collective-permute-start.10 = (bf16[640,1280]{1,0:T(8,128)(2,1)}, bf16[640,1280]{1,0:T(8,128)(2,1)}, u32[]{:S(2)}, u32[]{:S(2)}) collective-permute-start(bf16[640,1280]{1,0:T(8,128)(2,1)} %constant_dynamic-slice_fusion.1), channel_id=1, source_target_pairs={{0,2},{2,0},{1,3},{3,1},{4,6},{6,4},{5,7},{7,5},{8,10},{10,8},{9,1... | collective-permute-start | bytes 4915208 | tf_op jit(solution)/shard_map/ppermute | solution.py:50
  12.4 0.6 fusion
  14.3 0.9 constant_dynamic-slice_fusion.4.q_ref
  15.2 1.1 %constant_dynamic-slice_fusion.2 = (bf16[2,256,256]{2,1,0:T(8,128)(2,1)S(1)}, bf16[2,256,256]{2,1,0:T(8,128)(2,1)S(1)}) fusion(bf16[2,1024,1024]{2,1,0:T(8,128)(2,1)} %cached_ref.1, s32[]{:T(128)S(6)} %select_n.23, s32[]{:T(128)S(6)} %select_n.22, bf16[2,256,1024]{2,1,0:T(8,128)(2,1)} %fresh_ref.1), kind=kLoop, calls=%fused_computation.2 | loop fusion | bytes 1048584 | tf_op jit(solution)/shard_map/dynamic_slice | solution.py:152
  16.3 1.3 %own.1.refs_0_ = bf16[3,256,256]{2,1,0:T(8,128)(2,1)S(1)} custom-call(s32[6]{0:T(128)S(1)} %stack.31.where_ref, s32[2,2,8]{2,1,0:T(2,128)S(1)} %copy-done.5, bf16[256,256]{1,0:T(8,128)(2,1)S(1)} %constant_dynamic-slice_fusion.4.q_ref, bf16[2,256,256]{2,1,0:T(8,128)(2,1)S(1)} %get-tuple-element.70.fresh_ref, bf16[2,256,256]{2,1,0:T(8,128)(2,1)S(1)} %get-tuple-element.69.cached_ref), custom_call_target="tpu_custom_call" | custom-call | flops 49999998976 | tf_op jit(solution)/shard_map/own/pallas_call | solution.py:154
  17.6 0.7 copy-done.1
  18.4 0.6 collective-permute-done.2.refs_3_
  19.0 23.5 %collective-permute-done.1.refs_2_ = bf16[3,256,256]{2,1,0:T(8,128)(2,1)S(1)} collective-permute-done((bf16[3,256,256]{2,1,0:T(8,128)(2,1)}, bf16[3,256,256]{2,1,0:T(8,128)(2,1)S(1)}, u32[]{:S(2)}, u32[]{:S(2)}) %collective-permute-start.1) | collective-permute-done | bytes 393248 | tf_op jit(solution)/shard_map/ppermute | solution.py:50
  42.4 1.0 copy-done.2
  43.4 3.4 %attend.2 = bf16[4,128,256]{2,1,0:T(8,128)(2,1)S(1)} custom-call(s32[6]{0:T(128)S(1)} %stack.31.where_ref, bf16[3,256,256]{2,1,0:T(8,128)(2,1)S(1)} %copy-done.2, bf16[3,256,256]{2,1,0:T(8,128)(2,1)} %collective-permute-done.refs_1_, bf16[3,256,256]{2,1,0:T(8,128)(2,1)S(1)} %collective-permute-done.1.refs_2_, ...), custom_call_target="tpu_custom_call" | custom-call | flops 1 | tf_op jit(solution)/shard_map/attend/pallas_call | solution.py:409
  46.9 0.1 collective-permute-start.7
  46.9 3.0 %collective-permute-start.6 = (bf16[512,256]{1,0:T(8,128)(2,1)S(1)}, bf16[512,256]{1,0:T(8,128)(2,1)S(1)}, u32[]{:S(2)}, u32[]{:S(2)}) collective-permute-start(bf16[512,256]{1,0:T(8,128)(2,1)S(1)} %bitcast.12), channel_id=1, source_target_pairs={{0,4},{4,0},{8,12},{12,8},{1,5},{5,1},{9,13},{13,9},{2,6},{6,2},{1... | collective-permute-start | bytes 786440 | tf_op jit(solution)/shard_map/ppermute | solution.py:50
  50.0 3.4 %attend.3 = bf16[4,128,256]{2,1,0:T(8,128)(2,1)S(1)} custom-call(s32[6]{0:T(128)S(1)} %stack.31.where_ref, bf16[3,256,256]{2,1,0:T(8,128)(2,1)S(1)} %copy-done.2, bf16[3,256,256]{2,1,0:T(8,128)(2,1)} %collective-permute-done.refs_1_, bf16[3,256,256]{2,1,0:T(8,128)(2,1)S(1)} %collective-permute-done.1.refs_2_, ...), custom_call_target="tpu_custom_call" | custom-call | flops 1 | tf_op jit(solution)/shard_map/attend/pallas_call | solution.py:409
  53.4 1.6 %collective-permute-start.3 = (bf16[512,256]{1,0:T(8,128)(2,1)S(1)}, bf16[512,256]{1,0:T(8,128)(2,1)S(1)}, u32[]{:S(2)}, u32[]{:S(2)}) collective-permute-start(bf16[512,256]{1,0:T(8,128)(2,1)S(1)} %bitcast.15), channel_id=1, source_target_pairs={{0,2},{2,0},{1,3},{3,1},{4,6},{6,4},{5,7},{7,5},{8,10},{10,8},{9,1... | collective-permute-start | bytes 786440 | tf_op jit(solution)/shard_map/ppermute | solution.py:50
  55.0 1.3 %constant_dynamic-slice_fusion = bf16[384,1280]{1,0:T(8,128)(2,1)S(1)} fusion(bf16[640,1280]{1,0:T(8,128)(2,1)} %collective-permute-done.10.refs_7_.fetched_ref, s32[]{:T(128)S(6)} %select_n.25), kind=kLoop, calls=%fused_computation | loop fusion | bytes 1966084 | tf_op jit(solution)/shard_map/dynamic_slice | solution.py:559
  56.2 1.6 %collective-permute-start.11 = (bf16[384,1280]{1,0:T(8,128)(2,1)S(1)}, bf16[384,1280]{1,0:T(8,128)(2,1)S(1)}, u32[]{:S(2)}, u32[]{:S(2)}) collective-permute-start(bf16[384,1280]{1,0:T(8,128)(2,1)S(1)} %constant_dynamic-slice_fusion), channel_id=1, source_target_pairs={{0,16},{16,0},{1,17},{17,1},{2,18},{18,2},{3,19},{19,3},{4,20},{20... | collective-permute-start | bytes 2949128 | tf_op jit(solution)/shard_map/ppermute | solution.py:50
  57.8 1.5 %products.2.refs_4_ = f32[512,1280]{1,0:T(8,128)S(1)} custom-call(s32[6]{0:T(128)S(1)} %stack.31.where_ref, bf16[512,256]{1,0:T(8,128)(2,1)S(1)} %bitcast.13, bf16[1024,1280]{1,0:T(8,128)(2,1)S(1)} %copy-done), custom_call_target="tpu_custom_call" | custom-call | flops 20000000000 | tf_op jit(solution)/shard_map/products/pallas_call | solution.py:434
  59.4 0.7 collective-permute-done.3.refs_2_
  60.1 0.4 collective-permute-start.5
  60.5 1.7 %collective-permute-start.4 = (bf16[512,256]{1,0:T(8,128)(2,1)S(1)}, bf16[512,256]{1,0:T(8,128)(2,1)S(1)}, u32[]{:S(2)}, u32[]{:S(2)}) collective-permute-start(bf16[512,256]{1,0:T(8,128)(2,1)S(1)} %collective-permute-done.3.refs_2_), channel_id=1, source_target_pairs={{0,4},{4,0},{8,12},{12,8},{1,5},{5,1},{9,13},{13,9},{2,6},{6,2},{1... | collective-permute-start | bytes 786440 | tf_op jit(solution)/shard_map/ppermute | solution.py:50
  62.2 0.7 collective-permute-start.12
  62.9 1.3 %collective-permute-start.13 = (bf16[512,256]{1,0:T(8,128)(2,1)S(1)}, bf16[512,256]{1,0:T(8,128)(2,1)S(1)}, u32[]{:S(2)}, u32[]{:S(2)}) collective-permute-start(bf16[512,256]{1,0:T(8,128)(2,1)S(1)} %collective-permute-done.7.refs_0_), channel_id=1, source_target_pairs={{4,0},{8,12},{5,1},{9,13},{6,2},{10,14},{7,3},{11,15},{20,16},{24,... | collective-permute-start | bytes 786440 | tf_op jit(solution)/shard_map/ppermute | solution.py:575
  64.2 2.2 %products.3.refs_5_ = f32[512,1280]{1,0:T(8,128)S(1)} custom-call(s32[6]{0:T(128)S(1)} %stack.31.where_ref, bf16[512,256]{1,0:T(8,128)(2,1)S(1)} %collective-permute-done.7.refs_0_, bf16[512,256]{1,0:T(8,128)(2,1)S(1)} %collective-permute-done.6.refs_1_, bf16[1024,1280]{1,0:T(8,128)(2,1)S(1)} %copy-done, bf16[1024,1280]{1,0:T(8,128)(2,1)S(1)} %copy-done, ...), custom_call_target="tpu_custom_call" | custom-call | flops 1 | tf_op jit(solution)/shard_map/products/pallas_call | solution.py:434
  66.4 6.5 %collective-permute-done.5.refs_3_ = bf16[512,256]{1,0:T(8,128)(2,1)S(1)} collective-permute-done((bf16[512,256]{1,0:T(8,128)(2,1)S(1)}, bf16[512,256]{1,0:T(8,128)(2,1)S(1)}, u32[]{:S(2)}, u32[]{:S(2)}) %collective-permute-start.5) | collective-permute-done | bytes 262176 | tf_op jit(solution)/shard_map/ppermute | solution.py:50
  72.9 1.4 %collective-permute-done.4.refs_4_ = bf16[512,256]{1,0:T(8,128)(2,1)S(1)} collective-permute-done((bf16[512,256]{1,0:T(8,128)(2,1)S(1)}, bf16[512,256]{1,0:T(8,128)(2,1)S(1)}, u32[]{:S(2)}, u32[]{:S(2)}) %collective-permute-start.4) | collective-permute-done | bytes 262176 | tf_op jit(solution)/shard_map/ppermute | solution.py:50
  74.4 0.7 collective-permute-start.8
  75.0 1.3 %collective-permute-start.9 = (bf16[512,256]{1,0:T(8,128)(2,1)S(1)}, bf16[512,256]{1,0:T(8,128)(2,1)S(1)}, u32[]{:S(2)}, u32[]{:S(2)}) collective-permute-start(bf16[512,256]{1,0:T(8,128)(2,1)S(1)} %collective-permute-done.5.refs_3_), channel_id=1, source_target_pairs={{4,0},{8,12},{5,1},{9,13},{6,2},{10,14},{7,3},{11,15},{20,16},{24,... | collective-permute-start | bytes 786440 | tf_op jit(solution)/shard_map/ppermute | solution.py:575
  76.4 2.5 %collective-permute-done.13.refs_1_ = bf16[512,256]{1,0:T(8,128)(2,1)S(1)} collective-permute-done((bf16[512,256]{1,0:T(8,128)(2,1)S(1)}, bf16[512,256]{1,0:T(8,128)(2,1)S(1)}, u32[]{:S(2)}, u32[]{:S(2)}) %collective-permute-start.13) | collective-permute-done | bytes 262176 | tf_op jit(solution)/shard_map/ppermute | solution.py:575
  78.8 5.0 %first.1.acc_in = f32[512,1280]{1,0:T(8,128)S(1)} custom-call(s32[6]{0:T(128)S(1)} %stack.31.where_ref, bf16[512,256]{1,0:T(8,128)(2,1)S(1)} %collective-permute-done.12.refs_0_, bf16[512,256]{1,0:T(8,128)(2,1)S(1)} %collective-permute-done.13.refs_1_, bf16[512,256]{1,0:T(8,128)(2,1)S(1)} %collective-permute-done.3.refs_2_, ...), custom_call_target="tpu_custom_call" | custom-call | flops 1 | tf_op jit(solution)/shard_map/first/pallas_call | solution.py:482
  83.8 2.1 %second.3 = (bf16[4,64,640]{2,1,0:T(8,128)(2,1)S(1)}, bf16[4,64,640]{2,1,0:T(8,128)(2,1)S(1)}) custom-call(s32[6]{0:T(128)S(1)} %stack.31.where_ref, bf16[512,256]{1,0:T(8,128)(2,1)S(1)} %collective-permute-done.8.slot, bf16[512,256]{1,0:T(8,128)(2,1)S(1)} %collective-permute-done.9.more, bf16[640,1280]{1,0:T(8,128)(2,1)} %collective-permute-done.10.refs_7_.fetched_ref, ...), custom_call_target="tpu_custom_call" | custom-call | flops 1 | tf_op jit(solution)/shard_map/second/pallas_call | solution.py:523
  86.0 0.1 collective-permute-start.18
  86.1 2.1 %second.2 = (bf16[4,64,640]{2,1,0:T(8,128)(2,1)S(1)}, bf16[4,64,640]{2,1,0:T(8,128)(2,1)S(1)}) custom-call(s32[6]{0:T(128)S(1)} %stack.31.where_ref, bf16[512,256]{1,0:T(8,128)(2,1)S(1)} %collective-permute-done.8.slot, bf16[512,256]{1,0:T(8,128)(2,1)S(1)} %collective-permute-done.9.more, bf16[640,1280]{1,0:T(8,128)(2,1)} %collective-permute-done.10.refs_7_.fetched_ref, ...), custom_call_target="tpu_custom_call" | custom-call | flops 1 | tf_op jit(solution)/shard_map/second/pallas_call | solution.py:523
  88.2 0.6 collective-permute-start.14
  88.8 0.6 add.26
  89.4 2.0 %collective-permute-start.19 = (bf16[64,640]{1,0:T(8,128)(2,1)S(1)}, bf16[64,640]{1,0:T(8,128)(2,1)S(1)}, u32[]{:S(2)}, u32[]{:S(2)}) collective-permute-start(bf16[64,640]{1,0:T(8,128)(2,1)S(1)} %get-tuple-element.64), channel_id=1, source_target_pairs={{0,12},{4,8},{8,4},{12,0},{1,13},{5,9},{9,5},{13,1},{2,14},{6,10},... | collective-permute-start | bytes 245768 | tf_op jit(solution)/shard_map/ppermute | solution.py:50
  91.4 2.4 %collective-permute-start.21 = (bf16[64,640]{1,0:T(8,128)(2,1)S(1)}, bf16[64,640]{1,0:T(8,128)(2,1)S(1)}, u32[]{:S(2)}, u32[]{:S(2)}) collective-permute-start(bf16[64,640]{1,0:T(8,128)(2,1)S(1)} %get-tuple-element.66), channel_id=1, source_target_pairs={{0,4},{4,0},{8,12},{12,8},{1,5},{5,1},{9,13},{13,9},{2,6},{6,2},{1... | collective-permute-start | bytes 245768 | tf_op jit(solution)/shard_map/ppermute | solution.py:50
  93.9 0.6 add.25
  94.5 2.0 %collective-permute-start.15 = (bf16[64,640]{1,0:T(8,128)(2,1)S(1)}, bf16[64,640]{1,0:T(8,128)(2,1)S(1)}, u32[]{:S(2)}, u32[]{:S(2)}) collective-permute-start(bf16[64,640]{1,0:T(8,128)(2,1)S(1)} %get-tuple-element.58), channel_id=1, source_target_pairs={{0,12},{4,8},{8,4},{12,0},{1,13},{5,9},{9,5},{13,1},{2,14},{6,10},... | collective-permute-start | bytes 245768 | tf_op jit(solution)/shard_map/ppermute | solution.py:50
  96.5 0.1 collective-permute-done.19.refs_5_
  96.6 2.3 %collective-permute-start.17 = (bf16[64,640]{1,0:T(8,128)(2,1)S(1)}, bf16[64,640]{1,0:T(8,128)(2,1)S(1)}, u32[]{:S(2)}, u32[]{:S(2)}) collective-permute-start(bf16[64,640]{1,0:T(8,128)(2,1)S(1)} %get-tuple-element.60), channel_id=1, source_target_pairs={{0,4},{4,0},{8,12},{12,8},{1,5},{5,1},{9,13},{13,9},{2,6},{6,2},{1... | collective-permute-start | bytes 245768 | tf_op jit(solution)/shard_map/ppermute | solution.py:50
  98.9 2.9 %collective-permute-done.20.refs_6_ = bf16[64,640]{1,0:T(8,128)(2,1)S(1)} collective-permute-done((bf16[64,640]{1,0:T(8,128)(2,1)S(1)}, bf16[64,640]{1,0:T(8,128)(2,1)S(1)}, u32[]{:S(2)}, u32[]{:S(2)}) %collective-permute-start.20) | collective-permute-done | bytes 81952 | tf_op jit(solution)/shard_map/ppermute | solution.py:50
  101.9 4.3 %collective-permute-done.16.refs_2_ = bf16[64,640]{1,0:T(8,128)(2,1)S(1)} collective-permute-done((bf16[64,640]{1,0:T(8,128)(2,1)S(1)}, bf16[64,640]{1,0:T(8,128)(2,1)S(1)}, u32[]{:S(2)}, u32[]{:S(2)}) %collective-permute-start.16) | collective-permute-done | bytes 81952 | tf_op jit(solution)/shard_map/ppermute | solution.py:50
  106.2 1.6 %mix.1 = bf16[64,5120]{1,0:T(8,128)(2,1)} custom-call(s32[6]{0:T(128)S(1)} %stack.31.where_ref, bf16[64,5120]{1,0:T(8,128)(2,1)S(1)} %copy-done.3, f32[1,5120]{1,0:T(1,128)S(1)} %bitcast.16, bf16[64,640]{1,0:T(8,128)(2,1)S(1)} %get-tuple-element.57.refs_0_, bf16[64,640]{1,0:T(8,128)(2,1)S(1)} %collective-permute-done.15.refs_1_, ...), custom_call_target="tpu_custom_call" | custom-call | flops 1 | tf_op jit(solution)/shard_map/mix/pallas_call | solution.py:604
  (26 shorter events, 0.1 us)
Async XLA Ops:
  0.0 9.4 %copy-start = (bf16[1024,1280]{1,0:T(8,128)(2,1)S(1)}, bf16[1024,1280]{1,0:T(8,128)(2,1)}, u32[]{:S(2)}) copy-start(bf16[1024,1280]{1,0:T(8,128)(2,1)} %refs_6_) | copy-start | bytes 7864324
  3.5 12.8 %copy-start.5 = (s32[2,2,8]{2,1,0:T(2,128)S(1)}, s32[2,2,8]{2,1,0:T(2,128)}, u32[]{:S(2)}) copy-start(s32[2,2,8]{2,1,0:T(2,128)} %exps_ref.3) | copy-start | bytes 388
  3.6 15.4 %collective-permute-start.2 = (bf16[3,256,256]{2,1,0:T(8,128)(2,1)}, bf16[3,256,256]{2,1,0:T(8,128)(2,1)S(1)}, u32[]{:S(2)}, u32[]{:S(2)}) collective-permute-start(bf16[3,256,256]{2,1,0:T(8,128)(2,1)} %get-tuple-element.36), channel_id=1, source_target_pairs={{0,12},{4,8},{8,4},{12,0},{1,13},{5,9},{9,5},{13,1},{2,14},{6,10},... | collective-permute-start | bytes 1179656 | tf_op jit(solution)/shard_map/ppermute | solution.py:50
  8.7 33.8 %collective-permute-start.1 = (bf16[3,256,256]{2,1,0:T(8,128)(2,1)}, bf16[3,256,256]{2,1,0:T(8,128)(2,1)S(1)}, u32[]{:S(2)}, u32[]{:S(2)}) collective-permute-start(bf16[3,256,256]{2,1,0:T(8,128)(2,1)} %get-tuple-element.37), channel_id=1, source_target_pairs={{0,8},{4,12},{8,0},{12,4},{1,9},{5,13},{9,1},{13,5},{2,10},{6,14},... | collective-permute-start | bytes 1179656 | tf_op jit(solution)/shard_map/ppermute | solution.py:50
  8.7 33.8 %collective-permute-start = (bf16[3,256,256]{2,1,0:T(8,128)(2,1)}, bf16[3,256,256]{2,1,0:T(8,128)(2,1)}, u32[]{:S(2)}, u32[]{:S(2)}) collective-permute-start(bf16[3,256,256]{2,1,0:T(8,128)(2,1)} %get-tuple-element.38), channel_id=1, source_target_pairs={{0,4},{4,0},{8,12},{12,8},{1,5},{5,1},{9,13},{13,9},{2,6},{6,2},{1... | collective-permute-start | bytes 1179656 | tf_op jit(solution)/shard_map/ppermute | solution.py:50
  10.7 44.2 %collective-permute-start.10 = (bf16[640,1280]{1,0:T(8,128)(2,1)}, bf16[640,1280]{1,0:T(8,128)(2,1)}, u32[]{:S(2)}, u32[]{:S(2)}) collective-permute-start(bf16[640,1280]{1,0:T(8,128)(2,1)} %constant_dynamic-slice_fusion.1), channel_id=1, source_target_pairs={{0,2},{2,0},{1,3},{3,1},{4,6},{6,4},{5,7},{7,5},{8,10},{10,8},{9,1... | collective-permute-start | bytes 4915208 | tf_op jit(solution)/shard_map/ppermute | solution.py:50
  17.6 0.7 copy-start.1
  42.4 1.0 copy-start.2
  46.9 15.3 %collective-permute-start.7 = (bf16[512,256]{1,0:T(8,128)(2,1)S(1)}, bf16[512,256]{1,0:T(8,128)(2,1)S(1)}, u32[]{:S(2)}, u32[]{:S(2)}) collective-permute-start(bf16[512,256]{1,0:T(8,128)(2,1)S(1)} %bitcast.11), channel_id=1, source_target_pairs={{0,8},{4,12},{8,0},{12,4},{1,9},{5,13},{9,1},{13,5},{2,10},{6,14},... | collective-permute-start | bytes 786440 | tf_op jit(solution)/shard_map/ppermute | solution.py:50
  46.9 15.3 %collective-permute-start.6 = (bf16[512,256]{1,0:T(8,128)(2,1)S(1)}, bf16[512,256]{1,0:T(8,128)(2,1)S(1)}, u32[]{:S(2)}, u32[]{:S(2)}) collective-permute-start(bf16[512,256]{1,0:T(8,128)(2,1)S(1)} %bitcast.12), channel_id=1, source_target_pairs={{0,4},{4,0},{8,12},{12,8},{1,5},{5,1},{9,13},{13,9},{2,6},{6,2},{1... | collective-permute-start | bytes 786440 | tf_op jit(solution)/shard_map/ppermute | solution.py:50
  53.4 6.7 %collective-permute-start.3 = (bf16[512,256]{1,0:T(8,128)(2,1)S(1)}, bf16[512,256]{1,0:T(8,128)(2,1)S(1)}, u32[]{:S(2)}, u32[]{:S(2)}) collective-permute-start(bf16[512,256]{1,0:T(8,128)(2,1)S(1)} %bitcast.15), channel_id=1, source_target_pairs={{0,2},{2,0},{1,3},{3,1},{4,6},{6,4},{5,7},{7,5},{8,10},{10,8},{9,1... | collective-permute-start | bytes 786440 | tf_op jit(solution)/shard_map/ppermute | solution.py:50
  56.2 22.6 %collective-permute-start.11 = (bf16[384,1280]{1,0:T(8,128)(2,1)S(1)}, bf16[384,1280]{1,0:T(8,128)(2,1)S(1)}, u32[]{:S(2)}, u32[]{:S(2)}) collective-permute-start(bf16[384,1280]{1,0:T(8,128)(2,1)S(1)} %constant_dynamic-slice_fusion), channel_id=1, source_target_pairs={{0,16},{16,0},{1,17},{17,1},{2,18},{18,2},{3,19},{19,3},{4,20},{20... | collective-permute-start | bytes 2949128 | tf_op jit(solution)/shard_map/ppermute | solution.py:50
  60.1 12.8 %collective-permute-start.5 = (bf16[512,256]{1,0:T(8,128)(2,1)S(1)}, bf16[512,256]{1,0:T(8,128)(2,1)S(1)}, u32[]{:S(2)}, u32[]{:S(2)}) collective-permute-start(bf16[512,256]{1,0:T(8,128)(2,1)S(1)} %collective-permute-done.3.refs_2_), channel_id=1, source_target_pairs={{0,8},{4,12},{8,0},{12,4},{1,9},{5,13},{9,1},{13,5},{2,10},{6,14},... | collective-permute-start | bytes 786440 | tf_op jit(solution)/shard_map/ppermute | solution.py:50
  60.5 13.9 %collective-permute-start.4 = (bf16[512,256]{1,0:T(8,128)(2,1)S(1)}, bf16[512,256]{1,0:T(8,128)(2,1)S(1)}, u32[]{:S(2)}, u32[]{:S(2)}) collective-permute-start(bf16[512,256]{1,0:T(8,128)(2,1)S(1)} %collective-permute-done.3.refs_2_), channel_id=1, source_target_pairs={{0,4},{4,0},{8,12},{12,8},{1,5},{5,1},{9,13},{13,9},{2,6},{6,2},{1... | collective-permute-start | bytes 786440 | tf_op jit(solution)/shard_map/ppermute | solution.py:50
  62.2 14.1 %collective-permute-start.12 = (bf16[512,256]{1,0:T(8,128)(2,1)S(1)}, bf16[512,256]{1,0:T(8,128)(2,1)S(1)}, u32[]{:S(2)}, u32[]{:S(2)}) collective-permute-start(bf16[512,256]{1,0:T(8,128)(2,1)S(1)} %bitcast.14), channel_id=1, source_target_pairs={{4,8},{8,4},{5,9},{9,5},{6,10},{10,6},{7,11},{11,7},{20,24},{24,20... | collective-permute-start | bytes 786440 | tf_op jit(solution)/shard_map/ppermute | solution.py:50
  62.9 15.9 %collective-permute-start.13 = (bf16[512,256]{1,0:T(8,128)(2,1)S(1)}, bf16[512,256]{1,0:T(8,128)(2,1)S(1)}, u32[]{:S(2)}, u32[]{:S(2)}) collective-permute-start(bf16[512,256]{1,0:T(8,128)(2,1)S(1)} %collective-permute-done.7.refs_0_), channel_id=1, source_target_pairs={{4,0},{8,12},{5,1},{9,13},{6,2},{10,14},{7,3},{11,15},{20,16},{24,... | collective-permute-start | bytes 786440 | tf_op jit(solution)/shard_map/ppermute | solution.py:575
  74.4 9.4 %collective-permute-start.8 = (bf16[512,256]{1,0:T(8,128)(2,1)S(1)}, bf16[512,256]{1,0:T(8,128)(2,1)S(1)}, u32[]{:S(2)}, u32[]{:S(2)}) collective-permute-start(bf16[512,256]{1,0:T(8,128)(2,1)S(1)} %collective-permute-done.3.refs_2_), channel_id=1, source_target_pairs={{4,8},{8,4},{5,9},{9,5},{6,10},{10,6},{7,11},{11,7},{20,24},{24,20... | collective-permute-start | bytes 786440 | tf_op jit(solution)/shard_map/ppermute | solution.py:50
  75.0 8.8 %collective-permute-start.9 = (bf16[512,256]{1,0:T(8,128)(2,1)S(1)}, bf16[512,256]{1,0:T(8,128)(2,1)S(1)}, u32[]{:S(2)}, u32[]{:S(2)}) collective-permute-start(bf16[512,256]{1,0:T(8,128)(2,1)S(1)} %collective-permute-done.5.refs_3_), channel_id=1, source_target_pairs={{4,0},{8,12},{5,1},{9,13},{6,2},{10,14},{7,3},{11,15},{20,16},{24,... | collective-permute-start | bytes 786440 | tf_op jit(solution)/shard_map/ppermute | solution.py:575
  86.0 20.2 %copy-start.3 = (bf16[64,5120]{1,0:T(8,128)(2,1)S(1)}, bf16[64,5120]{1,0:T(8,128)(2,1)}, u32[]{:S(2)}) copy-start(bf16[64,5120]{1,0:T(8,128)(2,1)} %hidden_ref.1) | copy-start | bytes 1966084
  86.0 20.2 %copy-start.4 = (f32[5120]{0:T(1024)S(1)}, f32[5120]{0:T(1024)}, u32[]{:S(2)}) copy-start(f32[5120]{0:T(1024)} %param.13) | copy-start | bytes 61444
  86.0 2.8 %collective-permute-start.18 = (bf16[4,64,640]{2,1,0:T(8,128)(2,1)S(1)}, bf16[4,64,640]{2,1,0:T(8,128)(2,1)S(1)}, u32[]{:S(2)}, u32[]{:S(2)}) collective-permute-start(bf16[4,64,640]{2,1,0:T(8,128)(2,1)S(1)} %get-tuple-element.62), channel_id=1, source_target_pairs={{0,1},{1,0},{2,3},{3,2},{4,5},{5,4},{6,7},{7,6},{8,9},{9,8},{10,11... | collective-permute-start | bytes 983048 | tf_op jit(solution)/shard_map/ppermute | solution.py:50
  88.2 5.6 %collective-permute-start.14 = (bf16[4,64,640]{2,1,0:T(8,128)(2,1)S(1)}, bf16[4,64,640]{2,1,0:T(8,128)(2,1)S(1)}, u32[]{:S(2)}, u32[]{:S(2)}) collective-permute-start(bf16[4,64,640]{2,1,0:T(8,128)(2,1)S(1)} %get-tuple-element.56), channel_id=1, source_target_pairs={{0,1},{1,0},{2,3},{3,2},{4,5},{5,4},{6,7},{7,6},{8,9},{9,8},{10,11... | collective-permute-start | bytes 983048 | tf_op jit(solution)/shard_map/ppermute | solution.py:50
  89.4 7.2 %collective-permute-start.19 = (bf16[64,640]{1,0:T(8,128)(2,1)S(1)}, bf16[64,640]{1,0:T(8,128)(2,1)S(1)}, u32[]{:S(2)}, u32[]{:S(2)}) collective-permute-start(bf16[64,640]{1,0:T(8,128)(2,1)S(1)} %get-tuple-element.64), channel_id=1, source_target_pairs={{0,12},{4,8},{8,4},{12,0},{1,13},{5,9},{9,5},{13,1},{2,14},{6,10},... | collective-permute-start | bytes 245768 | tf_op jit(solution)/shard_map/ppermute | solution.py:50
  91.4 10.4 %collective-permute-start.20 = (bf16[64,640]{1,0:T(8,128)(2,1)S(1)}, bf16[64,640]{1,0:T(8,128)(2,1)S(1)}, u32[]{:S(2)}, u32[]{:S(2)}) collective-permute-start(bf16[64,640]{1,0:T(8,128)(2,1)S(1)} %get-tuple-element.65), channel_id=1, source_target_pairs={{0,8},{4,12},{8,0},{12,4},{1,9},{5,13},{9,1},{13,5},{2,10},{6,14},... | collective-permute-start | bytes 245768 | tf_op jit(solution)/shard_map/ppermute | solution.py:50
  91.4 10.4 %collective-permute-start.21 = (bf16[64,640]{1,0:T(8,128)(2,1)S(1)}, bf16[64,640]{1,0:T(8,128)(2,1)S(1)}, u32[]{:S(2)}, u32[]{:S(2)}) collective-permute-start(bf16[64,640]{1,0:T(8,128)(2,1)S(1)} %get-tuple-element.66), channel_id=1, source_target_pairs={{0,4},{4,0},{8,12},{12,8},{1,5},{5,1},{9,13},{13,9},{2,6},{6,2},{1... | collective-permute-start | bytes 245768 | tf_op jit(solution)/shard_map/ppermute | solution.py:50
  94.5 7.4 %collective-permute-start.15 = (bf16[64,640]{1,0:T(8,128)(2,1)S(1)}, bf16[64,640]{1,0:T(8,128)(2,1)S(1)}, u32[]{:S(2)}, u32[]{:S(2)}) collective-permute-start(bf16[64,640]{1,0:T(8,128)(2,1)S(1)} %get-tuple-element.58), channel_id=1, source_target_pairs={{0,12},{4,8},{8,4},{12,0},{1,13},{5,9},{9,5},{13,1},{2,14},{6,10},... | collective-permute-start | bytes 245768 | tf_op jit(solution)/shard_map/ppermute | solution.py:50
  96.5 9.7 %collective-permute-start.16 = (bf16[64,640]{1,0:T(8,128)(2,1)S(1)}, bf16[64,640]{1,0:T(8,128)(2,1)S(1)}, u32[]{:S(2)}, u32[]{:S(2)}) collective-permute-start(bf16[64,640]{1,0:T(8,128)(2,1)S(1)} %get-tuple-element.59), channel_id=1, source_target_pairs={{0,8},{4,12},{8,0},{12,4},{1,9},{5,13},{9,1},{13,5},{2,10},{6,14},... | collective-permute-start | bytes 245768 | tf_op jit(solution)/shard_map/ppermute | solution.py:50
  96.6 9.6 %collective-permute-start.17 = (bf16[64,640]{1,0:T(8,128)(2,1)S(1)}, bf16[64,640]{1,0:T(8,128)(2,1)S(1)}, u32[]{:S(2)}, u32[]{:S(2)}) collective-permute-start(bf16[64,640]{1,0:T(8,128)(2,1)S(1)} %get-tuple-element.60), channel_id=1, source_target_pairs={{0,4},{4,0},{8,12},{12,8},{1,5},{5,1},{9,13},{13,9},{2,6},{6,2},{1... | collective-permute-start | bytes 245768 | tf_op jit(solution)/shard_map/ppermute | solution.py:50

commit v17 on v16

--- a/solution.py
+++ b/solution.py
@@ -16,9 +16,9 @@
 PACK_VMEM_BYTES = 60 * 1024 * 1024
 ATTEND_FLOPS = 1
 PROJECT_FLOPS = 1
-OWN_FLOPS = 50_000_000_000
-FETCHED = 5
-ZERO_FLOPS = 20_000_000_000
+OWN_FLOPS = 1
+FETCHED = 4
+ZERO_FLOPS = 6_000_000_000
 HALF_FLOPS = 1
 
 PATCH, NEAR, HEAD, SUB, INNER, GRP = range(6)
@@ -555,6 +555,8 @@
     out_weight, where = lax.optimization_barrier((out_weight, where))
     start = lax.axis_index("grp") * pass_on
     fetched = swap(lax.dynamic_slice_in_dim(out_weight, start, fetch, 0), "head", 2, 1)
+    own, fetched = lax.optimization_barrier((pieces[0], fetched))
+    pieces = [own, *pieces[1:]]
     start = lax.axis_index("grp") * (fetch - pass_on)
     passed = swap(lax.dynamic_slice_in_dim(fetched, start, pass_on, 0), "grp", 2, 1)
 

time: 108 us -> 109 us (level)
  waiting for transfers between devices: 42.5 us -> 47.7 us
  local copies, waits for them, and re-layouts: 7.08 us -> 3.85 us
    ppermute x20, waiting for transfers between devices: 40.1 us -> 45 us  [swap(): return lax.ppermute(x, axes, pairs)]
    unnamed x12 -> x8, local copies, waits for them, and re-layouts: 1.76 us -> 0.02 us
    dynamic_slice x1 -> x0, local copies, waits for them, and re-layouts: 1.27 us -> none  [share_tail(): lax.dynamic_slice_in_dim(fetched, start, pass_on, 0)]
  transfers between devices with their start and end apart: 22 -> 22, of which waited for: 9 -> 9; matrix products, arithmetic and copies ran while one was open for 5% -> 2% of each run, Pallas kernels for 19% -> 18%
where the time goes in v17:
time: 109 us
  waiting for transfers between devices  47.7 us (44%)
  starting transfers between devices  28.4 us (26%)
  Pallas kernels  27.2 us (25%)
  local copies, waits for them, and re-layouts  3.85 us (4%)
  between operations  1.41 us (1%)
    ppermute x20, waiting for transfers between devices, swap(): return lax.ppermute(x, axes, pairs)  45 us
    ppermute x20, starting transfers between devices, swap(): return lax.ppermute(x, axes, pairs)  25.8 us
    pallas_call x2, Pallas kernels, attend_half(): call(functools.partial(attend_half_kernel, half), 'attend', out, 1, [spec...  6.91 us
    pallas_call x1, Pallas kernels, first_product(): call(first_kernel, 'first', jax.ShapeDtypeStruct(acc.shape, jnp.float32),...  4.67 us
    pallas_call x2, Pallas kernels, second_product(): call(second_kernel, 'second', [out] * 2, 1, [spec((rows, feat))] * 2 + [p...  4.15 us
    pallas_call x2, Pallas kernels, add_product(): call(functools.partial(add_product_kernel, len(rels)), 'products', jax.Sh...  3.79 us
    pallas_call x1, Pallas kernels, pack(): pl.pallas_call(functools.partial(pack_kernel, split, feat // HEAD_DIM), o...  3.54 us
    ppermute x2, waiting for transfers between devices, share_tail(): ends = lax.ppermute(far, 'patch', [(1, 0), (2, 3)])  2.75 us
  transfers between devices with their start and end apart: 22, of which 9 were waited for; matrix products, arithmetic and copies ran while one was open for 2% of the time, Pallas kernels for 18%

profile of v17, /device:TPU:0, one launch (start us, length us, event | category | flops | bytes accessed | tf_op | source)
XLA Modules:
  0.0 108.5 jit_solution(377767127401486364)
XLA Ops:
  0.0 3.5 %pack.1 = (bf16[3,256,256]{2,1,0:T(8,128)(2,1)}, bf16[3,256,256]{2,1,0:T(8,128)(2,1)}, bf16[3,256,256]{2,1,0:T(8,128)(2,1)}) custom-call(s32[2,2,8]{2,1,0:T(2,128)} %exps_ref.3, bf16[256,1024]{1,0:T(8,128)(2,1)} %q_ref.1, bf16[2,256,1024]{2,1,0:T(8,128)(2,1)} %fresh_ref.1, bf16[2,1024,1024]{2,1,0:T(8,128)(2,1)} %cached_ref.1), custom_call_target="tpu_custom_call" | custom-call | tf_op jit(solution)/shard_map/pack/pallas_call | solution.py:114
  3.6 0.0 copy-start.3
  3.6 0.1 stack.31.where_ref
  3.7 1.2 %constant_dynamic-slice_fusion = bf16[512,1280]{1,0:T(8,128)(2,1)} fusion(bf16[1024,1280]{1,0:T(8,128)(2,1)S(1)} %copy-done, s32[]{:T(128)S(6)} %select_n.21), kind=kLoop, calls=%fused_computation | loop fusion | bytes 2621444 | tf_op jit(solution)/shard_map/dynamic_slice | solution.py:557
  4.8 2.9 %collective-permute-start = (bf16[512,1280]{1,0:T(8,128)(2,1)}, bf16[512,1280]{1,0:T(8,128)(2,1)}, u32[]{:S(2)}, u32[]{:S(2)}) collective-permute-start(bf16[512,1280]{1,0:T(8,128)(2,1)} %constant_dynamic-slice_fusion), channel_id=1, source_target_pairs={{0,2},{2,0},{1,3},{3,1},{4,6},{6,4},{5,7},{7,5},{8,10},{10,8},{9,1... | collective-permute-start | bytes 3932168 | tf_op jit(solution)/shard_map/ppermute | solution.py:50
  7.8 3.6 %collective-permute-start.3 = (bf16[3,256,256]{2,1,0:T(8,128)(2,1)}, bf16[3,256,256]{2,1,0:T(8,128)(2,1)S(1)}, u32[]{:S(2)}, u32[]{:S(2)}) collective-permute-start(bf16[3,256,256]{2,1,0:T(8,128)(2,1)} %get-tuple-element.38), channel_id=1, source_target_pairs={{0,12},{4,8},{8,4},{12,0},{1,13},{5,9},{9,5},{13,1},{2,14},{6,10},... | collective-permute-start | bytes 1179656 | tf_op jit(solution)/shard_map/ppermute | solution.py:50
  11.4 0.8 collective-permute-start.1
  12.1 0.6 fusion
  13.3 0.9 constant_dynamic-slice_fusion.3.q_ref
  14.8 1.1 constant_dynamic-slice_fusion.1
  15.9 1.3 %own.1.refs_0_ = bf16[3,256,256]{2,1,0:T(8,128)(2,1)S(1)} custom-call(s32[6]{0:T(128)S(1)} %stack.31.where_ref, s32[2,2,8]{2,1,0:T(2,128)S(1)} %copy-done.3, bf16[256,256]{1,0:T(8,128)(2,1)S(1)} %constant_dynamic-slice_fusion.3.q_ref, bf16[2,256,256]{2,1,0:T(8,128)(2,1)S(1)} %get-tuple-element.74.fresh_ref, bf16[2,256,256]{2,1,0:T(8,128)(2,1)S(1)} %get-tuple-element.73.cached_ref), custom_call_target="tpu_custom_call" | custom-call | flops 1 | tf_op jit(solution)/shard_map/own/pallas_call | solution.py:154
  17.2 19.6 %collective-permute-done.refs_7_.fetched_ref = bf16[512,1280]{1,0:T(8,128)(2,1)} collective-permute-done((bf16[512,1280]{1,0:T(8,128)(2,1)}, bf16[512,1280]{1,0:T(8,128)(2,1)}, u32[]{:S(2)}, u32[]{:S(2)}) %collective-permute-start) | collective-permute-done | bytes 1310752 | tf_op jit(solution)/shard_map/ppermute | solution.py:50
  36.8 1.8 %collective-permute-start.11 = (bf16[512,1280]{1,0:T(8,128)(2,1)}, bf16[512,1280]{1,0:T(8,128)(2,1)S(1)}, u32[]{:S(2)}, u32[]{:S(2)}) collective-permute-start(bf16[512,1280]{1,0:T(8,128)(2,1)} %collective-permute-done.refs_7_.fetched_ref), channel_id=1, source_target_pairs={{0,16},{16,0},{1,17},{17,1},{2,18},{18,2},{3,19},{19,3},{4,20},{20... | collective-permute-start | bytes 3932168 | tf_op jit(solution)/shard_map/ppermute | solution.py:50
  38.6 6.2 %collective-permute-done.2.refs_2_ = bf16[3,256,256]{2,1,0:T(8,128)(2,1)S(1)} collective-permute-done((bf16[3,256,256]{2,1,0:T(8,128)(2,1)}, bf16[3,256,256]{2,1,0:T(8,128)(2,1)S(1)}, u32[]{:S(2)}, u32[]{:S(2)}) %collective-permute-start.2) | collective-permute-done | bytes 393248 | tf_op jit(solution)/shard_map/ppermute | solution.py:50
  44.8 3.5 %attend.2 = bf16[4,128,256]{2,1,0:T(8,128)(2,1)S(1)} custom-call(s32[6]{0:T(128)S(1)} %stack.31.where_ref, bf16[3,256,256]{2,1,0:T(8,128)(2,1)S(1)} %own.1.refs_0_, bf16[3,256,256]{2,1,0:T(8,128)(2,1)} %collective-permute-done.1.refs_1_, bf16[3,256,256]{2,1,0:T(8,128)(2,1)S(1)} %collective-permute-done.2.refs_2_, ...), custom_call_target="tpu_custom_call" | custom-call | flops 1 | tf_op jit(solution)/shard_map/attend/pallas_call | solution.py:409
  48.3 0.1 collective-permute-start.8
  48.4 3.0 %collective-permute-start.7 = (bf16[512,256]{1,0:T(8,128)(2,1)S(1)}, bf16[512,256]{1,0:T(8,128)(2,1)S(1)}, u32[]{:S(2)}, u32[]{:S(2)}) collective-permute-start(bf16[512,256]{1,0:T(8,128)(2,1)S(1)} %bitcast.12), channel_id=1, source_target_pairs={{0,4},{4,0},{8,12},{12,8},{1,5},{5,1},{9,13},{13,9},{2,6},{6,2},{1... | collective-permute-start | bytes 786440 | tf_op jit(solution)/shard_map/ppermute | solution.py:50
  51.4 3.5 %attend.3 = bf16[4,128,256]{2,1,0:T(8,128)(2,1)S(1)} custom-call(s32[6]{0:T(128)S(1)} %stack.31.where_ref, bf16[3,256,256]{2,1,0:T(8,128)(2,1)S(1)} %own.1.refs_0_, bf16[3,256,256]{2,1,0:T(8,128)(2,1)} %collective-permute-done.1.refs_1_, bf16[3,256,256]{2,1,0:T(8,128)(2,1)S(1)} %collective-permute-done.2.refs_2_, ...), custom_call_target="tpu_custom_call" | custom-call | flops 1 | tf_op jit(solution)/shard_map/attend/pallas_call | solution.py:409
  54.9 0.6 collective-permute-start.4
  55.5 1.5 %products.2.refs_4_ = f32[512,1280]{1,0:T(8,128)S(1)} custom-call(s32[6]{0:T(128)S(1)} %stack.31.where_ref, bf16[512,256]{1,0:T(8,128)(2,1)S(1)} %bitcast.13, bf16[1024,1280]{1,0:T(8,128)(2,1)S(1)} %copy-done), custom_call_target="tpu_custom_call" | custom-call | flops 6000000000 | tf_op jit(solution)/shard_map/products/pallas_call | solution.py:434
  57.0 4.3 %collective-permute-done.4.refs_2_ = bf16[512,256]{1,0:T(8,128)(2,1)S(1)} collective-permute-done((bf16[512,256]{1,0:T(8,128)(2,1)S(1)}, bf16[512,256]{1,0:T(8,128)(2,1)S(1)}, u32[]{:S(2)}, u32[]{:S(2)}) %collective-permute-start.4) | collective-permute-done | bytes 262176 | tf_op jit(solution)/shard_map/ppermute | solution.py:50
  61.3 0.6 collective-permute-start.6
  61.9 1.7 %collective-permute-start.5 = (bf16[512,256]{1,0:T(8,128)(2,1)S(1)}, bf16[512,256]{1,0:T(8,128)(2,1)S(1)}, u32[]{:S(2)}, u32[]{:S(2)}) collective-permute-start(bf16[512,256]{1,0:T(8,128)(2,1)S(1)} %collective-permute-done.4.refs_2_), channel_id=1, source_target_pairs={{0,4},{4,0},{8,12},{12,8},{1,5},{5,1},{9,13},{13,9},{2,6},{6,2},{1... | collective-permute-start | bytes 786440 | tf_op jit(solution)/shard_map/ppermute | solution.py:50
  63.6 0.7 collective-permute-start.12
  64.3 1.3 %collective-permute-start.13 = (bf16[512,256]{1,0:T(8,128)(2,1)S(1)}, bf16[512,256]{1,0:T(8,128)(2,1)S(1)}, u32[]{:S(2)}, u32[]{:S(2)}) collective-permute-start(bf16[512,256]{1,0:T(8,128)(2,1)S(1)} %collective-permute-done.8.refs_0_), channel_id=1, source_target_pairs={{4,0},{8,12},{5,1},{9,13},{6,2},{10,14},{7,3},{11,15},{20,16},{24,... | collective-permute-start | bytes 786440 | tf_op jit(solution)/shard_map/ppermute | solution.py:577
  65.6 2.2 %products.3.refs_5_ = f32[512,1280]{1,0:T(8,128)S(1)} custom-call(s32[6]{0:T(128)S(1)} %stack.31.where_ref, bf16[512,256]{1,0:T(8,128)(2,1)S(1)} %collective-permute-done.8.refs_0_, bf16[512,256]{1,0:T(8,128)(2,1)S(1)} %collective-permute-done.7.refs_1_, bf16[1024,1280]{1,0:T(8,128)(2,1)S(1)} %copy-done, bf16[1024,1280]{1,0:T(8,128)(2,1)S(1)} %copy-done, ...), custom_call_target="tpu_custom_call" | custom-call | flops 1 | tf_op jit(solution)/shard_map/products/pallas_call | solution.py:434
  67.8 6.3 %collective-permute-done.6.refs_3_ = bf16[512,256]{1,0:T(8,128)(2,1)S(1)} collective-permute-done((bf16[512,256]{1,0:T(8,128)(2,1)S(1)}, bf16[512,256]{1,0:T(8,128)(2,1)S(1)}, u32[]{:S(2)}, u32[]{:S(2)}) %collective-permute-start.6) | collective-permute-done | bytes 262176 | tf_op jit(solution)/shard_map/ppermute | solution.py:50
  74.2 1.1 %collective-permute-done.5.refs_4_ = bf16[512,256]{1,0:T(8,128)(2,1)S(1)} collective-permute-done((bf16[512,256]{1,0:T(8,128)(2,1)S(1)}, bf16[512,256]{1,0:T(8,128)(2,1)S(1)}, u32[]{:S(2)}, u32[]{:S(2)}) %collective-permute-start.5) | collective-permute-done | bytes 262176 | tf_op jit(solution)/shard_map/ppermute | solution.py:50
  75.3 0.7 collective-permute-start.9
  75.9 1.3 %collective-permute-start.10 = (bf16[512,256]{1,0:T(8,128)(2,1)S(1)}, bf16[512,256]{1,0:T(8,128)(2,1)S(1)}, u32[]{:S(2)}, u32[]{:S(2)}) collective-permute-start(bf16[512,256]{1,0:T(8,128)(2,1)S(1)} %collective-permute-done.6.refs_3_), channel_id=1, source_target_pairs={{4,0},{8,12},{5,1},{9,13},{6,2},{10,14},{7,3},{11,15},{20,16},{24,... | collective-permute-start | bytes 786440 | tf_op jit(solution)/shard_map/ppermute | solution.py:577
  77.2 2.7 %collective-permute-done.13.refs_1_ = bf16[512,256]{1,0:T(8,128)(2,1)S(1)} collective-permute-done((bf16[512,256]{1,0:T(8,128)(2,1)S(1)}, bf16[512,256]{1,0:T(8,128)(2,1)S(1)}, u32[]{:S(2)}, u32[]{:S(2)}) %collective-permute-start.13) | collective-permute-done | bytes 262176 | tf_op jit(solution)/shard_map/ppermute | solution.py:577
  80.0 4.7 %first.1.acc_in = f32[512,1280]{1,0:T(8,128)S(1)} custom-call(s32[6]{0:T(128)S(1)} %stack.31.where_ref, bf16[512,256]{1,0:T(8,128)(2,1)S(1)} %collective-permute-done.12.refs_0_, bf16[512,256]{1,0:T(8,128)(2,1)S(1)} %collective-permute-done.13.refs_1_, bf16[512,256]{1,0:T(8,128)(2,1)S(1)} %collective-permute-done.4.refs_2_, ...), custom_call_target="tpu_custom_call" | custom-call | flops 1 | tf_op jit(solution)/shard_map/first/pallas_call | solution.py:482
  84.7 2.1 %second.3 = (bf16[4,64,640]{2,1,0:T(8,128)(2,1)S(1)}, bf16[4,64,640]{2,1,0:T(8,128)(2,1)S(1)}) custom-call(s32[6]{0:T(128)S(1)} %stack.31.where_ref, bf16[512,256]{1,0:T(8,128)(2,1)S(1)} %collective-permute-done.9.slot, bf16[512,256]{1,0:T(8,128)(2,1)S(1)} %collective-permute-done.10.more, bf16[512,1280]{1,0:T(8,128)(2,1)} %collective-permute-done.refs_7_.fetched_ref, ...), custom_call_target="tpu_custom_call" | custom-call | flops 1 | tf_op jit(solution)/shard_map/second/pallas_call | solution.py:523
  86.8 0.0 copy-start.2
  86.8 0.1 collective-permute-start.18
  86.9 2.1 %second.2 = (bf16[4,64,640]{2,1,0:T(8,128)(2,1)S(1)}, bf16[4,64,640]{2,1,0:T(8,128)(2,1)S(1)}) custom-call(s32[6]{0:T(128)S(1)} %stack.31.where_ref, bf16[512,256]{1,0:T(8,128)(2,1)S(1)} %collective-permute-done.9.slot, bf16[512,256]{1,0:T(8,128)(2,1)S(1)} %collective-permute-done.10.more, bf16[512,1280]{1,0:T(8,128)(2,1)} %collective-permute-done.refs_7_.fetched_ref, ...), custom_call_target="tpu_custom_call" | custom-call | flops 1 | tf_op jit(solution)/shard_map/second/pallas_call | solution.py:523
  89.0 0.6 collective-permute-start.14
  89.5 0.6 add.22
  90.2 1.9 %collective-permute-start.19 = (bf16[64,640]{1,0:T(8,128)(2,1)S(1)}, bf16[64,640]{1,0:T(8,128)(2,1)S(1)}, u32[]{:S(2)}, u32[]{:S(2)}) collective-permute-start(bf16[64,640]{1,0:T(8,128)(2,1)S(1)} %get-tuple-element.68), channel_id=1, source_target_pairs={{0,12},{4,8},{8,4},{12,0},{1,13},{5,9},{9,5},{13,1},{2,14},{6,10},... | collective-permute-start | bytes 245768 | tf_op jit(solution)/shard_map/ppermute | solution.py:50
  92.1 2.5 %collective-permute-start.21 = (bf16[64,640]{1,0:T(8,128)(2,1)S(1)}, bf16[64,640]{1,0:T(8,128)(2,1)S(1)}, u32[]{:S(2)}, u32[]{:S(2)}) collective-permute-start(bf16[64,640]{1,0:T(8,128)(2,1)S(1)} %get-tuple-element.70), channel_id=1, source_target_pairs={{0,4},{4,0},{8,12},{12,8},{1,5},{5,1},{9,13},{13,9},{2,6},{6,2},{1... | collective-permute-start | bytes 245768 | tf_op jit(solution)/shard_map/ppermute | solution.py:50
  94.6 0.6 add.21
  95.2 1.9 %collective-permute-start.15 = (bf16[64,640]{1,0:T(8,128)(2,1)S(1)}, bf16[64,640]{1,0:T(8,128)(2,1)S(1)}, u32[]{:S(2)}, u32[]{:S(2)}) collective-permute-start(bf16[64,640]{1,0:T(8,128)(2,1)S(1)} %get-tuple-element.62), channel_id=1, source_target_pairs={{0,12},{4,8},{8,4},{12,0},{1,13},{5,9},{9,5},{13,1},{2,14},{6,10},... | collective-permute-start | bytes 245768 | tf_op jit(solution)/shard_map/ppermute | solution.py:50
  97.2 0.2 collective-permute-done.19.refs_5_
  97.4 2.3 %collective-permute-start.17 = (bf16[64,640]{1,0:T(8,128)(2,1)S(1)}, bf16[64,640]{1,0:T(8,128)(2,1)S(1)}, u32[]{:S(2)}, u32[]{:S(2)}) collective-permute-start(bf16[64,640]{1,0:T(8,128)(2,1)S(1)} %get-tuple-element.64), channel_id=1, source_target_pairs={{0,4},{4,0},{8,12},{12,8},{1,5},{5,1},{9,13},{13,9},{2,6},{6,2},{1... | collective-permute-start | bytes 245768 | tf_op jit(solution)/shard_map/ppermute | solution.py:50
  99.7 2.9 %collective-permute-done.20.refs_6_ = bf16[64,640]{1,0:T(8,128)(2,1)S(1)} collective-permute-done((bf16[64,640]{1,0:T(8,128)(2,1)S(1)}, bf16[64,640]{1,0:T(8,128)(2,1)S(1)}, u32[]{:S(2)}, u32[]{:S(2)}) %collective-permute-start.20) | collective-permute-done | bytes 81952 | tf_op jit(solution)/shard_map/ppermute | solution.py:50
  102.6 0.0 collective-permute-done.15.refs_1_
  102.6 4.3 %collective-permute-done.16.refs_2_ = bf16[64,640]{1,0:T(8,128)(2,1)S(1)} collective-permute-done((bf16[64,640]{1,0:T(8,128)(2,1)S(1)}, bf16[64,640]{1,0:T(8,128)(2,1)S(1)}, u32[]{:S(2)}, u32[]{:S(2)}) %collective-permute-start.16) | collective-permute-done | bytes 81952 | tf_op jit(solution)/shard_map/ppermute | solution.py:50
  106.9 1.6 %mix.1 = bf16[64,5120]{1,0:T(8,128)(2,1)} custom-call(s32[6]{0:T(128)S(1)} %stack.31.where_ref, bf16[64,5120]{1,0:T(8,128)(2,1)S(1)} %copy-done.1, f32[1,5120]{1,0:T(1,128)S(1)} %bitcast.16, bf16[64,640]{1,0:T(8,128)(2,1)S(1)} %get-tuple-element.61.refs_0_, bf16[64,640]{1,0:T(8,128)(2,1)S(1)} %collective-permute-done.15.refs_1_, ...), custom_call_target="tpu_custom_call" | custom-call | flops 1 | tf_op jit(solution)/shard_map/mix/pallas_call | solution.py:606
  (21 shorter events, 0.1 us)
Async XLA Ops:
  0.0 3.7 %copy-start = (bf16[1024,1280]{1,0:T(8,128)(2,1)S(1)}, bf16[1024,1280]{1,0:T(8,128)(2,1)}, u32[]{:S(2)}) copy-start(bf16[1024,1280]{1,0:T(8,128)(2,1)} %refs_6_) | copy-start | bytes 7864324
  3.6 12.4 %copy-start.3 = (s32[2,2,8]{2,1,0:T(2,128)S(1)}, s32[2,2,8]{2,1,0:T(2,128)}, u32[]{:S(2)}) copy-start(s32[2,2,8]{2,1,0:T(2,128)} %exps_ref.3) | copy-start | bytes 388
  4.8 32.0 %collective-permute-start = (bf16[512,1280]{1,0:T(8,128)(2,1)}, bf16[512,1280]{1,0:T(8,128)(2,1)}, u32[]{:S(2)}, u32[]{:S(2)}) collective-permute-start(bf16[512,1280]{1,0:T(8,128)(2,1)} %constant_dynamic-slice_fusion), channel_id=1, source_target_pairs={{0,2},{2,0},{1,3},{3,1},{4,6},{6,4},{5,7},{7,5},{8,10},{10,8},{9,1... | collective-permute-start | bytes 3932168 | tf_op jit(solution)/shard_map/ppermute | solution.py:50
  7.8 30.9 %collective-permute-start.3 = (bf16[3,256,256]{2,1,0:T(8,128)(2,1)}, bf16[3,256,256]{2,1,0:T(8,128)(2,1)S(1)}, u32[]{:S(2)}, u32[]{:S(2)}) collective-permute-start(bf16[3,256,256]{2,1,0:T(8,128)(2,1)} %get-tuple-element.38), channel_id=1, source_target_pairs={{0,12},{4,8},{8,4},{12,0},{1,13},{5,9},{9,5},{13,1},{2,14},{6,10},... | collective-permute-start | bytes 1179656 | tf_op jit(solution)/shard_map/ppermute | solution.py:50
  11.4 33.5 %collective-permute-start.2 = (bf16[3,256,256]{2,1,0:T(8,128)(2,1)}, bf16[3,256,256]{2,1,0:T(8,128)(2,1)S(1)}, u32[]{:S(2)}, u32[]{:S(2)}) collective-permute-start(bf16[3,256,256]{2,1,0:T(8,128)(2,1)} %get-tuple-element.39), channel_id=1, source_target_pairs={{0,8},{4,12},{8,0},{12,4},{1,9},{5,13},{9,1},{13,5},{2,10},{6,14},... | collective-permute-start | bytes 1179656 | tf_op jit(solution)/shard_map/ppermute | solution.py:50
  11.4 33.5 %collective-permute-start.1 = (bf16[3,256,256]{2,1,0:T(8,128)(2,1)}, bf16[3,256,256]{2,1,0:T(8,128)(2,1)}, u32[]{:S(2)}, u32[]{:S(2)}) collective-permute-start(bf16[3,256,256]{2,1,0:T(8,128)(2,1)} %get-tuple-element.40), channel_id=1, source_target_pairs={{0,4},{4,0},{8,12},{12,8},{1,5},{5,1},{9,13},{13,9},{2,6},{6,2},{1... | collective-permute-start | bytes 1179656 | tf_op jit(solution)/shard_map/ppermute | solution.py:50
  36.8 43.1 %collective-permute-start.11 = (bf16[512,1280]{1,0:T(8,128)(2,1)}, bf16[512,1280]{1,0:T(8,128)(2,1)S(1)}, u32[]{:S(2)}, u32[]{:S(2)}) collective-permute-start(bf16[512,1280]{1,0:T(8,128)(2,1)} %collective-permute-done.refs_7_.fetched_ref), channel_id=1, source_target_pairs={{0,16},{16,0},{1,17},{17,1},{2,18},{18,2},{3,19},{19,3},{4,20},{20... | collective-permute-start | bytes 3932168 | tf_op jit(solution)/shard_map/ppermute | solution.py:50
  48.3 15.3 %collective-permute-start.8 = (bf16[512,256]{1,0:T(8,128)(2,1)S(1)}, bf16[512,256]{1,0:T(8,128)(2,1)S(1)}, u32[]{:S(2)}, u32[]{:S(2)}) collective-permute-start(bf16[512,256]{1,0:T(8,128)(2,1)S(1)} %bitcast.11), channel_id=1, source_target_pairs={{0,8},{4,12},{8,0},{12,4},{1,9},{5,13},{9,1},{13,5},{2,10},{6,14},... | collective-permute-start | bytes 786440 | tf_op jit(solution)/shard_map/ppermute | solution.py:50
  48.4 15.2 %collective-permute-start.7 = (bf16[512,256]{1,0:T(8,128)(2,1)S(1)}, bf16[512,256]{1,0:T(8,128)(2,1)S(1)}, u32[]{:S(2)}, u32[]{:S(2)}) collective-permute-start(bf16[512,256]{1,0:T(8,128)(2,1)S(1)} %bitcast.12), channel_id=1, source_target_pairs={{0,4},{4,0},{8,12},{12,8},{1,5},{5,1},{9,13},{13,9},{2,6},{6,2},{1... | collective-permute-start | bytes 786440 | tf_op jit(solution)/shard_map/ppermute | solution.py:50
  54.9 6.4 %collective-permute-start.4 = (bf16[512,256]{1,0:T(8,128)(2,1)S(1)}, bf16[512,256]{1,0:T(8,128)(2,1)S(1)}, u32[]{:S(2)}, u32[]{:S(2)}) collective-permute-start(bf16[512,256]{1,0:T(8,128)(2,1)S(1)} %bitcast.15), channel_id=1, source_target_pairs={{0,2},{2,0},{1,3},{3,1},{4,6},{6,4},{5,7},{7,5},{8,10},{10,8},{9,1... | collective-permute-start | bytes 786440 | tf_op jit(solution)/shard_map/ppermute | solution.py:50
  61.3 12.9 %collective-permute-start.6 = (bf16[512,256]{1,0:T(8,128)(2,1)S(1)}, bf16[512,256]{1,0:T(8,128)(2,1)S(1)}, u32[]{:S(2)}, u32[]{:S(2)}) collective-permute-start(bf16[512,256]{1,0:T(8,128)(2,1)S(1)} %collective-permute-done.4.refs_2_), channel_id=1, source_target_pairs={{0,8},{4,12},{8,0},{12,4},{1,9},{5,13},{9,1},{13,5},{2,10},{6,14},... | collective-permute-start | bytes 786440 | tf_op jit(solution)/shard_map/ppermute | solution.py:50
  61.9 13.4 %collective-permute-start.5 = (bf16[512,256]{1,0:T(8,128)(2,1)S(1)}, bf16[512,256]{1,0:T(8,128)(2,1)S(1)}, u32[]{:S(2)}, u32[]{:S(2)}) collective-permute-start(bf16[512,256]{1,0:T(8,128)(2,1)S(1)} %collective-permute-done.4.refs_2_), channel_id=1, source_target_pairs={{0,4},{4,0},{8,12},{12,8},{1,5},{5,1},{9,13},{13,9},{2,6},{6,2},{1... | collective-permute-start | bytes 786440 | tf_op jit(solution)/shard_map/ppermute | solution.py:50
  63.6 13.6 %collective-permute-start.12 = (bf16[512,256]{1,0:T(8,128)(2,1)S(1)}, bf16[512,256]{1,0:T(8,128)(2,1)S(1)}, u32[]{:S(2)}, u32[]{:S(2)}) collective-permute-start(bf16[512,256]{1,0:T(8,128)(2,1)S(1)} %bitcast.14), channel_id=1, source_target_pairs={{4,8},{8,4},{5,9},{9,5},{6,10},{10,6},{7,11},{11,7},{20,24},{24,20... | collective-permute-start | bytes 786440 | tf_op jit(solution)/shard_map/ppermute | solution.py:50
  64.3 15.7 %collective-permute-start.13 = (bf16[512,256]{1,0:T(8,128)(2,1)S(1)}, bf16[512,256]{1,0:T(8,128)(2,1)S(1)}, u32[]{:S(2)}, u32[]{:S(2)}) collective-permute-start(bf16[512,256]{1,0:T(8,128)(2,1)S(1)} %collective-permute-done.8.refs_0_), channel_id=1, source_target_pairs={{4,0},{8,12},{5,1},{9,13},{6,2},{10,14},{7,3},{11,15},{20,16},{24,... | collective-permute-start | bytes 786440 | tf_op jit(solution)/shard_map/ppermute | solution.py:577
  75.3 9.4 %collective-permute-start.9 = (bf16[512,256]{1,0:T(8,128)(2,1)S(1)}, bf16[512,256]{1,0:T(8,128)(2,1)S(1)}, u32[]{:S(2)}, u32[]{:S(2)}) collective-permute-start(bf16[512,256]{1,0:T(8,128)(2,1)S(1)} %collective-permute-done.4.refs_2_), channel_id=1, source_target_pairs={{4,8},{8,4},{5,9},{9,5},{6,10},{10,6},{7,11},{11,7},{20,24},{24,20... | collective-permute-start | bytes 786440 | tf_op jit(solution)/shard_map/ppermute | solution.py:50
  75.9 8.8 %collective-permute-start.10 = (bf16[512,256]{1,0:T(8,128)(2,1)S(1)}, bf16[512,256]{1,0:T(8,128)(2,1)S(1)}, u32[]{:S(2)}, u32[]{:S(2)}) collective-permute-start(bf16[512,256]{1,0:T(8,128)(2,1)S(1)} %collective-permute-done.6.refs_3_), channel_id=1, source_target_pairs={{4,0},{8,12},{5,1},{9,13},{6,2},{10,14},{7,3},{11,15},{20,16},{24,... | collective-permute-start | bytes 786440 | tf_op jit(solution)/shard_map/ppermute | solution.py:577
  86.8 20.2 %copy-start.1 = (bf16[64,5120]{1,0:T(8,128)(2,1)S(1)}, bf16[64,5120]{1,0:T(8,128)(2,1)}, u32[]{:S(2)}) copy-start(bf16[64,5120]{1,0:T(8,128)(2,1)} %hidden_ref.1) | copy-start | bytes 1966084
  86.8 20.1 %copy-start.2 = (f32[5120]{0:T(1024)S(1)}, f32[5120]{0:T(1024)}, u32[]{:S(2)}) copy-start(f32[5120]{0:T(1024)} %param.13) | copy-start | bytes 61444
  86.8 2.7 %collective-permute-start.18 = (bf16[4,64,640]{2,1,0:T(8,128)(2,1)S(1)}, bf16[4,64,640]{2,1,0:T(8,128)(2,1)S(1)}, u32[]{:S(2)}, u32[]{:S(2)}) collective-permute-start(bf16[4,64,640]{2,1,0:T(8,128)(2,1)S(1)} %get-tuple-element.66), channel_id=1, source_target_pairs={{0,1},{1,0},{2,3},{3,2},{4,5},{5,4},{6,7},{7,6},{8,9},{9,8},{10,11... | collective-permute-start | bytes 983048 | tf_op jit(solution)/shard_map/ppermute | solution.py:50
  89.0 5.6 %collective-permute-start.14 = (bf16[4,64,640]{2,1,0:T(8,128)(2,1)S(1)}, bf16[4,64,640]{2,1,0:T(8,128)(2,1)S(1)}, u32[]{:S(2)}, u32[]{:S(2)}) collective-permute-start(bf16[4,64,640]{2,1,0:T(8,128)(2,1)S(1)} %get-tuple-element.60), channel_id=1, source_target_pairs={{0,1},{1,0},{2,3},{3,2},{4,5},{5,4},{6,7},{7,6},{8,9},{9,8},{10,11... | collective-permute-start | bytes 983048 | tf_op jit(solution)/shard_map/ppermute | solution.py:50
  90.2 7.2 %collective-permute-start.19 = (bf16[64,640]{1,0:T(8,128)(2,1)S(1)}, bf16[64,640]{1,0:T(8,128)(2,1)S(1)}, u32[]{:S(2)}, u32[]{:S(2)}) collective-permute-start(bf16[64,640]{1,0:T(8,128)(2,1)S(1)} %get-tuple-element.68), channel_id=1, source_target_pairs={{0,12},{4,8},{8,4},{12,0},{1,13},{5,9},{9,5},{13,1},{2,14},{6,10},... | collective-permute-start | bytes 245768 | tf_op jit(solution)/shard_map/ppermute | solution.py:50
  92.1 10.5 %collective-permute-start.20 = (bf16[64,640]{1,0:T(8,128)(2,1)S(1)}, bf16[64,640]{1,0:T(8,128)(2,1)S(1)}, u32[]{:S(2)}, u32[]{:S(2)}) collective-permute-start(bf16[64,640]{1,0:T(8,128)(2,1)S(1)} %get-tuple-element.69), channel_id=1, source_target_pairs={{0,8},{4,12},{8,0},{12,4},{1,9},{5,13},{9,1},{13,5},{2,10},{6,14},... | collective-permute-start | bytes 245768 | tf_op jit(solution)/shard_map/ppermute | solution.py:50
  92.1 10.5 %collective-permute-start.21 = (bf16[64,640]{1,0:T(8,128)(2,1)S(1)}, bf16[64,640]{1,0:T(8,128)(2,1)S(1)}, u32[]{:S(2)}, u32[]{:S(2)}) collective-permute-start(bf16[64,640]{1,0:T(8,128)(2,1)S(1)} %get-tuple-element.70), channel_id=1, source_target_pairs={{0,4},{4,0},{8,12},{12,8},{1,5},{5,1},{9,13},{13,9},{2,6},{6,2},{1... | collective-permute-start | bytes 245768 | tf_op jit(solution)/shard_map/ppermute | solution.py:50
  95.2 7.4 %collective-permute-start.15 = (bf16[64,640]{1,0:T(8,128)(2,1)S(1)}, bf16[64,640]{1,0:T(8,128)(2,1)S(1)}, u32[]{:S(2)}, u32[]{:S(2)}) collective-permute-start(bf16[64,640]{1,0:T(8,128)(2,1)S(1)} %get-tuple-element.62), channel_id=1, source_target_pairs={{0,12},{4,8},{8,4},{12,0},{1,13},{5,9},{9,5},{13,1},{2,14},{6,10},... | collective-permute-start | bytes 245768 | tf_op jit(solution)/shard_map/ppermute | solution.py:50
  97.2 9.7 %collective-permute-start.16 = (bf16[64,640]{1,0:T(8,128)(2,1)S(1)}, bf16[64,640]{1,0:T(8,128)(2,1)S(1)}, u32[]{:S(2)}, u32[]{:S(2)}) collective-permute-start(bf16[64,640]{1,0:T(8,128)(2,1)S(1)} %get-tuple-element.63), channel_id=1, source_target_pairs={{0,8},{4,12},{8,0},{12,4},{1,9},{5,13},{9,1},{13,5},{2,10},{6,14},... | collective-permute-start | bytes 245768 | tf_op jit(solution)/shard_map/ppermute | solution.py:50
  97.4 9.6 %collective-permute-start.17 = (bf16[64,640]{1,0:T(8,128)(2,1)S(1)}, bf16[64,640]{1,0:T(8,128)(2,1)S(1)}, u32[]{:S(2)}, u32[]{:S(2)}) collective-permute-start(bf16[64,640]{1,0:T(8,128)(2,1)S(1)} %get-tuple-element.64), channel_id=1, source_target_pairs={{0,4},{4,0},{8,12},{12,8},{1,5},{5,1},{9,13},{13,9},{2,6},{6,2},{1... | collective-permute-start | bytes 245768 | tf_op jit(solution)/shard_map/ppermute | solution.py:50

commit v18 on v15

--- a/solution.py
+++ b/solution.py
@@ -12,13 +12,13 @@
 SCALE_ROWS = 128
 SATURATION = 448.0
 PACK_ROWS = 64
-VMEM_BYTES = 16 * 1024 * 1024
+VMEM_BYTES = 32 * 1024 * 1024
 PACK_VMEM_BYTES = 60 * 1024 * 1024
 ATTEND_FLOPS = 1
 PROJECT_FLOPS = 1
-OWN_FLOPS = 50_000_000_000
-FETCHED = 5
-ZERO_FLOPS = 20_000_000_000
+OWN_FLOPS = 1
+FETCHED = 4
+ZERO_FLOPS = 6_000_000_000
 HALF_FLOPS = 1
 
 PATCH, NEAR, HEAD, SUB, INNER, GRP = range(6)
@@ -159,7 +159,6 @@
             pl.BlockSpec((2, tok, feat), lambda i, w: (0, w[PATCH], w[NEAR])),
         ],
         spec(out.shape),
-        flops=OWN_FLOPS,
     )(where, exponents, queries, fresh_kv, cached_kv)
 
 
@@ -550,13 +549,28 @@
     )(where, keep, term)
 
 
+def take_kernel(where_ref, weight_ref, out_ref):
+    out_ref[...] = weight_ref[...]
+
+
+def take_half(where, weight):
+    rows, cols = weight.shape[0] // 2, weight.shape[1]
+    return call(
+        take_kernel,
+        "take",
+        jax.ShapeDtypeStruct((rows, cols), weight.dtype),
+        2,
+        [pl.BlockSpec((rows // 2, cols), lambda i, w: (2 * w[GRP] + i, 0))],
+        pl.BlockSpec((rows // 2, cols), lambda i, w: (i, 0)),
+    )(where, weight)
+
+
 def share_tail(sizes, where, pieces, kv_pieces, out_weight, hidden_in, attn_gate):
-    fetch, pass_on = FETCHED * HEAD_DIM, (8 - FETCHED) * HEAD_DIM
     out_weight, where = lax.optimization_barrier((out_weight, where))
-    start = lax.axis_index("grp") * pass_on
-    fetched = swap(lax.dynamic_slice_in_dim(out_weight, start, fetch, 0), "head", 2, 1)
-    start = lax.axis_index("grp") * (fetch - pass_on)
-    passed = swap(lax.dynamic_slice_in_dim(fetched, start, pass_on, 0), "grp", 2, 1)
+    fetched = swap(take_half(where, out_weight), "head", 2, 1)
+    own, fetched = lax.optimization_barrier((pieces[0], fetched))
+    pieces = [own, *pieces[1:]]
+    passed = swap(fetched, "grp", 2, 1)
 
     pieces = [pieces[0], *pieces[:0:-1]]
     mine = attend_half(where, 0, pieces)

time: 108 us -> 105 us (0.972)
  waiting for transfers between devices: 44.3 us -> 50.5 us
  local copies, waits for them, and re-layouts: 6.63 us -> 2.32 us
  Pallas kernels: 27.4 us -> 23.2 us
    ppermute x20, waiting for transfers between devices: 41.8 us -> 46.8 us  [swap(): return lax.ppermute(x, axes, pairs)]
    dynamic_slice x2 -> x0, local copies, waits for them, and re-layouts: 2.59 us -> none  [the longest x1 1.33 us: share_tail(): lax.dynamic_slice_in_dim(out_weight, start, fetch, 0)]
    pallas_call x2, Pallas kernels: 4.27 us -> 2.21 us  [second_product(): call(second_kernel, 'second', [out] * 2, 1, [spec((rows, feat))] * 2 + [p...]
    pallas_call x2, Pallas kernels: 6.82 us -> 4.96 us  [attend_half(): call(functools.partial(attend_half_kernel, half), 'attend', out, 1, [spec...]
    unnamed x18 -> x20, local copies, waits for them, and re-layouts: 3.95 us -> 2.23 us
    ppermute x2, waiting for transfers between devices: 2.49 us -> 3.71 us  [share_tail(): ends = lax.ppermute(far, 'patch', [(1, 0), (2, 3)])]
  transfers between devices with their start and end apart: 22 -> 22, of which waited for: 9 -> 10; matrix products, arithmetic and copies ran while one was open for 2% -> 0% of each run, Pallas kernels for 19% -> 16%
where the time goes in v18:
time: 105 us
  waiting for transfers between devices  50.5 us (48%)
  starting transfers between devices  28.4 us (27%)
  Pallas kernels  23.2 us (22%)
  local copies, waits for them, and re-layouts  2.32 us (2%)
    ppermute x20, waiting for transfers between devices, swap(): return lax.ppermute(x, axes, pairs)  46.8 us
    ppermute x20, starting transfers between devices, swap(): return lax.ppermute(x, axes, pairs)  25.8 us
    pallas_call x2, Pallas kernels, attend_half(): call(functools.partial(attend_half_kernel, half), 'attend', out, 1, [spec...  4.96 us
    pallas_call x1, Pallas kernels, first_product(): call(first_kernel, 'first', jax.ShapeDtypeStruct(acc.shape, jnp.float32),...  3.96 us
    pallas_call x2, Pallas kernels, add_product(): call(functools.partial(add_product_kernel, len(rels)), 'products', jax.Sh...  3.79 us
    ppermute x2, waiting for transfers between devices, share_tail(): ends = lax.ppermute(far, 'patch', [(1, 0), (2, 3)])  3.71 us
    pallas_call x1, Pallas kernels, pack(): pl.pallas_call(functools.partial(pack_kernel, split, feat // HEAD_DIM), o...  3.53 us
    ppermute x2, starting transfers between devices, share_tail(): ends = lax.ppermute(far, 'patch', [(1, 0), (2, 3)])  2.58 us
  transfers between devices with their start and end apart: 22, of which 10 were waited for; matrix products, arithmetic and copies ran while one was open for 0% of the time, Pallas kernels for 16%

profile of v18, /device:TPU:0, one launch (start us, length us, event | category | flops | bytes accessed | tf_op | source)
XLA Modules:
  0.0 104.7 jit_solution(9868642836026534950)
XLA Ops:
  0.0 3.5 %pack.1 = (bf16[3,256,256]{2,1,0:T(8,128)(2,1)}, bf16[3,256,256]{2,1,0:T(8,128)(2,1)}, bf16[3,256,256]{2,1,0:T(8,128)(2,1)}) custom-call(s32[2,2,8]{2,1,0:T(2,128)} %exps_ref.3, bf16[256,1024]{1,0:T(8,128)(2,1)} %q_ref.3, bf16[2,256,1024]{2,1,0:T(8,128)(2,1)} %fresh_ref.3, bf16[2,1024,1024]{2,1,0:T(8,128)(2,1)} %cached_ref.3), custom_call_target="tpu_custom_call" | custom-call | tf_op jit(solution)/shard_map/pack/pallas_call | solution.py:114
  3.6 0.0 copy-start.3
  3.6 0.0 copy-start.6
  3.6 0.1 stack.31.where_ref
  3.7 0.7 take.1
  4.4 3.0 %collective-permute-start = (bf16[512,1280]{1,0:T(8,128)(2,1)S(1)}, bf16[512,1280]{1,0:T(8,128)(2,1)S(1)}, u32[]{:S(2)}, u32[]{:S(2)}) collective-permute-start(bf16[512,1280]{1,0:T(8,128)(2,1)S(1)} %take.1), channel_id=1, source_target_pairs={{0,2},{2,0},{1,3},{3,1},{4,6},{6,4},{5,7},{7,5},{8,10},{10,8},{9,1... | collective-permute-start | bytes 3932168 | tf_op jit(solution)/shard_map/ppermute | solution.py:50
  7.4 3.6 %collective-permute-start.3 = (bf16[3,256,256]{2,1,0:T(8,128)(2,1)S(1)}, bf16[3,256,256]{2,1,0:T(8,128)(2,1)S(1)}, u32[]{:S(2)}, u32[]{:S(2)}) collective-permute-start(bf16[3,256,256]{2,1,0:T(8,128)(2,1)S(1)} %copy-done.9), channel_id=1, source_target_pairs={{0,12},{4,8},{8,4},{12,0},{1,13},{5,9},{9,5},{13,1},{2,14},{6,10},... | collective-permute-start | bytes 1179656 | tf_op jit(solution)/shard_map/ppermute | solution.py:50
  11.0 0.8 collective-permute-start.1
  11.8 2.2 %copy-done.1 = bf16[2,1024,1024]{2,1,0:T(8,128)(2,1)S(1)} copy-done((bf16[2,1024,1024]{2,1,0:T(8,128)(2,1)S(1)}, bf16[2,1024,1024]{2,1,0:T(8,128)(2,1)}, u32[]{:S(2)}) %copy-start.1) | copy-done | bytes 4194328
  14.0 1.3 %own.1.refs_0_ = bf16[3,256,256]{2,1,0:T(8,128)(2,1)S(1)} custom-call(s32[6]{0:T(128)S(1)} %stack.31.where_ref, s32[2,2,8]{2,1,0:T(2,128)S(1)} %copy-done.6, bf16[256,1024]{1,0:T(8,128)(2,1)S(1)} %copy-done.3, bf16[2,256,1024]{2,1,0:T(8,128)(2,1)S(1)} %copy-done.2, bf16[2,1024,1024]{2,1,0:T(8,128)(2,1)S(1)} %copy-done.1), custom_call_target="tpu_custom_call" | custom-call | flops 1 | tf_op jit(solution)/shard_map/own/pallas_call | solution.py:150
  15.3 20.9 %collective-permute-done.refs_7_.fetched_ref = bf16[512,1280]{1,0:T(8,128)(2,1)S(1)} collective-permute-done((bf16[512,1280]{1,0:T(8,128)(2,1)S(1)}, bf16[512,1280]{1,0:T(8,128)(2,1)S(1)}, u32[]{:S(2)}, u32[]{:S(2)}) %collective-permute-start) | collective-permute-done | bytes 1310752 | tf_op jit(solution)/shard_map/ppermute | solution.py:50
  36.2 1.8 %collective-permute-start.11 = (bf16[512,1280]{1,0:T(8,128)(2,1)S(1)}, bf16[512,1280]{1,0:T(8,128)(2,1)S(1)}, u32[]{:S(2)}, u32[]{:S(2)}) collective-permute-start(bf16[512,1280]{1,0:T(8,128)(2,1)S(1)} %collective-permute-done.refs_7_.fetched_ref), channel_id=1, source_target_pairs={{0,16},{16,0},{1,17},{17,1},{2,18},{18,2},{3,19},{19,3},{4,20},{20... | collective-permute-start | bytes 3932168 | tf_op jit(solution)/shard_map/ppermute | solution.py:50
  37.9 6.3 %collective-permute-done.2.refs_2_ = bf16[3,256,256]{2,1,0:T(8,128)(2,1)S(1)} collective-permute-done((bf16[3,256,256]{2,1,0:T(8,128)(2,1)S(1)}, bf16[3,256,256]{2,1,0:T(8,128)(2,1)S(1)}, u32[]{:S(2)}, u32[]{:S(2)}) %collective-permute-start.2) | collective-permute-done | bytes 393248 | tf_op jit(solution)/shard_map/ppermute | solution.py:50
  44.2 2.5 %attend.2 = bf16[4,128,256]{2,1,0:T(8,128)(2,1)S(1)} custom-call(s32[6]{0:T(128)S(1)} %stack.31.where_ref, bf16[3,256,256]{2,1,0:T(8,128)(2,1)S(1)} %own.1.refs_0_, bf16[3,256,256]{2,1,0:T(8,128)(2,1)S(1)} %collective-permute-done.1.refs_1_, bf16[3,256,256]{2,1,0:T(8,128)(2,1)S(1)} %collective-permute-done.2.refs_2_, ...), custom_call_target="tpu_custom_call" | custom-call | flops 1 | tf_op jit(solution)/shard_map/attend/pallas_call | solution.py:408
  46.7 0.1 collective-permute-start.8
  46.8 3.0 %collective-permute-start.7 = (bf16[512,256]{1,0:T(8,128)(2,1)S(1)}, bf16[512,256]{1,0:T(8,128)(2,1)S(1)}, u32[]{:S(2)}, u32[]{:S(2)}) collective-permute-start(bf16[512,256]{1,0:T(8,128)(2,1)S(1)} %bitcast.10), channel_id=1, source_target_pairs={{0,4},{4,0},{8,12},{12,8},{1,5},{5,1},{9,13},{13,9},{2,6},{6,2},{1... | collective-permute-start | bytes 786440 | tf_op jit(solution)/shard_map/ppermute | solution.py:50
  49.8 2.5 %attend.3 = bf16[4,128,256]{2,1,0:T(8,128)(2,1)S(1)} custom-call(s32[6]{0:T(128)S(1)} %stack.31.where_ref, bf16[3,256,256]{2,1,0:T(8,128)(2,1)S(1)} %own.1.refs_0_, bf16[3,256,256]{2,1,0:T(8,128)(2,1)S(1)} %collective-permute-done.1.refs_1_, bf16[3,256,256]{2,1,0:T(8,128)(2,1)S(1)} %collective-permute-done.2.refs_2_, ...), custom_call_target="tpu_custom_call" | custom-call | flops 1 | tf_op jit(solution)/shard_map/attend/pallas_call | solution.py:408
  52.3 0.6 collective-permute-start.4
  53.0 1.5 %products.2.refs_4_ = f32[512,1280]{1,0:T(8,128)S(1)} custom-call(s32[6]{0:T(128)S(1)} %stack.31.where_ref, bf16[512,256]{1,0:T(8,128)(2,1)S(1)} %bitcast.11, bf16[1024,1280]{1,0:T(8,128)(2,1)S(1)} %copy-done), custom_call_target="tpu_custom_call" | custom-call | flops 6000000000 | tf_op jit(solution)/shard_map/products/pallas_call | solution.py:433
  54.5 4.3 %collective-permute-done.4.refs_2_ = bf16[512,256]{1,0:T(8,128)(2,1)S(1)} collective-permute-done((bf16[512,256]{1,0:T(8,128)(2,1)S(1)}, bf16[512,256]{1,0:T(8,128)(2,1)S(1)}, u32[]{:S(2)}, u32[]{:S(2)}) %collective-permute-start.4) | collective-permute-done | bytes 262176 | tf_op jit(solution)/shard_map/ppermute | solution.py:50
  58.8 0.6 collective-permute-start.6
  59.3 1.7 %collective-permute-start.5 = (bf16[512,256]{1,0:T(8,128)(2,1)S(1)}, bf16[512,256]{1,0:T(8,128)(2,1)S(1)}, u32[]{:S(2)}, u32[]{:S(2)}) collective-permute-start(bf16[512,256]{1,0:T(8,128)(2,1)S(1)} %collective-permute-done.4.refs_2_), channel_id=1, source_target_pairs={{0,4},{4,0},{8,12},{12,8},{1,5},{5,1},{9,13},{13,9},{2,6},{6,2},{1... | collective-permute-start | bytes 786440 | tf_op jit(solution)/shard_map/ppermute | solution.py:50
  61.1 0.7 collective-permute-start.12
  61.7 1.3 %collective-permute-start.13 = (bf16[512,256]{1,0:T(8,128)(2,1)S(1)}, bf16[512,256]{1,0:T(8,128)(2,1)S(1)}, u32[]{:S(2)}, u32[]{:S(2)}) collective-permute-start(bf16[512,256]{1,0:T(8,128)(2,1)S(1)} %collective-permute-done.8.refs_0_), channel_id=1, source_target_pairs={{4,0},{8,12},{5,1},{9,13},{6,2},{10,14},{7,3},{11,15},{20,16},{24,... | collective-permute-start | bytes 786440 | tf_op jit(solution)/shard_map/ppermute | solution.py:589
  63.0 2.2 %products.3.refs_5_ = f32[512,1280]{1,0:T(8,128)S(1)} custom-call(s32[6]{0:T(128)S(1)} %stack.31.where_ref, bf16[512,256]{1,0:T(8,128)(2,1)S(1)} %collective-permute-done.8.refs_0_, bf16[512,256]{1,0:T(8,128)(2,1)S(1)} %collective-permute-done.7.refs_1_, bf16[1024,1280]{1,0:T(8,128)(2,1)S(1)} %copy-done, bf16[1024,1280]{1,0:T(8,128)(2,1)S(1)} %copy-done, ...), custom_call_target="tpu_custom_call" | custom-call | flops 1 | tf_op jit(solution)/shard_map/products/pallas_call | solution.py:433
  65.3 6.3 %collective-permute-done.6.refs_3_ = bf16[512,256]{1,0:T(8,128)(2,1)S(1)} collective-permute-done((bf16[512,256]{1,0:T(8,128)(2,1)S(1)}, bf16[512,256]{1,0:T(8,128)(2,1)S(1)}, u32[]{:S(2)}, u32[]{:S(2)}) %collective-permute-start.6) | collective-permute-done | bytes 262176 | tf_op jit(solution)/shard_map/ppermute | solution.py:50
  71.6 1.5 %collective-permute-done.5.refs_4_ = bf16[512,256]{1,0:T(8,128)(2,1)S(1)} collective-permute-done((bf16[512,256]{1,0:T(8,128)(2,1)S(1)}, bf16[512,256]{1,0:T(8,128)(2,1)S(1)}, u32[]{:S(2)}, u32[]{:S(2)}) %collective-permute-start.5) | collective-permute-done | bytes 262176 | tf_op jit(solution)/shard_map/ppermute | solution.py:50
  73.1 0.7 collective-permute-start.9
  73.8 1.3 %collective-permute-start.10 = (bf16[512,256]{1,0:T(8,128)(2,1)S(1)}, bf16[512,256]{1,0:T(8,128)(2,1)S(1)}, u32[]{:S(2)}, u32[]{:S(2)}) collective-permute-start(bf16[512,256]{1,0:T(8,128)(2,1)S(1)} %collective-permute-done.6.refs_3_), channel_id=1, source_target_pairs={{4,0},{8,12},{5,1},{9,13},{6,2},{10,14},{7,3},{11,15},{20,16},{24,... | collective-permute-start | bytes 786440 | tf_op jit(solution)/shard_map/ppermute | solution.py:589
  75.1 2.8 %collective-permute-done.13.refs_1_ = bf16[512,256]{1,0:T(8,128)(2,1)S(1)} collective-permute-done((bf16[512,256]{1,0:T(8,128)(2,1)S(1)}, bf16[512,256]{1,0:T(8,128)(2,1)S(1)}, u32[]{:S(2)}, u32[]{:S(2)}) %collective-permute-start.13) | collective-permute-done | bytes 262176 | tf_op jit(solution)/shard_map/ppermute | solution.py:589
  77.9 4.0 %first.1.acc_in = f32[512,1280]{1,0:T(8,128)S(1)} custom-call(s32[6]{0:T(128)S(1)} %stack.31.where_ref, bf16[512,256]{1,0:T(8,128)(2,1)S(1)} %collective-permute-done.12.refs_0_, bf16[512,256]{1,0:T(8,128)(2,1)S(1)} %collective-permute-done.13.refs_1_, bf16[512,256]{1,0:T(8,128)(2,1)S(1)} %collective-permute-done.4.refs_2_, ...), custom_call_target="tpu_custom_call" | custom-call | flops 1 | tf_op jit(solution)/shard_map/first/pallas_call | solution.py:481
  81.9 0.9 collective-permute-done.10.more
  82.8 1.1 %second.3 = (bf16[4,64,640]{2,1,0:T(8,128)(2,1)S(1)}, bf16[4,64,640]{2,1,0:T(8,128)(2,1)S(1)}) custom-call(s32[6]{0:T(128)S(1)} %stack.31.where_ref, bf16[512,256]{1,0:T(8,128)(2,1)S(1)} %collective-permute-done.9.slot, bf16[512,256]{1,0:T(8,128)(2,1)S(1)} %collective-permute-done.10.more, bf16[512,1280]{1,0:T(8,128)(2,1)S(1)} %collective-permute-done.refs_7_.fetched_ref, ...), custom_call_target="tpu_custom_call" | custom-call | flops 1 | tf_op jit(solution)/shard_map/second/pallas_call | solution.py:522
  83.9 0.0 copy-start.5
  83.9 0.1 collective-permute-start.18
  84.0 1.1 %second.2 = (bf16[4,64,640]{2,1,0:T(8,128)(2,1)S(1)}, bf16[4,64,640]{2,1,0:T(8,128)(2,1)S(1)}) custom-call(s32[6]{0:T(128)S(1)} %stack.31.where_ref, bf16[512,256]{1,0:T(8,128)(2,1)S(1)} %collective-permute-done.9.slot, bf16[512,256]{1,0:T(8,128)(2,1)S(1)} %collective-permute-done.10.more, bf16[512,1280]{1,0:T(8,128)(2,1)S(1)} %collective-permute-done.refs_7_.fetched_ref, ...), custom_call_target="tpu_custom_call" | custom-call | flops 1 | tf_op jit(solution)/shard_map/second/pallas_call | solution.py:522
  85.1 0.6 collective-permute-start.14
  85.7 0.6 add.8
  86.3 1.9 %collective-permute-start.19 = (bf16[64,640]{1,0:T(8,128)(2,1)S(1)}, bf16[64,640]{1,0:T(8,128)(2,1)S(1)}, u32[]{:S(2)}, u32[]{:S(2)}) collective-permute-start(bf16[64,640]{1,0:T(8,128)(2,1)S(1)} %get-tuple-element.68), channel_id=1, source_target_pairs={{0,12},{4,8},{8,4},{12,0},{1,13},{5,9},{9,5},{13,1},{2,14},{6,10},... | collective-permute-start | bytes 245768 | tf_op jit(solution)/shard_map/ppermute | solution.py:50
  88.2 0.0 collective-permute-start.20
  88.2 2.6 %collective-permute-start.21 = (bf16[64,640]{1,0:T(8,128)(2,1)S(1)}, bf16[64,640]{1,0:T(8,128)(2,1)S(1)}, u32[]{:S(2)}, u32[]{:S(2)}) collective-permute-start(bf16[64,640]{1,0:T(8,128)(2,1)S(1)} %get-tuple-element.70), channel_id=1, source_target_pairs={{0,4},{4,0},{8,12},{12,8},{1,5},{5,1},{9,13},{13,9},{2,6},{6,2},{1... | collective-permute-start | bytes 245768 | tf_op jit(solution)/shard_map/ppermute | solution.py:50
  90.7 0.6 add.7
  91.4 1.9 %collective-permute-start.15 = (bf16[64,640]{1,0:T(8,128)(2,1)S(1)}, bf16[64,640]{1,0:T(8,128)(2,1)S(1)}, u32[]{:S(2)}, u32[]{:S(2)}) collective-permute-start(bf16[64,640]{1,0:T(8,128)(2,1)S(1)} %get-tuple-element.62), channel_id=1, source_target_pairs={{0,12},{4,8},{8,4},{12,0},{1,13},{5,9},{9,5},{13,1},{2,14},{6,10},... | collective-permute-start | bytes 245768 | tf_op jit(solution)/shard_map/ppermute | solution.py:50
  93.3 0.3 collective-permute-done.19.refs_5_
  93.5 2.3 %collective-permute-start.17 = (bf16[64,640]{1,0:T(8,128)(2,1)S(1)}, bf16[64,640]{1,0:T(8,128)(2,1)S(1)}, u32[]{:S(2)}, u32[]{:S(2)}) collective-permute-start(bf16[64,640]{1,0:T(8,128)(2,1)S(1)} %get-tuple-element.64), channel_id=1, source_target_pairs={{0,4},{4,0},{8,12},{12,8},{1,5},{5,1},{9,13},{13,9},{2,6},{6,2},{1... | collective-permute-start | bytes 245768 | tf_op jit(solution)/shard_map/ppermute | solution.py:50
  95.8 3.0 %collective-permute-done.20.refs_6_ = bf16[64,640]{1,0:T(8,128)(2,1)S(1)} collective-permute-done((bf16[64,640]{1,0:T(8,128)(2,1)S(1)}, bf16[64,640]{1,0:T(8,128)(2,1)S(1)}, u32[]{:S(2)}, u32[]{:S(2)}) %collective-permute-start.20) | collective-permute-done | bytes 81952 | tf_op jit(solution)/shard_map/ppermute | solution.py:50
  98.9 4.2 %collective-permute-done.16.refs_2_ = bf16[64,640]{1,0:T(8,128)(2,1)S(1)} collective-permute-done((bf16[64,640]{1,0:T(8,128)(2,1)S(1)}, bf16[64,640]{1,0:T(8,128)(2,1)S(1)}, u32[]{:S(2)}, u32[]{:S(2)}) %collective-permute-start.16) | collective-permute-done | bytes 81952 | tf_op jit(solution)/shard_map/ppermute | solution.py:50
  103.1 1.6 %mix.1 = bf16[64,5120]{1,0:T(8,128)(2,1)} custom-call(s32[6]{0:T(128)S(1)} %stack.31.where_ref, bf16[64,5120]{1,0:T(8,128)(2,1)S(1)} %copy-done.4, f32[1,5120]{1,0:T(1,128)S(1)} %bitcast.14, bf16[64,640]{1,0:T(8,128)(2,1)S(1)} %get-tuple-element.61.refs_0_, bf16[64,640]{1,0:T(8,128)(2,1)S(1)} %collective-permute-done.15.refs_1_, ...), custom_call_target="tpu_custom_call" | custom-call | flops 1 | tf_op jit(solution)/shard_map/mix/pallas_call | solution.py:618
  (30 shorter events, 0.1 us)
Async XLA Ops:
  0.0 3.7 %copy-start = (bf16[1024,1280]{1,0:T(8,128)(2,1)S(1)}, bf16[1024,1280]{1,0:T(8,128)(2,1)}, u32[]{:S(2)}) copy-start(bf16[1024,1280]{1,0:T(8,128)(2,1)} %refs_6_) | copy-start | bytes 7864324
  3.5 7.4 %copy-start.7 = (bf16[3,256,256]{2,1,0:T(8,128)(2,1)S(1)}, bf16[3,256,256]{2,1,0:T(8,128)(2,1)}, u32[]{:S(2)}) copy-start(bf16[3,256,256]{2,1,0:T(8,128)(2,1)} %get-tuple-element.40) | copy-start | bytes 1179652
  3.6 8.2 %copy-start.3 = (bf16[256,1024]{1,0:T(8,128)(2,1)S(1)}, bf16[256,1024]{1,0:T(8,128)(2,1)}, u32[]{:S(2)}) copy-start(bf16[256,1024]{1,0:T(8,128)(2,1)} %q_ref.3) | copy-start | bytes 1572868
  3.6 8.2 %copy-start.6 = (s32[2,2,8]{2,1,0:T(2,128)S(1)}, s32[2,2,8]{2,1,0:T(2,128)}, u32[]{:S(2)}) copy-start(s32[2,2,8]{2,1,0:T(2,128)} %exps_ref.3) | copy-start | bytes 388
  3.7 3.7 %copy-start.9 = (bf16[3,256,256]{2,1,0:T(8,128)(2,1)S(1)}, bf16[3,256,256]{2,1,0:T(8,128)(2,1)}, u32[]{:S(2)}) copy-start(bf16[3,256,256]{2,1,0:T(8,128)(2,1)} %get-tuple-element.38) | copy-start | bytes 1179652
  3.7 7.3 %copy-start.8 = (bf16[3,256,256]{2,1,0:T(8,128)(2,1)S(1)}, bf16[3,256,256]{2,1,0:T(8,128)(2,1)}, u32[]{:S(2)}) copy-start(bf16[3,256,256]{2,1,0:T(8,128)(2,1)} %get-tuple-element.39) | copy-start | bytes 1179652
  3.7 8.1 %copy-start.2 = (bf16[2,256,1024]{2,1,0:T(8,128)(2,1)S(1)}, bf16[2,256,1024]{2,1,0:T(8,128)(2,1)}, u32[]{:S(2)}) copy-start(bf16[2,256,1024]{2,1,0:T(8,128)(2,1)} %fresh_ref.3) | copy-start | bytes 3145732
  4.4 31.8 %collective-permute-start = (bf16[512,1280]{1,0:T(8,128)(2,1)S(1)}, bf16[512,1280]{1,0:T(8,128)(2,1)S(1)}, u32[]{:S(2)}, u32[]{:S(2)}) collective-permute-start(bf16[512,1280]{1,0:T(8,128)(2,1)S(1)} %take.1), channel_id=1, source_target_pairs={{0,2},{2,0},{1,3},{3,1},{4,6},{6,4},{5,7},{7,5},{8,10},{10,8},{9,1... | collective-permute-start | bytes 3932168 | tf_op jit(solution)/shard_map/ppermute | solution.py:50
  7.4 30.5 %collective-permute-start.3 = (bf16[3,256,256]{2,1,0:T(8,128)(2,1)S(1)}, bf16[3,256,256]{2,1,0:T(8,128)(2,1)S(1)}, u32[]{:S(2)}, u32[]{:S(2)}) collective-permute-start(bf16[3,256,256]{2,1,0:T(8,128)(2,1)S(1)} %copy-done.9), channel_id=1, source_target_pairs={{0,12},{4,8},{8,4},{12,0},{1,13},{5,9},{9,5},{13,1},{2,14},{6,10},... | collective-permute-start | bytes 1179656 | tf_op jit(solution)/shard_map/ppermute | solution.py:50
  11.0 33.3 %collective-permute-start.2 = (bf16[3,256,256]{2,1,0:T(8,128)(2,1)S(1)}, bf16[3,256,256]{2,1,0:T(8,128)(2,1)S(1)}, u32[]{:S(2)}, u32[]{:S(2)}) collective-permute-start(bf16[3,256,256]{2,1,0:T(8,128)(2,1)S(1)} %copy-done.8), channel_id=1, source_target_pairs={{0,8},{4,12},{8,0},{12,4},{1,9},{5,13},{9,1},{13,5},{2,10},{6,14},... | collective-permute-start | bytes 1179656 | tf_op jit(solution)/shard_map/ppermute | solution.py:50
  11.0 33.3 %collective-permute-start.1 = (bf16[3,256,256]{2,1,0:T(8,128)(2,1)S(1)}, bf16[3,256,256]{2,1,0:T(8,128)(2,1)S(1)}, u32[]{:S(2)}, u32[]{:S(2)}) collective-permute-start(bf16[3,256,256]{2,1,0:T(8,128)(2,1)S(1)} %copy-done.7), channel_id=1, source_target_pairs={{0,4},{4,0},{8,12},{12,8},{1,5},{5,1},{9,13},{13,9},{2,6},{6,2},{1... | collective-permute-start | bytes 1179656 | tf_op jit(solution)/shard_map/ppermute | solution.py:50
  11.8 2.2 %copy-start.1 = (bf16[2,1024,1024]{2,1,0:T(8,128)(2,1)S(1)}, bf16[2,1024,1024]{2,1,0:T(8,128)(2,1)}, u32[]{:S(2)}) copy-start(bf16[2,1024,1024]{2,1,0:T(8,128)(2,1)} %cached_ref.3) | copy-start | bytes 12582916
  36.2 41.7 %collective-permute-start.11 = (bf16[512,1280]{1,0:T(8,128)(2,1)S(1)}, bf16[512,1280]{1,0:T(8,128)(2,1)S(1)}, u32[]{:S(2)}, u32[]{:S(2)}) collective-permute-start(bf16[512,1280]{1,0:T(8,128)(2,1)S(1)} %collective-permute-done.refs_7_.fetched_ref), channel_id=1, source_target_pairs={{0,16},{16,0},{1,17},{17,1},{2,18},{18,2},{3,19},{19,3},{4,20},{20... | collective-permute-start | bytes 3932168 | tf_op jit(solution)/shard_map/ppermute | solution.py:50
  46.7 14.3 %collective-permute-start.8 = (bf16[512,256]{1,0:T(8,128)(2,1)S(1)}, bf16[512,256]{1,0:T(8,128)(2,1)S(1)}, u32[]{:S(2)}, u32[]{:S(2)}) collective-permute-start(bf16[512,256]{1,0:T(8,128)(2,1)S(1)} %bitcast.9), channel_id=1, source_target_pairs={{0,8},{4,12},{8,0},{12,4},{1,9},{5,13},{9,1},{13,5},{2,10},{6,14},... | collective-permute-start | bytes 786440 | tf_op jit(solution)/shard_map/ppermute | solution.py:50
  46.8 14.3 %collective-permute-start.7 = (bf16[512,256]{1,0:T(8,128)(2,1)S(1)}, bf16[512,256]{1,0:T(8,128)(2,1)S(1)}, u32[]{:S(2)}, u32[]{:S(2)}) collective-permute-start(bf16[512,256]{1,0:T(8,128)(2,1)S(1)} %bitcast.10), channel_id=1, source_target_pairs={{0,4},{4,0},{8,12},{12,8},{1,5},{5,1},{9,13},{13,9},{2,6},{6,2},{1... | collective-permute-start | bytes 786440 | tf_op jit(solution)/shard_map/ppermute | solution.py:50
  52.3 6.4 %collective-permute-start.4 = (bf16[512,256]{1,0:T(8,128)(2,1)S(1)}, bf16[512,256]{1,0:T(8,128)(2,1)S(1)}, u32[]{:S(2)}, u32[]{:S(2)}) collective-permute-start(bf16[512,256]{1,0:T(8,128)(2,1)S(1)} %bitcast.13), channel_id=1, source_target_pairs={{0,2},{2,0},{1,3},{3,1},{4,6},{6,4},{5,7},{7,5},{8,10},{10,8},{9,1... | collective-permute-start | bytes 786440 | tf_op jit(solution)/shard_map/ppermute | solution.py:50
  58.8 12.9 %collective-permute-start.6 = (bf16[512,256]{1,0:T(8,128)(2,1)S(1)}, bf16[512,256]{1,0:T(8,128)(2,1)S(1)}, u32[]{:S(2)}, u32[]{:S(2)}) collective-permute-start(bf16[512,256]{1,0:T(8,128)(2,1)S(1)} %collective-permute-done.4.refs_2_), channel_id=1, source_target_pairs={{0,8},{4,12},{8,0},{12,4},{1,9},{5,13},{9,1},{13,5},{2,10},{6,14},... | collective-permute-start | bytes 786440 | tf_op jit(solution)/shard_map/ppermute | solution.py:50
  59.3 13.8 %collective-permute-start.5 = (bf16[512,256]{1,0:T(8,128)(2,1)S(1)}, bf16[512,256]{1,0:T(8,128)(2,1)S(1)}, u32[]{:S(2)}, u32[]{:S(2)}) collective-permute-start(bf16[512,256]{1,0:T(8,128)(2,1)S(1)} %collective-permute-done.4.refs_2_), channel_id=1, source_target_pairs={{0,4},{4,0},{8,12},{12,8},{1,5},{5,1},{9,13},{13,9},{2,6},{6,2},{1... | collective-permute-start | bytes 786440 | tf_op jit(solution)/shard_map/ppermute | solution.py:50
  61.1 14.0 %collective-permute-start.12 = (bf16[512,256]{1,0:T(8,128)(2,1)S(1)}, bf16[512,256]{1,0:T(8,128)(2,1)S(1)}, u32[]{:S(2)}, u32[]{:S(2)}) collective-permute-start(bf16[512,256]{1,0:T(8,128)(2,1)S(1)} %bitcast.12), channel_id=1, source_target_pairs={{4,8},{8,4},{5,9},{9,5},{6,10},{10,6},{7,11},{11,7},{20,24},{24,20... | collective-permute-start | bytes 786440 | tf_op jit(solution)/shard_map/ppermute | solution.py:50
  61.7 16.1 %collective-permute-start.13 = (bf16[512,256]{1,0:T(8,128)(2,1)S(1)}, bf16[512,256]{1,0:T(8,128)(2,1)S(1)}, u32[]{:S(2)}, u32[]{:S(2)}) collective-permute-start(bf16[512,256]{1,0:T(8,128)(2,1)S(1)} %collective-permute-done.8.refs_0_), channel_id=1, source_target_pairs={{4,0},{8,12},{5,1},{9,13},{6,2},{10,14},{7,3},{11,15},{20,16},{24,... | collective-permute-start | bytes 786440 | tf_op jit(solution)/shard_map/ppermute | solution.py:589
  73.1 8.8 %collective-permute-start.9 = (bf16[512,256]{1,0:T(8,128)(2,1)S(1)}, bf16[512,256]{1,0:T(8,128)(2,1)S(1)}, u32[]{:S(2)}, u32[]{:S(2)}) collective-permute-start(bf16[512,256]{1,0:T(8,128)(2,1)S(1)} %collective-permute-done.4.refs_2_), channel_id=1, source_target_pairs={{4,8},{8,4},{5,9},{9,5},{6,10},{10,6},{7,11},{11,7},{20,24},{24,20... | collective-permute-start | bytes 786440 | tf_op jit(solution)/shard_map/ppermute | solution.py:50
  73.8 9.0 %collective-permute-start.10 = (bf16[512,256]{1,0:T(8,128)(2,1)S(1)}, bf16[512,256]{1,0:T(8,128)(2,1)S(1)}, u32[]{:S(2)}, u32[]{:S(2)}) collective-permute-start(bf16[512,256]{1,0:T(8,128)(2,1)S(1)} %collective-permute-done.6.refs_3_), channel_id=1, source_target_pairs={{4,0},{8,12},{5,1},{9,13},{6,2},{10,14},{7,3},{11,15},{20,16},{24,... | collective-permute-start | bytes 786440 | tf_op jit(solution)/shard_map/ppermute | solution.py:589
  83.9 19.2 %copy-start.4 = (bf16[64,5120]{1,0:T(8,128)(2,1)S(1)}, bf16[64,5120]{1,0:T(8,128)(2,1)}, u32[]{:S(2)}) copy-start(bf16[64,5120]{1,0:T(8,128)(2,1)} %hidden_ref.1) | copy-start | bytes 1966084
  83.9 19.2 %copy-start.5 = (f32[5120]{0:T(1024)S(1)}, f32[5120]{0:T(1024)}, u32[]{:S(2)}) copy-start(f32[5120]{0:T(1024)} %param.13) | copy-start | bytes 61444
  83.9 1.8 %collective-permute-start.18 = (bf16[4,64,640]{2,1,0:T(8,128)(2,1)S(1)}, bf16[4,64,640]{2,1,0:T(8,128)(2,1)S(1)}, u32[]{:S(2)}, u32[]{:S(2)}) collective-permute-start(bf16[4,64,640]{2,1,0:T(8,128)(2,1)S(1)} %get-tuple-element.66), channel_id=1, source_target_pairs={{0,1},{1,0},{2,3},{3,2},{4,5},{5,4},{6,7},{7,6},{8,9},{9,8},{10,11... | collective-permute-start | bytes 983048 | tf_op jit(solution)/shard_map/ppermute | solution.py:50
  85.1 5.6 %collective-permute-start.14 = (bf16[4,64,640]{2,1,0:T(8,128)(2,1)S(1)}, bf16[4,64,640]{2,1,0:T(8,128)(2,1)S(1)}, u32[]{:S(2)}, u32[]{:S(2)}) collective-permute-start(bf16[4,64,640]{2,1,0:T(8,128)(2,1)S(1)} %get-tuple-element.60), channel_id=1, source_target_pairs={{0,1},{1,0},{2,3},{3,2},{4,5},{5,4},{6,7},{7,6},{8,9},{9,8},{10,11... | collective-permute-start | bytes 983048 | tf_op jit(solution)/shard_map/ppermute | solution.py:50
  86.3 7.3 %collective-permute-start.19 = (bf16[64,640]{1,0:T(8,128)(2,1)S(1)}, bf16[64,640]{1,0:T(8,128)(2,1)S(1)}, u32[]{:S(2)}, u32[]{:S(2)}) collective-permute-start(bf16[64,640]{1,0:T(8,128)(2,1)S(1)} %get-tuple-element.68), channel_id=1, source_target_pairs={{0,12},{4,8},{8,4},{12,0},{1,13},{5,9},{9,5},{13,1},{2,14},{6,10},... | collective-permute-start | bytes 245768 | tf_op jit(solution)/shard_map/ppermute | solution.py:50
  88.2 10.7 %collective-permute-start.20 = (bf16[64,640]{1,0:T(8,128)(2,1)S(1)}, bf16[64,640]{1,0:T(8,128)(2,1)S(1)}, u32[]{:S(2)}, u32[]{:S(2)}) collective-permute-start(bf16[64,640]{1,0:T(8,128)(2,1)S(1)} %get-tuple-element.69), channel_id=1, source_target_pairs={{0,8},{4,12},{8,0},{12,4},{1,9},{5,13},{9,1},{13,5},{2,10},{6,14},... | collective-permute-start | bytes 245768 | tf_op jit(solution)/shard_map/ppermute | solution.py:50
  88.2 10.7 %collective-permute-start.21 = (bf16[64,640]{1,0:T(8,128)(2,1)S(1)}, bf16[64,640]{1,0:T(8,128)(2,1)S(1)}, u32[]{:S(2)}, u32[]{:S(2)}) collective-permute-start(bf16[64,640]{1,0:T(8,128)(2,1)S(1)} %get-tuple-element.70), channel_id=1, source_target_pairs={{0,4},{4,0},{8,12},{12,8},{1,5},{5,1},{9,13},{13,9},{2,6},{6,2},{1... | collective-permute-start | bytes 245768 | tf_op jit(solution)/shard_map/ppermute | solution.py:50
  91.4 7.5 %collective-permute-start.15 = (bf16[64,640]{1,0:T(8,128)(2,1)S(1)}, bf16[64,640]{1,0:T(8,128)(2,1)S(1)}, u32[]{:S(2)}, u32[]{:S(2)}) collective-permute-start(bf16[64,640]{1,0:T(8,128)(2,1)S(1)} %get-tuple-element.62), channel_id=1, source_target_pairs={{0,12},{4,8},{8,4},{12,0},{1,13},{5,9},{9,5},{13,1},{2,14},{6,10},... | collective-permute-start | bytes 245768 | tf_op jit(solution)/shard_map/ppermute | solution.py:50
  93.2 9.8 %collective-permute-start.16 = (bf16[64,640]{1,0:T(8,128)(2,1)S(1)}, bf16[64,640]{1,0:T(8,128)(2,1)S(1)}, u32[]{:S(2)}, u32[]{:S(2)}) collective-permute-start(bf16[64,640]{1,0:T(8,128)(2,1)S(1)} %get-tuple-element.63), channel_id=1, source_target_pairs={{0,8},{4,12},{8,0},{12,4},{1,9},{5,13},{9,1},{13,5},{2,10},{6,14},... | collective-permute-start | bytes 245768 | tf_op jit(solution)/shard_map/ppermute | solution.py:50
  93.5 9.6 %collective-permute-start.17 = (bf16[64,640]{1,0:T(8,128)(2,1)S(1)}, bf16[64,640]{1,0:T(8,128)(2,1)S(1)}, u32[]{:S(2)}, u32[]{:S(2)}) collective-permute-start(bf16[64,640]{1,0:T(8,128)(2,1)S(1)} %get-tuple-element.64), channel_id=1, source_target_pairs={{0,4},{4,0},{8,12},{12,8},{1,5},{5,1},{9,13},{13,9},{2,6},{6,2},{1... | collective-permute-start | bytes 245768 | tf_op jit(solution)/shard_map/ppermute | solution.py:50

commit v19 on v18

--- a/solution.py
+++ b/solution.py
@@ -50,18 +50,27 @@
     return lax.ppermute(x, axes, pairs)
 
 
+def power_of_two(exponent):
+    return lax.shift_left(jnp.int32(1), exponent + 15).astype(jnp.float32) * 2.0**-15
+
+
 def decode(fresh, cached, exponent):
-    power = jnp.full((1, HEAD_DIM), exponent.astype(jnp.float32))
     cached = cached.astype(jnp.float32)
     residual = fresh.astype(jnp.float32) - cached
-    codes = jnp.clip(residual * jnp.exp2(-power), -SATURATION, SATURATION).astype(jnp.bfloat16)
-    return (cached + codes.astype(jnp.float32) * jnp.exp2(power)).astype(jnp.bfloat16)
-
-
-def pack_kernel(split, per, exps_ref, q_ref, fresh_ref, cached_ref, *refs):
-    outs, bufs = refs[: split - 1], refs[split - 1 : 2 * split - 2]
-    q_buf, fresh_buf, cached_buf, sems, out_sems = refs[2 * split - 2 :]
+    scaled = residual * power_of_two(-exponent)
+    codes = jnp.clip(scaled, -SATURATION, SATURATION).astype(jnp.bfloat16)
+    return (cached + codes.astype(jnp.float32) * power_of_two(exponent)).astype(jnp.bfloat16)
+
+
+def pack_kernel(split, per, shares, exps_ref, q_ref, fresh_ref, cached_ref, weight_ref, *refs):
+    outs, part_ref, bufs = refs[: split - 1], refs[split - 1], refs[split : 2 * split - 1]
+    q_buf, fresh_buf, cached_buf, sems, out_sems, part_sem = refs[2 * split - 1 :]
     patch = lax.axis_index("patch")
+    count = part_ref.shape[0]
+    start = lax.axis_index("grp") * count if shares == 2 else 0
+    part = pltpu.make_async_copy(
+        weight_ref.at[pl.ds(pl.multiple_of(start, HEAD_DIM), count)], part_ref, part_sem
+    )
     near = lax.rem(patch, split)
     tok = q_buf.shape[0]
     copies, sent = [], []
@@ -77,6 +86,7 @@
         )
         for copy in copies[-1]:
             copy.start()
+    part.start()
     for block in range(tok // PACK_ROWS):
         rows = pl.ds(block * PACK_ROWS, PACK_ROWS)
         for copy in copies[block]:
@@ -104,18 +114,20 @@
             sent[-1].start()
     for copy in sent:
         copy.wait()
-
-
-def pack(split, exponents, queries, fresh_kv, cached_kv):
+    part.wait()
+
+
+def pack(split, shares, exponents, queries, fresh_kv, cached_kv, weight):
     tok, channels = queries.shape
     feat = channels // split
     blocks = tok // PACK_ROWS
     hbm = pl.BlockSpec(memory_space=pltpu.HBM)
     return pl.pallas_call(
-        functools.partial(pack_kernel, split, feat // HEAD_DIM),
-        out_shape=[jax.ShapeDtypeStruct((3, tok, feat), jnp.bfloat16)] * (split - 1),
-        in_specs=[pl.BlockSpec(memory_space=pltpu.SMEM), hbm, hbm, hbm],
-        out_specs=[hbm] * (split - 1),
+        functools.partial(pack_kernel, split, feat // HEAD_DIM, shares),
+        out_shape=[jax.ShapeDtypeStruct((3, tok, feat), jnp.bfloat16)] * (split - 1)
+        + [jax.ShapeDtypeStruct((weight.shape[0] // shares, weight.shape[1]), weight.dtype)],
+        in_specs=[pl.BlockSpec(memory_space=pltpu.SMEM), hbm, hbm, hbm, hbm],
+        out_specs=[hbm] * split,
         scratch_shapes=[pltpu.VMEM((3, tok, feat), jnp.bfloat16)] * (split - 1)
         + [
             pltpu.VMEM((tok, channels), jnp.bfloat16),
@@ -123,10 +135,11 @@
             pltpu.VMEM((2, tok, channels), jnp.bfloat16),
             pltpu.SemaphoreType.DMA((blocks, 3)),
             pltpu.SemaphoreType.DMA((blocks, split - 1)),
+            pltpu.SemaphoreType.DMA,
         ],
         compiler_params=pltpu.CompilerParams(vmem_limit_bytes=PACK_VMEM_BYTES),
         name="pack",
-    )(exponents, queries, fresh_kv, cached_kv)
+    )(exponents, queries, fresh_kv, cached_kv, weight)
 
 
 def own_kernel(per, where_ref, exps_ref, q_ref, fresh_ref, cached_ref, out_ref):
@@ -549,25 +562,8 @@
     )(where, keep, term)
 
 
-def take_kernel(where_ref, weight_ref, out_ref):
-    out_ref[...] = weight_ref[...]
-
-
-def take_half(where, weight):
-    rows, cols = weight.shape[0] // 2, weight.shape[1]
-    return call(
-        take_kernel,
-        "take",
-        jax.ShapeDtypeStruct((rows, cols), weight.dtype),
-        2,
-        [pl.BlockSpec((rows // 2, cols), lambda i, w: (2 * w[GRP] + i, 0))],
-        pl.BlockSpec((rows // 2, cols), lambda i, w: (i, 0)),
-    )(where, weight)
-
-
-def share_tail(sizes, where, pieces, kv_pieces, out_weight, hidden_in, attn_gate):
-    out_weight, where = lax.optimization_barrier((out_weight, where))
-    fetched = swap(take_half(where, out_weight), "head", 2, 1)
+def share_tail(sizes, where, pieces, out_weight, part, hidden_in, attn_gate):
+    fetched = swap(part, "head", 2, 1)
     own, fetched = lax.optimization_barrier((pieces[0], fetched))
     pieces = [own, *pieces[1:]]
     passed = swap(fetched, "grp", 2, 1)
@@ -645,20 +641,20 @@
     ).astype(jnp.int32)
 
     arrays = (exponents, queries, fresh_kv, cached_kv)
-    sent = pack(split, *arrays)
+    shared = (sizes["grp"], n_head, split, n_patch, heads) == (2, 2, 4, 4, 8)
+    shares = 2 if shared else out_weight.shape[0] // HEAD_DIM
+    *sent, part = pack(split, shares, *arrays, out_weight)
     far_first = [
         swap(x, "patch", n_patch, split - 1 - at) for at, x in enumerate(sent)
     ]
     where, sent = lax.optimization_barrier((where, sent))
     pieces = [pack_own(split, where, *arrays), *far_first]
+    if shared:
+        return share_tail(sizes, where, pieces, out_weight, part, hidden_in, attn_gate)
     kv_pieces = list(pieces)
     for rel in range(split, n_patch, split):
         kv_pieces += [swap(x, "patch", n_patch, rel) for x in pieces]
-
-    tail = (sizes, where, pieces, kv_pieces, out_weight, hidden_in, attn_gate)
-    if (sizes["grp"], n_head, split, n_patch) == (2, 2, 4, 4):
-        return share_tail(*tail)
-    return sum_tail(*tail)
+    return sum_tail(sizes, where, pieces, kv_pieces, out_weight, hidden_in, attn_gate)
 
 
 def solution(mesh):

time: 105 us -> 144 us (1.37)
  Pallas kernels: 23.2 us -> 63 us
    pallas_call x2 -> x1, Pallas kernels: 4.21 us -> 41.9 us  [pack(): pl.pallas_call(functools.partial(pack_kernel, split, feat // HEAD_DIM, sh...]
    pallas_call x2, Pallas kernels: 4.96 us -> 7.09 us  [attend_half(): call(functools.partial(attend_half_kernel, half), 'attend', out, 1, [spec...]
  transfers between devices with their start and end apart: 22 -> 22, of which waited for: 10 -> 9; matrix products, arithmetic and copies ran while one was open for 0% -> 0% of each run, Pallas kernels for 16% -> 13%
where the time goes in v19:
time: 144 us
  Pallas kernels  63 us (44%)
  waiting for transfers between devices  49.6 us (34%)
  starting transfers between devices  28.6 us (20%)
  local copies, waits for them, and re-layouts  2.3 us (2%)
    ppermute x20, waiting for transfers between devices, swap(): return lax.ppermute(x, axes, pairs)  46.5 us
    pallas_call x1, Pallas kernels, pack(): pl.pallas_call(functools.partial(pack_kernel, split, feat // HEAD_DIM, sh...  41.9 us
    ppermute x20, starting transfers between devices, swap(): return lax.ppermute(x, axes, pairs)  26 us
    pallas_call x2, Pallas kernels, attend_half(): call(functools.partial(attend_half_kernel, half), 'attend', out, 1, [spec...  7.09 us
    pallas_call x1, Pallas kernels, first_product(): call(first_kernel, 'first', jax.ShapeDtypeStruct(acc.shape, jnp.float32),...  3.96 us
    pallas_call x2, Pallas kernels, add_product(): call(functools.partial(add_product_kernel, len(rels)), 'products', jax.Sh...  3.79 us
    ppermute x2, waiting for transfers between devices, share_tail(): ends = lax.ppermute(far, 'patch', [(1, 0), (2, 3)])  3.11 us
  transfers between devices with their start and end apart: 22, of which 9 were waited for; matrix products, arithmetic and copies ran while one was open for 0% of the time, Pallas kernels for 13%

profile of v19, /device:TPU:0, one launch (start us, length us, event | category | flops | bytes accessed | tf_op | source)
XLA Modules:
  0.0 143.7 jit_solution(2486190879513339670)
XLA Ops:
  0.0 41.9 %pack.1 = (bf16[3,256,256]{2,1,0:T(8,128)(2,1)}, bf16[3,256,256]{2,1,0:T(8,128)(2,1)}, bf16[3,256,256]{2,1,0:T(8,128)(2,1)}, bf16[512,1280]{1,0:T(8,128)(2,1)}) custom-call(s32[2,2,8]{2,1,0:T(2,128)} %exps_ref.3, bf16[256,1024]{1,0:T(8,128)(2,1)} %q_ref.3, bf16[2,256,1024]{2,1,0:T(8,128)(2,1)} %fresh_ref.3, bf16[2,1024,1024]{2,1,0:T(8,128)(2,1)} %cached_ref.3, ...), custom_call_target="tpu_custom_call" | custom-call | tf_op jit(solution)/shard_map/pack/pallas_call | solution.py:125
  41.9 3.0 %collective-permute-start = (bf16[512,1280]{1,0:T(8,128)(2,1)}, bf16[512,1280]{1,0:T(8,128)(2,1)S(1)}, u32[]{:S(2)}, u32[]{:S(2)}) collective-permute-start(bf16[512,1280]{1,0:T(8,128)(2,1)} %get-tuple-element.41), channel_id=1, source_target_pairs={{0,2},{2,0},{1,3},{3,1},{4,6},{6,4},{5,7},{7,5},{8,10},{10,8},{9,1... | collective-permute-start | bytes 3932168 | tf_op jit(solution)/shard_map/ppermute | solution.py:50
  44.9 3.6 %collective-permute-start.3 = (bf16[3,256,256]{2,1,0:T(8,128)(2,1)}, bf16[3,256,256]{2,1,0:T(8,128)(2,1)S(1)}, u32[]{:S(2)}, u32[]{:S(2)}) collective-permute-start(bf16[3,256,256]{2,1,0:T(8,128)(2,1)} %get-tuple-element.37), channel_id=1, source_target_pairs={{0,12},{4,8},{8,4},{12,0},{1,13},{5,9},{9,5},{13,1},{2,14},{6,10},... | collective-permute-start | bytes 1179656 | tf_op jit(solution)/shard_map/ppermute | solution.py:50
  48.5 0.0 collective-permute-start.2
  48.5 0.8 collective-permute-start.1
  49.3 0.1 stack.31.where_ref
  49.4 0.0 copy-start.1
  49.4 2.2 %copy-done.1 = bf16[2,1024,1024]{2,1,0:T(8,128)(2,1)S(1)} copy-done((bf16[2,1024,1024]{2,1,0:T(8,128)(2,1)S(1)}, bf16[2,1024,1024]{2,1,0:T(8,128)(2,1)}, u32[]{:S(2)}) %copy-start.1) | copy-done | bytes 4194328
  51.6 1.3 own.1.refs_0_
  52.9 0.0 copy-start
  52.9 21.0 %collective-permute-done.refs_7_.fetched_ref = bf16[512,1280]{1,0:T(8,128)(2,1)S(1)} collective-permute-done((bf16[512,1280]{1,0:T(8,128)(2,1)}, bf16[512,1280]{1,0:T(8,128)(2,1)S(1)}, u32[]{:S(2)}, u32[]{:S(2)}) %collective-permute-start) | collective-permute-done | bytes 1310752 | tf_op jit(solution)/shard_map/ppermute | solution.py:50
  73.9 1.8 %collective-permute-start.11 = (bf16[512,1280]{1,0:T(8,128)(2,1)S(1)}, bf16[512,1280]{1,0:T(8,128)(2,1)S(1)}, u32[]{:S(2)}, u32[]{:S(2)}) collective-permute-start(bf16[512,1280]{1,0:T(8,128)(2,1)S(1)} %collective-permute-done.refs_7_.fetched_ref), channel_id=1, source_target_pairs={{0,16},{16,0},{1,17},{17,1},{2,18},{18,2},{3,19},{19,3},{4,20},{20... | collective-permute-start | bytes 3932168 | tf_op jit(solution)/shard_map/ppermute | solution.py:50
  75.7 6.4 %collective-permute-done.2.refs_2_ = bf16[3,256,256]{2,1,0:T(8,128)(2,1)} collective-permute-done((bf16[3,256,256]{2,1,0:T(8,128)(2,1)}, bf16[3,256,256]{2,1,0:T(8,128)(2,1)}, u32[]{:S(2)}, u32[]{:S(2)}) %collective-permute-start.2) | collective-permute-done | bytes 393248 | tf_op jit(solution)/shard_map/ppermute | solution.py:50
  82.1 0.0 collective-permute-done.1.refs_1_
  82.1 3.5 %attend.2 = bf16[4,128,256]{2,1,0:T(8,128)(2,1)S(1)} custom-call(s32[6]{0:T(128)S(1)} %stack.31.where_ref, bf16[3,256,256]{2,1,0:T(8,128)(2,1)S(1)} %own.1.refs_0_, bf16[3,256,256]{2,1,0:T(8,128)(2,1)} %collective-permute-done.1.refs_1_, bf16[3,256,256]{2,1,0:T(8,128)(2,1)} %collective-permute-done.2.refs_2_, ...), custom_call_target="tpu_custom_call" | custom-call | flops 1 | tf_op jit(solution)/shard_map/attend/pallas_call | solution.py:421
  85.6 0.1 collective-permute-start.8
  85.7 3.0 %collective-permute-start.7 = (bf16[512,256]{1,0:T(8,128)(2,1)S(1)}, bf16[512,256]{1,0:T(8,128)(2,1)S(1)}, u32[]{:S(2)}, u32[]{:S(2)}) collective-permute-start(bf16[512,256]{1,0:T(8,128)(2,1)S(1)} %bitcast.10), channel_id=1, source_target_pairs={{0,4},{4,0},{8,12},{12,8},{1,5},{5,1},{9,13},{13,9},{2,6},{6,2},{1... | collective-permute-start | bytes 786440 | tf_op jit(solution)/shard_map/ppermute | solution.py:50
  88.7 3.5 %attend.3 = bf16[4,128,256]{2,1,0:T(8,128)(2,1)S(1)} custom-call(s32[6]{0:T(128)S(1)} %stack.31.where_ref, bf16[3,256,256]{2,1,0:T(8,128)(2,1)S(1)} %own.1.refs_0_, bf16[3,256,256]{2,1,0:T(8,128)(2,1)} %collective-permute-done.1.refs_1_, bf16[3,256,256]{2,1,0:T(8,128)(2,1)} %collective-permute-done.2.refs_2_, ...), custom_call_target="tpu_custom_call" | custom-call | flops 1 | tf_op jit(solution)/shard_map/attend/pallas_call | solution.py:421
  92.3 0.6 collective-permute-start.4
  92.9 1.5 %products.2.refs_4_ = f32[512,1280]{1,0:T(8,128)S(1)} custom-call(s32[6]{0:T(128)S(1)} %stack.31.where_ref, bf16[512,256]{1,0:T(8,128)(2,1)S(1)} %bitcast.11, bf16[1024,1280]{1,0:T(8,128)(2,1)S(1)} %copy-done), custom_call_target="tpu_custom_call" | custom-call | flops 6000000000 | tf_op jit(solution)/shard_map/products/pallas_call | solution.py:446
  94.5 4.3 %collective-permute-done.4.refs_2_ = bf16[512,256]{1,0:T(8,128)(2,1)S(1)} collective-permute-done((bf16[512,256]{1,0:T(8,128)(2,1)S(1)}, bf16[512,256]{1,0:T(8,128)(2,1)S(1)}, u32[]{:S(2)}, u32[]{:S(2)}) %collective-permute-start.4) | collective-permute-done | bytes 262176 | tf_op jit(solution)/shard_map/ppermute | solution.py:50
  98.7 0.6 collective-permute-start.6
  99.3 1.7 %collective-permute-start.5 = (bf16[512,256]{1,0:T(8,128)(2,1)S(1)}, bf16[512,256]{1,0:T(8,128)(2,1)S(1)}, u32[]{:S(2)}, u32[]{:S(2)}) collective-permute-start(bf16[512,256]{1,0:T(8,128)(2,1)S(1)} %collective-permute-done.4.refs_2_), channel_id=1, source_target_pairs={{0,4},{4,0},{8,12},{12,8},{1,5},{5,1},{9,13},{13,9},{2,6},{6,2},{1... | collective-permute-start | bytes 786440 | tf_op jit(solution)/shard_map/ppermute | solution.py:50
  101.0 0.7 collective-permute-start.12
  101.7 1.3 collective-permute-start.13
  103.0 2.2 %products.3.refs_5_ = f32[512,1280]{1,0:T(8,128)S(1)} custom-call(s32[6]{0:T(128)S(1)} %stack.31.where_ref, bf16[512,256]{1,0:T(8,128)(2,1)S(1)} %collective-permute-done.8.refs_0_, bf16[512,256]{1,0:T(8,128)(2,1)S(1)} %collective-permute-done.7.refs_1_, bf16[1024,1280]{1,0:T(8,128)(2,1)S(1)} %copy-done, bf16[1024,1280]{1,0:T(8,128)(2,1)S(1)} %copy-done, ...), custom_call_target="tpu_custom_call" | custom-call | flops 1 | tf_op jit(solution)/shard_map/products/pallas_call | solution.py:446
  105.3 6.3 %collective-permute-done.6.refs_3_ = bf16[512,256]{1,0:T(8,128)(2,1)S(1)} collective-permute-done((bf16[512,256]{1,0:T(8,128)(2,1)S(1)}, bf16[512,256]{1,0:T(8,128)(2,1)S(1)}, u32[]{:S(2)}, u32[]{:S(2)}) %collective-permute-start.6) | collective-permute-done | bytes 262176 | tf_op jit(solution)/shard_map/ppermute | solution.py:50
  111.6 1.1 collective-permute-done.5.refs_4_
  112.7 0.7 collective-permute-start.9
  113.4 1.3 collective-permute-start.10
  114.7 2.7 %collective-permute-done.13.refs_1_ = bf16[512,256]{1,0:T(8,128)(2,1)S(1)} collective-permute-done((bf16[512,256]{1,0:T(8,128)(2,1)S(1)}, bf16[512,256]{1,0:T(8,128)(2,1)S(1)}, u32[]{:S(2)}, u32[]{:S(2)}) %collective-permute-start.13) | collective-permute-done | bytes 262176 | tf_op jit(solution)/shard_map/ppermute | solution.py:585
  117.4 4.0 %first.1.acc_in = f32[512,1280]{1,0:T(8,128)S(1)} custom-call(s32[6]{0:T(128)S(1)} %stack.31.where_ref, bf16[512,256]{1,0:T(8,128)(2,1)S(1)} %collective-permute-done.12.refs_0_, bf16[512,256]{1,0:T(8,128)(2,1)S(1)} %collective-permute-done.13.refs_1_, bf16[512,256]{1,0:T(8,128)(2,1)S(1)} %collective-permute-done.4.refs_2_, ...), custom_call_target="tpu_custom_call" | custom-call | flops 1 | tf_op jit(solution)/shard_map/first/pallas_call | solution.py:494
  121.4 0.4 collective-permute-done.10.more
  121.8 1.1 second.3
  122.9 0.0 copy-start.4
  122.9 0.0 copy-start.5
  122.9 0.1 collective-permute-start.18
  123.0 1.1 second.2
  124.1 0.6 collective-permute-start.14
  124.7 0.6 add.8
  125.3 2.2 %collective-permute-start.19 = (bf16[64,640]{1,0:T(8,128)(2,1)S(1)}, bf16[64,640]{1,0:T(8,128)(2,1)S(1)}, u32[]{:S(2)}, u32[]{:S(2)}) collective-permute-start(bf16[64,640]{1,0:T(8,128)(2,1)S(1)} %get-tuple-element.66), channel_id=1, source_target_pairs={{0,12},{4,8},{8,4},{12,0},{1,13},{5,9},{9,5},{13,1},{2,14},{6,10},... | collective-permute-start | bytes 245768 | tf_op jit(solution)/shard_map/ppermute | solution.py:50
  127.5 2.2 %collective-permute-start.21 = (bf16[64,640]{1,0:T(8,128)(2,1)S(1)}, bf16[64,640]{1,0:T(8,128)(2,1)S(1)}, u32[]{:S(2)}, u32[]{:S(2)}) collective-permute-start(bf16[64,640]{1,0:T(8,128)(2,1)S(1)} %get-tuple-element.68), channel_id=1, source_target_pairs={{0,4},{4,0},{8,12},{12,8},{1,5},{5,1},{9,13},{13,9},{2,6},{6,2},{1... | collective-permute-start | bytes 245768 | tf_op jit(solution)/shard_map/ppermute | solution.py:50
  129.8 0.6 add.7
  130.4 2.2 %collective-permute-start.15 = (bf16[64,640]{1,0:T(8,128)(2,1)S(1)}, bf16[64,640]{1,0:T(8,128)(2,1)S(1)}, u32[]{:S(2)}, u32[]{:S(2)}) collective-permute-start(bf16[64,640]{1,0:T(8,128)(2,1)S(1)} %get-tuple-element.60), channel_id=1, source_target_pairs={{0,12},{4,8},{8,4},{12,0},{1,13},{5,9},{9,5},{13,1},{2,14},{6,10},... | collective-permute-start | bytes 245768 | tf_op jit(solution)/shard_map/ppermute | solution.py:50
  132.6 2.2 %collective-permute-start.17 = (bf16[64,640]{1,0:T(8,128)(2,1)S(1)}, bf16[64,640]{1,0:T(8,128)(2,1)S(1)}, u32[]{:S(2)}, u32[]{:S(2)}) collective-permute-start(bf16[64,640]{1,0:T(8,128)(2,1)S(1)} %get-tuple-element.62), channel_id=1, source_target_pairs={{0,4},{4,0},{8,12},{12,8},{1,5},{5,1},{9,13},{13,9},{2,6},{6,2},{1... | collective-permute-start | bytes 245768 | tf_op jit(solution)/shard_map/ppermute | solution.py:50
  134.8 3.1 %collective-permute-done.20.refs_6_ = bf16[64,640]{1,0:T(8,128)(2,1)S(1)} collective-permute-done((bf16[64,640]{1,0:T(8,128)(2,1)S(1)}, bf16[64,640]{1,0:T(8,128)(2,1)S(1)}, u32[]{:S(2)}, u32[]{:S(2)}) %collective-permute-start.20) | collective-permute-done | bytes 81952 | tf_op jit(solution)/shard_map/ppermute | solution.py:50
  137.9 4.2 %collective-permute-done.16.refs_2_ = bf16[64,640]{1,0:T(8,128)(2,1)S(1)} collective-permute-done((bf16[64,640]{1,0:T(8,128)(2,1)S(1)}, bf16[64,640]{1,0:T(8,128)(2,1)S(1)}, u32[]{:S(2)}, u32[]{:S(2)}) %collective-permute-start.16) | collective-permute-done | bytes 81952 | tf_op jit(solution)/shard_map/ppermute | solution.py:50
  142.1 1.6 %mix.1 = bf16[64,5120]{1,0:T(8,128)(2,1)} custom-call(s32[6]{0:T(128)S(1)} %stack.31.where_ref, bf16[64,5120]{1,0:T(8,128)(2,1)S(1)} %copy-done.4, f32[1,5120]{1,0:T(1,128)S(1)} %bitcast.14, bf16[64,640]{1,0:T(8,128)(2,1)S(1)} %get-tuple-element.59.refs_0_, bf16[64,640]{1,0:T(8,128)(2,1)S(1)} %collective-permute-done.15.refs_1_, ...), custom_call_target="tpu_custom_call" | custom-call | flops 1 | tf_op jit(solution)/shard_map/mix/pallas_call | solution.py:614
  (23 shorter events, 0.1 us)
Async XLA Ops:
  0.0 49.4 %copy-start.6 = (s32[2,2,8]{2,1,0:T(2,128)S(1)}, s32[2,2,8]{2,1,0:T(2,128)}, u32[]{:S(2)}) copy-start(s32[2,2,8]{2,1,0:T(2,128)} %exps_ref.3) | copy-start | bytes 388
  0.0 49.4 %copy-start.2 = (bf16[2,256,1024]{2,1,0:T(8,128)(2,1)S(1)}, bf16[2,256,1024]{2,1,0:T(8,128)(2,1)}, u32[]{:S(2)}) copy-start(bf16[2,256,1024]{2,1,0:T(8,128)(2,1)} %fresh_ref.3) | copy-start | bytes 3145732
  0.0 49.4 %copy-start.3 = (bf16[256,1024]{1,0:T(8,128)(2,1)S(1)}, bf16[256,1024]{1,0:T(8,128)(2,1)}, u32[]{:S(2)}) copy-start(bf16[256,1024]{1,0:T(8,128)(2,1)} %q_ref.3) | copy-start | bytes 1572868
  41.9 32.0 %collective-permute-start = (bf16[512,1280]{1,0:T(8,128)(2,1)}, bf16[512,1280]{1,0:T(8,128)(2,1)S(1)}, u32[]{:S(2)}, u32[]{:S(2)}) collective-permute-start(bf16[512,1280]{1,0:T(8,128)(2,1)} %get-tuple-element.41), channel_id=1, source_target_pairs={{0,2},{2,0},{1,3},{3,1},{4,6},{6,4},{5,7},{7,5},{8,10},{10,8},{9,1... | collective-permute-start | bytes 3932168 | tf_op jit(solution)/shard_map/ppermute | solution.py:50
  44.9 30.8 %collective-permute-start.3 = (bf16[3,256,256]{2,1,0:T(8,128)(2,1)}, bf16[3,256,256]{2,1,0:T(8,128)(2,1)S(1)}, u32[]{:S(2)}, u32[]{:S(2)}) collective-permute-start(bf16[3,256,256]{2,1,0:T(8,128)(2,1)} %get-tuple-element.37), channel_id=1, source_target_pairs={{0,12},{4,8},{8,4},{12,0},{1,13},{5,9},{9,5},{13,1},{2,14},{6,10},... | collective-permute-start | bytes 1179656 | tf_op jit(solution)/shard_map/ppermute | solution.py:50
  48.5 33.6 %collective-permute-start.2 = (bf16[3,256,256]{2,1,0:T(8,128)(2,1)}, bf16[3,256,256]{2,1,0:T(8,128)(2,1)}, u32[]{:S(2)}, u32[]{:S(2)}) collective-permute-start(bf16[3,256,256]{2,1,0:T(8,128)(2,1)} %get-tuple-element.38), channel_id=1, source_target_pairs={{0,8},{4,12},{8,0},{12,4},{1,9},{5,13},{9,1},{13,5},{2,10},{6,14},... | collective-permute-start | bytes 1179656 | tf_op jit(solution)/shard_map/ppermute | solution.py:50
  48.5 33.6 %collective-permute-start.1 = (bf16[3,256,256]{2,1,0:T(8,128)(2,1)}, bf16[3,256,256]{2,1,0:T(8,128)(2,1)}, u32[]{:S(2)}, u32[]{:S(2)}) collective-permute-start(bf16[3,256,256]{2,1,0:T(8,128)(2,1)} %get-tuple-element.39), channel_id=1, source_target_pairs={{0,4},{4,0},{8,12},{12,8},{1,5},{5,1},{9,13},{13,9},{2,6},{6,2},{1... | collective-permute-start | bytes 1179656 | tf_op jit(solution)/shard_map/ppermute | solution.py:50
  49.4 2.2 %copy-start.1 = (bf16[2,1024,1024]{2,1,0:T(8,128)(2,1)S(1)}, bf16[2,1024,1024]{2,1,0:T(8,128)(2,1)}, u32[]{:S(2)}) copy-start(bf16[2,1024,1024]{2,1,0:T(8,128)(2,1)} %cached_ref.3) | copy-start | bytes 12582916
  52.9 40.0 %copy-start = (bf16[1024,1280]{1,0:T(8,128)(2,1)S(1)}, bf16[1024,1280]{1,0:T(8,128)(2,1)}, u32[]{:S(2)}) copy-start(bf16[1024,1280]{1,0:T(8,128)(2,1)} %refs_6_.1) | copy-start | bytes 7864324
  73.9 43.5 %collective-permute-start.11 = (bf16[512,1280]{1,0:T(8,128)(2,1)S(1)}, bf16[512,1280]{1,0:T(8,128)(2,1)S(1)}, u32[]{:S(2)}, u32[]{:S(2)}) collective-permute-start(bf16[512,1280]{1,0:T(8,128)(2,1)S(1)} %collective-permute-done.refs_7_.fetched_ref), channel_id=1, source_target_pairs={{0,16},{16,0},{1,17},{17,1},{2,18},{18,2},{3,19},{19,3},{4,20},{20... | collective-permute-start | bytes 3932168 | tf_op jit(solution)/shard_map/ppermute | solution.py:50
  85.6 15.4 %collective-permute-start.8 = (bf16[512,256]{1,0:T(8,128)(2,1)S(1)}, bf16[512,256]{1,0:T(8,128)(2,1)S(1)}, u32[]{:S(2)}, u32[]{:S(2)}) collective-permute-start(bf16[512,256]{1,0:T(8,128)(2,1)S(1)} %bitcast.9), channel_id=1, source_target_pairs={{0,8},{4,12},{8,0},{12,4},{1,9},{5,13},{9,1},{13,5},{2,10},{6,14},... | collective-permute-start | bytes 786440 | tf_op jit(solution)/shard_map/ppermute | solution.py:50
  85.7 15.3 %collective-permute-start.7 = (bf16[512,256]{1,0:T(8,128)(2,1)S(1)}, bf16[512,256]{1,0:T(8,128)(2,1)S(1)}, u32[]{:S(2)}, u32[]{:S(2)}) collective-permute-start(bf16[512,256]{1,0:T(8,128)(2,1)S(1)} %bitcast.10), channel_id=1, source_target_pairs={{0,4},{4,0},{8,12},{12,8},{1,5},{5,1},{9,13},{13,9},{2,6},{6,2},{1... | collective-permute-start | bytes 786440 | tf_op jit(solution)/shard_map/ppermute | solution.py:50
  92.3 6.4 %collective-permute-start.4 = (bf16[512,256]{1,0:T(8,128)(2,1)S(1)}, bf16[512,256]{1,0:T(8,128)(2,1)S(1)}, u32[]{:S(2)}, u32[]{:S(2)}) collective-permute-start(bf16[512,256]{1,0:T(8,128)(2,1)S(1)} %bitcast.13), channel_id=1, source_target_pairs={{0,2},{2,0},{1,3},{3,1},{4,6},{6,4},{5,7},{7,5},{8,10},{10,8},{9,1... | collective-permute-start | bytes 786440 | tf_op jit(solution)/shard_map/ppermute | solution.py:50
  98.7 12.8 %collective-permute-start.6 = (bf16[512,256]{1,0:T(8,128)(2,1)S(1)}, bf16[512,256]{1,0:T(8,128)(2,1)S(1)}, u32[]{:S(2)}, u32[]{:S(2)}) collective-permute-start(bf16[512,256]{1,0:T(8,128)(2,1)S(1)} %collective-permute-done.4.refs_2_), channel_id=1, source_target_pairs={{0,8},{4,12},{8,0},{12,4},{1,9},{5,13},{9,1},{13,5},{2,10},{6,14},... | collective-permute-start | bytes 786440 | tf_op jit(solution)/shard_map/ppermute | solution.py:50
  99.3 13.4 %collective-permute-start.5 = (bf16[512,256]{1,0:T(8,128)(2,1)S(1)}, bf16[512,256]{1,0:T(8,128)(2,1)S(1)}, u32[]{:S(2)}, u32[]{:S(2)}) collective-permute-start(bf16[512,256]{1,0:T(8,128)(2,1)S(1)} %collective-permute-done.4.refs_2_), channel_id=1, source_target_pairs={{0,4},{4,0},{8,12},{12,8},{1,5},{5,1},{9,13},{13,9},{2,6},{6,2},{1... | collective-permute-start | bytes 786440 | tf_op jit(solution)/shard_map/ppermute | solution.py:50
  101.0 13.6 %collective-permute-start.12 = (bf16[512,256]{1,0:T(8,128)(2,1)S(1)}, bf16[512,256]{1,0:T(8,128)(2,1)S(1)}, u32[]{:S(2)}, u32[]{:S(2)}) collective-permute-start(bf16[512,256]{1,0:T(8,128)(2,1)S(1)} %bitcast.12), channel_id=1, source_target_pairs={{4,8},{8,4},{5,9},{9,5},{6,10},{10,6},{7,11},{11,7},{20,24},{24,20... | collective-permute-start | bytes 786440 | tf_op jit(solution)/shard_map/ppermute | solution.py:50
  101.7 15.7 %collective-permute-start.13 = (bf16[512,256]{1,0:T(8,128)(2,1)S(1)}, bf16[512,256]{1,0:T(8,128)(2,1)S(1)}, u32[]{:S(2)}, u32[]{:S(2)}) collective-permute-start(bf16[512,256]{1,0:T(8,128)(2,1)S(1)} %collective-permute-done.8.refs_0_), channel_id=1, source_target_pairs={{4,0},{8,12},{5,1},{9,13},{6,2},{10,14},{7,3},{11,15},{20,16},{24,... | collective-permute-start | bytes 786440 | tf_op jit(solution)/shard_map/ppermute | solution.py:585
  112.7 8.7 %collective-permute-start.9 = (bf16[512,256]{1,0:T(8,128)(2,1)S(1)}, bf16[512,256]{1,0:T(8,128)(2,1)S(1)}, u32[]{:S(2)}, u32[]{:S(2)}) collective-permute-start(bf16[512,256]{1,0:T(8,128)(2,1)S(1)} %collective-permute-done.4.refs_2_), channel_id=1, source_target_pairs={{4,8},{8,4},{5,9},{9,5},{6,10},{10,6},{7,11},{11,7},{20,24},{24,20... | collective-permute-start | bytes 786440 | tf_op jit(solution)/shard_map/ppermute | solution.py:50
  113.4 8.4 %collective-permute-start.10 = (bf16[512,256]{1,0:T(8,128)(2,1)S(1)}, bf16[512,256]{1,0:T(8,128)(2,1)S(1)}, u32[]{:S(2)}, u32[]{:S(2)}) collective-permute-start(bf16[512,256]{1,0:T(8,128)(2,1)S(1)} %collective-permute-done.6.refs_3_), channel_id=1, source_target_pairs={{4,0},{8,12},{5,1},{9,13},{6,2},{10,14},{7,3},{11,15},{20,16},{24,... | collective-permute-start | bytes 786440 | tf_op jit(solution)/shard_map/ppermute | solution.py:585
  122.9 19.2 %copy-start.4 = (bf16[64,5120]{1,0:T(8,128)(2,1)S(1)}, bf16[64,5120]{1,0:T(8,128)(2,1)}, u32[]{:S(2)}) copy-start(bf16[64,5120]{1,0:T(8,128)(2,1)} %hidden_ref.1) | copy-start | bytes 1966084
  122.9 19.2 %copy-start.5 = (f32[5120]{0:T(1024)S(1)}, f32[5120]{0:T(1024)}, u32[]{:S(2)}) copy-start(f32[5120]{0:T(1024)} %param.13) | copy-start | bytes 61444
  122.9 1.7 %collective-permute-start.18 = (bf16[4,64,640]{2,1,0:T(8,128)(2,1)S(1)}, bf16[4,64,640]{2,1,0:T(8,128)(2,1)S(1)}, u32[]{:S(2)}, u32[]{:S(2)}) collective-permute-start(bf16[4,64,640]{2,1,0:T(8,128)(2,1)S(1)} %get-tuple-element.64), channel_id=1, source_target_pairs={{0,1},{1,0},{2,3},{3,2},{4,5},{5,4},{6,7},{7,6},{8,9},{9,8},{10,11... | collective-permute-start | bytes 983048 | tf_op jit(solution)/shard_map/ppermute | solution.py:50
  124.1 5.6 %collective-permute-start.14 = (bf16[4,64,640]{2,1,0:T(8,128)(2,1)S(1)}, bf16[4,64,640]{2,1,0:T(8,128)(2,1)S(1)}, u32[]{:S(2)}, u32[]{:S(2)}) collective-permute-start(bf16[4,64,640]{2,1,0:T(8,128)(2,1)S(1)} %get-tuple-element.58), channel_id=1, source_target_pairs={{0,1},{1,0},{2,3},{3,2},{4,5},{5,4},{6,7},{7,6},{8,9},{9,8},{10,11... | collective-permute-start | bytes 983048 | tf_op jit(solution)/shard_map/ppermute | solution.py:50
  125.3 7.3 %collective-permute-start.19 = (bf16[64,640]{1,0:T(8,128)(2,1)S(1)}, bf16[64,640]{1,0:T(8,128)(2,1)S(1)}, u32[]{:S(2)}, u32[]{:S(2)}) collective-permute-start(bf16[64,640]{1,0:T(8,128)(2,1)S(1)} %get-tuple-element.66), channel_id=1, source_target_pairs={{0,12},{4,8},{8,4},{12,0},{1,13},{5,9},{9,5},{13,1},{2,14},{6,10},... | collective-permute-start | bytes 245768 | tf_op jit(solution)/shard_map/ppermute | solution.py:50
  127.5 10.4 %collective-permute-start.20 = (bf16[64,640]{1,0:T(8,128)(2,1)S(1)}, bf16[64,640]{1,0:T(8,128)(2,1)S(1)}, u32[]{:S(2)}, u32[]{:S(2)}) collective-permute-start(bf16[64,640]{1,0:T(8,128)(2,1)S(1)} %get-tuple-element.67), channel_id=1, source_target_pairs={{0,8},{4,12},{8,0},{12,4},{1,9},{5,13},{9,1},{13,5},{2,10},{6,14},... | collective-permute-start | bytes 245768 | tf_op jit(solution)/shard_map/ppermute | solution.py:50
  127.5 10.4 %collective-permute-start.21 = (bf16[64,640]{1,0:T(8,128)(2,1)S(1)}, bf16[64,640]{1,0:T(8,128)(2,1)S(1)}, u32[]{:S(2)}, u32[]{:S(2)}) collective-permute-start(bf16[64,640]{1,0:T(8,128)(2,1)S(1)} %get-tuple-element.68), channel_id=1, source_target_pairs={{0,4},{4,0},{8,12},{12,8},{1,5},{5,1},{9,13},{13,9},{2,6},{6,2},{1... | collective-permute-start | bytes 245768 | tf_op jit(solution)/shard_map/ppermute | solution.py:50
  130.4 7.5 %collective-permute-start.15 = (bf16[64,640]{1,0:T(8,128)(2,1)S(1)}, bf16[64,640]{1,0:T(8,128)(2,1)S(1)}, u32[]{:S(2)}, u32[]{:S(2)}) collective-permute-start(bf16[64,640]{1,0:T(8,128)(2,1)S(1)} %get-tuple-element.60), channel_id=1, source_target_pairs={{0,12},{4,8},{8,4},{12,0},{1,13},{5,9},{9,5},{13,1},{2,14},{6,10},... | collective-permute-start | bytes 245768 | tf_op jit(solution)/shard_map/ppermute | solution.py:50
  132.6 9.5 %collective-permute-start.16 = (bf16[64,640]{1,0:T(8,128)(2,1)S(1)}, bf16[64,640]{1,0:T(8,128)(2,1)S(1)}, u32[]{:S(2)}, u32[]{:S(2)}) collective-permute-start(bf16[64,640]{1,0:T(8,128)(2,1)S(1)} %get-tuple-element.61), channel_id=1, source_target_pairs={{0,8},{4,12},{8,0},{12,4},{1,9},{5,13},{9,1},{13,5},{2,10},{6,14},... | collective-permute-start | bytes 245768 | tf_op jit(solution)/shard_map/ppermute | solution.py:50
  132.6 9.5 %collective-permute-start.17 = (bf16[64,640]{1,0:T(8,128)(2,1)S(1)}, bf16[64,640]{1,0:T(8,128)(2,1)S(1)}, u32[]{:S(2)}, u32[]{:S(2)}) collective-permute-start(bf16[64,640]{1,0:T(8,128)(2,1)S(1)} %get-tuple-element.62), channel_id=1, source_target_pairs={{0,4},{4,0},{8,12},{12,8},{1,5},{5,1},{9,13},{13,9},{2,6},{6,2},{1... | collective-permute-start | bytes 245768 | tf_op jit(solution)/shard_map/ppermute | solution.py:50

commit v20 on v19

--- a/solution.py
+++ b/solution.py
@@ -64,13 +64,14 @@
 
 def pack_kernel(split, per, shares, exps_ref, q_ref, fresh_ref, cached_ref, weight_ref, *refs):
     outs, part_ref, bufs = refs[: split - 1], refs[split - 1], refs[split : 2 * split - 1]
-    q_buf, fresh_buf, cached_buf, sems, out_sems, part_sem = refs[2 * split - 1 :]
+    q_buf, fresh_buf, cached_buf, part_buf, sems, out_sems, part_sems = refs[2 * split - 1 :]
     patch = lax.axis_index("patch")
     count = part_ref.shape[0]
     start = lax.axis_index("grp") * count if shares == 2 else 0
-    part = pltpu.make_async_copy(
-        weight_ref.at[pl.ds(pl.multiple_of(start, HEAD_DIM), count)], part_ref, part_sem
+    part_in = pltpu.make_async_copy(
+        weight_ref.at[pl.ds(pl.multiple_of(start, HEAD_DIM), count)], part_buf, part_sems.at[0]
     )
+    part_out = pltpu.make_async_copy(part_buf, part_ref, part_sems.at[1])
     near = lax.rem(patch, split)
     tok = q_buf.shape[0]
     copies, sent = [], []
@@ -86,7 +87,7 @@
         )
         for copy in copies[-1]:
             copy.start()
-    part.start()
+    part_in.start()
     for block in range(tok // PACK_ROWS):
         rows = pl.ds(block * PACK_ROWS, PACK_ROWS)
         for copy in copies[block]:
@@ -112,9 +113,12 @@
                 )
             )
             sent[-1].start()
+        if block == tok // PACK_ROWS - 2:
+            part_in.wait()
+            part_out.start()
     for copy in sent:
         copy.wait()
-    part.wait()
+    part_out.wait()
 
 
 def pack(split, shares, exponents, queries, fresh_kv, cached_kv, weight):
@@ -133,9 +137,10 @@
             pltpu.VMEM((tok, channels), jnp.bfloat16),
             pltpu.VMEM((2, tok, channels), jnp.bfloat16),
             pltpu.VMEM((2, tok, channels), jnp.bfloat16),
+            pltpu.VMEM((weight.shape[0] // shares, weight.shape[1]), weight.dtype),
             pltpu.SemaphoreType.DMA((blocks, 3)),
             pltpu.SemaphoreType.DMA((blocks, split - 1)),
-            pltpu.SemaphoreType.DMA,
+            pltpu.SemaphoreType.DMA((2,)),
         ],
         compiler_params=pltpu.CompilerParams(vmem_limit_bytes=PACK_VMEM_BYTES),
         name="pack",

time: 144 us -> 106 us (0.74)
  Pallas kernels: 63 us -> 25.5 us
    pallas_call x1, Pallas kernels: 41.9 us -> 4.37 us  [pack(): pl.pallas_call(functools.partial(pack_kernel, split, feat // HEAD_DIM, sh...]
  transfers between devices with their start and end apart: 22 -> 22, of which waited for: 9 -> 9; matrix products, arithmetic and copies ran while one was open for 0% -> 0% of each run, Pallas kernels for 13% -> 17%
where the time goes in v20:
time: 106 us
  waiting for transfers between devices  49.6 us (47%)
  starting transfers between devices  28.6 us (27%)
  Pallas kernels  25.5 us (24%)
  local copies, waits for them, and re-layouts  2.3 us (2%)
    ppermute x20, waiting for transfers between devices, swap(): return lax.ppermute(x, axes, pairs)  46.5 us
    ppermute x20, starting transfers between devices, swap(): return lax.ppermute(x, axes, pairs)  26 us
    pallas_call x2, Pallas kernels, attend_half(): call(functools.partial(attend_half_kernel, half), 'attend', out, 1, [spec...  7.09 us
    pallas_call x1, Pallas kernels, pack(): pl.pallas_call(functools.partial(pack_kernel, split, feat // HEAD_DIM, sh...  4.37 us
    pallas_call x1, Pallas kernels, first_product(): call(first_kernel, 'first', jax.ShapeDtypeStruct(acc.shape, jnp.float32),...  3.96 us
    pallas_call x2, Pallas kernels, add_product(): call(functools.partial(add_product_kernel, len(rels)), 'products', jax.Sh...  3.79 us
    ppermute x2, waiting for transfers between devices, share_tail(): ends = lax.ppermute(far, 'patch', [(1, 0), (2, 3)])  3.09 us
    ppermute x2, starting transfers between devices, share_tail(): ends = lax.ppermute(far, 'patch', [(1, 0), (2, 3)])  2.58 us
  transfers between devices with their start and end apart: 22, of which 9 were waited for; matrix products, arithmetic and copies ran while one was open for 0% of the time, Pallas kernels for 17%

profile of v20, /device:TPU:0, one launch (start us, length us, event | category | flops | bytes accessed | tf_op | source)
XLA Modules:
  0.0 106.2 jit_solution(13354702753057788463)
XLA Ops:
  0.0 4.4 %pack.1 = (bf16[3,256,256]{2,1,0:T(8,128)(2,1)}, bf16[3,256,256]{2,1,0:T(8,128)(2,1)}, bf16[3,256,256]{2,1,0:T(8,128)(2,1)}, bf16[512,1280]{1,0:T(8,128)(2,1)}) custom-call(s32[2,2,8]{2,1,0:T(2,128)} %exps_ref.3, bf16[256,1024]{1,0:T(8,128)(2,1)} %q_ref.3, bf16[2,256,1024]{2,1,0:T(8,128)(2,1)} %fresh_ref.3, bf16[2,1024,1024]{2,1,0:T(8,128)(2,1)} %cached_ref.3, ...), custom_call_target="tpu_custom_call" | custom-call | tf_op jit(solution)/shard_map/pack/pallas_call | solution.py:129
  4.4 3.0 %collective-permute-start = (bf16[512,1280]{1,0:T(8,128)(2,1)}, bf16[512,1280]{1,0:T(8,128)(2,1)S(1)}, u32[]{:S(2)}, u32[]{:S(2)}) collective-permute-start(bf16[512,1280]{1,0:T(8,128)(2,1)} %get-tuple-element.41), channel_id=1, source_target_pairs={{0,2},{2,0},{1,3},{3,1},{4,6},{6,4},{5,7},{7,5},{8,10},{10,8},{9,1... | collective-permute-start | bytes 3932168 | tf_op jit(solution)/shard_map/ppermute | solution.py:50
  7.4 3.6 %collective-permute-start.3 = (bf16[3,256,256]{2,1,0:T(8,128)(2,1)}, bf16[3,256,256]{2,1,0:T(8,128)(2,1)S(1)}, u32[]{:S(2)}, u32[]{:S(2)}) collective-permute-start(bf16[3,256,256]{2,1,0:T(8,128)(2,1)} %get-tuple-element.37), channel_id=1, source_target_pairs={{0,12},{4,8},{8,4},{12,0},{1,13},{5,9},{9,5},{13,1},{2,14},{6,10},... | collective-permute-start | bytes 1179656 | tf_op jit(solution)/shard_map/ppermute | solution.py:50
  11.0 0.8 collective-permute-start.1
  11.8 0.1 stack.31.where_ref
  11.9 0.0 copy-start.1
  11.9 2.2 %copy-done.1 = bf16[2,1024,1024]{2,1,0:T(8,128)(2,1)S(1)} copy-done((bf16[2,1024,1024]{2,1,0:T(8,128)(2,1)S(1)}, bf16[2,1024,1024]{2,1,0:T(8,128)(2,1)}, u32[]{:S(2)}) %copy-start.1) | copy-done | bytes 4194328
  14.1 1.3 %own.1.refs_0_ = bf16[3,256,256]{2,1,0:T(8,128)(2,1)S(1)} custom-call(s32[6]{0:T(128)S(1)} %stack.31.where_ref, s32[2,2,8]{2,1,0:T(2,128)S(1)} %copy-done.6, bf16[256,1024]{1,0:T(8,128)(2,1)S(1)} %copy-done.3, bf16[2,256,1024]{2,1,0:T(8,128)(2,1)S(1)} %copy-done.2, bf16[2,1024,1024]{2,1,0:T(8,128)(2,1)S(1)} %copy-done.1), custom_call_target="tpu_custom_call" | custom-call | flops 1 | tf_op jit(solution)/shard_map/own/pallas_call | solution.py:168
  15.4 0.0 copy-start
  15.4 21.0 %collective-permute-done.refs_7_.fetched_ref = bf16[512,1280]{1,0:T(8,128)(2,1)S(1)} collective-permute-done((bf16[512,1280]{1,0:T(8,128)(2,1)}, bf16[512,1280]{1,0:T(8,128)(2,1)S(1)}, u32[]{:S(2)}, u32[]{:S(2)}) %collective-permute-start) | collective-permute-done | bytes 1310752 | tf_op jit(solution)/shard_map/ppermute | solution.py:50
  36.4 1.8 %collective-permute-start.11 = (bf16[512,1280]{1,0:T(8,128)(2,1)S(1)}, bf16[512,1280]{1,0:T(8,128)(2,1)S(1)}, u32[]{:S(2)}, u32[]{:S(2)}) collective-permute-start(bf16[512,1280]{1,0:T(8,128)(2,1)S(1)} %collective-permute-done.refs_7_.fetched_ref), channel_id=1, source_target_pairs={{0,16},{16,0},{1,17},{17,1},{2,18},{18,2},{3,19},{19,3},{4,20},{20... | collective-permute-start | bytes 3932168 | tf_op jit(solution)/shard_map/ppermute | solution.py:50
  38.2 0.0 collective-permute-done.3.refs_3_
  38.2 6.4 %collective-permute-done.2.refs_2_ = bf16[3,256,256]{2,1,0:T(8,128)(2,1)} collective-permute-done((bf16[3,256,256]{2,1,0:T(8,128)(2,1)}, bf16[3,256,256]{2,1,0:T(8,128)(2,1)}, u32[]{:S(2)}, u32[]{:S(2)}) %collective-permute-start.2) | collective-permute-done | bytes 393248 | tf_op jit(solution)/shard_map/ppermute | solution.py:50
  44.6 0.0 collective-permute-done.1.refs_1_
  44.6 3.5 %attend.2 = bf16[4,128,256]{2,1,0:T(8,128)(2,1)S(1)} custom-call(s32[6]{0:T(128)S(1)} %stack.31.where_ref, bf16[3,256,256]{2,1,0:T(8,128)(2,1)S(1)} %own.1.refs_0_, bf16[3,256,256]{2,1,0:T(8,128)(2,1)} %collective-permute-done.1.refs_1_, bf16[3,256,256]{2,1,0:T(8,128)(2,1)} %collective-permute-done.2.refs_2_, ...), custom_call_target="tpu_custom_call" | custom-call | flops 1 | tf_op jit(solution)/shard_map/attend/pallas_call | solution.py:426
  48.1 0.1 collective-permute-start.8
  48.2 3.0 %collective-permute-start.7 = (bf16[512,256]{1,0:T(8,128)(2,1)S(1)}, bf16[512,256]{1,0:T(8,128)(2,1)S(1)}, u32[]{:S(2)}, u32[]{:S(2)}) collective-permute-start(bf16[512,256]{1,0:T(8,128)(2,1)S(1)} %bitcast.10), channel_id=1, source_target_pairs={{0,4},{4,0},{8,12},{12,8},{1,5},{5,1},{9,13},{13,9},{2,6},{6,2},{1... | collective-permute-start | bytes 786440 | tf_op jit(solution)/shard_map/ppermute | solution.py:50
  51.2 3.5 %attend.3 = bf16[4,128,256]{2,1,0:T(8,128)(2,1)S(1)} custom-call(s32[6]{0:T(128)S(1)} %stack.31.where_ref, bf16[3,256,256]{2,1,0:T(8,128)(2,1)S(1)} %own.1.refs_0_, bf16[3,256,256]{2,1,0:T(8,128)(2,1)} %collective-permute-done.1.refs_1_, bf16[3,256,256]{2,1,0:T(8,128)(2,1)} %collective-permute-done.2.refs_2_, ...), custom_call_target="tpu_custom_call" | custom-call | flops 1 | tf_op jit(solution)/shard_map/attend/pallas_call | solution.py:426
  54.8 0.6 collective-permute-start.4
  55.4 1.5 %products.2.refs_4_ = f32[512,1280]{1,0:T(8,128)S(1)} custom-call(s32[6]{0:T(128)S(1)} %stack.31.where_ref, bf16[512,256]{1,0:T(8,128)(2,1)S(1)} %bitcast.11, bf16[1024,1280]{1,0:T(8,128)(2,1)S(1)} %copy-done), custom_call_target="tpu_custom_call" | custom-call | flops 6000000000 | tf_op jit(solution)/shard_map/products/pallas_call | solution.py:451
  56.9 4.3 %collective-permute-done.4.refs_2_ = bf16[512,256]{1,0:T(8,128)(2,1)S(1)} collective-permute-done((bf16[512,256]{1,0:T(8,128)(2,1)S(1)}, bf16[512,256]{1,0:T(8,128)(2,1)S(1)}, u32[]{:S(2)}, u32[]{:S(2)}) %collective-permute-start.4) | collective-permute-done | bytes 262176 | tf_op jit(solution)/shard_map/ppermute | solution.py:50
  61.2 0.6 collective-permute-start.6
  61.8 1.7 %collective-permute-start.5 = (bf16[512,256]{1,0:T(8,128)(2,1)S(1)}, bf16[512,256]{1,0:T(8,128)(2,1)S(1)}, u32[]{:S(2)}, u32[]{:S(2)}) collective-permute-start(bf16[512,256]{1,0:T(8,128)(2,1)S(1)} %collective-permute-done.4.refs_2_), channel_id=1, source_target_pairs={{0,4},{4,0},{8,12},{12,8},{1,5},{5,1},{9,13},{13,9},{2,6},{6,2},{1... | collective-permute-start | bytes 786440 | tf_op jit(solution)/shard_map/ppermute | solution.py:50
  63.5 0.7 collective-permute-start.12
  64.2 1.3 %collective-permute-start.13 = (bf16[512,256]{1,0:T(8,128)(2,1)S(1)}, bf16[512,256]{1,0:T(8,128)(2,1)S(1)}, u32[]{:S(2)}, u32[]{:S(2)}) collective-permute-start(bf16[512,256]{1,0:T(8,128)(2,1)S(1)} %collective-permute-done.8.refs_0_), channel_id=1, source_target_pairs={{4,0},{8,12},{5,1},{9,13},{6,2},{10,14},{7,3},{11,15},{20,16},{24,... | collective-permute-start | bytes 786440 | tf_op jit(solution)/shard_map/ppermute | solution.py:590
  65.5 2.2 %products.3.refs_5_ = f32[512,1280]{1,0:T(8,128)S(1)} custom-call(s32[6]{0:T(128)S(1)} %stack.31.where_ref, bf16[512,256]{1,0:T(8,128)(2,1)S(1)} %collective-permute-done.8.refs_0_, bf16[512,256]{1,0:T(8,128)(2,1)S(1)} %collective-permute-done.7.refs_1_, bf16[1024,1280]{1,0:T(8,128)(2,1)S(1)} %copy-done, bf16[1024,1280]{1,0:T(8,128)(2,1)S(1)} %copy-done, ...), custom_call_target="tpu_custom_call" | custom-call | flops 1 | tf_op jit(solution)/shard_map/products/pallas_call | solution.py:451
  67.8 6.3 %collective-permute-done.6.refs_3_ = bf16[512,256]{1,0:T(8,128)(2,1)S(1)} collective-permute-done((bf16[512,256]{1,0:T(8,128)(2,1)S(1)}, bf16[512,256]{1,0:T(8,128)(2,1)S(1)}, u32[]{:S(2)}, u32[]{:S(2)}) %collective-permute-start.6) | collective-permute-done | bytes 262176 | tf_op jit(solution)/shard_map/ppermute | solution.py:50
  74.1 1.2 %collective-permute-done.5.refs_4_ = bf16[512,256]{1,0:T(8,128)(2,1)S(1)} collective-permute-done((bf16[512,256]{1,0:T(8,128)(2,1)S(1)}, bf16[512,256]{1,0:T(8,128)(2,1)S(1)}, u32[]{:S(2)}, u32[]{:S(2)}) %collective-permute-start.5) | collective-permute-done | bytes 262176 | tf_op jit(solution)/shard_map/ppermute | solution.py:50
  75.2 0.7 collective-permute-start.9
  75.9 1.3 %collective-permute-start.10 = (bf16[512,256]{1,0:T(8,128)(2,1)S(1)}, bf16[512,256]{1,0:T(8,128)(2,1)S(1)}, u32[]{:S(2)}, u32[]{:S(2)}) collective-permute-start(bf16[512,256]{1,0:T(8,128)(2,1)S(1)} %collective-permute-done.6.refs_3_), channel_id=1, source_target_pairs={{4,0},{8,12},{5,1},{9,13},{6,2},{10,14},{7,3},{11,15},{20,16},{24,... | collective-permute-start | bytes 786440 | tf_op jit(solution)/shard_map/ppermute | solution.py:590
  77.2 2.7 %collective-permute-done.13.refs_1_ = bf16[512,256]{1,0:T(8,128)(2,1)S(1)} collective-permute-done((bf16[512,256]{1,0:T(8,128)(2,1)S(1)}, bf16[512,256]{1,0:T(8,128)(2,1)S(1)}, u32[]{:S(2)}, u32[]{:S(2)}) %collective-permute-start.13) | collective-permute-done | bytes 262176 | tf_op jit(solution)/shard_map/ppermute | solution.py:590
  79.9 4.0 %first.1.acc_in = f32[512,1280]{1,0:T(8,128)S(1)} custom-call(s32[6]{0:T(128)S(1)} %stack.31.where_ref, bf16[512,256]{1,0:T(8,128)(2,1)S(1)} %collective-permute-done.12.refs_0_, bf16[512,256]{1,0:T(8,128)(2,1)S(1)} %collective-permute-done.13.refs_1_, bf16[512,256]{1,0:T(8,128)(2,1)S(1)} %collective-permute-done.4.refs_2_, ...), custom_call_target="tpu_custom_call" | custom-call | flops 1 | tf_op jit(solution)/shard_map/first/pallas_call | solution.py:499
  83.9 0.4 collective-permute-done.10.more
  84.3 1.1 %second.3 = (bf16[4,64,640]{2,1,0:T(8,128)(2,1)S(1)}, bf16[4,64,640]{2,1,0:T(8,128)(2,1)S(1)}) custom-call(s32[6]{0:T(128)S(1)} %stack.31.where_ref, bf16[512,256]{1,0:T(8,128)(2,1)S(1)} %collective-permute-done.9.slot, bf16[512,256]{1,0:T(8,128)(2,1)S(1)} %collective-permute-done.10.more, bf16[512,1280]{1,0:T(8,128)(2,1)S(1)} %collective-permute-done.refs_7_.fetched_ref, ...), custom_call_target="tpu_custom_call" | custom-call | flops 1 | tf_op jit(solution)/shard_map/second/pallas_call | solution.py:540
  85.4 0.0 copy-start.4
  85.4 0.0 copy-start.5
  85.4 0.1 collective-permute-start.18
  85.5 1.1 %second.2 = (bf16[4,64,640]{2,1,0:T(8,128)(2,1)S(1)}, bf16[4,64,640]{2,1,0:T(8,128)(2,1)S(1)}) custom-call(s32[6]{0:T(128)S(1)} %stack.31.where_ref, bf16[512,256]{1,0:T(8,128)(2,1)S(1)} %collective-permute-done.9.slot, bf16[512,256]{1,0:T(8,128)(2,1)S(1)} %collective-permute-done.10.more, bf16[512,1280]{1,0:T(8,128)(2,1)S(1)} %collective-permute-done.refs_7_.fetched_ref, ...), custom_call_target="tpu_custom_call" | custom-call | flops 1 | tf_op jit(solution)/shard_map/second/pallas_call | solution.py:540
  86.6 0.6 collective-permute-start.14
  87.2 0.6 add.8
  87.8 2.2 %collective-permute-start.19 = (bf16[64,640]{1,0:T(8,128)(2,1)S(1)}, bf16[64,640]{1,0:T(8,128)(2,1)S(1)}, u32[]{:S(2)}, u32[]{:S(2)}) collective-permute-start(bf16[64,640]{1,0:T(8,128)(2,1)S(1)} %get-tuple-element.66), channel_id=1, source_target_pairs={{0,12},{4,8},{8,4},{12,0},{1,13},{5,9},{9,5},{13,1},{2,14},{6,10},... | collective-permute-start | bytes 245768 | tf_op jit(solution)/shard_map/ppermute | solution.py:50
  90.0 2.2 %collective-permute-start.21 = (bf16[64,640]{1,0:T(8,128)(2,1)S(1)}, bf16[64,640]{1,0:T(8,128)(2,1)S(1)}, u32[]{:S(2)}, u32[]{:S(2)}) collective-permute-start(bf16[64,640]{1,0:T(8,128)(2,1)S(1)} %get-tuple-element.68), channel_id=1, source_target_pairs={{0,4},{4,0},{8,12},{12,8},{1,5},{5,1},{9,13},{13,9},{2,6},{6,2},{1... | collective-permute-start | bytes 245768 | tf_op jit(solution)/shard_map/ppermute | solution.py:50
  92.3 0.6 add.7
  92.9 2.2 %collective-permute-start.15 = (bf16[64,640]{1,0:T(8,128)(2,1)S(1)}, bf16[64,640]{1,0:T(8,128)(2,1)S(1)}, u32[]{:S(2)}, u32[]{:S(2)}) collective-permute-start(bf16[64,640]{1,0:T(8,128)(2,1)S(1)} %get-tuple-element.60), channel_id=1, source_target_pairs={{0,12},{4,8},{8,4},{12,0},{1,13},{5,9},{9,5},{13,1},{2,14},{6,10},... | collective-permute-start | bytes 245768 | tf_op jit(solution)/shard_map/ppermute | solution.py:50
  95.1 2.2 %collective-permute-start.17 = (bf16[64,640]{1,0:T(8,128)(2,1)S(1)}, bf16[64,640]{1,0:T(8,128)(2,1)S(1)}, u32[]{:S(2)}, u32[]{:S(2)}) collective-permute-start(bf16[64,640]{1,0:T(8,128)(2,1)S(1)} %get-tuple-element.62), channel_id=1, source_target_pairs={{0,4},{4,0},{8,12},{12,8},{1,5},{5,1},{9,13},{13,9},{2,6},{6,2},{1... | collective-permute-start | bytes 245768 | tf_op jit(solution)/shard_map/ppermute | solution.py:50
  97.3 3.1 %collective-permute-done.20.refs_6_ = bf16[64,640]{1,0:T(8,128)(2,1)S(1)} collective-permute-done((bf16[64,640]{1,0:T(8,128)(2,1)S(1)}, bf16[64,640]{1,0:T(8,128)(2,1)S(1)}, u32[]{:S(2)}, u32[]{:S(2)}) %collective-permute-start.20) | collective-permute-done | bytes 81952 | tf_op jit(solution)/shard_map/ppermute | solution.py:50
  100.4 4.2 %collective-permute-done.16.refs_2_ = bf16[64,640]{1,0:T(8,128)(2,1)S(1)} collective-permute-done((bf16[64,640]{1,0:T(8,128)(2,1)S(1)}, bf16[64,640]{1,0:T(8,128)(2,1)S(1)}, u32[]{:S(2)}, u32[]{:S(2)}) %collective-permute-start.16) | collective-permute-done | bytes 81952 | tf_op jit(solution)/shard_map/ppermute | solution.py:50
  104.6 1.6 %mix.1 = bf16[64,5120]{1,0:T(8,128)(2,1)} custom-call(s32[6]{0:T(128)S(1)} %stack.31.where_ref, bf16[64,5120]{1,0:T(8,128)(2,1)S(1)} %copy-done.4, f32[1,5120]{1,0:T(1,128)S(1)} %bitcast.14, bf16[64,640]{1,0:T(8,128)(2,1)S(1)} %get-tuple-element.59.refs_0_, bf16[64,640]{1,0:T(8,128)(2,1)S(1)} %collective-permute-done.15.refs_1_, ...), custom_call_target="tpu_custom_call" | custom-call | flops 1 | tf_op jit(solution)/shard_map/mix/pallas_call | solution.py:619
  (23 shorter events, 0.1 us)
Async XLA Ops:
  0.0 11.9 %copy-start.6 = (s32[2,2,8]{2,1,0:T(2,128)S(1)}, s32[2,2,8]{2,1,0:T(2,128)}, u32[]{:S(2)}) copy-start(s32[2,2,8]{2,1,0:T(2,128)} %exps_ref.3) | copy-start | bytes 388
  0.0 11.9 %copy-start.2 = (bf16[2,256,1024]{2,1,0:T(8,128)(2,1)S(1)}, bf16[2,256,1024]{2,1,0:T(8,128)(2,1)}, u32[]{:S(2)}) copy-start(bf16[2,256,1024]{2,1,0:T(8,128)(2,1)} %fresh_ref.3) | copy-start | bytes 3145732
  0.0 11.9 %copy-start.3 = (bf16[256,1024]{1,0:T(8,128)(2,1)S(1)}, bf16[256,1024]{1,0:T(8,128)(2,1)}, u32[]{:S(2)}) copy-start(bf16[256,1024]{1,0:T(8,128)(2,1)} %q_ref.3) | copy-start | bytes 1572868
  4.4 32.0 %collective-permute-start = (bf16[512,1280]{1,0:T(8,128)(2,1)}, bf16[512,1280]{1,0:T(8,128)(2,1)S(1)}, u32[]{:S(2)}, u32[]{:S(2)}) collective-permute-start(bf16[512,1280]{1,0:T(8,128)(2,1)} %get-tuple-element.41), channel_id=1, source_target_pairs={{0,2},{2,0},{1,3},{3,1},{4,6},{6,4},{5,7},{7,5},{8,10},{10,8},{9,1... | collective-permute-start | bytes 3932168 | tf_op jit(solution)/shard_map/ppermute | solution.py:50
  7.4 30.8 %collective-permute-start.3 = (bf16[3,256,256]{2,1,0:T(8,128)(2,1)}, bf16[3,256,256]{2,1,0:T(8,128)(2,1)S(1)}, u32[]{:S(2)}, u32[]{:S(2)}) collective-permute-start(bf16[3,256,256]{2,1,0:T(8,128)(2,1)} %get-tuple-element.37), channel_id=1, source_target_pairs={{0,12},{4,8},{8,4},{12,0},{1,13},{5,9},{9,5},{13,1},{2,14},{6,10},... | collective-permute-start | bytes 1179656 | tf_op jit(solution)/shard_map/ppermute | solution.py:50
  11.0 33.6 %collective-permute-start.2 = (bf16[3,256,256]{2,1,0:T(8,128)(2,1)}, bf16[3,256,256]{2,1,0:T(8,128)(2,1)}, u32[]{:S(2)}, u32[]{:S(2)}) collective-permute-start(bf16[3,256,256]{2,1,0:T(8,128)(2,1)} %get-tuple-element.38), channel_id=1, source_target_pairs={{0,8},{4,12},{8,0},{12,4},{1,9},{5,13},{9,1},{13,5},{2,10},{6,14},... | collective-permute-start | bytes 1179656 | tf_op jit(solution)/shard_map/ppermute | solution.py:50
  11.0 33.6 %collective-permute-start.1 = (bf16[3,256,256]{2,1,0:T(8,128)(2,1)}, bf16[3,256,256]{2,1,0:T(8,128)(2,1)}, u32[]{:S(2)}, u32[]{:S(2)}) collective-permute-start(bf16[3,256,256]{2,1,0:T(8,128)(2,1)} %get-tuple-element.39), channel_id=1, source_target_pairs={{0,4},{4,0},{8,12},{12,8},{1,5},{5,1},{9,13},{13,9},{2,6},{6,2},{1... | collective-permute-start | bytes 1179656 | tf_op jit(solution)/shard_map/ppermute | solution.py:50
  11.9 2.2 %copy-start.1 = (bf16[2,1024,1024]{2,1,0:T(8,128)(2,1)S(1)}, bf16[2,1024,1024]{2,1,0:T(8,128)(2,1)}, u32[]{:S(2)}) copy-start(bf16[2,1024,1024]{2,1,0:T(8,128)(2,1)} %cached_ref.3) | copy-start | bytes 12582916
  15.4 40.0 %copy-start = (bf16[1024,1280]{1,0:T(8,128)(2,1)S(1)}, bf16[1024,1280]{1,0:T(8,128)(2,1)}, u32[]{:S(2)}) copy-start(bf16[1024,1280]{1,0:T(8,128)(2,1)} %refs_6_.1) | copy-start | bytes 7864324
  36.4 43.5 %collective-permute-start.11 = (bf16[512,1280]{1,0:T(8,128)(2,1)S(1)}, bf16[512,1280]{1,0:T(8,128)(2,1)S(1)}, u32[]{:S(2)}, u32[]{:S(2)}) collective-permute-start(bf16[512,1280]{1,0:T(8,128)(2,1)S(1)} %collective-permute-done.refs_7_.fetched_ref), channel_id=1, source_target_pairs={{0,16},{16,0},{1,17},{17,1},{2,18},{18,2},{3,19},{19,3},{4,20},{20... | collective-permute-start | bytes 3932168 | tf_op jit(solution)/shard_map/ppermute | solution.py:50
  48.1 15.4 %collective-permute-start.8 = (bf16[512,256]{1,0:T(8,128)(2,1)S(1)}, bf16[512,256]{1,0:T(8,128)(2,1)S(1)}, u32[]{:S(2)}, u32[]{:S(2)}) collective-permute-start(bf16[512,256]{1,0:T(8,128)(2,1)S(1)} %bitcast.9), channel_id=1, source_target_pairs={{0,8},{4,12},{8,0},{12,4},{1,9},{5,13},{9,1},{13,5},{2,10},{6,14},... | collective-permute-start | bytes 786440 | tf_op jit(solution)/shard_map/ppermute | solution.py:50
  48.2 15.3 %collective-permute-start.7 = (bf16[512,256]{1,0:T(8,128)(2,1)S(1)}, bf16[512,256]{1,0:T(8,128)(2,1)S(1)}, u32[]{:S(2)}, u32[]{:S(2)}) collective-permute-start(bf16[512,256]{1,0:T(8,128)(2,1)S(1)} %bitcast.10), channel_id=1, source_target_pairs={{0,4},{4,0},{8,12},{12,8},{1,5},{5,1},{9,13},{13,9},{2,6},{6,2},{1... | collective-permute-start | bytes 786440 | tf_op jit(solution)/shard_map/ppermute | solution.py:50
  54.8 6.4 %collective-permute-start.4 = (bf16[512,256]{1,0:T(8,128)(2,1)S(1)}, bf16[512,256]{1,0:T(8,128)(2,1)S(1)}, u32[]{:S(2)}, u32[]{:S(2)}) collective-permute-start(bf16[512,256]{1,0:T(8,128)(2,1)S(1)} %bitcast.13), channel_id=1, source_target_pairs={{0,2},{2,0},{1,3},{3,1},{4,6},{6,4},{5,7},{7,5},{8,10},{10,8},{9,1... | collective-permute-start | bytes 786440 | tf_op jit(solution)/shard_map/ppermute | solution.py:50
  61.2 12.8 %collective-permute-start.6 = (bf16[512,256]{1,0:T(8,128)(2,1)S(1)}, bf16[512,256]{1,0:T(8,128)(2,1)S(1)}, u32[]{:S(2)}, u32[]{:S(2)}) collective-permute-start(bf16[512,256]{1,0:T(8,128)(2,1)S(1)} %collective-permute-done.4.refs_2_), channel_id=1, source_target_pairs={{0,8},{4,12},{8,0},{12,4},{1,9},{5,13},{9,1},{13,5},{2,10},{6,14},... | collective-permute-start | bytes 786440 | tf_op jit(solution)/shard_map/ppermute | solution.py:50
  61.8 13.4 %collective-permute-start.5 = (bf16[512,256]{1,0:T(8,128)(2,1)S(1)}, bf16[512,256]{1,0:T(8,128)(2,1)S(1)}, u32[]{:S(2)}, u32[]{:S(2)}) collective-permute-start(bf16[512,256]{1,0:T(8,128)(2,1)S(1)} %collective-permute-done.4.refs_2_), channel_id=1, source_target_pairs={{0,4},{4,0},{8,12},{12,8},{1,5},{5,1},{9,13},{13,9},{2,6},{6,2},{1... | collective-permute-start | bytes 786440 | tf_op jit(solution)/shard_map/ppermute | solution.py:50
  63.5 13.7 %collective-permute-start.12 = (bf16[512,256]{1,0:T(8,128)(2,1)S(1)}, bf16[512,256]{1,0:T(8,128)(2,1)S(1)}, u32[]{:S(2)}, u32[]{:S(2)}) collective-permute-start(bf16[512,256]{1,0:T(8,128)(2,1)S(1)} %bitcast.12), channel_id=1, source_target_pairs={{4,8},{8,4},{5,9},{9,5},{6,10},{10,6},{7,11},{11,7},{20,24},{24,20... | collective-permute-start | bytes 786440 | tf_op jit(solution)/shard_map/ppermute | solution.py:50
  64.2 15.7 %collective-permute-start.13 = (bf16[512,256]{1,0:T(8,128)(2,1)S(1)}, bf16[512,256]{1,0:T(8,128)(2,1)S(1)}, u32[]{:S(2)}, u32[]{:S(2)}) collective-permute-start(bf16[512,256]{1,0:T(8,128)(2,1)S(1)} %collective-permute-done.8.refs_0_), channel_id=1, source_target_pairs={{4,0},{8,12},{5,1},{9,13},{6,2},{10,14},{7,3},{11,15},{20,16},{24,... | collective-permute-start | bytes 786440 | tf_op jit(solution)/shard_map/ppermute | solution.py:590
  75.2 8.7 %collective-permute-start.9 = (bf16[512,256]{1,0:T(8,128)(2,1)S(1)}, bf16[512,256]{1,0:T(8,128)(2,1)S(1)}, u32[]{:S(2)}, u32[]{:S(2)}) collective-permute-start(bf16[512,256]{1,0:T(8,128)(2,1)S(1)} %collective-permute-done.4.refs_2_), channel_id=1, source_target_pairs={{4,8},{8,4},{5,9},{9,5},{6,10},{10,6},{7,11},{11,7},{20,24},{24,20... | collective-permute-start | bytes 786440 | tf_op jit(solution)/shard_map/ppermute | solution.py:50
  75.9 8.4 %collective-permute-start.10 = (bf16[512,256]{1,0:T(8,128)(2,1)S(1)}, bf16[512,256]{1,0:T(8,128)(2,1)S(1)}, u32[]{:S(2)}, u32[]{:S(2)}) collective-permute-start(bf16[512,256]{1,0:T(8,128)(2,1)S(1)} %collective-permute-done.6.refs_3_), channel_id=1, source_target_pairs={{4,0},{8,12},{5,1},{9,13},{6,2},{10,14},{7,3},{11,15},{20,16},{24,... | collective-permute-start | bytes 786440 | tf_op jit(solution)/shard_map/ppermute | solution.py:590
  85.4 19.2 %copy-start.4 = (bf16[64,5120]{1,0:T(8,128)(2,1)S(1)}, bf16[64,5120]{1,0:T(8,128)(2,1)}, u32[]{:S(2)}) copy-start(bf16[64,5120]{1,0:T(8,128)(2,1)} %hidden_ref.1) | copy-start | bytes 1966084
  85.4 19.2 %copy-start.5 = (f32[5120]{0:T(1024)S(1)}, f32[5120]{0:T(1024)}, u32[]{:S(2)}) copy-start(f32[5120]{0:T(1024)} %param.13) | copy-start | bytes 61444
  85.4 1.7 %collective-permute-start.18 = (bf16[4,64,640]{2,1,0:T(8,128)(2,1)S(1)}, bf16[4,64,640]{2,1,0:T(8,128)(2,1)S(1)}, u32[]{:S(2)}, u32[]{:S(2)}) collective-permute-start(bf16[4,64,640]{2,1,0:T(8,128)(2,1)S(1)} %get-tuple-element.64), channel_id=1, source_target_pairs={{0,1},{1,0},{2,3},{3,2},{4,5},{5,4},{6,7},{7,6},{8,9},{9,8},{10,11... | collective-permute-start | bytes 983048 | tf_op jit(solution)/shard_map/ppermute | solution.py:50
  86.6 5.6 %collective-permute-start.14 = (bf16[4,64,640]{2,1,0:T(8,128)(2,1)S(1)}, bf16[4,64,640]{2,1,0:T(8,128)(2,1)S(1)}, u32[]{:S(2)}, u32[]{:S(2)}) collective-permute-start(bf16[4,64,640]{2,1,0:T(8,128)(2,1)S(1)} %get-tuple-element.58), channel_id=1, source_target_pairs={{0,1},{1,0},{2,3},{3,2},{4,5},{5,4},{6,7},{7,6},{8,9},{9,8},{10,11... | collective-permute-start | bytes 983048 | tf_op jit(solution)/shard_map/ppermute | solution.py:50
  87.8 7.3 %collective-permute-start.19 = (bf16[64,640]{1,0:T(8,128)(2,1)S(1)}, bf16[64,640]{1,0:T(8,128)(2,1)S(1)}, u32[]{:S(2)}, u32[]{:S(2)}) collective-permute-start(bf16[64,640]{1,0:T(8,128)(2,1)S(1)} %get-tuple-element.66), channel_id=1, source_target_pairs={{0,12},{4,8},{8,4},{12,0},{1,13},{5,9},{9,5},{13,1},{2,14},{6,10},... | collective-permute-start | bytes 245768 | tf_op jit(solution)/shard_map/ppermute | solution.py:50
  90.0 10.4 %collective-permute-start.20 = (bf16[64,640]{1,0:T(8,128)(2,1)S(1)}, bf16[64,640]{1,0:T(8,128)(2,1)S(1)}, u32[]{:S(2)}, u32[]{:S(2)}) collective-permute-start(bf16[64,640]{1,0:T(8,128)(2,1)S(1)} %get-tuple-element.67), channel_id=1, source_target_pairs={{0,8},{4,12},{8,0},{12,4},{1,9},{5,13},{9,1},{13,5},{2,10},{6,14},... | collective-permute-start | bytes 245768 | tf_op jit(solution)/shard_map/ppermute | solution.py:50
  90.0 10.4 %collective-permute-start.21 = (bf16[64,640]{1,0:T(8,128)(2,1)S(1)}, bf16[64,640]{1,0:T(8,128)(2,1)S(1)}, u32[]{:S(2)}, u32[]{:S(2)}) collective-permute-start(bf16[64,640]{1,0:T(8,128)(2,1)S(1)} %get-tuple-element.68), channel_id=1, source_target_pairs={{0,4},{4,0},{8,12},{12,8},{1,5},{5,1},{9,13},{13,9},{2,6},{6,2},{1... | collective-permute-start | bytes 245768 | tf_op jit(solution)/shard_map/ppermute | solution.py:50
  92.9 7.5 %collective-permute-start.15 = (bf16[64,640]{1,0:T(8,128)(2,1)S(1)}, bf16[64,640]{1,0:T(8,128)(2,1)S(1)}, u32[]{:S(2)}, u32[]{:S(2)}) collective-permute-start(bf16[64,640]{1,0:T(8,128)(2,1)S(1)} %get-tuple-element.60), channel_id=1, source_target_pairs={{0,12},{4,8},{8,4},{12,0},{1,13},{5,9},{9,5},{13,1},{2,14},{6,10},... | collective-permute-start | bytes 245768 | tf_op jit(solution)/shard_map/ppermute | solution.py:50
  95.1 9.5 %collective-permute-start.16 = (bf16[64,640]{1,0:T(8,128)(2,1)S(1)}, bf16[64,640]{1,0:T(8,128)(2,1)S(1)}, u32[]{:S(2)}, u32[]{:S(2)}) collective-permute-start(bf16[64,640]{1,0:T(8,128)(2,1)S(1)} %get-tuple-element.61), channel_id=1, source_target_pairs={{0,8},{4,12},{8,0},{12,4},{1,9},{5,13},{9,1},{13,5},{2,10},{6,14},... | collective-permute-start | bytes 245768 | tf_op jit(solution)/shard_map/ppermute | solution.py:50
  95.1 9.5 %collective-permute-start.17 = (bf16[64,640]{1,0:T(8,128)(2,1)S(1)}, bf16[64,640]{1,0:T(8,128)(2,1)S(1)}, u32[]{:S(2)}, u32[]{:S(2)}) collective-permute-start(bf16[64,640]{1,0:T(8,128)(2,1)S(1)} %get-tuple-element.62), channel_id=1, source_target_pairs={{0,4},{4,0},{8,12},{12,8},{1,5},{5,1},{9,13},{13,9},{2,6},{6,2},{1... | collective-permute-start | bytes 245768 | tf_op jit(solution)/shard_map/ppermute | solution.py:50

commit v21 on v18

--- a/solution.py
+++ b/solution.py
@@ -56,6 +56,10 @@
     residual = fresh.astype(jnp.float32) - cached
     codes = jnp.clip(residual * jnp.exp2(-power), -SATURATION, SATURATION).astype(jnp.bfloat16)
     return (cached + codes.astype(jnp.float32) * jnp.exp2(power)).astype(jnp.bfloat16)
+
+
+def send_order(split):
+    return sorted(range(1, split), key=lambda rel: (rel != split // 2, -rel))
 
 
 def pack_kernel(split, per, exps_ref, q_ref, fresh_ref, cached_ref, *refs):
@@ -81,8 +85,8 @@
         rows = pl.ds(block * PACK_ROWS, PACK_ROWS)
         for copy in copies[block]:
             copy.wait()
-        for rel in range(split - 1, 0, -1):
-            buf = bufs[split - 1 - rel]
+        for number, rel in enumerate(send_order(split)):
+            buf = bufs[number]
             for chunk in range(per):
                 head = (near ^ rel) * per + chunk
                 lanes = pl.ds(pl.multiple_of(head * HEAD_DIM, HEAD_DIM), HEAD_DIM)
@@ -96,9 +100,7 @@
                     )
             sent.append(
                 pltpu.make_async_copy(
-                    buf.at[:, rows],
-                    outs[split - 1 - rel].at[:, rows],
-                    out_sems.at[block, rel - 1],
+                    buf.at[:, rows], outs[number].at[:, rows], out_sems.at[block, number]
                 )
             )
             sent[-1].start()
@@ -595,7 +597,7 @@
     blocks = []
     for keep, send in terms:
         total = add(where, keep, swap(send, "sub", 2, 1))
-        blocks.append([total[0]] + [swap(total[rel], "patch", 4, rel) for rel in range(3, 0, -1)])
+        blocks.append([total[0]] + [swap(total[rel], "patch", 4, rel) for rel in (2, 3, 1)])
     return mix_columns(where, hidden_in, attn_gate, blocks)
 
 
@@ -603,7 +605,7 @@
     blocks, out_ref = refs[:-1], refs[-1]
     cols = blocks[0].shape[1]
     for chunk in range(2):
-        for at, rel in enumerate((0, 3, 2, 1)):
+        for at, rel in enumerate((0, 2, 3, 1)):
             start = (2 * (where_ref[PATCH] ^ rel) + chunk) * cols
             lanes = pl.ds(pl.multiple_of(start, HEAD_DIM), cols)
             mixed = hidden_ref[:, lanes].astype(jnp.float32) + gate_ref[:, lanes] * blocks[
@@ -646,11 +648,9 @@
 
     arrays = (exponents, queries, fresh_kv, cached_kv)
     sent = pack(split, *arrays)
-    far_first = [
-        swap(x, "patch", n_patch, split - 1 - at) for at, x in enumerate(sent)
-    ]
+    arrived = {rel: swap(x, "patch", n_patch, rel) for rel, x in zip(send_order(split), sent)}
     where, sent = lax.optimization_barrier((where, sent))
-    pieces = [pack_own(split, where, *arrays), *far_first]
+    pieces = [pack_own(split, where, *arrays), *[arrived[rel] for rel in range(split - 1, 0, -1)]]
     kv_pieces = list(pieces)
     for rel in range(split, n_patch, split):
         kv_pieces += [swap(x, "patch", n_patch, rel) for x in pieces]

time: 105 us -> 106 us (level)
  starting transfers between devices: 28.4 us -> 32.2 us
  waiting for transfers between devices: 50.5 us -> 47.8 us
    ppermute x20, starting transfers between devices: 25.8 us -> 29.6 us  [swap(): return lax.ppermute(x, axes, pairs)]
    ppermute x20, waiting for transfers between devices: 46.8 us -> 43.6 us  [swap(): return lax.ppermute(x, axes, pairs)]
  transfers between devices with their start and end apart: 22 -> 22, of which waited for: 10 -> 10; matrix products, arithmetic and copies ran while one was open for 0% -> 0% of each run, Pallas kernels for 16% -> 15%
where the time goes in v21:
time: 106 us
  waiting for transfers between devices  47.8 us (45%)
  starting transfers between devices  32.2 us (30%)
  Pallas kernels  23.2 us (22%)
  local copies, waits for them, and re-layouts  2.32 us (2%)
    ppermute x20, waiting for transfers between devices, swap(): return lax.ppermute(x, axes, pairs)  43.6 us
    ppermute x20, starting transfers between devices, swap(): return lax.ppermute(x, axes, pairs)  29.6 us
    pallas_call x2, Pallas kernels, attend_half(): call(functools.partial(attend_half_kernel, half), 'attend', out, 1, [spec...  4.96 us
    ppermute x2, waiting for transfers between devices, share_tail(): ends = lax.ppermute(far, 'patch', [(1, 0), (2, 3)])  4.24 us
    pallas_call x1, Pallas kernels, first_product(): call(first_kernel, 'first', jax.ShapeDtypeStruct(acc.shape, jnp.float32),...  3.96 us
    pallas_call x2, Pallas kernels, add_product(): call(functools.partial(add_product_kernel, len(rels)), 'products', jax.Sh...  3.79 us
    pallas_call x1, Pallas kernels, pack(): pl.pallas_call(functools.partial(pack_kernel, split, feat // HEAD_DIM), o...  3.53 us
    ppermute x2, starting transfers between devices, share_tail(): ends = lax.ppermute(far, 'patch', [(1, 0), (2, 3)])  2.58 us
  transfers between devices with their start and end apart: 22, of which 10 were waited for; matrix products, arithmetic and copies ran while one was open for 0% of the time, Pallas kernels for 15%

profile of v21, /device:TPU:0, one launch (start us, length us, event | category | flops | bytes accessed | tf_op | source)
XLA Modules:
  0.0 105.8 jit_solution(11924793048078009822)
XLA Ops:
  0.0 3.5 %pack.1 = (bf16[3,256,256]{2,1,0:T(8,128)(2,1)}, bf16[3,256,256]{2,1,0:T(8,128)(2,1)}, bf16[3,256,256]{2,1,0:T(8,128)(2,1)}) custom-call(s32[2,2,8]{2,1,0:T(2,128)} %exps_ref.3, bf16[256,1024]{1,0:T(8,128)(2,1)} %q_ref.3, bf16[2,256,1024]{2,1,0:T(8,128)(2,1)} %fresh_ref.3, bf16[2,1024,1024]{2,1,0:T(8,128)(2,1)} %cached_ref.3), custom_call_target="tpu_custom_call" | custom-call | tf_op jit(solution)/shard_map/pack/pallas_call | solution.py:116
  3.6 0.0 copy-start.6
  3.6 0.1 stack.31.where_ref
  3.7 0.7 take.1
  4.4 3.0 %collective-permute-start = (bf16[512,1280]{1,0:T(8,128)(2,1)S(1)}, bf16[512,1280]{1,0:T(8,128)(2,1)S(1)}, u32[]{:S(2)}, u32[]{:S(2)}) collective-permute-start(bf16[512,1280]{1,0:T(8,128)(2,1)S(1)} %take.1), channel_id=1, source_target_pairs={{0,2},{2,0},{1,3},{3,1},{4,6},{6,4},{5,7},{7,5},{8,10},{10,8},{9,1... | collective-permute-start | bytes 3932168 | tf_op jit(solution)/shard_map/ppermute | solution.py:50
  7.4 2.6 %collective-permute-start.2 = (bf16[3,256,256]{2,1,0:T(8,128)(2,1)S(1)}, bf16[3,256,256]{2,1,0:T(8,128)(2,1)S(1)}, u32[]{:S(2)}, u32[]{:S(2)}) collective-permute-start(bf16[3,256,256]{2,1,0:T(8,128)(2,1)S(1)} %copy-done.9), channel_id=1, source_target_pairs={{0,8},{4,12},{8,0},{12,4},{1,9},{5,13},{9,1},{13,5},{2,10},{6,14},... | collective-permute-start | bytes 1179656 | tf_op jit(solution)/shard_map/ppermute | solution.py:50
  10.0 1.3 %collective-permute-start.3 = (bf16[3,256,256]{2,1,0:T(8,128)(2,1)S(1)}, bf16[3,256,256]{2,1,0:T(8,128)(2,1)S(1)}, u32[]{:S(2)}, u32[]{:S(2)}) collective-permute-start(bf16[3,256,256]{2,1,0:T(8,128)(2,1)S(1)} %copy-done.8), channel_id=1, source_target_pairs={{0,12},{4,8},{8,4},{12,0},{1,13},{5,9},{9,5},{13,1},{2,14},{6,10},... | collective-permute-start | bytes 1179656 | tf_op jit(solution)/shard_map/ppermute | solution.py:50
  11.3 0.3 collective-permute-start.1
  11.6 2.2 %copy-done.1 = bf16[2,1024,1024]{2,1,0:T(8,128)(2,1)S(1)} copy-done((bf16[2,1024,1024]{2,1,0:T(8,128)(2,1)S(1)}, bf16[2,1024,1024]{2,1,0:T(8,128)(2,1)}, u32[]{:S(2)}) %copy-start.1) | copy-done | bytes 4194328
  13.8 1.3 %own.1.refs_0_ = bf16[3,256,256]{2,1,0:T(8,128)(2,1)S(1)} custom-call(s32[6]{0:T(128)S(1)} %stack.31.where_ref, s32[2,2,8]{2,1,0:T(2,128)S(1)} %copy-done.6, bf16[256,1024]{1,0:T(8,128)(2,1)S(1)} %copy-done.3, bf16[2,256,1024]{2,1,0:T(8,128)(2,1)S(1)} %copy-done.2, bf16[2,1024,1024]{2,1,0:T(8,128)(2,1)S(1)} %copy-done.1), custom_call_target="tpu_custom_call" | custom-call | flops 1 | tf_op jit(solution)/shard_map/own/pallas_call | solution.py:152
  15.1 21.0 %collective-permute-done.refs_7_.fetched_ref = bf16[512,1280]{1,0:T(8,128)(2,1)S(1)} collective-permute-done((bf16[512,1280]{1,0:T(8,128)(2,1)S(1)}, bf16[512,1280]{1,0:T(8,128)(2,1)S(1)}, u32[]{:S(2)}, u32[]{:S(2)}) %collective-permute-start) | collective-permute-done | bytes 1310752 | tf_op jit(solution)/shard_map/ppermute | solution.py:50
  36.2 1.8 %collective-permute-start.11 = (bf16[512,1280]{1,0:T(8,128)(2,1)S(1)}, bf16[512,1280]{1,0:T(8,128)(2,1)S(1)}, u32[]{:S(2)}, u32[]{:S(2)}) collective-permute-start(bf16[512,1280]{1,0:T(8,128)(2,1)S(1)} %collective-permute-done.refs_7_.fetched_ref), channel_id=1, source_target_pairs={{0,16},{16,0},{1,17},{17,1},{2,18},{18,2},{3,19},{19,3},{4,20},{20... | collective-permute-start | bytes 3932168 | tf_op jit(solution)/shard_map/ppermute | solution.py:50
  37.9 2.5 %attend.2 = bf16[4,128,256]{2,1,0:T(8,128)(2,1)S(1)} custom-call(s32[6]{0:T(128)S(1)} %stack.31.where_ref, bf16[3,256,256]{2,1,0:T(8,128)(2,1)S(1)} %own.1.refs_0_, bf16[3,256,256]{2,1,0:T(8,128)(2,1)S(1)} %collective-permute-done.1.refs_1_, bf16[3,256,256]{2,1,0:T(8,128)(2,1)S(1)} %collective-permute-done.2.refs_2_, ...), custom_call_target="tpu_custom_call" | custom-call | flops 1 | tf_op jit(solution)/shard_map/attend/pallas_call | solution.py:410
  40.4 8.9 %collective-permute-start.8 = (bf16[512,256]{1,0:T(8,128)(2,1)S(1)}, bf16[512,256]{1,0:T(8,128)(2,1)S(1)}, u32[]{:S(2)}, u32[]{:S(2)}) collective-permute-start(bf16[512,256]{1,0:T(8,128)(2,1)S(1)} %bitcast.9), channel_id=1, source_target_pairs={{0,8},{4,12},{8,0},{12,4},{1,9},{5,13},{9,1},{13,5},{2,10},{6,14},... | collective-permute-start | bytes 786440 | tf_op jit(solution)/shard_map/ppermute | solution.py:50
  49.3 2.5 %attend.3 = bf16[4,128,256]{2,1,0:T(8,128)(2,1)S(1)} custom-call(s32[6]{0:T(128)S(1)} %stack.31.where_ref, bf16[3,256,256]{2,1,0:T(8,128)(2,1)S(1)} %own.1.refs_0_, bf16[3,256,256]{2,1,0:T(8,128)(2,1)S(1)} %collective-permute-done.1.refs_1_, bf16[3,256,256]{2,1,0:T(8,128)(2,1)S(1)} %collective-permute-done.2.refs_2_, ...), custom_call_target="tpu_custom_call" | custom-call | flops 1 | tf_op jit(solution)/shard_map/attend/pallas_call | solution.py:410
  51.8 0.6 collective-permute-start.4
  52.4 1.5 %products.2.refs_4_ = f32[512,1280]{1,0:T(8,128)S(1)} custom-call(s32[6]{0:T(128)S(1)} %stack.31.where_ref, bf16[512,256]{1,0:T(8,128)(2,1)S(1)} %bitcast.11, bf16[1024,1280]{1,0:T(8,128)(2,1)S(1)} %copy-done), custom_call_target="tpu_custom_call" | custom-call | flops 6000000000 | tf_op jit(solution)/shard_map/products/pallas_call | solution.py:435
  54.0 5.8 %collective-permute-done.4.refs_2_ = bf16[512,256]{1,0:T(8,128)(2,1)S(1)} collective-permute-done((bf16[512,256]{1,0:T(8,128)(2,1)S(1)}, bf16[512,256]{1,0:T(8,128)(2,1)S(1)}, u32[]{:S(2)}, u32[]{:S(2)}) %collective-permute-start.4) | collective-permute-done | bytes 262176 | tf_op jit(solution)/shard_map/ppermute | solution.py:50
  59.8 0.7 collective-permute-start.6
  60.5 1.4 %collective-permute-start.5 = (bf16[512,256]{1,0:T(8,128)(2,1)S(1)}, bf16[512,256]{1,0:T(8,128)(2,1)S(1)}, u32[]{:S(2)}, u32[]{:S(2)}) collective-permute-start(bf16[512,256]{1,0:T(8,128)(2,1)S(1)} %collective-permute-done.4.refs_2_), channel_id=1, source_target_pairs={{0,4},{4,0},{8,12},{12,8},{1,5},{5,1},{9,13},{13,9},{2,6},{6,2},{1... | collective-permute-start | bytes 786440 | tf_op jit(solution)/shard_map/ppermute | solution.py:50
  61.9 2.7 %collective-permute-done.7.refs_1_ = bf16[512,256]{1,0:T(8,128)(2,1)S(1)} collective-permute-done((bf16[512,256]{1,0:T(8,128)(2,1)S(1)}, bf16[512,256]{1,0:T(8,128)(2,1)S(1)}, u32[]{:S(2)}, u32[]{:S(2)}) %collective-permute-start.7) | collective-permute-done | bytes 262176 | tf_op jit(solution)/shard_map/ppermute | solution.py:50
  64.6 0.7 collective-permute-start.12
  65.3 1.3 %collective-permute-start.13 = (bf16[512,256]{1,0:T(8,128)(2,1)S(1)}, bf16[512,256]{1,0:T(8,128)(2,1)S(1)}, u32[]{:S(2)}, u32[]{:S(2)}) collective-permute-start(bf16[512,256]{1,0:T(8,128)(2,1)S(1)} %collective-permute-done.8.refs_0_), channel_id=1, source_target_pairs={{4,0},{8,12},{5,1},{9,13},{6,2},{10,14},{7,3},{11,15},{20,16},{24,... | collective-permute-start | bytes 786440 | tf_op jit(solution)/shard_map/ppermute | solution.py:591
  66.6 2.2 %products.3.refs_5_ = f32[512,1280]{1,0:T(8,128)S(1)} custom-call(s32[6]{0:T(128)S(1)} %stack.31.where_ref, bf16[512,256]{1,0:T(8,128)(2,1)S(1)} %collective-permute-done.8.refs_0_, bf16[512,256]{1,0:T(8,128)(2,1)S(1)} %collective-permute-done.7.refs_1_, bf16[1024,1280]{1,0:T(8,128)(2,1)S(1)} %copy-done, bf16[1024,1280]{1,0:T(8,128)(2,1)S(1)} %copy-done, ...), custom_call_target="tpu_custom_call" | custom-call | flops 1 | tf_op jit(solution)/shard_map/products/pallas_call | solution.py:435
  68.8 5.6 %collective-permute-done.6.refs_3_ = bf16[512,256]{1,0:T(8,128)(2,1)S(1)} collective-permute-done((bf16[512,256]{1,0:T(8,128)(2,1)S(1)}, bf16[512,256]{1,0:T(8,128)(2,1)S(1)}, u32[]{:S(2)}, u32[]{:S(2)}) %collective-permute-start.6) | collective-permute-done | bytes 262176 | tf_op jit(solution)/shard_map/ppermute | solution.py:50
  74.5 0.4 collective-permute-done.5.refs_4_
  74.9 0.7 collective-permute-start.9
  75.6 1.3 %collective-permute-start.10 = (bf16[512,256]{1,0:T(8,128)(2,1)S(1)}, bf16[512,256]{1,0:T(8,128)(2,1)S(1)}, u32[]{:S(2)}, u32[]{:S(2)}) collective-permute-start(bf16[512,256]{1,0:T(8,128)(2,1)S(1)} %collective-permute-done.6.refs_3_), channel_id=1, source_target_pairs={{4,0},{8,12},{5,1},{9,13},{6,2},{10,14},{7,3},{11,15},{20,16},{24,... | collective-permute-start | bytes 786440 | tf_op jit(solution)/shard_map/ppermute | solution.py:591
  76.9 3.6 %collective-permute-done.13.refs_1_ = bf16[512,256]{1,0:T(8,128)(2,1)S(1)} collective-permute-done((bf16[512,256]{1,0:T(8,128)(2,1)S(1)}, bf16[512,256]{1,0:T(8,128)(2,1)S(1)}, u32[]{:S(2)}, u32[]{:S(2)}) %collective-permute-start.13) | collective-permute-done | bytes 262176 | tf_op jit(solution)/shard_map/ppermute | solution.py:591
  80.5 4.0 %first.1.acc_in = f32[512,1280]{1,0:T(8,128)S(1)} custom-call(s32[6]{0:T(128)S(1)} %stack.31.where_ref, bf16[512,256]{1,0:T(8,128)(2,1)S(1)} %collective-permute-done.12.refs_0_, bf16[512,256]{1,0:T(8,128)(2,1)S(1)} %collective-permute-done.13.refs_1_, bf16[512,256]{1,0:T(8,128)(2,1)S(1)} %collective-permute-done.4.refs_2_, ...), custom_call_target="tpu_custom_call" | custom-call | flops 1 | tf_op jit(solution)/shard_map/first/pallas_call | solution.py:483
  84.5 0.6 collective-permute-done.10.more
  85.1 1.1 %second.3 = (bf16[4,64,640]{2,1,0:T(8,128)(2,1)S(1)}, bf16[4,64,640]{2,1,0:T(8,128)(2,1)S(1)}) custom-call(s32[6]{0:T(128)S(1)} %stack.31.where_ref, bf16[512,256]{1,0:T(8,128)(2,1)S(1)} %collective-permute-done.9.slot, bf16[512,256]{1,0:T(8,128)(2,1)S(1)} %collective-permute-done.10.more, bf16[512,1280]{1,0:T(8,128)(2,1)S(1)} %collective-permute-done.refs_7_.fetched_ref, ...), custom_call_target="tpu_custom_call" | custom-call | flops 1 | tf_op jit(solution)/shard_map/second/pallas_call | solution.py:524
  86.2 0.0 copy-start.4
  86.2 0.1 collective-permute-start.18
  86.3 1.1 %second.2 = (bf16[4,64,640]{2,1,0:T(8,128)(2,1)S(1)}, bf16[4,64,640]{2,1,0:T(8,128)(2,1)S(1)}) custom-call(s32[6]{0:T(128)S(1)} %stack.31.where_ref, bf16[512,256]{1,0:T(8,128)(2,1)S(1)} %collective-permute-done.9.slot, bf16[512,256]{1,0:T(8,128)(2,1)S(1)} %collective-permute-done.10.more, bf16[512,1280]{1,0:T(8,128)(2,1)S(1)} %collective-permute-done.refs_7_.fetched_ref, ...), custom_call_target="tpu_custom_call" | custom-call | flops 1 | tf_op jit(solution)/shard_map/second/pallas_call | solution.py:524
  87.4 0.6 collective-permute-start.14
  88.0 0.6 add.8
  88.6 0.3 collective-permute-start.19
  88.9 2.3 %collective-permute-start.20 = (bf16[64,640]{1,0:T(8,128)(2,1)S(1)}, bf16[64,640]{1,0:T(8,128)(2,1)S(1)}, u32[]{:S(2)}, u32[]{:S(2)}) collective-permute-start(bf16[64,640]{1,0:T(8,128)(2,1)S(1)} %get-tuple-element.69), channel_id=1, source_target_pairs={{0,12},{4,8},{8,4},{12,0},{1,13},{5,9},{9,5},{13,1},{2,14},{6,10},... | collective-permute-start | bytes 245768 | tf_op jit(solution)/shard_map/ppermute | solution.py:50
  91.2 1.0 collective-permute-start.21
  92.2 0.6 add.7
  92.8 1.2 %collective-permute-start.15 = (bf16[64,640]{1,0:T(8,128)(2,1)S(1)}, bf16[64,640]{1,0:T(8,128)(2,1)S(1)}, u32[]{:S(2)}, u32[]{:S(2)}) collective-permute-start(bf16[64,640]{1,0:T(8,128)(2,1)S(1)} %get-tuple-element.62), channel_id=1, source_target_pairs={{0,8},{4,12},{8,0},{12,4},{1,9},{5,13},{9,1},{13,5},{2,10},{6,14},... | collective-permute-start | bytes 245768 | tf_op jit(solution)/shard_map/ppermute | solution.py:50
  94.0 2.3 %collective-permute-start.16 = (bf16[64,640]{1,0:T(8,128)(2,1)S(1)}, bf16[64,640]{1,0:T(8,128)(2,1)S(1)}, u32[]{:S(2)}, u32[]{:S(2)}) collective-permute-start(bf16[64,640]{1,0:T(8,128)(2,1)S(1)} %get-tuple-element.63), channel_id=1, source_target_pairs={{0,12},{4,8},{8,4},{12,0},{1,13},{5,9},{9,5},{13,1},{2,14},{6,10},... | collective-permute-start | bytes 245768 | tf_op jit(solution)/shard_map/ppermute | solution.py:50
  96.3 1.5 %collective-permute-done.19.refs_5_ = bf16[64,640]{1,0:T(8,128)(2,1)S(1)} collective-permute-done((bf16[64,640]{1,0:T(8,128)(2,1)S(1)}, bf16[64,640]{1,0:T(8,128)(2,1)S(1)}, u32[]{:S(2)}, u32[]{:S(2)}) %collective-permute-start.19) | collective-permute-done | bytes 81952 | tf_op jit(solution)/shard_map/ppermute | solution.py:50
  97.8 0.8 collective-permute-done.21.refs_7_
  98.7 5.6 %collective-permute-done.15.refs_1_ = bf16[64,640]{1,0:T(8,128)(2,1)S(1)} collective-permute-done((bf16[64,640]{1,0:T(8,128)(2,1)S(1)}, bf16[64,640]{1,0:T(8,128)(2,1)S(1)}, u32[]{:S(2)}, u32[]{:S(2)}) %collective-permute-start.15) | collective-permute-done | bytes 81952 | tf_op jit(solution)/shard_map/ppermute | solution.py:50
  104.2 0.0 collective-permute-done.17.refs_3_
  104.3 1.6 %mix.1 = bf16[64,5120]{1,0:T(8,128)(2,1)} custom-call(s32[6]{0:T(128)S(1)} %stack.31.where_ref, bf16[64,5120]{1,0:T(8,128)(2,1)S(1)} %copy-done.4, f32[1,5120]{1,0:T(1,128)S(1)} %bitcast.14, bf16[64,640]{1,0:T(8,128)(2,1)S(1)} %get-tuple-element.61.refs_0_, bf16[64,640]{1,0:T(8,128)(2,1)S(1)} %collective-permute-done.15.refs_1_, ...), custom_call_target="tpu_custom_call" | custom-call | flops 1 | tf_op jit(solution)/shard_map/mix/pallas_call | solution.py:620
  (30 shorter events, 0.1 us)
Async XLA Ops:
  0.0 3.7 %copy-start = (bf16[1024,1280]{1,0:T(8,128)(2,1)S(1)}, bf16[1024,1280]{1,0:T(8,128)(2,1)}, u32[]{:S(2)}) copy-start(bf16[1024,1280]{1,0:T(8,128)(2,1)} %refs_6_) | copy-start | bytes 7864324
  3.5 7.8 %copy-start.7 = (bf16[3,256,256]{2,1,0:T(8,128)(2,1)S(1)}, bf16[3,256,256]{2,1,0:T(8,128)(2,1)}, u32[]{:S(2)}) copy-start(bf16[3,256,256]{2,1,0:T(8,128)(2,1)} %get-tuple-element.40) | copy-start | bytes 1179652
  3.6 8.1 %copy-start.3 = (bf16[256,1024]{1,0:T(8,128)(2,1)S(1)}, bf16[256,1024]{1,0:T(8,128)(2,1)}, u32[]{:S(2)}) copy-start(bf16[256,1024]{1,0:T(8,128)(2,1)} %q_ref.3) | copy-start | bytes 1572868
  3.6 8.1 %copy-start.6 = (s32[2,2,8]{2,1,0:T(2,128)S(1)}, s32[2,2,8]{2,1,0:T(2,128)}, u32[]{:S(2)}) copy-start(s32[2,2,8]{2,1,0:T(2,128)} %exps_ref.3) | copy-start | bytes 388
  3.7 3.7 %copy-start.9 = (bf16[3,256,256]{2,1,0:T(8,128)(2,1)S(1)}, bf16[3,256,256]{2,1,0:T(8,128)(2,1)}, u32[]{:S(2)}) copy-start(bf16[3,256,256]{2,1,0:T(8,128)(2,1)} %get-tuple-element.38) | copy-start | bytes 1179652
  3.7 6.3 %copy-start.8 = (bf16[3,256,256]{2,1,0:T(8,128)(2,1)S(1)}, bf16[3,256,256]{2,1,0:T(8,128)(2,1)}, u32[]{:S(2)}) copy-start(bf16[3,256,256]{2,1,0:T(8,128)(2,1)} %get-tuple-element.39) | copy-start | bytes 1179652
  3.7 8.0 %copy-start.2 = (bf16[2,256,1024]{2,1,0:T(8,128)(2,1)S(1)}, bf16[2,256,1024]{2,1,0:T(8,128)(2,1)}, u32[]{:S(2)}) copy-start(bf16[2,256,1024]{2,1,0:T(8,128)(2,1)} %fresh_ref.3) | copy-start | bytes 3145732
  4.4 31.8 %collective-permute-start = (bf16[512,1280]{1,0:T(8,128)(2,1)S(1)}, bf16[512,1280]{1,0:T(8,128)(2,1)S(1)}, u32[]{:S(2)}, u32[]{:S(2)}) collective-permute-start(bf16[512,1280]{1,0:T(8,128)(2,1)S(1)} %take.1), channel_id=1, source_target_pairs={{0,2},{2,0},{1,3},{3,1},{4,6},{6,4},{5,7},{7,5},{8,10},{10,8},{9,1... | collective-permute-start | bytes 3932168 | tf_op jit(solution)/shard_map/ppermute | solution.py:50
  7.4 30.5 %collective-permute-start.2 = (bf16[3,256,256]{2,1,0:T(8,128)(2,1)S(1)}, bf16[3,256,256]{2,1,0:T(8,128)(2,1)S(1)}, u32[]{:S(2)}, u32[]{:S(2)}) collective-permute-start(bf16[3,256,256]{2,1,0:T(8,128)(2,1)S(1)} %copy-done.9), channel_id=1, source_target_pairs={{0,8},{4,12},{8,0},{12,4},{1,9},{5,13},{9,1},{13,5},{2,10},{6,14},... | collective-permute-start | bytes 1179656 | tf_op jit(solution)/shard_map/ppermute | solution.py:50
  10.0 28.0 %collective-permute-start.3 = (bf16[3,256,256]{2,1,0:T(8,128)(2,1)S(1)}, bf16[3,256,256]{2,1,0:T(8,128)(2,1)S(1)}, u32[]{:S(2)}, u32[]{:S(2)}) collective-permute-start(bf16[3,256,256]{2,1,0:T(8,128)(2,1)S(1)} %copy-done.8), channel_id=1, source_target_pairs={{0,12},{4,8},{8,4},{12,0},{1,13},{5,9},{9,5},{13,1},{2,14},{6,10},... | collective-permute-start | bytes 1179656 | tf_op jit(solution)/shard_map/ppermute | solution.py:50
  11.3 26.6 %collective-permute-start.1 = (bf16[3,256,256]{2,1,0:T(8,128)(2,1)S(1)}, bf16[3,256,256]{2,1,0:T(8,128)(2,1)S(1)}, u32[]{:S(2)}, u32[]{:S(2)}) collective-permute-start(bf16[3,256,256]{2,1,0:T(8,128)(2,1)S(1)} %copy-done.7), channel_id=1, source_target_pairs={{0,4},{4,0},{8,12},{12,8},{1,5},{5,1},{9,13},{13,9},{2,6},{6,2},{1... | collective-permute-start | bytes 1179656 | tf_op jit(solution)/shard_map/ppermute | solution.py:50
  11.6 2.2 %copy-start.1 = (bf16[2,1024,1024]{2,1,0:T(8,128)(2,1)S(1)}, bf16[2,1024,1024]{2,1,0:T(8,128)(2,1)}, u32[]{:S(2)}) copy-start(bf16[2,1024,1024]{2,1,0:T(8,128)(2,1)} %cached_ref.3) | copy-start | bytes 12582916
  36.2 44.4 %collective-permute-start.11 = (bf16[512,1280]{1,0:T(8,128)(2,1)S(1)}, bf16[512,1280]{1,0:T(8,128)(2,1)S(1)}, u32[]{:S(2)}, u32[]{:S(2)}) collective-permute-start(bf16[512,1280]{1,0:T(8,128)(2,1)S(1)} %collective-permute-done.refs_7_.fetched_ref), channel_id=1, source_target_pairs={{0,16},{16,0},{1,17},{17,1},{2,18},{18,2},{3,19},{19,3},{4,20},{20... | collective-permute-start | bytes 3932168 | tf_op jit(solution)/shard_map/ppermute | solution.py:50
  40.4 21.5 %collective-permute-start.8 = (bf16[512,256]{1,0:T(8,128)(2,1)S(1)}, bf16[512,256]{1,0:T(8,128)(2,1)S(1)}, u32[]{:S(2)}, u32[]{:S(2)}) collective-permute-start(bf16[512,256]{1,0:T(8,128)(2,1)S(1)} %bitcast.9), channel_id=1, source_target_pairs={{0,8},{4,12},{8,0},{12,4},{1,9},{5,13},{9,1},{13,5},{2,10},{6,14},... | collective-permute-start | bytes 786440 | tf_op jit(solution)/shard_map/ppermute | solution.py:50
  49.3 15.3 %collective-permute-start.7 = (bf16[512,256]{1,0:T(8,128)(2,1)S(1)}, bf16[512,256]{1,0:T(8,128)(2,1)S(1)}, u32[]{:S(2)}, u32[]{:S(2)}) collective-permute-start(bf16[512,256]{1,0:T(8,128)(2,1)S(1)} %bitcast.10), channel_id=1, source_target_pairs={{0,4},{4,0},{8,12},{12,8},{1,5},{5,1},{9,13},{13,9},{2,6},{6,2},{1... | collective-permute-start | bytes 786440 | tf_op jit(solution)/shard_map/ppermute | solution.py:50
  51.8 8.0 %collective-permute-start.4 = (bf16[512,256]{1,0:T(8,128)(2,1)S(1)}, bf16[512,256]{1,0:T(8,128)(2,1)S(1)}, u32[]{:S(2)}, u32[]{:S(2)}) collective-permute-start(bf16[512,256]{1,0:T(8,128)(2,1)S(1)} %bitcast.13), channel_id=1, source_target_pairs={{0,2},{2,0},{1,3},{3,1},{4,6},{6,4},{5,7},{7,5},{8,10},{10,8},{9,1... | collective-permute-start | bytes 786440 | tf_op jit(solution)/shard_map/ppermute | solution.py:50
  59.8 14.6 %collective-permute-start.6 = (bf16[512,256]{1,0:T(8,128)(2,1)S(1)}, bf16[512,256]{1,0:T(8,128)(2,1)S(1)}, u32[]{:S(2)}, u32[]{:S(2)}) collective-permute-start(bf16[512,256]{1,0:T(8,128)(2,1)S(1)} %collective-permute-done.4.refs_2_), channel_id=1, source_target_pairs={{0,8},{4,12},{8,0},{12,4},{1,9},{5,13},{9,1},{13,5},{2,10},{6,14},... | collective-permute-start | bytes 786440 | tf_op jit(solution)/shard_map/ppermute | solution.py:50
  60.5 14.3 %collective-permute-start.5 = (bf16[512,256]{1,0:T(8,128)(2,1)S(1)}, bf16[512,256]{1,0:T(8,128)(2,1)S(1)}, u32[]{:S(2)}, u32[]{:S(2)}) collective-permute-start(bf16[512,256]{1,0:T(8,128)(2,1)S(1)} %collective-permute-done.4.refs_2_), channel_id=1, source_target_pairs={{0,4},{4,0},{8,12},{12,8},{1,5},{5,1},{9,13},{13,9},{2,6},{6,2},{1... | collective-permute-start | bytes 786440 | tf_op jit(solution)/shard_map/ppermute | solution.py:50
  64.6 12.2 %collective-permute-start.12 = (bf16[512,256]{1,0:T(8,128)(2,1)S(1)}, bf16[512,256]{1,0:T(8,128)(2,1)S(1)}, u32[]{:S(2)}, u32[]{:S(2)}) collective-permute-start(bf16[512,256]{1,0:T(8,128)(2,1)S(1)} %bitcast.12), channel_id=1, source_target_pairs={{4,8},{8,4},{5,9},{9,5},{6,10},{10,6},{7,11},{11,7},{20,24},{24,20... | collective-permute-start | bytes 786440 | tf_op jit(solution)/shard_map/ppermute | solution.py:50
  65.3 15.2 %collective-permute-start.13 = (bf16[512,256]{1,0:T(8,128)(2,1)S(1)}, bf16[512,256]{1,0:T(8,128)(2,1)S(1)}, u32[]{:S(2)}, u32[]{:S(2)}) collective-permute-start(bf16[512,256]{1,0:T(8,128)(2,1)S(1)} %collective-permute-done.8.refs_0_), channel_id=1, source_target_pairs={{4,0},{8,12},{5,1},{9,13},{6,2},{10,14},{7,3},{11,15},{20,16},{24,... | collective-permute-start | bytes 786440 | tf_op jit(solution)/shard_map/ppermute | solution.py:591
  74.9 9.6 %collective-permute-start.9 = (bf16[512,256]{1,0:T(8,128)(2,1)S(1)}, bf16[512,256]{1,0:T(8,128)(2,1)S(1)}, u32[]{:S(2)}, u32[]{:S(2)}) collective-permute-start(bf16[512,256]{1,0:T(8,128)(2,1)S(1)} %collective-permute-done.4.refs_2_), channel_id=1, source_target_pairs={{4,8},{8,4},{5,9},{9,5},{6,10},{10,6},{7,11},{11,7},{20,24},{24,20... | collective-permute-start | bytes 786440 | tf_op jit(solution)/shard_map/ppermute | solution.py:50
  75.6 9.5 %collective-permute-start.10 = (bf16[512,256]{1,0:T(8,128)(2,1)S(1)}, bf16[512,256]{1,0:T(8,128)(2,1)S(1)}, u32[]{:S(2)}, u32[]{:S(2)}) collective-permute-start(bf16[512,256]{1,0:T(8,128)(2,1)S(1)} %collective-permute-done.6.refs_3_), channel_id=1, source_target_pairs={{4,0},{8,12},{5,1},{9,13},{6,2},{10,14},{7,3},{11,15},{20,16},{24,... | collective-permute-start | bytes 786440 | tf_op jit(solution)/shard_map/ppermute | solution.py:591
  86.2 18.1 %copy-start.4 = (bf16[64,5120]{1,0:T(8,128)(2,1)S(1)}, bf16[64,5120]{1,0:T(8,128)(2,1)}, u32[]{:S(2)}) copy-start(bf16[64,5120]{1,0:T(8,128)(2,1)} %hidden_ref.1) | copy-start | bytes 1966084
  86.2 18.0 %copy-start.5 = (f32[5120]{0:T(1024)S(1)}, f32[5120]{0:T(1024)}, u32[]{:S(2)}) copy-start(f32[5120]{0:T(1024)} %param.13) | copy-start | bytes 61444
  86.2 1.8 %collective-permute-start.18 = (bf16[4,64,640]{2,1,0:T(8,128)(2,1)S(1)}, bf16[4,64,640]{2,1,0:T(8,128)(2,1)S(1)}, u32[]{:S(2)}, u32[]{:S(2)}) collective-permute-start(bf16[4,64,640]{2,1,0:T(8,128)(2,1)S(1)} %get-tuple-element.66), channel_id=1, source_target_pairs={{0,1},{1,0},{2,3},{3,2},{4,5},{5,4},{6,7},{7,6},{8,9},{9,8},{10,11... | collective-permute-start | bytes 983048 | tf_op jit(solution)/shard_map/ppermute | solution.py:50
  87.4 4.7 %collective-permute-start.14 = (bf16[4,64,640]{2,1,0:T(8,128)(2,1)S(1)}, bf16[4,64,640]{2,1,0:T(8,128)(2,1)S(1)}, u32[]{:S(2)}, u32[]{:S(2)}) collective-permute-start(bf16[4,64,640]{2,1,0:T(8,128)(2,1)S(1)} %get-tuple-element.60), channel_id=1, source_target_pairs={{0,1},{1,0},{2,3},{3,2},{4,5},{5,4},{6,7},{7,6},{8,9},{9,8},{10,11... | collective-permute-start | bytes 983048 | tf_op jit(solution)/shard_map/ppermute | solution.py:50
  88.6 9.2 %collective-permute-start.19 = (bf16[64,640]{1,0:T(8,128)(2,1)S(1)}, bf16[64,640]{1,0:T(8,128)(2,1)S(1)}, u32[]{:S(2)}, u32[]{:S(2)}) collective-permute-start(bf16[64,640]{1,0:T(8,128)(2,1)S(1)} %get-tuple-element.68), channel_id=1, source_target_pairs={{0,8},{4,12},{8,0},{12,4},{1,9},{5,13},{9,1},{13,5},{2,10},{6,14},... | collective-permute-start | bytes 245768 | tf_op jit(solution)/shard_map/ppermute | solution.py:50
  88.9 8.9 %collective-permute-start.20 = (bf16[64,640]{1,0:T(8,128)(2,1)S(1)}, bf16[64,640]{1,0:T(8,128)(2,1)S(1)}, u32[]{:S(2)}, u32[]{:S(2)}) collective-permute-start(bf16[64,640]{1,0:T(8,128)(2,1)S(1)} %get-tuple-element.69), channel_id=1, source_target_pairs={{0,12},{4,8},{8,4},{12,0},{1,13},{5,9},{9,5},{13,1},{2,14},{6,10},... | collective-permute-start | bytes 245768 | tf_op jit(solution)/shard_map/ppermute | solution.py:50
  91.2 7.5 %collective-permute-start.21 = (bf16[64,640]{1,0:T(8,128)(2,1)S(1)}, bf16[64,640]{1,0:T(8,128)(2,1)S(1)}, u32[]{:S(2)}, u32[]{:S(2)}) collective-permute-start(bf16[64,640]{1,0:T(8,128)(2,1)S(1)} %get-tuple-element.70), channel_id=1, source_target_pairs={{0,4},{4,0},{8,12},{12,8},{1,5},{5,1},{9,13},{13,9},{2,6},{6,2},{1... | collective-permute-start | bytes 245768 | tf_op jit(solution)/shard_map/ppermute | solution.py:50
  92.8 11.4 %collective-permute-start.15 = (bf16[64,640]{1,0:T(8,128)(2,1)S(1)}, bf16[64,640]{1,0:T(8,128)(2,1)S(1)}, u32[]{:S(2)}, u32[]{:S(2)}) collective-permute-start(bf16[64,640]{1,0:T(8,128)(2,1)S(1)} %get-tuple-element.62), channel_id=1, source_target_pairs={{0,8},{4,12},{8,0},{12,4},{1,9},{5,13},{9,1},{13,5},{2,10},{6,14},... | collective-permute-start | bytes 245768 | tf_op jit(solution)/shard_map/ppermute | solution.py:50
  94.0 10.3 %collective-permute-start.16 = (bf16[64,640]{1,0:T(8,128)(2,1)S(1)}, bf16[64,640]{1,0:T(8,128)(2,1)S(1)}, u32[]{:S(2)}, u32[]{:S(2)}) collective-permute-start(bf16[64,640]{1,0:T(8,128)(2,1)S(1)} %get-tuple-element.63), channel_id=1, source_target_pairs={{0,12},{4,8},{8,4},{12,0},{1,13},{5,9},{9,5},{13,1},{2,14},{6,10},... | collective-permute-start | bytes 245768 | tf_op jit(solution)/shard_map/ppermute | solution.py:50
  97.8 6.4 %collective-permute-start.17 = (bf16[64,640]{1,0:T(8,128)(2,1)S(1)}, bf16[64,640]{1,0:T(8,128)(2,1)S(1)}, u32[]{:S(2)}, u32[]{:S(2)}) collective-permute-start(bf16[64,640]{1,0:T(8,128)(2,1)S(1)} %get-tuple-element.64), channel_id=1, source_target_pairs={{0,4},{4,0},{8,12},{12,8},{1,5},{5,1},{9,13},{13,9},{2,6},{6,2},{1... | collective-permute-start | bytes 245768 | tf_op jit(solution)/shard_map/ppermute | solution.py:50

commit v22 on v21

--- a/solution.py
+++ b/solution.py
@@ -392,16 +392,21 @@
         keys = jnp.concatenate([ref[1, :, lanes] for ref in pieces], axis=0)
         values = jnp.concatenate([ref[2, :, lanes] for ref in pieces], axis=0)
         values = jnp.concatenate([values, jnp.ones_like(values)], axis=1)
-        query = jnp.concatenate([ref[0, pl.ds(start, rows), lanes] for ref in pieces], axis=0)
-        scores = lax.dot_general(
-            query, keys, (((1,), (1,)), ((), ())), preferred_element_type=jnp.float32
-        )
-        peak = jnp.max(scores, axis=1, keepdims=True)
-        expo = jnp.exp2((scores - peak) * factor).astype(jnp.bfloat16)
-        mix = jnp.dot(expo, values, preferred_element_type=jnp.float32)
-        mix = (mix[:, :HEAD_DIM] / mix[:, HEAD_DIM:]).astype(jnp.bfloat16)
-        for rel in range(len(pieces)):
-            out[where_ref[NEAR] ^ rel, :, lanes] = mix[rel * rows : (rel + 1) * rows]
+        for first in range(0, len(pieces), 2):
+            query = [ref[0, pl.ds(start, rows), lanes] for ref in pieces[first : first + 2]]
+            scores = lax.dot_general(
+                jnp.concatenate(query, axis=0),
+                keys,
+                (((1,), (1,)), ((), ())),
+                preferred_element_type=jnp.float32,
+            )
+            peak = jnp.max(scores, axis=1, keepdims=True)
+            expo = jnp.exp2((scores - peak) * factor).astype(jnp.bfloat16)
+            mix = jnp.dot(expo, values, preferred_element_type=jnp.float32)
+            mix = (mix[:, :HEAD_DIM] / mix[:, HEAD_DIM:]).astype(jnp.bfloat16)
+            for at in range(len(query)):
+                block = mix[at * rows : (at + 1) * rows]
+                out[where_ref[NEAR] ^ (first + at), :, lanes] = block
 
 
 def attend_half(where, half, pieces):
@@ -597,7 +602,7 @@
     blocks = []
     for keep, send in terms:
         total = add(where, keep, swap(send, "sub", 2, 1))
-        blocks.append([total[0]] + [swap(total[rel], "patch", 4, rel) for rel in (2, 3, 1)])
+        blocks.append([total[0]] + [swap(total[rel], "patch", 4, rel) for rel in range(3, 0, -1)])
     return mix_columns(where, hidden_in, attn_gate, blocks)
 
 
@@ -605,7 +610,7 @@
     blocks, out_ref = refs[:-1], refs[-1]
     cols = blocks[0].shape[1]
     for chunk in range(2):
-        for at, rel in enumerate((0, 2, 3, 1)):
+        for at, rel in enumerate((0, 3, 2, 1)):
             start = (2 * (where_ref[PATCH] ^ rel) + chunk) * cols
             lanes = pl.ds(pl.multiple_of(start, HEAD_DIM), cols)
             mixed = hidden_ref[:, lanes].astype(jnp.float32) + gate_ref[:, lanes] * blocks[

time: 106 us -> 107 us (level)
  starting transfers between devices: 32.2 us -> 33.5 us
    ppermute x20, starting transfers between devices: 29.6 us -> 30.9 us  [swap(): return lax.ppermute(x, axes, pairs)]
where the time goes in v22:
time: 107 us
  waiting for transfers between devices  47.9 us (45%)
  starting transfers between devices  33.5 us (31%)
  Pallas kernels  22.9 us (21%)
  local copies, waits for them, and re-layouts  2.32 us (2%)
    ppermute x20, waiting for transfers between devices, swap(): return lax.ppermute(x, axes, pairs)  43.7 us
    ppermute x20, starting transfers between devices, swap(): return lax.ppermute(x, axes, pairs)  30.9 us
    pallas_call x2, Pallas kernels, attend_half(): call(functools.partial(attend_half_kernel, half), 'attend', out, 1, [spec...  4.64 us
    ppermute x2, waiting for transfers between devices, share_tail(): ends = lax.ppermute(far, 'patch', [(1, 0), (2, 3)])  4.24 us
    pallas_call x1, Pallas kernels, first_product(): call(first_kernel, 'first', jax.ShapeDtypeStruct(acc.shape, jnp.float32),...  3.96 us
    pallas_call x2, Pallas kernels, add_product(): call(functools.partial(add_product_kernel, len(rels)), 'products', jax.Sh...  3.79 us
    pallas_call x1, Pallas kernels, pack(): pl.pallas_call(functools.partial(pack_kernel, split, feat // HEAD_DIM), o...  3.53 us
    ppermute x2, starting transfers between devices, share_tail(): ends = lax.ppermute(far, 'patch', [(1, 0), (2, 3)])  2.58 us
  transfers between devices with their start and end apart: 22, of which 10 were waited for; matrix products, arithmetic and copies ran while one was open for 0% of the time, Pallas kernels for 15%

profile of v22, /device:TPU:0, one launch (start us, length us, event | category | flops | bytes accessed | tf_op | source)
XLA Modules:
  0.0 106.8 jit_solution(10115645092709134690)
XLA Ops:
  0.0 3.5 %pack.1 = (bf16[3,256,256]{2,1,0:T(8,128)(2,1)}, bf16[3,256,256]{2,1,0:T(8,128)(2,1)}, bf16[3,256,256]{2,1,0:T(8,128)(2,1)}) custom-call(s32[2,2,8]{2,1,0:T(2,128)} %exps_ref.3, bf16[256,1024]{1,0:T(8,128)(2,1)} %q_ref.3, bf16[2,256,1024]{2,1,0:T(8,128)(2,1)} %fresh_ref.3, bf16[2,1024,1024]{2,1,0:T(8,128)(2,1)} %cached_ref.3), custom_call_target="tpu_custom_call" | custom-call | tf_op jit(solution)/shard_map/pack/pallas_call | solution.py:116
  3.6 0.0 copy-start.3
  3.6 0.1 stack.31.where_ref
  3.7 0.7 take.1
  4.4 3.0 %collective-permute-start = (bf16[512,1280]{1,0:T(8,128)(2,1)S(1)}, bf16[512,1280]{1,0:T(8,128)(2,1)S(1)}, u32[]{:S(2)}, u32[]{:S(2)}) collective-permute-start(bf16[512,1280]{1,0:T(8,128)(2,1)S(1)} %take.1), channel_id=1, source_target_pairs={{0,2},{2,0},{1,3},{3,1},{4,6},{6,4},{5,7},{7,5},{8,10},{10,8},{9,1... | collective-permute-start | bytes 3932168 | tf_op jit(solution)/shard_map/ppermute | solution.py:50
  7.4 2.6 %collective-permute-start.2 = (bf16[3,256,256]{2,1,0:T(8,128)(2,1)S(1)}, bf16[3,256,256]{2,1,0:T(8,128)(2,1)S(1)}, u32[]{:S(2)}, u32[]{:S(2)}) collective-permute-start(bf16[3,256,256]{2,1,0:T(8,128)(2,1)S(1)} %copy-done.9), channel_id=1, source_target_pairs={{0,8},{4,12},{8,0},{12,4},{1,9},{5,13},{9,1},{13,5},{2,10},{6,14},... | collective-permute-start | bytes 1179656 | tf_op jit(solution)/shard_map/ppermute | solution.py:50
  10.0 1.3 %collective-permute-start.3 = (bf16[3,256,256]{2,1,0:T(8,128)(2,1)S(1)}, bf16[3,256,256]{2,1,0:T(8,128)(2,1)S(1)}, u32[]{:S(2)}, u32[]{:S(2)}) collective-permute-start(bf16[3,256,256]{2,1,0:T(8,128)(2,1)S(1)} %copy-done.8), channel_id=1, source_target_pairs={{0,12},{4,8},{8,4},{12,0},{1,13},{5,9},{9,5},{13,1},{2,14},{6,10},... | collective-permute-start | bytes 1179656 | tf_op jit(solution)/shard_map/ppermute | solution.py:50
  11.3 0.3 collective-permute-start.1
  11.6 2.2 %copy-done.1 = bf16[2,1024,1024]{2,1,0:T(8,128)(2,1)S(1)} copy-done((bf16[2,1024,1024]{2,1,0:T(8,128)(2,1)S(1)}, bf16[2,1024,1024]{2,1,0:T(8,128)(2,1)}, u32[]{:S(2)}) %copy-start.1) | copy-done | bytes 4194328
  13.8 1.3 %own.1.refs_0_ = bf16[3,256,256]{2,1,0:T(8,128)(2,1)S(1)} custom-call(s32[6]{0:T(128)S(1)} %stack.31.where_ref, s32[2,2,8]{2,1,0:T(2,128)S(1)} %copy-done.6, bf16[256,1024]{1,0:T(8,128)(2,1)S(1)} %copy-done.3, bf16[2,256,1024]{2,1,0:T(8,128)(2,1)S(1)} %copy-done.2, bf16[2,1024,1024]{2,1,0:T(8,128)(2,1)S(1)} %copy-done.1), custom_call_target="tpu_custom_call" | custom-call | flops 1 | tf_op jit(solution)/shard_map/own/pallas_call | solution.py:152
  15.1 21.0 %collective-permute-done.refs_7_.fetched_ref = bf16[512,1280]{1,0:T(8,128)(2,1)S(1)} collective-permute-done((bf16[512,1280]{1,0:T(8,128)(2,1)S(1)}, bf16[512,1280]{1,0:T(8,128)(2,1)S(1)}, u32[]{:S(2)}, u32[]{:S(2)}) %collective-permute-start) | collective-permute-done | bytes 1310752 | tf_op jit(solution)/shard_map/ppermute | solution.py:50
  36.2 1.8 %collective-permute-start.11 = (bf16[512,1280]{1,0:T(8,128)(2,1)S(1)}, bf16[512,1280]{1,0:T(8,128)(2,1)S(1)}, u32[]{:S(2)}, u32[]{:S(2)}) collective-permute-start(bf16[512,1280]{1,0:T(8,128)(2,1)S(1)} %collective-permute-done.refs_7_.fetched_ref), channel_id=1, source_target_pairs={{0,16},{16,0},{1,17},{17,1},{2,18},{18,2},{3,19},{19,3},{4,20},{20... | collective-permute-start | bytes 3932168 | tf_op jit(solution)/shard_map/ppermute | solution.py:50
  37.9 2.3 %attend.2 = bf16[4,128,256]{2,1,0:T(8,128)(2,1)S(1)} custom-call(s32[6]{0:T(128)S(1)} %stack.31.where_ref, bf16[3,256,256]{2,1,0:T(8,128)(2,1)S(1)} %own.1.refs_0_, bf16[3,256,256]{2,1,0:T(8,128)(2,1)S(1)} %collective-permute-done.1.refs_1_, bf16[3,256,256]{2,1,0:T(8,128)(2,1)S(1)} %collective-permute-done.2.refs_2_, ...), custom_call_target="tpu_custom_call" | custom-call | flops 1 | tf_op jit(solution)/shard_map/attend/pallas_call | solution.py:415
  40.3 8.9 %collective-permute-start.8 = (bf16[512,256]{1,0:T(8,128)(2,1)S(1)}, bf16[512,256]{1,0:T(8,128)(2,1)S(1)}, u32[]{:S(2)}, u32[]{:S(2)}) collective-permute-start(bf16[512,256]{1,0:T(8,128)(2,1)S(1)} %bitcast.9), channel_id=1, source_target_pairs={{0,8},{4,12},{8,0},{12,4},{1,9},{5,13},{9,1},{13,5},{2,10},{6,14},... | collective-permute-start | bytes 786440 | tf_op jit(solution)/shard_map/ppermute | solution.py:50
  49.2 2.3 %attend.3 = bf16[4,128,256]{2,1,0:T(8,128)(2,1)S(1)} custom-call(s32[6]{0:T(128)S(1)} %stack.31.where_ref, bf16[3,256,256]{2,1,0:T(8,128)(2,1)S(1)} %own.1.refs_0_, bf16[3,256,256]{2,1,0:T(8,128)(2,1)S(1)} %collective-permute-done.1.refs_1_, bf16[3,256,256]{2,1,0:T(8,128)(2,1)S(1)} %collective-permute-done.2.refs_2_, ...), custom_call_target="tpu_custom_call" | custom-call | flops 1 | tf_op jit(solution)/shard_map/attend/pallas_call | solution.py:415
  51.5 0.6 collective-permute-start.4
  52.1 1.5 %products.2.refs_4_ = f32[512,1280]{1,0:T(8,128)S(1)} custom-call(s32[6]{0:T(128)S(1)} %stack.31.where_ref, bf16[512,256]{1,0:T(8,128)(2,1)S(1)} %bitcast.11, bf16[1024,1280]{1,0:T(8,128)(2,1)S(1)} %copy-done), custom_call_target="tpu_custom_call" | custom-call | flops 6000000000 | tf_op jit(solution)/shard_map/products/pallas_call | solution.py:440
  53.7 5.8 %collective-permute-done.4.refs_2_ = bf16[512,256]{1,0:T(8,128)(2,1)S(1)} collective-permute-done((bf16[512,256]{1,0:T(8,128)(2,1)S(1)}, bf16[512,256]{1,0:T(8,128)(2,1)S(1)}, u32[]{:S(2)}, u32[]{:S(2)}) %collective-permute-start.4) | collective-permute-done | bytes 262176 | tf_op jit(solution)/shard_map/ppermute | solution.py:50
  59.5 0.7 collective-permute-start.6
  60.2 1.4 %collective-permute-start.5 = (bf16[512,256]{1,0:T(8,128)(2,1)S(1)}, bf16[512,256]{1,0:T(8,128)(2,1)S(1)}, u32[]{:S(2)}, u32[]{:S(2)}) collective-permute-start(bf16[512,256]{1,0:T(8,128)(2,1)S(1)} %collective-permute-done.4.refs_2_), channel_id=1, source_target_pairs={{0,4},{4,0},{8,12},{12,8},{1,5},{5,1},{9,13},{13,9},{2,6},{6,2},{1... | collective-permute-start | bytes 786440 | tf_op jit(solution)/shard_map/ppermute | solution.py:50
  61.6 2.9 %collective-permute-done.7.refs_1_ = bf16[512,256]{1,0:T(8,128)(2,1)S(1)} collective-permute-done((bf16[512,256]{1,0:T(8,128)(2,1)S(1)}, bf16[512,256]{1,0:T(8,128)(2,1)S(1)}, u32[]{:S(2)}, u32[]{:S(2)}) %collective-permute-start.7) | collective-permute-done | bytes 262176 | tf_op jit(solution)/shard_map/ppermute | solution.py:50
  64.5 0.7 collective-permute-start.12
  65.1 1.3 %collective-permute-start.13 = (bf16[512,256]{1,0:T(8,128)(2,1)S(1)}, bf16[512,256]{1,0:T(8,128)(2,1)S(1)}, u32[]{:S(2)}, u32[]{:S(2)}) collective-permute-start(bf16[512,256]{1,0:T(8,128)(2,1)S(1)} %collective-permute-done.8.refs_0_), channel_id=1, source_target_pairs={{4,0},{8,12},{5,1},{9,13},{6,2},{10,14},{7,3},{11,15},{20,16},{24,... | collective-permute-start | bytes 786440 | tf_op jit(solution)/shard_map/ppermute | solution.py:596
  66.4 2.2 %products.3.refs_5_ = f32[512,1280]{1,0:T(8,128)S(1)} custom-call(s32[6]{0:T(128)S(1)} %stack.31.where_ref, bf16[512,256]{1,0:T(8,128)(2,1)S(1)} %collective-permute-done.8.refs_0_, bf16[512,256]{1,0:T(8,128)(2,1)S(1)} %collective-permute-done.7.refs_1_, bf16[1024,1280]{1,0:T(8,128)(2,1)S(1)} %copy-done, bf16[1024,1280]{1,0:T(8,128)(2,1)S(1)} %copy-done, ...), custom_call_target="tpu_custom_call" | custom-call | flops 1 | tf_op jit(solution)/shard_map/products/pallas_call | solution.py:440
  68.7 5.5 %collective-permute-done.6.refs_3_ = bf16[512,256]{1,0:T(8,128)(2,1)S(1)} collective-permute-done((bf16[512,256]{1,0:T(8,128)(2,1)S(1)}, bf16[512,256]{1,0:T(8,128)(2,1)S(1)}, u32[]{:S(2)}, u32[]{:S(2)}) %collective-permute-start.6) | collective-permute-done | bytes 262176 | tf_op jit(solution)/shard_map/ppermute | solution.py:50
  74.1 0.6 collective-permute-done.5.refs_4_
  74.7 0.7 collective-permute-start.9
  75.4 1.3 %collective-permute-start.10 = (bf16[512,256]{1,0:T(8,128)(2,1)S(1)}, bf16[512,256]{1,0:T(8,128)(2,1)S(1)}, u32[]{:S(2)}, u32[]{:S(2)}) collective-permute-start(bf16[512,256]{1,0:T(8,128)(2,1)S(1)} %collective-permute-done.6.refs_3_), channel_id=1, source_target_pairs={{4,0},{8,12},{5,1},{9,13},{6,2},{10,14},{7,3},{11,15},{20,16},{24,... | collective-permute-start | bytes 786440 | tf_op jit(solution)/shard_map/ppermute | solution.py:596
  76.7 3.6 %collective-permute-done.13.refs_1_ = bf16[512,256]{1,0:T(8,128)(2,1)S(1)} collective-permute-done((bf16[512,256]{1,0:T(8,128)(2,1)S(1)}, bf16[512,256]{1,0:T(8,128)(2,1)S(1)}, u32[]{:S(2)}, u32[]{:S(2)}) %collective-permute-start.13) | collective-permute-done | bytes 262176 | tf_op jit(solution)/shard_map/ppermute | solution.py:596
  80.3 4.0 %first.1.acc_in = f32[512,1280]{1,0:T(8,128)S(1)} custom-call(s32[6]{0:T(128)S(1)} %stack.31.where_ref, bf16[512,256]{1,0:T(8,128)(2,1)S(1)} %collective-permute-done.12.refs_0_, bf16[512,256]{1,0:T(8,128)(2,1)S(1)} %collective-permute-done.13.refs_1_, bf16[512,256]{1,0:T(8,128)(2,1)S(1)} %collective-permute-done.4.refs_2_, ...), custom_call_target="tpu_custom_call" | custom-call | flops 1 | tf_op jit(solution)/shard_map/first/pallas_call | solution.py:488
  84.3 0.6 collective-permute-done.10.more
  84.9 1.1 %second.3 = (bf16[4,64,640]{2,1,0:T(8,128)(2,1)S(1)}, bf16[4,64,640]{2,1,0:T(8,128)(2,1)S(1)}) custom-call(s32[6]{0:T(128)S(1)} %stack.31.where_ref, bf16[512,256]{1,0:T(8,128)(2,1)S(1)} %collective-permute-done.9.slot, bf16[512,256]{1,0:T(8,128)(2,1)S(1)} %collective-permute-done.10.more, bf16[512,1280]{1,0:T(8,128)(2,1)S(1)} %collective-permute-done.refs_7_.fetched_ref, ...), custom_call_target="tpu_custom_call" | custom-call | flops 1 | tf_op jit(solution)/shard_map/second/pallas_call | solution.py:529
  86.1 0.0 copy-start.5
  86.1 0.1 collective-permute-start.18
  86.1 1.1 %second.2 = (bf16[4,64,640]{2,1,0:T(8,128)(2,1)S(1)}, bf16[4,64,640]{2,1,0:T(8,128)(2,1)S(1)}) custom-call(s32[6]{0:T(128)S(1)} %stack.31.where_ref, bf16[512,256]{1,0:T(8,128)(2,1)S(1)} %collective-permute-done.9.slot, bf16[512,256]{1,0:T(8,128)(2,1)S(1)} %collective-permute-done.10.more, bf16[512,1280]{1,0:T(8,128)(2,1)S(1)} %collective-permute-done.refs_7_.fetched_ref, ...), custom_call_target="tpu_custom_call" | custom-call | flops 1 | tf_op jit(solution)/shard_map/second/pallas_call | solution.py:529
  87.3 0.6 collective-permute-start.14
  87.8 0.6 add.8
  88.4 1.2 %collective-permute-start.19 = (bf16[64,640]{1,0:T(8,128)(2,1)S(1)}, bf16[64,640]{1,0:T(8,128)(2,1)S(1)}, u32[]{:S(2)}, u32[]{:S(2)}) collective-permute-start(bf16[64,640]{1,0:T(8,128)(2,1)S(1)} %get-tuple-element.68), channel_id=1, source_target_pairs={{0,12},{4,8},{8,4},{12,0},{1,13},{5,9},{9,5},{13,1},{2,14},{6,10},... | collective-permute-start | bytes 245768 | tf_op jit(solution)/shard_map/ppermute | solution.py:50
  89.7 0.3 collective-permute-start.20
  90.0 2.9 %collective-permute-start.21 = (bf16[64,640]{1,0:T(8,128)(2,1)S(1)}, bf16[64,640]{1,0:T(8,128)(2,1)S(1)}, u32[]{:S(2)}, u32[]{:S(2)}) collective-permute-start(bf16[64,640]{1,0:T(8,128)(2,1)S(1)} %get-tuple-element.70), channel_id=1, source_target_pairs={{0,4},{4,0},{8,12},{12,8},{1,5},{5,1},{9,13},{13,9},{2,6},{6,2},{1... | collective-permute-start | bytes 245768 | tf_op jit(solution)/shard_map/ppermute | solution.py:50
  92.9 0.6 add.7
  93.5 1.2 %collective-permute-start.15 = (bf16[64,640]{1,0:T(8,128)(2,1)S(1)}, bf16[64,640]{1,0:T(8,128)(2,1)S(1)}, u32[]{:S(2)}, u32[]{:S(2)}) collective-permute-start(bf16[64,640]{1,0:T(8,128)(2,1)S(1)} %get-tuple-element.62), channel_id=1, source_target_pairs={{0,12},{4,8},{8,4},{12,0},{1,13},{5,9},{9,5},{13,1},{2,14},{6,10},... | collective-permute-start | bytes 245768 | tf_op jit(solution)/shard_map/ppermute | solution.py:50
  94.8 0.3 collective-permute-start.16
  95.1 0.6 collective-permute-done.19.refs_5_
  95.7 2.3 %collective-permute-start.17 = (bf16[64,640]{1,0:T(8,128)(2,1)S(1)}, bf16[64,640]{1,0:T(8,128)(2,1)S(1)}, u32[]{:S(2)}, u32[]{:S(2)}) collective-permute-start(bf16[64,640]{1,0:T(8,128)(2,1)S(1)} %get-tuple-element.64), channel_id=1, source_target_pairs={{0,4},{4,0},{8,12},{12,8},{1,5},{5,1},{9,13},{13,9},{2,6},{6,2},{1... | collective-permute-start | bytes 245768 | tf_op jit(solution)/shard_map/ppermute | solution.py:50
  98.0 3.0 %collective-permute-done.20.refs_6_ = bf16[64,640]{1,0:T(8,128)(2,1)S(1)} collective-permute-done((bf16[64,640]{1,0:T(8,128)(2,1)S(1)}, bf16[64,640]{1,0:T(8,128)(2,1)S(1)}, u32[]{:S(2)}, u32[]{:S(2)}) %collective-permute-start.20) | collective-permute-done | bytes 81952 | tf_op jit(solution)/shard_map/ppermute | solution.py:50
  101.0 4.2 %collective-permute-done.16.refs_2_ = bf16[64,640]{1,0:T(8,128)(2,1)S(1)} collective-permute-done((bf16[64,640]{1,0:T(8,128)(2,1)S(1)}, bf16[64,640]{1,0:T(8,128)(2,1)S(1)}, u32[]{:S(2)}, u32[]{:S(2)}) %collective-permute-start.16) | collective-permute-done | bytes 81952 | tf_op jit(solution)/shard_map/ppermute | solution.py:50
  105.3 1.6 %mix.1 = bf16[64,5120]{1,0:T(8,128)(2,1)} custom-call(s32[6]{0:T(128)S(1)} %stack.31.where_ref, bf16[64,5120]{1,0:T(8,128)(2,1)S(1)} %copy-done.4, f32[1,5120]{1,0:T(1,128)S(1)} %bitcast.14, bf16[64,640]{1,0:T(8,128)(2,1)S(1)} %get-tuple-element.61.refs_0_, bf16[64,640]{1,0:T(8,128)(2,1)S(1)} %collective-permute-done.15.refs_1_, ...), custom_call_target="tpu_custom_call" | custom-call | flops 1 | tf_op jit(solution)/shard_map/mix/pallas_call | solution.py:625
  (30 shorter events, 0.1 us)
Async XLA Ops:
  0.0 3.7 %copy-start = (bf16[1024,1280]{1,0:T(8,128)(2,1)S(1)}, bf16[1024,1280]{1,0:T(8,128)(2,1)}, u32[]{:S(2)}) copy-start(bf16[1024,1280]{1,0:T(8,128)(2,1)} %refs_6_) | copy-start | bytes 7864324
  3.5 7.8 %copy-start.7 = (bf16[3,256,256]{2,1,0:T(8,128)(2,1)S(1)}, bf16[3,256,256]{2,1,0:T(8,128)(2,1)}, u32[]{:S(2)}) copy-start(bf16[3,256,256]{2,1,0:T(8,128)(2,1)} %get-tuple-element.40) | copy-start | bytes 1179652
  3.6 8.1 %copy-start.3 = (bf16[256,1024]{1,0:T(8,128)(2,1)S(1)}, bf16[256,1024]{1,0:T(8,128)(2,1)}, u32[]{:S(2)}) copy-start(bf16[256,1024]{1,0:T(8,128)(2,1)} %q_ref.3) | copy-start | bytes 1572868
  3.6 8.1 %copy-start.6 = (s32[2,2,8]{2,1,0:T(2,128)S(1)}, s32[2,2,8]{2,1,0:T(2,128)}, u32[]{:S(2)}) copy-start(s32[2,2,8]{2,1,0:T(2,128)} %exps_ref.3) | copy-start | bytes 388
  3.7 3.7 %copy-start.9 = (bf16[3,256,256]{2,1,0:T(8,128)(2,1)S(1)}, bf16[3,256,256]{2,1,0:T(8,128)(2,1)}, u32[]{:S(2)}) copy-start(bf16[3,256,256]{2,1,0:T(8,128)(2,1)} %get-tuple-element.38) | copy-start | bytes 1179652
  3.7 6.3 %copy-start.8 = (bf16[3,256,256]{2,1,0:T(8,128)(2,1)S(1)}, bf16[3,256,256]{2,1,0:T(8,128)(2,1)}, u32[]{:S(2)}) copy-start(bf16[3,256,256]{2,1,0:T(8,128)(2,1)} %get-tuple-element.39) | copy-start | bytes 1179652
  3.7 8.0 %copy-start.2 = (bf16[2,256,1024]{2,1,0:T(8,128)(2,1)S(1)}, bf16[2,256,1024]{2,1,0:T(8,128)(2,1)}, u32[]{:S(2)}) copy-start(bf16[2,256,1024]{2,1,0:T(8,128)(2,1)} %fresh_ref.3) | copy-start | bytes 3145732
  4.4 31.8 %collective-permute-start = (bf16[512,1280]{1,0:T(8,128)(2,1)S(1)}, bf16[512,1280]{1,0:T(8,128)(2,1)S(1)}, u32[]{:S(2)}, u32[]{:S(2)}) collective-permute-start(bf16[512,1280]{1,0:T(8,128)(2,1)S(1)} %take.1), channel_id=1, source_target_pairs={{0,2},{2,0},{1,3},{3,1},{4,6},{6,4},{5,7},{7,5},{8,10},{10,8},{9,1... | collective-permute-start | bytes 3932168 | tf_op jit(solution)/shard_map/ppermute | solution.py:50
  7.4 30.5 %collective-permute-start.2 = (bf16[3,256,256]{2,1,0:T(8,128)(2,1)S(1)}, bf16[3,256,256]{2,1,0:T(8,128)(2,1)S(1)}, u32[]{:S(2)}, u32[]{:S(2)}) collective-permute-start(bf16[3,256,256]{2,1,0:T(8,128)(2,1)S(1)} %copy-done.9), channel_id=1, source_target_pairs={{0,8},{4,12},{8,0},{12,4},{1,9},{5,13},{9,1},{13,5},{2,10},{6,14},... | collective-permute-start | bytes 1179656 | tf_op jit(solution)/shard_map/ppermute | solution.py:50
  10.0 28.0 %collective-permute-start.3 = (bf16[3,256,256]{2,1,0:T(8,128)(2,1)S(1)}, bf16[3,256,256]{2,1,0:T(8,128)(2,1)S(1)}, u32[]{:S(2)}, u32[]{:S(2)}) collective-permute-start(bf16[3,256,256]{2,1,0:T(8,128)(2,1)S(1)} %copy-done.8), channel_id=1, source_target_pairs={{0,12},{4,8},{8,4},{12,0},{1,13},{5,9},{9,5},{13,1},{2,14},{6,10},... | collective-permute-start | bytes 1179656 | tf_op jit(solution)/shard_map/ppermute | solution.py:50
  11.3 26.6 %collective-permute-start.1 = (bf16[3,256,256]{2,1,0:T(8,128)(2,1)S(1)}, bf16[3,256,256]{2,1,0:T(8,128)(2,1)S(1)}, u32[]{:S(2)}, u32[]{:S(2)}) collective-permute-start(bf16[3,256,256]{2,1,0:T(8,128)(2,1)S(1)} %copy-done.7), channel_id=1, source_target_pairs={{0,4},{4,0},{8,12},{12,8},{1,5},{5,1},{9,13},{13,9},{2,6},{6,2},{1... | collective-permute-start | bytes 1179656 | tf_op jit(solution)/shard_map/ppermute | solution.py:50
  11.6 2.2 %copy-start.1 = (bf16[2,1024,1024]{2,1,0:T(8,128)(2,1)S(1)}, bf16[2,1024,1024]{2,1,0:T(8,128)(2,1)}, u32[]{:S(2)}) copy-start(bf16[2,1024,1024]{2,1,0:T(8,128)(2,1)} %cached_ref.3) | copy-start | bytes 12582916
  36.2 44.2 %collective-permute-start.11 = (bf16[512,1280]{1,0:T(8,128)(2,1)S(1)}, bf16[512,1280]{1,0:T(8,128)(2,1)S(1)}, u32[]{:S(2)}, u32[]{:S(2)}) collective-permute-start(bf16[512,1280]{1,0:T(8,128)(2,1)S(1)} %collective-permute-done.refs_7_.fetched_ref), channel_id=1, source_target_pairs={{0,16},{16,0},{1,17},{17,1},{2,18},{18,2},{3,19},{19,3},{4,20},{20... | collective-permute-start | bytes 3932168 | tf_op jit(solution)/shard_map/ppermute | solution.py:50
  40.3 21.3 %collective-permute-start.8 = (bf16[512,256]{1,0:T(8,128)(2,1)S(1)}, bf16[512,256]{1,0:T(8,128)(2,1)S(1)}, u32[]{:S(2)}, u32[]{:S(2)}) collective-permute-start(bf16[512,256]{1,0:T(8,128)(2,1)S(1)} %bitcast.9), channel_id=1, source_target_pairs={{0,8},{4,12},{8,0},{12,4},{1,9},{5,13},{9,1},{13,5},{2,10},{6,14},... | collective-permute-start | bytes 786440 | tf_op jit(solution)/shard_map/ppermute | solution.py:50
  49.2 15.3 %collective-permute-start.7 = (bf16[512,256]{1,0:T(8,128)(2,1)S(1)}, bf16[512,256]{1,0:T(8,128)(2,1)S(1)}, u32[]{:S(2)}, u32[]{:S(2)}) collective-permute-start(bf16[512,256]{1,0:T(8,128)(2,1)S(1)} %bitcast.10), channel_id=1, source_target_pairs={{0,4},{4,0},{8,12},{12,8},{1,5},{5,1},{9,13},{13,9},{2,6},{6,2},{1... | collective-permute-start | bytes 786440 | tf_op jit(solution)/shard_map/ppermute | solution.py:50
  51.5 8.0 %collective-permute-start.4 = (bf16[512,256]{1,0:T(8,128)(2,1)S(1)}, bf16[512,256]{1,0:T(8,128)(2,1)S(1)}, u32[]{:S(2)}, u32[]{:S(2)}) collective-permute-start(bf16[512,256]{1,0:T(8,128)(2,1)S(1)} %bitcast.13), channel_id=1, source_target_pairs={{0,2},{2,0},{1,3},{3,1},{4,6},{6,4},{5,7},{7,5},{8,10},{10,8},{9,1... | collective-permute-start | bytes 786440 | tf_op jit(solution)/shard_map/ppermute | solution.py:50
  59.5 14.6 %collective-permute-start.6 = (bf16[512,256]{1,0:T(8,128)(2,1)S(1)}, bf16[512,256]{1,0:T(8,128)(2,1)S(1)}, u32[]{:S(2)}, u32[]{:S(2)}) collective-permute-start(bf16[512,256]{1,0:T(8,128)(2,1)S(1)} %collective-permute-done.4.refs_2_), channel_id=1, source_target_pairs={{0,8},{4,12},{8,0},{12,4},{1,9},{5,13},{9,1},{13,5},{2,10},{6,14},... | collective-permute-start | bytes 786440 | tf_op jit(solution)/shard_map/ppermute | solution.py:50
  60.2 14.5 %collective-permute-start.5 = (bf16[512,256]{1,0:T(8,128)(2,1)S(1)}, bf16[512,256]{1,0:T(8,128)(2,1)S(1)}, u32[]{:S(2)}, u32[]{:S(2)}) collective-permute-start(bf16[512,256]{1,0:T(8,128)(2,1)S(1)} %collective-permute-done.4.refs_2_), channel_id=1, source_target_pairs={{0,4},{4,0},{8,12},{12,8},{1,5},{5,1},{9,13},{13,9},{2,6},{6,2},{1... | collective-permute-start | bytes 786440 | tf_op jit(solution)/shard_map/ppermute | solution.py:50
  64.5 12.2 %collective-permute-start.12 = (bf16[512,256]{1,0:T(8,128)(2,1)S(1)}, bf16[512,256]{1,0:T(8,128)(2,1)S(1)}, u32[]{:S(2)}, u32[]{:S(2)}) collective-permute-start(bf16[512,256]{1,0:T(8,128)(2,1)S(1)} %bitcast.12), channel_id=1, source_target_pairs={{4,8},{8,4},{5,9},{9,5},{6,10},{10,6},{7,11},{11,7},{20,24},{24,20... | collective-permute-start | bytes 786440 | tf_op jit(solution)/shard_map/ppermute | solution.py:50
  65.1 15.2 %collective-permute-start.13 = (bf16[512,256]{1,0:T(8,128)(2,1)S(1)}, bf16[512,256]{1,0:T(8,128)(2,1)S(1)}, u32[]{:S(2)}, u32[]{:S(2)}) collective-permute-start(bf16[512,256]{1,0:T(8,128)(2,1)S(1)} %collective-permute-done.8.refs_0_), channel_id=1, source_target_pairs={{4,0},{8,12},{5,1},{9,13},{6,2},{10,14},{7,3},{11,15},{20,16},{24,... | collective-permute-start | bytes 786440 | tf_op jit(solution)/shard_map/ppermute | solution.py:596
  74.7 9.6 %collective-permute-start.9 = (bf16[512,256]{1,0:T(8,128)(2,1)S(1)}, bf16[512,256]{1,0:T(8,128)(2,1)S(1)}, u32[]{:S(2)}, u32[]{:S(2)}) collective-permute-start(bf16[512,256]{1,0:T(8,128)(2,1)S(1)} %collective-permute-done.4.refs_2_), channel_id=1, source_target_pairs={{4,8},{8,4},{5,9},{9,5},{6,10},{10,6},{7,11},{11,7},{20,24},{24,20... | collective-permute-start | bytes 786440 | tf_op jit(solution)/shard_map/ppermute | solution.py:50
  75.4 9.5 %collective-permute-start.10 = (bf16[512,256]{1,0:T(8,128)(2,1)S(1)}, bf16[512,256]{1,0:T(8,128)(2,1)S(1)}, u32[]{:S(2)}, u32[]{:S(2)}) collective-permute-start(bf16[512,256]{1,0:T(8,128)(2,1)S(1)} %collective-permute-done.6.refs_3_), channel_id=1, source_target_pairs={{4,0},{8,12},{5,1},{9,13},{6,2},{10,14},{7,3},{11,15},{20,16},{24,... | collective-permute-start | bytes 786440 | tf_op jit(solution)/shard_map/ppermute | solution.py:596
  86.0 19.2 %copy-start.4 = (bf16[64,5120]{1,0:T(8,128)(2,1)S(1)}, bf16[64,5120]{1,0:T(8,128)(2,1)}, u32[]{:S(2)}) copy-start(bf16[64,5120]{1,0:T(8,128)(2,1)} %hidden_ref.1) | copy-start | bytes 1966084
  86.1 19.2 %copy-start.5 = (f32[5120]{0:T(1024)S(1)}, f32[5120]{0:T(1024)}, u32[]{:S(2)}) copy-start(f32[5120]{0:T(1024)} %param.13) | copy-start | bytes 61444
  86.1 1.8 %collective-permute-start.18 = (bf16[4,64,640]{2,1,0:T(8,128)(2,1)S(1)}, bf16[4,64,640]{2,1,0:T(8,128)(2,1)S(1)}, u32[]{:S(2)}, u32[]{:S(2)}) collective-permute-start(bf16[4,64,640]{2,1,0:T(8,128)(2,1)S(1)} %get-tuple-element.66), channel_id=1, source_target_pairs={{0,1},{1,0},{2,3},{3,2},{4,5},{5,4},{6,7},{7,6},{8,9},{9,8},{10,11... | collective-permute-start | bytes 983048 | tf_op jit(solution)/shard_map/ppermute | solution.py:50
  87.3 5.6 %collective-permute-start.14 = (bf16[4,64,640]{2,1,0:T(8,128)(2,1)S(1)}, bf16[4,64,640]{2,1,0:T(8,128)(2,1)S(1)}, u32[]{:S(2)}, u32[]{:S(2)}) collective-permute-start(bf16[4,64,640]{2,1,0:T(8,128)(2,1)S(1)} %get-tuple-element.60), channel_id=1, source_target_pairs={{0,1},{1,0},{2,3},{3,2},{4,5},{5,4},{6,7},{7,6},{8,9},{9,8},{10,11... | collective-permute-start | bytes 983048 | tf_op jit(solution)/shard_map/ppermute | solution.py:50
  88.4 7.3 %collective-permute-start.19 = (bf16[64,640]{1,0:T(8,128)(2,1)S(1)}, bf16[64,640]{1,0:T(8,128)(2,1)S(1)}, u32[]{:S(2)}, u32[]{:S(2)}) collective-permute-start(bf16[64,640]{1,0:T(8,128)(2,1)S(1)} %get-tuple-element.68), channel_id=1, source_target_pairs={{0,12},{4,8},{8,4},{12,0},{1,13},{5,9},{9,5},{13,1},{2,14},{6,10},... | collective-permute-start | bytes 245768 | tf_op jit(solution)/shard_map/ppermute | solution.py:50
  89.7 11.3 %collective-permute-start.20 = (bf16[64,640]{1,0:T(8,128)(2,1)S(1)}, bf16[64,640]{1,0:T(8,128)(2,1)S(1)}, u32[]{:S(2)}, u32[]{:S(2)}) collective-permute-start(bf16[64,640]{1,0:T(8,128)(2,1)S(1)} %get-tuple-element.69), channel_id=1, source_target_pairs={{0,8},{4,12},{8,0},{12,4},{1,9},{5,13},{9,1},{13,5},{2,10},{6,14},... | collective-permute-start | bytes 245768 | tf_op jit(solution)/shard_map/ppermute | solution.py:50
  90.0 11.1 %collective-permute-start.21 = (bf16[64,640]{1,0:T(8,128)(2,1)S(1)}, bf16[64,640]{1,0:T(8,128)(2,1)S(1)}, u32[]{:S(2)}, u32[]{:S(2)}) collective-permute-start(bf16[64,640]{1,0:T(8,128)(2,1)S(1)} %get-tuple-element.70), channel_id=1, source_target_pairs={{0,4},{4,0},{8,12},{12,8},{1,5},{5,1},{9,13},{13,9},{2,6},{6,2},{1... | collective-permute-start | bytes 245768 | tf_op jit(solution)/shard_map/ppermute | solution.py:50
  93.5 7.5 %collective-permute-start.15 = (bf16[64,640]{1,0:T(8,128)(2,1)S(1)}, bf16[64,640]{1,0:T(8,128)(2,1)S(1)}, u32[]{:S(2)}, u32[]{:S(2)}) collective-permute-start(bf16[64,640]{1,0:T(8,128)(2,1)S(1)} %get-tuple-element.62), channel_id=1, source_target_pairs={{0,12},{4,8},{8,4},{12,0},{1,13},{5,9},{9,5},{13,1},{2,14},{6,10},... | collective-permute-start | bytes 245768 | tf_op jit(solution)/shard_map/ppermute | solution.py:50
  94.8 10.5 %collective-permute-start.16 = (bf16[64,640]{1,0:T(8,128)(2,1)S(1)}, bf16[64,640]{1,0:T(8,128)(2,1)S(1)}, u32[]{:S(2)}, u32[]{:S(2)}) collective-permute-start(bf16[64,640]{1,0:T(8,128)(2,1)S(1)} %get-tuple-element.63), channel_id=1, source_target_pairs={{0,8},{4,12},{8,0},{12,4},{1,9},{5,13},{9,1},{13,5},{2,10},{6,14},... | collective-permute-start | bytes 245768 | tf_op jit(solution)/shard_map/ppermute | solution.py:50
  95.7 9.6 %collective-permute-start.17 = (bf16[64,640]{1,0:T(8,128)(2,1)S(1)}, bf16[64,640]{1,0:T(8,128)(2,1)S(1)}, u32[]{:S(2)}, u32[]{:S(2)}) collective-permute-start(bf16[64,640]{1,0:T(8,128)(2,1)S(1)} %get-tuple-element.64), channel_id=1, source_target_pairs={{0,4},{4,0},{8,12},{12,8},{1,5},{5,1},{9,13},{13,9},{2,6},{6,2},{1... | collective-permute-start | bytes 245768 | tf_op jit(solution)/shard_map/ppermute | solution.py:50

commit v23 on v18

--- a/solution.py
+++ b/solution.py
@@ -11,7 +11,7 @@
 HEAD_DIM = 128
 SCALE_ROWS = 128
 SATURATION = 448.0
-PACK_ROWS = 64
+PACK_ROWS = 32
 VMEM_BYTES = 32 * 1024 * 1024
 PACK_VMEM_BYTES = 60 * 1024 * 1024
 ATTEND_FLOPS = 1
@@ -390,16 +390,18 @@
         keys = jnp.concatenate([ref[1, :, lanes] for ref in pieces], axis=0)
         values = jnp.concatenate([ref[2, :, lanes] for ref in pieces], axis=0)
         values = jnp.concatenate([values, jnp.ones_like(values)], axis=1)
-        query = jnp.concatenate([ref[0, pl.ds(start, rows), lanes] for ref in pieces], axis=0)
-        scores = lax.dot_general(
-            query, keys, (((1,), (1,)), ((), ())), preferred_element_type=jnp.float32
-        )
-        peak = jnp.max(scores, axis=1, keepdims=True)
-        expo = jnp.exp2((scores - peak) * factor).astype(jnp.bfloat16)
-        mix = jnp.dot(expo, values, preferred_element_type=jnp.float32)
-        mix = (mix[:, :HEAD_DIM] / mix[:, HEAD_DIM:]).astype(jnp.bfloat16)
-        for rel in range(len(pieces)):
-            out[where_ref[NEAR] ^ rel, :, lanes] = mix[rel * rows : (rel + 1) * rows]
+        for rel, ref in enumerate(pieces):
+            scores = lax.dot_general(
+                ref[0, pl.ds(start, rows), lanes],
+                keys,
+                (((1,), (1,)), ((), ())),
+                preferred_element_type=jnp.float32,
+            )
+            peak = jnp.max(scores, axis=1, keepdims=True)
+            expo = jnp.exp2((scores - peak) * factor).astype(jnp.bfloat16)
+            mix = jnp.dot(expo, values, preferred_element_type=jnp.float32)
+            mix = (mix[:, :HEAD_DIM] / mix[:, HEAD_DIM:]).astype(jnp.bfloat16)
+            out[where_ref[NEAR] ^ rel, :, lanes] = mix
 
 
 def attend_half(where, half, pieces):

time: 105 us -> 105 us (level)
  transfers between devices with their start and end apart: 22 -> 22, of which waited for: 10 -> 11; matrix products, arithmetic and copies ran while one was open for 0% -> 0% of each run, Pallas kernels for 16% -> 15%
where the time goes in v23:
time: 105 us
  waiting for transfers between devices  50.7 us (48%)
  starting transfers between devices  28.4 us (27%)
  Pallas kernels  23.1 us (22%)
  local copies, waits for them, and re-layouts  2.32 us (2%)
    ppermute x20, waiting for transfers between devices, swap(): return lax.ppermute(x, axes, pairs)  46.8 us
    ppermute x20, starting transfers between devices, swap(): return lax.ppermute(x, axes, pairs)  25.8 us
    pallas_call x2, Pallas kernels, attend_half(): call(functools.partial(attend_half_kernel, half), 'attend', out, 1, [spec...  4.62 us
    pallas_call x1, Pallas kernels, first_product(): call(first_kernel, 'first', jax.ShapeDtypeStruct(acc.shape, jnp.float32),...  3.96 us
    ppermute x2, waiting for transfers between devices, share_tail(): ends = lax.ppermute(far, 'patch', [(1, 0), (2, 3)])  3.88 us
    pallas_call x2, Pallas kernels, add_product(): call(functools.partial(add_product_kernel, len(rels)), 'products', jax.Sh...  3.79 us
    pallas_call x1, Pallas kernels, pack(): pl.pallas_call(functools.partial(pack_kernel, split, feat // HEAD_DIM), o...  3.71 us
    ppermute x2, starting transfers between devices, share_tail(): ends = lax.ppermute(far, 'patch', [(1, 0), (2, 3)])  2.58 us
  transfers between devices with their start and end apart: 22, of which 11 were waited for; matrix products, arithmetic and copies ran while one was open for 0% of the time, Pallas kernels for 15%

profile of v23, /device:TPU:0, one launch (start us, length us, event | category | flops | bytes accessed | tf_op | source)
XLA Modules:
  0.0 104.7 jit_solution(5883259824902862606)
XLA Ops:
  0.0 3.7 %pack.1 = (bf16[3,256,256]{2,1,0:T(8,128)(2,1)}, bf16[3,256,256]{2,1,0:T(8,128)(2,1)}, bf16[3,256,256]{2,1,0:T(8,128)(2,1)}) custom-call(s32[2,2,8]{2,1,0:T(2,128)} %exps_ref.3, bf16[256,1024]{1,0:T(8,128)(2,1)} %q_ref.3, bf16[2,256,1024]{2,1,0:T(8,128)(2,1)} %fresh_ref.3, bf16[2,1024,1024]{2,1,0:T(8,128)(2,1)} %cached_ref.3), custom_call_target="tpu_custom_call" | custom-call | tf_op jit(solution)/shard_map/pack/pallas_call | solution.py:114
  3.7 0.0 copy-start.3
  3.7 0.0 copy-start.6
  3.8 0.1 stack.31.where_ref
  3.9 0.7 take.1
  4.6 3.0 %collective-permute-start = (bf16[512,1280]{1,0:T(8,128)(2,1)S(1)}, bf16[512,1280]{1,0:T(8,128)(2,1)S(1)}, u32[]{:S(2)}, u32[]{:S(2)}) collective-permute-start(bf16[512,1280]{1,0:T(8,128)(2,1)S(1)} %take.1), channel_id=1, source_target_pairs={{0,2},{2,0},{1,3},{3,1},{4,6},{6,4},{5,7},{7,5},{8,10},{10,8},{9,1... | collective-permute-start | bytes 3932168 | tf_op jit(solution)/shard_map/ppermute | solution.py:50
  7.6 3.6 %collective-permute-start.3 = (bf16[3,256,256]{2,1,0:T(8,128)(2,1)S(1)}, bf16[3,256,256]{2,1,0:T(8,128)(2,1)S(1)}, u32[]{:S(2)}, u32[]{:S(2)}) collective-permute-start(bf16[3,256,256]{2,1,0:T(8,128)(2,1)S(1)} %copy-done.9), channel_id=1, source_target_pairs={{0,12},{4,8},{8,4},{12,0},{1,13},{5,9},{9,5},{13,1},{2,14},{6,10},... | collective-permute-start | bytes 1179656 | tf_op jit(solution)/shard_map/ppermute | solution.py:50
  11.2 0.8 collective-permute-start.1
  12.0 2.2 %copy-done.1 = bf16[2,1024,1024]{2,1,0:T(8,128)(2,1)S(1)} copy-done((bf16[2,1024,1024]{2,1,0:T(8,128)(2,1)S(1)}, bf16[2,1024,1024]{2,1,0:T(8,128)(2,1)}, u32[]{:S(2)}) %copy-start.1) | copy-done | bytes 4194328
  14.1 1.3 %own.1.refs_0_ = bf16[3,256,256]{2,1,0:T(8,128)(2,1)S(1)} custom-call(s32[6]{0:T(128)S(1)} %stack.31.where_ref, s32[2,2,8]{2,1,0:T(2,128)S(1)} %copy-done.6, bf16[256,1024]{1,0:T(8,128)(2,1)S(1)} %copy-done.3, bf16[2,256,1024]{2,1,0:T(8,128)(2,1)S(1)} %copy-done.2, bf16[2,1024,1024]{2,1,0:T(8,128)(2,1)S(1)} %copy-done.1), custom_call_target="tpu_custom_call" | custom-call | flops 1 | tf_op jit(solution)/shard_map/own/pallas_call | solution.py:150
  15.4 20.9 %collective-permute-done.refs_7_.fetched_ref = bf16[512,1280]{1,0:T(8,128)(2,1)S(1)} collective-permute-done((bf16[512,1280]{1,0:T(8,128)(2,1)S(1)}, bf16[512,1280]{1,0:T(8,128)(2,1)S(1)}, u32[]{:S(2)}, u32[]{:S(2)}) %collective-permute-start) | collective-permute-done | bytes 1310752 | tf_op jit(solution)/shard_map/ppermute | solution.py:50
  36.3 1.8 %collective-permute-start.11 = (bf16[512,1280]{1,0:T(8,128)(2,1)S(1)}, bf16[512,1280]{1,0:T(8,128)(2,1)S(1)}, u32[]{:S(2)}, u32[]{:S(2)}) collective-permute-start(bf16[512,1280]{1,0:T(8,128)(2,1)S(1)} %collective-permute-done.refs_7_.fetched_ref), channel_id=1, source_target_pairs={{0,16},{16,0},{1,17},{17,1},{2,18},{18,2},{3,19},{19,3},{4,20},{20... | collective-permute-start | bytes 3932168 | tf_op jit(solution)/shard_map/ppermute | solution.py:50
  38.1 6.3 %collective-permute-done.2.refs_2_ = bf16[3,256,256]{2,1,0:T(8,128)(2,1)S(1)} collective-permute-done((bf16[3,256,256]{2,1,0:T(8,128)(2,1)S(1)}, bf16[3,256,256]{2,1,0:T(8,128)(2,1)S(1)}, u32[]{:S(2)}, u32[]{:S(2)}) %collective-permute-start.2) | collective-permute-done | bytes 393248 | tf_op jit(solution)/shard_map/ppermute | solution.py:50
  44.4 2.3 %attend.2 = bf16[4,128,256]{2,1,0:T(8,128)(2,1)S(1)} custom-call(s32[6]{0:T(128)S(1)} %stack.31.where_ref, bf16[3,256,256]{2,1,0:T(8,128)(2,1)S(1)} %own.1.refs_0_, bf16[3,256,256]{2,1,0:T(8,128)(2,1)S(1)} %collective-permute-done.1.refs_1_, bf16[3,256,256]{2,1,0:T(8,128)(2,1)S(1)} %collective-permute-done.2.refs_2_, ...), custom_call_target="tpu_custom_call" | custom-call | flops 1 | tf_op jit(solution)/shard_map/attend/pallas_call | solution.py:410
  46.7 0.1 collective-permute-start.8
  46.8 3.0 %collective-permute-start.7 = (bf16[512,256]{1,0:T(8,128)(2,1)S(1)}, bf16[512,256]{1,0:T(8,128)(2,1)S(1)}, u32[]{:S(2)}, u32[]{:S(2)}) collective-permute-start(bf16[512,256]{1,0:T(8,128)(2,1)S(1)} %bitcast.10), channel_id=1, source_target_pairs={{0,4},{4,0},{8,12},{12,8},{1,5},{5,1},{9,13},{13,9},{2,6},{6,2},{1... | collective-permute-start | bytes 786440 | tf_op jit(solution)/shard_map/ppermute | solution.py:50
  49.8 2.3 %attend.3 = bf16[4,128,256]{2,1,0:T(8,128)(2,1)S(1)} custom-call(s32[6]{0:T(128)S(1)} %stack.31.where_ref, bf16[3,256,256]{2,1,0:T(8,128)(2,1)S(1)} %own.1.refs_0_, bf16[3,256,256]{2,1,0:T(8,128)(2,1)S(1)} %collective-permute-done.1.refs_1_, bf16[3,256,256]{2,1,0:T(8,128)(2,1)S(1)} %collective-permute-done.2.refs_2_, ...), custom_call_target="tpu_custom_call" | custom-call | flops 1 | tf_op jit(solution)/shard_map/attend/pallas_call | solution.py:410
  52.2 0.6 collective-permute-start.4
  52.8 1.5 %products.2.refs_4_ = f32[512,1280]{1,0:T(8,128)S(1)} custom-call(s32[6]{0:T(128)S(1)} %stack.31.where_ref, bf16[512,256]{1,0:T(8,128)(2,1)S(1)} %bitcast.11, bf16[1024,1280]{1,0:T(8,128)(2,1)S(1)} %copy-done), custom_call_target="tpu_custom_call" | custom-call | flops 6000000000 | tf_op jit(solution)/shard_map/products/pallas_call | solution.py:435
  54.3 4.3 %collective-permute-done.4.refs_2_ = bf16[512,256]{1,0:T(8,128)(2,1)S(1)} collective-permute-done((bf16[512,256]{1,0:T(8,128)(2,1)S(1)}, bf16[512,256]{1,0:T(8,128)(2,1)S(1)}, u32[]{:S(2)}, u32[]{:S(2)}) %collective-permute-start.4) | collective-permute-done | bytes 262176 | tf_op jit(solution)/shard_map/ppermute | solution.py:50
  58.6 0.6 collective-permute-start.6
  59.2 1.7 %collective-permute-start.5 = (bf16[512,256]{1,0:T(8,128)(2,1)S(1)}, bf16[512,256]{1,0:T(8,128)(2,1)S(1)}, u32[]{:S(2)}, u32[]{:S(2)}) collective-permute-start(bf16[512,256]{1,0:T(8,128)(2,1)S(1)} %collective-permute-done.4.refs_2_), channel_id=1, source_target_pairs={{0,4},{4,0},{8,12},{12,8},{1,5},{5,1},{9,13},{13,9},{2,6},{6,2},{1... | collective-permute-start | bytes 786440 | tf_op jit(solution)/shard_map/ppermute | solution.py:50
  60.9 0.1 collective-permute-done.8.refs_0_
  61.0 0.7 collective-permute-start.12
  61.7 1.3 %collective-permute-start.13 = (bf16[512,256]{1,0:T(8,128)(2,1)S(1)}, bf16[512,256]{1,0:T(8,128)(2,1)S(1)}, u32[]{:S(2)}, u32[]{:S(2)}) collective-permute-start(bf16[512,256]{1,0:T(8,128)(2,1)S(1)} %collective-permute-done.8.refs_0_), channel_id=1, source_target_pairs={{4,0},{8,12},{5,1},{9,13},{6,2},{10,14},{7,3},{11,15},{20,16},{24,... | collective-permute-start | bytes 786440 | tf_op jit(solution)/shard_map/ppermute | solution.py:591
  63.0 2.2 %products.3.refs_5_ = f32[512,1280]{1,0:T(8,128)S(1)} custom-call(s32[6]{0:T(128)S(1)} %stack.31.where_ref, bf16[512,256]{1,0:T(8,128)(2,1)S(1)} %collective-permute-done.8.refs_0_, bf16[512,256]{1,0:T(8,128)(2,1)S(1)} %collective-permute-done.7.refs_1_, bf16[1024,1280]{1,0:T(8,128)(2,1)S(1)} %copy-done, bf16[1024,1280]{1,0:T(8,128)(2,1)S(1)} %copy-done, ...), custom_call_target="tpu_custom_call" | custom-call | flops 1 | tf_op jit(solution)/shard_map/products/pallas_call | solution.py:435
  65.2 6.3 %collective-permute-done.6.refs_3_ = bf16[512,256]{1,0:T(8,128)(2,1)S(1)} collective-permute-done((bf16[512,256]{1,0:T(8,128)(2,1)S(1)}, bf16[512,256]{1,0:T(8,128)(2,1)S(1)}, u32[]{:S(2)}, u32[]{:S(2)}) %collective-permute-start.6) | collective-permute-done | bytes 262176 | tf_op jit(solution)/shard_map/ppermute | solution.py:50
  71.5 1.4 %collective-permute-done.5.refs_4_ = bf16[512,256]{1,0:T(8,128)(2,1)S(1)} collective-permute-done((bf16[512,256]{1,0:T(8,128)(2,1)S(1)}, bf16[512,256]{1,0:T(8,128)(2,1)S(1)}, u32[]{:S(2)}, u32[]{:S(2)}) %collective-permute-start.5) | collective-permute-done | bytes 262176 | tf_op jit(solution)/shard_map/ppermute | solution.py:50
  72.9 0.7 collective-permute-start.9
  73.6 1.3 %collective-permute-start.10 = (bf16[512,256]{1,0:T(8,128)(2,1)S(1)}, bf16[512,256]{1,0:T(8,128)(2,1)S(1)}, u32[]{:S(2)}, u32[]{:S(2)}) collective-permute-start(bf16[512,256]{1,0:T(8,128)(2,1)S(1)} %collective-permute-done.6.refs_3_), channel_id=1, source_target_pairs={{4,0},{8,12},{5,1},{9,13},{6,2},{10,14},{7,3},{11,15},{20,16},{24,... | collective-permute-start | bytes 786440 | tf_op jit(solution)/shard_map/ppermute | solution.py:591
  74.9 2.9 %collective-permute-done.13.refs_1_ = bf16[512,256]{1,0:T(8,128)(2,1)S(1)} collective-permute-done((bf16[512,256]{1,0:T(8,128)(2,1)S(1)}, bf16[512,256]{1,0:T(8,128)(2,1)S(1)}, u32[]{:S(2)}, u32[]{:S(2)}) %collective-permute-start.13) | collective-permute-done | bytes 262176 | tf_op jit(solution)/shard_map/ppermute | solution.py:591
  77.8 4.0 %first.1.acc_in = f32[512,1280]{1,0:T(8,128)S(1)} custom-call(s32[6]{0:T(128)S(1)} %stack.31.where_ref, bf16[512,256]{1,0:T(8,128)(2,1)S(1)} %collective-permute-done.12.refs_0_, bf16[512,256]{1,0:T(8,128)(2,1)S(1)} %collective-permute-done.13.refs_1_, bf16[512,256]{1,0:T(8,128)(2,1)S(1)} %collective-permute-done.4.refs_2_, ...), custom_call_target="tpu_custom_call" | custom-call | flops 1 | tf_op jit(solution)/shard_map/first/pallas_call | solution.py:483
  81.8 1.0 collective-permute-done.10.more
  82.8 1.1 %second.3 = (bf16[4,64,640]{2,1,0:T(8,128)(2,1)S(1)}, bf16[4,64,640]{2,1,0:T(8,128)(2,1)S(1)}) custom-call(s32[6]{0:T(128)S(1)} %stack.31.where_ref, bf16[512,256]{1,0:T(8,128)(2,1)S(1)} %collective-permute-done.9.slot, bf16[512,256]{1,0:T(8,128)(2,1)S(1)} %collective-permute-done.10.more, bf16[512,1280]{1,0:T(8,128)(2,1)S(1)} %collective-permute-done.refs_7_.fetched_ref, ...), custom_call_target="tpu_custom_call" | custom-call | flops 1 | tf_op jit(solution)/shard_map/second/pallas_call | solution.py:524
  83.9 0.1 collective-permute-start.18
  84.0 1.1 %second.2 = (bf16[4,64,640]{2,1,0:T(8,128)(2,1)S(1)}, bf16[4,64,640]{2,1,0:T(8,128)(2,1)S(1)}) custom-call(s32[6]{0:T(128)S(1)} %stack.31.where_ref, bf16[512,256]{1,0:T(8,128)(2,1)S(1)} %collective-permute-done.9.slot, bf16[512,256]{1,0:T(8,128)(2,1)S(1)} %collective-permute-done.10.more, bf16[512,1280]{1,0:T(8,128)(2,1)S(1)} %collective-permute-done.refs_7_.fetched_ref, ...), custom_call_target="tpu_custom_call" | custom-call | flops 1 | tf_op jit(solution)/shard_map/second/pallas_call | solution.py:524
  85.1 0.6 collective-permute-start.14
  85.7 0.6 add.8
  86.3 1.9 %collective-permute-start.19 = (bf16[64,640]{1,0:T(8,128)(2,1)S(1)}, bf16[64,640]{1,0:T(8,128)(2,1)S(1)}, u32[]{:S(2)}, u32[]{:S(2)}) collective-permute-start(bf16[64,640]{1,0:T(8,128)(2,1)S(1)} %get-tuple-element.68), channel_id=1, source_target_pairs={{0,12},{4,8},{8,4},{12,0},{1,13},{5,9},{9,5},{13,1},{2,14},{6,10},... | collective-permute-start | bytes 245768 | tf_op jit(solution)/shard_map/ppermute | solution.py:50
  88.2 0.0 collective-permute-start.20
  88.2 2.5 %collective-permute-start.21 = (bf16[64,640]{1,0:T(8,128)(2,1)S(1)}, bf16[64,640]{1,0:T(8,128)(2,1)S(1)}, u32[]{:S(2)}, u32[]{:S(2)}) collective-permute-start(bf16[64,640]{1,0:T(8,128)(2,1)S(1)} %get-tuple-element.70), channel_id=1, source_target_pairs={{0,4},{4,0},{8,12},{12,8},{1,5},{5,1},{9,13},{13,9},{2,6},{6,2},{1... | collective-permute-start | bytes 245768 | tf_op jit(solution)/shard_map/ppermute | solution.py:50
  90.7 0.6 add.7
  91.4 1.9 %collective-permute-start.15 = (bf16[64,640]{1,0:T(8,128)(2,1)S(1)}, bf16[64,640]{1,0:T(8,128)(2,1)S(1)}, u32[]{:S(2)}, u32[]{:S(2)}) collective-permute-start(bf16[64,640]{1,0:T(8,128)(2,1)S(1)} %get-tuple-element.62), channel_id=1, source_target_pairs={{0,12},{4,8},{8,4},{12,0},{1,13},{5,9},{9,5},{13,1},{2,14},{6,10},... | collective-permute-start | bytes 245768 | tf_op jit(solution)/shard_map/ppermute | solution.py:50
  93.3 0.3 collective-permute-done.19.refs_5_
  93.5 2.3 %collective-permute-start.17 = (bf16[64,640]{1,0:T(8,128)(2,1)S(1)}, bf16[64,640]{1,0:T(8,128)(2,1)S(1)}, u32[]{:S(2)}, u32[]{:S(2)}) collective-permute-start(bf16[64,640]{1,0:T(8,128)(2,1)S(1)} %get-tuple-element.64), channel_id=1, source_target_pairs={{0,4},{4,0},{8,12},{12,8},{1,5},{5,1},{9,13},{13,9},{2,6},{6,2},{1... | collective-permute-start | bytes 245768 | tf_op jit(solution)/shard_map/ppermute | solution.py:50
  95.8 3.0 %collective-permute-done.20.refs_6_ = bf16[64,640]{1,0:T(8,128)(2,1)S(1)} collective-permute-done((bf16[64,640]{1,0:T(8,128)(2,1)S(1)}, bf16[64,640]{1,0:T(8,128)(2,1)S(1)}, u32[]{:S(2)}, u32[]{:S(2)}) %collective-permute-start.20) | collective-permute-done | bytes 81952 | tf_op jit(solution)/shard_map/ppermute | solution.py:50
  98.9 4.2 %collective-permute-done.16.refs_2_ = bf16[64,640]{1,0:T(8,128)(2,1)S(1)} collective-permute-done((bf16[64,640]{1,0:T(8,128)(2,1)S(1)}, bf16[64,640]{1,0:T(8,128)(2,1)S(1)}, u32[]{:S(2)}, u32[]{:S(2)}) %collective-permute-start.16) | collective-permute-done | bytes 81952 | tf_op jit(solution)/shard_map/ppermute | solution.py:50
  103.1 1.6 %mix.1 = bf16[64,5120]{1,0:T(8,128)(2,1)} custom-call(s32[6]{0:T(128)S(1)} %stack.31.where_ref, bf16[64,5120]{1,0:T(8,128)(2,1)S(1)} %copy-done.4, f32[1,5120]{1,0:T(1,128)S(1)} %bitcast.14, bf16[64,640]{1,0:T(8,128)(2,1)S(1)} %get-tuple-element.61.refs_0_, bf16[64,640]{1,0:T(8,128)(2,1)S(1)} %collective-permute-done.15.refs_1_, ...), custom_call_target="tpu_custom_call" | custom-call | flops 1 | tf_op jit(solution)/shard_map/mix/pallas_call | solution.py:620
  (30 shorter events, 0.1 us)
Async XLA Ops:
  0.0 3.9 %copy-start = (bf16[1024,1280]{1,0:T(8,128)(2,1)S(1)}, bf16[1024,1280]{1,0:T(8,128)(2,1)}, u32[]{:S(2)}) copy-start(bf16[1024,1280]{1,0:T(8,128)(2,1)} %refs_6_) | copy-start | bytes 7864324
  3.7 7.4 %copy-start.7 = (bf16[3,256,256]{2,1,0:T(8,128)(2,1)S(1)}, bf16[3,256,256]{2,1,0:T(8,128)(2,1)}, u32[]{:S(2)}) copy-start(bf16[3,256,256]{2,1,0:T(8,128)(2,1)} %get-tuple-element.40) | copy-start | bytes 1179652
  3.7 8.2 %copy-start.3 = (bf16[256,1024]{1,0:T(8,128)(2,1)S(1)}, bf16[256,1024]{1,0:T(8,128)(2,1)}, u32[]{:S(2)}) copy-start(bf16[256,1024]{1,0:T(8,128)(2,1)} %q_ref.3) | copy-start | bytes 1572868
  3.7 8.2 %copy-start.6 = (s32[2,2,8]{2,1,0:T(2,128)S(1)}, s32[2,2,8]{2,1,0:T(2,128)}, u32[]{:S(2)}) copy-start(s32[2,2,8]{2,1,0:T(2,128)} %exps_ref.3) | copy-start | bytes 388
  3.8 3.7 %copy-start.9 = (bf16[3,256,256]{2,1,0:T(8,128)(2,1)S(1)}, bf16[3,256,256]{2,1,0:T(8,128)(2,1)}, u32[]{:S(2)}) copy-start(bf16[3,256,256]{2,1,0:T(8,128)(2,1)} %get-tuple-element.38) | copy-start | bytes 1179652
  3.8 7.3 %copy-start.8 = (bf16[3,256,256]{2,1,0:T(8,128)(2,1)S(1)}, bf16[3,256,256]{2,1,0:T(8,128)(2,1)}, u32[]{:S(2)}) copy-start(bf16[3,256,256]{2,1,0:T(8,128)(2,1)} %get-tuple-element.39) | copy-start | bytes 1179652
  3.8 8.1 %copy-start.2 = (bf16[2,256,1024]{2,1,0:T(8,128)(2,1)S(1)}, bf16[2,256,1024]{2,1,0:T(8,128)(2,1)}, u32[]{:S(2)}) copy-start(bf16[2,256,1024]{2,1,0:T(8,128)(2,1)} %fresh_ref.3) | copy-start | bytes 3145732
  4.6 31.8 %collective-permute-start = (bf16[512,1280]{1,0:T(8,128)(2,1)S(1)}, bf16[512,1280]{1,0:T(8,128)(2,1)S(1)}, u32[]{:S(2)}, u32[]{:S(2)}) collective-permute-start(bf16[512,1280]{1,0:T(8,128)(2,1)S(1)} %take.1), channel_id=1, source_target_pairs={{0,2},{2,0},{1,3},{3,1},{4,6},{6,4},{5,7},{7,5},{8,10},{10,8},{9,1... | collective-permute-start | bytes 3932168 | tf_op jit(solution)/shard_map/ppermute | solution.py:50
  7.6 30.5 %collective-permute-start.3 = (bf16[3,256,256]{2,1,0:T(8,128)(2,1)S(1)}, bf16[3,256,256]{2,1,0:T(8,128)(2,1)S(1)}, u32[]{:S(2)}, u32[]{:S(2)}) collective-permute-start(bf16[3,256,256]{2,1,0:T(8,128)(2,1)S(1)} %copy-done.9), channel_id=1, source_target_pairs={{0,12},{4,8},{8,4},{12,0},{1,13},{5,9},{9,5},{13,1},{2,14},{6,10},... | collective-permute-start | bytes 1179656 | tf_op jit(solution)/shard_map/ppermute | solution.py:50
  11.2 33.3 %collective-permute-start.2 = (bf16[3,256,256]{2,1,0:T(8,128)(2,1)S(1)}, bf16[3,256,256]{2,1,0:T(8,128)(2,1)S(1)}, u32[]{:S(2)}, u32[]{:S(2)}) collective-permute-start(bf16[3,256,256]{2,1,0:T(8,128)(2,1)S(1)} %copy-done.8), channel_id=1, source_target_pairs={{0,8},{4,12},{8,0},{12,4},{1,9},{5,13},{9,1},{13,5},{2,10},{6,14},... | collective-permute-start | bytes 1179656 | tf_op jit(solution)/shard_map/ppermute | solution.py:50
  11.2 33.3 %collective-permute-start.1 = (bf16[3,256,256]{2,1,0:T(8,128)(2,1)S(1)}, bf16[3,256,256]{2,1,0:T(8,128)(2,1)S(1)}, u32[]{:S(2)}, u32[]{:S(2)}) collective-permute-start(bf16[3,256,256]{2,1,0:T(8,128)(2,1)S(1)} %copy-done.7), channel_id=1, source_target_pairs={{0,4},{4,0},{8,12},{12,8},{1,5},{5,1},{9,13},{13,9},{2,6},{6,2},{1... | collective-permute-start | bytes 1179656 | tf_op jit(solution)/shard_map/ppermute | solution.py:50
  12.0 2.2 %copy-start.1 = (bf16[2,1024,1024]{2,1,0:T(8,128)(2,1)S(1)}, bf16[2,1024,1024]{2,1,0:T(8,128)(2,1)}, u32[]{:S(2)}) copy-start(bf16[2,1024,1024]{2,1,0:T(8,128)(2,1)} %cached_ref.3) | copy-start | bytes 12582916
  36.3 41.4 %collective-permute-start.11 = (bf16[512,1280]{1,0:T(8,128)(2,1)S(1)}, bf16[512,1280]{1,0:T(8,128)(2,1)S(1)}, u32[]{:S(2)}, u32[]{:S(2)}) collective-permute-start(bf16[512,1280]{1,0:T(8,128)(2,1)S(1)} %collective-permute-done.refs_7_.fetched_ref), channel_id=1, source_target_pairs={{0,16},{16,0},{1,17},{17,1},{2,18},{18,2},{3,19},{19,3},{4,20},{20... | collective-permute-start | bytes 3932168 | tf_op jit(solution)/shard_map/ppermute | solution.py:50
  46.7 14.2 %collective-permute-start.8 = (bf16[512,256]{1,0:T(8,128)(2,1)S(1)}, bf16[512,256]{1,0:T(8,128)(2,1)S(1)}, u32[]{:S(2)}, u32[]{:S(2)}) collective-permute-start(bf16[512,256]{1,0:T(8,128)(2,1)S(1)} %bitcast.9), channel_id=1, source_target_pairs={{0,8},{4,12},{8,0},{12,4},{1,9},{5,13},{9,1},{13,5},{2,10},{6,14},... | collective-permute-start | bytes 786440 | tf_op jit(solution)/shard_map/ppermute | solution.py:50
  46.8 14.2 %collective-permute-start.7 = (bf16[512,256]{1,0:T(8,128)(2,1)S(1)}, bf16[512,256]{1,0:T(8,128)(2,1)S(1)}, u32[]{:S(2)}, u32[]{:S(2)}) collective-permute-start(bf16[512,256]{1,0:T(8,128)(2,1)S(1)} %bitcast.10), channel_id=1, source_target_pairs={{0,4},{4,0},{8,12},{12,8},{1,5},{5,1},{9,13},{13,9},{2,6},{6,2},{1... | collective-permute-start | bytes 786440 | tf_op jit(solution)/shard_map/ppermute | solution.py:50
  52.2 6.4 %collective-permute-start.4 = (bf16[512,256]{1,0:T(8,128)(2,1)S(1)}, bf16[512,256]{1,0:T(8,128)(2,1)S(1)}, u32[]{:S(2)}, u32[]{:S(2)}) collective-permute-start(bf16[512,256]{1,0:T(8,128)(2,1)S(1)} %bitcast.13), channel_id=1, source_target_pairs={{0,2},{2,0},{1,3},{3,1},{4,6},{6,4},{5,7},{7,5},{8,10},{10,8},{9,1... | collective-permute-start | bytes 786440 | tf_op jit(solution)/shard_map/ppermute | solution.py:50
  58.6 12.9 %collective-permute-start.6 = (bf16[512,256]{1,0:T(8,128)(2,1)S(1)}, bf16[512,256]{1,0:T(8,128)(2,1)S(1)}, u32[]{:S(2)}, u32[]{:S(2)}) collective-permute-start(bf16[512,256]{1,0:T(8,128)(2,1)S(1)} %collective-permute-done.4.refs_2_), channel_id=1, source_target_pairs={{0,8},{4,12},{8,0},{12,4},{1,9},{5,13},{9,1},{13,5},{2,10},{6,14},... | collective-permute-start | bytes 786440 | tf_op jit(solution)/shard_map/ppermute | solution.py:50
  59.2 13.8 %collective-permute-start.5 = (bf16[512,256]{1,0:T(8,128)(2,1)S(1)}, bf16[512,256]{1,0:T(8,128)(2,1)S(1)}, u32[]{:S(2)}, u32[]{:S(2)}) collective-permute-start(bf16[512,256]{1,0:T(8,128)(2,1)S(1)} %collective-permute-done.4.refs_2_), channel_id=1, source_target_pairs={{0,4},{4,0},{8,12},{12,8},{1,5},{5,1},{9,13},{13,9},{2,6},{6,2},{1... | collective-permute-start | bytes 786440 | tf_op jit(solution)/shard_map/ppermute | solution.py:50
  61.0 13.9 %collective-permute-start.12 = (bf16[512,256]{1,0:T(8,128)(2,1)S(1)}, bf16[512,256]{1,0:T(8,128)(2,1)S(1)}, u32[]{:S(2)}, u32[]{:S(2)}) collective-permute-start(bf16[512,256]{1,0:T(8,128)(2,1)S(1)} %bitcast.12), channel_id=1, source_target_pairs={{4,8},{8,4},{5,9},{9,5},{6,10},{10,6},{7,11},{11,7},{20,24},{24,20... | collective-permute-start | bytes 786440 | tf_op jit(solution)/shard_map/ppermute | solution.py:50
  61.7 16.1 %collective-permute-start.13 = (bf16[512,256]{1,0:T(8,128)(2,1)S(1)}, bf16[512,256]{1,0:T(8,128)(2,1)S(1)}, u32[]{:S(2)}, u32[]{:S(2)}) collective-permute-start(bf16[512,256]{1,0:T(8,128)(2,1)S(1)} %collective-permute-done.8.refs_0_), channel_id=1, source_target_pairs={{4,0},{8,12},{5,1},{9,13},{6,2},{10,14},{7,3},{11,15},{20,16},{24,... | collective-permute-start | bytes 786440 | tf_op jit(solution)/shard_map/ppermute | solution.py:591
  72.9 8.8 %collective-permute-start.9 = (bf16[512,256]{1,0:T(8,128)(2,1)S(1)}, bf16[512,256]{1,0:T(8,128)(2,1)S(1)}, u32[]{:S(2)}, u32[]{:S(2)}) collective-permute-start(bf16[512,256]{1,0:T(8,128)(2,1)S(1)} %collective-permute-done.4.refs_2_), channel_id=1, source_target_pairs={{4,8},{8,4},{5,9},{9,5},{6,10},{10,6},{7,11},{11,7},{20,24},{24,20... | collective-permute-start | bytes 786440 | tf_op jit(solution)/shard_map/ppermute | solution.py:50
  73.6 9.2 %collective-permute-start.10 = (bf16[512,256]{1,0:T(8,128)(2,1)S(1)}, bf16[512,256]{1,0:T(8,128)(2,1)S(1)}, u32[]{:S(2)}, u32[]{:S(2)}) collective-permute-start(bf16[512,256]{1,0:T(8,128)(2,1)S(1)} %collective-permute-done.6.refs_3_), channel_id=1, source_target_pairs={{4,0},{8,12},{5,1},{9,13},{6,2},{10,14},{7,3},{11,15},{20,16},{24,... | collective-permute-start | bytes 786440 | tf_op jit(solution)/shard_map/ppermute | solution.py:591
  83.9 19.2 %copy-start.4 = (bf16[64,5120]{1,0:T(8,128)(2,1)S(1)}, bf16[64,5120]{1,0:T(8,128)(2,1)}, u32[]{:S(2)}) copy-start(bf16[64,5120]{1,0:T(8,128)(2,1)} %hidden_ref.1) | copy-start | bytes 1966084
  83.9 19.2 %copy-start.5 = (f32[5120]{0:T(1024)S(1)}, f32[5120]{0:T(1024)}, u32[]{:S(2)}) copy-start(f32[5120]{0:T(1024)} %param.13) | copy-start | bytes 61444
  83.9 1.8 %collective-permute-start.18 = (bf16[4,64,640]{2,1,0:T(8,128)(2,1)S(1)}, bf16[4,64,640]{2,1,0:T(8,128)(2,1)S(1)}, u32[]{:S(2)}, u32[]{:S(2)}) collective-permute-start(bf16[4,64,640]{2,1,0:T(8,128)(2,1)S(1)} %get-tuple-element.66), channel_id=1, source_target_pairs={{0,1},{1,0},{2,3},{3,2},{4,5},{5,4},{6,7},{7,6},{8,9},{9,8},{10,11... | collective-permute-start | bytes 983048 | tf_op jit(solution)/shard_map/ppermute | solution.py:50
  85.1 5.6 %collective-permute-start.14 = (bf16[4,64,640]{2,1,0:T(8,128)(2,1)S(1)}, bf16[4,64,640]{2,1,0:T(8,128)(2,1)S(1)}, u32[]{:S(2)}, u32[]{:S(2)}) collective-permute-start(bf16[4,64,640]{2,1,0:T(8,128)(2,1)S(1)} %get-tuple-element.60), channel_id=1, source_target_pairs={{0,1},{1,0},{2,3},{3,2},{4,5},{5,4},{6,7},{7,6},{8,9},{9,8},{10,11... | collective-permute-start | bytes 983048 | tf_op jit(solution)/shard_map/ppermute | solution.py:50
  86.3 7.3 %collective-permute-start.19 = (bf16[64,640]{1,0:T(8,128)(2,1)S(1)}, bf16[64,640]{1,0:T(8,128)(2,1)S(1)}, u32[]{:S(2)}, u32[]{:S(2)}) collective-permute-start(bf16[64,640]{1,0:T(8,128)(2,1)S(1)} %get-tuple-element.68), channel_id=1, source_target_pairs={{0,12},{4,8},{8,4},{12,0},{1,13},{5,9},{9,5},{13,1},{2,14},{6,10},... | collective-permute-start | bytes 245768 | tf_op jit(solution)/shard_map/ppermute | solution.py:50
  88.2 10.7 %collective-permute-start.20 = (bf16[64,640]{1,0:T(8,128)(2,1)S(1)}, bf16[64,640]{1,0:T(8,128)(2,1)S(1)}, u32[]{:S(2)}, u32[]{:S(2)}) collective-permute-start(bf16[64,640]{1,0:T(8,128)(2,1)S(1)} %get-tuple-element.69), channel_id=1, source_target_pairs={{0,8},{4,12},{8,0},{12,4},{1,9},{5,13},{9,1},{13,5},{2,10},{6,14},... | collective-permute-start | bytes 245768 | tf_op jit(solution)/shard_map/ppermute | solution.py:50
  88.2 10.7 %collective-permute-start.21 = (bf16[64,640]{1,0:T(8,128)(2,1)S(1)}, bf16[64,640]{1,0:T(8,128)(2,1)S(1)}, u32[]{:S(2)}, u32[]{:S(2)}) collective-permute-start(bf16[64,640]{1,0:T(8,128)(2,1)S(1)} %get-tuple-element.70), channel_id=1, source_target_pairs={{0,4},{4,0},{8,12},{12,8},{1,5},{5,1},{9,13},{13,9},{2,6},{6,2},{1... | collective-permute-start | bytes 245768 | tf_op jit(solution)/shard_map/ppermute | solution.py:50
  91.4 7.5 %collective-permute-start.15 = (bf16[64,640]{1,0:T(8,128)(2,1)S(1)}, bf16[64,640]{1,0:T(8,128)(2,1)S(1)}, u32[]{:S(2)}, u32[]{:S(2)}) collective-permute-start(bf16[64,640]{1,0:T(8,128)(2,1)S(1)} %get-tuple-element.62), channel_id=1, source_target_pairs={{0,12},{4,8},{8,4},{12,0},{1,13},{5,9},{9,5},{13,1},{2,14},{6,10},... | collective-permute-start | bytes 245768 | tf_op jit(solution)/shard_map/ppermute | solution.py:50
  93.3 9.8 %collective-permute-start.16 = (bf16[64,640]{1,0:T(8,128)(2,1)S(1)}, bf16[64,640]{1,0:T(8,128)(2,1)S(1)}, u32[]{:S(2)}, u32[]{:S(2)}) collective-permute-start(bf16[64,640]{1,0:T(8,128)(2,1)S(1)} %get-tuple-element.63), channel_id=1, source_target_pairs={{0,8},{4,12},{8,0},{12,4},{1,9},{5,13},{9,1},{13,5},{2,10},{6,14},... | collective-permute-start | bytes 245768 | tf_op jit(solution)/shard_map/ppermute | solution.py:50
  93.5 9.6 %collective-permute-start.17 = (bf16[64,640]{1,0:T(8,128)(2,1)S(1)}, bf16[64,640]{1,0:T(8,128)(2,1)S(1)}, u32[]{:S(2)}, u32[]{:S(2)}) collective-permute-start(bf16[64,640]{1,0:T(8,128)(2,1)S(1)} %get-tuple-element.64), channel_id=1, source_target_pairs={{0,4},{4,0},{8,12},{12,8},{1,5},{5,1},{9,13},{13,9},{2,6},{6,2},{1... | collective-permute-start | bytes 245768 | tf_op jit(solution)/shard_map/ppermute | solution.py:50

commit v24 on v22

--- a/solution.py
+++ b/solution.py
@@ -588,7 +588,7 @@
     slots = []
     for at, x in enumerate((mine, other)):
         next_to, far = swap(x, "patch", 4, 1), swap(x, "patch", 4, 2)
-        next_to, far, other, x = lax.optimization_barrier((next_to, far, other, x))
+        far, next_to, other, x = lax.optimization_barrier((far, next_to, other, x))
         if at == 1:
             acc = add_product(where, {2: slots[0][2], 1: slots[0][1]}, out_weight, acc)
             far, x, acc = lax.optimization_barrier((far, x, acc))

time: 107 us -> 109 us (1.019)
  starting transfers between devices: 33.5 us -> 34.7 us
    ppermute x20, waiting for transfers between devices: 43.7 us -> 45.4 us  [swap(): return lax.ppermute(x, axes, pairs)]
    ppermute x2, waiting for transfers between devices: 4.24 us -> 2.95 us  [share_tail(): ends = lax.ppermute(far, 'patch', [(1, 0), (2, 3)])]
    ppermute x20, starting transfers between devices: 30.9 us -> 32.1 us  [swap(): return lax.ppermute(x, axes, pairs)]
  transfers between devices with their start and end apart: 22 -> 22, of which waited for: 10 -> 8; matrix products, arithmetic and copies ran while one was open for 0% -> 0% of each run, Pallas kernels for 15% -> 15%
where the time goes in v24:
time: 109 us
  waiting for transfers between devices  48.4 us (44%)
  starting transfers between devices  34.7 us (32%)
  Pallas kernels  22.9 us (21%)
  local copies, waits for them, and re-layouts  2.32 us (2%)
    ppermute x20, waiting for transfers between devices, swap(): return lax.ppermute(x, axes, pairs)  45.4 us
    ppermute x20, starting transfers between devices, swap(): return lax.ppermute(x, axes, pairs)  32.1 us
    pallas_call x2, Pallas kernels, attend_half(): call(functools.partial(attend_half_kernel, half), 'attend', out, 1, [spec...  4.64 us
    pallas_call x1, Pallas kernels, first_product(): call(first_kernel, 'first', jax.ShapeDtypeStruct(acc.shape, jnp.float32),...  3.96 us
    pallas_call x2, Pallas kernels, add_product(): call(functools.partial(add_product_kernel, len(rels)), 'products', jax.Sh...  3.79 us
    pallas_call x1, Pallas kernels, pack(): pl.pallas_call(functools.partial(pack_kernel, split, feat // HEAD_DIM), o...  3.53 us
    ppermute x2, waiting for transfers between devices, share_tail(): ends = lax.ppermute(far, 'patch', [(1, 0), (2, 3)])  2.95 us
    ppermute x2, starting transfers between devices, share_tail(): ends = lax.ppermute(far, 'patch', [(1, 0), (2, 3)])  2.58 us
  transfers between devices with their start and end apart: 22, of which 8 were waited for; matrix products, arithmetic and copies ran while one was open for 0% of the time, Pallas kernels for 15%

profile of v24, /device:TPU:0, one launch (start us, length us, event | category | flops | bytes accessed | tf_op | source)
XLA Modules:
  0.0 108.5 jit_solution(14384442683144646676)
XLA Ops:
  0.0 3.5 %pack.1 = (bf16[3,256,256]{2,1,0:T(8,128)(2,1)}, bf16[3,256,256]{2,1,0:T(8,128)(2,1)}, bf16[3,256,256]{2,1,0:T(8,128)(2,1)}) custom-call(s32[2,2,8]{2,1,0:T(2,128)} %exps_ref.3, bf16[256,1024]{1,0:T(8,128)(2,1)} %q_ref.3, bf16[2,256,1024]{2,1,0:T(8,128)(2,1)} %fresh_ref.3, bf16[2,1024,1024]{2,1,0:T(8,128)(2,1)} %cached_ref.3), custom_call_target="tpu_custom_call" | custom-call | tf_op jit(solution)/shard_map/pack/pallas_call | solution.py:116
  3.6 0.0 copy-start.3
  3.6 0.1 stack.31.where_ref
  3.7 0.7 take.1
  4.4 3.0 %collective-permute-start = (bf16[512,1280]{1,0:T(8,128)(2,1)S(1)}, bf16[512,1280]{1,0:T(8,128)(2,1)S(1)}, u32[]{:S(2)}, u32[]{:S(2)}) collective-permute-start(bf16[512,1280]{1,0:T(8,128)(2,1)S(1)} %take.1), channel_id=1, source_target_pairs={{0,2},{2,0},{1,3},{3,1},{4,6},{6,4},{5,7},{7,5},{8,10},{10,8},{9,1... | collective-permute-start | bytes 3932168 | tf_op jit(solution)/shard_map/ppermute | solution.py:50
  7.4 2.6 %collective-permute-start.2 = (bf16[3,256,256]{2,1,0:T(8,128)(2,1)S(1)}, bf16[3,256,256]{2,1,0:T(8,128)(2,1)S(1)}, u32[]{:S(2)}, u32[]{:S(2)}) collective-permute-start(bf16[3,256,256]{2,1,0:T(8,128)(2,1)S(1)} %copy-done.9), channel_id=1, source_target_pairs={{0,8},{4,12},{8,0},{12,4},{1,9},{5,13},{9,1},{13,5},{2,10},{6,14},... | collective-permute-start | bytes 1179656 | tf_op jit(solution)/shard_map/ppermute | solution.py:50
  10.0 1.3 %collective-permute-start.3 = (bf16[3,256,256]{2,1,0:T(8,128)(2,1)S(1)}, bf16[3,256,256]{2,1,0:T(8,128)(2,1)S(1)}, u32[]{:S(2)}, u32[]{:S(2)}) collective-permute-start(bf16[3,256,256]{2,1,0:T(8,128)(2,1)S(1)} %copy-done.8), channel_id=1, source_target_pairs={{0,12},{4,8},{8,4},{12,0},{1,13},{5,9},{9,5},{13,1},{2,14},{6,10},... | collective-permute-start | bytes 1179656 | tf_op jit(solution)/shard_map/ppermute | solution.py:50
  11.3 0.3 collective-permute-start.1
  11.6 2.2 %copy-done.1 = bf16[2,1024,1024]{2,1,0:T(8,128)(2,1)S(1)} copy-done((bf16[2,1024,1024]{2,1,0:T(8,128)(2,1)S(1)}, bf16[2,1024,1024]{2,1,0:T(8,128)(2,1)}, u32[]{:S(2)}) %copy-start.1) | copy-done | bytes 4194328
  13.8 1.3 %own.1.refs_0_ = bf16[3,256,256]{2,1,0:T(8,128)(2,1)S(1)} custom-call(s32[6]{0:T(128)S(1)} %stack.31.where_ref, s32[2,2,8]{2,1,0:T(2,128)S(1)} %copy-done.6, bf16[256,1024]{1,0:T(8,128)(2,1)S(1)} %copy-done.3, bf16[2,256,1024]{2,1,0:T(8,128)(2,1)S(1)} %copy-done.2, bf16[2,1024,1024]{2,1,0:T(8,128)(2,1)S(1)} %copy-done.1), custom_call_target="tpu_custom_call" | custom-call | flops 1 | tf_op jit(solution)/shard_map/own/pallas_call | solution.py:152
  15.1 21.0 %collective-permute-done.refs_7_.fetched_ref = bf16[512,1280]{1,0:T(8,128)(2,1)S(1)} collective-permute-done((bf16[512,1280]{1,0:T(8,128)(2,1)S(1)}, bf16[512,1280]{1,0:T(8,128)(2,1)S(1)}, u32[]{:S(2)}, u32[]{:S(2)}) %collective-permute-start) | collective-permute-done | bytes 1310752 | tf_op jit(solution)/shard_map/ppermute | solution.py:50
  36.2 1.8 %collective-permute-start.11 = (bf16[512,1280]{1,0:T(8,128)(2,1)S(1)}, bf16[512,1280]{1,0:T(8,128)(2,1)S(1)}, u32[]{:S(2)}, u32[]{:S(2)}) collective-permute-start(bf16[512,1280]{1,0:T(8,128)(2,1)S(1)} %collective-permute-done.refs_7_.fetched_ref), channel_id=1, source_target_pairs={{0,16},{16,0},{1,17},{17,1},{2,18},{18,2},{3,19},{19,3},{4,20},{20... | collective-permute-start | bytes 3932168 | tf_op jit(solution)/shard_map/ppermute | solution.py:50
  37.9 2.3 %attend.2 = bf16[4,128,256]{2,1,0:T(8,128)(2,1)S(1)} custom-call(s32[6]{0:T(128)S(1)} %stack.31.where_ref, bf16[3,256,256]{2,1,0:T(8,128)(2,1)S(1)} %own.1.refs_0_, bf16[3,256,256]{2,1,0:T(8,128)(2,1)S(1)} %collective-permute-done.1.refs_1_, bf16[3,256,256]{2,1,0:T(8,128)(2,1)S(1)} %collective-permute-done.2.refs_2_, ...), custom_call_target="tpu_custom_call" | custom-call | flops 1 | tf_op jit(solution)/shard_map/attend/pallas_call | solution.py:415
  40.3 7.0 %collective-permute-start.8 = (bf16[512,256]{1,0:T(8,128)(2,1)S(1)}, bf16[512,256]{1,0:T(8,128)(2,1)S(1)}, u32[]{:S(2)}, u32[]{:S(2)}) collective-permute-start(bf16[512,256]{1,0:T(8,128)(2,1)S(1)} %bitcast.9), channel_id=1, source_target_pairs={{0,4},{4,0},{8,12},{12,8},{1,5},{5,1},{9,13},{13,9},{2,6},{6,2},{1... | collective-permute-start | bytes 786440 | tf_op jit(solution)/shard_map/ppermute | solution.py:50
  47.2 2.0 %collective-permute-start.7 = (bf16[512,256]{1,0:T(8,128)(2,1)S(1)}, bf16[512,256]{1,0:T(8,128)(2,1)S(1)}, u32[]{:S(2)}, u32[]{:S(2)}) collective-permute-start(bf16[512,256]{1,0:T(8,128)(2,1)S(1)} %bitcast.10), channel_id=1, source_target_pairs={{0,8},{4,12},{8,0},{12,4},{1,9},{5,13},{9,1},{13,5},{2,10},{6,14},... | collective-permute-start | bytes 786440 | tf_op jit(solution)/shard_map/ppermute | solution.py:50
  49.2 2.3 %attend.3 = bf16[4,128,256]{2,1,0:T(8,128)(2,1)S(1)} custom-call(s32[6]{0:T(128)S(1)} %stack.31.where_ref, bf16[3,256,256]{2,1,0:T(8,128)(2,1)S(1)} %own.1.refs_0_, bf16[3,256,256]{2,1,0:T(8,128)(2,1)S(1)} %collective-permute-done.1.refs_1_, bf16[3,256,256]{2,1,0:T(8,128)(2,1)S(1)} %collective-permute-done.2.refs_2_, ...), custom_call_target="tpu_custom_call" | custom-call | flops 1 | tf_op jit(solution)/shard_map/attend/pallas_call | solution.py:415
  51.6 0.6 collective-permute-start.4
  52.2 1.5 %products.2.refs_4_ = f32[512,1280]{1,0:T(8,128)S(1)} custom-call(s32[6]{0:T(128)S(1)} %stack.31.where_ref, bf16[512,256]{1,0:T(8,128)(2,1)S(1)} %bitcast.11, bf16[1024,1280]{1,0:T(8,128)(2,1)S(1)} %copy-done), custom_call_target="tpu_custom_call" | custom-call | flops 6000000000 | tf_op jit(solution)/shard_map/products/pallas_call | solution.py:440
  53.7 5.8 %collective-permute-done.4.refs_2_ = bf16[512,256]{1,0:T(8,128)(2,1)S(1)} collective-permute-done((bf16[512,256]{1,0:T(8,128)(2,1)S(1)}, bf16[512,256]{1,0:T(8,128)(2,1)S(1)}, u32[]{:S(2)}, u32[]{:S(2)}) %collective-permute-start.4) | collective-permute-done | bytes 262176 | tf_op jit(solution)/shard_map/ppermute | solution.py:50
  59.6 1.7 %collective-permute-start.6 = (bf16[512,256]{1,0:T(8,128)(2,1)S(1)}, bf16[512,256]{1,0:T(8,128)(2,1)S(1)}, u32[]{:S(2)}, u32[]{:S(2)}) collective-permute-start(bf16[512,256]{1,0:T(8,128)(2,1)S(1)} %collective-permute-done.4.refs_2_), channel_id=1, source_target_pairs={{0,4},{4,0},{8,12},{12,8},{1,5},{5,1},{9,13},{13,9},{2,6},{6,2},{1... | collective-permute-start | bytes 786440 | tf_op jit(solution)/shard_map/ppermute | solution.py:50
  61.2 0.3 collective-permute-start.5
  61.5 0.7 collective-permute-start.12
  62.2 1.3 %collective-permute-start.13 = (bf16[512,256]{1,0:T(8,128)(2,1)S(1)}, bf16[512,256]{1,0:T(8,128)(2,1)S(1)}, u32[]{:S(2)}, u32[]{:S(2)}) collective-permute-start(bf16[512,256]{1,0:T(8,128)(2,1)S(1)} %collective-permute-done.7.refs_0_), channel_id=1, source_target_pairs={{4,0},{8,12},{5,1},{9,13},{6,2},{10,14},{7,3},{11,15},{20,16},{24,... | collective-permute-start | bytes 786440 | tf_op jit(solution)/shard_map/ppermute | solution.py:596
  63.5 2.2 %products.3.refs_5_ = f32[512,1280]{1,0:T(8,128)S(1)} custom-call(s32[6]{0:T(128)S(1)} %stack.31.where_ref, bf16[512,256]{1,0:T(8,128)(2,1)S(1)} %collective-permute-done.7.refs_0_, bf16[512,256]{1,0:T(8,128)(2,1)S(1)} %collective-permute-done.8.refs_1_, bf16[1024,1280]{1,0:T(8,128)(2,1)S(1)} %copy-done, bf16[1024,1280]{1,0:T(8,128)(2,1)S(1)} %copy-done, ...), custom_call_target="tpu_custom_call" | custom-call | flops 1 | tf_op jit(solution)/shard_map/products/pallas_call | solution.py:440
  65.8 7.0 %collective-permute-done.6.refs_4_ = bf16[512,256]{1,0:T(8,128)(2,1)S(1)} collective-permute-done((bf16[512,256]{1,0:T(8,128)(2,1)S(1)}, bf16[512,256]{1,0:T(8,128)(2,1)S(1)}, u32[]{:S(2)}, u32[]{:S(2)}) %collective-permute-start.6) | collective-permute-done | bytes 262176 | tf_op jit(solution)/shard_map/ppermute | solution.py:50
  72.7 4.3 %collective-permute-done.5.refs_3_ = bf16[512,256]{1,0:T(8,128)(2,1)S(1)} collective-permute-done((bf16[512,256]{1,0:T(8,128)(2,1)S(1)}, bf16[512,256]{1,0:T(8,128)(2,1)S(1)}, u32[]{:S(2)}, u32[]{:S(2)}) %collective-permute-start.5) | collective-permute-done | bytes 262176 | tf_op jit(solution)/shard_map/ppermute | solution.py:50
  77.0 0.7 collective-permute-start.9
  77.7 1.3 %collective-permute-start.10 = (bf16[512,256]{1,0:T(8,128)(2,1)S(1)}, bf16[512,256]{1,0:T(8,128)(2,1)S(1)}, u32[]{:S(2)}, u32[]{:S(2)}) collective-permute-start(bf16[512,256]{1,0:T(8,128)(2,1)S(1)} %collective-permute-done.5.refs_3_), channel_id=1, source_target_pairs={{4,0},{8,12},{5,1},{9,13},{6,2},{10,14},{7,3},{11,15},{20,16},{24,... | collective-permute-start | bytes 786440 | tf_op jit(solution)/shard_map/ppermute | solution.py:596
  79.0 4.0 %first.1.acc_in = f32[512,1280]{1,0:T(8,128)S(1)} custom-call(s32[6]{0:T(128)S(1)} %stack.31.where_ref, bf16[512,256]{1,0:T(8,128)(2,1)S(1)} %collective-permute-done.12.refs_0_, bf16[512,256]{1,0:T(8,128)(2,1)S(1)} %collective-permute-done.13.refs_1_, bf16[512,256]{1,0:T(8,128)(2,1)S(1)} %collective-permute-done.4.refs_2_, ...), custom_call_target="tpu_custom_call" | custom-call | flops 1 | tf_op jit(solution)/shard_map/first/pallas_call | solution.py:488
  83.0 3.0 %collective-permute-done.10.more = bf16[512,256]{1,0:T(8,128)(2,1)S(1)} collective-permute-done((bf16[512,256]{1,0:T(8,128)(2,1)S(1)}, bf16[512,256]{1,0:T(8,128)(2,1)S(1)}, u32[]{:S(2)}, u32[]{:S(2)}) %collective-permute-start.10) | collective-permute-done | bytes 262176 | tf_op jit(solution)/shard_map/ppermute | solution.py:596
  85.9 1.1 %second.3 = (bf16[4,64,640]{2,1,0:T(8,128)(2,1)S(1)}, bf16[4,64,640]{2,1,0:T(8,128)(2,1)S(1)}) custom-call(s32[6]{0:T(128)S(1)} %stack.31.where_ref, bf16[512,256]{1,0:T(8,128)(2,1)S(1)} %collective-permute-done.9.slot, bf16[512,256]{1,0:T(8,128)(2,1)S(1)} %collective-permute-done.10.more, bf16[512,1280]{1,0:T(8,128)(2,1)S(1)} %collective-permute-done.refs_7_.fetched_ref, ...), custom_call_target="tpu_custom_call" | custom-call | flops 1 | tf_op jit(solution)/shard_map/second/pallas_call | solution.py:529
  87.0 0.0 copy-start.4
  87.1 0.0 copy-start.5
  87.1 0.1 collective-permute-start.18
  87.2 1.1 %second.2 = (bf16[4,64,640]{2,1,0:T(8,128)(2,1)S(1)}, bf16[4,64,640]{2,1,0:T(8,128)(2,1)S(1)}) custom-call(s32[6]{0:T(128)S(1)} %stack.31.where_ref, bf16[512,256]{1,0:T(8,128)(2,1)S(1)} %collective-permute-done.9.slot, bf16[512,256]{1,0:T(8,128)(2,1)S(1)} %collective-permute-done.10.more, bf16[512,1280]{1,0:T(8,128)(2,1)S(1)} %collective-permute-done.refs_7_.fetched_ref, ...), custom_call_target="tpu_custom_call" | custom-call | flops 1 | tf_op jit(solution)/shard_map/second/pallas_call | solution.py:529
  88.3 0.6 collective-permute-start.14
  88.8 0.6 add.8
  89.5 1.1 %collective-permute-start.19 = (bf16[64,640]{1,0:T(8,128)(2,1)S(1)}, bf16[64,640]{1,0:T(8,128)(2,1)S(1)}, u32[]{:S(2)}, u32[]{:S(2)}) collective-permute-start(bf16[64,640]{1,0:T(8,128)(2,1)S(1)} %get-tuple-element.68), channel_id=1, source_target_pairs={{0,12},{4,8},{8,4},{12,0},{1,13},{5,9},{9,5},{13,1},{2,14},{6,10},... | collective-permute-start | bytes 245768 | tf_op jit(solution)/shard_map/ppermute | solution.py:50
  90.6 1.6 %collective-permute-start.20 = (bf16[64,640]{1,0:T(8,128)(2,1)S(1)}, bf16[64,640]{1,0:T(8,128)(2,1)S(1)}, u32[]{:S(2)}, u32[]{:S(2)}) collective-permute-start(bf16[64,640]{1,0:T(8,128)(2,1)S(1)} %get-tuple-element.69), channel_id=1, source_target_pairs={{0,8},{4,12},{8,0},{12,4},{1,9},{5,13},{9,1},{13,5},{2,10},{6,14},... | collective-permute-start | bytes 245768 | tf_op jit(solution)/shard_map/ppermute | solution.py:50
  92.2 1.7 %collective-permute-start.21 = (bf16[64,640]{1,0:T(8,128)(2,1)S(1)}, bf16[64,640]{1,0:T(8,128)(2,1)S(1)}, u32[]{:S(2)}, u32[]{:S(2)}) collective-permute-start(bf16[64,640]{1,0:T(8,128)(2,1)S(1)} %get-tuple-element.70), channel_id=1, source_target_pairs={{0,4},{4,0},{8,12},{12,8},{1,5},{5,1},{9,13},{13,9},{2,6},{6,2},{1... | collective-permute-start | bytes 245768 | tf_op jit(solution)/shard_map/ppermute | solution.py:50
  93.9 0.6 add.7
  94.5 1.1 %collective-permute-start.15 = (bf16[64,640]{1,0:T(8,128)(2,1)S(1)}, bf16[64,640]{1,0:T(8,128)(2,1)S(1)}, u32[]{:S(2)}, u32[]{:S(2)}) collective-permute-start(bf16[64,640]{1,0:T(8,128)(2,1)S(1)} %get-tuple-element.62), channel_id=1, source_target_pairs={{0,12},{4,8},{8,4},{12,0},{1,13},{5,9},{9,5},{13,1},{2,14},{6,10},... | collective-permute-start | bytes 245768 | tf_op jit(solution)/shard_map/ppermute | solution.py:50
  95.7 0.7 collective-permute-start.16
  96.4 0.3 collective-permute-done.19.refs_5_
  96.7 3.2 %collective-permute-start.17 = (bf16[64,640]{1,0:T(8,128)(2,1)S(1)}, bf16[64,640]{1,0:T(8,128)(2,1)S(1)}, u32[]{:S(2)}, u32[]{:S(2)}) collective-permute-start(bf16[64,640]{1,0:T(8,128)(2,1)S(1)} %get-tuple-element.64), channel_id=1, source_target_pairs={{0,4},{4,0},{8,12},{12,8},{1,5},{5,1},{9,13},{13,9},{2,6},{6,2},{1... | collective-permute-start | bytes 245768 | tf_op jit(solution)/shard_map/ppermute | solution.py:50
  99.9 4.2 %collective-permute-done.20.refs_6_ = bf16[64,640]{1,0:T(8,128)(2,1)S(1)} collective-permute-done((bf16[64,640]{1,0:T(8,128)(2,1)S(1)}, bf16[64,640]{1,0:T(8,128)(2,1)S(1)}, u32[]{:S(2)}, u32[]{:S(2)}) %collective-permute-start.20) | collective-permute-done | bytes 81952 | tf_op jit(solution)/shard_map/ppermute | solution.py:50
  104.2 2.7 %collective-permute-done.16.refs_2_ = bf16[64,640]{1,0:T(8,128)(2,1)S(1)} collective-permute-done((bf16[64,640]{1,0:T(8,128)(2,1)S(1)}, bf16[64,640]{1,0:T(8,128)(2,1)S(1)}, u32[]{:S(2)}, u32[]{:S(2)}) %collective-permute-start.16) | collective-permute-done | bytes 81952 | tf_op jit(solution)/shard_map/ppermute | solution.py:50
  106.9 1.6 %mix.1 = bf16[64,5120]{1,0:T(8,128)(2,1)} custom-call(s32[6]{0:T(128)S(1)} %stack.31.where_ref, bf16[64,5120]{1,0:T(8,128)(2,1)S(1)} %copy-done.4, f32[1,5120]{1,0:T(1,128)S(1)} %bitcast.14, bf16[64,640]{1,0:T(8,128)(2,1)S(1)} %get-tuple-element.61.refs_0_, bf16[64,640]{1,0:T(8,128)(2,1)S(1)} %collective-permute-done.15.refs_1_, ...), custom_call_target="tpu_custom_call" | custom-call | flops 1 | tf_op jit(solution)/shard_map/mix/pallas_call | solution.py:625
  (30 shorter events, 0.1 us)
Async XLA Ops:
  0.0 3.7 %copy-start = (bf16[1024,1280]{1,0:T(8,128)(2,1)S(1)}, bf16[1024,1280]{1,0:T(8,128)(2,1)}, u32[]{:S(2)}) copy-start(bf16[1024,1280]{1,0:T(8,128)(2,1)} %refs_6_) | copy-start | bytes 7864324
  3.5 7.8 %copy-start.7 = (bf16[3,256,256]{2,1,0:T(8,128)(2,1)S(1)}, bf16[3,256,256]{2,1,0:T(8,128)(2,1)}, u32[]{:S(2)}) copy-start(bf16[3,256,256]{2,1,0:T(8,128)(2,1)} %get-tuple-element.40) | copy-start | bytes 1179652
  3.6 8.1 %copy-start.3 = (bf16[256,1024]{1,0:T(8,128)(2,1)S(1)}, bf16[256,1024]{1,0:T(8,128)(2,1)}, u32[]{:S(2)}) copy-start(bf16[256,1024]{1,0:T(8,128)(2,1)} %q_ref.3) | copy-start | bytes 1572868
  3.6 8.1 %copy-start.6 = (s32[2,2,8]{2,1,0:T(2,128)S(1)}, s32[2,2,8]{2,1,0:T(2,128)}, u32[]{:S(2)}) copy-start(s32[2,2,8]{2,1,0:T(2,128)} %exps_ref.3) | copy-start | bytes 388
  3.7 3.7 %copy-start.9 = (bf16[3,256,256]{2,1,0:T(8,128)(2,1)S(1)}, bf16[3,256,256]{2,1,0:T(8,128)(2,1)}, u32[]{:S(2)}) copy-start(bf16[3,256,256]{2,1,0:T(8,128)(2,1)} %get-tuple-element.38) | copy-start | bytes 1179652
  3.7 6.3 %copy-start.8 = (bf16[3,256,256]{2,1,0:T(8,128)(2,1)S(1)}, bf16[3,256,256]{2,1,0:T(8,128)(2,1)}, u32[]{:S(2)}) copy-start(bf16[3,256,256]{2,1,0:T(8,128)(2,1)} %get-tuple-element.39) | copy-start | bytes 1179652
  3.7 8.0 %copy-start.2 = (bf16[2,256,1024]{2,1,0:T(8,128)(2,1)S(1)}, bf16[2,256,1024]{2,1,0:T(8,128)(2,1)}, u32[]{:S(2)}) copy-start(bf16[2,256,1024]{2,1,0:T(8,128)(2,1)} %fresh_ref.3) | copy-start | bytes 3145732
  4.4 31.8 %collective-permute-start = (bf16[512,1280]{1,0:T(8,128)(2,1)S(1)}, bf16[512,1280]{1,0:T(8,128)(2,1)S(1)}, u32[]{:S(2)}, u32[]{:S(2)}) collective-permute-start(bf16[512,1280]{1,0:T(8,128)(2,1)S(1)} %take.1), channel_id=1, source_target_pairs={{0,2},{2,0},{1,3},{3,1},{4,6},{6,4},{5,7},{7,5},{8,10},{10,8},{9,1... | collective-permute-start | bytes 3932168 | tf_op jit(solution)/shard_map/ppermute | solution.py:50
  7.4 30.5 %collective-permute-start.2 = (bf16[3,256,256]{2,1,0:T(8,128)(2,1)S(1)}, bf16[3,256,256]{2,1,0:T(8,128)(2,1)S(1)}, u32[]{:S(2)}, u32[]{:S(2)}) collective-permute-start(bf16[3,256,256]{2,1,0:T(8,128)(2,1)S(1)} %copy-done.9), channel_id=1, source_target_pairs={{0,8},{4,12},{8,0},{12,4},{1,9},{5,13},{9,1},{13,5},{2,10},{6,14},... | collective-permute-start | bytes 1179656 | tf_op jit(solution)/shard_map/ppermute | solution.py:50
  10.0 28.0 %collective-permute-start.3 = (bf16[3,256,256]{2,1,0:T(8,128)(2,1)S(1)}, bf16[3,256,256]{2,1,0:T(8,128)(2,1)S(1)}, u32[]{:S(2)}, u32[]{:S(2)}) collective-permute-start(bf16[3,256,256]{2,1,0:T(8,128)(2,1)S(1)} %copy-done.8), channel_id=1, source_target_pairs={{0,12},{4,8},{8,4},{12,0},{1,13},{5,9},{9,5},{13,1},{2,14},{6,10},... | collective-permute-start | bytes 1179656 | tf_op jit(solution)/shard_map/ppermute | solution.py:50
  11.3 26.6 %collective-permute-start.1 = (bf16[3,256,256]{2,1,0:T(8,128)(2,1)S(1)}, bf16[3,256,256]{2,1,0:T(8,128)(2,1)S(1)}, u32[]{:S(2)}, u32[]{:S(2)}) collective-permute-start(bf16[3,256,256]{2,1,0:T(8,128)(2,1)S(1)} %copy-done.7), channel_id=1, source_target_pairs={{0,4},{4,0},{8,12},{12,8},{1,5},{5,1},{9,13},{13,9},{2,6},{6,2},{1... | collective-permute-start | bytes 1179656 | tf_op jit(solution)/shard_map/ppermute | solution.py:50
  11.6 2.2 %copy-start.1 = (bf16[2,1024,1024]{2,1,0:T(8,128)(2,1)S(1)}, bf16[2,1024,1024]{2,1,0:T(8,128)(2,1)}, u32[]{:S(2)}) copy-start(bf16[2,1024,1024]{2,1,0:T(8,128)(2,1)} %cached_ref.3) | copy-start | bytes 12582916
  36.2 42.8 %collective-permute-start.11 = (bf16[512,1280]{1,0:T(8,128)(2,1)S(1)}, bf16[512,1280]{1,0:T(8,128)(2,1)S(1)}, u32[]{:S(2)}, u32[]{:S(2)}) collective-permute-start(bf16[512,1280]{1,0:T(8,128)(2,1)S(1)} %collective-permute-done.refs_7_.fetched_ref), channel_id=1, source_target_pairs={{0,16},{16,0},{1,17},{17,1},{2,18},{18,2},{3,19},{19,3},{4,20},{20... | collective-permute-start | bytes 3932168 | tf_op jit(solution)/shard_map/ppermute | solution.py:50
  40.3 21.3 %collective-permute-start.8 = (bf16[512,256]{1,0:T(8,128)(2,1)S(1)}, bf16[512,256]{1,0:T(8,128)(2,1)S(1)}, u32[]{:S(2)}, u32[]{:S(2)}) collective-permute-start(bf16[512,256]{1,0:T(8,128)(2,1)S(1)} %bitcast.9), channel_id=1, source_target_pairs={{0,4},{4,0},{8,12},{12,8},{1,5},{5,1},{9,13},{13,9},{2,6},{6,2},{1... | collective-permute-start | bytes 786440 | tf_op jit(solution)/shard_map/ppermute | solution.py:50
  47.2 14.3 %collective-permute-start.7 = (bf16[512,256]{1,0:T(8,128)(2,1)S(1)}, bf16[512,256]{1,0:T(8,128)(2,1)S(1)}, u32[]{:S(2)}, u32[]{:S(2)}) collective-permute-start(bf16[512,256]{1,0:T(8,128)(2,1)S(1)} %bitcast.10), channel_id=1, source_target_pairs={{0,8},{4,12},{8,0},{12,4},{1,9},{5,13},{9,1},{13,5},{2,10},{6,14},... | collective-permute-start | bytes 786440 | tf_op jit(solution)/shard_map/ppermute | solution.py:50
  51.6 8.0 %collective-permute-start.4 = (bf16[512,256]{1,0:T(8,128)(2,1)S(1)}, bf16[512,256]{1,0:T(8,128)(2,1)S(1)}, u32[]{:S(2)}, u32[]{:S(2)}) collective-permute-start(bf16[512,256]{1,0:T(8,128)(2,1)S(1)} %bitcast.13), channel_id=1, source_target_pairs={{0,2},{2,0},{1,3},{3,1},{4,6},{6,4},{5,7},{7,5},{8,10},{10,8},{9,1... | collective-permute-start | bytes 786440 | tf_op jit(solution)/shard_map/ppermute | solution.py:50
  59.6 13.2 %collective-permute-start.6 = (bf16[512,256]{1,0:T(8,128)(2,1)S(1)}, bf16[512,256]{1,0:T(8,128)(2,1)S(1)}, u32[]{:S(2)}, u32[]{:S(2)}) collective-permute-start(bf16[512,256]{1,0:T(8,128)(2,1)S(1)} %collective-permute-done.4.refs_2_), channel_id=1, source_target_pairs={{0,4},{4,0},{8,12},{12,8},{1,5},{5,1},{9,13},{13,9},{2,6},{6,2},{1... | collective-permute-start | bytes 786440 | tf_op jit(solution)/shard_map/ppermute | solution.py:50
  61.2 15.8 %collective-permute-start.5 = (bf16[512,256]{1,0:T(8,128)(2,1)S(1)}, bf16[512,256]{1,0:T(8,128)(2,1)S(1)}, u32[]{:S(2)}, u32[]{:S(2)}) collective-permute-start(bf16[512,256]{1,0:T(8,128)(2,1)S(1)} %collective-permute-done.4.refs_2_), channel_id=1, source_target_pairs={{0,8},{4,12},{8,0},{12,4},{1,9},{5,13},{9,1},{13,5},{2,10},{6,14},... | collective-permute-start | bytes 786440 | tf_op jit(solution)/shard_map/ppermute | solution.py:50
  61.5 17.4 %collective-permute-start.12 = (bf16[512,256]{1,0:T(8,128)(2,1)S(1)}, bf16[512,256]{1,0:T(8,128)(2,1)S(1)}, u32[]{:S(2)}, u32[]{:S(2)}) collective-permute-start(bf16[512,256]{1,0:T(8,128)(2,1)S(1)} %bitcast.12), channel_id=1, source_target_pairs={{4,8},{8,4},{5,9},{9,5},{6,10},{10,6},{7,11},{11,7},{20,24},{24,20... | collective-permute-start | bytes 786440 | tf_op jit(solution)/shard_map/ppermute | solution.py:50
  62.2 16.8 %collective-permute-start.13 = (bf16[512,256]{1,0:T(8,128)(2,1)S(1)}, bf16[512,256]{1,0:T(8,128)(2,1)S(1)}, u32[]{:S(2)}, u32[]{:S(2)}) collective-permute-start(bf16[512,256]{1,0:T(8,128)(2,1)S(1)} %collective-permute-done.7.refs_0_), channel_id=1, source_target_pairs={{4,0},{8,12},{5,1},{9,13},{6,2},{10,14},{7,3},{11,15},{20,16},{24,... | collective-permute-start | bytes 786440 | tf_op jit(solution)/shard_map/ppermute | solution.py:596
  77.0 6.0 %collective-permute-start.9 = (bf16[512,256]{1,0:T(8,128)(2,1)S(1)}, bf16[512,256]{1,0:T(8,128)(2,1)S(1)}, u32[]{:S(2)}, u32[]{:S(2)}) collective-permute-start(bf16[512,256]{1,0:T(8,128)(2,1)S(1)} %collective-permute-done.4.refs_2_), channel_id=1, source_target_pairs={{4,8},{8,4},{5,9},{9,5},{6,10},{10,6},{7,11},{11,7},{20,24},{24,20... | collective-permute-start | bytes 786440 | tf_op jit(solution)/shard_map/ppermute | solution.py:50
  77.7 8.3 %collective-permute-start.10 = (bf16[512,256]{1,0:T(8,128)(2,1)S(1)}, bf16[512,256]{1,0:T(8,128)(2,1)S(1)}, u32[]{:S(2)}, u32[]{:S(2)}) collective-permute-start(bf16[512,256]{1,0:T(8,128)(2,1)S(1)} %collective-permute-done.5.refs_3_), channel_id=1, source_target_pairs={{4,0},{8,12},{5,1},{9,13},{6,2},{10,14},{7,3},{11,15},{20,16},{24,... | collective-permute-start | bytes 786440 | tf_op jit(solution)/shard_map/ppermute | solution.py:596
  87.0 19.9 %copy-start.4 = (bf16[64,5120]{1,0:T(8,128)(2,1)S(1)}, bf16[64,5120]{1,0:T(8,128)(2,1)}, u32[]{:S(2)}) copy-start(bf16[64,5120]{1,0:T(8,128)(2,1)} %hidden_ref.1) | copy-start | bytes 1966084
  87.1 19.9 %copy-start.5 = (f32[5120]{0:T(1024)S(1)}, f32[5120]{0:T(1024)}, u32[]{:S(2)}) copy-start(f32[5120]{0:T(1024)} %param.13) | copy-start | bytes 61444
  87.1 1.8 %collective-permute-start.18 = (bf16[4,64,640]{2,1,0:T(8,128)(2,1)S(1)}, bf16[4,64,640]{2,1,0:T(8,128)(2,1)S(1)}, u32[]{:S(2)}, u32[]{:S(2)}) collective-permute-start(bf16[4,64,640]{2,1,0:T(8,128)(2,1)S(1)} %get-tuple-element.66), channel_id=1, source_target_pairs={{0,1},{1,0},{2,3},{3,2},{4,5},{5,4},{6,7},{7,6},{8,9},{9,8},{10,11... | collective-permute-start | bytes 983048 | tf_op jit(solution)/shard_map/ppermute | solution.py:50
  88.3 5.6 %collective-permute-start.14 = (bf16[4,64,640]{2,1,0:T(8,128)(2,1)S(1)}, bf16[4,64,640]{2,1,0:T(8,128)(2,1)S(1)}, u32[]{:S(2)}, u32[]{:S(2)}) collective-permute-start(bf16[4,64,640]{2,1,0:T(8,128)(2,1)S(1)} %get-tuple-element.60), channel_id=1, source_target_pairs={{0,1},{1,0},{2,3},{3,2},{4,5},{5,4},{6,7},{7,6},{8,9},{9,8},{10,11... | collective-permute-start | bytes 983048 | tf_op jit(solution)/shard_map/ppermute | solution.py:50
  89.5 7.3 %collective-permute-start.19 = (bf16[64,640]{1,0:T(8,128)(2,1)S(1)}, bf16[64,640]{1,0:T(8,128)(2,1)S(1)}, u32[]{:S(2)}, u32[]{:S(2)}) collective-permute-start(bf16[64,640]{1,0:T(8,128)(2,1)S(1)} %get-tuple-element.68), channel_id=1, source_target_pairs={{0,12},{4,8},{8,4},{12,0},{1,13},{5,9},{9,5},{13,1},{2,14},{6,10},... | collective-permute-start | bytes 245768 | tf_op jit(solution)/shard_map/ppermute | solution.py:50
  90.6 13.6 %collective-permute-start.20 = (bf16[64,640]{1,0:T(8,128)(2,1)S(1)}, bf16[64,640]{1,0:T(8,128)(2,1)S(1)}, u32[]{:S(2)}, u32[]{:S(2)}) collective-permute-start(bf16[64,640]{1,0:T(8,128)(2,1)S(1)} %get-tuple-element.69), channel_id=1, source_target_pairs={{0,8},{4,12},{8,0},{12,4},{1,9},{5,13},{9,1},{13,5},{2,10},{6,14},... | collective-permute-start | bytes 245768 | tf_op jit(solution)/shard_map/ppermute | solution.py:50
  92.2 12.0 %collective-permute-start.21 = (bf16[64,640]{1,0:T(8,128)(2,1)S(1)}, bf16[64,640]{1,0:T(8,128)(2,1)S(1)}, u32[]{:S(2)}, u32[]{:S(2)}) collective-permute-start(bf16[64,640]{1,0:T(8,128)(2,1)S(1)} %get-tuple-element.70), channel_id=1, source_target_pairs={{0,4},{4,0},{8,12},{12,8},{1,5},{5,1},{9,13},{13,9},{2,6},{6,2},{1... | collective-permute-start | bytes 245768 | tf_op jit(solution)/shard_map/ppermute | solution.py:50
  94.5 9.6 %collective-permute-start.15 = (bf16[64,640]{1,0:T(8,128)(2,1)S(1)}, bf16[64,640]{1,0:T(8,128)(2,1)S(1)}, u32[]{:S(2)}, u32[]{:S(2)}) collective-permute-start(bf16[64,640]{1,0:T(8,128)(2,1)S(1)} %get-tuple-element.62), channel_id=1, source_target_pairs={{0,12},{4,8},{8,4},{12,0},{1,13},{5,9},{9,5},{13,1},{2,14},{6,10},... | collective-permute-start | bytes 245768 | tf_op jit(solution)/shard_map/ppermute | solution.py:50
  95.7 11.2 %collective-permute-start.16 = (bf16[64,640]{1,0:T(8,128)(2,1)S(1)}, bf16[64,640]{1,0:T(8,128)(2,1)S(1)}, u32[]{:S(2)}, u32[]{:S(2)}) collective-permute-start(bf16[64,640]{1,0:T(8,128)(2,1)S(1)} %get-tuple-element.63), channel_id=1, source_target_pairs={{0,8},{4,12},{8,0},{12,4},{1,9},{5,13},{9,1},{13,5},{2,10},{6,14},... | collective-permute-start | bytes 245768 | tf_op jit(solution)/shard_map/ppermute | solution.py:50
  96.7 10.2 %collective-permute-start.17 = (bf16[64,640]{1,0:T(8,128)(2,1)S(1)}, bf16[64,640]{1,0:T(8,128)(2,1)S(1)}, u32[]{:S(2)}, u32[]{:S(2)}) collective-permute-start(bf16[64,640]{1,0:T(8,128)(2,1)S(1)} %get-tuple-element.64), channel_id=1, source_target_pairs={{0,4},{4,0},{8,12},{12,8},{1,5},{5,1},{9,13},{13,9},{2,6},{6,2},{1... | collective-permute-start | bytes 245768 | tf_op jit(solution)/shard_map/ppermute | solution.py:50

commit v25 on v23

--- a/solution.py
+++ b/solution.py
@@ -11,7 +11,7 @@
 HEAD_DIM = 128
 SCALE_ROWS = 128
 SATURATION = 448.0
-PACK_ROWS = 32
+PACK_ROWS = 64
 VMEM_BYTES = 32 * 1024 * 1024
 PACK_VMEM_BYTES = 60 * 1024 * 1024
 ATTEND_FLOPS = 1
@@ -390,9 +390,10 @@
         keys = jnp.concatenate([ref[1, :, lanes] for ref in pieces], axis=0)
         values = jnp.concatenate([ref[2, :, lanes] for ref in pieces], axis=0)
         values = jnp.concatenate([values, jnp.ones_like(values)], axis=1)
-        for rel, ref in enumerate(pieces):
+        for first in range(0, len(pieces), 2):
+            query = [ref[0, pl.ds(start, rows), lanes] for ref in pieces[first : first + 2]]
             scores = lax.dot_general(
-                ref[0, pl.ds(start, rows), lanes],
+                jnp.concatenate(query, axis=0),
                 keys,
                 (((1,), (1,)), ((), ())),
                 preferred_element_type=jnp.float32,
@@ -401,7 +402,9 @@
             expo = jnp.exp2((scores - peak) * factor).astype(jnp.bfloat16)
             mix = jnp.dot(expo, values, preferred_element_type=jnp.float32)
             mix = (mix[:, :HEAD_DIM] / mix[:, HEAD_DIM:]).astype(jnp.bfloat16)
-            out[where_ref[NEAR] ^ rel, :, lanes] = mix
+            for at in range(len(query)):
+                block = mix[at * rows : (at + 1) * rows]
+                out[where_ref[NEAR] ^ (first + at), :, lanes] = block
 
 
 def attend_half(where, half, pieces):
@@ -449,10 +452,19 @@
     return (head + FETCHED * where_ref[GRP]) % 8
 
 
+def from_next(where_ref, up, down):
+    return jnp.where(where_ref[PATCH] % 2 == 1, up[...], down[...])
+
+
+def from_last(where_ref, up, down, ends):
+    inner = jnp.where(where_ref[PATCH] % 2 == 1, down[...], up[...])
+    return jnp.where(where_ref[INNER] == 1, inner, ends[...])
+
+
 def first_kernel(where_ref, *refs):
-    last, more, slots = refs[0], refs[1], refs[2:5]
-    acc_ref, own_ref, fetched_ref, passed_ref, out_ref, held_ref = refs[5:]
-    rows, feat = last.shape
+    mine, (own, far, up, down), refs = refs[:3], refs[3:7], refs[7:]
+    acc_ref, near_ref, last_ref, fetched_ref, passed_ref, out_ref, held_ref = refs
+    rows, feat = own.shape
     cut = fetched_ref.shape[0]
 
     def put(at, block):
@@ -463,20 +475,24 @@
 
     @pl.when(pl.program_id(0) == 0)
     def arrange():
-        for at, slot in zip((0, 2, 1), slots):
-            put(at, slot[...])
+        put(0, own[...])
+        put(2, far[...])
+        put(1, from_next(where_ref, up, down))
         put(3, jnp.zeros((rows, feat), jnp.bfloat16))
 
-    block = jnp.where(where_ref[INNER] == 1, last[...], more[...])
+    block = jnp.concatenate(
+        [from_next(where_ref, *mine[:2]), from_last(where_ref, *mine)], axis=1
+    )
+    weight = jnp.concatenate([near_ref[...], last_ref[...]], axis=0)
     acc = acc_ref[...]
-    acc += jnp.dot(block, own_ref[...], preferred_element_type=jnp.float32)
+    acc += jnp.dot(block, weight, preferred_element_type=jnp.float32)
     acc += jnp.dot(held_ref[:, :cut], fetched_ref[...], preferred_element_type=jnp.float32)
     acc += jnp.dot(held_ref[:, cut:], passed_ref[...], preferred_element_type=jnp.float32)
     out_ref[...] = acc
 
 
-def first_product(where, last, more, slots, acc, weights):
-    rows, feat = last.shape
+def first_product(where, mine, partner, acc, weights):
+    rows, feat = mine[0].shape
     own, fetched, passed = weights
     wide = own.shape[1] // 2
     whole = pl.BlockSpec((rows, wide), lambda i, w: (0, i))
@@ -485,15 +501,18 @@
         "first",
         jax.ShapeDtypeStruct(acc.shape, jnp.float32),
         2,
-        [spec((rows, feat))] * 5
-        + [whole, pl.BlockSpec((feat, wide), lambda i, w: (w[NEAR] ^ 3, i))]
+        [spec((rows, feat))] * 7
+        + [whole]
+        + [pl.BlockSpec((feat, wide), lambda i, w, at=at: (w[NEAR] ^ at, i)) for at in (1, 3)]
         + [pl.BlockSpec((x.shape[0], wide), lambda i, w: (0, i)) for x in (fetched, passed)],
         whole,
         [pltpu.VMEM((rows, 4 * feat), jnp.bfloat16)],
-    )(where, last, more, *slots, acc, own, fetched, passed)
-
-
-def second_kernel(where_ref, slot, more, fetched_ref, passed_ref, acc_in, keep_ref, send_ref, acc_ref):
+    )(where, *mine, *partner, acc, own, own, fetched, passed)
+
+
+def second_kernel(where_ref, *refs):
+    slots, refs = refs[:3], refs[3:]
+    fetched_ref, passed_ref, acc_in, keep_ref, send_ref, acc_ref = refs
     weight = []
     for head in range(2):
         place = partner_place(where_ref, 2 * (where_ref[NEAR] ^ 3) + head)
@@ -506,9 +525,8 @@
                 passed_ref[pl.ds(pl.multiple_of(there, HEAD_DIM), HEAD_DIM), :],
             )
         )
-    block = jnp.where(where_ref[INNER] == 1, slot[...], more[...])
     acc = acc_in[...] + jnp.dot(
-        block, jnp.concatenate(weight, axis=0), preferred_element_type=jnp.float32
+        from_last(where_ref, *slots), jnp.concatenate(weight, axis=0), preferred_element_type=jnp.float32
     )
     acc_ref[...] = acc.reshape(acc_ref.shape)
     for sub, out in enumerate((keep_ref, send_ref)):
@@ -516,8 +534,8 @@
             out[at] = acc_ref[where_ref[NEAR] ^ at, where_ref[SUB] ^ sub].astype(jnp.bfloat16)
 
 
-def second_product(where, chunk, slot, more, weights, acc):
-    rows, feat = slot.shape
+def second_product(where, chunk, slots, weights, acc):
+    rows, feat = slots[0].shape
     cols = weights[0].shape[1]
     wide = cols // 2
     out = jax.ShapeDtypeStruct((4, rows // 8, wide), jnp.bfloat16)
@@ -526,12 +544,12 @@
         "second",
         [out] * 2,
         1,
-        [spec((rows, feat))] * 2
+        [spec((rows, feat))] * 3
         + [pl.BlockSpec((x.shape[0], wide), lambda i, w: (0, chunk)) for x in weights]
         + [pl.BlockSpec((rows, wide), lambda i, w: (0, chunk))],
         [spec(out.shape)] * 2,
         [pltpu.VMEM((4, 2, rows // 8, wide), jnp.float32)],
-    )(where, slot, more, *weights, acc)
+    )(where, *slots, *weights, acc)
 
 
 def add_kernel(where_ref, keep_ref, term_ref, *outs):
@@ -582,18 +600,18 @@
     other, acc = lax.optimization_barrier((other, acc))
     slots = []
     for at, x in enumerate((mine, other)):
-        next_to, far = swap(x, "patch", 4, 1), swap(x, "patch", 4, 2)
-        next_to, far, other, x = lax.optimization_barrier((next_to, far, other, x))
+        down = lax.ppermute(x, "patch", [(1, 0), (2, 1), (3, 2)])
+        up = lax.ppermute(x, "patch", [(0, 1), (1, 2), (2, 3)])
+        far = swap(x, "patch", 4, 2)
+        down, up, far, other, x = lax.optimization_barrier((down, up, far, other, x))
         if at == 1:
-            acc = add_product(where, {2: slots[0][2], 1: slots[0][1]}, out_weight, acc)
+            acc = add_product(where, {2: slots[0][1]}, out_weight, acc)
             far, x, acc = lax.optimization_barrier((far, x, acc))
-        middle = swap(x, "patch", 4, 3, (1, 2))
         ends = lax.ppermute(far, "patch", [(1, 0), (2, 3)])
-        slots.append([x, next_to, far, middle, ends])
+        slots.append([x, far, up, down, ends])
     weights = [out_weight, fetched, passed]
-    partner = [slots[1][at] for at in (0, 2, 1)]
-    acc = first_product(where, *slots[0][3:], partner, acc, weights)
-    terms = [second_product(where, at, *slots[1][3:], [fetched, passed], acc) for at in range(2)]
+    acc = first_product(where, slots[0][2:], slots[1][:4], acc, weights)
+    terms = [second_product(where, at, slots[1][2:], [fetched, passed], acc) for at in range(2)]
     blocks = []
     for keep, send in terms:
         total = add(where, keep, swap(send, "sub", 2, 1))

time: 105 us -> 114 us (1.086)
  starting transfers between devices: 28.4 us -> 33.7 us
  waiting for transfers between devices: 50.7 us -> 54.6 us
    ppermute x0 -> x4, starting transfers between devices: none -> 9.73 us  [the longest x2 7.15 us: share_tail(): up = lax.ppermute(x, 'patch', [(0, 1), (1, 2), (2, 3)])]
    ppermute x0 -> x4, waiting for transfers between devices: none -> 5.64 us  [the longest x2 5.64 us: share_tail(): down = lax.ppermute(x, 'patch', [(1, 0), (2, 1), (3, 2)])]
    ppermute x20 -> x16, starting transfers between devices: 25.8 us -> 21.4 us  [swap(): return lax.ppermute(x, axes, pairs)]
    ppermute x20 -> x16, waiting for transfers between devices: 46.8 us -> 44.6 us  [swap(): return lax.ppermute(x, axes, pairs)]
  transfers between devices with their start and end apart: 22 -> 22, of which waited for: 11 -> 10; matrix products, arithmetic and copies ran while one was open for 0% -> 0% of each run, Pallas kernels for 15% -> 14%
where the time goes in v25:
time: 114 us
  waiting for transfers between devices  54.6 us (48%)
  starting transfers between devices  33.7 us (30%)
  Pallas kernels  22.9 us (20%)
  local copies, waits for them, and re-layouts  2.32 us (2%)
    ppermute x16, waiting for transfers between devices, swap(): return lax.ppermute(x, axes, pairs)  44.6 us
    ppermute x16, starting transfers between devices, swap(): return lax.ppermute(x, axes, pairs)  21.4 us
    ppermute x2, starting transfers between devices, share_tail(): up = lax.ppermute(x, 'patch', [(0, 1), (1, 2), (2, 3)])  7.15 us
    ppermute x2, waiting for transfers between devices, share_tail(): down = lax.ppermute(x, 'patch', [(1, 0), (2, 1), (3, 2)])  5.64 us
    pallas_call x2, Pallas kernels, attend_half(): call(functools.partial(attend_half_kernel, half), 'attend', out, 1, [spec...  4.63 us
    pallas_call x1, Pallas kernels, first_product(): call(first_kernel, 'first', jax.ShapeDtypeStruct(acc.shape, jnp.float32),...  4.41 us
    ppermute x2, waiting for transfers between devices, share_tail(): ends = lax.ppermute(far, 'patch', [(1, 0), (2, 3)])  4.33 us
    pallas_call x1, Pallas kernels, pack(): pl.pallas_call(functools.partial(pack_kernel, split, feat // HEAD_DIM), o...  3.53 us
  transfers between devices with their start and end apart: 22, of which 10 were waited for; matrix products, arithmetic and copies ran while one was open for 0% of the time, Pallas kernels for 14%

profile of v25, /device:TPU:0, one launch (start us, length us, event | category | flops | bytes accessed | tf_op | source)
XLA Modules:
  0.0 113.7 jit_solution(11075028213758954562)
XLA Ops:
  0.0 3.5 %pack.1 = (bf16[3,256,256]{2,1,0:T(8,128)(2,1)}, bf16[3,256,256]{2,1,0:T(8,128)(2,1)}, bf16[3,256,256]{2,1,0:T(8,128)(2,1)}) custom-call(s32[2,2,8]{2,1,0:T(2,128)} %exps_ref.3, bf16[256,1024]{1,0:T(8,128)(2,1)} %q_ref.3, bf16[2,256,1024]{2,1,0:T(8,128)(2,1)} %fresh_ref.3, bf16[2,1024,1024]{2,1,0:T(8,128)(2,1)} %cached_ref.3), custom_call_target="tpu_custom_call" | custom-call | tf_op jit(solution)/shard_map/pack/pallas_call | solution.py:114
  3.6 0.0 copy-start.6
  3.6 0.1 stack.31.where_ref
  3.7 0.7 take.1
  4.4 3.0 %collective-permute-start = (bf16[512,1280]{1,0:T(8,128)(2,1)S(1)}, bf16[512,1280]{1,0:T(8,128)(2,1)S(1)}, u32[]{:S(2)}, u32[]{:S(2)}) collective-permute-start(bf16[512,1280]{1,0:T(8,128)(2,1)S(1)} %take.1), channel_id=1, source_target_pairs={{0,2},{2,0},{1,3},{3,1},{4,6},{6,4},{5,7},{7,5},{8,10},{10,8},{9,1... | collective-permute-start | bytes 3932168 | tf_op jit(solution)/shard_map/ppermute | solution.py:50
  7.4 3.6 %collective-permute-start.3 = (bf16[3,256,256]{2,1,0:T(8,128)(2,1)S(1)}, bf16[3,256,256]{2,1,0:T(8,128)(2,1)S(1)}, u32[]{:S(2)}, u32[]{:S(2)}) collective-permute-start(bf16[3,256,256]{2,1,0:T(8,128)(2,1)S(1)} %copy-done.9), channel_id=1, source_target_pairs={{0,12},{4,8},{8,4},{12,0},{1,13},{5,9},{9,5},{13,1},{2,14},{6,10},... | collective-permute-start | bytes 1179656 | tf_op jit(solution)/shard_map/ppermute | solution.py:50
  11.0 0.8 collective-permute-start.1
  11.8 2.2 %copy-done.1 = bf16[2,1024,1024]{2,1,0:T(8,128)(2,1)S(1)} copy-done((bf16[2,1024,1024]{2,1,0:T(8,128)(2,1)S(1)}, bf16[2,1024,1024]{2,1,0:T(8,128)(2,1)}, u32[]{:S(2)}) %copy-start.1) | copy-done | bytes 4194328
  14.0 1.3 %own.1.refs_0_ = bf16[3,256,256]{2,1,0:T(8,128)(2,1)S(1)} custom-call(s32[6]{0:T(128)S(1)} %stack.31.where_ref, s32[2,2,8]{2,1,0:T(2,128)S(1)} %copy-done.6, bf16[256,1024]{1,0:T(8,128)(2,1)S(1)} %copy-done.3, bf16[2,256,1024]{2,1,0:T(8,128)(2,1)S(1)} %copy-done.2, bf16[2,1024,1024]{2,1,0:T(8,128)(2,1)S(1)} %copy-done.1), custom_call_target="tpu_custom_call" | custom-call | flops 1 | tf_op jit(solution)/shard_map/own/pallas_call | solution.py:150
  15.3 20.9 %collective-permute-done.refs_10_.refs_3_ = bf16[512,1280]{1,0:T(8,128)(2,1)S(1)} collective-permute-done((bf16[512,1280]{1,0:T(8,128)(2,1)S(1)}, bf16[512,1280]{1,0:T(8,128)(2,1)S(1)}, u32[]{:S(2)}, u32[]{:S(2)}) %collective-permute-start) | collective-permute-done | bytes 1310752 | tf_op jit(solution)/shard_map/ppermute | solution.py:50
  36.2 1.8 %collective-permute-start.12 = (bf16[512,1280]{1,0:T(8,128)(2,1)S(1)}, bf16[512,1280]{1,0:T(8,128)(2,1)S(1)}, u32[]{:S(2)}, u32[]{:S(2)}) collective-permute-start(bf16[512,1280]{1,0:T(8,128)(2,1)S(1)} %collective-permute-done.refs_10_.refs_3_), channel_id=1, source_target_pairs={{0,16},{16,0},{1,17},{17,1},{2,18},{18,2},{3,19},{19,3},{4,20},{20... | collective-permute-start | bytes 3932168 | tf_op jit(solution)/shard_map/ppermute | solution.py:50
  37.9 6.3 %collective-permute-done.2.refs_2_ = bf16[3,256,256]{2,1,0:T(8,128)(2,1)S(1)} collective-permute-done((bf16[3,256,256]{2,1,0:T(8,128)(2,1)S(1)}, bf16[3,256,256]{2,1,0:T(8,128)(2,1)S(1)}, u32[]{:S(2)}, u32[]{:S(2)}) %collective-permute-start.2) | collective-permute-done | bytes 393248 | tf_op jit(solution)/shard_map/ppermute | solution.py:50
  44.2 2.3 %attend.2 = bf16[4,128,256]{2,1,0:T(8,128)(2,1)S(1)} custom-call(s32[6]{0:T(128)S(1)} %stack.31.where_ref, bf16[3,256,256]{2,1,0:T(8,128)(2,1)S(1)} %own.1.refs_0_, bf16[3,256,256]{2,1,0:T(8,128)(2,1)S(1)} %collective-permute-done.1.refs_1_, bf16[3,256,256]{2,1,0:T(8,128)(2,1)S(1)} %collective-permute-done.2.refs_2_, ...), custom_call_target="tpu_custom_call" | custom-call | flops 1 | tf_op jit(solution)/shard_map/attend/pallas_call | solution.py:413
  46.6 0.1 collective-permute-start.10
  46.6 4.9 %collective-permute-start.9 = (bf16[512,256]{1,0:T(8,128)(2,1)S(1)}, bf16[512,256]{1,0:T(8,128)(2,1)S(1)}, u32[]{:S(2)}, u32[]{:S(2)}) collective-permute-start(bf16[512,256]{1,0:T(8,128)(2,1)S(1)} %bitcast.10), channel_id=1, source_target_pairs={{0,4},{4,8},{8,12},{1,5},{5,9},{9,13},{2,6},{6,10},{10,14},{3,7},{... | collective-permute-start | bytes 786440 | tf_op jit(solution)/shard_map/ppermute | solution.py:604
  51.6 1.3 %collective-permute-start.8 = (bf16[512,256]{1,0:T(8,128)(2,1)S(1)}, bf16[512,256]{1,0:T(8,128)(2,1)S(1)}, u32[]{:S(2)}, u32[]{:S(2)}) collective-permute-start(bf16[512,256]{1,0:T(8,128)(2,1)S(1)} %bitcast.11), channel_id=1, source_target_pairs={{4,0},{8,4},{12,8},{5,1},{9,5},{13,9},{6,2},{10,6},{14,10},{7,3},{... | collective-permute-start | bytes 786440 | tf_op jit(solution)/shard_map/ppermute | solution.py:603
  52.9 2.3 %attend.3 = bf16[4,128,256]{2,1,0:T(8,128)(2,1)S(1)} custom-call(s32[6]{0:T(128)S(1)} %stack.31.where_ref, bf16[3,256,256]{2,1,0:T(8,128)(2,1)S(1)} %own.1.refs_0_, bf16[3,256,256]{2,1,0:T(8,128)(2,1)S(1)} %collective-permute-done.1.refs_1_, bf16[3,256,256]{2,1,0:T(8,128)(2,1)S(1)} %collective-permute-done.2.refs_2_, ...), custom_call_target="tpu_custom_call" | custom-call | flops 1 | tf_op jit(solution)/shard_map/attend/pallas_call | solution.py:413
  55.2 0.6 collective-permute-start.4
  55.8 1.5 %products.2.refs_2_ = f32[512,1280]{1,0:T(8,128)S(1)} custom-call(s32[6]{0:T(128)S(1)} %stack.31.where_ref, bf16[512,256]{1,0:T(8,128)(2,1)S(1)} %bitcast.12, bf16[1024,1280]{1,0:T(8,128)(2,1)S(1)} %copy-done), custom_call_target="tpu_custom_call" | custom-call | flops 6000000000 | tf_op jit(solution)/shard_map/products/pallas_call | solution.py:438
  57.4 4.3 %collective-permute-done.4.refs_3_ = bf16[512,256]{1,0:T(8,128)(2,1)S(1)} collective-permute-done((bf16[512,256]{1,0:T(8,128)(2,1)S(1)}, bf16[512,256]{1,0:T(8,128)(2,1)S(1)}, u32[]{:S(2)}, u32[]{:S(2)}) %collective-permute-start.4) | collective-permute-done | bytes 262176 | tf_op jit(solution)/shard_map/ppermute | solution.py:50
  61.7 2.6 %collective-permute-start.7 = (bf16[512,256]{1,0:T(8,128)(2,1)S(1)}, bf16[512,256]{1,0:T(8,128)(2,1)S(1)}, u32[]{:S(2)}, u32[]{:S(2)}) collective-permute-start(bf16[512,256]{1,0:T(8,128)(2,1)S(1)} %collective-permute-done.4.refs_3_), channel_id=1, source_target_pairs={{0,8},{4,12},{8,0},{12,4},{1,9},{5,13},{9,1},{13,5},{2,10},{6,14},... | collective-permute-start | bytes 786440 | tf_op jit(solution)/shard_map/ppermute | solution.py:50
  64.3 2.2 %collective-permute-start.6 = (bf16[512,256]{1,0:T(8,128)(2,1)S(1)}, bf16[512,256]{1,0:T(8,128)(2,1)S(1)}, u32[]{:S(2)}, u32[]{:S(2)}) collective-permute-start(bf16[512,256]{1,0:T(8,128)(2,1)S(1)} %collective-permute-done.4.refs_3_), channel_id=1, source_target_pairs={{0,4},{4,8},{8,12},{1,5},{5,9},{9,13},{2,6},{6,10},{10,14},{3,7},{... | collective-permute-start | bytes 786440 | tf_op jit(solution)/shard_map/ppermute | solution.py:604
  66.5 1.3 %collective-permute-start.5 = (bf16[512,256]{1,0:T(8,128)(2,1)S(1)}, bf16[512,256]{1,0:T(8,128)(2,1)S(1)}, u32[]{:S(2)}, u32[]{:S(2)}) collective-permute-start(bf16[512,256]{1,0:T(8,128)(2,1)S(1)} %collective-permute-done.4.refs_3_), channel_id=1, source_target_pairs={{4,0},{8,4},{12,8},{5,1},{9,5},{13,9},{6,2},{10,6},{14,10},{7,3},{... | collective-permute-start | bytes 786440 | tf_op jit(solution)/shard_map/ppermute | solution.py:603
  67.8 1.3 %collective-permute-start.13 = (bf16[512,256]{1,0:T(8,128)(2,1)S(1)}, bf16[512,256]{1,0:T(8,128)(2,1)S(1)}, u32[]{:S(2)}, u32[]{:S(2)}) collective-permute-start(bf16[512,256]{1,0:T(8,128)(2,1)S(1)} %collective-permute-done.10.refs_0_), channel_id=1, source_target_pairs={{4,0},{8,12},{5,1},{9,13},{6,2},{10,14},{7,3},{11,15},{20,16},{24,... | collective-permute-start | bytes 786440 | tf_op jit(solution)/shard_map/ppermute | solution.py:610
  69.1 1.7 %products.3.refs_7_ = f32[512,1280]{1,0:T(8,128)S(1)} custom-call(s32[6]{0:T(128)S(1)} %stack.31.where_ref, bf16[512,256]{1,0:T(8,128)(2,1)S(1)} %collective-permute-done.10.refs_0_, bf16[1024,1280]{1,0:T(8,128)(2,1)S(1)} %copy-done, f32[512,1280]{1,0:T(8,128)S(1)} %products.2.refs_2_), custom_call_target="tpu_custom_call" | custom-call | flops 1 | tf_op jit(solution)/shard_map/products/pallas_call | solution.py:438
  70.9 6.0 %collective-permute-done.7.refs_4_ = bf16[512,256]{1,0:T(8,128)(2,1)S(1)} collective-permute-done((bf16[512,256]{1,0:T(8,128)(2,1)S(1)}, bf16[512,256]{1,0:T(8,128)(2,1)S(1)}, u32[]{:S(2)}, u32[]{:S(2)}) %collective-permute-start.7) | collective-permute-done | bytes 262176 | tf_op jit(solution)/shard_map/ppermute | solution.py:50
  76.9 5.6 %collective-permute-done.5.refs_6_.refs_1_ = bf16[512,256]{1,0:T(8,128)(2,1)S(1)} collective-permute-done((bf16[512,256]{1,0:T(8,128)(2,1)S(1)}, bf16[512,256]{1,0:T(8,128)(2,1)S(1)}, u32[]{:S(2)}, u32[]{:S(2)}) %collective-permute-start.5) | collective-permute-done | bytes 262176 | tf_op jit(solution)/shard_map/ppermute | solution.py:603
  82.5 1.3 %collective-permute-start.11 = (bf16[512,256]{1,0:T(8,128)(2,1)S(1)}, bf16[512,256]{1,0:T(8,128)(2,1)S(1)}, u32[]{:S(2)}, u32[]{:S(2)}) collective-permute-start(bf16[512,256]{1,0:T(8,128)(2,1)S(1)} %collective-permute-done.7.refs_4_), channel_id=1, source_target_pairs={{4,0},{8,12},{5,1},{9,13},{6,2},{10,14},{7,3},{11,15},{20,16},{24,... | collective-permute-start | bytes 786440 | tf_op jit(solution)/shard_map/ppermute | solution.py:610
  83.8 4.3 %collective-permute-done.13.refs_2_ = bf16[512,256]{1,0:T(8,128)(2,1)S(1)} collective-permute-done((bf16[512,256]{1,0:T(8,128)(2,1)S(1)}, bf16[512,256]{1,0:T(8,128)(2,1)S(1)}, u32[]{:S(2)}, u32[]{:S(2)}) %collective-permute-start.13) | collective-permute-done | bytes 262176 | tf_op jit(solution)/shard_map/ppermute | solution.py:610
  88.1 4.4 %first.1.refs_5_ = f32[512,1280]{1,0:T(8,128)S(1)} custom-call(s32[6]{0:T(128)S(1)} %stack.31.where_ref, bf16[512,256]{1,0:T(8,128)(2,1)S(1)} %collective-permute-done.9.refs_0_, bf16[512,256]{1,0:T(8,128)(2,1)S(1)} %collective-permute-done.8.refs_1_, bf16[512,256]{1,0:T(8,128)(2,1)S(1)} %collective-permute-done.13.refs_2_, ...), custom_call_target="tpu_custom_call" | custom-call | flops 1 | tf_op jit(solution)/shard_map/first/pallas_call | solution.py:499
  92.6 1.1 second.3
  93.7 0.0 copy-start.5
  93.7 0.1 collective-permute-start.18
  93.8 1.1 second.2
  94.9 0.6 collective-permute-start.14
  95.5 0.6 add.8
  96.1 0.1 collective-permute-start.19
  96.2 1.0 collective-permute-start.20
  97.2 3.4 %collective-permute-start.21 = (bf16[64,640]{1,0:T(8,128)(2,1)S(1)}, bf16[64,640]{1,0:T(8,128)(2,1)S(1)}, u32[]{:S(2)}, u32[]{:S(2)}) collective-permute-start(bf16[64,640]{1,0:T(8,128)(2,1)S(1)} %get-tuple-element.72), channel_id=1, source_target_pairs={{0,4},{4,0},{8,12},{12,8},{1,5},{5,1},{9,13},{13,9},{2,6},{6,2},{1... | collective-permute-start | bytes 245768 | tf_op jit(solution)/shard_map/ppermute | solution.py:50
  100.6 0.6 add.7
  101.2 0.1 collective-permute-start.15
  101.3 1.4 %collective-permute-start.16 = (bf16[64,640]{1,0:T(8,128)(2,1)S(1)}, bf16[64,640]{1,0:T(8,128)(2,1)S(1)}, u32[]{:S(2)}, u32[]{:S(2)}) collective-permute-start(bf16[64,640]{1,0:T(8,128)(2,1)S(1)} %get-tuple-element.65), channel_id=1, source_target_pairs={{0,8},{4,12},{8,0},{12,4},{1,9},{5,13},{9,1},{13,5},{2,10},{6,14},... | collective-permute-start | bytes 245768 | tf_op jit(solution)/shard_map/ppermute | solution.py:50
  102.7 0.6 collective-permute-done.19.refs_5_
  103.4 2.3 %collective-permute-start.17 = (bf16[64,640]{1,0:T(8,128)(2,1)S(1)}, bf16[64,640]{1,0:T(8,128)(2,1)S(1)}, u32[]{:S(2)}, u32[]{:S(2)}) collective-permute-start(bf16[64,640]{1,0:T(8,128)(2,1)S(1)} %get-tuple-element.66), channel_id=1, source_target_pairs={{0,4},{4,0},{8,12},{12,8},{1,5},{5,1},{9,13},{13,9},{2,6},{6,2},{1... | collective-permute-start | bytes 245768 | tf_op jit(solution)/shard_map/ppermute | solution.py:50
  105.7 1.1 collective-permute-done.20.refs_6_
  106.8 1.9 %collective-permute-done.15.refs_1_ = bf16[64,640]{1,0:T(8,128)(2,1)S(1)} collective-permute-done((bf16[64,640]{1,0:T(8,128)(2,1)S(1)}, bf16[64,640]{1,0:T(8,128)(2,1)S(1)}, u32[]{:S(2)}, u32[]{:S(2)}) %collective-permute-start.15) | collective-permute-done | bytes 81952 | tf_op jit(solution)/shard_map/ppermute | solution.py:50
  108.6 3.5 %collective-permute-done.16.refs_2_ = bf16[64,640]{1,0:T(8,128)(2,1)S(1)} collective-permute-done((bf16[64,640]{1,0:T(8,128)(2,1)S(1)}, bf16[64,640]{1,0:T(8,128)(2,1)S(1)}, u32[]{:S(2)}, u32[]{:S(2)}) %collective-permute-start.16) | collective-permute-done | bytes 81952 | tf_op jit(solution)/shard_map/ppermute | solution.py:50
  112.1 1.6 %mix.1 = bf16[64,5120]{1,0:T(8,128)(2,1)} custom-call(s32[6]{0:T(128)S(1)} %stack.31.where_ref, bf16[64,5120]{1,0:T(8,128)(2,1)S(1)} %copy-done.4, f32[1,5120]{1,0:T(1,128)S(1)} %bitcast.14, bf16[64,640]{1,0:T(8,128)(2,1)S(1)} %get-tuple-element.63.refs_0_, bf16[64,640]{1,0:T(8,128)(2,1)S(1)} %collective-permute-done.15.refs_1_, ...), custom_call_target="tpu_custom_call" | custom-call | flops 1 | tf_op jit(solution)/shard_map/mix/pallas_call | solution.py:638
  (30 shorter events, 0.1 us)
Async XLA Ops:
  0.0 3.7 %copy-start = (bf16[1024,1280]{1,0:T(8,128)(2,1)S(1)}, bf16[1024,1280]{1,0:T(8,128)(2,1)}, u32[]{:S(2)}) copy-start(bf16[1024,1280]{1,0:T(8,128)(2,1)} %refs_9_) | copy-start | bytes 7864324
  3.5 7.4 %copy-start.7 = (bf16[3,256,256]{2,1,0:T(8,128)(2,1)S(1)}, bf16[3,256,256]{2,1,0:T(8,128)(2,1)}, u32[]{:S(2)}) copy-start(bf16[3,256,256]{2,1,0:T(8,128)(2,1)} %get-tuple-element.41) | copy-start | bytes 1179652
  3.6 8.2 %copy-start.3 = (bf16[256,1024]{1,0:T(8,128)(2,1)S(1)}, bf16[256,1024]{1,0:T(8,128)(2,1)}, u32[]{:S(2)}) copy-start(bf16[256,1024]{1,0:T(8,128)(2,1)} %q_ref.3) | copy-start | bytes 1572868
  3.6 8.2 %copy-start.6 = (s32[2,2,8]{2,1,0:T(2,128)S(1)}, s32[2,2,8]{2,1,0:T(2,128)}, u32[]{:S(2)}) copy-start(s32[2,2,8]{2,1,0:T(2,128)} %exps_ref.3) | copy-start | bytes 388
  3.7 3.7 %copy-start.9 = (bf16[3,256,256]{2,1,0:T(8,128)(2,1)S(1)}, bf16[3,256,256]{2,1,0:T(8,128)(2,1)}, u32[]{:S(2)}) copy-start(bf16[3,256,256]{2,1,0:T(8,128)(2,1)} %get-tuple-element.39) | copy-start | bytes 1179652
  3.7 7.3 %copy-start.8 = (bf16[3,256,256]{2,1,0:T(8,128)(2,1)S(1)}, bf16[3,256,256]{2,1,0:T(8,128)(2,1)}, u32[]{:S(2)}) copy-start(bf16[3,256,256]{2,1,0:T(8,128)(2,1)} %get-tuple-element.40) | copy-start | bytes 1179652
  3.7 8.1 %copy-start.2 = (bf16[2,256,1024]{2,1,0:T(8,128)(2,1)S(1)}, bf16[2,256,1024]{2,1,0:T(8,128)(2,1)}, u32[]{:S(2)}) copy-start(bf16[2,256,1024]{2,1,0:T(8,128)(2,1)} %fresh_ref.3) | copy-start | bytes 3145732
  4.4 31.8 %collective-permute-start = (bf16[512,1280]{1,0:T(8,128)(2,1)S(1)}, bf16[512,1280]{1,0:T(8,128)(2,1)S(1)}, u32[]{:S(2)}, u32[]{:S(2)}) collective-permute-start(bf16[512,1280]{1,0:T(8,128)(2,1)S(1)} %take.1), channel_id=1, source_target_pairs={{0,2},{2,0},{1,3},{3,1},{4,6},{6,4},{5,7},{7,5},{8,10},{10,8},{9,1... | collective-permute-start | bytes 3932168 | tf_op jit(solution)/shard_map/ppermute | solution.py:50
  7.4 30.5 %collective-permute-start.3 = (bf16[3,256,256]{2,1,0:T(8,128)(2,1)S(1)}, bf16[3,256,256]{2,1,0:T(8,128)(2,1)S(1)}, u32[]{:S(2)}, u32[]{:S(2)}) collective-permute-start(bf16[3,256,256]{2,1,0:T(8,128)(2,1)S(1)} %copy-done.9), channel_id=1, source_target_pairs={{0,12},{4,8},{8,4},{12,0},{1,13},{5,9},{9,5},{13,1},{2,14},{6,10},... | collective-permute-start | bytes 1179656 | tf_op jit(solution)/shard_map/ppermute | solution.py:50
  11.0 33.3 %collective-permute-start.2 = (bf16[3,256,256]{2,1,0:T(8,128)(2,1)S(1)}, bf16[3,256,256]{2,1,0:T(8,128)(2,1)S(1)}, u32[]{:S(2)}, u32[]{:S(2)}) collective-permute-start(bf16[3,256,256]{2,1,0:T(8,128)(2,1)S(1)} %copy-done.8), channel_id=1, source_target_pairs={{0,8},{4,12},{8,0},{12,4},{1,9},{5,13},{9,1},{13,5},{2,10},{6,14},... | collective-permute-start | bytes 1179656 | tf_op jit(solution)/shard_map/ppermute | solution.py:50
  11.0 33.3 %collective-permute-start.1 = (bf16[3,256,256]{2,1,0:T(8,128)(2,1)S(1)}, bf16[3,256,256]{2,1,0:T(8,128)(2,1)S(1)}, u32[]{:S(2)}, u32[]{:S(2)}) collective-permute-start(bf16[3,256,256]{2,1,0:T(8,128)(2,1)S(1)} %copy-done.7), channel_id=1, source_target_pairs={{0,4},{4,0},{8,12},{12,8},{1,5},{5,1},{9,13},{13,9},{2,6},{6,2},{1... | collective-permute-start | bytes 1179656 | tf_op jit(solution)/shard_map/ppermute | solution.py:50
  11.8 2.2 %copy-start.1 = (bf16[2,1024,1024]{2,1,0:T(8,128)(2,1)S(1)}, bf16[2,1024,1024]{2,1,0:T(8,128)(2,1)}, u32[]{:S(2)}) copy-start(bf16[2,1024,1024]{2,1,0:T(8,128)(2,1)} %cached_ref.3) | copy-start | bytes 12582916
  36.2 52.0 %collective-permute-start.12 = (bf16[512,1280]{1,0:T(8,128)(2,1)S(1)}, bf16[512,1280]{1,0:T(8,128)(2,1)S(1)}, u32[]{:S(2)}, u32[]{:S(2)}) collective-permute-start(bf16[512,1280]{1,0:T(8,128)(2,1)S(1)} %collective-permute-done.refs_10_.refs_3_), channel_id=1, source_target_pairs={{0,16},{16,0},{1,17},{17,1},{2,18},{18,2},{3,19},{19,3},{4,20},{20... | collective-permute-start | bytes 3932168 | tf_op jit(solution)/shard_map/ppermute | solution.py:50
  46.6 17.7 %collective-permute-start.10 = (bf16[512,256]{1,0:T(8,128)(2,1)S(1)}, bf16[512,256]{1,0:T(8,128)(2,1)S(1)}, u32[]{:S(2)}, u32[]{:S(2)}) collective-permute-start(bf16[512,256]{1,0:T(8,128)(2,1)S(1)} %bitcast.9), channel_id=1, source_target_pairs={{0,8},{4,12},{8,0},{12,4},{1,9},{5,13},{9,1},{13,5},{2,10},{6,14},... | collective-permute-start | bytes 786440 | tf_op jit(solution)/shard_map/ppermute | solution.py:50
  46.6 19.9 %collective-permute-start.9 = (bf16[512,256]{1,0:T(8,128)(2,1)S(1)}, bf16[512,256]{1,0:T(8,128)(2,1)S(1)}, u32[]{:S(2)}, u32[]{:S(2)}) collective-permute-start(bf16[512,256]{1,0:T(8,128)(2,1)S(1)} %bitcast.10), channel_id=1, source_target_pairs={{0,4},{4,8},{8,12},{1,5},{5,9},{9,13},{2,6},{6,10},{10,14},{3,7},{... | collective-permute-start | bytes 786440 | tf_op jit(solution)/shard_map/ppermute | solution.py:604
  51.6 16.2 %collective-permute-start.8 = (bf16[512,256]{1,0:T(8,128)(2,1)S(1)}, bf16[512,256]{1,0:T(8,128)(2,1)S(1)}, u32[]{:S(2)}, u32[]{:S(2)}) collective-permute-start(bf16[512,256]{1,0:T(8,128)(2,1)S(1)} %bitcast.11), channel_id=1, source_target_pairs={{4,0},{8,4},{12,8},{5,1},{9,5},{13,9},{6,2},{10,6},{14,10},{7,3},{... | collective-permute-start | bytes 786440 | tf_op jit(solution)/shard_map/ppermute | solution.py:603
  55.2 6.4 %collective-permute-start.4 = (bf16[512,256]{1,0:T(8,128)(2,1)S(1)}, bf16[512,256]{1,0:T(8,128)(2,1)S(1)}, u32[]{:S(2)}, u32[]{:S(2)}) collective-permute-start(bf16[512,256]{1,0:T(8,128)(2,1)S(1)} %bitcast.13), channel_id=1, source_target_pairs={{0,2},{2,0},{1,3},{3,1},{4,6},{6,4},{5,7},{7,5},{8,10},{10,8},{9,1... | collective-permute-start | bytes 786440 | tf_op jit(solution)/shard_map/ppermute | solution.py:50
  61.7 15.2 %collective-permute-start.7 = (bf16[512,256]{1,0:T(8,128)(2,1)S(1)}, bf16[512,256]{1,0:T(8,128)(2,1)S(1)}, u32[]{:S(2)}, u32[]{:S(2)}) collective-permute-start(bf16[512,256]{1,0:T(8,128)(2,1)S(1)} %collective-permute-done.4.refs_3_), channel_id=1, source_target_pairs={{0,8},{4,12},{8,0},{12,4},{1,9},{5,13},{9,1},{13,5},{2,10},{6,14},... | collective-permute-start | bytes 786440 | tf_op jit(solution)/shard_map/ppermute | solution.py:50
  64.3 12.6 %collective-permute-start.6 = (bf16[512,256]{1,0:T(8,128)(2,1)S(1)}, bf16[512,256]{1,0:T(8,128)(2,1)S(1)}, u32[]{:S(2)}, u32[]{:S(2)}) collective-permute-start(bf16[512,256]{1,0:T(8,128)(2,1)S(1)} %collective-permute-done.4.refs_3_), channel_id=1, source_target_pairs={{0,4},{4,8},{8,12},{1,5},{5,9},{9,13},{2,6},{6,10},{10,14},{3,7},{... | collective-permute-start | bytes 786440 | tf_op jit(solution)/shard_map/ppermute | solution.py:604
  66.5 16.0 %collective-permute-start.5 = (bf16[512,256]{1,0:T(8,128)(2,1)S(1)}, bf16[512,256]{1,0:T(8,128)(2,1)S(1)}, u32[]{:S(2)}, u32[]{:S(2)}) collective-permute-start(bf16[512,256]{1,0:T(8,128)(2,1)S(1)} %collective-permute-done.4.refs_3_), channel_id=1, source_target_pairs={{4,0},{8,4},{12,8},{5,1},{9,5},{13,9},{6,2},{10,6},{14,10},{7,3},{... | collective-permute-start | bytes 786440 | tf_op jit(solution)/shard_map/ppermute | solution.py:603
  67.8 20.3 %collective-permute-start.13 = (bf16[512,256]{1,0:T(8,128)(2,1)S(1)}, bf16[512,256]{1,0:T(8,128)(2,1)S(1)}, u32[]{:S(2)}, u32[]{:S(2)}) collective-permute-start(bf16[512,256]{1,0:T(8,128)(2,1)S(1)} %collective-permute-done.10.refs_0_), channel_id=1, source_target_pairs={{4,0},{8,12},{5,1},{9,13},{6,2},{10,14},{7,3},{11,15},{20,16},{24,... | collective-permute-start | bytes 786440 | tf_op jit(solution)/shard_map/ppermute | solution.py:610
  82.5 10.0 %collective-permute-start.11 = (bf16[512,256]{1,0:T(8,128)(2,1)S(1)}, bf16[512,256]{1,0:T(8,128)(2,1)S(1)}, u32[]{:S(2)}, u32[]{:S(2)}) collective-permute-start(bf16[512,256]{1,0:T(8,128)(2,1)S(1)} %collective-permute-done.7.refs_4_), channel_id=1, source_target_pairs={{4,0},{8,12},{5,1},{9,13},{6,2},{10,14},{7,3},{11,15},{20,16},{24,... | collective-permute-start | bytes 786440 | tf_op jit(solution)/shard_map/ppermute | solution.py:610
  93.7 18.4 %copy-start.4 = (bf16[64,5120]{1,0:T(8,128)(2,1)S(1)}, bf16[64,5120]{1,0:T(8,128)(2,1)}, u32[]{:S(2)}) copy-start(bf16[64,5120]{1,0:T(8,128)(2,1)} %hidden_ref.1) | copy-start | bytes 1966084
  93.7 18.4 %copy-start.5 = (f32[5120]{0:T(1024)S(1)}, f32[5120]{0:T(1024)}, u32[]{:S(2)}) copy-start(f32[5120]{0:T(1024)} %param.13) | copy-start | bytes 61444
  93.7 1.8 %collective-permute-start.18 = (bf16[4,64,640]{2,1,0:T(8,128)(2,1)S(1)}, bf16[4,64,640]{2,1,0:T(8,128)(2,1)S(1)}, u32[]{:S(2)}, u32[]{:S(2)}) collective-permute-start(bf16[4,64,640]{2,1,0:T(8,128)(2,1)S(1)} %get-tuple-element.68), channel_id=1, source_target_pairs={{0,1},{1,0},{2,3},{3,2},{4,5},{5,4},{6,7},{7,6},{8,9},{9,8},{10,11... | collective-permute-start | bytes 983048 | tf_op jit(solution)/shard_map/ppermute | solution.py:50
  94.9 5.6 %collective-permute-start.14 = (bf16[4,64,640]{2,1,0:T(8,128)(2,1)S(1)}, bf16[4,64,640]{2,1,0:T(8,128)(2,1)S(1)}, u32[]{:S(2)}, u32[]{:S(2)}) collective-permute-start(bf16[4,64,640]{2,1,0:T(8,128)(2,1)S(1)} %get-tuple-element.62), channel_id=1, source_target_pairs={{0,1},{1,0},{2,3},{3,2},{4,5},{5,4},{6,7},{7,6},{8,9},{9,8},{10,11... | collective-permute-start | bytes 983048 | tf_op jit(solution)/shard_map/ppermute | solution.py:50
  96.1 7.3 %collective-permute-start.19 = (bf16[64,640]{1,0:T(8,128)(2,1)S(1)}, bf16[64,640]{1,0:T(8,128)(2,1)S(1)}, u32[]{:S(2)}, u32[]{:S(2)}) collective-permute-start(bf16[64,640]{1,0:T(8,128)(2,1)S(1)} %get-tuple-element.70), channel_id=1, source_target_pairs={{0,12},{4,8},{8,4},{12,0},{1,13},{5,9},{9,5},{13,1},{2,14},{6,10},... | collective-permute-start | bytes 245768 | tf_op jit(solution)/shard_map/ppermute | solution.py:50
  96.2 10.6 %collective-permute-start.20 = (bf16[64,640]{1,0:T(8,128)(2,1)S(1)}, bf16[64,640]{1,0:T(8,128)(2,1)S(1)}, u32[]{:S(2)}, u32[]{:S(2)}) collective-permute-start(bf16[64,640]{1,0:T(8,128)(2,1)S(1)} %get-tuple-element.71), channel_id=1, source_target_pairs={{0,8},{4,12},{8,0},{12,4},{1,9},{5,13},{9,1},{13,5},{2,10},{6,14},... | collective-permute-start | bytes 245768 | tf_op jit(solution)/shard_map/ppermute | solution.py:50
  97.2 9.6 %collective-permute-start.21 = (bf16[64,640]{1,0:T(8,128)(2,1)S(1)}, bf16[64,640]{1,0:T(8,128)(2,1)S(1)}, u32[]{:S(2)}, u32[]{:S(2)}) collective-permute-start(bf16[64,640]{1,0:T(8,128)(2,1)S(1)} %get-tuple-element.72), channel_id=1, source_target_pairs={{0,4},{4,0},{8,12},{12,8},{1,5},{5,1},{9,13},{13,9},{2,6},{6,2},{1... | collective-permute-start | bytes 245768 | tf_op jit(solution)/shard_map/ppermute | solution.py:50
  101.2 7.4 %collective-permute-start.15 = (bf16[64,640]{1,0:T(8,128)(2,1)S(1)}, bf16[64,640]{1,0:T(8,128)(2,1)S(1)}, u32[]{:S(2)}, u32[]{:S(2)}) collective-permute-start(bf16[64,640]{1,0:T(8,128)(2,1)S(1)} %get-tuple-element.64), channel_id=1, source_target_pairs={{0,12},{4,8},{8,4},{12,0},{1,13},{5,9},{9,5},{13,1},{2,14},{6,10},... | collective-permute-start | bytes 245768 | tf_op jit(solution)/shard_map/ppermute | solution.py:50
  101.3 10.8 %collective-permute-start.16 = (bf16[64,640]{1,0:T(8,128)(2,1)S(1)}, bf16[64,640]{1,0:T(8,128)(2,1)S(1)}, u32[]{:S(2)}, u32[]{:S(2)}) collective-permute-start(bf16[64,640]{1,0:T(8,128)(2,1)S(1)} %get-tuple-element.65), channel_id=1, source_target_pairs={{0,8},{4,12},{8,0},{12,4},{1,9},{5,13},{9,1},{13,5},{2,10},{6,14},... | collective-permute-start | bytes 245768 | tf_op jit(solution)/shard_map/ppermute | solution.py:50
  103.4 8.7 %collective-permute-start.17 = (bf16[64,640]{1,0:T(8,128)(2,1)S(1)}, bf16[64,640]{1,0:T(8,128)(2,1)S(1)}, u32[]{:S(2)}, u32[]{:S(2)}) collective-permute-start(bf16[64,640]{1,0:T(8,128)(2,1)S(1)} %get-tuple-element.66), channel_id=1, source_target_pairs={{0,4},{4,0},{8,12},{12,8},{1,5},{5,1},{9,13},{13,9},{2,6},{6,2},{1... | collective-permute-start | bytes 245768 | tf_op jit(solution)/shard_map/ppermute | solution.py:50

commit v26 on v23

--- a/solution.py
+++ b/solution.py
@@ -11,7 +11,7 @@
 HEAD_DIM = 128
 SCALE_ROWS = 128
 SATURATION = 448.0
-PACK_ROWS = 32
+PACK_ROWS = 64
 VMEM_BYTES = 32 * 1024 * 1024
 PACK_VMEM_BYTES = 60 * 1024 * 1024
 ATTEND_FLOPS = 1
@@ -390,9 +390,10 @@
         keys = jnp.concatenate([ref[1, :, lanes] for ref in pieces], axis=0)
         values = jnp.concatenate([ref[2, :, lanes] for ref in pieces], axis=0)
         values = jnp.concatenate([values, jnp.ones_like(values)], axis=1)
-        for rel, ref in enumerate(pieces):
+        for first in range(0, len(pieces), 2):
+            query = [ref[0, pl.ds(start, rows), lanes] for ref in pieces[first : first + 2]]
             scores = lax.dot_general(
-                ref[0, pl.ds(start, rows), lanes],
+                jnp.concatenate(query, axis=0),
                 keys,
                 (((1,), (1,)), ((), ())),
                 preferred_element_type=jnp.float32,
@@ -401,7 +402,9 @@
             expo = jnp.exp2((scores - peak) * factor).astype(jnp.bfloat16)
             mix = jnp.dot(expo, values, preferred_element_type=jnp.float32)
             mix = (mix[:, :HEAD_DIM] / mix[:, HEAD_DIM:]).astype(jnp.bfloat16)
-            out[where_ref[NEAR] ^ rel, :, lanes] = mix
+            for at in range(len(query)):
+                block = mix[at * rows : (at + 1) * rows]
+                out[where_ref[NEAR] ^ (first + at), :, lanes] = block
 
 
 def attend_half(where, half, pieces):

time: 105 us -> 105 us (level)
  no operation moved by 1% of the time
where the time goes in v26:
time: 105 us
  waiting for transfers between devices  50.7 us (48%)
  starting transfers between devices  28.4 us (27%)
  Pallas kernels  22.9 us (22%)
  local copies, waits for them, and re-layouts  2.32 us (2%)
    ppermute x20, waiting for transfers between devices, swap(): return lax.ppermute(x, axes, pairs)  46.8 us
    ppermute x20, starting transfers between devices, swap(): return lax.ppermute(x, axes, pairs)  25.8 us
    pallas_call x2, Pallas kernels, attend_half(): call(functools.partial(attend_half_kernel, half), 'attend', out, 1, [spec...  4.63 us
    pallas_call x1, Pallas kernels, first_product(): call(first_kernel, 'first', jax.ShapeDtypeStruct(acc.shape, jnp.float32),...  3.96 us
    ppermute x2, waiting for transfers between devices, share_tail(): ends = lax.ppermute(far, 'patch', [(1, 0), (2, 3)])  3.87 us
    pallas_call x2, Pallas kernels, add_product(): call(functools.partial(add_product_kernel, len(rels)), 'products', jax.Sh...  3.79 us
    pallas_call x1, Pallas kernels, pack(): pl.pallas_call(functools.partial(pack_kernel, split, feat // HEAD_DIM), o...  3.53 us
    ppermute x2, starting transfers between devices, share_tail(): ends = lax.ppermute(far, 'patch', [(1, 0), (2, 3)])  2.58 us
  transfers between devices with their start and end apart: 22, of which 11 were waited for; matrix products, arithmetic and copies ran while one was open for 0% of the time, Pallas kernels for 15%

profile of v26, /device:TPU:0, one launch (start us, length us, event | category | flops | bytes accessed | tf_op | source)
XLA Modules:
  0.0 104.5 jit_solution(6647629584680814179)
XLA Ops:
  0.0 3.5 %pack.1 = (bf16[3,256,256]{2,1,0:T(8,128)(2,1)}, bf16[3,256,256]{2,1,0:T(8,128)(2,1)}, bf16[3,256,256]{2,1,0:T(8,128)(2,1)}) custom-call(s32[2,2,8]{2,1,0:T(2,128)} %exps_ref.3, bf16[256,1024]{1,0:T(8,128)(2,1)} %q_ref.3, bf16[2,256,1024]{2,1,0:T(8,128)(2,1)} %fresh_ref.3, bf16[2,1024,1024]{2,1,0:T(8,128)(2,1)} %cached_ref.3), custom_call_target="tpu_custom_call" | custom-call | tf_op jit(solution)/shard_map/pack/pallas_call | solution.py:114
  3.6 0.0 copy-start.3
  3.6 0.1 stack.31.where_ref
  3.7 0.7 take.1
  4.4 3.0 %collective-permute-start = (bf16[512,1280]{1,0:T(8,128)(2,1)S(1)}, bf16[512,1280]{1,0:T(8,128)(2,1)S(1)}, u32[]{:S(2)}, u32[]{:S(2)}) collective-permute-start(bf16[512,1280]{1,0:T(8,128)(2,1)S(1)} %take.1), channel_id=1, source_target_pairs={{0,2},{2,0},{1,3},{3,1},{4,6},{6,4},{5,7},{7,5},{8,10},{10,8},{9,1... | collective-permute-start | bytes 3932168 | tf_op jit(solution)/shard_map/ppermute | solution.py:50
  7.4 3.6 %collective-permute-start.3 = (bf16[3,256,256]{2,1,0:T(8,128)(2,1)S(1)}, bf16[3,256,256]{2,1,0:T(8,128)(2,1)S(1)}, u32[]{:S(2)}, u32[]{:S(2)}) collective-permute-start(bf16[3,256,256]{2,1,0:T(8,128)(2,1)S(1)} %copy-done.9), channel_id=1, source_target_pairs={{0,12},{4,8},{8,4},{12,0},{1,13},{5,9},{9,5},{13,1},{2,14},{6,10},... | collective-permute-start | bytes 1179656 | tf_op jit(solution)/shard_map/ppermute | solution.py:50
  11.0 0.8 collective-permute-start.1
  11.8 2.2 %copy-done.1 = bf16[2,1024,1024]{2,1,0:T(8,128)(2,1)S(1)} copy-done((bf16[2,1024,1024]{2,1,0:T(8,128)(2,1)S(1)}, bf16[2,1024,1024]{2,1,0:T(8,128)(2,1)}, u32[]{:S(2)}) %copy-start.1) | copy-done | bytes 4194328
  14.0 1.3 %own.1.refs_0_ = bf16[3,256,256]{2,1,0:T(8,128)(2,1)S(1)} custom-call(s32[6]{0:T(128)S(1)} %stack.31.where_ref, s32[2,2,8]{2,1,0:T(2,128)S(1)} %copy-done.6, bf16[256,1024]{1,0:T(8,128)(2,1)S(1)} %copy-done.3, bf16[2,256,1024]{2,1,0:T(8,128)(2,1)S(1)} %copy-done.2, bf16[2,1024,1024]{2,1,0:T(8,128)(2,1)S(1)} %copy-done.1), custom_call_target="tpu_custom_call" | custom-call | flops 1 | tf_op jit(solution)/shard_map/own/pallas_call | solution.py:150
  15.3 20.9 %collective-permute-done.refs_7_.fetched_ref = bf16[512,1280]{1,0:T(8,128)(2,1)S(1)} collective-permute-done((bf16[512,1280]{1,0:T(8,128)(2,1)S(1)}, bf16[512,1280]{1,0:T(8,128)(2,1)S(1)}, u32[]{:S(2)}, u32[]{:S(2)}) %collective-permute-start) | collective-permute-done | bytes 1310752 | tf_op jit(solution)/shard_map/ppermute | solution.py:50
  36.2 1.8 %collective-permute-start.11 = (bf16[512,1280]{1,0:T(8,128)(2,1)S(1)}, bf16[512,1280]{1,0:T(8,128)(2,1)S(1)}, u32[]{:S(2)}, u32[]{:S(2)}) collective-permute-start(bf16[512,1280]{1,0:T(8,128)(2,1)S(1)} %collective-permute-done.refs_7_.fetched_ref), channel_id=1, source_target_pairs={{0,16},{16,0},{1,17},{17,1},{2,18},{18,2},{3,19},{19,3},{4,20},{20... | collective-permute-start | bytes 3932168 | tf_op jit(solution)/shard_map/ppermute | solution.py:50
  37.9 6.3 %collective-permute-done.2.refs_2_ = bf16[3,256,256]{2,1,0:T(8,128)(2,1)S(1)} collective-permute-done((bf16[3,256,256]{2,1,0:T(8,128)(2,1)S(1)}, bf16[3,256,256]{2,1,0:T(8,128)(2,1)S(1)}, u32[]{:S(2)}, u32[]{:S(2)}) %collective-permute-start.2) | collective-permute-done | bytes 393248 | tf_op jit(solution)/shard_map/ppermute | solution.py:50
  44.2 2.3 %attend.2 = bf16[4,128,256]{2,1,0:T(8,128)(2,1)S(1)} custom-call(s32[6]{0:T(128)S(1)} %stack.31.where_ref, bf16[3,256,256]{2,1,0:T(8,128)(2,1)S(1)} %own.1.refs_0_, bf16[3,256,256]{2,1,0:T(8,128)(2,1)S(1)} %collective-permute-done.1.refs_1_, bf16[3,256,256]{2,1,0:T(8,128)(2,1)S(1)} %collective-permute-done.2.refs_2_, ...), custom_call_target="tpu_custom_call" | custom-call | flops 1 | tf_op jit(solution)/shard_map/attend/pallas_call | solution.py:413
  46.6 0.1 collective-permute-start.8
  46.6 3.0 %collective-permute-start.7 = (bf16[512,256]{1,0:T(8,128)(2,1)S(1)}, bf16[512,256]{1,0:T(8,128)(2,1)S(1)}, u32[]{:S(2)}, u32[]{:S(2)}) collective-permute-start(bf16[512,256]{1,0:T(8,128)(2,1)S(1)} %bitcast.10), channel_id=1, source_target_pairs={{0,4},{4,0},{8,12},{12,8},{1,5},{5,1},{9,13},{13,9},{2,6},{6,2},{1... | collective-permute-start | bytes 786440 | tf_op jit(solution)/shard_map/ppermute | solution.py:50
  49.7 2.3 %attend.3 = bf16[4,128,256]{2,1,0:T(8,128)(2,1)S(1)} custom-call(s32[6]{0:T(128)S(1)} %stack.31.where_ref, bf16[3,256,256]{2,1,0:T(8,128)(2,1)S(1)} %own.1.refs_0_, bf16[3,256,256]{2,1,0:T(8,128)(2,1)S(1)} %collective-permute-done.1.refs_1_, bf16[3,256,256]{2,1,0:T(8,128)(2,1)S(1)} %collective-permute-done.2.refs_2_, ...), custom_call_target="tpu_custom_call" | custom-call | flops 1 | tf_op jit(solution)/shard_map/attend/pallas_call | solution.py:413
  52.0 0.6 collective-permute-start.4
  52.6 1.5 %products.2.refs_4_ = f32[512,1280]{1,0:T(8,128)S(1)} custom-call(s32[6]{0:T(128)S(1)} %stack.31.where_ref, bf16[512,256]{1,0:T(8,128)(2,1)S(1)} %bitcast.11, bf16[1024,1280]{1,0:T(8,128)(2,1)S(1)} %copy-done), custom_call_target="tpu_custom_call" | custom-call | flops 6000000000 | tf_op jit(solution)/shard_map/products/pallas_call | solution.py:438
  54.2 4.3 %collective-permute-done.4.refs_2_ = bf16[512,256]{1,0:T(8,128)(2,1)S(1)} collective-permute-done((bf16[512,256]{1,0:T(8,128)(2,1)S(1)}, bf16[512,256]{1,0:T(8,128)(2,1)S(1)}, u32[]{:S(2)}, u32[]{:S(2)}) %collective-permute-start.4) | collective-permute-done | bytes 262176 | tf_op jit(solution)/shard_map/ppermute | solution.py:50
  58.4 0.6 collective-permute-start.6
  59.0 1.7 %collective-permute-start.5 = (bf16[512,256]{1,0:T(8,128)(2,1)S(1)}, bf16[512,256]{1,0:T(8,128)(2,1)S(1)}, u32[]{:S(2)}, u32[]{:S(2)}) collective-permute-start(bf16[512,256]{1,0:T(8,128)(2,1)S(1)} %collective-permute-done.4.refs_2_), channel_id=1, source_target_pairs={{0,4},{4,0},{8,12},{12,8},{1,5},{5,1},{9,13},{13,9},{2,6},{6,2},{1... | collective-permute-start | bytes 786440 | tf_op jit(solution)/shard_map/ppermute | solution.py:50
  60.7 0.1 collective-permute-done.8.refs_0_
  60.8 0.7 collective-permute-start.12
  61.5 1.3 %collective-permute-start.13 = (bf16[512,256]{1,0:T(8,128)(2,1)S(1)}, bf16[512,256]{1,0:T(8,128)(2,1)S(1)}, u32[]{:S(2)}, u32[]{:S(2)}) collective-permute-start(bf16[512,256]{1,0:T(8,128)(2,1)S(1)} %collective-permute-done.8.refs_0_), channel_id=1, source_target_pairs={{4,0},{8,12},{5,1},{9,13},{6,2},{10,14},{7,3},{11,15},{20,16},{24,... | collective-permute-start | bytes 786440 | tf_op jit(solution)/shard_map/ppermute | solution.py:594
  62.8 2.2 %products.3.refs_5_ = f32[512,1280]{1,0:T(8,128)S(1)} custom-call(s32[6]{0:T(128)S(1)} %stack.31.where_ref, bf16[512,256]{1,0:T(8,128)(2,1)S(1)} %collective-permute-done.8.refs_0_, bf16[512,256]{1,0:T(8,128)(2,1)S(1)} %collective-permute-done.7.refs_1_, bf16[1024,1280]{1,0:T(8,128)(2,1)S(1)} %copy-done, bf16[1024,1280]{1,0:T(8,128)(2,1)S(1)} %copy-done, ...), custom_call_target="tpu_custom_call" | custom-call | flops 1 | tf_op jit(solution)/shard_map/products/pallas_call | solution.py:438
  65.0 6.3 %collective-permute-done.6.refs_3_ = bf16[512,256]{1,0:T(8,128)(2,1)S(1)} collective-permute-done((bf16[512,256]{1,0:T(8,128)(2,1)S(1)}, bf16[512,256]{1,0:T(8,128)(2,1)S(1)}, u32[]{:S(2)}, u32[]{:S(2)}) %collective-permute-start.6) | collective-permute-done | bytes 262176 | tf_op jit(solution)/shard_map/ppermute | solution.py:50
  71.3 1.4 %collective-permute-done.5.refs_4_ = bf16[512,256]{1,0:T(8,128)(2,1)S(1)} collective-permute-done((bf16[512,256]{1,0:T(8,128)(2,1)S(1)}, bf16[512,256]{1,0:T(8,128)(2,1)S(1)}, u32[]{:S(2)}, u32[]{:S(2)}) %collective-permute-start.5) | collective-permute-done | bytes 262176 | tf_op jit(solution)/shard_map/ppermute | solution.py:50
  72.8 0.7 collective-permute-start.9
  73.4 1.3 %collective-permute-start.10 = (bf16[512,256]{1,0:T(8,128)(2,1)S(1)}, bf16[512,256]{1,0:T(8,128)(2,1)S(1)}, u32[]{:S(2)}, u32[]{:S(2)}) collective-permute-start(bf16[512,256]{1,0:T(8,128)(2,1)S(1)} %collective-permute-done.6.refs_3_), channel_id=1, source_target_pairs={{4,0},{8,12},{5,1},{9,13},{6,2},{10,14},{7,3},{11,15},{20,16},{24,... | collective-permute-start | bytes 786440 | tf_op jit(solution)/shard_map/ppermute | solution.py:594
  74.7 2.9 %collective-permute-done.13.refs_1_ = bf16[512,256]{1,0:T(8,128)(2,1)S(1)} collective-permute-done((bf16[512,256]{1,0:T(8,128)(2,1)S(1)}, bf16[512,256]{1,0:T(8,128)(2,1)S(1)}, u32[]{:S(2)}, u32[]{:S(2)}) %collective-permute-start.13) | collective-permute-done | bytes 262176 | tf_op jit(solution)/shard_map/ppermute | solution.py:594
  77.6 4.0 %first.1.acc_in = f32[512,1280]{1,0:T(8,128)S(1)} custom-call(s32[6]{0:T(128)S(1)} %stack.31.where_ref, bf16[512,256]{1,0:T(8,128)(2,1)S(1)} %collective-permute-done.12.refs_0_, bf16[512,256]{1,0:T(8,128)(2,1)S(1)} %collective-permute-done.13.refs_1_, bf16[512,256]{1,0:T(8,128)(2,1)S(1)} %collective-permute-done.4.refs_2_, ...), custom_call_target="tpu_custom_call" | custom-call | flops 1 | tf_op jit(solution)/shard_map/first/pallas_call | solution.py:486
  81.6 1.0 collective-permute-done.10.more
  82.6 1.1 %second.3 = (bf16[4,64,640]{2,1,0:T(8,128)(2,1)S(1)}, bf16[4,64,640]{2,1,0:T(8,128)(2,1)S(1)}) custom-call(s32[6]{0:T(128)S(1)} %stack.31.where_ref, bf16[512,256]{1,0:T(8,128)(2,1)S(1)} %collective-permute-done.9.slot, bf16[512,256]{1,0:T(8,128)(2,1)S(1)} %collective-permute-done.10.more, bf16[512,1280]{1,0:T(8,128)(2,1)S(1)} %collective-permute-done.refs_7_.fetched_ref, ...), custom_call_target="tpu_custom_call" | custom-call | flops 1 | tf_op jit(solution)/shard_map/second/pallas_call | solution.py:527
  83.7 0.0 copy-start.4
  83.7 0.1 collective-permute-start.18
  83.8 1.1 %second.2 = (bf16[4,64,640]{2,1,0:T(8,128)(2,1)S(1)}, bf16[4,64,640]{2,1,0:T(8,128)(2,1)S(1)}) custom-call(s32[6]{0:T(128)S(1)} %stack.31.where_ref, bf16[512,256]{1,0:T(8,128)(2,1)S(1)} %collective-permute-done.9.slot, bf16[512,256]{1,0:T(8,128)(2,1)S(1)} %collective-permute-done.10.more, bf16[512,1280]{1,0:T(8,128)(2,1)S(1)} %collective-permute-done.refs_7_.fetched_ref, ...), custom_call_target="tpu_custom_call" | custom-call | flops 1 | tf_op jit(solution)/shard_map/second/pallas_call | solution.py:527
  84.9 0.6 collective-permute-start.14
  85.5 0.6 add.8
  86.1 1.9 %collective-permute-start.19 = (bf16[64,640]{1,0:T(8,128)(2,1)S(1)}, bf16[64,640]{1,0:T(8,128)(2,1)S(1)}, u32[]{:S(2)}, u32[]{:S(2)}) collective-permute-start(bf16[64,640]{1,0:T(8,128)(2,1)S(1)} %get-tuple-element.68), channel_id=1, source_target_pairs={{0,12},{4,8},{8,4},{12,0},{1,13},{5,9},{9,5},{13,1},{2,14},{6,10},... | collective-permute-start | bytes 245768 | tf_op jit(solution)/shard_map/ppermute | solution.py:50
  88.0 0.0 collective-permute-start.20
  88.0 2.6 %collective-permute-start.21 = (bf16[64,640]{1,0:T(8,128)(2,1)S(1)}, bf16[64,640]{1,0:T(8,128)(2,1)S(1)}, u32[]{:S(2)}, u32[]{:S(2)}) collective-permute-start(bf16[64,640]{1,0:T(8,128)(2,1)S(1)} %get-tuple-element.70), channel_id=1, source_target_pairs={{0,4},{4,0},{8,12},{12,8},{1,5},{5,1},{9,13},{13,9},{2,6},{6,2},{1... | collective-permute-start | bytes 245768 | tf_op jit(solution)/shard_map/ppermute | solution.py:50
  90.6 0.6 add.7
  91.2 1.9 %collective-permute-start.15 = (bf16[64,640]{1,0:T(8,128)(2,1)S(1)}, bf16[64,640]{1,0:T(8,128)(2,1)S(1)}, u32[]{:S(2)}, u32[]{:S(2)}) collective-permute-start(bf16[64,640]{1,0:T(8,128)(2,1)S(1)} %get-tuple-element.62), channel_id=1, source_target_pairs={{0,12},{4,8},{8,4},{12,0},{1,13},{5,9},{9,5},{13,1},{2,14},{6,10},... | collective-permute-start | bytes 245768 | tf_op jit(solution)/shard_map/ppermute | solution.py:50
  93.1 0.3 collective-permute-done.19.refs_5_
  93.4 2.3 %collective-permute-start.17 = (bf16[64,640]{1,0:T(8,128)(2,1)S(1)}, bf16[64,640]{1,0:T(8,128)(2,1)S(1)}, u32[]{:S(2)}, u32[]{:S(2)}) collective-permute-start(bf16[64,640]{1,0:T(8,128)(2,1)S(1)} %get-tuple-element.64), channel_id=1, source_target_pairs={{0,4},{4,0},{8,12},{12,8},{1,5},{5,1},{9,13},{13,9},{2,6},{6,2},{1... | collective-permute-start | bytes 245768 | tf_op jit(solution)/shard_map/ppermute | solution.py:50
  95.7 3.0 %collective-permute-done.20.refs_6_ = bf16[64,640]{1,0:T(8,128)(2,1)S(1)} collective-permute-done((bf16[64,640]{1,0:T(8,128)(2,1)S(1)}, bf16[64,640]{1,0:T(8,128)(2,1)S(1)}, u32[]{:S(2)}, u32[]{:S(2)}) %collective-permute-start.20) | collective-permute-done | bytes 81952 | tf_op jit(solution)/shard_map/ppermute | solution.py:50
  98.7 4.2 %collective-permute-done.16.refs_2_ = bf16[64,640]{1,0:T(8,128)(2,1)S(1)} collective-permute-done((bf16[64,640]{1,0:T(8,128)(2,1)S(1)}, bf16[64,640]{1,0:T(8,128)(2,1)S(1)}, u32[]{:S(2)}, u32[]{:S(2)}) %collective-permute-start.16) | collective-permute-done | bytes 81952 | tf_op jit(solution)/shard_map/ppermute | solution.py:50
  102.9 1.6 %mix.1 = bf16[64,5120]{1,0:T(8,128)(2,1)} custom-call(s32[6]{0:T(128)S(1)} %stack.31.where_ref, bf16[64,5120]{1,0:T(8,128)(2,1)S(1)} %copy-done.4, f32[1,5120]{1,0:T(1,128)S(1)} %bitcast.14, bf16[64,640]{1,0:T(8,128)(2,1)S(1)} %get-tuple-element.61.refs_0_, bf16[64,640]{1,0:T(8,128)(2,1)S(1)} %collective-permute-done.15.refs_1_, ...), custom_call_target="tpu_custom_call" | custom-call | flops 1 | tf_op jit(solution)/shard_map/mix/pallas_call | solution.py:623
  (30 shorter events, 0.1 us)
Async XLA Ops:
  0.0 3.7 %copy-start = (bf16[1024,1280]{1,0:T(8,128)(2,1)S(1)}, bf16[1024,1280]{1,0:T(8,128)(2,1)}, u32[]{:S(2)}) copy-start(bf16[1024,1280]{1,0:T(8,128)(2,1)} %refs_6_) | copy-start | bytes 7864324
  3.5 7.4 %copy-start.7 = (bf16[3,256,256]{2,1,0:T(8,128)(2,1)S(1)}, bf16[3,256,256]{2,1,0:T(8,128)(2,1)}, u32[]{:S(2)}) copy-start(bf16[3,256,256]{2,1,0:T(8,128)(2,1)} %get-tuple-element.40) | copy-start | bytes 1179652
  3.6 8.2 %copy-start.3 = (bf16[256,1024]{1,0:T(8,128)(2,1)S(1)}, bf16[256,1024]{1,0:T(8,128)(2,1)}, u32[]{:S(2)}) copy-start(bf16[256,1024]{1,0:T(8,128)(2,1)} %q_ref.3) | copy-start | bytes 1572868
  3.6 8.2 %copy-start.6 = (s32[2,2,8]{2,1,0:T(2,128)S(1)}, s32[2,2,8]{2,1,0:T(2,128)}, u32[]{:S(2)}) copy-start(s32[2,2,8]{2,1,0:T(2,128)} %exps_ref.3) | copy-start | bytes 388
  3.7 3.7 %copy-start.9 = (bf16[3,256,256]{2,1,0:T(8,128)(2,1)S(1)}, bf16[3,256,256]{2,1,0:T(8,128)(2,1)}, u32[]{:S(2)}) copy-start(bf16[3,256,256]{2,1,0:T(8,128)(2,1)} %get-tuple-element.38) | copy-start | bytes 1179652
  3.7 7.3 %copy-start.8 = (bf16[3,256,256]{2,1,0:T(8,128)(2,1)S(1)}, bf16[3,256,256]{2,1,0:T(8,128)(2,1)}, u32[]{:S(2)}) copy-start(bf16[3,256,256]{2,1,0:T(8,128)(2,1)} %get-tuple-element.39) | copy-start | bytes 1179652
  3.7 8.1 %copy-start.2 = (bf16[2,256,1024]{2,1,0:T(8,128)(2,1)S(1)}, bf16[2,256,1024]{2,1,0:T(8,128)(2,1)}, u32[]{:S(2)}) copy-start(bf16[2,256,1024]{2,1,0:T(8,128)(2,1)} %fresh_ref.3) | copy-start | bytes 3145732
  4.4 31.8 %collective-permute-start = (bf16[512,1280]{1,0:T(8,128)(2,1)S(1)}, bf16[512,1280]{1,0:T(8,128)(2,1)S(1)}, u32[]{:S(2)}, u32[]{:S(2)}) collective-permute-start(bf16[512,1280]{1,0:T(8,128)(2,1)S(1)} %take.1), channel_id=1, source_target_pairs={{0,2},{2,0},{1,3},{3,1},{4,6},{6,4},{5,7},{7,5},{8,10},{10,8},{9,1... | collective-permute-start | bytes 3932168 | tf_op jit(solution)/shard_map/ppermute | solution.py:50
  7.4 30.5 %collective-permute-start.3 = (bf16[3,256,256]{2,1,0:T(8,128)(2,1)S(1)}, bf16[3,256,256]{2,1,0:T(8,128)(2,1)S(1)}, u32[]{:S(2)}, u32[]{:S(2)}) collective-permute-start(bf16[3,256,256]{2,1,0:T(8,128)(2,1)S(1)} %copy-done.9), channel_id=1, source_target_pairs={{0,12},{4,8},{8,4},{12,0},{1,13},{5,9},{9,5},{13,1},{2,14},{6,10},... | collective-permute-start | bytes 1179656 | tf_op jit(solution)/shard_map/ppermute | solution.py:50
  11.0 33.3 %collective-permute-start.2 = (bf16[3,256,256]{2,1,0:T(8,128)(2,1)S(1)}, bf16[3,256,256]{2,1,0:T(8,128)(2,1)S(1)}, u32[]{:S(2)}, u32[]{:S(2)}) collective-permute-start(bf16[3,256,256]{2,1,0:T(8,128)(2,1)S(1)} %copy-done.8), channel_id=1, source_target_pairs={{0,8},{4,12},{8,0},{12,4},{1,9},{5,13},{9,1},{13,5},{2,10},{6,14},... | collective-permute-start | bytes 1179656 | tf_op jit(solution)/shard_map/ppermute | solution.py:50
  11.0 33.3 %collective-permute-start.1 = (bf16[3,256,256]{2,1,0:T(8,128)(2,1)S(1)}, bf16[3,256,256]{2,1,0:T(8,128)(2,1)S(1)}, u32[]{:S(2)}, u32[]{:S(2)}) collective-permute-start(bf16[3,256,256]{2,1,0:T(8,128)(2,1)S(1)} %copy-done.7), channel_id=1, source_target_pairs={{0,4},{4,0},{8,12},{12,8},{1,5},{5,1},{9,13},{13,9},{2,6},{6,2},{1... | collective-permute-start | bytes 1179656 | tf_op jit(solution)/shard_map/ppermute | solution.py:50
  11.8 2.2 %copy-start.1 = (bf16[2,1024,1024]{2,1,0:T(8,128)(2,1)S(1)}, bf16[2,1024,1024]{2,1,0:T(8,128)(2,1)}, u32[]{:S(2)}) copy-start(bf16[2,1024,1024]{2,1,0:T(8,128)(2,1)} %cached_ref.3) | copy-start | bytes 12582916
  36.2 41.5 %collective-permute-start.11 = (bf16[512,1280]{1,0:T(8,128)(2,1)S(1)}, bf16[512,1280]{1,0:T(8,128)(2,1)S(1)}, u32[]{:S(2)}, u32[]{:S(2)}) collective-permute-start(bf16[512,1280]{1,0:T(8,128)(2,1)S(1)} %collective-permute-done.refs_7_.fetched_ref), channel_id=1, source_target_pairs={{0,16},{16,0},{1,17},{17,1},{2,18},{18,2},{3,19},{19,3},{4,20},{20... | collective-permute-start | bytes 3932168 | tf_op jit(solution)/shard_map/ppermute | solution.py:50
  46.6 14.2 %collective-permute-start.8 = (bf16[512,256]{1,0:T(8,128)(2,1)S(1)}, bf16[512,256]{1,0:T(8,128)(2,1)S(1)}, u32[]{:S(2)}, u32[]{:S(2)}) collective-permute-start(bf16[512,256]{1,0:T(8,128)(2,1)S(1)} %bitcast.9), channel_id=1, source_target_pairs={{0,8},{4,12},{8,0},{12,4},{1,9},{5,13},{9,1},{13,5},{2,10},{6,14},... | collective-permute-start | bytes 786440 | tf_op jit(solution)/shard_map/ppermute | solution.py:50
  46.6 14.2 %collective-permute-start.7 = (bf16[512,256]{1,0:T(8,128)(2,1)S(1)}, bf16[512,256]{1,0:T(8,128)(2,1)S(1)}, u32[]{:S(2)}, u32[]{:S(2)}) collective-permute-start(bf16[512,256]{1,0:T(8,128)(2,1)S(1)} %bitcast.10), channel_id=1, source_target_pairs={{0,4},{4,0},{8,12},{12,8},{1,5},{5,1},{9,13},{13,9},{2,6},{6,2},{1... | collective-permute-start | bytes 786440 | tf_op jit(solution)/shard_map/ppermute | solution.py:50
  52.0 6.4 %collective-permute-start.4 = (bf16[512,256]{1,0:T(8,128)(2,1)S(1)}, bf16[512,256]{1,0:T(8,128)(2,1)S(1)}, u32[]{:S(2)}, u32[]{:S(2)}) collective-permute-start(bf16[512,256]{1,0:T(8,128)(2,1)S(1)} %bitcast.13), channel_id=1, source_target_pairs={{0,2},{2,0},{1,3},{3,1},{4,6},{6,4},{5,7},{7,5},{8,10},{10,8},{9,1... | collective-permute-start | bytes 786440 | tf_op jit(solution)/shard_map/ppermute | solution.py:50
  58.4 12.9 %collective-permute-start.6 = (bf16[512,256]{1,0:T(8,128)(2,1)S(1)}, bf16[512,256]{1,0:T(8,128)(2,1)S(1)}, u32[]{:S(2)}, u32[]{:S(2)}) collective-permute-start(bf16[512,256]{1,0:T(8,128)(2,1)S(1)} %collective-permute-done.4.refs_2_), channel_id=1, source_target_pairs={{0,8},{4,12},{8,0},{12,4},{1,9},{5,13},{9,1},{13,5},{2,10},{6,14},... | collective-permute-start | bytes 786440 | tf_op jit(solution)/shard_map/ppermute | solution.py:50
  59.0 13.8 %collective-permute-start.5 = (bf16[512,256]{1,0:T(8,128)(2,1)S(1)}, bf16[512,256]{1,0:T(8,128)(2,1)S(1)}, u32[]{:S(2)}, u32[]{:S(2)}) collective-permute-start(bf16[512,256]{1,0:T(8,128)(2,1)S(1)} %collective-permute-done.4.refs_2_), channel_id=1, source_target_pairs={{0,4},{4,0},{8,12},{12,8},{1,5},{5,1},{9,13},{13,9},{2,6},{6,2},{1... | collective-permute-start | bytes 786440 | tf_op jit(solution)/shard_map/ppermute | solution.py:50
  60.8 13.9 %collective-permute-start.12 = (bf16[512,256]{1,0:T(8,128)(2,1)S(1)}, bf16[512,256]{1,0:T(8,128)(2,1)S(1)}, u32[]{:S(2)}, u32[]{:S(2)}) collective-permute-start(bf16[512,256]{1,0:T(8,128)(2,1)S(1)} %bitcast.12), channel_id=1, source_target_pairs={{4,8},{8,4},{5,9},{9,5},{6,10},{10,6},{7,11},{11,7},{20,24},{24,20... | collective-permute-start | bytes 786440 | tf_op jit(solution)/shard_map/ppermute | solution.py:50
  61.5 16.1 %collective-permute-start.13 = (bf16[512,256]{1,0:T(8,128)(2,1)S(1)}, bf16[512,256]{1,0:T(8,128)(2,1)S(1)}, u32[]{:S(2)}, u32[]{:S(2)}) collective-permute-start(bf16[512,256]{1,0:T(8,128)(2,1)S(1)} %collective-permute-done.8.refs_0_), channel_id=1, source_target_pairs={{4,0},{8,12},{5,1},{9,13},{6,2},{10,14},{7,3},{11,15},{20,16},{24,... | collective-permute-start | bytes 786440 | tf_op jit(solution)/shard_map/ppermute | solution.py:594
  72.8 8.8 %collective-permute-start.9 = (bf16[512,256]{1,0:T(8,128)(2,1)S(1)}, bf16[512,256]{1,0:T(8,128)(2,1)S(1)}, u32[]{:S(2)}, u32[]{:S(2)}) collective-permute-start(bf16[512,256]{1,0:T(8,128)(2,1)S(1)} %collective-permute-done.4.refs_2_), channel_id=1, source_target_pairs={{4,8},{8,4},{5,9},{9,5},{6,10},{10,6},{7,11},{11,7},{20,24},{24,20... | collective-permute-start | bytes 786440 | tf_op jit(solution)/shard_map/ppermute | solution.py:50
  73.4 9.2 %collective-permute-start.10 = (bf16[512,256]{1,0:T(8,128)(2,1)S(1)}, bf16[512,256]{1,0:T(8,128)(2,1)S(1)}, u32[]{:S(2)}, u32[]{:S(2)}) collective-permute-start(bf16[512,256]{1,0:T(8,128)(2,1)S(1)} %collective-permute-done.6.refs_3_), channel_id=1, source_target_pairs={{4,0},{8,12},{5,1},{9,13},{6,2},{10,14},{7,3},{11,15},{20,16},{24,... | collective-permute-start | bytes 786440 | tf_op jit(solution)/shard_map/ppermute | solution.py:594
  83.7 19.2 %copy-start.4 = (bf16[64,5120]{1,0:T(8,128)(2,1)S(1)}, bf16[64,5120]{1,0:T(8,128)(2,1)}, u32[]{:S(2)}) copy-start(bf16[64,5120]{1,0:T(8,128)(2,1)} %hidden_ref.1) | copy-start | bytes 1966084
  83.7 19.2 %copy-start.5 = (f32[5120]{0:T(1024)S(1)}, f32[5120]{0:T(1024)}, u32[]{:S(2)}) copy-start(f32[5120]{0:T(1024)} %param.13) | copy-start | bytes 61444
  83.7 1.8 %collective-permute-start.18 = (bf16[4,64,640]{2,1,0:T(8,128)(2,1)S(1)}, bf16[4,64,640]{2,1,0:T(8,128)(2,1)S(1)}, u32[]{:S(2)}, u32[]{:S(2)}) collective-permute-start(bf16[4,64,640]{2,1,0:T(8,128)(2,1)S(1)} %get-tuple-element.66), channel_id=1, source_target_pairs={{0,1},{1,0},{2,3},{3,2},{4,5},{5,4},{6,7},{7,6},{8,9},{9,8},{10,11... | collective-permute-start | bytes 983048 | tf_op jit(solution)/shard_map/ppermute | solution.py:50
  84.9 5.6 %collective-permute-start.14 = (bf16[4,64,640]{2,1,0:T(8,128)(2,1)S(1)}, bf16[4,64,640]{2,1,0:T(8,128)(2,1)S(1)}, u32[]{:S(2)}, u32[]{:S(2)}) collective-permute-start(bf16[4,64,640]{2,1,0:T(8,128)(2,1)S(1)} %get-tuple-element.60), channel_id=1, source_target_pairs={{0,1},{1,0},{2,3},{3,2},{4,5},{5,4},{6,7},{7,6},{8,9},{9,8},{10,11... | collective-permute-start | bytes 983048 | tf_op jit(solution)/shard_map/ppermute | solution.py:50
  86.1 7.3 %collective-permute-start.19 = (bf16[64,640]{1,0:T(8,128)(2,1)S(1)}, bf16[64,640]{1,0:T(8,128)(2,1)S(1)}, u32[]{:S(2)}, u32[]{:S(2)}) collective-permute-start(bf16[64,640]{1,0:T(8,128)(2,1)S(1)} %get-tuple-element.68), channel_id=1, source_target_pairs={{0,12},{4,8},{8,4},{12,0},{1,13},{5,9},{9,5},{13,1},{2,14},{6,10},... | collective-permute-start | bytes 245768 | tf_op jit(solution)/shard_map/ppermute | solution.py:50
  88.0 10.7 %collective-permute-start.20 = (bf16[64,640]{1,0:T(8,128)(2,1)S(1)}, bf16[64,640]{1,0:T(8,128)(2,1)S(1)}, u32[]{:S(2)}, u32[]{:S(2)}) collective-permute-start(bf16[64,640]{1,0:T(8,128)(2,1)S(1)} %get-tuple-element.69), channel_id=1, source_target_pairs={{0,8},{4,12},{8,0},{12,4},{1,9},{5,13},{9,1},{13,5},{2,10},{6,14},... | collective-permute-start | bytes 245768 | tf_op jit(solution)/shard_map/ppermute | solution.py:50
  88.0 10.7 %collective-permute-start.21 = (bf16[64,640]{1,0:T(8,128)(2,1)S(1)}, bf16[64,640]{1,0:T(8,128)(2,1)S(1)}, u32[]{:S(2)}, u32[]{:S(2)}) collective-permute-start(bf16[64,640]{1,0:T(8,128)(2,1)S(1)} %get-tuple-element.70), channel_id=1, source_target_pairs={{0,4},{4,0},{8,12},{12,8},{1,5},{5,1},{9,13},{13,9},{2,6},{6,2},{1... | collective-permute-start | bytes 245768 | tf_op jit(solution)/shard_map/ppermute | solution.py:50
  91.2 7.5 %collective-permute-start.15 = (bf16[64,640]{1,0:T(8,128)(2,1)S(1)}, bf16[64,640]{1,0:T(8,128)(2,1)S(1)}, u32[]{:S(2)}, u32[]{:S(2)}) collective-permute-start(bf16[64,640]{1,0:T(8,128)(2,1)S(1)} %get-tuple-element.62), channel_id=1, source_target_pairs={{0,12},{4,8},{8,4},{12,0},{1,13},{5,9},{9,5},{13,1},{2,14},{6,10},... | collective-permute-start | bytes 245768 | tf_op jit(solution)/shard_map/ppermute | solution.py:50
  93.1 9.9 %collective-permute-start.16 = (bf16[64,640]{1,0:T(8,128)(2,1)S(1)}, bf16[64,640]{1,0:T(8,128)(2,1)S(1)}, u32[]{:S(2)}, u32[]{:S(2)}) collective-permute-start(bf16[64,640]{1,0:T(8,128)(2,1)S(1)} %get-tuple-element.63), channel_id=1, source_target_pairs={{0,8},{4,12},{8,0},{12,4},{1,9},{5,13},{9,1},{13,5},{2,10},{6,14},... | collective-permute-start | bytes 245768 | tf_op jit(solution)/shard_map/ppermute | solution.py:50
  93.4 9.6 %collective-permute-start.17 = (bf16[64,640]{1,0:T(8,128)(2,1)S(1)}, bf16[64,640]{1,0:T(8,128)(2,1)S(1)}, u32[]{:S(2)}, u32[]{:S(2)}) collective-permute-start(bf16[64,640]{1,0:T(8,128)(2,1)S(1)} %get-tuple-element.64), channel_id=1, source_target_pairs={{0,4},{4,0},{8,12},{12,8},{1,5},{5,1},{9,13},{13,9},{2,6},{6,2},{1... | collective-permute-start | bytes 245768 | tf_op jit(solution)/shard_map/ppermute | solution.py:50

commit v27 on v26

--- a/solution.py
+++ b/solution.py
@@ -583,14 +583,308 @@
     other = swap(attend_half(where, 1, pieces), "head", 2, 1)
     acc = add_product(where, {0: mine}, out_weight)
     other, acc = lax.optimization_barrier((other, acc))
-    slots = []
+    slots, last = [], other
     for at, x in enumerate((mine, other)):
         next_to, far = swap(x, "patch", 4, 1), swap(x, "patch", 4, 2)
         next_to, far, other, x = lax.optimization_barrier((next_to, far, other, x))
         if at == 1:
             acc = add_product(where, {2: slots[0][2], 1: slots[0][1]}, out_weight, acc)
             far, x, acc = lax.optimization_barrier((far, x, acc))
-        middle = swap(x, "patch", 4, 3, (1, 2))
+        middle = swap((mine, last)[at], "patch", 4, 3, (1, 2))
+        ends = lax.ppermute(far[at], "patch", [(1, 0), (2, 3)])
+        if at + 1 < len(parts):
+            ends, far[at + 1], next_to[at + 1] = lax.optimization_barrier(
+                (ends, far[at + 1], next_to[at + 1])
+            )
+        out.append(([x, next_to[at], far[at], middle], [ends]))
+    return out
+
+
+def add_sub_kernel(n_sub, where_ref, *refs):
+    terms, kept_ref, outs = refs[:n_sub], refs[n_sub], refs[n_sub + 1 :]
+    for head in range(len(outs) + 1):
+        total = terms[0][head].astype(jnp.float32)
+        for term in terms[1:]:
+            total += term[head].astype(jnp.float32)
+        if head == 0:
+            kept_ref[...] = total
+        else:
+            outs[head - 1][...] = total.astype(jnp.bfloat16)
+
+
+def add_head_kernel(n_more, where_ref, kept_ref, *refs):
+    for at, out in enumerate(refs[n_more:]):
+        total = kept_ref[at]
+        for term in refs[:n_more]:
+            total += term[at].astype(jnp.float32)
+        out[...] = total.astype(jnp.bfloat16)
+
+
+def reduce_sub(sizes, where, terms):
+    n_sub, n_head = sizes["sub"], sizes["head"]
+    terms = [terms[0]] + [swap(terms[rel], "sub", n_sub, rel) for rel in range(1, n_sub)]
+    shape = terms[0].shape[1:]
+    return call(
+        functools.partial(add_sub_kernel, n_sub),
+        "add_sub",
+        [jax.ShapeDtypeStruct(shape, jnp.float32)]
+        + [jax.ShapeDtypeStruct(shape, jnp.bfloat16)] * (n_head - 1),
+        1,
+        [spec(terms[0].shape)] * n_sub,
+        [spec(shape)] * n_head,
+    )(where, *terms)
+
+
+def reduce_head(sizes, where, sums):
+    n_head = sizes["head"]
+    shape = sums[0].shape
+    sums = [sums[0]] + [swap(sums[rel], "head", n_head, rel) for rel in range(1, n_head)]
+    return call(
+        functools.partial(add_head_kernel, n_head - 1),
+        "add_head",
+        [jax.ShapeDtypeStruct(shape[1:], jnp.bfloat16)] * shape[0],
+        1,
+        [spec(shape)] * n_head,
+        [spec(shape[1:])] * shape[0],
+    )(where, *sums)
+
+
+def sum_tail(sizes, where, pieces, kv_pieces, out_weight, hidden_in, attn_gate):
+    n_patch, n_head, n_sub = sizes["patch"], sizes["head"], sizes["sub"]
+    split, tok = len(pieces), pieces[0].shape[1]
+    count = n_head * n_sub
+    piece = tok // count
+    parts = 2 if piece % 32 == 0 else 1
+    attended = []
+    for part in range(parts):
+        rows = (part * (piece // parts), piece // parts)
+        x = attend(where, rows, count, pieces, kv_pieces)
+        attended.append(x.reshape(-1, x.shape[2]))
+    slots = gather(attended, n_patch)
+    blocks = []
+    for part in range(parts):
+        terms = project(split, where, *slots[part], out_weight, n_head, n_sub)
+        total = reduce_head(sizes, where, reduce_sub(sizes, where, terms))
+        blocks.append(
+            [total[0]] + [swap(total[rel], "patch", n_patch, rel) for rel in range(1, n_patch)]
+        )
+    return mix(where, hidden_in, attn_gate, blocks)
+
+
+def attend_half_kernel(half, where_ref, *refs):
+    pieces, out = refs[:-1], refs[-1]
+    factor = HEAD_DIM**-0.5 * math.log2(math.e)
+    rows, feat = out.shape[1:]
+    start = pl.multiple_of((where_ref[HEAD] ^ half) * rows, rows)
+    for head in range(feat // HEAD_DIM):
+        lanes = pl.ds(head * HEAD_DIM, HEAD_DIM)
+        keys = jnp.concatenate([ref[1, :, lanes] for ref in pieces], axis=0)
+        values = jnp.concatenate([ref[2, :, lanes] for ref in pieces], axis=0)
+        values = jnp.concatenate([values, jnp.ones_like(values)], axis=1)
+        for first in range(0, len(pieces), 2):
+            query = [ref[0, pl.ds(start, rows), lanes] for ref in pieces[first : first + 2]]
+            scores = lax.dot_general(
+                jnp.concatenate(query, axis=0),
+                keys,
+                (((1,), (1,)), ((), ())),
+                preferred_element_type=jnp.float32,
+            )
+            peak = jnp.max(scores, axis=1, keepdims=True)
+            expo = jnp.exp2((scores - peak) * factor).astype(jnp.bfloat16)
+            mix = jnp.dot(expo, values, preferred_element_type=jnp.float32)
+            mix = (mix[:, :HEAD_DIM] / mix[:, HEAD_DIM:]).astype(jnp.bfloat16)
+            for at in range(len(query)):
+                block = mix[at * rows : (at + 1) * rows]
+                out[where_ref[NEAR] ^ (first + at), :, lanes] = block
+
+
+def attend_half(where, half, pieces):
+    _, tok, feat = pieces[0].shape
+    out = jax.ShapeDtypeStruct((len(pieces), tok // 2, feat), jnp.bfloat16)
+    return call(
+        functools.partial(attend_half_kernel, half),
+        "attend",
+        out,
+        1,
+        [spec((3, tok, feat))] * len(pieces),
+        spec(out.shape),
+        flops=HALF_FLOPS,
+    )(where, *pieces).reshape(-1, feat)
+
+
+def add_product_kernel(count, where_ref, *refs):
+    total = refs[2 * count][...] if len(refs) > 2 * count + 1 else None
+    for slot, weight in zip(refs[:count], refs[count : 2 * count]):
+        term = jnp.dot(slot[...], weight[...], preferred_element_type=jnp.float32)
+        total = term if total is None else total + term
+    refs[-1][...] = total
+
+
+def add_product(where, slots, weight, acc=None):
+    rows, feat = next(iter(slots.values())).shape
+    cols = weight.shape[1]
+    wide = cols // 2
+    whole = pl.BlockSpec((rows, wide), lambda i, w: (0, i))
+    rels = list(slots)
+    return call(
+        functools.partial(add_product_kernel, len(rels)),
+        "products",
+        jax.ShapeDtypeStruct((rows, cols), jnp.float32),
+        2,
+        [spec((rows, feat))] * len(rels)
+        + [pl.BlockSpec((feat, wide), lambda i, w, rel=rel: (w[NEAR] ^ rel, i)) for rel in rels]
+        + ([] if acc is None else [whole]),
+        whole,
+        flops=ZERO_FLOPS if acc is None else 1,
+    )(where, *slots.values(), *[weight] * len(rels), *([] if acc is None else [acc]))
+
+
+def partner_place(where_ref, head):
+    return (head + FETCHED * where_ref[GRP]) % 8
+
+
+def first_kernel(where_ref, *refs):
+    last, more, slots = refs[0], refs[1], refs[2:5]
+    acc_ref, own_ref, fetched_ref, passed_ref, out_ref, held_ref = refs[5:]
+    rows, feat = last.shape
+    cut = fetched_ref.shape[0]
+
+    def put(at, block):
+        for head in range(2):
+            there = partner_place(where_ref, 2 * (where_ref[NEAR] ^ at) + head)
+            lanes = pl.ds(pl.multiple_of(there * HEAD_DIM, HEAD_DIM), HEAD_DIM)
+            held_ref[:, lanes] = block[:, head * HEAD_DIM : (head + 1) * HEAD_DIM]
+
+    @pl.when(pl.program_id(0) == 0)
+    def arrange():
+        for at, slot in zip((0, 2, 1), slots):
+            put(at, slot[...])
+        put(3, jnp.zeros((rows, feat), jnp.bfloat16))
+
+    block = jnp.where(where_ref[INNER] == 1, last[...], more[...])
+    acc = acc_ref[...]
+    acc += jnp.dot(block, own_ref[...], preferred_element_type=jnp.float32)
+    acc += jnp.dot(held_ref[:, :cut], fetched_ref[...], preferred_element_type=jnp.float32)
+    acc += jnp.dot(held_ref[:, cut:], passed_ref[...], preferred_element_type=jnp.float32)
+    out_ref[...] = acc
+
+
+def first_product(where, last, more, slots, acc, weights):
+    rows, feat = last.shape
+    own, fetched, passed = weights
+    wide = own.shape[1] // 2
+    whole = pl.BlockSpec((rows, wide), lambda i, w: (0, i))
+    return call(
+        first_kernel,
+        "first",
+        jax.ShapeDtypeStruct(acc.shape, jnp.float32),
+        2,
+        [spec((rows, feat))] * 5
+        + [whole, pl.BlockSpec((feat, wide), lambda i, w: (w[NEAR] ^ 3, i))]
+        + [pl.BlockSpec((x.shape[0], wide), lambda i, w: (0, i)) for x in (fetched, passed)],
+        whole,
+        [pltpu.VMEM((rows, 4 * feat), jnp.bfloat16)],
+    )(where, last, more, *slots, acc, own, fetched, passed)
+
+
+def second_kernel(where_ref, slot, more, fetched_ref, passed_ref, acc_in, keep_ref, send_ref, acc_ref):
+    weight = []
+    for head in range(2):
+        place = partner_place(where_ref, 2 * (where_ref[NEAR] ^ 3) + head)
+        here = jnp.minimum(place, FETCHED - 1) * HEAD_DIM
+        there = jnp.maximum(place - FETCHED, 0) * HEAD_DIM
+        weight.append(
+            jnp.where(
+                place < FETCHED,
+                fetched_ref[pl.ds(pl.multiple_of(here, HEAD_DIM), HEAD_DIM), :],
+                passed_ref[pl.ds(pl.multiple_of(there, HEAD_DIM), HEAD_DIM), :],
+            )
+        )
+    block = jnp.where(where_ref[INNER] == 1, slot[...], more[...])
+    acc = acc_in[...] + jnp.dot(
+        block, jnp.concatenate(weight, axis=0), preferred_element_type=jnp.float32
+    )
+    acc_ref[...] = acc.reshape(acc_ref.shape)
+    for sub, out in enumerate((keep_ref, send_ref)):
+        for at in range(4):
+            out[at] = acc_ref[where_ref[NEAR] ^ at, where_ref[SUB] ^ sub].astype(jnp.bfloat16)
+
+
+def second_product(where, chunk, slot, more, weights, acc):
+    rows, feat = slot.shape
+    cols = weights[0].shape[1]
+    wide = cols // 2
+    out = jax.ShapeDtypeStruct((4, rows // 8, wide), jnp.bfloat16)
+    return call(
+        second_kernel,
+        "second",
+        [out] * 2,
+        1,
+        [spec((rows, feat))] * 2
+        + [pl.BlockSpec((x.shape[0], wide), lambda i, w: (0, chunk)) for x in weights]
+        + [pl.BlockSpec((rows, wide), lambda i, w: (0, chunk))],
+        [spec(out.shape)] * 2,
+        [pltpu.VMEM((4, 2, rows // 8, wide), jnp.float32)],
+    )(where, slot, more, *weights, acc)
+
+
+def add_kernel(where_ref, keep_ref, term_ref, *outs):
+    for at, out in enumerate(outs):
+        total = keep_ref[at].astype(jnp.float32) + term_ref[at].astype(jnp.float32)
+        out[...] = total.astype(jnp.bfloat16)
+
+
+def add(where, keep, term):
+    return call(
+        add_kernel,
+        "add",
+        [jax.ShapeDtypeStruct(keep.shape[1:], jnp.bfloat16)] * keep.shape[0],
+        1,
+        [spec(keep.shape)] * 2,
+        [spec(keep.shape[1:])] * keep.shape[0],
+    )(where, keep, term)
+
+
+def take_kernel(where_ref, weight_ref, out_ref):
+    out_ref[...] = weight_ref[...]
+
+
+def take_half(where, weight):
+    rows, cols = weight.shape[0] // 2, weight.shape[1]
+    return call(
+        take_kernel,
+        "take",
+        jax.ShapeDtypeStruct((rows, cols), weight.dtype),
+        2,
+        [pl.BlockSpec((rows // 2, cols), lambda i, w: (2 * w[GRP] + i, 0))],
+        pl.BlockSpec((rows // 2, cols), lambda i, w: (i, 0)),
+    )(where, weight)
+
+
+def share_tail(sizes, where, pieces, kv_pieces, out_weight, hidden_in, attn_gate):
+    out_weight, where = lax.optimization_barrier((out_weight, where))
+    fetched = swap(take_half(where, out_weight), "head", 2, 1)
+    own, fetched = lax.optimization_barrier((pieces[0], fetched))
+    pieces = [own, *pieces[1:]]
+    passed = swap(fetched, "grp", 2, 1)
+
+    pieces = [pieces[0], *pieces[:0:-1]]
+    mine = attend_half(where, 0, pieces)
+    where, mine = lax.optimization_barrier((where, mine))
+    other = swap(attend_half(where, 1, pieces), "head", 2, 1)
+    acc = add_product(where, {0: mine}, out_weight)
+    other, acc = lax.optimization_barrier((other, acc))
+    slots, last = [], other
+    for at, x in enumerate((mine, other)):
+        next_to, far = swap(x, "patch", 4, 1), swap(x, "patch", 4, 2)
+        next_to, far, other, x = lax.optimization_barrier((next_to, far, other, x))
+        if at == 1:
+            acc = add_product(where, {2: slots[0][2], 1: slots[0][1]}, out_weight, acc)
+            far, x, acc = lax.optimization_barrier((far, x, acc))
+        if at == 0:
+            middle = swap(x, "patch", 4, 3, (1, 2))
+        else:
+            middle = swap(last, "patch", 4, 3, (1, 2))
         ends = lax.ppermute(far, "patch", [(1, 0), (2, 3)])
         slots.append([x, next_to, far, middle, ends])
     weights = [out_weight, fetched, passed]

time: 105 us -> 107 us (1.019)
  starting transfers between devices: 28.4 us -> 30.9 us
    ppermute x20, starting transfers between devices: 25.8 us -> 28.4 us  [swap(): return lax.ppermute(x, axes, pairs)]
    ppermute x20, waiting for transfers between devices: 46.8 us -> 45.6 us  [swap(): return lax.ppermute(x, axes, pairs)]
  transfers between devices with their start and end apart: 22 -> 22, of which waited for: 11 -> 10; matrix products, arithmetic and copies ran while one was open for 0% -> 0% of each run, Pallas kernels for 15% -> 15%
where the time goes in v27:
time: 107 us
  waiting for transfers between devices  50.1 us (47%)
  starting transfers between devices  30.9 us (29%)
  Pallas kernels  22.9 us (21%)
  local copies, waits for them, and re-layouts  2.32 us (2%)
    ppermute x20, waiting for transfers between devices, swap(): return lax.ppermute(x, axes, pairs)  45.6 us
    ppermute x20, starting transfers between devices, swap(): return lax.ppermute(x, axes, pairs)  28.4 us
    pallas_call x2, Pallas kernels, attend_half(): call(functools.partial(attend_half_kernel, half), 'attend', out, 1, [spec...  4.63 us
    ppermute x2, waiting for transfers between devices, share_tail(): ends = lax.ppermute(far, 'patch', [(1, 0), (2, 3)])  4.57 us
    pallas_call x1, Pallas kernels, first_product(): call(first_kernel, 'first', jax.ShapeDtypeStruct(acc.shape, jnp.float32),...  3.96 us
    pallas_call x2, Pallas kernels, add_product(): call(functools.partial(add_product_kernel, len(rels)), 'products', jax.Sh...  3.79 us
    pallas_call x1, Pallas kernels, pack(): pl.pallas_call(functools.partial(pack_kernel, split, feat // HEAD_DIM), o...  3.53 us
    ppermute x2, starting transfers between devices, share_tail(): ends = lax.ppermute(far, 'patch', [(1, 0), (2, 3)])  2.57 us
  transfers between devices with their start and end apart: 22, of which 10 were waited for; matrix products, arithmetic and copies ran while one was open for 0% of the time, Pallas kernels for 15%

profile of v27, /device:TPU:0, one launch (start us, length us, event | category | flops | bytes accessed | tf_op | source)
XLA Modules:
  0.0 106.5 jit_solution(877838938430016347)
XLA Ops:
  0.0 3.5 %pack.1 = (bf16[3,256,256]{2,1,0:T(8,128)(2,1)}, bf16[3,256,256]{2,1,0:T(8,128)(2,1)}, bf16[3,256,256]{2,1,0:T(8,128)(2,1)}) custom-call(s32[2,2,8]{2,1,0:T(2,128)} %exps_ref.3, bf16[256,1024]{1,0:T(8,128)(2,1)} %q_ref.3, bf16[2,256,1024]{2,1,0:T(8,128)(2,1)} %fresh_ref.3, bf16[2,1024,1024]{2,1,0:T(8,128)(2,1)} %cached_ref.3), custom_call_target="tpu_custom_call" | custom-call | tf_op jit(solution)/shard_map/pack/pallas_call | solution.py:114
  3.6 0.0 copy-start.3
  3.6 0.0 copy-start.6
  3.6 0.1 stack.31.where_ref
  3.7 0.7 take.1
  4.4 3.0 %collective-permute-start = (bf16[512,1280]{1,0:T(8,128)(2,1)S(1)}, bf16[512,1280]{1,0:T(8,128)(2,1)S(1)}, u32[]{:S(2)}, u32[]{:S(2)}) collective-permute-start(bf16[512,1280]{1,0:T(8,128)(2,1)S(1)} %take.1), channel_id=1, source_target_pairs={{0,2},{2,0},{1,3},{3,1},{4,6},{6,4},{5,7},{7,5},{8,10},{10,8},{9,1... | collective-permute-start | bytes 3932168 | tf_op jit(solution)/shard_map/ppermute | solution.py:50
  7.4 3.6 %collective-permute-start.3 = (bf16[3,256,256]{2,1,0:T(8,128)(2,1)S(1)}, bf16[3,256,256]{2,1,0:T(8,128)(2,1)S(1)}, u32[]{:S(2)}, u32[]{:S(2)}) collective-permute-start(bf16[3,256,256]{2,1,0:T(8,128)(2,1)S(1)} %copy-done.9), channel_id=1, source_target_pairs={{0,12},{4,8},{8,4},{12,0},{1,13},{5,9},{9,5},{13,1},{2,14},{6,10},... | collective-permute-start | bytes 1179656 | tf_op jit(solution)/shard_map/ppermute | solution.py:50
  11.0 0.8 collective-permute-start.1
  11.8 2.2 %copy-done.1 = bf16[2,1024,1024]{2,1,0:T(8,128)(2,1)S(1)} copy-done((bf16[2,1024,1024]{2,1,0:T(8,128)(2,1)S(1)}, bf16[2,1024,1024]{2,1,0:T(8,128)(2,1)}, u32[]{:S(2)}) %copy-start.1) | copy-done | bytes 4194328
  14.0 1.3 %own.1.refs_0_ = bf16[3,256,256]{2,1,0:T(8,128)(2,1)S(1)} custom-call(s32[6]{0:T(128)S(1)} %stack.31.where_ref, s32[2,2,8]{2,1,0:T(2,128)S(1)} %copy-done.6, bf16[256,1024]{1,0:T(8,128)(2,1)S(1)} %copy-done.3, bf16[2,256,1024]{2,1,0:T(8,128)(2,1)S(1)} %copy-done.2, bf16[2,1024,1024]{2,1,0:T(8,128)(2,1)S(1)} %copy-done.1), custom_call_target="tpu_custom_call" | custom-call | flops 1 | tf_op jit(solution)/shard_map/own/pallas_call | solution.py:150
  15.3 20.9 %collective-permute-done.refs_7_.fetched_ref = bf16[512,1280]{1,0:T(8,128)(2,1)S(1)} collective-permute-done((bf16[512,1280]{1,0:T(8,128)(2,1)S(1)}, bf16[512,1280]{1,0:T(8,128)(2,1)S(1)}, u32[]{:S(2)}, u32[]{:S(2)}) %collective-permute-start) | collective-permute-done | bytes 1310752 | tf_op jit(solution)/shard_map/ppermute | solution.py:50
  36.2 1.8 %collective-permute-start.11 = (bf16[512,1280]{1,0:T(8,128)(2,1)S(1)}, bf16[512,1280]{1,0:T(8,128)(2,1)S(1)}, u32[]{:S(2)}, u32[]{:S(2)}) collective-permute-start(bf16[512,1280]{1,0:T(8,128)(2,1)S(1)} %collective-permute-done.refs_7_.fetched_ref), channel_id=1, source_target_pairs={{0,16},{16,0},{1,17},{17,1},{2,18},{18,2},{3,19},{19,3},{4,20},{20... | collective-permute-start | bytes 3932168 | tf_op jit(solution)/shard_map/ppermute | solution.py:50
  37.9 6.3 %collective-permute-done.2.refs_2_ = bf16[3,256,256]{2,1,0:T(8,128)(2,1)S(1)} collective-permute-done((bf16[3,256,256]{2,1,0:T(8,128)(2,1)S(1)}, bf16[3,256,256]{2,1,0:T(8,128)(2,1)S(1)}, u32[]{:S(2)}, u32[]{:S(2)}) %collective-permute-start.2) | collective-permute-done | bytes 393248 | tf_op jit(solution)/shard_map/ppermute | solution.py:50
  44.2 2.3 %attend.2 = bf16[4,128,256]{2,1,0:T(8,128)(2,1)S(1)} custom-call(s32[6]{0:T(128)S(1)} %stack.31.where_ref, bf16[3,256,256]{2,1,0:T(8,128)(2,1)S(1)} %own.1.refs_0_, bf16[3,256,256]{2,1,0:T(8,128)(2,1)S(1)} %collective-permute-done.1.refs_1_, bf16[3,256,256]{2,1,0:T(8,128)(2,1)S(1)} %collective-permute-done.2.refs_2_, ...), custom_call_target="tpu_custom_call" | custom-call | flops 1 | tf_op jit(solution)/shard_map/attend/pallas_call | solution.py:704
  46.6 0.1 collective-permute-start.9
  46.6 3.0 %collective-permute-start.8 = (bf16[512,256]{1,0:T(8,128)(2,1)S(1)}, bf16[512,256]{1,0:T(8,128)(2,1)S(1)}, u32[]{:S(2)}, u32[]{:S(2)}) collective-permute-start(bf16[512,256]{1,0:T(8,128)(2,1)S(1)} %bitcast.10), channel_id=1, source_target_pairs={{0,4},{4,0},{8,12},{12,8},{1,5},{5,1},{9,13},{13,9},{2,6},{6,2},{1... | collective-permute-start | bytes 786440 | tf_op jit(solution)/shard_map/ppermute | solution.py:50
  49.7 2.3 %attend.3 = bf16[4,128,256]{2,1,0:T(8,128)(2,1)S(1)} custom-call(s32[6]{0:T(128)S(1)} %stack.31.where_ref, bf16[3,256,256]{2,1,0:T(8,128)(2,1)S(1)} %own.1.refs_0_, bf16[3,256,256]{2,1,0:T(8,128)(2,1)S(1)} %collective-permute-done.1.refs_1_, bf16[3,256,256]{2,1,0:T(8,128)(2,1)S(1)} %collective-permute-done.2.refs_2_, ...), custom_call_target="tpu_custom_call" | custom-call | flops 1 | tf_op jit(solution)/shard_map/attend/pallas_call | solution.py:704
  52.0 0.6 collective-permute-start.4
  52.6 1.5 %products.2.refs_4_ = f32[512,1280]{1,0:T(8,128)S(1)} custom-call(s32[6]{0:T(128)S(1)} %stack.31.where_ref, bf16[512,256]{1,0:T(8,128)(2,1)S(1)} %bitcast.11, bf16[1024,1280]{1,0:T(8,128)(2,1)S(1)} %copy-done), custom_call_target="tpu_custom_call" | custom-call | flops 6000000000 | tf_op jit(solution)/shard_map/products/pallas_call | solution.py:729
  54.2 4.3 %collective-permute-done.4.refs_2_ = bf16[512,256]{1,0:T(8,128)(2,1)S(1)} collective-permute-done((bf16[512,256]{1,0:T(8,128)(2,1)S(1)}, bf16[512,256]{1,0:T(8,128)(2,1)S(1)}, u32[]{:S(2)}, u32[]{:S(2)}) %collective-permute-start.4) | collective-permute-done | bytes 262176 | tf_op jit(solution)/shard_map/ppermute | solution.py:50
  58.4 0.6 collective-permute-start.7
  59.0 1.7 %collective-permute-start.6 = (bf16[512,256]{1,0:T(8,128)(2,1)S(1)}, bf16[512,256]{1,0:T(8,128)(2,1)S(1)}, u32[]{:S(2)}, u32[]{:S(2)}) collective-permute-start(bf16[512,256]{1,0:T(8,128)(2,1)S(1)} %collective-permute-done.4.refs_2_), channel_id=1, source_target_pairs={{0,4},{4,0},{8,12},{12,8},{1,5},{5,1},{9,13},{13,9},{2,6},{6,2},{1... | collective-permute-start | bytes 786440 | tf_op jit(solution)/shard_map/ppermute | solution.py:50
  60.7 0.1 collective-permute-done.9.refs_0_
  60.8 0.7 collective-permute-start.5
  61.5 1.3 %collective-permute-start.13 = (bf16[512,256]{1,0:T(8,128)(2,1)S(1)}, bf16[512,256]{1,0:T(8,128)(2,1)S(1)}, u32[]{:S(2)}, u32[]{:S(2)}) collective-permute-start(bf16[512,256]{1,0:T(8,128)(2,1)S(1)} %collective-permute-done.9.refs_0_), channel_id=1, source_target_pairs={{4,0},{8,12},{5,1},{9,13},{6,2},{10,14},{7,3},{11,15},{20,16},{24,... | collective-permute-start | bytes 786440 | tf_op jit(solution)/shard_map/ppermute | solution.py:888
  62.8 2.2 %products.3.refs_5_ = f32[512,1280]{1,0:T(8,128)S(1)} custom-call(s32[6]{0:T(128)S(1)} %stack.31.where_ref, bf16[512,256]{1,0:T(8,128)(2,1)S(1)} %collective-permute-done.9.refs_0_, bf16[512,256]{1,0:T(8,128)(2,1)S(1)} %collective-permute-done.8.refs_1_, bf16[1024,1280]{1,0:T(8,128)(2,1)S(1)} %copy-done, bf16[1024,1280]{1,0:T(8,128)(2,1)S(1)} %copy-done, ...), custom_call_target="tpu_custom_call" | custom-call | flops 1 | tf_op jit(solution)/shard_map/products/pallas_call | solution.py:729
  65.0 6.3 %collective-permute-done.7.refs_3_ = bf16[512,256]{1,0:T(8,128)(2,1)S(1)} collective-permute-done((bf16[512,256]{1,0:T(8,128)(2,1)S(1)}, bf16[512,256]{1,0:T(8,128)(2,1)S(1)}, u32[]{:S(2)}, u32[]{:S(2)}) %collective-permute-start.7) | collective-permute-done | bytes 262176 | tf_op jit(solution)/shard_map/ppermute | solution.py:50
  71.3 0.7 collective-permute-start.12
  72.0 0.7 collective-permute-done.6.refs_4_
  72.8 1.3 %collective-permute-start.10 = (bf16[512,256]{1,0:T(8,128)(2,1)S(1)}, bf16[512,256]{1,0:T(8,128)(2,1)S(1)}, u32[]{:S(2)}, u32[]{:S(2)}) collective-permute-start(bf16[512,256]{1,0:T(8,128)(2,1)S(1)} %collective-permute-done.7.refs_3_), channel_id=1, source_target_pairs={{4,0},{8,12},{5,1},{9,13},{6,2},{10,14},{7,3},{11,15},{20,16},{24,... | collective-permute-start | bytes 786440 | tf_op jit(solution)/shard_map/ppermute | solution.py:888
  74.1 3.5 %collective-permute-done.13.refs_1_ = bf16[512,256]{1,0:T(8,128)(2,1)S(1)} collective-permute-done((bf16[512,256]{1,0:T(8,128)(2,1)S(1)}, bf16[512,256]{1,0:T(8,128)(2,1)S(1)}, u32[]{:S(2)}, u32[]{:S(2)}) %collective-permute-start.13) | collective-permute-done | bytes 262176 | tf_op jit(solution)/shard_map/ppermute | solution.py:888
  77.6 4.0 %first.1.acc_in = f32[512,1280]{1,0:T(8,128)S(1)} custom-call(s32[6]{0:T(128)S(1)} %stack.31.where_ref, bf16[512,256]{1,0:T(8,128)(2,1)S(1)} %collective-permute-done.12.refs_0_, bf16[512,256]{1,0:T(8,128)(2,1)S(1)} %collective-permute-done.13.refs_1_, bf16[512,256]{1,0:T(8,128)(2,1)S(1)} %collective-permute-done.4.refs_2_, ...), custom_call_target="tpu_custom_call" | custom-call | flops 1 | tf_op jit(solution)/shard_map/first/pallas_call | solution.py:777
  81.6 1.0 collective-permute-done.10.more
  82.6 1.1 %second.3 = (bf16[4,64,640]{2,1,0:T(8,128)(2,1)S(1)}, bf16[4,64,640]{2,1,0:T(8,128)(2,1)S(1)}) custom-call(s32[6]{0:T(128)S(1)} %stack.31.where_ref, bf16[512,256]{1,0:T(8,128)(2,1)S(1)} %collective-permute-done.5.slot, bf16[512,256]{1,0:T(8,128)(2,1)S(1)} %collective-permute-done.10.more, bf16[512,1280]{1,0:T(8,128)(2,1)S(1)} %collective-permute-done.refs_7_.fetched_ref, ...), custom_call_target="tpu_custom_call" | custom-call | flops 1 | tf_op jit(solution)/shard_map/second/pallas_call | solution.py:818
  83.7 0.0 copy-start.4
  83.7 0.1 collective-permute-start.18
  83.8 1.1 %second.2 = (bf16[4,64,640]{2,1,0:T(8,128)(2,1)S(1)}, bf16[4,64,640]{2,1,0:T(8,128)(2,1)S(1)}) custom-call(s32[6]{0:T(128)S(1)} %stack.31.where_ref, bf16[512,256]{1,0:T(8,128)(2,1)S(1)} %collective-permute-done.5.slot, bf16[512,256]{1,0:T(8,128)(2,1)S(1)} %collective-permute-done.10.more, bf16[512,1280]{1,0:T(8,128)(2,1)S(1)} %collective-permute-done.refs_7_.fetched_ref, ...), custom_call_target="tpu_custom_call" | custom-call | flops 1 | tf_op jit(solution)/shard_map/second/pallas_call | solution.py:818
  84.9 0.6 collective-permute-start.14
  85.5 0.6 add.8
  86.1 1.9 %collective-permute-start.19 = (bf16[64,640]{1,0:T(8,128)(2,1)S(1)}, bf16[64,640]{1,0:T(8,128)(2,1)S(1)}, u32[]{:S(2)}, u32[]{:S(2)}) collective-permute-start(bf16[64,640]{1,0:T(8,128)(2,1)S(1)} %get-tuple-element.68), channel_id=1, source_target_pairs={{0,12},{4,8},{8,4},{12,0},{1,13},{5,9},{9,5},{13,1},{2,14},{6,10},... | collective-permute-start | bytes 245768 | tf_op jit(solution)/shard_map/ppermute | solution.py:50
  88.0 4.0 %collective-permute-start.20 = (bf16[64,640]{1,0:T(8,128)(2,1)S(1)}, bf16[64,640]{1,0:T(8,128)(2,1)S(1)}, u32[]{:S(2)}, u32[]{:S(2)}) collective-permute-start(bf16[64,640]{1,0:T(8,128)(2,1)S(1)} %get-tuple-element.69), channel_id=1, source_target_pairs={{0,8},{4,12},{8,0},{12,4},{1,9},{5,13},{9,1},{13,5},{2,10},{6,14},... | collective-permute-start | bytes 245768 | tf_op jit(solution)/shard_map/ppermute | solution.py:50
  92.0 0.6 add.7
  92.6 1.9 %collective-permute-start.15 = (bf16[64,640]{1,0:T(8,128)(2,1)S(1)}, bf16[64,640]{1,0:T(8,128)(2,1)S(1)}, u32[]{:S(2)}, u32[]{:S(2)}) collective-permute-start(bf16[64,640]{1,0:T(8,128)(2,1)S(1)} %get-tuple-element.62), channel_id=1, source_target_pairs={{0,12},{4,8},{8,4},{12,0},{1,13},{5,9},{9,5},{13,1},{2,14},{6,10},... | collective-permute-start | bytes 245768 | tf_op jit(solution)/shard_map/ppermute | solution.py:50
  94.5 1.7 %collective-permute-start.16 = (bf16[64,640]{1,0:T(8,128)(2,1)S(1)}, bf16[64,640]{1,0:T(8,128)(2,1)S(1)}, u32[]{:S(2)}, u32[]{:S(2)}) collective-permute-start(bf16[64,640]{1,0:T(8,128)(2,1)S(1)} %get-tuple-element.63), channel_id=1, source_target_pairs={{0,8},{4,12},{8,0},{12,4},{1,9},{5,13},{9,1},{13,5},{2,10},{6,14},... | collective-permute-start | bytes 245768 | tf_op jit(solution)/shard_map/ppermute | solution.py:50
  96.2 1.8 %collective-permute-start.17 = (bf16[64,640]{1,0:T(8,128)(2,1)S(1)}, bf16[64,640]{1,0:T(8,128)(2,1)S(1)}, u32[]{:S(2)}, u32[]{:S(2)}) collective-permute-start(bf16[64,640]{1,0:T(8,128)(2,1)S(1)} %get-tuple-element.64), channel_id=1, source_target_pairs={{0,4},{4,0},{8,12},{12,8},{1,5},{5,1},{9,13},{13,9},{2,6},{6,2},{1... | collective-permute-start | bytes 245768 | tf_op jit(solution)/shard_map/ppermute | solution.py:50
  98.0 4.3 %collective-permute-done.20.refs_6_ = bf16[64,640]{1,0:T(8,128)(2,1)S(1)} collective-permute-done((bf16[64,640]{1,0:T(8,128)(2,1)S(1)}, bf16[64,640]{1,0:T(8,128)(2,1)S(1)}, u32[]{:S(2)}, u32[]{:S(2)}) %collective-permute-start.20) | collective-permute-done | bytes 81952 | tf_op jit(solution)/shard_map/ppermute | solution.py:50
  102.3 2.6 %collective-permute-done.16.refs_2_ = bf16[64,640]{1,0:T(8,128)(2,1)S(1)} collective-permute-done((bf16[64,640]{1,0:T(8,128)(2,1)S(1)}, bf16[64,640]{1,0:T(8,128)(2,1)S(1)}, u32[]{:S(2)}, u32[]{:S(2)}) %collective-permute-start.16) | collective-permute-done | bytes 81952 | tf_op jit(solution)/shard_map/ppermute | solution.py:50
  105.0 1.6 %mix.1 = bf16[64,5120]{1,0:T(8,128)(2,1)} custom-call(s32[6]{0:T(128)S(1)} %stack.31.where_ref, bf16[64,5120]{1,0:T(8,128)(2,1)S(1)} %copy-done.4, f32[1,5120]{1,0:T(1,128)S(1)} %bitcast.14, bf16[64,640]{1,0:T(8,128)(2,1)S(1)} %get-tuple-element.61.refs_0_, bf16[64,640]{1,0:T(8,128)(2,1)S(1)} %collective-permute-done.15.refs_1_, ...), custom_call_target="tpu_custom_call" | custom-call | flops 1 | tf_op jit(solution)/shard_map/mix/pallas_call | solution.py:917
  (30 shorter events, 0.1 us)
Async XLA Ops:
  0.0 3.7 %copy-start = (bf16[1024,1280]{1,0:T(8,128)(2,1)S(1)}, bf16[1024,1280]{1,0:T(8,128)(2,1)}, u32[]{:S(2)}) copy-start(bf16[1024,1280]{1,0:T(8,128)(2,1)} %refs_6_) | copy-start | bytes 7864324
  3.5 7.4 %copy-start.7 = (bf16[3,256,256]{2,1,0:T(8,128)(2,1)S(1)}, bf16[3,256,256]{2,1,0:T(8,128)(2,1)}, u32[]{:S(2)}) copy-start(bf16[3,256,256]{2,1,0:T(8,128)(2,1)} %get-tuple-element.40) | copy-start | bytes 1179652
  3.6 8.2 %copy-start.3 = (bf16[256,1024]{1,0:T(8,128)(2,1)S(1)}, bf16[256,1024]{1,0:T(8,128)(2,1)}, u32[]{:S(2)}) copy-start(bf16[256,1024]{1,0:T(8,128)(2,1)} %q_ref.3) | copy-start | bytes 1572868
  3.6 8.2 %copy-start.6 = (s32[2,2,8]{2,1,0:T(2,128)S(1)}, s32[2,2,8]{2,1,0:T(2,128)}, u32[]{:S(2)}) copy-start(s32[2,2,8]{2,1,0:T(2,128)} %exps_ref.3) | copy-start | bytes 388
  3.7 3.7 %copy-start.9 = (bf16[3,256,256]{2,1,0:T(8,128)(2,1)S(1)}, bf16[3,256,256]{2,1,0:T(8,128)(2,1)}, u32[]{:S(2)}) copy-start(bf16[3,256,256]{2,1,0:T(8,128)(2,1)} %get-tuple-element.38) | copy-start | bytes 1179652
  3.7 7.3 %copy-start.8 = (bf16[3,256,256]{2,1,0:T(8,128)(2,1)S(1)}, bf16[3,256,256]{2,1,0:T(8,128)(2,1)}, u32[]{:S(2)}) copy-start(bf16[3,256,256]{2,1,0:T(8,128)(2,1)} %get-tuple-element.39) | copy-start | bytes 1179652
  3.7 8.1 %copy-start.2 = (bf16[2,256,1024]{2,1,0:T(8,128)(2,1)S(1)}, bf16[2,256,1024]{2,1,0:T(8,128)(2,1)}, u32[]{:S(2)}) copy-start(bf16[2,256,1024]{2,1,0:T(8,128)(2,1)} %fresh_ref.3) | copy-start | bytes 3145732
  4.4 31.8 %collective-permute-start = (bf16[512,1280]{1,0:T(8,128)(2,1)S(1)}, bf16[512,1280]{1,0:T(8,128)(2,1)S(1)}, u32[]{:S(2)}, u32[]{:S(2)}) collective-permute-start(bf16[512,1280]{1,0:T(8,128)(2,1)S(1)} %take.1), channel_id=1, source_target_pairs={{0,2},{2,0},{1,3},{3,1},{4,6},{6,4},{5,7},{7,5},{8,10},{10,8},{9,1... | collective-permute-start | bytes 3932168 | tf_op jit(solution)/shard_map/ppermute | solution.py:50
  7.4 30.5 %collective-permute-start.3 = (bf16[3,256,256]{2,1,0:T(8,128)(2,1)S(1)}, bf16[3,256,256]{2,1,0:T(8,128)(2,1)S(1)}, u32[]{:S(2)}, u32[]{:S(2)}) collective-permute-start(bf16[3,256,256]{2,1,0:T(8,128)(2,1)S(1)} %copy-done.9), channel_id=1, source_target_pairs={{0,12},{4,8},{8,4},{12,0},{1,13},{5,9},{9,5},{13,1},{2,14},{6,10},... | collective-permute-start | bytes 1179656 | tf_op jit(solution)/shard_map/ppermute | solution.py:50
  11.0 33.3 %collective-permute-start.2 = (bf16[3,256,256]{2,1,0:T(8,128)(2,1)S(1)}, bf16[3,256,256]{2,1,0:T(8,128)(2,1)S(1)}, u32[]{:S(2)}, u32[]{:S(2)}) collective-permute-start(bf16[3,256,256]{2,1,0:T(8,128)(2,1)S(1)} %copy-done.8), channel_id=1, source_target_pairs={{0,8},{4,12},{8,0},{12,4},{1,9},{5,13},{9,1},{13,5},{2,10},{6,14},... | collective-permute-start | bytes 1179656 | tf_op jit(solution)/shard_map/ppermute | solution.py:50
  11.0 33.3 %collective-permute-start.1 = (bf16[3,256,256]{2,1,0:T(8,128)(2,1)S(1)}, bf16[3,256,256]{2,1,0:T(8,128)(2,1)S(1)}, u32[]{:S(2)}, u32[]{:S(2)}) collective-permute-start(bf16[3,256,256]{2,1,0:T(8,128)(2,1)S(1)} %copy-done.7), channel_id=1, source_target_pairs={{0,4},{4,0},{8,12},{12,8},{1,5},{5,1},{9,13},{13,9},{2,6},{6,2},{1... | collective-permute-start | bytes 1179656 | tf_op jit(solution)/shard_map/ppermute | solution.py:50
  11.8 2.2 %copy-start.1 = (bf16[2,1024,1024]{2,1,0:T(8,128)(2,1)S(1)}, bf16[2,1024,1024]{2,1,0:T(8,128)(2,1)}, u32[]{:S(2)}) copy-start(bf16[2,1024,1024]{2,1,0:T(8,128)(2,1)} %cached_ref.3) | copy-start | bytes 12582916
  36.2 41.5 %collective-permute-start.11 = (bf16[512,1280]{1,0:T(8,128)(2,1)S(1)}, bf16[512,1280]{1,0:T(8,128)(2,1)S(1)}, u32[]{:S(2)}, u32[]{:S(2)}) collective-permute-start(bf16[512,1280]{1,0:T(8,128)(2,1)S(1)} %collective-permute-done.refs_7_.fetched_ref), channel_id=1, source_target_pairs={{0,16},{16,0},{1,17},{17,1},{2,18},{18,2},{3,19},{19,3},{4,20},{20... | collective-permute-start | bytes 3932168 | tf_op jit(solution)/shard_map/ppermute | solution.py:50
  46.6 14.2 %collective-permute-start.9 = (bf16[512,256]{1,0:T(8,128)(2,1)S(1)}, bf16[512,256]{1,0:T(8,128)(2,1)S(1)}, u32[]{:S(2)}, u32[]{:S(2)}) collective-permute-start(bf16[512,256]{1,0:T(8,128)(2,1)S(1)} %bitcast.9), channel_id=1, source_target_pairs={{0,8},{4,12},{8,0},{12,4},{1,9},{5,13},{9,1},{13,5},{2,10},{6,14},... | collective-permute-start | bytes 786440 | tf_op jit(solution)/shard_map/ppermute | solution.py:50
  46.6 14.8 %collective-permute-start.8 = (bf16[512,256]{1,0:T(8,128)(2,1)S(1)}, bf16[512,256]{1,0:T(8,128)(2,1)S(1)}, u32[]{:S(2)}, u32[]{:S(2)}) collective-permute-start(bf16[512,256]{1,0:T(8,128)(2,1)S(1)} %bitcast.10), channel_id=1, source_target_pairs={{0,4},{4,0},{8,12},{12,8},{1,5},{5,1},{9,13},{13,9},{2,6},{6,2},{1... | collective-permute-start | bytes 786440 | tf_op jit(solution)/shard_map/ppermute | solution.py:50
  52.0 6.4 %collective-permute-start.4 = (bf16[512,256]{1,0:T(8,128)(2,1)S(1)}, bf16[512,256]{1,0:T(8,128)(2,1)S(1)}, u32[]{:S(2)}, u32[]{:S(2)}) collective-permute-start(bf16[512,256]{1,0:T(8,128)(2,1)S(1)} %bitcast.13), channel_id=1, source_target_pairs={{0,2},{2,0},{1,3},{3,1},{4,6},{6,4},{5,7},{7,5},{8,10},{10,8},{9,1... | collective-permute-start | bytes 786440 | tf_op jit(solution)/shard_map/ppermute | solution.py:50
  58.4 12.9 %collective-permute-start.7 = (bf16[512,256]{1,0:T(8,128)(2,1)S(1)}, bf16[512,256]{1,0:T(8,128)(2,1)S(1)}, u32[]{:S(2)}, u32[]{:S(2)}) collective-permute-start(bf16[512,256]{1,0:T(8,128)(2,1)S(1)} %collective-permute-done.4.refs_2_), channel_id=1, source_target_pairs={{0,8},{4,12},{8,0},{12,4},{1,9},{5,13},{9,1},{13,5},{2,10},{6,14},... | collective-permute-start | bytes 786440 | tf_op jit(solution)/shard_map/ppermute | solution.py:50
  59.0 13.8 %collective-permute-start.6 = (bf16[512,256]{1,0:T(8,128)(2,1)S(1)}, bf16[512,256]{1,0:T(8,128)(2,1)S(1)}, u32[]{:S(2)}, u32[]{:S(2)}) collective-permute-start(bf16[512,256]{1,0:T(8,128)(2,1)S(1)} %collective-permute-done.4.refs_2_), channel_id=1, source_target_pairs={{0,4},{4,0},{8,12},{12,8},{1,5},{5,1},{9,13},{13,9},{2,6},{6,2},{1... | collective-permute-start | bytes 786440 | tf_op jit(solution)/shard_map/ppermute | solution.py:50
  60.8 20.8 %collective-permute-start.5 = (bf16[512,256]{1,0:T(8,128)(2,1)S(1)}, bf16[512,256]{1,0:T(8,128)(2,1)S(1)}, u32[]{:S(2)}, u32[]{:S(2)}) collective-permute-start(bf16[512,256]{1,0:T(8,128)(2,1)S(1)} %collective-permute-done.4.refs_2_), channel_id=1, source_target_pairs={{4,8},{8,4},{5,9},{9,5},{6,10},{10,6},{7,11},{11,7},{20,24},{24,20... | collective-permute-start | bytes 786440 | tf_op jit(solution)/shard_map/ppermute | solution.py:50
  61.5 16.1 %collective-permute-start.13 = (bf16[512,256]{1,0:T(8,128)(2,1)S(1)}, bf16[512,256]{1,0:T(8,128)(2,1)S(1)}, u32[]{:S(2)}, u32[]{:S(2)}) collective-permute-start(bf16[512,256]{1,0:T(8,128)(2,1)S(1)} %collective-permute-done.9.refs_0_), channel_id=1, source_target_pairs={{4,0},{8,12},{5,1},{9,13},{6,2},{10,14},{7,3},{11,15},{20,16},{24,... | collective-permute-start | bytes 786440 | tf_op jit(solution)/shard_map/ppermute | solution.py:888
  71.3 2.7 %collective-permute-start.12 = (bf16[512,256]{1,0:T(8,128)(2,1)S(1)}, bf16[512,256]{1,0:T(8,128)(2,1)S(1)}, u32[]{:S(2)}, u32[]{:S(2)}) collective-permute-start(bf16[512,256]{1,0:T(8,128)(2,1)S(1)} %bitcast.12), channel_id=1, source_target_pairs={{4,8},{8,4},{5,9},{9,5},{6,10},{10,6},{7,11},{11,7},{20,24},{24,20... | collective-permute-start | bytes 786440 | tf_op jit(solution)/shard_map/ppermute | solution.py:50
  72.8 9.8 %collective-permute-start.10 = (bf16[512,256]{1,0:T(8,128)(2,1)S(1)}, bf16[512,256]{1,0:T(8,128)(2,1)S(1)}, u32[]{:S(2)}, u32[]{:S(2)}) collective-permute-start(bf16[512,256]{1,0:T(8,128)(2,1)S(1)} %collective-permute-done.7.refs_3_), channel_id=1, source_target_pairs={{4,0},{8,12},{5,1},{9,13},{6,2},{10,14},{7,3},{11,15},{20,16},{24,... | collective-permute-start | bytes 786440 | tf_op jit(solution)/shard_map/ppermute | solution.py:888
  83.7 21.2 %copy-start.4 = (bf16[64,5120]{1,0:T(8,128)(2,1)S(1)}, bf16[64,5120]{1,0:T(8,128)(2,1)}, u32[]{:S(2)}) copy-start(bf16[64,5120]{1,0:T(8,128)(2,1)} %hidden_ref.1) | copy-start | bytes 1966084
  83.7 21.2 %copy-start.5 = (f32[5120]{0:T(1024)S(1)}, f32[5120]{0:T(1024)}, u32[]{:S(2)}) copy-start(f32[5120]{0:T(1024)} %param.13) | copy-start | bytes 61444
  83.7 1.8 %collective-permute-start.18 = (bf16[4,64,640]{2,1,0:T(8,128)(2,1)S(1)}, bf16[4,64,640]{2,1,0:T(8,128)(2,1)S(1)}, u32[]{:S(2)}, u32[]{:S(2)}) collective-permute-start(bf16[4,64,640]{2,1,0:T(8,128)(2,1)S(1)} %get-tuple-element.66), channel_id=1, source_target_pairs={{0,1},{1,0},{2,3},{3,2},{4,5},{5,4},{6,7},{7,6},{8,9},{9,8},{10,11... | collective-permute-start | bytes 983048 | tf_op jit(solution)/shard_map/ppermute | solution.py:50
  84.9 7.1 %collective-permute-start.14 = (bf16[4,64,640]{2,1,0:T(8,128)(2,1)S(1)}, bf16[4,64,640]{2,1,0:T(8,128)(2,1)S(1)}, u32[]{:S(2)}, u32[]{:S(2)}) collective-permute-start(bf16[4,64,640]{2,1,0:T(8,128)(2,1)S(1)} %get-tuple-element.60), channel_id=1, source_target_pairs={{0,1},{1,0},{2,3},{3,2},{4,5},{5,4},{6,7},{7,6},{8,9},{9,8},{10,11... | collective-permute-start | bytes 983048 | tf_op jit(solution)/shard_map/ppermute | solution.py:50
  86.1 10.1 %collective-permute-start.19 = (bf16[64,640]{1,0:T(8,128)(2,1)S(1)}, bf16[64,640]{1,0:T(8,128)(2,1)S(1)}, u32[]{:S(2)}, u32[]{:S(2)}) collective-permute-start(bf16[64,640]{1,0:T(8,128)(2,1)S(1)} %get-tuple-element.68), channel_id=1, source_target_pairs={{0,12},{4,8},{8,4},{12,0},{1,13},{5,9},{9,5},{13,1},{2,14},{6,10},... | collective-permute-start | bytes 245768 | tf_op jit(solution)/shard_map/ppermute | solution.py:50
  88.0 14.3 %collective-permute-start.20 = (bf16[64,640]{1,0:T(8,128)(2,1)S(1)}, bf16[64,640]{1,0:T(8,128)(2,1)S(1)}, u32[]{:S(2)}, u32[]{:S(2)}) collective-permute-start(bf16[64,640]{1,0:T(8,128)(2,1)S(1)} %get-tuple-element.69), channel_id=1, source_target_pairs={{0,8},{4,12},{8,0},{12,4},{1,9},{5,13},{9,1},{13,5},{2,10},{6,14},... | collective-permute-start | bytes 245768 | tf_op jit(solution)/shard_map/ppermute | solution.py:50
  92.0 10.3 %collective-permute-start.21 = (bf16[64,640]{1,0:T(8,128)(2,1)S(1)}, bf16[64,640]{1,0:T(8,128)(2,1)S(1)}, u32[]{:S(2)}, u32[]{:S(2)}) collective-permute-start(bf16[64,640]{1,0:T(8,128)(2,1)S(1)} %get-tuple-element.70), channel_id=1, source_target_pairs={{0,4},{4,0},{8,12},{12,8},{1,5},{5,1},{9,13},{13,9},{2,6},{6,2},{1... | collective-permute-start | bytes 245768 | tf_op jit(solution)/shard_map/ppermute | solution.py:50
  92.6 9.7 %collective-permute-start.15 = (bf16[64,640]{1,0:T(8,128)(2,1)S(1)}, bf16[64,640]{1,0:T(8,128)(2,1)S(1)}, u32[]{:S(2)}, u32[]{:S(2)}) collective-permute-start(bf16[64,640]{1,0:T(8,128)(2,1)S(1)} %get-tuple-element.62), channel_id=1, source_target_pairs={{0,12},{4,8},{8,4},{12,0},{1,13},{5,9},{9,5},{13,1},{2,14},{6,10},... | collective-permute-start | bytes 245768 | tf_op jit(solution)/shard_map/ppermute | solution.py:50
  94.5 10.4 %collective-permute-start.16 = (bf16[64,640]{1,0:T(8,128)(2,1)S(1)}, bf16[64,640]{1,0:T(8,128)(2,1)S(1)}, u32[]{:S(2)}, u32[]{:S(2)}) collective-permute-start(bf16[64,640]{1,0:T(8,128)(2,1)S(1)} %get-tuple-element.63), channel_id=1, source_target_pairs={{0,8},{4,12},{8,0},{12,4},{1,9},{5,13},{9,1},{13,5},{2,10},{6,14},... | collective-permute-start | bytes 245768 | tf_op jit(solution)/shard_map/ppermute | solution.py:50
  96.2 8.7 %collective-permute-start.17 = (bf16[64,640]{1,0:T(8,128)(2,1)S(1)}, bf16[64,640]{1,0:T(8,128)(2,1)S(1)}, u32[]{:S(2)}, u32[]{:S(2)}) collective-permute-start(bf16[64,640]{1,0:T(8,128)(2,1)S(1)} %get-tuple-element.64), channel_id=1, source_target_pairs={{0,4},{4,0},{8,12},{12,8},{1,5},{5,1},{9,13},{13,9},{2,6},{6,2},{1... | collective-permute-start | bytes 245768 | tf_op jit(solution)/shard_map/ppermute | solution.py:50
